TPU v7x, 32 devices: a whole 2x2x4 slice. The times are simulated.
32 devices in a mesh: groups: 2 (over y), rows: 4 (over z), frames: 2 (over x), heads: 2 (over core).
Axes of the slice: x: 2, y: 2, z: 4, core: 2. Of those that a mesh axis runs over, the one named last changes fastest.
Arguments:
- latents: bfloat16 [4, 512, 3072], P(('groups', 'frames'), 'rows'), parts along dimension 0
- w_qkv: bfloat16 [3072, 3, 3072], P('rows', None, ('frames', 'heads')), may hold values from -0.109375 to 0.109375
- w_out: bfloat16 [3072, 3072], P(('frames', 'heads'), 'rows'), may hold values from -0.109375 to 0.109375
- win_blocks: int32 [16, 4], P(('groups', 'rows')), parts along dimension 0, may hold values from 0 to 7, as said below
- win_counts: int32 [16], P(('groups', 'rows')), parts along dimension 0, may hold values from 1 to 4, as said below
- block_window: int32 [16], P(('groups', 'rows')), parts along dimension 0, may hold values from 0 to 7, as said below
Outputs:
- mixed: bfloat16 [4, 512, 3072], P(('groups', 'frames'), ('rows', 'heads')), parts along dimension 0
There are 2 independent parts, one for each index of `groups`. A program takes and returns all parts, laid end to end along the dimension named above; an argument that names none is the same for every part. Nothing has to cross between parts.
Inputs may be any that keep to these rules, and one draw needn't show every extreme that they name: `win_blocks`: row w lists 4 different blocks; its first entry is w, and every entry c has c // 2 equal to w // 2 or one more or one less, counted cyclically modulo 8 // 2. `win_counts`: some window has 4 used entries. block_window[b] // 2 equals b // 2.
All inputs are finite; a program needn't handle non-finite values.
Results may differ from a plain program's by a relative error of at most 0.012.
The roundings to bfloat16 on the way count: a program that leaves them out, or rounds other values in their place, can miss the bound.
Values may be sent and summed in bfloat16 or wider, within the bound.
No kernel may reach another device: no remote copies, remote signals or barrier semaphores. Data moves between devices by JAX's collectives and lax.ppermute only.
A program may use at most 128 MiB of HBM per device.

v0:
```python
import math

import jax
import jax.numpy as jnp
from jax import lax
from jax.sharding import PartitionSpec as P

HD = 128
BS = 64
MAXB = 4


def with_halo(value, sides, width):
    for axis, dim in sides:
        peers, length = (lax.axis_size(axis), value.shape[dim])
        up = [(i, (i + 1) % peers) for i in range(peers)]
        down = [(j, i) for i, j in up]
        last = lax.slice_in_dim(value, length - width, length, axis=dim)
        first = lax.slice_in_dim(value, 0, width, axis=dim)
        before = lax.ppermute(last, axis, up)
        after = lax.ppermute(first, axis, down)
        value = jnp.concatenate([before, value, after], axis=dim)
    return value


def local(latents, w_qkv, w_out, win_blocks, win_counts, block_window):
    rows_n = lax.axis_size("rows")
    shard_idx = lax.axis_index("rows")
    frames = latents.shape[0] * lax.axis_size("frames")
    tok_frame = latents.shape[1]
    model_width = latents.shape[2]
    local_cols = w_qkv.shape[2]
    per_shard = tok_frame // BS
    block_total = per_shard * rows_n
    heads_here = local_cols // HD
    block_len = frames * BS
    score_scale = 1.0 / math.sqrt(HD)
    gathered = lax.all_gather(latents, "frames", axis=0, tiled=True)
    flat_tokens = gathered.reshape(frames * tok_frame, model_width)
    weight_rows = lax.all_gather(w_qkv, "rows", axis=0, tiled=True)
    projected = jnp.dot(
        flat_tokens,
        weight_rows.reshape(weight_rows.shape[0], 3 * local_cols),
        preferred_element_type=jnp.float32,
    ).astype(jnp.bfloat16)
    blocked = projected.reshape(frames, per_shard, BS, 3, local_cols).transpose(1, 0, 2, 3, 4)
    blocked = blocked.reshape(per_shard, block_len, 3, local_cols)
    queries = blocked[:, :, 0]
    keyvals = blocked[:, :, 1:]
    nearby = with_halo(keyvals, (("rows", 0),), per_shard)
    first_block = shard_idx * per_shard
    owners = block_window - first_block
    members = win_blocks[owners]
    lengths = win_counts[owners]
    positions = (members - first_block + per_shard + block_total) % block_total

    def attend(query_rows, picked, live_mask):
        key_count = picked.shape[0]
        key_blocks = nearby[picked]
        key_part = key_blocks[:, :, 0].reshape(key_count * block_len, heads_here, HD)
        value_part = key_blocks[:, :, 1].reshape(key_count * block_len, heads_here, HD)
        scores = (
            jnp.einsum(
                "qhd,khd->hqk",
                query_rows.reshape(block_len, heads_here, HD),
                key_part,
                preferred_element_type=jnp.float32,
            )
            * score_scale
        )
        scores = jnp.where(live_mask[None, None, :], scores, -jnp.inf)
        row_max = jnp.max(scores, axis=-1, keepdims=True)
        raised = jnp.exp(scores - row_max)
        weights = (raised / jnp.sum(raised, axis=-1, keepdims=True)).astype(jnp.bfloat16)
        blended = jnp.einsum(
            "hqk,khd->qhd", weights, value_part, preferred_element_type=jnp.float32
        )
        return blended.reshape(block_len, local_cols).astype(jnp.bfloat16)

    def one_block(block_item):
        query_rows, picked, length = block_item
        live_mask = jnp.repeat(jnp.arange(MAXB) < length, block_len)
        return attend(query_rows, picked, live_mask)

    attended = lax.map(one_block, (queries, positions, lengths))
    ordered = attended.reshape(per_shard, frames, BS, local_cols).transpose(1, 0, 2, 3)
    ordered = ordered.reshape(frames * tok_frame, local_cols)
    w_full = lax.all_gather(w_out, "rows", axis=1, tiled=True)
    group_count = lax.axis_size(("frames", "heads"))
    out_rows = frames * tok_frame // group_count
    summed = lax.psum_scatter(
        jnp.dot(ordered, w_full, preferred_element_type=jnp.float32).astype(jnp.bfloat16),
        ("frames", "heads"),
        scatter_dimension=0,
        tiled=True,
    )
    return summed.reshape(1, out_rows, model_width)


def solution(mesh):
    in_specs = (
        P(("groups", "frames"), "rows", None),
        P("rows", None, ("frames", "heads")),
        P(("frames", "heads"), "rows"),
        P(("groups", "rows"), None),
        P(("groups", "rows")),
        P(("groups", "rows")),
    )
    out_specs = P(("groups", "frames"), ("rows", "heads"), None)
    return jax.shard_map(local, mesh=mesh, in_specs=in_specs, out_specs=out_specs, check_vma=False)
```

profile of v0, /device:TPU:0, one launch (start us, length us, event | category | flops | bytes accessed | tf_op | source)
XLA Modules:
  0.0 456.9 jit_solution(11301492291758976709)
XLA Ops:
  6.5 0.7 all-gather.4.cloned.1.call-update
  7.3 6.0 %copy.32 = bf16[768,3,768]{0,2,1:T(8,128)(2,1)} copy(bf16[768,3,768]{2,0,1:T(8,128)(2,1)} %param.9) | data formatting | bytes 7077888 | tf_op args[1]
  13.4 0.0 all-gather.8.cloned.1.call-start
  13.4 0.7 all-gather.8.cloned.1.call-update
  14.2 24.7 %all-gather.4.cloned.1.call-done = bf16[2,128,3072]{2,1,0:T(8,128)(2,1)} async-done(((bf16[1,128,3072]{2,1,0:T(8,128)(2,1)}), bf16[2,128,3072]{2,1,0:T(8,128)(2,1)}) %all-gather.4.cloned.1.call-update) | async-done | bytes 1572880 | tf_op jit(solution)/shard_map/all_gather | solution.py:38
  38.8 245.5 %all-gather.6.cloned.1.call-done = bf16[3072,3,768]{0,2,1:T(8,128)(2,1)} async-done(((bf16[768,3,768]{0,2,1:T(8,128)(2,1)}), bf16[3072,3,768]{0,2,1:T(8,128)(2,1)}) %all-gather.6.cloned.1.call-update) | async-done | bytes 14155792 | tf_op jit(solution)/shard_map/all_gather | solution.py:40
  284.4 9.4 %convolution_convert_fusion.2 = bf16[256,2304]{1,0:T(8,128)(2,1)S(1)} fusion(bf16[256,3072]{1,0:T(8,128)(2,1)} %bitcast.57, bf16[3072,2304]{0,1:T(8,128)(2,1)} %bitcast.56), kind=kOutput, calls=%fused_computation.24 | convolution fusion | flops 3624468480 | bytes 16908288 | tf_op jit(solution)/shard_map/dot_general | solution.py:41
  293.7 0.6 reshape.71
  294.3 0.2 copy.33
  294.5 0.1 slice.22
  294.6 0.1 collective-permute-start
  294.6 3.8 collective-permute-start.1
  298.5 0.6 gather_fusion.1
  299.0 0.6 gather_fusion.2
  299.7 33.9 %collective-permute-done = bf16[2,128,2,768]{3,1,2,0:T(8,128)(2,1)S(1)} collective-permute-done((bf16[2,128,2,768]{3,1,2,0:T(8,128)(2,1)S(1)}, bf16[2,128,2,768]{3,1,2,0:T(8,128)(2,1)S(1)}, u32[]{:S(2)}, u32[]{:S(2)}) %collective-permute-start) | collective-permute-done | bytes 786464 | tf_op jit(solution)/shard_map/ppermute | solution.py:20
  333.6 30.4 %collective-permute-done.1 = bf16[2,128,2,768]{3,1,2,0:T(8,128)(2,1)} collective-permute-done((bf16[2,128,2,768]{3,1,2,0:T(8,128)(2,1)S(1)}, bf16[2,128,2,768]{3,1,2,0:T(8,128)(2,1)}, u32[]{:S(2)}, u32[]{:S(2)}) %collective-permute-start.1) | collective-permute-done | bytes 786464 | tf_op jit(solution)/shard_map/ppermute | solution.py:21
  364.1 1.4 pad_maximum_fusion
  365.5 3.8 copy.34
  369.3 45.5 %while.10 = (s32[]{:T(128)}, bf16[2,128,768]{2,1,0:T(8,128)(2,1)}, s32[2,4]{1,0:T(2,128)S(1)}, bf16[6,128,2,768]{3,2,1,0:T(2,128)(2,1)}, s32[2]{0:T(128)S(1)}, /*index=5*/bf16[2,128,768]{2,1,0:T(8,128)(2,1)S(1)}, s32[]{:T(128)}) while((s32[]{:T(128)}, bf16[2,128,768]{2,1,0:T(8,128)(2,1)}, s32[2,4]{1,0:T(2,128)S(1)}, ...), condition=%wide.region_3.4_spmd, body=%wide.region_0.3_spmd.sunk | while | flops 203785744 | bytes 17706668 | solution.py:85
  369.3 5.6 %gather_fusion = bf16[4,128,2,768]{3,2,1,0:T(2,128)(2,1)S(1)} fusion(bf16[6,128,2,768]{3,2,1,0:T(2,128)(2,1)} %get-tuple-element.140, s32[1024]{0:T(1024)S(1)} %pad_clamp_fusion.3), kind=kCustom, calls=%fused_computation.clone.1 | custom fusion | bytes 3145744 | tf_op jit(solution)/shard_map/while/body/eval_jaxpr/gather | solution.py:59
  374.9 6.6 %slice_reduce_fusion.2 = (bf16[4,128,768]{2,1,0:T(8,128)(2,1)}, bf16[4,128,1,768]{3,2,1,0:T(2,128)(2,1)S(1)}) fusion(bf16[4,128,2,768]{3,2,1,0:T(2,128)(2,1)S(1)} %gather_fusion), kind=kLoop, calls=%fused_computation.5.clone.1 | loop fusion | bytes 3145728 | tf_op jit(solution)/shard_map/while/body/eval_jaxpr/slice | solution.py:60
  381.5 2.0 reshape.109
  383.5 0.2 copy.60
  383.7 0.7 dynamic_slice.25
  384.3 0.7 iota_compare_fusion.2
  385.0 0.1 broadcast_bitcast_fusion.2
  385.1 1.8 fusion.32
  386.9 2.1 copy.59
  389.0 0.3 squeeze.21
  389.3 1.9 convolution_convert_fusion.4
  391.2 0.1 copy.61
  391.4 0.7 constant_dynamic-update-slice_fusion.2
  392.1 5.5 %gather_fusion = bf16[4,128,2,768]{3,2,1,0:T(2,128)(2,1)S(1)} fusion(bf16[6,128,2,768]{3,2,1,0:T(2,128)(2,1)} %get-tuple-element.140, s32[1024]{0:T(1024)S(1)} %pad_clamp_fusion.3), kind=kCustom, calls=%fused_computation.clone.1 | custom fusion | bytes 3145744 | tf_op jit(solution)/shard_map/while/body/eval_jaxpr/gather | solution.py:59
  397.6 6.6 %slice_reduce_fusion.2 = (bf16[4,128,768]{2,1,0:T(8,128)(2,1)}, bf16[4,128,1,768]{3,2,1,0:T(2,128)(2,1)S(1)}) fusion(bf16[4,128,2,768]{3,2,1,0:T(2,128)(2,1)S(1)} %gather_fusion), kind=kLoop, calls=%fused_computation.5.clone.1 | loop fusion | bytes 3145728 | tf_op jit(solution)/shard_map/while/body/eval_jaxpr/slice | solution.py:60
  404.2 2.0 reshape.109
  406.2 0.2 copy.60
  406.4 0.7 dynamic_slice.25
  407.1 0.7 iota_compare_fusion.2
  407.8 0.1 broadcast_bitcast_fusion.2
  407.8 1.8 fusion.32
  409.7 2.1 copy.59
  411.8 0.3 squeeze.21
  412.1 1.9 convolution_convert_fusion.4
  414.0 0.1 copy.61
  414.1 0.7 constant_dynamic-update-slice_fusion.2
  414.8 1.0 copy.37
  415.9 4.9 %convolution_convert_fusion.1 = bf16[256,3072]{1,0:T(8,128)(2,1)} fusion(bf16[256,768]{1,0:T(8,128)(2,1)S(1)} %bitcast.55, bf16[768,3072]{1,0:T(8,128)(2,1)} %all-gather.8.cloned.1.call-done), kind=kOutput, calls=%fused_computation.23 | convolution fusion | flops 1208745984 | bytes 6684672 | tf_op jit(solution)/shard_map/dot_general | solution.py:92
  420.8 29.5 %reduce-scatter.2.cloned.1.call-done = bf16[64,3072]{1,0:T(8,128)(2,1)} async-done(((bf16[256,3072]{1,0:T(8,128)(2,1)}), bf16[64,3072]{1,0:T(8,128)(2,1)}) %reduce-scatter.2.cloned.1.call-update) | async-done | bytes 393232 | tf_op jit(solution)/shard_map/reduce_scatter | solution.py:91
  (23 shorter events, 0.3 us)
Async XLA Ops:
  6.5 291.9 %copy-start = (s32[2,4]{1,0:T(2,128)S(1)}, s32[2,4]{1,0:T(2,128)}, u32[]{:S(2)}) copy-start(s32[2,4]{1,0:T(2,128)} %param.11) | copy-start | bytes 100
  6.5 32.3 %all-gather.4.cloned.1.call-start = ((), (), s32[]{:S(2)}) async-start(), calls=%async_computation.1 | async-start | bytes 2359296 | tf_op jit(solution)/shard_map/all_gather | solution.py:38
  7.3 277.1 %all-gather.6.cloned.1.call-start = ((), (), s32[]{:S(2)}) async-start(), calls=%async_computation.2 | async-start | bytes 17694720 | tf_op jit(solution)/shard_map/all_gather | solution.py:40
  13.4 402.5 %all-gather.8.cloned.1.call-start = ((), (), s32[]{:S(2)}) async-start(), calls=%async_computation.3 | async-start | bytes 5898240 | tf_op jit(solution)/shard_map/all_gather | solution.py:88
  14.1 436.2 %reduce-scatter.2.cloned.1.call-start = ((), (), s32[]{:S(2)}) async-start(), calls=%async_computation.4 | async-start | bytes 1966080 | tf_op jit(solution)/shard_map/reduce_scatter | solution.py:91
  294.3 4.1 copy-start.2
  294.3 4.7 %copy-start.1 = (s32[2]{0:T(128)S(1)}, s32[2]{0:T(128)}, u32[]{:S(2)}) copy-start(s32[2]{0:T(128)} %param.12) | copy-start | bytes 28
  294.6 39.1 %collective-permute-start = (bf16[2,128,2,768]{3,1,2,0:T(8,128)(2,1)S(1)}, bf16[2,128,2,768]{3,1,2,0:T(8,128)(2,1)S(1)}, u32[]{:S(2)}, u32[]{:S(2)}) collective-permute-start(bf16[2,128,2,768]{3,1,2,0:T(8,128)(2,1)S(1)} %slice.22), channel_id=1, source_target_pairs={{0,4},{4,8},{8,12},{12,0},{1,5},{5,9},{9,13},{13,1},{2,6},{6,10},{... | collective-permute-start | bytes 2359304 | tf_op jit(solution)/shard_map/ppermute | solution.py:20
  294.6 69.5 %collective-permute-start.1 = (bf16[2,128,2,768]{3,1,2,0:T(8,128)(2,1)S(1)}, bf16[2,128,2,768]{3,1,2,0:T(8,128)(2,1)}, u32[]{:S(2)}, u32[]{:S(2)}) collective-permute-start(bf16[2,128,2,768]{3,1,2,0:T(8,128)(2,1)S(1)} %slice.22), channel_id=1, source_target_pairs={{4,0},{8,4},{12,8},{0,12},{5,1},{9,5},{13,9},{1,13},{6,2},{10,6},{... | collective-permute-start | bytes 2359304 | tf_op jit(solution)/shard_map/ppermute | solution.py:21
Sparse Core Ops, SparseCore 0:
  8.9 29.8 all-gather.3
  40.4 243.9 all-gather.5
  285.9 121.0 all-gather.7
  420.9 29.3 reduce-scatter.1
where the time goes:
time: 457 us
  waiting for transfers between devices  366 us (80%)
  local copies, waits for them, and re-layouts  49.5 us (11%)
  matrix products  21.7 us (5%)
  between operations  13.2 us (3%)
    all_gather x1, waiting for transfers between devices, local(): weight_rows = lax.all_gather(w_qkv, 'rows', axis=0, tiled=True)  246 us
    ppermute x1, waiting for transfers between devices, with_halo(): before = lax.ppermute(last, axis, up)  33.9 us
    ppermute x1, waiting for transfers between devices, with_halo(): after = lax.ppermute(first, axis, down)  30.4 us
    reduce_scatter x1, waiting for transfers between devices, local(): lax.psum_scatter(jnp.dot(ordered, w_full, preferred_element_type=jnp.floa...  29.5 us
    all_gather x1, waiting for transfers between devices, local(): gathered = lax.all_gather(latents, 'frames', axis=0, tiled=True)  24.7 us
    slice x2, local copies, waits for them, and re-layouts, attend(): key_blocks[:, :, 0].reshape(key_count * block_len, heads_here, HD)  13.2 us
    gather x2, local copies, waits for them, and re-layouts, attend(): key_blocks = nearby[picked]  11.1 us
    dot_general x1, matrix products, local(): jnp.dot(flat_tokens, weight_rows.reshape(weight_rows.shape[0], 3 * local_...  9.36 us
  transfers between devices with their start and end apart: 6, of which 5 were waited for; matrix products, arithmetic and copies ran while one was open for 15% of the time, Pallas kernels for 0%

commit v1 on v0

--- a/solution.py
+++ b/solution.py
@@ -3,11 +3,15 @@
 import jax
 import jax.numpy as jnp
 from jax import lax
+from jax.experimental import pallas as pl
+from jax.experimental.pallas import tpu as pltpu
 from jax.sharding import PartitionSpec as P
 
 HD = 128
 BS = 64
 MAXB = 4
+VMEM_BYTES = 48 * 1024 * 1024
+EXP2_SCALE = math.log2(math.e) / math.sqrt(HD)
 
 
 def with_halo(value, sides, width):
@@ -23,7 +27,7 @@
     return value
 
 
-def local(latents, w_qkv, w_out, win_blocks, win_counts, block_window):
+def by_tokens(latents, w_qkv, w_out, win_blocks, win_counts, block_window):
     rows_n = lax.axis_size("rows")
     shard_idx = lax.axis_index("rows")
     frames = latents.shape[0] * lax.axis_size("frames")
@@ -97,6 +101,209 @@
     return summed.reshape(1, out_rows, model_width)
 
 
+def swap(value, axis):
+    return lax.ppermute(value, axis, [(0, 1), (1, 0)])
+
+
+def call(kernel, out_shape, prefetch, operands, scratch=(), flops=0, read=0):
+    return pl.pallas_call(
+        kernel,
+        out_shape=out_shape,
+        grid_spec=pltpu.PrefetchScalarGridSpec(
+            num_scalar_prefetch=len(prefetch),
+            grid=(),
+            in_specs=[pl.BlockSpec(memory_space=pltpu.VMEM)] * len(operands),
+            out_specs=jax.tree.map(lambda _: pl.BlockSpec(memory_space=pltpu.VMEM), out_shape),
+            scratch_shapes=scratch,
+        ),
+        compiler_params=pltpu.CompilerParams(vmem_limit_bytes=VMEM_BYTES),
+        cost_estimate=pl.CostEstimate(flops=flops, bytes_accessed=read, transcendentals=0),
+    )(*prefetch, *operands)
+
+
+def project_part(tokens, chunk_ids, chunks, total):
+    rows, depth, cols = tokens.shape[0], chunks[0].shape[1], chunks[0].shape[2]
+    last = total is not None
+
+    def kernel(ids_ref, tok_ref, *refs):
+        w_refs = refs[: len(chunks)]
+        rest = refs[len(chunks) :]
+        for part in range(3):
+            where = slice(part * cols, (part + 1) * cols)
+            acc = rest[0][:, where] if last else None
+            for i, w_ref in enumerate(w_refs):
+                start = pl.multiple_of(ids_ref[i] * depth, depth)
+                term = jnp.dot(
+                    tok_ref[:, pl.ds(start, depth)], w_ref[part], preferred_element_type=jnp.float32
+                )
+                acc = term if acc is None else acc + term
+            if not last:
+                rest[0][:, where] = acc
+            elif part == 0:
+                rest[1][...] = acc.astype(jnp.bfloat16)
+            else:
+                rest[2][:, (part - 1) * cols : part * cols] = acc.astype(jnp.bfloat16)
+
+    if last:
+        out_shape = (
+            jax.ShapeDtypeStruct((rows, cols), jnp.bfloat16),
+            jax.ShapeDtypeStruct((rows, 2 * cols), jnp.bfloat16),
+        )
+    else:
+        out_shape = jax.ShapeDtypeStruct((rows, 3 * cols), jnp.float32)
+    operands = [tokens, *chunks] + ([total] if last else [])
+    flops = 2 * rows * depth * len(chunks) * 3 * cols
+    return call(kernel, out_shape, [chunk_ids], operands, flops=flops, read=flops // 200)
+
+
+def attend_all(core, members, counts, queries, own, other, block_len):
+    rows, cols = queries.shape
+    blocks = rows // block_len
+
+    def kernel(core_ref, members_ref, counts_ref, q_ref, own_ref, other_ref, out_ref, kv_ref):
+        kv_ref[0] = own_ref[...].reshape(blocks, block_len, 2 * cols)
+        kv_ref[1] = other_ref[...].reshape(blocks, block_len, 2 * cols)
+        column = lax.broadcasted_iota(jnp.int32, (block_len, MAXB * block_len), 1)
+        for b in range(blocks):
+            live = column < counts_ref[b] * block_len
+            listed = []
+            for j in range(MAXB):
+                member = members_ref[b * MAXB + j]
+                side = (member + core_ref[0]) % 2
+                listed.append(kv_ref[side, member // 2])
+            q_rows = q_ref[b * block_len : (b + 1) * block_len, :]
+            for h in range(cols // HD):
+                at = slice(h * HD, (h + 1) * HD)
+                at_v = slice(cols + h * HD, cols + (h + 1) * HD)
+                keys = jnp.concatenate([block[:, at] for block in listed], axis=0)
+                values = jnp.concatenate([block[:, at_v] for block in listed], axis=0)
+                scores = lax.dot_general(
+                    q_rows[:, at], keys, (((1,), (1,)), ((), ())), preferred_element_type=jnp.float32
+                )
+                scores = jnp.where(live, scores, -jnp.inf)
+                raised = jnp.exp2((scores - jnp.max(scores, axis=-1, keepdims=True)) * EXP2_SCALE)
+                weights = raised * (1.0 / jnp.sum(raised, axis=-1, keepdims=True))
+                blended = jnp.dot(
+                    weights.astype(jnp.bfloat16), values, preferred_element_type=jnp.float32
+                )
+                out_ref[b, :, at] = blended.astype(jnp.bfloat16)
+
+    return call(
+        kernel,
+        jax.ShapeDtypeStruct((blocks, block_len, cols), jnp.bfloat16),
+        [core, members, counts],
+        [queries, own, other],
+        scratch=[pltpu.VMEM((2, blocks, block_len, 2 * cols), jnp.bfloat16)],
+        flops=4 * rows * MAXB * block_len * cols,
+        read=8 * rows * cols,
+    )
+
+
+def mix(places, frame, attended, w_parts):
+    _, block_len, depth = attended.shape
+    peers, _, cols = w_parts[0].shape
+    half = block_len // 2
+
+    def kernel(places_ref, frame_ref, a_ref, w0, w1, w2, w3, keep_ref, send_ref, sum_ref):
+        for r in range(peers):
+            def term(refs, at):
+                acc = None
+                for i, ref in enumerate(refs):
+                    part = jnp.dot(a_ref[places_ref[at + i]], ref[r], preferred_element_type=jnp.float32)
+                    acc = part if acc is None else acc + part
+                return acc.astype(jnp.bfloat16).astype(jnp.float32)
+
+            sum_ref[...] = term((w0, w1), 0) + term((w2, w3), 2)
+            mine = pl.multiple_of(frame_ref[0] * half, half)
+            theirs = pl.multiple_of((1 - frame_ref[0]) * half, half)
+            keep_ref[:, r * cols : (r + 1) * cols] = sum_ref[pl.ds(mine, half), :]
+            send_ref[:, r * cols : (r + 1) * cols] = sum_ref[pl.ds(theirs, half), :].astype(jnp.bfloat16)
+
+    shape = (half, peers * cols)
+    return call(
+        kernel,
+        (jax.ShapeDtypeStruct(shape, jnp.float32), jax.ShapeDtypeStruct(shape, jnp.bfloat16)),
+        [places, frame],
+        [attended, *w_parts],
+        scratch=[pltpu.VMEM((block_len, cols), jnp.float32)],
+        flops=2 * block_len * depth * 4 * peers * cols,
+        read=8 * depth * peers * cols,
+    )
+
+
+def by_heads(latents, w_qkv, w_out, win_blocks, win_counts, block_window):
+    rows_n, heads_n = lax.axis_size("rows"), lax.axis_size("heads")
+    group, row = lax.axis_index("groups"), lax.axis_index("rows")
+    frame, core = lax.axis_index("frames"), lax.axis_index("heads")
+    model_width = latents.shape[2]
+    depth, _, local_cols = w_qkv.shape
+    block_len = 2 * BS
+    span = rows_n // heads_n
+    cols = local_cols // span
+    half = depth // 2
+
+    tables = jnp.concatenate([win_blocks, win_counts[:, None], block_window[:, None]], axis=1)
+    tables = lax.all_gather(tables, "rows", axis=0, tiled=True)
+    windows = lax.dynamic_index_in_dim(
+        tables[:, MAXB + 1].reshape(rows_n, heads_n), core, axis=1, keepdims=False
+    )
+    picked = tables[windows]
+    members, counts = picked[:, :MAXB].reshape(-1), picked[:, MAXB]
+
+    mine = lax.dynamic_slice_in_dim(latents[0], core * BS, BS, axis=0)
+    tokens = lax.all_gather(mine, ("rows", "frames"), axis=0, tiled=True)
+
+    w_half = lax.dynamic_slice_in_dim(w_qkv.transpose(1, 0, 2), group * half, half, axis=1)
+    chunks, ids = [], []
+    for k in range(span):
+        pairs = [
+            (r * heads_n + h, (h * span + (k + r) % span) * heads_n + r // span)
+            for r in range(rows_n)
+            for h in range(heads_n)
+        ]
+        piece = lax.dynamic_slice_in_dim(w_half, (k + row) % span * cols, cols, axis=2)
+        here = lax.ppermute(piece, ("rows", "heads"), pairs)
+        there = swap(here, "groups")
+        chunks += [here, there]
+        source = core * span + (row - k) % span
+        ids += [2 * source + group, 2 * source + 1 - group]
+    ids = jnp.stack(ids).astype(jnp.int32)
+    other_ids = (ids + (1 - 2 * core) * 2 * span).astype(jnp.int32)
+    total = project_part(tokens, ids, chunks, None)
+    queries, keyvals = project_part(tokens, other_ids, [swap(c, "heads") for c in chunks], total)
+
+    attended = attend_all(
+        core.reshape(1), members, counts, queries, keyvals, swap(keyvals, "heads"), block_len
+    )
+    attended = lax.all_to_all(attended, "rows", 0, 0, tiled=True)
+
+    out_half = lax.dynamic_slice_in_dim(w_out, group * cols, cols, axis=0)
+    out_here = lax.all_gather(out_half, "rows", axis=0).reshape(rows_n, cols, w_out.shape[1])
+    out_there = swap(out_here, "groups")
+    first = core * span
+    second = (1 - core) * span
+    places = jnp.stack([first + group, first + 1 - group, second + group, second + 1 - group])
+    keep, send = mix(
+        places.astype(jnp.int32),
+        frame.reshape(1),
+        attended,
+        [out_here, out_there, swap(out_here, "heads"), swap(out_there, "heads")],
+    )
+    out = keep + swap(send, "frames").astype(jnp.float32)
+    return out.astype(jnp.bfloat16).reshape(1, BS, model_width)
+
+
+def local(latents, w_qkv, w_out, win_blocks, win_counts, block_window):
+    rows_n = lax.axis_size("rows")
+    pairs = all(lax.axis_size(axis) == 2 for axis in ("groups", "frames", "heads"))
+    heads_here = w_qkv.shape[2] // HD
+    if pairs and rows_n == 4 and heads_here % 2 == 0 and latents.shape[:2] == (1, 2 * BS):
+        plan = by_heads
+    else:
+        plan = by_tokens
+    return plan(latents, w_qkv, w_out, win_blocks, win_counts, block_window)
+
+
 def solution(mesh):
     in_specs = (
         P(("groups", "frames"), "rows", None),

time: 457 us -> 233 us (0.51)
  waiting for transfers between devices: 366 us -> 112 us
  starting transfers between devices: 3.99 us -> 50.8 us
  local copies, waits for them, and re-layouts: 49.5 us -> 14.9 us
  Pallas kernels: 0 us -> 26 us
  matrix products: 21.7 us -> 0 us
  blocking collectives: 0 us -> 14.4 us
    all_gather x3 -> x2, waiting for transfers between devices: 270 us -> 51.6 us  [the longest x1 51.6 us: by_heads(): lax.all_gather(out_half, 'rows', axis=0)]
    ppermute x2 -> x13, starting transfers between devices: 3.87 us -> 46.6 us  [the longest x11 45.8 us: swap(): return lax.ppermute(value, axis, [(0, 1), (1, 0)])]
    reduce_scatter x1 -> x0, waiting for transfers between devices: 29.5 us -> none  [local(): lax.psum_scatter(jnp.dot(ordered, w_full, preferred_element_type=jnp.floa...]
    pallas_call x0 -> x4, Pallas kernels: none -> 26 us  [call(): pl.pallas_call(kernel, out_shape=out_shape, grid_spec=pltpu.PrefetchScala...]
    dot_general x4 -> x0, matrix products: 18 us -> none  [the longest x1 9.36 us: local(): jnp.dot(flat_tokens, weight_rows.reshape(weight_rows.shape[0], 3 * local_...]
    slice x5 -> x2, local copies, waits for them, and re-layouts: 17.4 us -> 0.36 us  [the longest x1 0.18 us: by_heads(): members, counts = (picked[:, :MAXB].reshape(-1), picked[:, MAXB])]
    ppermute x2 -> x13, waiting for transfers between devices: 64.4 us -> 49.6 us  [the longest x2 32.9 us: by_heads(): here = lax.ppermute(piece, ('rows', 'heads'), pairs)]
    all_gather x0 -> x1, blocking collectives: none -> 14.4 us  [by_heads(): tables = lax.all_gather(tables, 'rows', axis=0, tiled=True)]
  transfers between devices with their start and end apart: 6 -> 16, of which waited for: 5 -> 6; matrix products, arithmetic and copies ran while one was open for 15% -> 3% of each run, Pallas kernels for 0% -> 9%
where the time goes in v1:
time: 233 us
  waiting for transfers between devices  112 us (48%)
  starting transfers between devices  50.8 us (22%)
  Pallas kernels  26 us (11%)
  local copies, waits for them, and re-layouts  14.9 us (6%)
  blocking collectives  14.4 us (6%)
  between operations  13.6 us (6%)
    all_gather x1, waiting for transfers between devices, by_heads(): lax.all_gather(out_half, 'rows', axis=0)  51.6 us
    ppermute x11, starting transfers between devices, swap(): return lax.ppermute(value, axis, [(0, 1), (1, 0)])  45.8 us
    ppermute x2, waiting for transfers between devices, by_heads(): here = lax.ppermute(piece, ('rows', 'heads'), pairs)  32.9 us
    pallas_call x4, Pallas kernels, call(): pl.pallas_call(kernel, out_shape=out_shape, grid_spec=pltpu.PrefetchScala...  26 us
    ppermute x11, waiting for transfers between devices, swap(): return lax.ppermute(value, axis, [(0, 1), (1, 0)])  16.7 us
    all_gather x1, blocking collectives, by_heads(): tables = lax.all_gather(tables, 'rows', axis=0, tiled=True)  14.4 us
    all_to_all x1, waiting for transfers between devices, by_heads(): attended = lax.all_to_all(attended, 'rows', 0, 0, tiled=True)  10.5 us
    unnamed x26, local copies, waits for them, and re-layouts  8.19 us
  transfers between devices with their start and end apart: 16, of which 6 were waited for; matrix products, arithmetic and copies ran while one was open for 3% of the time, Pallas kernels for 9%

profile of v1, /device:TPU:0, one launch (start us, length us, event | category | flops | bytes accessed | tf_op | source)
XLA Modules:
  0.0 232.6 jit_solution(11583489673216118015)
XLA Ops:
  6.5 1.3 copy-done
  7.8 0.9 constant_dynamic-slice_fusion
  8.7 0.0 all-gather.6.cloned.1.call-start
  8.7 1.8 constant_dynamic-slice_fusion.1
  10.5 0.0 all-gather.6.cloned.1.call-update
  10.5 51.6 %all-gather.8.cloned.1.call-done = bf16[1536,768]{1,0:T(8,128)(2,1)} async-done(((bf16[384,768]{1,0:T(8,128)(2,1)}), bf16[1536,768]{1,0:T(8,128)(2,1)}) %all-gather.8.cloned.1.call-update) | async-done | bytes 2359312 | tf_op jit(solution)/shard_map/all_gather | solution.py:281
  62.1 1.5 collective-permute-start.9
  63.6 2.8 %dynamic-slice_bitcast_fusion = (bf16[3,384,384]{2,1,0:T(8,128)(2,1)S(1)}, bf16[3,384,384]{2,1,0:T(8,128)(2,1)S(1)}) fusion(bf16[768,3,768]{2,0,1:T(8,128)(2,1)} %param.7, s32[]{:T(128)S(6)} %select_n.50, s32[]{:T(128)S(6)} %select_n.55, s32[]{:T(128)S(6)} %select_n.52), kind=kLoop, calls=%fused_computation.1 | loop fusion | bytes 3538956 | tf_op jit(solution)/shard_map/dynamic_slice | solution.py:264
  66.4 0.7 collective-permute-start
  67.1 0.1 collective-permute-start.4
  67.2 0.8 collective-permute-start.2
  68.0 32.9 %collective-permute-done.4.refs_2_ = bf16[3,384,384]{2,1,0:T(8,128)(2,1)} collective-permute-done((bf16[3,384,384]{2,1,0:T(8,128)(2,1)S(1)}, bf16[3,384,384]{2,1,0:T(8,128)(2,1)}, u32[]{:S(2)}, u32[]{:S(2)}) %collective-permute-start.4) | collective-permute-done | bytes 884768 | tf_op jit(solution)/shard_map/ppermute | solution.py:265
  100.8 0.3 collective-permute-start.6
  101.2 20.0 %collective-permute-start.1 = (bf16[3,384,384]{2,1,0:T(8,128)(2,1)S(1)}, bf16[3,384,384]{2,1,0:T(8,128)(2,1)S(1)}, u32[]{:S(2)}, u32[]{:S(2)}) collective-permute-start(bf16[3,384,384]{2,1,0:T(8,128)(2,1)S(1)} %collective-permute-done.refs_0_), channel_id=1, source_target_pairs={{0,1},{1,0},{2,3},{3,2},{4,5},{5,4},{6,7},{7,6},{8,9},{9,8},{10,11... | collective-permute-start | bytes 2654216 | tf_op jit(solution)/shard_map/ppermute | solution.py:105
  121.2 0.9 copy-done.4
  122.1 5.2 %collective-permute-done.2.refs_1_ = bf16[3,384,384]{2,1,0:T(8,128)(2,1)} collective-permute-done((bf16[3,384,384]{2,1,0:T(8,128)(2,1)S(1)}, bf16[3,384,384]{2,1,0:T(8,128)(2,1)}, u32[]{:S(2)}, u32[]{:S(2)}) %collective-permute-start.2) | collective-permute-done | bytes 884768 | tf_op jit(solution)/shard_map/ppermute | solution.py:105
  127.3 14.3 %collective-permute-start.3 = (bf16[3,384,384]{2,1,0:T(8,128)(2,1)}, bf16[3,384,384]{2,1,0:T(8,128)(2,1)}, u32[]{:S(2)}, u32[]{:S(2)}) collective-permute-start(bf16[3,384,384]{2,1,0:T(8,128)(2,1)} %collective-permute-done.2.refs_1_), channel_id=1, source_target_pairs={{0,1},{1,0},{2,3},{3,2},{4,5},{5,4},{6,7},{7,6},{8,9},{9,8},{10,11... | collective-permute-start | bytes 2654216 | tf_op jit(solution)/shard_map/ppermute | solution.py:105
  141.6 4.7 %collective-permute-done.6.refs_3_ = bf16[3,384,384]{2,1,0:T(8,128)(2,1)} collective-permute-done((bf16[3,384,384]{2,1,0:T(8,128)(2,1)}, bf16[3,384,384]{2,1,0:T(8,128)(2,1)}, u32[]{:S(2)}, u32[]{:S(2)}) %collective-permute-start.6) | collective-permute-done | bytes 884768 | tf_op jit(solution)/shard_map/ppermute | solution.py:105
  146.2 6.9 %collective-permute-start.7 = (bf16[3,384,384]{2,1,0:T(8,128)(2,1)}, bf16[3,384,384]{2,1,0:T(8,128)(2,1)}, u32[]{:S(2)}, u32[]{:S(2)}) collective-permute-start(bf16[3,384,384]{2,1,0:T(8,128)(2,1)} %collective-permute-done.6.refs_3_), channel_id=1, source_target_pairs={{0,1},{1,0},{2,3},{3,2},{4,5},{5,4},{6,7},{7,6},{8,9},{9,8},{10,11... | collective-permute-start | bytes 2654216 | tf_op jit(solution)/shard_map/ppermute | solution.py:105
  153.2 0.9 copy-done.6
  154.1 0.5 collective-permute-start.11
  154.6 0.1 broadcast_add_fusion
  154.7 1.2 copy-done.5
  155.8 6.3 %shard_map.64.refs_4_ = f32[512,1152]{1,0:T(8,128)S(1)} custom-call(s32[4]{0:T(128)S(1)} %get-tuple-element.14.ids_ref, bf16[512,3072]{1,0:T(8,128)(2,1)} %bitcast.27, bf16[3,384,384]{2,1,0:T(8,128)(2,1)S(1)} %copy-done.5, bf16[3,384,384]{2,1,0:T(8,128)(2,1)} %collective-permute-done.2.refs_1_, bf16[3,384,384]{2,1,0:T(8,128)(2,1)} %collective-permute-done.4.refs_2_, ...), custom_call_target="tpu_custom_call" | custom-call | flops 1811939328 | bytes 9059696 | tf_op jit(solution)/shard_map/pallas_call | solution.py:109
  162.1 1.4 copy-done.1
  163.6 7.9 %shard_map.65 = (bf16[512,384]{1,0:T(8,128)(2,1)S(1)}, bf16[512,768]{1,0:T(8,128)(2,1)}) custom-call(s32[4]{0:T(128)S(1)} %get-tuple-element.13.ids_ref, bf16[512,3072]{1,0:T(8,128)(2,1)} %bitcast.28, bf16[3,384,384]{2,1,0:T(8,128)(2,1)S(1)} %copy-done.7, bf16[3,384,384]{2,1,0:T(8,128)(2,1)} %collective-permute-done.3.refs_1_, ...), custom_call_target="tpu_custom_call" | custom-call | flops 1811939328 | bytes 9059696 | tf_op jit(solution)/shard_map/pallas_call | solution.py:109
  171.5 0.7 copy-done.8
  172.3 0.1 collective-permute-start.8
  172.3 0.1 copy.11
  172.4 0.1 copy.12
  172.5 0.1 add_bitcast_fusion
  172.6 14.4 %all-gather.2 = s32[4,2,6]{2,1,0:T(2,128)S(1)} all-gather(s32[1,2,6]{2,1,0:T(2,128)S(1)} %add_bitcast_fusion), channel_id=1, replica_groups=mesh['groups'=2,'rows'=4,'frames'=2,'heads'=2] {'rows'}, dimensions={0}, use_global_device_ids=true | all-gather | bytes 240 | tf_op jit(solution)/shard_map/all_gather | solution.py:246
  187.0 0.2 slice_reduce_fusion
  187.2 0.1 reshape_squeeze.3
  187.3 0.2 fusion.1
  187.5 0.6 gather_fusion
  188.1 0.1 reshape.15.members_ref
  188.1 0.2 slice_reduce_fusion.1.counts_ref
  188.3 1.0 copy-done.9
  189.3 6.2 %shard_map.66 = bf16[4,128,384]{2,1,0:T(8,128)(2,1)S(1)} custom-call(s32[1]{0:T(128)} %bitcast.5.core_ref, s32[16]{0:T(128)S(1)} %reshape.15.members_ref, s32[4]{0:T(128)S(1)} %slice_reduce_fusion.1.counts_ref, bf16[512,384]{1,0:T(8,128)(2,1)S(1)} %copy-done.9, bf16[512,768]{1,0:T(8,128)(2,1)} %get-tuple-element.10.own_ref, ...), custom_call_target="tpu_custom_call" | custom-call | flops 402653184 | bytes 1572864 | tf_op jit(solution)/shard_map/pallas_call | solution.py:109
  195.6 0.7 copy-done.3
  196.3 4.1 %all-to-all-start = ((bf16[4,128,384]{2,1,0:T(8,128)(2,1)}), bf16[4,128,384]{2,1,0:T(8,128)(2,1)}, u32[]{:S(2)}, u32[]{:S(2)}) async-start(bf16[4,128,384]{2,1,0:T(8,128)(2,1)} %copy-done.3), calls=%async_computation | async-start | bytes 786432 | tf_op jit(solution)/shard_map/all_to_all | solution.py:278
  200.4 0.1 pad_add_fusion.places_ref
  200.5 10.5 %all-to-all-done.a_ref = bf16[4,128,384]{2,1,0:T(8,128)(2,1)} async-done(((bf16[4,128,384]{2,1,0:T(8,128)(2,1)}), bf16[4,128,384]{2,1,0:T(8,128)(2,1)}, u32[]{:S(2)}, u32[]{:S(2)}) %all-to-all-start) | async-done | bytes 393248 | tf_op jit(solution)/shard_map/all_to_all | solution.py:278
  211.0 5.6 %shard_map.67 = (f32[64,3072]{1,0:T(8,128)S(1)}, bf16[64,3072]{1,0:T(8,128)(2,1)S(1)}) custom-call(s32[4]{0:T(128)S(1)} %pad_add_fusion.places_ref, s32[1]{0:T(128)} %bitcast.4.frame_ref, bf16[4,128,384]{2,1,0:T(8,128)(2,1)} %all-to-all-done.a_ref, bf16[4,384,768]{2,1,0:T(8,128)(2,1)S(1)} %bitcast.26, bf16[4,384,768]{2,1,0:T(8,128)(2,1)} %collective-permute-done.9.w1, ...), custom_call_target="tpu_custom_call" | custom-call | flops 1207959552 | bytes 9437184 | tf_op jit(solution)/shard_map/pallas_call | solution.py:109
  216.7 1.5 collective-permute-start.12
  218.2 6.8 %collective-permute-done.12 = bf16[64,3072]{1,0:T(8,128)(2,1)S(1)} collective-permute-done((bf16[64,3072]{1,0:T(8,128)(2,1)S(1)}, bf16[64,3072]{1,0:T(8,128)(2,1)S(1)}, u32[]{:S(2)}, u32[]{:S(2)}) %collective-permute-start.12) | collective-permute-done | bytes 393248 | tf_op jit(solution)/shard_map/ppermute | solution.py:105
  225.0 0.8 fusion
  (33 shorter events, 0.1 us)
Async XLA Ops:
  6.5 1.3 copy-start
  6.5 55.6 %all-gather.8.cloned.1.call-start = ((), (), s32[]{:S(2)}) async-start(), calls=%async_computation.2 | async-start | bytes 2949120 | tf_op jit(solution)/shard_map/all_gather | solution.py:281
  8.7 146.0 %all-gather.6.cloned.1.call-start = ((), (), s32[]{:S(2)}) async-start(), calls=%async_computation.1 | async-start | bytes 3538944 | tf_op jit(solution)/shard_map/all_gather | solution.py:254
  62.1 91.9 %copy-start.2 = (bf16[1536,768]{1,0:T(8,128)(2,1)S(1)}, bf16[1536,768]{1,0:T(8,128)(2,1)}, u32[]{:S(2)}) copy-start(bf16[1536,768]{1,0:T(8,128)(2,1)} %all-gather.8.cloned.1.call-done) | copy-start | bytes 7077892
  62.1 91.9 %collective-permute-start.9 = (bf16[4,384,768]{2,1,0:T(8,128)(2,1)}, bf16[4,384,768]{2,1,0:T(8,128)(2,1)}, u32[]{:S(2)}, u32[]{:S(2)}) collective-permute-start(bf16[4,384,768]{2,1,0:T(8,128)(2,1)} %bitcast.24), channel_id=1, source_target_pairs={{0,16},{16,0},{1,17},{17,1},{2,18},{18,2},{3,19},{19,3},{4,20},{20... | collective-permute-start | bytes 7077896 | tf_op jit(solution)/shard_map/ppermute | solution.py:105
  66.4 0.8 collective-permute-start
  67.1 33.7 %collective-permute-start.4 = (bf16[3,384,384]{2,1,0:T(8,128)(2,1)S(1)}, bf16[3,384,384]{2,1,0:T(8,128)(2,1)}, u32[]{:S(2)}, u32[]{:S(2)}) collective-permute-start(bf16[3,384,384]{2,1,0:T(8,128)(2,1)S(1)} %get-tuple-element.15), channel_id=1, source_target_pairs={{0,4},{1,12},{4,0},{5,8},{8,5},{9,13},{12,1},{13,9},{2,6},{3,14},{... | collective-permute-start | bytes 2654216 | tf_op jit(solution)/shard_map/ppermute | solution.py:265
  67.2 60.1 %collective-permute-start.2 = (bf16[3,384,384]{2,1,0:T(8,128)(2,1)S(1)}, bf16[3,384,384]{2,1,0:T(8,128)(2,1)}, u32[]{:S(2)}, u32[]{:S(2)}) collective-permute-start(bf16[3,384,384]{2,1,0:T(8,128)(2,1)S(1)} %collective-permute-done.refs_0_), channel_id=1, source_target_pairs={{0,16},{16,0},{1,17},{17,1},{2,18},{18,2},{3,19},{19,3},{4,20},{20... | collective-permute-start | bytes 2654216 | tf_op jit(solution)/shard_map/ppermute | solution.py:105
  100.8 45.4 %collective-permute-start.6 = (bf16[3,384,384]{2,1,0:T(8,128)(2,1)}, bf16[3,384,384]{2,1,0:T(8,128)(2,1)}, u32[]{:S(2)}, u32[]{:S(2)}) collective-permute-start(bf16[3,384,384]{2,1,0:T(8,128)(2,1)} %collective-permute-done.4.refs_2_), channel_id=1, source_target_pairs={{0,16},{16,0},{1,17},{17,1},{2,18},{18,2},{3,19},{19,3},{4,20},{20... | collective-permute-start | bytes 2654216 | tf_op jit(solution)/shard_map/ppermute | solution.py:105
  101.2 52.0 %collective-permute-start.1 = (bf16[3,384,384]{2,1,0:T(8,128)(2,1)S(1)}, bf16[3,384,384]{2,1,0:T(8,128)(2,1)S(1)}, u32[]{:S(2)}, u32[]{:S(2)}) collective-permute-start(bf16[3,384,384]{2,1,0:T(8,128)(2,1)S(1)} %collective-permute-done.refs_0_), channel_id=1, source_target_pairs={{0,1},{1,0},{2,3},{3,2},{4,5},{5,4},{6,7},{7,6},{8,9},{9,8},{10,11... | collective-permute-start | bytes 2654216 | tf_op jit(solution)/shard_map/ppermute | solution.py:105
  121.2 0.9 copy-start.4
  122.1 41.4 %collective-permute-start.5 = (bf16[3,384,384]{2,1,0:T(8,128)(2,1)}, bf16[3,384,384]{2,1,0:T(8,128)(2,1)}, u32[]{:S(2)}, u32[]{:S(2)}) collective-permute-start(bf16[3,384,384]{2,1,0:T(8,128)(2,1)} %collective-permute-done.4.refs_2_), channel_id=1, source_target_pairs={{0,1},{1,0},{2,3},{3,2},{4,5},{5,4},{6,7},{7,6},{8,9},{9,8},{10,11... | collective-permute-start | bytes 2654216 | tf_op jit(solution)/shard_map/ppermute | solution.py:105
  127.3 36.2 %collective-permute-start.3 = (bf16[3,384,384]{2,1,0:T(8,128)(2,1)}, bf16[3,384,384]{2,1,0:T(8,128)(2,1)}, u32[]{:S(2)}, u32[]{:S(2)}) collective-permute-start(bf16[3,384,384]{2,1,0:T(8,128)(2,1)} %collective-permute-done.2.refs_1_), channel_id=1, source_target_pairs={{0,1},{1,0},{2,3},{3,2},{4,5},{5,4},{6,7},{7,6},{8,9},{9,8},{10,11... | collective-permute-start | bytes 2654216 | tf_op jit(solution)/shard_map/ppermute | solution.py:105
  146.2 17.3 %collective-permute-start.7 = (bf16[3,384,384]{2,1,0:T(8,128)(2,1)}, bf16[3,384,384]{2,1,0:T(8,128)(2,1)}, u32[]{:S(2)}, u32[]{:S(2)}) collective-permute-start(bf16[3,384,384]{2,1,0:T(8,128)(2,1)} %collective-permute-done.6.refs_3_), channel_id=1, source_target_pairs={{0,1},{1,0},{2,3},{3,2},{4,5},{5,4},{6,7},{7,6},{8,9},{9,8},{10,11... | collective-permute-start | bytes 2654216 | tf_op jit(solution)/shard_map/ppermute | solution.py:105
  153.2 0.9 copy-start.6
  154.1 46.4 %collective-permute-start.10 = (bf16[4,384,768]{2,1,0:T(8,128)(2,1)S(1)}, bf16[4,384,768]{2,1,0:T(8,128)(2,1)}, u32[]{:S(2)}, u32[]{:S(2)}) collective-permute-start(bf16[4,384,768]{2,1,0:T(8,128)(2,1)S(1)} %bitcast.25), channel_id=1, source_target_pairs={{0,1},{1,0},{2,3},{3,2},{4,5},{5,4},{6,7},{7,6},{8,9},{9,8},{10,11... | collective-permute-start | bytes 7077896 | tf_op jit(solution)/shard_map/ppermute | solution.py:105
  154.1 57.0 %collective-permute-start.11 = (bf16[4,384,768]{2,1,0:T(8,128)(2,1)}, bf16[4,384,768]{2,1,0:T(8,128)(2,1)}, u32[]{:S(2)}, u32[]{:S(2)}) collective-permute-start(bf16[4,384,768]{2,1,0:T(8,128)(2,1)} %collective-permute-done.9.w1), channel_id=1, source_target_pairs={{0,1},{1,0},{2,3},{3,2},{4,5},{5,4},{6,7},{7,6},{8,9},{9,8},{10,11... | collective-permute-start | bytes 7077896 | tf_op jit(solution)/shard_map/ppermute | solution.py:105
  154.7 1.2 copy-start.5
  155.8 7.7 %copy-start.7 = (bf16[3,384,384]{2,1,0:T(8,128)(2,1)S(1)}, bf16[3,384,384]{2,1,0:T(8,128)(2,1)}, u32[]{:S(2)}) copy-start(bf16[3,384,384]{2,1,0:T(8,128)(2,1)} %copy-done.6) | copy-start | bytes 2654212
  162.1 1.4 copy-start.1
  163.5 8.8 %copy-start.11 = (s32[2]{0:T(128)S(1)}, s32[2]{0:T(128)}, u32[]{:S(2)}) copy-start(s32[2]{0:T(128)} %param.10) | copy-start | bytes 28
  163.6 8.9 %copy-start.12 = (s32[2]{0:T(128)S(1)}, s32[2]{0:T(128)}, u32[]{:S(2)}) copy-start(s32[2]{0:T(128)} %param.11) | copy-start | bytes 28
  163.6 9.0 %copy-start.10 = (s32[2,4]{1,0:T(2,128)S(1)}, s32[2,4]{1,0:T(2,128)}, u32[]{:S(2)}) copy-start(s32[2,4]{1,0:T(2,128)} %param.9) | copy-start | bytes 100
  171.5 0.7 copy-start.8
  172.3 16.1 %collective-permute-start.8 = (bf16[512,768]{1,0:T(8,128)(2,1)}, bf16[512,768]{1,0:T(8,128)(2,1)}, u32[]{:S(2)}, u32[]{:S(2)}) collective-permute-start(bf16[512,768]{1,0:T(8,128)(2,1)} %get-tuple-element.10.own_ref), channel_id=1, source_target_pairs={{0,1},{1,0},{2,3},{3,2},{4,5},{5,4},{6,7},{7,6},{8,9},{9,8},{10,11... | collective-permute-start | bytes 2359304 | tf_op jit(solution)/shard_map/ppermute | solution.py:105
  188.3 1.0 copy-start.9
  195.6 0.7 copy-start.3
  196.3 14.7 %all-to-all-start = ((bf16[4,128,384]{2,1,0:T(8,128)(2,1)}), bf16[4,128,384]{2,1,0:T(8,128)(2,1)}, u32[]{:S(2)}, u32[]{:S(2)}) async-start(bf16[4,128,384]{2,1,0:T(8,128)(2,1)} %copy-done.3), calls=%async_computation | async-start | bytes 786432 | tf_op jit(solution)/shard_map/all_to_all | solution.py:278
  216.7 8.3 %collective-permute-start.12 = (bf16[64,3072]{1,0:T(8,128)(2,1)S(1)}, bf16[64,3072]{1,0:T(8,128)(2,1)S(1)}, u32[]{:S(2)}, u32[]{:S(2)}) collective-permute-start(bf16[64,3072]{1,0:T(8,128)(2,1)S(1)} %get-tuple-element.12), channel_id=1, source_target_pairs={{0,2},{2,0},{1,3},{3,1},{4,6},{6,4},{5,7},{7,5},{8,10},{10,8},{9,1... | collective-permute-start | bytes 1179656 | tf_op jit(solution)/shard_map/ppermute | solution.py:105
Sparse Core Ops, SparseCore 0:
  8.9 53.1 all-gather.7
  64.3 78.9 all-gather.5

commit v2 on v1

--- a/solution.py
+++ b/solution.py
@@ -121,64 +121,83 @@
     )(*prefetch, *operands)
 
 
-def project_part(tokens, chunk_ids, chunks, total):
-    rows, depth, cols = tokens.shape[0], chunks[0].shape[1], chunks[0].shape[2]
-    last = total is not None
-
-    def kernel(ids_ref, tok_ref, *refs):
+def project(tokens, ids, chunks):
+    peers, frames, count, width = tokens.shape
+    _, depth, cols = chunks[0].shape
+    rows = frames * count
+
+    def kernel(ids_ref, core_ref, tok_ref, *refs):
         w_refs = refs[: len(chunks)]
-        rest = refs[len(chunks) :]
+        q_keep, kv_keep, q_send, kv_send, q_all = refs[len(chunks) :]
         for part in range(3):
-            where = slice(part * cols, (part + 1) * cols)
-            acc = rest[0][:, where] if last else None
+            acc = None
             for i, w_ref in enumerate(w_refs):
                 start = pl.multiple_of(ids_ref[i] * depth, depth)
-                term = jnp.dot(
-                    tok_ref[:, pl.ds(start, depth)], w_ref[part], preferred_element_type=jnp.float32
-                )
+                piece = tok_ref[0, :, :, pl.ds(start, depth)].reshape(rows, depth)
+                term = jnp.dot(piece, w_ref[part], preferred_element_type=jnp.float32)
                 acc = term if acc is None else acc + term
-            if not last:
-                rest[0][:, where] = acc
-            elif part == 0:
-                rest[1][...] = acc.astype(jnp.bfloat16)
+            if part == 0:
+                q_all[...] = acc.reshape(frames, count, cols)
+                own = pl.multiple_of(core_ref[0] * BS, BS)
+                other = pl.multiple_of((1 - core_ref[0]) * BS, BS)
+                q_keep[0] = q_all[:, pl.ds(own, BS), :].reshape(frames * BS, cols)
+                q_send[0] = q_all[:, pl.ds(other, BS), :].reshape(frames * BS, cols).astype(jnp.bfloat16)
             else:
-                rest[2][:, (part - 1) * cols : part * cols] = acc.astype(jnp.bfloat16)
-
-    if last:
-        out_shape = (
-            jax.ShapeDtypeStruct((rows, cols), jnp.bfloat16),
-            jax.ShapeDtypeStruct((rows, 2 * cols), jnp.bfloat16),
-        )
-    else:
-        out_shape = jax.ShapeDtypeStruct((rows, 3 * cols), jnp.float32)
-    operands = [tokens, *chunks] + ([total] if last else [])
-    flops = 2 * rows * depth * len(chunks) * 3 * cols
-    return call(kernel, out_shape, [chunk_ids], operands, flops=flops, read=flops // 200)
-
-
-def attend_all(core, members, counts, queries, own, other, block_len):
-    rows, cols = queries.shape
-    blocks = rows // block_len
-
-    def kernel(core_ref, members_ref, counts_ref, q_ref, own_ref, other_ref, out_ref, kv_ref):
-        kv_ref[0] = own_ref[...].reshape(blocks, block_len, 2 * cols)
-        kv_ref[1] = other_ref[...].reshape(blocks, block_len, 2 * cols)
+                where = slice((part - 1) * cols, part * cols)
+                kv_keep[0, :, :, where] = acc.reshape(frames, count, cols)
+                kv_send[0, :, :, where] = acc.reshape(frames, count, cols).astype(jnp.bfloat16)
+
+    def at_row(*shape):
+        return pl.BlockSpec((1, *shape), lambda i, *_: (i,) + (0,) * len(shape))
+
+    def whole(shape):
+        return pl.BlockSpec(shape, lambda i, *_: (0,) * len(shape))
+
+    q_block, kv_block = (frames * BS, cols), (frames, count, 2 * cols)
+    flops = 2 * peers * rows * width * 3 * cols
+    return pl.pallas_call(
+        kernel,
+        out_shape=(
+            jax.ShapeDtypeStruct((peers, *q_block), jnp.float32),
+            jax.ShapeDtypeStruct((peers, *kv_block), jnp.float32),
+            jax.ShapeDtypeStruct((peers, *q_block), jnp.bfloat16),
+            jax.ShapeDtypeStruct((peers, *kv_block), jnp.bfloat16),
+        ),
+        grid_spec=pltpu.PrefetchScalarGridSpec(
+            num_scalar_prefetch=2,
+            grid=(peers,),
+            in_specs=[at_row(frames, count, width)] + [whole(c.shape) for c in chunks],
+            out_specs=(at_row(*q_block), at_row(*kv_block), at_row(*q_block), at_row(*kv_block)),
+            scratch_shapes=[pltpu.VMEM((frames, count, cols), jnp.float32)],
+        ),
+        compiler_params=pltpu.CompilerParams(vmem_limit_bytes=VMEM_BYTES),
+        cost_estimate=pl.CostEstimate(flops=flops, bytes_accessed=flops // 300, transcendentals=0),
+    )(ids, lax.axis_index("heads").reshape(1), tokens, *chunks)
+
+
+def attend_all(members, counts, queries, keyvals, other_queries, other_keyvals):
+    blocks, block_len, cols = queries.shape
+    frames, count = keyvals.shape[1:3]
+    per_row = count // BS
+
+    def kernel(members_ref, counts_ref, q_ref, kv_ref, q_more, kv_more, out_ref, q_sum, kv_sum):
+        q_sum[...] = (q_ref[...] + q_more[...].astype(jnp.float32)).astype(jnp.bfloat16)
+        for r in range(blocks):
+            both = (kv_ref[r] + kv_more[r].astype(jnp.float32)).astype(jnp.bfloat16)
+            for j in range(per_row):
+                part = both[:, j * BS : (j + 1) * BS, :]
+                kv_sum[r * per_row + j] = part.reshape(block_len, 2 * cols)
         column = lax.broadcasted_iota(jnp.int32, (block_len, MAXB * block_len), 1)
         for b in range(blocks):
             live = column < counts_ref[b] * block_len
-            listed = []
-            for j in range(MAXB):
-                member = members_ref[b * MAXB + j]
-                side = (member + core_ref[0]) % 2
-                listed.append(kv_ref[side, member // 2])
-            q_rows = q_ref[b * block_len : (b + 1) * block_len, :]
+            listed = [kv_sum.at[members_ref[b * MAXB + j]] for j in range(MAXB)]
             for h in range(cols // HD):
                 at = slice(h * HD, (h + 1) * HD)
                 at_v = slice(cols + h * HD, cols + (h + 1) * HD)
                 keys = jnp.concatenate([block[:, at] for block in listed], axis=0)
                 values = jnp.concatenate([block[:, at_v] for block in listed], axis=0)
                 scores = lax.dot_general(
-                    q_rows[:, at], keys, (((1,), (1,)), ((), ())), preferred_element_type=jnp.float32
+                    q_sum[b, :, at], keys, (((1,), (1,)), ((), ())), preferred_element_type=jnp.float32
                 )
                 scores = jnp.where(live, scores, -jnp.inf)
                 raised = jnp.exp2((scores - jnp.max(scores, axis=-1, keepdims=True)) * EXP2_SCALE)
@@ -191,11 +210,14 @@
     return call(
         kernel,
         jax.ShapeDtypeStruct((blocks, block_len, cols), jnp.bfloat16),
-        [core, members, counts],
-        [queries, own, other],
-        scratch=[pltpu.VMEM((2, blocks, block_len, 2 * cols), jnp.bfloat16)],
-        flops=4 * rows * MAXB * block_len * cols,
-        read=8 * rows * cols,
+        [members, counts],
+        [queries, keyvals, other_queries, other_keyvals],
+        scratch=[
+            pltpu.VMEM((blocks, block_len, cols), jnp.bfloat16),
+            pltpu.VMEM((blocks * per_row, block_len, 2 * cols), jnp.bfloat16),
+        ],
+        flops=4 * blocks * block_len * MAXB * block_len * cols,
+        read=16 * blocks * block_len * cols,
     )
 
 
@@ -235,23 +257,11 @@
     rows_n, heads_n = lax.axis_size("rows"), lax.axis_size("heads")
     group, row = lax.axis_index("groups"), lax.axis_index("rows")
     frame, core = lax.axis_index("frames"), lax.axis_index("heads")
-    model_width = latents.shape[2]
+    _, count, model_width = latents.shape
     depth, _, local_cols = w_qkv.shape
-    block_len = 2 * BS
     span = rows_n // heads_n
     cols = local_cols // span
     half = depth // 2
-
-    tables = jnp.concatenate([win_blocks, win_counts[:, None], block_window[:, None]], axis=1)
-    tables = lax.all_gather(tables, "rows", axis=0, tiled=True)
-    windows = lax.dynamic_index_in_dim(
-        tables[:, MAXB + 1].reshape(rows_n, heads_n), core, axis=1, keepdims=False
-    )
-    picked = tables[windows]
-    members, counts = picked[:, :MAXB].reshape(-1), picked[:, MAXB]
-
-    mine = lax.dynamic_slice_in_dim(latents[0], core * BS, BS, axis=0)
-    tokens = lax.all_gather(mine, ("rows", "frames"), axis=0, tiled=True)
 
     w_half = lax.dynamic_slice_in_dim(w_qkv.transpose(1, 0, 2), group * half, half, axis=1)
     chunks, ids = [], []
@@ -263,21 +273,34 @@
         ]
         piece = lax.dynamic_slice_in_dim(w_half, (k + row) % span * cols, cols, axis=2)
         here = lax.ppermute(piece, ("rows", "heads"), pairs)
-        there = swap(here, "groups")
-        chunks += [here, there]
-        source = core * span + (row - k) % span
+        chunks += [here, swap(here, "groups")]
+        source = (row - k) % span
         ids += [2 * source + group, 2 * source + 1 - group]
-    ids = jnp.stack(ids).astype(jnp.int32)
-    other_ids = (ids + (1 - 2 * core) * 2 * span).astype(jnp.int32)
-    total = project_part(tokens, ids, chunks, None)
-    queries, keyvals = project_part(tokens, other_ids, [swap(c, "heads") for c in chunks], total)
-
+
+    mine = lax.dynamic_slice_in_dim(latents[0], core * span * depth, span * depth, axis=1)
+    tokens = lax.all_gather(mine, ("rows", "frames"), axis=0)
+    tokens = tokens.reshape(rows_n, 2, count, span * depth)
+
+    tables = jnp.concatenate([win_blocks, win_counts[:, None], block_window[:, None]], axis=1)
+    found = [tables]
+    for step in range(1, rows_n):
+        found.append(lax.ppermute(tables, "rows", [(r, (r + step) % rows_n) for r in range(rows_n)]))
+    places = (row - jnp.arange(rows_n)) % rows_n
+    tables = jnp.stack(found)[places].reshape(rows_n * heads_n, MAXB + 2)
+    windows = lax.dynamic_index_in_dim(
+        tables[:, MAXB + 1].reshape(rows_n, heads_n), core, axis=1, keepdims=False
+    )
+    picked = tables[windows]
+    members, counts = picked[:, :MAXB].reshape(-1), picked[:, MAXB]
+
+    partial = project(tokens, jnp.stack(ids).astype(jnp.int32), chunks)
     attended = attend_all(
-        core.reshape(1), members, counts, queries, keyvals, swap(keyvals, "heads"), block_len
+        members, counts, *partial[:2], swap(partial[2], "heads"), swap(partial[3], "heads")
     )
     attended = lax.all_to_all(attended, "rows", 0, 0, tiled=True)
 
     out_half = lax.dynamic_slice_in_dim(w_out, group * cols, cols, axis=0)
+    out_half, _, _ = lax.optimization_barrier((out_half, tokens, chunks[-2]))
     out_here = lax.all_gather(out_half, "rows", axis=0).reshape(rows_n, cols, w_out.shape[1])
     out_there = swap(out_here, "groups")
     first = core * span

time: 233 us -> 300 us (1.29)
  waiting for transfers between devices: 112 us -> 206 us
  blocking collectives: 14.4 us -> 0 us
  starting transfers between devices: 50.8 us -> 38.8 us
  Pallas kernels: 26 us -> 22.9 us
    ppermute x11 -> x8, waiting for transfers between devices: 16.7 us -> 71.6 us  [swap(): return lax.ppermute(value, axis, [(0, 1), (1, 0)])]
    all_gather x1, waiting for transfers between devices: 0.01 us -> 36.8 us  [by_heads(): tokens = lax.all_gather(mine, ('rows', 'frames'), axis=0)]
    ppermute x11 -> x8, starting transfers between devices: 45.8 us -> 26.5 us  [swap(): return lax.ppermute(value, axis, [(0, 1), (1, 0)])]
    all_gather x1 -> x0, blocking collectives: 14.4 us -> none  [by_heads(): tables = lax.all_gather(tables, 'rows', axis=0, tiled=True)]
    pallas_call x4 -> x2, Pallas kernels: 26 us -> 12.9 us  [call(): pl.pallas_call(kernel, out_shape=out_shape, grid_spec=pltpu.PrefetchScala...]
    pallas_call x0 -> x1, Pallas kernels: none -> 9.93 us  [project(): pl.pallas_call(kernel, out_shape=(jax.ShapeDtypeStruct((peers, *q_block),...]
    ppermute x0 -> x3, waiting for transfers between devices: none -> 4.53 us  [by_heads(): lax.ppermute(tables, 'rows', [(r, (r + step) % rows_n) for r in range(row...]
    ppermute x2, starting transfers between devices: 0.79 us -> 4.82 us  [by_heads(): here = lax.ppermute(piece, ('rows', 'heads'), pairs)]
  transfers between devices with their start and end apart: 16 -> 16, of which waited for: 6 -> 11; matrix products, arithmetic and copies ran while one was open for 3% -> 3% of each run, Pallas kernels for 9% -> 6%
where the time goes in v2:
time: 300 us; the launch traced here: 299 us
  waiting for transfers between devices  206 us (69%)
  starting transfers between devices  38.8 us (13%)
  Pallas kernels  22.9 us (8%)
  local copies, waits for them, and re-layouts  15.4 us (5%)
  between operations  13.5 us (4%)
    ppermute x8, waiting for transfers between devices, swap(): return lax.ppermute(value, axis, [(0, 1), (1, 0)])  71.6 us
    all_gather x1, waiting for transfers between devices, by_heads(): lax.all_gather(out_half, 'rows', axis=0)  50.7 us
    all_gather x1, waiting for transfers between devices, by_heads(): tokens = lax.all_gather(mine, ('rows', 'frames'), axis=0)  36.8 us
    ppermute x2, waiting for transfers between devices, by_heads(): here = lax.ppermute(piece, ('rows', 'heads'), pairs)  31.7 us
    ppermute x8, starting transfers between devices, swap(): return lax.ppermute(value, axis, [(0, 1), (1, 0)])  26.5 us
    pallas_call x2, Pallas kernels, call(): pl.pallas_call(kernel, out_shape=out_shape, grid_spec=pltpu.PrefetchScala...  12.9 us
    all_to_all x1, waiting for transfers between devices, by_heads(): attended = lax.all_to_all(attended, 'rows', 0, 0, tiled=True)  11.1 us
    pallas_call x1, Pallas kernels, project(): pl.pallas_call(kernel, out_shape=(jax.ShapeDtypeStruct((peers, *q_block),...  9.93 us
  transfers between devices with their start and end apart: 16, of which 11 were waited for; matrix products, arithmetic and copies ran while one was open for 3% of the time, Pallas kernels for 6%

profile of v2, /device:TPU:0, one launch (start us, length us, event | category | flops | bytes accessed | tf_op | source)
XLA Modules:
  0.0 299.2 jit_solution(11575958180142139248)
XLA Ops:
  6.5 1.9 constant_dynamic-slice_fusion.1
  8.5 3.7 %dynamic-slice_bitcast_fusion = (bf16[3,384,384]{2,1,0:T(8,128)(2,1)S(1)}, bf16[3,384,384]{2,1,0:T(8,128)(2,1)}) fusion(bf16[768,3,768]{2,0,1:T(8,128)(2,1)} %param.7, s32[]{:T(128)S(6)} %select_n.75, s32[]{:T(128)S(6)} %select_n.80, s32[]{:T(128)S(6)} %select_n.77), kind=kLoop, calls=%fused_computation.2 | loop fusion | bytes 3538956 | tf_op jit(solution)/shard_map/dynamic_slice | solution.py:274
  12.2 3.0 %collective-permute-start.5 = (bf16[3,384,384]{2,1,0:T(8,128)(2,1)S(1)}, bf16[3,384,384]{2,1,0:T(8,128)(2,1)S(1)}, u32[]{:S(2)}, u32[]{:S(2)}) collective-permute-start(bf16[3,384,384]{2,1,0:T(8,128)(2,1)S(1)} %get-tuple-element.19), channel_id=1, source_target_pairs={{0,4},{1,12},{4,0},{5,8},{8,5},{9,13},{12,1},{13,9},{2,6},{3,14},{... | collective-permute-start | bytes 2654216 | tf_op jit(solution)/shard_map/ppermute | solution.py:275
  15.2 0.9 constant_dynamic-slice_fusion
  16.1 31.7 %collective-permute-done.5.refs_2_ = bf16[3,384,384]{2,1,0:T(8,128)(2,1)S(1)} collective-permute-done((bf16[3,384,384]{2,1,0:T(8,128)(2,1)S(1)}, bf16[3,384,384]{2,1,0:T(8,128)(2,1)S(1)}, u32[]{:S(2)}, u32[]{:S(2)}) %collective-permute-start.5) | collective-permute-done | bytes 884768 | tf_op jit(solution)/shard_map/ppermute | solution.py:275
  47.7 36.8 %all-gather.4.cloned.1.call-done = bf16[8,128,1536]{2,1,0:T(8,128)(2,1)} async-done(((bf16[1,128,1536]{2,1,0:T(8,128)(2,1)}), bf16[8,128,1536]{2,1,0:T(8,128)(2,1)}) %all-gather.4.cloned.1.call-update) | async-done | bytes 3145744 | tf_op jit(solution)/shard_map/all_gather | solution.py:281
  84.6 50.7 %all-gather.6.cloned.1.call-done = bf16[1536,768]{1,0:T(8,128)(2,1)} async-done(((bf16[384,768]{1,0:T(8,128)(2,1)}), bf16[1536,768]{1,0:T(8,128)(2,1)}) %all-gather.6.cloned.1.call-update) | async-done | bytes 2359312 | tf_op jit(solution)/shard_map/all_gather | solution.py:304
  135.3 1.5 collective-permute-start.9
  136.8 1.8 collective-permute-start.3
  138.6 0.6 collective-permute-start.4
  139.1 1.5 collective-permute-start.6
  140.7 21.2 %collective-permute-start.10 = (bf16[4,384,768]{2,1,0:T(8,128)(2,1)}, bf16[4,384,768]{2,1,0:T(8,128)(2,1)}, u32[]{:S(2)}, u32[]{:S(2)}) collective-permute-start(bf16[4,384,768]{2,1,0:T(8,128)(2,1)} %bitcast.28), channel_id=1, source_target_pairs={{0,1},{1,0},{2,3},{3,2},{4,5},{5,4},{6,7},{7,6},{8,9},{9,8},{10,11... | collective-permute-start | bytes 7077896 | tf_op jit(solution)/shard_map/ppermute | solution.py:105
  161.9 27.8 %collective-permute-done.9.w1 = bf16[4,384,768]{2,1,0:T(8,128)(2,1)} collective-permute-done((bf16[4,384,768]{2,1,0:T(8,128)(2,1)}, bf16[4,384,768]{2,1,0:T(8,128)(2,1)}, u32[]{:S(2)}, u32[]{:S(2)}) %collective-permute-start.9) | collective-permute-done | bytes 2359328 | tf_op jit(solution)/shard_map/ppermute | solution.py:105
  189.8 19.0 %collective-permute-done.4.refs_1_ = bf16[3,384,384]{2,1,0:T(8,128)(2,1)} collective-permute-done((bf16[3,384,384]{2,1,0:T(8,128)(2,1)S(1)}, bf16[3,384,384]{2,1,0:T(8,128)(2,1)}, u32[]{:S(2)}, u32[]{:S(2)}) %collective-permute-start.4) | collective-permute-done | bytes 884768 | tf_op jit(solution)/shard_map/ppermute | solution.py:105
  208.7 17.8 %collective-permute-done.6.refs_3_ = bf16[3,384,384]{2,1,0:T(8,128)(2,1)} collective-permute-done((bf16[3,384,384]{2,1,0:T(8,128)(2,1)S(1)}, bf16[3,384,384]{2,1,0:T(8,128)(2,1)}, u32[]{:S(2)}, u32[]{:S(2)}) %collective-permute-start.6) | collective-permute-done | bytes 884768 | tf_op jit(solution)/shard_map/ppermute | solution.py:105
  226.5 9.9 %shard_map.64 = (f32[4,128,384]{2,1,0:T(8,128)S(1)}, f32[4,2,128,768]{3,2,1,0:T(8,128)}, bf16[4,128,384]{2,1,0:T(8,128)(2,1)S(1)}, bf16[4,2,128,768]{3,2,1,0:T(8,128)(2,1)}) custom-call(s32[4]{0:T(128)S(1)} %pad_add_fusion.3.ids_ref, s32[1]{0:T(128)} %bitcast.16.core_ref, bf16[4,2,128,1536]{3,2,1,0:T(8,128)(2,1)} %bitcast.35, ...), custom_call_target="tpu_custom_call" | custom-call | flops 3623878656 | bytes 12079595 | tf_op jit(solution)/shard_map/pallas_call | solution.py:158
  236.4 0.9 copy-done.5
  237.3 0.1 copy.11
  237.4 0.1 copy.12
  237.6 1.2 collective-permute-start.2
  238.8 0.9 collective-permute-start
  239.6 0.1 fusion.2
  239.8 1.3 collective-permute-done.2
  241.2 1.3 collective-permute-start.1
  242.4 1.8 collective-permute-done
  244.2 1.4 collective-permute-done.1
  245.6 0.7 pad_add_fusion
  246.3 0.6 gather_fusion
  246.9 0.2 slice_reduce_fusion
  247.1 0.1 reshape_squeeze.3
  247.2 0.2 fusion.3
  247.4 0.6 gather_fusion.1
  247.9 0.1 reshape.71.members_ref
  248.0 0.2 slice_reduce_fusion.1.counts_ref
  248.2 0.7 copy-done.7
  248.9 1.2 copy-done.2
  250.1 1.4 copy-done.3
  251.5 1.1 copy-done.6
  252.6 1.0 copy-done.8
  253.6 7.3 %shard_map.65 = bf16[4,128,384]{2,1,0:T(8,128)(2,1)S(1)} custom-call(s32[16]{0:T(128)S(1)} %reshape.71.members_ref, s32[4]{0:T(128)S(1)} %slice_reduce_fusion.1.counts_ref, f32[4,128,384]{2,1,0:T(8,128)S(1)} %copy-done.6, f32[4,2,128,768]{3,2,1,0:T(8,128)} %get-tuple-element.13.kv_ref, bf16[4,128,384]{2,1,0:T(8,128)(2,1)S(1)} %copy-done.8, ...), custom_call_target="tpu_custom_call" | custom-call | flops 402653184 | bytes 3145728 | tf_op jit(solution)/shard_map/pallas_call | solution.py:109
  261.0 0.7 copy-done.4
  261.7 4.2 %all-to-all-start = ((bf16[4,128,384]{2,1,0:T(8,128)(2,1)}), bf16[4,128,384]{2,1,0:T(8,128)(2,1)}, u32[]{:S(2)}, u32[]{:S(2)}) async-start(bf16[4,128,384]{2,1,0:T(8,128)(2,1)} %copy-done.4), calls=%async_computation | async-start | bytes 786432 | tf_op jit(solution)/shard_map/all_to_all | solution.py:300
  265.9 0.1 pad_add_fusion.2.places_ref
  266.0 11.1 %all-to-all-done.a_ref = bf16[4,128,384]{2,1,0:T(8,128)(2,1)} async-done(((bf16[4,128,384]{2,1,0:T(8,128)(2,1)}), bf16[4,128,384]{2,1,0:T(8,128)(2,1)}, u32[]{:S(2)}, u32[]{:S(2)}) %all-to-all-start) | async-done | bytes 393248 | tf_op jit(solution)/shard_map/all_to_all | solution.py:300
  277.1 5.6 %shard_map.66 = (f32[64,3072]{1,0:T(8,128)S(1)}, bf16[64,3072]{1,0:T(8,128)(2,1)S(1)}) custom-call(s32[4]{0:T(128)S(1)} %pad_add_fusion.2.places_ref, s32[1]{0:T(128)} %bitcast.4.frame_ref, bf16[4,128,384]{2,1,0:T(8,128)(2,1)} %all-to-all-done.a_ref, bf16[4,384,768]{2,1,0:T(8,128)(2,1)S(1)} %bitcast.29, bf16[4,384,768]{2,1,0:T(8,128)(2,1)} %collective-permute-done.9.w1, ...), custom_call_target="tpu_custom_call" | custom-call | flops 1207959552 | bytes 9437184 | tf_op jit(solution)/shard_map/pallas_call | solution.py:109
  282.7 1.8 collective-permute-start.12
  284.5 7.0 %collective-permute-done.12 = bf16[64,3072]{1,0:T(8,128)(2,1)S(1)} collective-permute-done((bf16[64,3072]{1,0:T(8,128)(2,1)S(1)}, bf16[64,3072]{1,0:T(8,128)(2,1)S(1)}, u32[]{:S(2)}, u32[]{:S(2)}) %collective-permute-start.12) | collective-permute-done | bytes 393248 | tf_op jit(solution)/shard_map/ppermute | solution.py:105
  291.5 0.8 fusion
  (34 shorter events, 0.4 us)
Async XLA Ops:
  6.5 8.7 %copy-start = (bf16[768,768]{1,0:T(8,128)(2,1)S(1)}, bf16[768,768]{1,0:T(8,128)(2,1)}, u32[]{:S(2)}) copy-start(bf16[768,768]{1,0:T(8,128)(2,1)} %param.8) | copy-start | bytes 3538948
  6.5 78.1 %all-gather.4.cloned.1.call-start = ((), (), s32[]{:S(2)}) async-start(), calls=%async_computation.1 | async-start | bytes 3538944 | tf_op jit(solution)/shard_map/all_gather | solution.py:281
  8.4 126.9 %all-gather.6.cloned.1.call-start = ((), (), s32[]{:S(2)}) async-start(), calls=%async_computation.2 | async-start | bytes 2949120 | tf_op jit(solution)/shard_map/all_gather | solution.py:304
  12.2 35.5 %collective-permute-start.5 = (bf16[3,384,384]{2,1,0:T(8,128)(2,1)S(1)}, bf16[3,384,384]{2,1,0:T(8,128)(2,1)S(1)}, u32[]{:S(2)}, u32[]{:S(2)}) collective-permute-start(bf16[3,384,384]{2,1,0:T(8,128)(2,1)S(1)} %get-tuple-element.19), channel_id=1, source_target_pairs={{0,4},{1,12},{4,0},{5,8},{8,5},{9,13},{12,1},{13,9},{2,6},{3,14},{... | collective-permute-start | bytes 2654216 | tf_op jit(solution)/shard_map/ppermute | solution.py:275
  135.3 54.5 %collective-permute-start.9 = (bf16[4,384,768]{2,1,0:T(8,128)(2,1)}, bf16[4,384,768]{2,1,0:T(8,128)(2,1)}, u32[]{:S(2)}, u32[]{:S(2)}) collective-permute-start(bf16[4,384,768]{2,1,0:T(8,128)(2,1)} %bitcast.27), channel_id=1, source_target_pairs={{0,16},{16,0},{1,17},{17,1},{2,18},{18,2},{3,19},{19,3},{4,20},{20... | collective-permute-start | bytes 7077896 | tf_op jit(solution)/shard_map/ppermute | solution.py:105
  136.8 1.8 collective-permute-start.3
  138.6 70.1 %collective-permute-start.4 = (bf16[3,384,384]{2,1,0:T(8,128)(2,1)S(1)}, bf16[3,384,384]{2,1,0:T(8,128)(2,1)}, u32[]{:S(2)}, u32[]{:S(2)}) collective-permute-start(bf16[3,384,384]{2,1,0:T(8,128)(2,1)S(1)} %collective-permute-done.3.refs_0_), channel_id=1, source_target_pairs={{0,16},{16,0},{1,17},{17,1},{2,18},{18,2},{3,19},{19,3},{4,20},{20... | collective-permute-start | bytes 2654216 | tf_op jit(solution)/shard_map/ppermute | solution.py:105
  139.1 87.3 %collective-permute-start.6 = (bf16[3,384,384]{2,1,0:T(8,128)(2,1)S(1)}, bf16[3,384,384]{2,1,0:T(8,128)(2,1)}, u32[]{:S(2)}, u32[]{:S(2)}) collective-permute-start(bf16[3,384,384]{2,1,0:T(8,128)(2,1)S(1)} %collective-permute-done.5.refs_2_), channel_id=1, source_target_pairs={{0,16},{16,0},{1,17},{17,1},{2,18},{18,2},{3,19},{19,3},{4,20},{20... | collective-permute-start | bytes 2654216 | tf_op jit(solution)/shard_map/ppermute | solution.py:105
  140.7 136.4 %collective-permute-start.10 = (bf16[4,384,768]{2,1,0:T(8,128)(2,1)}, bf16[4,384,768]{2,1,0:T(8,128)(2,1)}, u32[]{:S(2)}, u32[]{:S(2)}) collective-permute-start(bf16[4,384,768]{2,1,0:T(8,128)(2,1)} %bitcast.28), channel_id=1, source_target_pairs={{0,1},{1,0},{2,3},{3,2},{4,5},{5,4},{6,7},{7,6},{8,9},{9,8},{10,11... | collective-permute-start | bytes 7077896 | tf_op jit(solution)/shard_map/ppermute | solution.py:105
  189.8 87.3 %collective-permute-start.11 = (bf16[4,384,768]{2,1,0:T(8,128)(2,1)}, bf16[4,384,768]{2,1,0:T(8,128)(2,1)}, u32[]{:S(2)}, u32[]{:S(2)}) collective-permute-start(bf16[4,384,768]{2,1,0:T(8,128)(2,1)} %collective-permute-done.9.w1), channel_id=1, source_target_pairs={{0,1},{1,0},{2,3},{3,2},{4,5},{5,4},{6,7},{7,6},{8,9},{9,8},{10,11... | collective-permute-start | bytes 7077896 | tf_op jit(solution)/shard_map/ppermute | solution.py:105
  226.5 10.8 %copy-start.10 = (s32[2]{0:T(128)S(1)}, s32[2]{0:T(128)}, u32[]{:S(2)}) copy-start(s32[2]{0:T(128)} %param.10) | copy-start | bytes 28
  226.5 10.9 %copy-start.11 = (s32[2]{0:T(128)S(1)}, s32[2]{0:T(128)}, u32[]{:S(2)}) copy-start(s32[2]{0:T(128)} %param.11) | copy-start | bytes 28
  226.5 11.0 %copy-start.9 = (s32[2,4]{1,0:T(2,128)S(1)}, s32[2,4]{1,0:T(2,128)}, u32[]{:S(2)}) copy-start(s32[2,4]{1,0:T(2,128)} %param.9) | copy-start | bytes 100
  236.4 0.9 copy-start.5
  237.3 11.6 %collective-permute-start.8 = (bf16[4,2,128,768]{3,2,1,0:T(8,128)(2,1)}, bf16[4,2,128,768]{3,2,1,0:T(8,128)(2,1)S(1)}, u32[]{:S(2)}, u32[]{:S(2)}) collective-permute-start(bf16[4,2,128,768]{3,2,1,0:T(8,128)(2,1)} %get-tuple-element.15), channel_id=1, source_target_pairs={{0,1},{1,0},{2,3},{3,2},{4,5},{5,4},{6,7},{7,6},{8,9},{9,8},{10,11... | collective-permute-start | bytes 4718600 | tf_op jit(solution)/shard_map/ppermute | solution.py:105
  237.6 3.6 %collective-permute-start.2 = (s32[2,6]{1,0:T(2,128)S(1)}, s32[2,6]{1,0:T(2,128)S(1)}, u32[]{:S(2)}, u32[]{:S(2)}) collective-permute-start(s32[2,6]{1,0:T(2,128)S(1)} %pad_add_fusion.1), channel_id=1, source_target_pairs={{0,12},{4,0},{8,4},{12,8},{1,13},{5,1},{9,5},{13,9},{2,14},{6,2},{... | collective-permute-start | bytes 152 | tf_op jit(solution)/shard_map/ppermute | solution.py:287
  238.8 5.5 %collective-permute-start = (s32[2,6]{1,0:T(2,128)S(1)}, s32[2,6]{1,0:T(2,128)}, u32[]{:S(2)}, u32[]{:S(2)}) collective-permute-start(s32[2,6]{1,0:T(2,128)S(1)} %pad_add_fusion.1), channel_id=1, source_target_pairs={{0,4},{4,8},{8,12},{12,0},{1,5},{5,9},{9,13},{13,1},{2,6},{6,10},{... | collective-permute-start | bytes 152 | tf_op jit(solution)/shard_map/ppermute | solution.py:287
  241.2 4.5 %collective-permute-start.1 = (s32[2,6]{1,0:T(2,128)S(1)}, s32[2,6]{1,0:T(2,128)S(1)}, u32[]{:S(2)}, u32[]{:S(2)}) collective-permute-start(s32[2,6]{1,0:T(2,128)S(1)} %pad_add_fusion.1), channel_id=1, source_target_pairs={{0,8},{4,12},{8,0},{12,4},{1,9},{5,13},{9,1},{13,5},{2,10},{6,14},... | collective-permute-start | bytes 152 | tf_op jit(solution)/shard_map/ppermute | solution.py:287
  244.2 4.0 %collective-permute-start.7 = (bf16[4,128,384]{2,1,0:T(8,128)(2,1)S(1)}, bf16[4,128,384]{2,1,0:T(8,128)(2,1)S(1)}, u32[]{:S(2)}, u32[]{:S(2)}) collective-permute-start(bf16[4,128,384]{2,1,0:T(8,128)(2,1)S(1)} %get-tuple-element.14), channel_id=1, source_target_pairs={{0,1},{1,0},{2,3},{3,2},{4,5},{5,4},{6,7},{7,6},{8,9},{9,8},{10,11... | collective-permute-start | bytes 1179656 | tf_op jit(solution)/shard_map/ppermute | solution.py:105
  248.2 0.7 copy-start.7
  248.9 1.2 copy-start.2
  250.1 1.4 copy-start.3
  251.5 1.1 copy-start.6
  252.6 1.0 copy-start.8
  253.6 23.5 %copy-start.1 = (bf16[1536,768]{1,0:T(8,128)(2,1)S(1)}, bf16[1536,768]{1,0:T(8,128)(2,1)}, u32[]{:S(2)}) copy-start(bf16[1536,768]{1,0:T(8,128)(2,1)} %all-gather.6.cloned.1.call-done) | copy-start | bytes 7077892
  261.0 0.7 copy-start.4
  261.7 15.4 %all-to-all-start = ((bf16[4,128,384]{2,1,0:T(8,128)(2,1)}), bf16[4,128,384]{2,1,0:T(8,128)(2,1)}, u32[]{:S(2)}, u32[]{:S(2)}) async-start(bf16[4,128,384]{2,1,0:T(8,128)(2,1)} %copy-done.4), calls=%async_computation | async-start | bytes 786432 | tf_op jit(solution)/shard_map/all_to_all | solution.py:300
  282.7 8.8 %collective-permute-start.12 = (bf16[64,3072]{1,0:T(8,128)(2,1)S(1)}, bf16[64,3072]{1,0:T(8,128)(2,1)S(1)}, u32[]{:S(2)}, u32[]{:S(2)}) collective-permute-start(bf16[64,3072]{1,0:T(8,128)(2,1)S(1)} %get-tuple-element.18), channel_id=1, source_target_pairs={{0,2},{2,0},{1,3},{3,1},{4,6},{6,4},{5,7},{7,5},{8,10},{10,8},{9,1... | collective-permute-start | bytes 1179656 | tf_op jit(solution)/shard_map/ppermute | solution.py:105
Sparse Core Ops, SparseCore 0:
  9.5 75.0 all-gather.3
  86.2 49.1 all-gather.5

commit v3 on v0

--- a/solution.py
+++ b/solution.py
@@ -3,11 +3,15 @@
 import jax
 import jax.numpy as jnp
 from jax import lax
+from jax.experimental import pallas as pl
+from jax.experimental.pallas import tpu as pltpu
 from jax.sharding import PartitionSpec as P
 
 HD = 128
 BS = 64
 MAXB = 4
+VMEM_BYTES = 48 * 1024 * 1024
+EXP2_SCALE = math.log2(math.e) / math.sqrt(HD)
 
 
 def with_halo(value, sides, width):
@@ -23,7 +27,7 @@
     return value
 
 
-def local(latents, w_qkv, w_out, win_blocks, win_counts, block_window):
+def by_tokens(latents, w_qkv, w_out, win_blocks, win_counts, block_window):
     rows_n = lax.axis_size("rows")
     shard_idx = lax.axis_index("rows")
     frames = latents.shape[0] * lax.axis_size("frames")
@@ -97,6 +101,294 @@
     return summed.reshape(1, out_rows, model_width)
 
 
+def swap(value, axis, step=1):
+    peers = lax.axis_size(axis)
+    return lax.ppermute(value, axis, [(i, i ^ step) for i in range(peers)])
+
+
+def after(value, *others):
+    return lax.optimization_barrier((value, *others))[0]
+
+
+def call(kernel, out_shape, prefetch, operands, scratch=(), flops=0, read=0):
+    return pl.pallas_call(
+        kernel,
+        out_shape=out_shape,
+        grid_spec=pltpu.PrefetchScalarGridSpec(
+            num_scalar_prefetch=len(prefetch),
+            grid=(),
+            in_specs=[pl.BlockSpec(memory_space=pltpu.VMEM)] * len(operands),
+            out_specs=jax.tree.map(lambda _: pl.BlockSpec(memory_space=pltpu.VMEM), out_shape),
+            scratch_shapes=scratch,
+        ),
+        compiler_params=pltpu.CompilerParams(vmem_limit_bytes=VMEM_BYTES),
+        cost_estimate=pl.CostEstimate(flops=flops, bytes_accessed=read, transcendentals=0),
+    )(*prefetch, *operands)
+
+
+def project(place, mine, theirs, chunks):
+    peers, count, depth = mine[0].shape
+    slices = len(mine)
+    half, cols = chunks[0][0][0].shape
+    flat = [w for of_round in chunks for of_part in of_round for w in of_part]
+
+    def kernel(place_ref, *refs):
+        row, group, frame, core = (place_ref[i] for i in range(4))
+        x_refs, w_refs = refs[: 2 * slices], refs[2 * slices : 2 * slices + len(flat)]
+        q_keep, kv_keep, send, x_all, q_all = refs[2 * slices + len(flat) :]
+        for c in range(slices):
+            x_all[c, frame] = x_refs[c][0]
+            x_all[c, 1 - frame] = x_refs[slices + c][0]
+        for part in range(3):
+            acc = None
+            for k in range(slices):
+                at = (row + slices - k) % slices
+                for g in range(2):
+                    start = pl.multiple_of((group + g) % 2 * half, half)
+                    piece = x_all[at, :, :, pl.ds(start, half)].reshape(2 * count, half)
+                    w_ref = w_refs[(k * 3 + part) * 2 + g]
+                    term = jnp.dot(piece, w_ref[...], preferred_element_type=jnp.float32)
+                    acc = term if acc is None else acc + term
+            if part == 0:
+                q_all[...] = acc.reshape(2, count, cols)
+                own = pl.multiple_of(core * BS, BS)
+                other = pl.multiple_of((1 - core) * BS, BS)
+                q_keep[0] = q_all[:, pl.ds(own, BS), :].reshape(2 * BS, cols)
+                for f in range(2):
+                    send[0, 2 * count :, f * cols : (f + 1) * cols] = q_all[f, pl.ds(other, BS), :].astype(
+                        jnp.bfloat16
+                    )
+            else:
+                where = slice((part - 1) * cols, part * cols)
+                kv_keep[0, :, where] = acc
+                send[0, : 2 * count, where] = acc.astype(jnp.bfloat16)
+
+    def at_row(*shape):
+        return pl.BlockSpec((1, *shape), lambda i, *_: (i,) + (0,) * len(shape))
+
+    def whole(shape):
+        return pl.BlockSpec(shape, lambda i, *_: (0,) * len(shape))
+
+    shapes = ((2 * BS, cols), (2 * count, 2 * cols), (2 * count + BS, 2 * cols))
+    flops = 2 * peers * 2 * count * slices * depth * 3 * cols
+    return pl.pallas_call(
+        kernel,
+        out_shape=(
+            jax.ShapeDtypeStruct((peers, *shapes[0]), jnp.float32),
+            jax.ShapeDtypeStruct((peers, *shapes[1]), jnp.float32),
+            jax.ShapeDtypeStruct((peers, *shapes[2]), jnp.bfloat16),
+        ),
+        grid_spec=pltpu.PrefetchScalarGridSpec(
+            num_scalar_prefetch=1,
+            grid=(peers,),
+            in_specs=[at_row(count, depth)] * (2 * slices) + [whole(w.shape) for w in flat],
+            out_specs=tuple(at_row(*shape) for shape in shapes),
+            scratch_shapes=[
+                pltpu.VMEM((slices, 2, count, depth), jnp.bfloat16),
+                pltpu.VMEM((2, count, cols), jnp.float32),
+            ],
+        ),
+        compiler_params=pltpu.CompilerParams(vmem_limit_bytes=VMEM_BYTES),
+        cost_estimate=pl.CostEstimate(flops=flops, bytes_accessed=flops // 300, transcendentals=0),
+    )(place, *mine, *theirs, *flat)
+
+
+def attend_all(place, members, counts, queries, keyvals, more):
+    blocks, block_len, cols = queries.shape
+    rows = keyvals.shape[1]
+    per_row = rows // block_len
+
+    def kernel(place_ref, members_ref, counts_ref, q_ref, kv_ref, more_ref, same_ref, diff_ref, q_sum, kv_sum, out):
+        for r in range(blocks):
+            added = more_ref[r, rows:, :].astype(jnp.float32)
+            added = jnp.concatenate([added[:, :cols], added[:, cols:]], axis=0)
+            q_sum[r] = (q_ref[r] + added).astype(jnp.bfloat16)
+            both = (kv_ref[r] + more_ref[r, :rows, :].astype(jnp.float32)).astype(jnp.bfloat16)
+            both = both.reshape(2, rows // 2, 2 * cols)
+            for j in range(per_row):
+                part = both[:, j * BS : (j + 1) * BS, :]
+                kv_sum[r * per_row + j] = part.reshape(block_len, 2 * cols)
+        column = lax.broadcasted_iota(jnp.int32, (block_len, MAXB * block_len), 1)
+        for b in range(blocks):
+            live = column < counts_ref[b] * block_len
+            listed = [kv_sum.at[members_ref[b * MAXB + j]] for j in range(MAXB)]
+            for h in range(cols // HD):
+                at = slice(h * HD, (h + 1) * HD)
+                at_v = slice(cols + h * HD, cols + (h + 1) * HD)
+                keys = jnp.concatenate([block[:, at] for block in listed], axis=0)
+                values = jnp.concatenate([block[:, at_v] for block in listed], axis=0)
+                scores = lax.dot_general(
+                    q_sum[b, :, at], keys, (((1,), (1,)), ((), ())), preferred_element_type=jnp.float32
+                )
+                scores = jnp.where(live, scores, -jnp.inf)
+                raised = jnp.exp2((scores - jnp.max(scores, axis=-1, keepdims=True)) * EXP2_SCALE)
+                weights = raised * (1.0 / jnp.sum(raised, axis=-1, keepdims=True))
+                blended = jnp.dot(
+                    weights.astype(jnp.bfloat16), values, preferred_element_type=jnp.float32
+                )
+                out[(b + place_ref[0]) % 2, b // 2, :, at] = blended.astype(jnp.bfloat16)
+        same_ref[...] = out[0]
+        diff_ref[...] = out[1]
+
+    half = jax.ShapeDtypeStruct((blocks // 2, block_len, cols), jnp.bfloat16)
+    return call(
+        kernel,
+        (half, half),
+        [place, members, counts],
+        [queries, keyvals, more],
+        scratch=[
+            pltpu.VMEM((blocks, block_len, cols), jnp.bfloat16),
+            pltpu.VMEM((blocks * per_row, block_len, 2 * cols), jnp.bfloat16),
+            pltpu.VMEM((2, blocks // 2, block_len, cols), jnp.bfloat16),
+        ],
+        flops=4 * blocks * block_len * MAXB * block_len * cols,
+        read=16 * blocks * block_len * cols,
+    )
+
+
+def mix(place, attended, w_parts):
+    blocks, block_len, cols = attended[0].shape
+    width = w_parts[0].shape[1]
+
+    def kernel(place_ref, *refs):
+        row, _, frame, core = (place_ref[i] for i in range(4))
+        a_refs, w_refs = refs[:4], refs[4:8]
+        keep, over_x, over_z, over_both, a_all, sums = refs[8:]
+        for s in range(4):
+            a_all[s] = a_refs[s][...].reshape(blocks * block_len, cols)
+
+        def term(w_ref, side):
+            first = a_all[(2 * side) ^ row]
+            second = a_all[(2 * side + 1) ^ row]
+            acc = jnp.dot(first, w_ref[:cols], preferred_element_type=jnp.float32)
+            acc = acc + jnp.dot(second, w_ref[cols:], preferred_element_type=jnp.float32)
+            return acc.astype(jnp.bfloat16).astype(jnp.float32)
+
+        for c in range(2):
+            total = term(w_refs[c], core) + term(w_refs[2 + c], 1 - core)
+            sums[...] = total.reshape(blocks, 2, BS, width)
+            at = (row + c) % 2
+            keep[at] = sums[row // 2, frame]
+            over_x[at] = sums[row // 2, 1 - frame].astype(jnp.bfloat16)
+            over_z[at] = sums[1 - row // 2, frame].astype(jnp.bfloat16)
+            over_both[at] = sums[1 - row // 2, 1 - frame].astype(jnp.bfloat16)
+
+    shape = (2, BS, width)
+    sent = jax.ShapeDtypeStruct(shape, jnp.bfloat16)
+    return call(
+        kernel,
+        (jax.ShapeDtypeStruct(shape, jnp.float32), sent, sent, sent),
+        [place],
+        [*attended, *w_parts],
+        scratch=[
+            pltpu.VMEM((4, blocks * block_len, cols), jnp.bfloat16),
+            pltpu.VMEM((blocks, 2, BS, width), jnp.float32),
+        ],
+        flops=2 * blocks * block_len * 4 * cols * 2 * width,
+        read=16 * cols * width,
+    )
+
+
+def finish(place, keep, from_x, from_z, from_both):
+    halves, rows, width = keep.shape
+
+    def kernel(place_ref, keep_ref, x_ref, z_ref, both_ref, out_ref):
+        pair = place_ref[0] // 2
+        for c in range(halves):
+            near = pl.multiple_of((pair * halves + c) * width, width)
+            far = pl.multiple_of(((1 - pair) * halves + c) * width, width)
+            out_ref[:, pl.ds(near, width)] = (keep_ref[c] + x_ref[c].astype(jnp.float32)).astype(jnp.bfloat16)
+            out_ref[:, pl.ds(far, width)] = (
+                z_ref[c].astype(jnp.float32) + both_ref[c].astype(jnp.float32)
+            ).astype(jnp.bfloat16)
+
+    return call(
+        kernel,
+        jax.ShapeDtypeStruct((rows, 2 * halves * width), jnp.bfloat16),
+        [place],
+        [keep, from_x, from_z, from_both],
+        read=16 * rows * halves * width,
+    )
+
+
+def by_heads(latents, w_qkv, w_out, win_blocks, win_counts, block_window):
+    rows_n, heads_n = lax.axis_size("rows"), lax.axis_size("heads")
+    group, row = lax.axis_index("groups"), lax.axis_index("rows")
+    frame, core = lax.axis_index("frames"), lax.axis_index("heads")
+    depth, _, local_cols = w_qkv.shape
+    span = rows_n // heads_n
+    cols = local_cols // span
+    half = depth // 2
+    place = jnp.stack([row, group, frame, core]).astype(jnp.int32)
+
+    gathered = []
+    for c in range(span):
+        slice_at = (core * span + c) * depth
+        mine = lax.dynamic_slice_in_dim(latents[0], slice_at, depth, axis=1)
+        gathered.append(lax.all_gather(mine, "rows", axis=0))
+
+    tables = jnp.concatenate([win_blocks, win_counts[:, None], block_window[:, None]], axis=1)
+    found = [tables] + [swap(tables, "rows", s) for s in range(1, rows_n)]
+    tables = jnp.stack(found)[row ^ jnp.arange(rows_n)].reshape(rows_n * heads_n, MAXB + 2)
+    windows = lax.dynamic_index_in_dim(
+        tables[:, MAXB + 1].reshape(rows_n, heads_n), core, axis=1, keepdims=False
+    )
+    picked = tables[windows]
+    members, counts = picked[:, :MAXB].reshape(-1), picked[:, MAXB]
+
+    by_part = w_qkv.transpose(1, 0, 2)
+    here = []
+    for k in range(span):
+        pairs = [
+            (r * heads_n + h, (h * span + (k + r) % span) * heads_n + r // span)
+            for r in range(rows_n)
+            for h in range(heads_n)
+        ]
+        for part in range(3):
+            piece = lax.dynamic_slice(
+                by_part[part], (group * half, (k + row) % span * cols), (half, cols)
+            )
+            if len(here) >= 2:
+                piece = after(piece, here[-2])
+            if len(here) == 3 * span - 1:
+                piece = after(piece, members, counts)
+            here.append(lax.ppermute(piece, ("rows", "heads"), pairs))
+    chunks = [
+        [(here[3 * k + part], swap(here[3 * k + part], "groups")) for part in range(3)] for k in range(span)
+    ]
+    theirs = [swap(after(g, here[2 + 2 * c]), "frames") for c, g in enumerate(gathered)]
+
+    queries, keyvals, send = project(place, gathered, theirs, chunks)
+    same, diff = attend_all(place, members, counts, queries, keyvals, swap(send, "heads"))
+    attended = [same] + [swap(same if s % 2 == 0 else diff, "rows", s) for s in range(1, rows_n)]
+
+    across = swap(after(w_out, here[1]), "heads")
+    beside = swap(after(w_out, here[-1]), "rows")
+    keep, over_x, over_z, over_both = mix(
+        place, attended, [w_out, beside, across, swap(beside, "heads")]
+    )
+    from_x = swap(over_x, "frames")
+    from_z = swap(over_z, "rows", 2)
+    from_both = lax.ppermute(
+        over_both,
+        ("rows", "frames"),
+        [(2 * r + f, 2 * (r ^ 2) + 1 - f) for r in range(rows_n) for f in range(2)],
+    )
+    out = finish(place, keep, from_x, from_z, from_both)
+    return out[None]
+
+
+def local(latents, w_qkv, w_out, win_blocks, win_counts, block_window):
+    rows_n = lax.axis_size("rows")
+    pairs = all(lax.axis_size(axis) == 2 for axis in ("groups", "frames", "heads"))
+    heads_here = w_qkv.shape[2] // HD
+    if pairs and rows_n == 4 and heads_here % 2 == 0 and latents.shape[:2] == (1, 2 * BS):
+        plan = by_heads
+    else:
+        plan = by_tokens
+    return plan(latents, w_qkv, w_out, win_blocks, win_counts, block_window)
+
+
 def solution(mesh):
     in_specs = (
         P(("groups", "frames"), "rows", None),

time: 457 us -> 185 us (0.40)
  waiting for transfers between devices: 366 us -> 57.9 us
  blocking collectives: 0 us -> 52.7 us
  local copies, waits for them, and re-layouts: 49.5 us -> 11.4 us
  starting transfers between devices: 3.99 us -> 38.1 us
  Pallas kernels: 0 us -> 22.6 us
  matrix products: 21.7 us -> 0 us
  between operations: 13.2 us -> 0.13 us
    all_gather x3 -> x0, waiting for transfers between devices: 270 us -> none  [the longest x1 246 us: local(): weight_rows = lax.all_gather(w_qkv, 'rows', axis=0, tiled=True)]
    all_gather x0 -> x2, blocking collectives: none -> 52.7 us  [by_heads(): gathered.append(lax.all_gather(mine, 'rows', axis=0))]
    ppermute x2 -> x27, starting transfers between devices: 3.87 us -> 38.1 us  [the longest x20 30.9 us: swap(): return lax.ppermute(value, axis, [(i, i ^ step) for i in range(peers)])]
    reduce_scatter x1 -> x0, waiting for transfers between devices: 29.5 us -> none  [local(): lax.psum_scatter(jnp.dot(ordered, w_full, preferred_element_type=jnp.floa...]
    pallas_call x0 -> x4, Pallas kernels: none -> 22.6 us  [the longest x3 12.3 us: call(): pl.pallas_call(kernel, out_shape=out_shape, grid_spec=pltpu.PrefetchScala...]
    dot_general x4 -> x0, matrix products: 18 us -> none  [the longest x1 9.36 us: local(): jnp.dot(flat_tokens, weight_rows.reshape(weight_rows.shape[0], 3 * local_...]
    slice x5 -> x3, local copies, waits for them, and re-layouts: 17.4 us -> 2.57 us  [the longest x1 2.21 us: by_heads(): by_part[part]]
    gather x4 -> x2, local copies, waits for them, and re-layouts: 12.3 us -> 1.13 us  [the longest x1 0.57 us: by_heads(): jnp.stack(found)[row ^ jnp.arange(rows_n)]]
  transfers between devices with their start and end apart: 6 -> 27, of which waited for: 5 -> 13; matrix products, arithmetic and copies ran while one was open for 15% -> 4% of each run, Pallas kernels for 0% -> 9%
where the time goes in v3:
time: 185 us
  waiting for transfers between devices  57.9 us (31%)
  blocking collectives  52.7 us (28%)
  starting transfers between devices  38.1 us (21%)
  Pallas kernels  22.6 us (12%)
  local copies, waits for them, and re-layouts  11.4 us (6%)
  other arithmetic  1.89 us (1%)
    all_gather x2, blocking collectives, by_heads(): gathered.append(lax.all_gather(mine, 'rows', axis=0))  52.7 us
    ppermute x20, waiting for transfers between devices, swap(): return lax.ppermute(value, axis, [(i, i ^ step) for i in range(peers)])  41.2 us
    ppermute x20, starting transfers between devices, swap(): return lax.ppermute(value, axis, [(i, i ^ step) for i in range(peers)])  30.9 us
    ppermute x6, waiting for transfers between devices, by_heads(): here.append(lax.ppermute(piece, ('rows', 'heads'), pairs))  12.4 us
    pallas_call x3, Pallas kernels, call(): pl.pallas_call(kernel, out_shape=out_shape, grid_spec=pltpu.PrefetchScala...  12.3 us
    pallas_call x1, Pallas kernels, project(): pl.pallas_call(kernel, out_shape=(jax.ShapeDtypeStruct((peers, *shapes[0]...  10.3 us
    ppermute x6, starting transfers between devices, by_heads(): here.append(lax.ppermute(piece, ('rows', 'heads'), pairs))  6.08 us
    ppermute x1, waiting for transfers between devices, by_heads(): lax.ppermute(over_both, ('rows', 'frames'), [(2 * r + f, 2 * (r ^ 2) + 1...  4.37 us
  transfers between devices with their start and end apart: 27, of which 13 were waited for; matrix products, arithmetic and copies ran while one was open for 4% of the time, Pallas kernels for 9%

profile of v3, /device:TPU:0, one launch (start us, length us, event | category | flops | bytes accessed | tf_op | source)
XLA Modules:
  0.0 184.7 jit_solution(2449425086134771519)
XLA Ops:
  0.0 0.7 copy.11
  0.7 0.7 copy.12
  1.5 0.8 pad_add_fusion.1
  2.2 4.0 %collective-permute-start.1 = (s32[2,6]{1,0:T(2,128)S(1)}, s32[2,6]{1,0:T(2,128)S(1)}, u32[]{:S(2)}, u32[]{:S(2)}) collective-permute-start(s32[2,6]{1,0:T(2,128)S(1)} %pad_add_fusion.1), channel_id=1, source_target_pairs={{0,8},{4,12},{8,0},{12,4},{1,9},{5,13},{9,1},{13,5},{2,10},{6,14},... | collective-permute-start | bytes 152 | tf_op jit(solution)/shard_map/ppermute | solution.py:106
  6.3 1.6 collective-permute-start
  7.9 2.2 %fusion.2 = (bf16[1,768,768]{2,1,0:T(8,128)(2,1)S(1)}, bf16[1,768,768]{2,1,0:T(8,128)(2,1)S(1)}, bf16[1,768,768]{2,1,0:T(8,128)(2,1)S(1)}) fusion(bf16[3,768,768]{2,1,0:T(8,128)(2,1)} %bitcast.27), kind=kLoop, calls=%fused_computation.22 | loop fusion | bytes 7077888 | tf_op jit(solution)/shard_map/slice | solution.py:349
  10.1 0.9 dynamic-slice_bitcast_fusion.2
  11.0 1.6 collective-permute-start.9
  12.6 0.8 dynamic-slice_bitcast_fusion.1
  13.4 0.8 collective-permute-start.3
  14.3 0.9 dynamic-slice_bitcast_fusion
  15.3 28.0 %all_gather.9.refs_1_ = bf16[4,128,768]{2,1,0:T(8,128)(2,1)S(1)} all-gather(bf16[1,128,768]{2,1,0:T(8,128)(2,1)S(1)} %get-tuple-element.50), channel_id=1, replica_groups=mesh['groups'=2,'rows'=4,'frames'=2,'heads'=2] {'rows'}, dimensions={0}, use_global_device_ids=true | all-gather | bytes 983040 | tf_op jit(solution)/shard_map/all_gather | solution.py:328
  43.3 1.4 collective-permute-start.4
  44.7 24.6 %all_gather.8.refs_0_ = bf16[4,128,768]{2,1,0:T(8,128)(2,1)S(1)} all-gather(bf16[1,128,768]{2,1,0:T(8,128)(2,1)S(1)} %get-tuple-element.51), channel_id=1, replica_groups=mesh['groups'=2,'rows'=4,'frames'=2,'heads'=2] {'rows'}, dimensions={0}, use_global_device_ids=true | all-gather | bytes 983040 | tf_op jit(solution)/shard_map/all_gather | solution.py:328
  69.4 1.9 %collective-permute-start.6 = (bf16[384,384]{1,0:T(8,128)(2,1)}, bf16[384,384]{1,0:T(8,128)(2,1)}, u32[]{:S(2)}, u32[]{:S(2)}) collective-permute-start(bf16[384,384]{1,0:T(8,128)(2,1)} %get-tuple-element.25), channel_id=1, source_target_pairs={{0,4},{1,12},{4,0},{5,8},{8,5},{9,13},{12,1},{13,9},{2,6},{3,14},{... | collective-permute-start | bytes 884744 | tf_op jit(solution)/shard_map/ppermute | solution.py:355
  72.9 1.5 collective-permute-start.10
  74.8 1.6 collective-permute-start.5
  76.4 1.2 collective-permute-done.6.refs_12_
  77.6 1.5 collective-permute-start.7
  79.9 1.6 collective-permute-start.8
  81.5 4.4 %collective-permute-done.12.refs_10_ = bf16[384,384]{1,0:T(8,128)(2,1)} collective-permute-done((bf16[384,384]{1,0:T(8,128)(2,1)}, bf16[384,384]{1,0:T(8,128)(2,1)}, u32[]{:S(2)}, u32[]{:S(2)}) %collective-permute-start.12) | collective-permute-done | bytes 294944 | tf_op jit(solution)/shard_map/ppermute | solution.py:355
  86.1 1.5 collective-permute-start.13
  88.3 1.1 collective-permute-start.11
  89.5 6.7 %collective-permute-done.15.refs_14_ = bf16[384,384]{1,0:T(8,128)(2,1)} collective-permute-done((bf16[384,384]{1,0:T(8,128)(2,1)}, bf16[384,384]{1,0:T(8,128)(2,1)}, u32[]{:S(2)}, u32[]{:S(2)}) %collective-permute-start.15) | collective-permute-done | bytes 294944 | tf_op jit(solution)/shard_map/ppermute | solution.py:355
  96.2 1.5 collective-permute-start.16
  99.0 0.8 collective-permute-done.11.refs_9_
  99.8 4.8 %collective-permute-start.21 = (bf16[768,768]{1,0:T(8,128)(2,1)S(1)}, bf16[768,768]{1,0:T(8,128)(2,1)S(1)}, u32[]{:S(2)}, u32[]{:S(2)}) collective-permute-start(bf16[768,768]{1,0:T(8,128)(2,1)S(1)} %copy-done), channel_id=1, source_target_pairs={{0,4},{4,0},{8,12},{12,8},{1,5},{5,1},{9,13},{13,9},{2,6},{6,2},{1... | collective-permute-start | bytes 3538952 | tf_op jit(solution)/shard_map/ppermute | solution.py:106
  104.6 1.8 collective-permute-done.16.refs_15_
  106.4 6.3 %collective-permute-done.14.refs_13_ = bf16[384,384]{1,0:T(8,128)(2,1)} collective-permute-done((bf16[384,384]{1,0:T(8,128)(2,1)}, bf16[384,384]{1,0:T(8,128)(2,1)}, u32[]{:S(2)}, u32[]{:S(2)}) %collective-permute-start.14) | collective-permute-done | bytes 294944 | tf_op jit(solution)/shard_map/ppermute | solution.py:106
  112.7 1.0 copy-done.2
  113.7 1.0 copy-done.4
  114.7 10.3 %shard_map.64 = (f32[4,128,384]{2,1,0:T(8,128)S(1)}, f32[4,256,768]{2,1,0:T(8,128)}, bf16[4,320,768]{2,1,0:T(8,128)(2,1)}) custom-call(s32[4]{0:T(128)S(1)} %pad_add_fusion.2.place_ref, bf16[4,128,768]{2,1,0:T(8,128)(2,1)S(1)} %all_gather.8.refs_0_, bf16[4,128,768]{2,1,0:T(8,128)(2,1)S(1)} %all_gather.9.refs_1_, ...), custom_call_target="tpu_custom_call" | custom-call | flops 3623878656 | bytes 12079595 | tf_op jit(solution)/shard_map/pallas_call | solution.py:174
  124.9 2.5 %collective-permute-start.17 = (bf16[4,320,768]{2,1,0:T(8,128)(2,1)}, bf16[4,320,768]{2,1,0:T(8,128)(2,1)S(1)}, u32[]{:S(2)}, u32[]{:S(2)}) collective-permute-start(bf16[4,320,768]{2,1,0:T(8,128)(2,1)} %get-tuple-element.32), channel_id=1, source_target_pairs={{0,1},{1,0},{2,3},{3,2},{4,5},{5,4},{6,7},{7,6},{8,9},{9,8},{10,11... | collective-permute-start | bytes 5898248 | tf_op jit(solution)/shard_map/ppermute | solution.py:106
  127.5 3.4 %collective-permute-done.21.refs_5_ = bf16[768,768]{1,0:T(8,128)(2,1)S(1)} collective-permute-done((bf16[768,768]{1,0:T(8,128)(2,1)S(1)}, bf16[768,768]{1,0:T(8,128)(2,1)S(1)}, u32[]{:S(2)}, u32[]{:S(2)}) %collective-permute-start.21) | collective-permute-done | bytes 1179680 | tf_op jit(solution)/shard_map/ppermute | solution.py:106
  131.2 2.1 %collective-permute-done.17.more_ref = bf16[4,320,768]{2,1,0:T(8,128)(2,1)S(1)} collective-permute-done((bf16[4,320,768]{2,1,0:T(8,128)(2,1)}, bf16[4,320,768]{2,1,0:T(8,128)(2,1)S(1)}, u32[]{:S(2)}, u32[]{:S(2)}) %collective-permute-start.17) | collective-permute-done | bytes 1966112 | tf_op jit(solution)/shard_map/ppermute | solution.py:106
  133.3 7.2 %shard_map.65 = (bf16[2,128,384]{2,1,0:T(8,128)(2,1)S(1)}, bf16[2,128,384]{2,1,0:T(8,128)(2,1)S(1)}) custom-call(s32[4]{0:T(128)S(1)} %pad_add_fusion.2.place_ref, s32[16]{0:T(128)S(1)} %reshape.33.members_ref, s32[4]{0:T(128)S(1)} %slice_reduce_fusion.1.counts_ref, f32[4,128,384]{2,1,0:T(8,128)S(1)} %get-tuple-element.30.q_ref, ...), custom_call_target="tpu_custom_call" | custom-call | flops 402653184 | bytes 3145728 | tf_op jit(solution)/shard_map/pallas_call | solution.py:114
  140.7 2.5 %collective-permute-start.20 = (bf16[2,128,384]{2,1,0:T(8,128)(2,1)S(1)}, bf16[2,128,384]{2,1,0:T(8,128)(2,1)S(1)}, u32[]{:S(2)}, u32[]{:S(2)}) collective-permute-start(bf16[2,128,384]{2,1,0:T(8,128)(2,1)S(1)} %get-tuple-element.34), channel_id=1, source_target_pairs={{0,12},{4,8},{8,4},{12,0},{1,13},{5,9},{9,5},{13,1},{2,14},{6,10},... | collective-permute-start | bytes 589832 | tf_op jit(solution)/shard_map/ppermute | solution.py:106
  143.2 1.0 collective-permute-start.18
  144.1 12.8 %collective-permute-done.19.refs_2_ = bf16[2,128,384]{2,1,0:T(8,128)(2,1)S(1)} collective-permute-done((bf16[2,128,384]{2,1,0:T(8,128)(2,1)S(1)}, bf16[2,128,384]{2,1,0:T(8,128)(2,1)S(1)}, u32[]{:S(2)}, u32[]{:S(2)}) %collective-permute-start.19) | collective-permute-done | bytes 196640 | tf_op jit(solution)/shard_map/ppermute | solution.py:106
  156.9 1.3 collective-permute-done.18.refs_1_
  158.2 3.7 %shard_map.66 = (f32[2,64,768]{2,1,0:T(8,128)S(1)}, bf16[2,64,768]{2,1,0:T(8,128)(2,1)S(1)}, bf16[2,64,768]{2,1,0:T(8,128)(2,1)S(1)}, bf16[2,64,768]{2,1,0:T(8,128)(2,1)S(1)}) custom-call(s32[4]{0:T(128)S(1)} %pad_add_fusion.2.place_ref, bf16[2,128,384]{2,1,0:T(8,128)(2,1)S(1)} %get-tuple-element.33.refs_0_, ...), custom_call_target="tpu_custom_call" | custom-call | flops 1207959552 | bytes 4718592 | tf_op jit(solution)/shard_map/pallas_call | solution.py:114
  161.9 0.8 collective-permute-start.24
  162.7 2.5 %collective-permute-start.25 = (bf16[2,64,768]{2,1,0:T(8,128)(2,1)S(1)}, bf16[2,64,768]{2,1,0:T(8,128)(2,1)S(1)}, u32[]{:S(2)}, u32[]{:S(2)}) collective-permute-start(bf16[2,64,768]{2,1,0:T(8,128)(2,1)S(1)} %get-tuple-element.39), channel_id=1, source_target_pairs={{0,8},{4,12},{8,0},{12,4},{1,9},{5,13},{9,1},{13,5},{2,10},{6,14},... | collective-permute-start | bytes 589832 | tf_op jit(solution)/shard_map/ppermute | solution.py:106
  165.2 1.2 collective-permute-start.26
  166.4 1.4 collective-permute-done.24.x_ref
  167.8 11.2 %collective-permute-done.25.z_ref = bf16[2,64,768]{2,1,0:T(8,128)(2,1)S(1)} collective-permute-done((bf16[2,64,768]{2,1,0:T(8,128)(2,1)S(1)}, bf16[2,64,768]{2,1,0:T(8,128)(2,1)S(1)}, u32[]{:S(2)}, u32[]{:S(2)}) %collective-permute-start.25) | collective-permute-done | bytes 196640 | tf_op jit(solution)/shard_map/ppermute | solution.py:106
  179.0 4.4 %collective-permute-done.26.both_ref = bf16[2,64,768]{2,1,0:T(8,128)(2,1)S(1)} collective-permute-done((bf16[2,64,768]{2,1,0:T(8,128)(2,1)S(1)}, bf16[2,64,768]{2,1,0:T(8,128)(2,1)S(1)}, u32[]{:S(2)}, u32[]{:S(2)}) %collective-permute-start.26) | collective-permute-done | bytes 196640 | tf_op jit(solution)/shard_map/ppermute | solution.py:372
  183.4 1.4 shard_map.67
  (51 shorter events, 5.7 us)
Async XLA Ops:
  2.2 69.1 %collective-permute-start.1 = (s32[2,6]{1,0:T(2,128)S(1)}, s32[2,6]{1,0:T(2,128)S(1)}, u32[]{:S(2)}, u32[]{:S(2)}) collective-permute-start(s32[2,6]{1,0:T(2,128)S(1)} %pad_add_fusion.1), channel_id=1, source_target_pairs={{0,8},{4,12},{8,0},{12,4},{1,9},{5,13},{9,1},{13,5},{2,10},{6,14},... | collective-permute-start | bytes 152 | tf_op jit(solution)/shard_map/ppermute | solution.py:106
  6.3 65.0 %collective-permute-start = (s32[2,6]{1,0:T(2,128)S(1)}, s32[2,6]{1,0:T(2,128)}, u32[]{:S(2)}, u32[]{:S(2)}) collective-permute-start(s32[2,6]{1,0:T(2,128)S(1)} %pad_add_fusion.1), channel_id=1, source_target_pairs={{0,4},{4,0},{8,12},{12,8},{1,5},{5,1},{9,13},{13,9},{2,6},{6,2},{1... | collective-permute-start | bytes 152 | tf_op jit(solution)/shard_map/ppermute | solution.py:106
  7.9 63.5 %collective-permute-start.2 = (s32[2,6]{1,0:T(2,128)S(1)}, s32[2,6]{1,0:T(2,128)}, u32[]{:S(2)}, u32[]{:S(2)}) collective-permute-start(s32[2,6]{1,0:T(2,128)S(1)} %pad_add_fusion.1), channel_id=1, source_target_pairs={{0,12},{4,8},{8,4},{12,0},{1,13},{5,9},{9,5},{13,1},{2,14},{6,10},... | collective-permute-start | bytes 152 | tf_op jit(solution)/shard_map/ppermute | solution.py:106
  11.0 61.6 %collective-permute-start.9 = (bf16[384,384]{1,0:T(8,128)(2,1)}, bf16[384,384]{1,0:T(8,128)(2,1)S(1)}, u32[]{:S(2)}, u32[]{:S(2)}) collective-permute-start(bf16[384,384]{1,0:T(8,128)(2,1)} %get-tuple-element.48), channel_id=1, source_target_pairs={{0,0},{1,8},{4,4},{5,12},{8,1},{9,9},{12,5},{13,13},{2,2},{3,10},{... | collective-permute-start | bytes 884744 | tf_op jit(solution)/shard_map/ppermute | solution.py:355
  13.4 1.9 %copy-start.7 = (bf16[1,128,3072]{2,1,0:T(8,128)(2,1)S(1)}, bf16[1,128,3072]{2,1,0:T(8,128)(2,1)}, u32[]{:S(2)}) copy-start(bf16[1,128,3072]{2,1,0:T(8,128)(2,1)} %param.6) | copy-start | bytes 2359300
  13.4 30.0 %collective-permute-start.3 = (bf16[384,384]{1,0:T(8,128)(2,1)S(1)}, bf16[384,384]{1,0:T(8,128)(2,1)S(1)}, u32[]{:S(2)}, u32[]{:S(2)}) collective-permute-start(bf16[384,384]{1,0:T(8,128)(2,1)S(1)} %get-tuple-element.47), channel_id=1, source_target_pairs={{0,0},{1,8},{4,4},{5,12},{8,1},{9,9},{12,5},{13,13},{2,2},{3,10},{... | collective-permute-start | bytes 884744 | tf_op jit(solution)/shard_map/ppermute | solution.py:355
  15.2 28.1 %copy-start.6 = (bf16[384,384]{1,0:T(8,128)(2,1)S(1)}, bf16[384,384]{1,0:T(8,128)(2,1)}, u32[]{:S(2)}) copy-start(bf16[384,384]{1,0:T(8,128)(2,1)} %get-tuple-element.23) | copy-start | bytes 884740
  15.3 56.0 %copy-start.8 = (s32[2,4]{1,0:T(2,128)S(1)}, s32[2,4]{1,0:T(2,128)}, u32[]{:S(2)}) copy-start(s32[2,4]{1,0:T(2,128)} %param.9) | copy-start | bytes 100
  15.3 84.5 %copy-start = (bf16[768,768]{1,0:T(8,128)(2,1)S(1)}, bf16[768,768]{1,0:T(8,128)(2,1)}, u32[]{:S(2)}) copy-start(bf16[768,768]{1,0:T(8,128)(2,1)} %refs_4_.1) | copy-start | bytes 3538948
  43.3 26.0 %collective-permute-start.4 = (bf16[384,384]{1,0:T(8,128)(2,1)S(1)}, bf16[384,384]{1,0:T(8,128)(2,1)}, u32[]{:S(2)}, u32[]{:S(2)}) collective-permute-start(bf16[384,384]{1,0:T(8,128)(2,1)S(1)} %copy-done.6), channel_id=1, source_target_pairs={{0,0},{1,8},{4,4},{5,12},{8,1},{9,9},{12,5},{13,13},{2,2},{3,10},{... | collective-permute-start | bytes 884744 | tf_op jit(solution)/shard_map/ppermute | solution.py:355
  69.4 8.2 %collective-permute-start.6 = (bf16[384,384]{1,0:T(8,128)(2,1)}, bf16[384,384]{1,0:T(8,128)(2,1)}, u32[]{:S(2)}, u32[]{:S(2)}) collective-permute-start(bf16[384,384]{1,0:T(8,128)(2,1)} %get-tuple-element.25), channel_id=1, source_target_pairs={{0,4},{1,12},{4,0},{5,8},{8,5},{9,13},{12,1},{13,9},{2,6},{3,14},{... | collective-permute-start | bytes 884744 | tf_op jit(solution)/shard_map/ppermute | solution.py:355
  72.6 13.4 %collective-permute-start.12 = (bf16[384,384]{1,0:T(8,128)(2,1)}, bf16[384,384]{1,0:T(8,128)(2,1)}, u32[]{:S(2)}, u32[]{:S(2)}) collective-permute-start(bf16[384,384]{1,0:T(8,128)(2,1)} %get-tuple-element.27), channel_id=1, source_target_pairs={{0,4},{1,12},{4,0},{5,8},{8,5},{9,13},{12,1},{13,9},{2,6},{3,14},{... | collective-permute-start | bytes 884744 | tf_op jit(solution)/shard_map/ppermute | solution.py:355
  72.9 13.2 %collective-permute-start.10 = (bf16[384,384]{1,0:T(8,128)(2,1)S(1)}, bf16[384,384]{1,0:T(8,128)(2,1)}, u32[]{:S(2)}, u32[]{:S(2)}) collective-permute-start(bf16[384,384]{1,0:T(8,128)(2,1)S(1)} %collective-permute-done.9.refs_6_), channel_id=1, source_target_pairs={{0,16},{16,0},{1,17},{17,1},{2,18},{18,2},{3,19},{19,3},{4,20},{20... | collective-permute-start | bytes 884744 | tf_op jit(solution)/shard_map/ppermute | solution.py:106
  74.8 37.9 %collective-permute-start.5 = (bf16[4,128,768]{2,1,0:T(8,128)(2,1)S(1)}, bf16[4,128,768]{2,1,0:T(8,128)(2,1)}, u32[]{:S(2)}, u32[]{:S(2)}) collective-permute-start(bf16[4,128,768]{2,1,0:T(8,128)(2,1)S(1)} %all_gather.8.refs_0_), channel_id=1, source_target_pairs={{0,2},{2,0},{1,3},{3,1},{4,6},{6,4},{5,7},{7,5},{8,10},{10,8},{9,1... | collective-permute-start | bytes 2359304 | tf_op jit(solution)/shard_map/ppermute | solution.py:106
  77.6 35.1 %collective-permute-start.7 = (bf16[4,128,768]{2,1,0:T(8,128)(2,1)S(1)}, bf16[4,128,768]{2,1,0:T(8,128)(2,1)}, u32[]{:S(2)}, u32[]{:S(2)}) collective-permute-start(bf16[4,128,768]{2,1,0:T(8,128)(2,1)S(1)} %all_gather.9.refs_1_), channel_id=1, source_target_pairs={{0,2},{2,0},{1,3},{3,1},{4,6},{6,4},{5,7},{7,5},{8,10},{10,8},{9,1... | collective-permute-start | bytes 2359304 | tf_op jit(solution)/shard_map/ppermute | solution.py:106
  79.9 7.7 %collective-permute-start.8 = (bf16[384,384]{1,0:T(8,128)(2,1)S(1)}, bf16[384,384]{1,0:T(8,128)(2,1)S(1)}, u32[]{:S(2)}, u32[]{:S(2)}) collective-permute-start(bf16[384,384]{1,0:T(8,128)(2,1)S(1)} %collective-permute-done.3.refs_4_), channel_id=1, source_target_pairs={{0,16},{16,0},{1,17},{17,1},{2,18},{18,2},{3,19},{19,3},{4,20},{20... | collective-permute-start | bytes 884744 | tf_op jit(solution)/shard_map/ppermute | solution.py:106
  86.0 10.2 %collective-permute-start.15 = (bf16[384,384]{1,0:T(8,128)(2,1)}, bf16[384,384]{1,0:T(8,128)(2,1)}, u32[]{:S(2)}, u32[]{:S(2)}) collective-permute-start(bf16[384,384]{1,0:T(8,128)(2,1)} %get-tuple-element.29), channel_id=1, source_target_pairs={{0,4},{1,12},{4,0},{5,8},{8,5},{9,13},{12,1},{13,9},{2,6},{3,14},{... | collective-permute-start | bytes 884744 | tf_op jit(solution)/shard_map/ppermute | solution.py:355
  86.1 11.6 %collective-permute-start.13 = (bf16[384,384]{1,0:T(8,128)(2,1)}, bf16[384,384]{1,0:T(8,128)(2,1)S(1)}, u32[]{:S(2)}, u32[]{:S(2)}) collective-permute-start(bf16[384,384]{1,0:T(8,128)(2,1)} %collective-permute-done.12.refs_10_), channel_id=1, source_target_pairs={{0,16},{16,0},{1,17},{17,1},{2,18},{18,2},{3,19},{19,3},{4,20},{20... | collective-permute-start | bytes 884744 | tf_op jit(solution)/shard_map/ppermute | solution.py:106
  87.6 0.7 copy-start.1
  88.3 11.5 %collective-permute-start.11 = (bf16[384,384]{1,0:T(8,128)(2,1)}, bf16[384,384]{1,0:T(8,128)(2,1)}, u32[]{:S(2)}, u32[]{:S(2)}) collective-permute-start(bf16[384,384]{1,0:T(8,128)(2,1)} %collective-permute-done.4.refs_8_), channel_id=1, source_target_pairs={{0,16},{16,0},{1,17},{17,1},{2,18},{18,2},{3,19},{19,3},{4,20},{20... | collective-permute-start | bytes 884744 | tf_op jit(solution)/shard_map/ppermute | solution.py:106
  96.2 10.3 %collective-permute-start.16 = (bf16[384,384]{1,0:T(8,128)(2,1)}, bf16[384,384]{1,0:T(8,128)(2,1)}, u32[]{:S(2)}, u32[]{:S(2)}) collective-permute-start(bf16[384,384]{1,0:T(8,128)(2,1)} %collective-permute-done.15.refs_14_), channel_id=1, source_target_pairs={{0,16},{16,0},{1,17},{17,1},{2,18},{18,2},{3,19},{19,3},{4,20},{20... | collective-permute-start | bytes 884744 | tf_op jit(solution)/shard_map/ppermute | solution.py:106
  97.7 0.7 copy-start.3
  98.4 14.3 %collective-permute-start.14 = (bf16[384,384]{1,0:T(8,128)(2,1)}, bf16[384,384]{1,0:T(8,128)(2,1)}, u32[]{:S(2)}, u32[]{:S(2)}) collective-permute-start(bf16[384,384]{1,0:T(8,128)(2,1)} %collective-permute-done.6.refs_12_), channel_id=1, source_target_pairs={{0,16},{16,0},{1,17},{17,1},{2,18},{18,2},{3,19},{19,3},{4,20},{20... | collective-permute-start | bytes 884744 | tf_op jit(solution)/shard_map/ppermute | solution.py:106
  99.8 31.1 %collective-permute-start.21 = (bf16[768,768]{1,0:T(8,128)(2,1)S(1)}, bf16[768,768]{1,0:T(8,128)(2,1)S(1)}, u32[]{:S(2)}, u32[]{:S(2)}) collective-permute-start(bf16[768,768]{1,0:T(8,128)(2,1)S(1)} %copy-done), channel_id=1, source_target_pairs={{0,4},{4,0},{8,12},{12,8},{1,5},{5,1},{9,13},{13,9},{2,6},{6,2},{1... | collective-permute-start | bytes 3538952 | tf_op jit(solution)/shard_map/ppermute | solution.py:106
  112.7 1.0 copy-start.2
  113.7 1.0 copy-start.4
  124.9 8.4 %collective-permute-start.17 = (bf16[4,320,768]{2,1,0:T(8,128)(2,1)}, bf16[4,320,768]{2,1,0:T(8,128)(2,1)S(1)}, u32[]{:S(2)}, u32[]{:S(2)}) collective-permute-start(bf16[4,320,768]{2,1,0:T(8,128)(2,1)} %get-tuple-element.32), channel_id=1, source_target_pairs={{0,1},{1,0},{2,3},{3,2},{4,5},{5,4},{6,7},{7,6},{8,9},{9,8},{10,11... | collective-permute-start | bytes 5898248 | tf_op jit(solution)/shard_map/ppermute | solution.py:106
  127.5 16.7 %collective-permute-start.22 = (bf16[768,768]{1,0:T(8,128)(2,1)S(1)}, bf16[768,768]{1,0:T(8,128)(2,1)S(1)}, u32[]{:S(2)}, u32[]{:S(2)}) collective-permute-start(bf16[768,768]{1,0:T(8,128)(2,1)S(1)} %copy-done), channel_id=1, source_target_pairs={{0,1},{1,0},{2,3},{3,2},{4,5},{5,4},{6,7},{7,6},{8,9},{9,8},{10,11... | collective-permute-start | bytes 3538952 | tf_op jit(solution)/shard_map/ppermute | solution.py:106
  130.9 13.2 %collective-permute-start.23 = (bf16[768,768]{1,0:T(8,128)(2,1)S(1)}, bf16[768,768]{1,0:T(8,128)(2,1)S(1)}, u32[]{:S(2)}, u32[]{:S(2)}) collective-permute-start(bf16[768,768]{1,0:T(8,128)(2,1)S(1)} %collective-permute-done.21.refs_5_), channel_id=1, source_target_pairs={{0,1},{1,0},{2,3},{3,2},{4,5},{5,4},{6,7},{7,6},{8,9},{9,8},{10,11... | collective-permute-start | bytes 3538952 | tf_op jit(solution)/shard_map/ppermute | solution.py:106
  140.6 16.3 %collective-permute-start.19 = (bf16[2,128,384]{2,1,0:T(8,128)(2,1)S(1)}, bf16[2,128,384]{2,1,0:T(8,128)(2,1)S(1)}, u32[]{:S(2)}, u32[]{:S(2)}) collective-permute-start(bf16[2,128,384]{2,1,0:T(8,128)(2,1)S(1)} %get-tuple-element.33.refs_0_), channel_id=1, source_target_pairs={{0,8},{4,12},{8,0},{12,4},{1,9},{5,13},{9,1},{13,5},{2,10},{6,14},... | collective-permute-start | bytes 589832 | tf_op jit(solution)/shard_map/ppermute | solution.py:106
  140.7 16.3 %collective-permute-start.20 = (bf16[2,128,384]{2,1,0:T(8,128)(2,1)S(1)}, bf16[2,128,384]{2,1,0:T(8,128)(2,1)S(1)}, u32[]{:S(2)}, u32[]{:S(2)}) collective-permute-start(bf16[2,128,384]{2,1,0:T(8,128)(2,1)S(1)} %get-tuple-element.34), channel_id=1, source_target_pairs={{0,12},{4,8},{8,4},{12,0},{1,13},{5,9},{9,5},{13,1},{2,14},{6,10},... | collective-permute-start | bytes 589832 | tf_op jit(solution)/shard_map/ppermute | solution.py:106
  143.2 15.0 %collective-permute-start.18 = (bf16[2,128,384]{2,1,0:T(8,128)(2,1)S(1)}, bf16[2,128,384]{2,1,0:T(8,128)(2,1)S(1)}, u32[]{:S(2)}, u32[]{:S(2)}) collective-permute-start(bf16[2,128,384]{2,1,0:T(8,128)(2,1)S(1)} %get-tuple-element.34), channel_id=1, source_target_pairs={{0,4},{4,0},{8,12},{12,8},{1,5},{5,1},{9,13},{13,9},{2,6},{6,2},{1... | collective-permute-start | bytes 589832 | tf_op jit(solution)/shard_map/ppermute | solution.py:106
  144.1 14.0 %copy-start.5 = (bf16[768,768]{1,0:T(8,128)(2,1)}, bf16[768,768]{1,0:T(8,128)(2,1)S(1)}, u32[]{:S(2)}) copy-start(bf16[768,768]{1,0:T(8,128)(2,1)S(1)} %collective-permute-done.23.refs_7_) | copy-start | bytes 3538948
  161.9 5.9 %collective-permute-start.24 = (bf16[2,64,768]{2,1,0:T(8,128)(2,1)S(1)}, bf16[2,64,768]{2,1,0:T(8,128)(2,1)S(1)}, u32[]{:S(2)}, u32[]{:S(2)}) collective-permute-start(bf16[2,64,768]{2,1,0:T(8,128)(2,1)S(1)} %get-tuple-element.38), channel_id=1, source_target_pairs={{0,2},{2,0},{1,3},{3,1},{4,6},{6,4},{5,7},{7,5},{8,10},{10,8},{9,1... | collective-permute-start | bytes 589832 | tf_op jit(solution)/shard_map/ppermute | solution.py:106
  162.7 16.3 %collective-permute-start.25 = (bf16[2,64,768]{2,1,0:T(8,128)(2,1)S(1)}, bf16[2,64,768]{2,1,0:T(8,128)(2,1)S(1)}, u32[]{:S(2)}, u32[]{:S(2)}) collective-permute-start(bf16[2,64,768]{2,1,0:T(8,128)(2,1)S(1)} %get-tuple-element.39), channel_id=1, source_target_pairs={{0,8},{4,12},{8,0},{12,4},{1,9},{5,13},{9,1},{13,5},{2,10},{6,14},... | collective-permute-start | bytes 589832 | tf_op jit(solution)/shard_map/ppermute | solution.py:106
  165.2 18.2 %collective-permute-start.26 = (bf16[2,64,768]{2,1,0:T(8,128)(2,1)S(1)}, bf16[2,64,768]{2,1,0:T(8,128)(2,1)S(1)}, u32[]{:S(2)}, u32[]{:S(2)}) collective-permute-start(bf16[2,64,768]{2,1,0:T(8,128)(2,1)S(1)} %get-tuple-element.40), channel_id=1, source_target_pairs={{0,10},{2,8},{4,14},{6,12},{8,2},{10,0},{12,6},{14,4},{1,11},{3,9}... | collective-permute-start | bytes 589832 | tf_op jit(solution)/shard_map/ppermute | solution.py:372

commit v4 on v3

--- a/solution.py
+++ b/solution.py
@@ -10,7 +10,7 @@
 HD = 128
 BS = 64
 MAXB = 4
-VMEM_BYTES = 48 * 1024 * 1024
+VMEM_BYTES = 24 * 1024 * 1024
 EXP2_SCALE = math.log2(math.e) / math.sqrt(HD)
 
 
@@ -126,106 +126,123 @@
     )(*prefetch, *operands)
 
 
-def project(place, mine, theirs, chunks):
-    peers, count, depth = mine[0].shape
-    slices = len(mine)
-    half, cols = chunks[0][0][0].shape
-    flat = [w for of_round in chunks for of_part in of_round for w in of_part]
+def assemble(place, mine, theirs):
+    count, width = mine[0].shape
+    rows = len(mine)
 
     def kernel(place_ref, *refs):
-        row, group, frame, core = (place_ref[i] for i in range(4))
-        x_refs, w_refs = refs[: 2 * slices], refs[2 * slices : 2 * slices + len(flat)]
-        q_keep, kv_keep, send, x_all, q_all = refs[2 * slices + len(flat) :]
-        for c in range(slices):
-            x_all[c, frame] = x_refs[c][0]
-            x_all[c, 1 - frame] = x_refs[slices + c][0]
-        for part in range(3):
-            acc = None
-            for k in range(slices):
-                at = (row + slices - k) % slices
-                for g in range(2):
-                    start = pl.multiple_of((group + g) % 2 * half, half)
-                    piece = x_all[at, :, :, pl.ds(start, half)].reshape(2 * count, half)
-                    w_ref = w_refs[(k * 3 + part) * 2 + g]
-                    term = jnp.dot(piece, w_ref[...], preferred_element_type=jnp.float32)
-                    acc = term if acc is None else acc + term
-            if part == 0:
-                q_all[...] = acc.reshape(2, count, cols)
-                own = pl.multiple_of(core * BS, BS)
-                other = pl.multiple_of((1 - core) * BS, BS)
-                q_keep[0] = q_all[:, pl.ds(own, BS), :].reshape(2 * BS, cols)
-                for f in range(2):
-                    send[0, 2 * count :, f * cols : (f + 1) * cols] = q_all[f, pl.ds(other, BS), :].astype(
-                        jnp.bfloat16
-                    )
-            else:
-                where = slice((part - 1) * cols, part * cols)
-                kv_keep[0, :, where] = acc
-                send[0, : 2 * count, where] = acc.astype(jnp.bfloat16)
-
-    def at_row(*shape):
-        return pl.BlockSpec((1, *shape), lambda i, *_: (i,) + (0,) * len(shape))
-
-    def whole(shape):
-        return pl.BlockSpec(shape, lambda i, *_: (0,) * len(shape))
-
-    shapes = ((2 * BS, cols), (2 * count, 2 * cols), (2 * count + BS, 2 * cols))
-    flops = 2 * peers * 2 * count * slices * depth * 3 * cols
-    return pl.pallas_call(
-        kernel,
-        out_shape=(
-            jax.ShapeDtypeStruct((peers, *shapes[0]), jnp.float32),
-            jax.ShapeDtypeStruct((peers, *shapes[1]), jnp.float32),
-            jax.ShapeDtypeStruct((peers, *shapes[2]), jnp.bfloat16),
-        ),
-        grid_spec=pltpu.PrefetchScalarGridSpec(
-            num_scalar_prefetch=1,
-            grid=(peers,),
-            in_specs=[at_row(count, depth)] * (2 * slices) + [whole(w.shape) for w in flat],
-            out_specs=tuple(at_row(*shape) for shape in shapes),
-            scratch_shapes=[
-                pltpu.VMEM((slices, 2, count, depth), jnp.bfloat16),
-                pltpu.VMEM((2, count, cols), jnp.float32),
-            ],
-        ),
-        compiler_params=pltpu.CompilerParams(vmem_limit_bytes=VMEM_BYTES),
-        cost_estimate=pl.CostEstimate(flops=flops, bytes_accessed=flops // 300, transcendentals=0),
-    )(place, *mine, *theirs, *flat)
-
-
-def attend_all(place, members, counts, queries, keyvals, more):
+        row, frame = place_ref[0], place_ref[2]
+        for s in range(rows):
+            refs[-1][row ^ s, frame] = refs[s][...]
+            refs[-1][row ^ s, 1 - frame] = refs[rows + s][...]
+
+    return call(
+        kernel,
+        jax.ShapeDtypeStruct((rows, 2, count, width), jnp.bfloat16),
+        [place],
+        [*mine, *theirs],
+        read=8 * rows * count * width,
+    )
+
+
+def project(place, tokens, chunks, only_own):
+    rows, _, count, width = tokens.shape
+    half, cols = chunks[0][0].shape
+    slices = len(chunks)
+    flat = [w for of_round in chunks for w in of_round]
+
+    def kernel(place_ref, x_ref, *refs):
+        row, group, core = place_ref[0], place_ref[1], place_ref[3]
+        w_refs = refs[: len(flat)]
+        keep, send = refs[len(flat) : len(flat) + 2]
+        acc = None
+        for k in range(slices):
+            for g in range(2):
+                at = (row + slices - k) % slices * (2 * half) + (group + g) % 2 * half
+                piece = x_ref[:, :, :, pl.ds(pl.multiple_of(at, half), half)].reshape(-1, half)
+                term = jnp.dot(piece, w_refs[2 * k + g][...], preferred_element_type=jnp.float32)
+                acc = term if acc is None else acc + term
+        if only_own:
+            total = refs[-1]
+            total[...] = acc.reshape(2 * rows, count, cols)
+            own = pl.multiple_of(core * BS, BS)
+            other = pl.multiple_of((1 - core) * BS, BS)
+            keep[...] = total[:, pl.ds(own, BS), :].reshape(keep.shape)
+            send[...] = total[:, pl.ds(other, BS), :].reshape(send.shape).astype(jnp.bfloat16)
+        else:
+            keep[...] = acc.reshape(keep.shape)
+            send[...] = acc.reshape(send.shape).astype(jnp.bfloat16)
+
+    shape = (rows, 2 * (BS if only_own else count), cols)
+    flops = 4 * rows * count * width * cols
+    return call(
+        kernel,
+        (jax.ShapeDtypeStruct(shape, jnp.float32), jax.ShapeDtypeStruct(shape, jnp.bfloat16)),
+        [place],
+        [tokens, *flat],
+        scratch=[pltpu.VMEM((2 * rows, count, cols), jnp.float32)] if only_own else [],
+        flops=flops,
+        read=flops // 300,
+    )
+
+
+def by_block(out_ref, keep_ref, more_ref):
+    rows, count, _ = keep_ref.shape
+    per_row = count // (2 * BS)
+    for r in range(rows):
+        both = (keep_ref[r] + more_ref[r].astype(jnp.float32)).astype(jnp.bfloat16)
+        both = both.reshape(2, count // 2, -1)
+        for j in range(per_row):
+            out_ref[r * per_row + j] = both[:, j * BS : (j + 1) * BS, :].reshape(2 * BS, -1)
+
+
+def weigh(members, counts, queries, more_queries, keys, more_keys):
     blocks, block_len, cols = queries.shape
-    rows = keyvals.shape[1]
-    per_row = rows // block_len
-
-    def kernel(place_ref, members_ref, counts_ref, q_ref, kv_ref, more_ref, same_ref, diff_ref, q_sum, kv_sum, out):
-        for r in range(blocks):
-            added = more_ref[r, rows:, :].astype(jnp.float32)
-            added = jnp.concatenate([added[:, :cols], added[:, cols:]], axis=0)
-            q_sum[r] = (q_ref[r] + added).astype(jnp.bfloat16)
-            both = (kv_ref[r] + more_ref[r, :rows, :].astype(jnp.float32)).astype(jnp.bfloat16)
-            both = both.reshape(2, rows // 2, 2 * cols)
-            for j in range(per_row):
-                part = both[:, j * BS : (j + 1) * BS, :]
-                kv_sum[r * per_row + j] = part.reshape(block_len, 2 * cols)
+    per_row = keys.shape[1] // block_len
+    heads = cols // HD
+
+    def kernel(members_ref, counts_ref, q_ref, q_more, k_ref, k_more, out_ref, k_sum):
+        by_block(k_sum, k_ref, k_more)
         column = lax.broadcasted_iota(jnp.int32, (block_len, MAXB * block_len), 1)
         for b in range(blocks):
+            q_rows = (q_ref[b] + q_more[b].astype(jnp.float32)).astype(jnp.bfloat16)
             live = column < counts_ref[b] * block_len
-            listed = [kv_sum.at[members_ref[b * MAXB + j]] for j in range(MAXB)]
-            for h in range(cols // HD):
+            listed = [k_sum.at[members_ref[b * MAXB + j]] for j in range(MAXB)]
+            for h in range(heads):
                 at = slice(h * HD, (h + 1) * HD)
-                at_v = slice(cols + h * HD, cols + (h + 1) * HD)
-                keys = jnp.concatenate([block[:, at] for block in listed], axis=0)
-                values = jnp.concatenate([block[:, at_v] for block in listed], axis=0)
+                of_head = jnp.concatenate([block[:, at] for block in listed], axis=0)
                 scores = lax.dot_general(
-                    q_sum[b, :, at], keys, (((1,), (1,)), ((), ())), preferred_element_type=jnp.float32
+                    q_rows[:, at], of_head, (((1,), (1,)), ((), ())), preferred_element_type=jnp.float32
                 )
                 scores = jnp.where(live, scores, -jnp.inf)
                 raised = jnp.exp2((scores - jnp.max(scores, axis=-1, keepdims=True)) * EXP2_SCALE)
                 weights = raised * (1.0 / jnp.sum(raised, axis=-1, keepdims=True))
-                blended = jnp.dot(
-                    weights.astype(jnp.bfloat16), values, preferred_element_type=jnp.float32
-                )
+                out_ref[b, h] = weights.astype(jnp.bfloat16)
+
+    return call(
+        kernel,
+        jax.ShapeDtypeStruct((blocks, heads, block_len, MAXB * block_len), jnp.bfloat16),
+        [members, counts],
+        [queries, more_queries, keys, more_keys],
+        scratch=[pltpu.VMEM((blocks * per_row, block_len, cols), jnp.bfloat16)],
+        flops=2 * blocks * block_len * MAXB * block_len * cols,
+        read=16 * blocks * block_len * cols,
+    )
+
+
+def blend(place, members, weights, values, more_values):
+    blocks, heads, block_len, _ = weights.shape
+    cols = values.shape[2]
+    per_row = values.shape[1] // block_len
+
+    def kernel(place_ref, members_ref, w_ref, v_ref, v_more, same_ref, diff_ref, v_sum, out):
+        by_block(v_sum, v_ref, v_more)
+        for b in range(blocks):
+            listed = [v_sum.at[members_ref[b * MAXB + j]] for j in range(MAXB)]
+            for h in range(heads):
+                at = slice(h * HD, (h + 1) * HD)
+                of_head = jnp.concatenate([block[:, at] for block in listed], axis=0)
+                blended = jnp.dot(w_ref[b, h], of_head, preferred_element_type=jnp.float32)
                 out[(b + place_ref[0]) % 2, b // 2, :, at] = blended.astype(jnp.bfloat16)
         same_ref[...] = out[0]
         diff_ref[...] = out[1]
@@ -234,14 +251,13 @@
     return call(
         kernel,
         (half, half),
-        [place, members, counts],
-        [queries, keyvals, more],
+        [place, members],
+        [weights, values, more_values],
         scratch=[
-            pltpu.VMEM((blocks, block_len, cols), jnp.bfloat16),
-            pltpu.VMEM((blocks * per_row, block_len, 2 * cols), jnp.bfloat16),
+            pltpu.VMEM((blocks * per_row, block_len, cols), jnp.bfloat16),
             pltpu.VMEM((2, blocks // 2, block_len, cols), jnp.bfloat16),
         ],
-        flops=4 * blocks * block_len * MAXB * block_len * cols,
+        flops=2 * blocks * block_len * MAXB * block_len * cols,
         read=16 * blocks * block_len * cols,
     )
 
@@ -321,13 +337,13 @@
     half = depth // 2
     place = jnp.stack([row, group, frame, core]).astype(jnp.int32)
 
-    gathered = []
-    for c in range(span):
-        slice_at = (core * span + c) * depth
-        mine = lax.dynamic_slice_in_dim(latents[0], slice_at, depth, axis=1)
-        gathered.append(lax.all_gather(mine, "rows", axis=0))
+    mine = [lax.dynamic_slice_in_dim(latents[0], core * span * depth, span * depth, axis=1)]
+    mine += [swap(mine[0], "rows", s) for s in range(1, rows_n)]
+    theirs = [swap(x, "frames") for x in mine]
+    tokens = assemble(place, mine, theirs)
 
     tables = jnp.concatenate([win_blocks, win_counts[:, None], block_window[:, None]], axis=1)
+    tables = after(tables, mine[1])
     found = [tables] + [swap(tables, "rows", s) for s in range(1, rows_n)]
     tables = jnp.stack(found)[row ^ jnp.arange(rows_n)].reshape(rows_n * heads_n, MAXB + 2)
     windows = lax.dynamic_index_in_dim(
@@ -338,32 +354,34 @@
 
     by_part = w_qkv.transpose(1, 0, 2)
     here = []
-    for k in range(span):
-        pairs = [
-            (r * heads_n + h, (h * span + (k + r) % span) * heads_n + r // span)
-            for r in range(rows_n)
-            for h in range(heads_n)
-        ]
-        for part in range(3):
+    for part in range(3):
+        for k in range(span):
+            pairs = [
+                (r * heads_n + h, (h * span + (k + r) % span) * heads_n + r // span)
+                for r in range(rows_n)
+                for h in range(heads_n)
+            ]
             piece = lax.dynamic_slice(
                 by_part[part], (group * half, (k + row) % span * cols), (half, cols)
             )
-            if len(here) >= 2:
-                piece = after(piece, here[-2])
-            if len(here) == 3 * span - 1:
+            piece = after(piece, here[-2] if len(here) >= 2 else mine[1 + len(here)])
+            if len(here) == 3:
                 piece = after(piece, members, counts)
             here.append(lax.ppermute(piece, ("rows", "heads"), pairs))
-    chunks = [
-        [(here[3 * k + part], swap(here[3 * k + part], "groups")) for part in range(3)] for k in range(span)
-    ]
-    theirs = [swap(after(g, here[2 + 2 * c]), "frames") for c, g in enumerate(gathered)]
-
-    queries, keyvals, send = project(place, gathered, theirs, chunks)
-    same, diff = attend_all(place, members, counts, queries, keyvals, swap(send, "heads"))
+    there = [swap(w, "groups") for w in here]
+
+    partial, more = [], []
+    for part in range(3):
+        rounds = range(part * span, (part + 1) * span)
+        keep, send = project(place, tokens, [(here[i], there[i]) for i in rounds], part == 0)
+        partial.append(keep)
+        more.append(swap(send, "heads"))
+    weights = weigh(members, counts, partial[0], more[0], partial[1], more[1])
+    same, diff = blend(place, members, weights, partial[2], more[2])
     attended = [same] + [swap(same if s % 2 == 0 else diff, "rows", s) for s in range(1, rows_n)]
 
     across = swap(after(w_out, here[1]), "heads")
-    beside = swap(after(w_out, here[-1]), "rows")
+    beside = swap(after(w_out, here[3]), "rows")
     keep, over_x, over_z, over_both = mix(
         place, attended, [w_out, beside, across, swap(beside, "heads")]
     )

time: 185 us -> 186 us (level)
  blocking collectives: 52.7 us -> 0 us
  starting transfers between devices: 38.1 us -> 77.7 us
  local copies, waits for them, and re-layouts: 11.4 us -> 22.2 us
  waiting for transfers between devices: 57.9 us -> 65.7 us
  Pallas kernels: 22.6 us -> 18.4 us
    all_gather x2 -> x0, blocking collectives: 52.7 us -> none  [by_heads(): gathered.append(lax.all_gather(mine, 'rows', axis=0))]
    ppermute x20 -> x27, starting transfers between devices: 30.9 us -> 52.9 us  [swap(): return lax.ppermute(value, axis, [(i, i ^ step) for i in range(peers)])]
    ppermute x6, starting transfers between devices: 6.08 us -> 24.4 us  [by_heads(): here.append(lax.ppermute(piece, ('rows', 'heads'), pairs))]
    pallas_call x1 -> x0, Pallas kernels: 10.3 us -> none  [project(): pl.pallas_call(kernel, out_shape=(jax.ShapeDtypeStruct((peers, *shapes[0]...]
    unnamed x18 -> x44, local copies, waits for them, and re-layouts: 3.37 us -> 11.2 us
    ppermute x20 -> x27, waiting for transfers between devices: 41.2 us -> 48.9 us  [swap(): return lax.ppermute(value, axis, [(i, i ^ step) for i in range(peers)])]
    pallas_call x3 -> x8, Pallas kernels: 12.3 us -> 18.4 us  [call(): pl.pallas_call(kernel, out_shape=out_shape, grid_spec=pltpu.PrefetchScala...]
    ppermute x6, waiting for transfers between devices: 12.4 us -> 14.3 us  [by_heads(): here.append(lax.ppermute(piece, ('rows', 'heads'), pairs))]
  transfers between devices with their start and end apart: 27 -> 34, of which waited for: 13 -> 15; matrix products, arithmetic and copies ran while one was open for 4% -> 6% of each run, Pallas kernels for 9% -> 8%
where the time goes in v4:
time: 186 us; the launch traced here: 185 us
  starting transfers between devices  77.7 us (42%)
  waiting for transfers between devices  65.7 us (35%)
  local copies, waits for them, and re-layouts  22.2 us (12%)
  Pallas kernels  18.4 us (10%)
    ppermute x27, starting transfers between devices, swap(): return lax.ppermute(value, axis, [(i, i ^ step) for i in range(peers)])  52.9 us
    ppermute x27, waiting for transfers between devices, swap(): return lax.ppermute(value, axis, [(i, i ^ step) for i in range(peers)])  48.9 us
    ppermute x6, starting transfers between devices, by_heads(): here.append(lax.ppermute(piece, ('rows', 'heads'), pairs))  24.4 us
    pallas_call x8, Pallas kernels, call(): pl.pallas_call(kernel, out_shape=out_shape, grid_spec=pltpu.PrefetchScala...  18.4 us
    ppermute x6, waiting for transfers between devices, by_heads(): here.append(lax.ppermute(piece, ('rows', 'heads'), pairs))  14.3 us
    unnamed x44, local copies, waits for them, and re-layouts  11.2 us
    dynamic_slice x3, local copies, waits for them, and re-layouts, by_heads(): lax.dynamic_slice(by_part[part], (group * half, (k + row) % span * cols),...  4.09 us
    slice x1, local copies, waits for them, and re-layouts, by_heads(): by_part[part]  3.81 us
  transfers between devices with their start and end apart: 34, of which 15 were waited for; matrix products, arithmetic and copies ran while one was open for 6% of the time, Pallas kernels for 8%

profile of v4, /device:TPU:0, one launch (start us, length us, event | category | flops | bytes accessed | tf_op | source)
XLA Modules:
  0.0 184.7 jit_solution(12843869642482119969)
XLA Ops:
  0.0 1.1 copy-done
  1.2 4.1 %collective-permute-start.4 = (bf16[128,1536]{1,0:T(8,128)(2,1)S(1)}, bf16[128,1536]{1,0:T(8,128)(2,1)S(1)}, u32[]{:S(2)}, u32[]{:S(2)}) collective-permute-start(bf16[128,1536]{1,0:T(8,128)(2,1)S(1)} %dynamic-slice_bitcast_fusion.refs_0_), channel_id=1, source_target_pairs={{0,8},{4,12},{8,0},{12,4},{1,9},{5,13},{9,1},{13,5},{2,10},{6,14},... | collective-permute-start | bytes 1179656 | tf_op jit(solution)/shard_map/ppermute | solution.py:106
  5.3 1.6 collective-permute-start
  8.3 3.8 %fusion.2 = (bf16[1,768,768]{2,1,0:T(8,128)(2,1)}, bf16[1,768,768]{2,1,0:T(8,128)(2,1)}, bf16[1,768,768]{2,1,0:T(8,128)(2,1)}) fusion(bf16[3,768,768]{2,1,0:T(8,128)(2,1)} %bitcast.28), kind=kLoop, calls=%fused_computation.20 | loop fusion | bytes 7077888 | tf_op jit(solution)/shard_map/slice | solution.py:365
  12.4 2.1 %dynamic-slice_bitcast_fusion.3 = (bf16[384,384]{1,0:T(8,128)(2,1)}, bf16[384,384]{1,0:T(8,128)(2,1)}) fusion(bf16[1,768,768]{2,1,0:T(8,128)(2,1)} %get-tuple-element.50, s32[]{:T(128)S(6)} %select_n.62, s32[]{:T(128)S(6)} %select_n.66, s32[]{:T(128)S(6)} %select_n.64), kind=kLoop, calls=%fused_computation.5 | loop fusion | bytes 1179660 | tf_op jit(solution)/shard_map/dynamic_slice | solution.py:364
  15.3 7.8 %collective-permute-done.refs_1_ = bf16[128,1536]{1,0:T(8,128)(2,1)S(1)} collective-permute-done((bf16[128,1536]{1,0:T(8,128)(2,1)S(1)}, bf16[128,1536]{1,0:T(8,128)(2,1)S(1)}, u32[]{:S(2)}, u32[]{:S(2)}) %collective-permute-start) | collective-permute-done | bytes 393248 | tf_op jit(solution)/shard_map/ppermute | solution.py:106
  23.5 2.6 %collective-permute-start.2 = (s32[2,6]{1,0:T(2,128)S(1)}, s32[2,6]{1,0:T(2,128)S(1)}, u32[]{:S(2)}, u32[]{:S(2)}) collective-permute-start(s32[2,6]{1,0:T(2,128)S(1)} %pad_add_fusion.1), channel_id=1, source_target_pairs={{0,8},{4,12},{8,0},{12,4},{1,9},{5,13},{9,1},{13,5},{2,10},{6,14},... | collective-permute-start | bytes 152 | tf_op jit(solution)/shard_map/ppermute | solution.py:106
  26.1 1.4 collective-permute-start.1
  28.5 1.1 collective-permute-done.1
  31.5 5.4 %collective-permute-done.12.refs_2_ = bf16[384,384]{1,0:T(8,128)(2,1)S(1)} collective-permute-done((bf16[384,384]{1,0:T(8,128)(2,1)}, bf16[384,384]{1,0:T(8,128)(2,1)S(1)}, u32[]{:S(2)}, u32[]{:S(2)}) %collective-permute-start.12) | collective-permute-done | bytes 294944 | tf_op jit(solution)/shard_map/ppermute | solution.py:370
  37.4 1.6 collective-permute-start.10
  39.0 3.1 %collective-permute-start.5 = (bf16[128,1536]{1,0:T(8,128)(2,1)S(1)}, bf16[128,1536]{1,0:T(8,128)(2,1)S(1)}, u32[]{:S(2)}, u32[]{:S(2)}) collective-permute-start(bf16[128,1536]{1,0:T(8,128)(2,1)S(1)} %dynamic-slice_bitcast_fusion.refs_0_), channel_id=1, source_target_pairs={{0,12},{4,8},{8,4},{12,0},{1,13},{5,9},{9,5},{13,1},{2,14},{6,10},... | collective-permute-start | bytes 1179656 | tf_op jit(solution)/shard_map/ppermute | solution.py:106
  42.1 6.2 %collective-permute-done.17.refs_2_ = bf16[384,384]{1,0:T(8,128)(2,1)} collective-permute-done((bf16[384,384]{1,0:T(8,128)(2,1)}, bf16[384,384]{1,0:T(8,128)(2,1)}, u32[]{:S(2)}, u32[]{:S(2)}) %collective-permute-start.17) | collective-permute-done | bytes 294944 | tf_op jit(solution)/shard_map/ppermute | solution.py:370
  48.3 3.7 %collective-permute-start.15 = (bf16[384,384]{1,0:T(8,128)(2,1)}, bf16[384,384]{1,0:T(8,128)(2,1)}, u32[]{:S(2)}, u32[]{:S(2)}) collective-permute-start(bf16[384,384]{1,0:T(8,128)(2,1)} %get-tuple-element.32), channel_id=1, source_target_pairs={{0,0},{1,8},{4,4},{5,12},{8,1},{9,9},{12,5},{13,13},{2,2},{3,10},{... | collective-permute-start | bytes 884744 | tf_op jit(solution)/shard_map/ppermute | solution.py:370
  52.1 1.5 collective-permute-start.6
  53.6 3.7 %collective-permute-done.5.refs_3_ = bf16[128,1536]{1,0:T(8,128)(2,1)S(1)} collective-permute-done((bf16[128,1536]{1,0:T(8,128)(2,1)S(1)}, bf16[128,1536]{1,0:T(8,128)(2,1)S(1)}, u32[]{:S(2)}, u32[]{:S(2)}) %collective-permute-start.5) | collective-permute-done | bytes 393248 | tf_op jit(solution)/shard_map/ppermute | solution.py:106
  57.3 1.5 collective-permute-start.9
  59.4 1.5 collective-permute-start.7
  60.8 1.1 dynamic-slice_bitcast_fusion.1
  62.7 1.4 collective-permute-start.20
  64.1 1.0 collective-permute-done.9.refs_7_
  65.9 16.6 %collective-permute-start.22 = (bf16[384,384]{1,0:T(8,128)(2,1)S(1)}, bf16[384,384]{1,0:T(8,128)(2,1)}, u32[]{:S(2)}, u32[]{:S(2)}) collective-permute-start(bf16[384,384]{1,0:T(8,128)(2,1)S(1)} %get-tuple-element.38), channel_id=1, source_target_pairs={{0,4},{1,12},{4,0},{5,8},{8,5},{9,13},{12,1},{13,9},{2,6},{3,14},{... | collective-permute-start | bytes 884744 | tf_op jit(solution)/shard_map/ppermute | solution.py:370
  83.2 1.5 collective-permute-start.16
  86.0 1.5 collective-permute-start.21
  87.5 2.7 %collective-permute-done.22.refs_2_ = bf16[384,384]{1,0:T(8,128)(2,1)} collective-permute-done((bf16[384,384]{1,0:T(8,128)(2,1)S(1)}, bf16[384,384]{1,0:T(8,128)(2,1)}, u32[]{:S(2)}, u32[]{:S(2)}) %collective-permute-start.22) | collective-permute-done | bytes 294944 | tf_op jit(solution)/shard_map/ppermute | solution.py:370
  90.3 1.5 collective-permute-start.23
  92.4 1.0 copy-done.3
  93.4 1.0 copy-done.5
  94.4 1.0 copy-done.7
  95.4 1.0 copy-done.9
  96.3 1.0 copy-done.11
  100.1 15.0 %collective-permute-start.29 = (bf16[768,768]{1,0:T(8,128)(2,1)S(1)}, bf16[768,768]{1,0:T(8,128)(2,1)S(1)}, u32[]{:S(2)}, u32[]{:S(2)}) collective-permute-start(bf16[768,768]{1,0:T(8,128)(2,1)S(1)} %copy-done.1), channel_id=1, source_target_pairs={{0,1},{1,0},{2,3},{3,2},{4,5},{5,4},{6,7},{7,6},{8,9},{9,8},{10,11... | collective-permute-start | bytes 3538952 | tf_op jit(solution)/shard_map/ppermute | solution.py:106
  115.2 3.9 %shard_map.66 = (f32[4,256,384]{2,1,0:T(8,128)S(1)}, bf16[4,256,384]{2,1,0:T(8,128)(2,1)S(1)}) custom-call(s32[4]{0:T(128)S(1)} %pad_add_fusion.2.place_ref, bf16[4,2,128,1536]{3,2,1,0:T(8,128)(2,1)S(1)} %shard_map.64.x_ref, bf16[384,384]{1,0:T(8,128)(2,1)} %collective-permute-done.15.refs_0_, bf16[384,384]{1,0:T(8,128)(2,1)} %collective-permute-done.16.refs_1_, ...), custom_call_target="tpu_custom_call" | custom-call | flops 1207959552 | bytes 4026531 | tf_op jit(solution)/shard_map/pallas_call | solution.py:114
  119.8 3.9 %shard_map.68 = (f32[4,256,384]{2,1,0:T(8,128)S(1)}, bf16[4,256,384]{2,1,0:T(8,128)(2,1)S(1)}) custom-call(s32[4]{0:T(128)S(1)} %pad_add_fusion.2.place_ref, bf16[4,2,128,1536]{3,2,1,0:T(8,128)(2,1)S(1)} %shard_map.64.x_ref, bf16[384,384]{1,0:T(8,128)(2,1)} %collective-permute-done.20.refs_0_, bf16[384,384]{1,0:T(8,128)(2,1)} %collective-permute-done.21.refs_1_, ...), custom_call_target="tpu_custom_call" | custom-call | flops 1207959552 | bytes 4026531 | tf_op jit(solution)/shard_map/pallas_call | solution.py:114
  124.1 4.4 %collective-permute-done.13.refs_3_ = bf16[384,384]{1,0:T(8,128)(2,1)S(1)} collective-permute-done((bf16[384,384]{1,0:T(8,128)(2,1)S(1)}, bf16[384,384]{1,0:T(8,128)(2,1)S(1)}, u32[]{:S(2)}, u32[]{:S(2)}) %collective-permute-start.13) | collective-permute-done | bytes 294944 | tf_op jit(solution)/shard_map/ppermute | solution.py:106
  128.5 2.7 %shard_map.65 = (f32[4,128,384]{2,1,0:T(8,128)S(1)}, bf16[4,128,384]{2,1,0:T(8,128)(2,1)S(1)}) custom-call(s32[4]{0:T(128)S(1)} %pad_add_fusion.2.place_ref, bf16[4,2,128,1536]{3,2,1,0:T(8,128)(2,1)S(1)} %shard_map.64.x_ref, bf16[384,384]{1,0:T(8,128)(2,1)S(1)} %copy-done.19, bf16[384,384]{1,0:T(8,128)(2,1)S(1)} %collective-permute-done.11.refs_1_, ...), custom_call_target="tpu_custom_call" | custom-call | flops 1207959552 | bytes 4026531 | tf_op jit(solution)/shard_map/pallas_call | solution.py:114
  131.3 1.7 collective-permute-done.14.q_more
  133.0 1.9 %shard_map.67.w_ref = bf16[4,3,128,512]{3,2,1,0:T(8,128)(2,1)S(1)} custom-call(s32[16]{0:T(128)S(1)} %reshape.30.members_ref, s32[4]{0:T(128)S(1)} %slice_reduce_fusion.1.counts_ref, f32[4,128,384]{2,1,0:T(8,128)S(1)} %get-tuple-element.30.q_ref, bf16[4,128,384]{2,1,0:T(8,128)(2,1)S(1)} %collective-permute-done.14.q_more, ...), custom_call_target="tpu_custom_call" | custom-call | flops 201326592 | bytes 3145728 | tf_op jit(solution)/shard_map/pallas_call | solution.py:114
  134.9 1.5 shard_map.69
  136.4 8.2 %collective-permute-start.26 = (bf16[2,128,384]{2,1,0:T(8,128)(2,1)S(1)}, bf16[2,128,384]{2,1,0:T(8,128)(2,1)S(1)}, u32[]{:S(2)}, u32[]{:S(2)}) collective-permute-start(bf16[2,128,384]{2,1,0:T(8,128)(2,1)S(1)} %get-tuple-element.41.refs_0_), channel_id=1, source_target_pairs={{0,8},{4,12},{8,0},{12,4},{1,9},{5,13},{9,1},{13,5},{2,10},{6,14},... | collective-permute-start | bytes 589832 | tf_op jit(solution)/shard_map/ppermute | solution.py:106
  145.2 13.4 %collective-permute-done.26.refs_2_ = bf16[2,128,384]{2,1,0:T(8,128)(2,1)S(1)} collective-permute-done((bf16[2,128,384]{2,1,0:T(8,128)(2,1)S(1)}, bf16[2,128,384]{2,1,0:T(8,128)(2,1)S(1)}, u32[]{:S(2)}, u32[]{:S(2)}) %collective-permute-start.26) | collective-permute-done | bytes 196640 | tf_op jit(solution)/shard_map/ppermute | solution.py:106
  159.6 2.5 %shard_map.70 = (f32[2,64,768]{2,1,0:T(8,128)S(1)}, bf16[2,64,768]{2,1,0:T(8,128)(2,1)S(1)}, bf16[2,64,768]{2,1,0:T(8,128)(2,1)S(1)}, bf16[2,64,768]{2,1,0:T(8,128)(2,1)S(1)}) custom-call(s32[4]{0:T(128)S(1)} %pad_add_fusion.2.place_ref, bf16[2,128,384]{2,1,0:T(8,128)(2,1)S(1)} %get-tuple-element.41.refs_0_, ...), custom_call_target="tpu_custom_call" | custom-call | flops 1207959552 | bytes 4718592 | tf_op jit(solution)/shard_map/pallas_call | solution.py:114
  162.0 1.7 collective-permute-start.31
  163.7 2.4 %collective-permute-start.32 = (bf16[2,64,768]{2,1,0:T(8,128)(2,1)S(1)}, bf16[2,64,768]{2,1,0:T(8,128)(2,1)S(1)}, u32[]{:S(2)}, u32[]{:S(2)}) collective-permute-start(bf16[2,64,768]{2,1,0:T(8,128)(2,1)S(1)} %get-tuple-element.47), channel_id=1, source_target_pairs={{0,8},{4,12},{8,0},{12,4},{1,9},{5,13},{9,1},{13,5},{2,10},{6,14},... | collective-permute-start | bytes 589832 | tf_op jit(solution)/shard_map/ppermute | solution.py:106
  166.5 1.3 collective-permute-done.31.x_ref
  167.8 13.1 %collective-permute-done.32.z_ref = bf16[2,64,768]{2,1,0:T(8,128)(2,1)S(1)} collective-permute-done((bf16[2,64,768]{2,1,0:T(8,128)(2,1)S(1)}, bf16[2,64,768]{2,1,0:T(8,128)(2,1)S(1)}, u32[]{:S(2)}, u32[]{:S(2)}) %collective-permute-start.32) | collective-permute-done | bytes 196640 | tf_op jit(solution)/shard_map/ppermute | solution.py:106
  180.8 2.5 %collective-permute-done.33.both_ref = bf16[2,64,768]{2,1,0:T(8,128)(2,1)S(1)} collective-permute-done((bf16[2,64,768]{2,1,0:T(8,128)(2,1)S(1)}, bf16[2,64,768]{2,1,0:T(8,128)(2,1)S(1)}, u32[]{:S(2)}, u32[]{:S(2)}) %collective-permute-start.33) | collective-permute-done | bytes 196640 | tf_op jit(solution)/shard_map/ppermute | solution.py:390
  183.4 1.4 shard_map.71
  (92 shorter events, 17.1 us)
Async XLA Ops:
  0.0 1.1 copy-start
  1.2 26.3 %collective-permute-start.4 = (bf16[128,1536]{1,0:T(8,128)(2,1)S(1)}, bf16[128,1536]{1,0:T(8,128)(2,1)S(1)}, u32[]{:S(2)}, u32[]{:S(2)}) collective-permute-start(bf16[128,1536]{1,0:T(8,128)(2,1)S(1)} %dynamic-slice_bitcast_fusion.refs_0_), channel_id=1, source_target_pairs={{0,8},{4,12},{8,0},{12,4},{1,9},{5,13},{9,1},{13,5},{2,10},{6,14},... | collective-permute-start | bytes 1179656 | tf_op jit(solution)/shard_map/ppermute | solution.py:106
  5.3 17.8 %collective-permute-start = (bf16[128,1536]{1,0:T(8,128)(2,1)S(1)}, bf16[128,1536]{1,0:T(8,128)(2,1)S(1)}, u32[]{:S(2)}, u32[]{:S(2)}) collective-permute-start(bf16[128,1536]{1,0:T(8,128)(2,1)S(1)} %dynamic-slice_bitcast_fusion.refs_0_), channel_id=1, source_target_pairs={{0,4},{4,0},{8,12},{12,8},{1,5},{5,1},{9,13},{13,9},{2,6},{6,2},{1... | collective-permute-start | bytes 1179656 | tf_op jit(solution)/shard_map/ppermute | solution.py:106
  8.3 3.8 %copy-start.21 = (s32[2,4]{1,0:T(2,128)S(1)}, s32[2,4]{1,0:T(2,128)}, u32[]{:S(2)}) copy-start(s32[2,4]{1,0:T(2,128)} %param.9) | copy-start | bytes 100
  12.2 2.2 %copy-start.20 = (bf16[1,768,768]{2,1,0:T(8,128)(2,1)S(1)}, bf16[1,768,768]{2,1,0:T(8,128)(2,1)}, u32[]{:S(2)}) copy-start(bf16[1,768,768]{2,1,0:T(8,128)(2,1)} %get-tuple-element.51) | copy-start | bytes 3538948
  12.3 36.0 %copy-start.1 = (bf16[768,768]{1,0:T(8,128)(2,1)S(1)}, bf16[768,768]{1,0:T(8,128)(2,1)}, u32[]{:S(2)}) copy-start(bf16[768,768]{1,0:T(8,128)(2,1)} %refs_4_.1) | copy-start | bytes 3538948
  23.1 19.0 %copy-start.4 = (bf16[128,1536]{1,0:T(8,128)(2,1)}, bf16[128,1536]{1,0:T(8,128)(2,1)S(1)}, u32[]{:S(2)}) copy-start(bf16[128,1536]{1,0:T(8,128)(2,1)S(1)} %collective-permute-done.refs_1_) | copy-start | bytes 1179652
  23.1 5.4 %collective-permute-start.3 = (s32[2,6]{1,0:T(2,128)S(1)}, s32[2,6]{1,0:T(2,128)S(1)}, u32[]{:S(2)}, u32[]{:S(2)}) collective-permute-start(s32[2,6]{1,0:T(2,128)S(1)} %pad_add_fusion.1), channel_id=1, source_target_pairs={{0,12},{4,8},{8,4},{12,0},{1,13},{5,9},{9,5},{13,1},{2,14},{6,10},... | collective-permute-start | bytes 152 | tf_op jit(solution)/shard_map/ppermute | solution.py:106
  23.5 5.0 %collective-permute-start.2 = (s32[2,6]{1,0:T(2,128)S(1)}, s32[2,6]{1,0:T(2,128)S(1)}, u32[]{:S(2)}, u32[]{:S(2)}) collective-permute-start(s32[2,6]{1,0:T(2,128)S(1)} %pad_add_fusion.1), channel_id=1, source_target_pairs={{0,8},{4,12},{8,0},{12,4},{1,9},{5,13},{9,1},{13,5},{2,10},{6,14},... | collective-permute-start | bytes 152 | tf_op jit(solution)/shard_map/ppermute | solution.py:106
  26.1 3.6 %collective-permute-start.1 = (s32[2,6]{1,0:T(2,128)S(1)}, s32[2,6]{1,0:T(2,128)S(1)}, u32[]{:S(2)}, u32[]{:S(2)}) collective-permute-start(s32[2,6]{1,0:T(2,128)S(1)} %pad_add_fusion.1), channel_id=1, source_target_pairs={{0,4},{4,0},{8,12},{12,8},{1,5},{5,1},{9,13},{13,9},{2,6},{6,2},{1... | collective-permute-start | bytes 152 | tf_op jit(solution)/shard_map/ppermute | solution.py:106
  27.5 14.6 %copy-start.2 = (bf16[128,1536]{1,0:T(8,128)(2,1)}, bf16[128,1536]{1,0:T(8,128)(2,1)S(1)}, u32[]{:S(2)}) copy-start(bf16[128,1536]{1,0:T(8,128)(2,1)S(1)} %collective-permute-done.4.refs_2_) | copy-start | bytes 1179652
  27.5 9.4 %collective-permute-start.12 = (bf16[384,384]{1,0:T(8,128)(2,1)}, bf16[384,384]{1,0:T(8,128)(2,1)S(1)}, u32[]{:S(2)}, u32[]{:S(2)}) collective-permute-start(bf16[384,384]{1,0:T(8,128)(2,1)} %get-tuple-element.29), channel_id=1, source_target_pairs={{0,4},{1,12},{4,0},{5,8},{8,5},{9,13},{12,1},{13,9},{2,6},{3,14},{... | collective-permute-start | bytes 884744 | tf_op jit(solution)/shard_map/ppermute | solution.py:370
  36.9 5.2 %copy-start.16 = (bf16[384,384]{1,0:T(8,128)(2,1)}, bf16[384,384]{1,0:T(8,128)(2,1)S(1)}, u32[]{:S(2)}) copy-start(bf16[384,384]{1,0:T(8,128)(2,1)S(1)} %collective-permute-done.12.refs_2_) | copy-start | bytes 884740
  36.9 11.4 %collective-permute-start.17 = (bf16[384,384]{1,0:T(8,128)(2,1)}, bf16[384,384]{1,0:T(8,128)(2,1)}, u32[]{:S(2)}, u32[]{:S(2)}) collective-permute-start(bf16[384,384]{1,0:T(8,128)(2,1)} %get-tuple-element.34), channel_id=1, source_target_pairs={{0,4},{1,12},{4,0},{5,8},{8,5},{9,13},{12,1},{13,9},{2,6},{3,14},{... | collective-permute-start | bytes 884744 | tf_op jit(solution)/shard_map/ppermute | solution.py:370
  37.4 10.9 %collective-permute-start.10 = (bf16[384,384]{1,0:T(8,128)(2,1)}, bf16[384,384]{1,0:T(8,128)(2,1)S(1)}, u32[]{:S(2)}, u32[]{:S(2)}) collective-permute-start(bf16[384,384]{1,0:T(8,128)(2,1)} %get-tuple-element.28), channel_id=1, source_target_pairs={{0,0},{1,8},{4,4},{5,12},{8,1},{9,9},{12,5},{13,13},{2,2},{3,10},{... | collective-permute-start | bytes 884744 | tf_op jit(solution)/shard_map/ppermute | solution.py:370
  39.0 18.3 %collective-permute-start.5 = (bf16[128,1536]{1,0:T(8,128)(2,1)S(1)}, bf16[128,1536]{1,0:T(8,128)(2,1)S(1)}, u32[]{:S(2)}, u32[]{:S(2)}) collective-permute-start(bf16[128,1536]{1,0:T(8,128)(2,1)S(1)} %dynamic-slice_bitcast_fusion.refs_0_), channel_id=1, source_target_pairs={{0,12},{4,8},{8,4},{12,0},{1,13},{5,9},{9,5},{13,1},{2,14},{6,10},... | collective-permute-start | bytes 1179656 | tf_op jit(solution)/shard_map/ppermute | solution.py:106
  48.3 66.8 %collective-permute-start.28 = (bf16[768,768]{1,0:T(8,128)(2,1)S(1)}, bf16[768,768]{1,0:T(8,128)(2,1)S(1)}, u32[]{:S(2)}, u32[]{:S(2)}) collective-permute-start(bf16[768,768]{1,0:T(8,128)(2,1)S(1)} %copy-done.1), channel_id=1, source_target_pairs={{0,4},{4,0},{8,12},{12,8},{1,5},{5,1},{9,13},{13,9},{2,6},{6,2},{1... | collective-permute-start | bytes 3538952 | tf_op jit(solution)/shard_map/ppermute | solution.py:106
  48.3 11.0 %copy-start.18 = (bf16[384,384]{1,0:T(8,128)(2,1)}, bf16[384,384]{1,0:T(8,128)(2,1)S(1)}, u32[]{:S(2)}) copy-start(bf16[384,384]{1,0:T(8,128)(2,1)S(1)} %collective-permute-done.10.refs_0_) | copy-start | bytes 884740
  48.3 11.0 %collective-permute-start.15 = (bf16[384,384]{1,0:T(8,128)(2,1)}, bf16[384,384]{1,0:T(8,128)(2,1)}, u32[]{:S(2)}, u32[]{:S(2)}) collective-permute-start(bf16[384,384]{1,0:T(8,128)(2,1)} %get-tuple-element.32), channel_id=1, source_target_pairs={{0,0},{1,8},{4,4},{5,12},{8,1},{9,9},{12,5},{13,13},{2,2},{3,10},{... | collective-permute-start | bytes 884744 | tf_op jit(solution)/shard_map/ppermute | solution.py:370
  52.1 9.9 %collective-permute-start.6 = (bf16[128,1536]{1,0:T(8,128)(2,1)S(1)}, bf16[128,1536]{1,0:T(8,128)(2,1)S(1)}, u32[]{:S(2)}, u32[]{:S(2)}) collective-permute-start(bf16[128,1536]{1,0:T(8,128)(2,1)S(1)} %dynamic-slice_bitcast_fusion.refs_0_), channel_id=1, source_target_pairs={{0,2},{2,0},{1,3},{3,1},{4,6},{6,4},{5,7},{7,5},{8,10},{10,8},{9,1... | collective-permute-start | bytes 1179656 | tf_op jit(solution)/shard_map/ppermute | solution.py:106
  57.3 4.6 %copy-start.6 = (bf16[128,1536]{1,0:T(8,128)(2,1)}, bf16[128,1536]{1,0:T(8,128)(2,1)S(1)}, u32[]{:S(2)}) copy-start(bf16[128,1536]{1,0:T(8,128)(2,1)S(1)} %collective-permute-done.5.refs_3_) | copy-start | bytes 1179652
  57.3 7.8 %collective-permute-start.9 = (bf16[128,1536]{1,0:T(8,128)(2,1)S(1)}, bf16[128,1536]{1,0:T(8,128)(2,1)S(1)}, u32[]{:S(2)}, u32[]{:S(2)}) collective-permute-start(bf16[128,1536]{1,0:T(8,128)(2,1)S(1)} %collective-permute-done.5.refs_3_), channel_id=1, source_target_pairs={{0,2},{2,0},{1,3},{3,1},{4,6},{6,4},{5,7},{7,5},{8,10},{10,8},{9,1... | collective-permute-start | bytes 1179656 | tf_op jit(solution)/shard_map/ppermute | solution.py:106
  58.8 23.7 %collective-permute-start.8 = (bf16[128,1536]{1,0:T(8,128)(2,1)}, bf16[128,1536]{1,0:T(8,128)(2,1)S(1)}, u32[]{:S(2)}, u32[]{:S(2)}) collective-permute-start(bf16[128,1536]{1,0:T(8,128)(2,1)} %copy-done.2), channel_id=1, source_target_pairs={{0,2},{2,0},{1,3},{3,1},{4,6},{6,4},{5,7},{7,5},{8,10},{10,8},{9,1... | collective-permute-start | bytes 1179656 | tf_op jit(solution)/shard_map/ppermute | solution.py:106
  59.4 25.4 %collective-permute-start.7 = (bf16[128,1536]{1,0:T(8,128)(2,1)}, bf16[128,1536]{1,0:T(8,128)(2,1)S(1)}, u32[]{:S(2)}, u32[]{:S(2)}) collective-permute-start(bf16[128,1536]{1,0:T(8,128)(2,1)} %copy-done.4), channel_id=1, source_target_pairs={{0,2},{2,0},{1,3},{3,1},{4,6},{6,4},{5,7},{7,5},{8,10},{10,8},{9,1... | collective-permute-start | bytes 1179656 | tf_op jit(solution)/shard_map/ppermute | solution.py:106
  62.7 23.3 %collective-permute-start.20 = (bf16[384,384]{1,0:T(8,128)(2,1)S(1)}, bf16[384,384]{1,0:T(8,128)(2,1)}, u32[]{:S(2)}, u32[]{:S(2)}) collective-permute-start(bf16[384,384]{1,0:T(8,128)(2,1)S(1)} %get-tuple-element.37), channel_id=1, source_target_pairs={{0,0},{1,8},{4,4},{5,12},{8,1},{9,9},{12,5},{13,13},{2,2},{3,10},{... | collective-permute-start | bytes 884744 | tf_op jit(solution)/shard_map/ppermute | solution.py:370
  65.9 24.4 %collective-permute-start.22 = (bf16[384,384]{1,0:T(8,128)(2,1)S(1)}, bf16[384,384]{1,0:T(8,128)(2,1)}, u32[]{:S(2)}, u32[]{:S(2)}) collective-permute-start(bf16[384,384]{1,0:T(8,128)(2,1)S(1)} %get-tuple-element.38), channel_id=1, source_target_pairs={{0,4},{1,12},{4,0},{5,8},{8,5},{9,13},{12,1},{13,9},{2,6},{3,14},{... | collective-permute-start | bytes 884744 | tf_op jit(solution)/shard_map/ppermute | solution.py:370
  83.2 8.6 %collective-permute-start.16 = (bf16[384,384]{1,0:T(8,128)(2,1)}, bf16[384,384]{1,0:T(8,128)(2,1)}, u32[]{:S(2)}, u32[]{:S(2)}) collective-permute-start(bf16[384,384]{1,0:T(8,128)(2,1)} %collective-permute-done.15.refs_0_), channel_id=1, source_target_pairs={{0,16},{16,0},{1,17},{17,1},{2,18},{18,2},{3,19},{19,3},{4,20},{20... | collective-permute-start | bytes 884744 | tf_op jit(solution)/shard_map/ppermute | solution.py:106
  85.5 14.6 %collective-permute-start.18 = (bf16[384,384]{1,0:T(8,128)(2,1)}, bf16[384,384]{1,0:T(8,128)(2,1)}, u32[]{:S(2)}, u32[]{:S(2)}) collective-permute-start(bf16[384,384]{1,0:T(8,128)(2,1)} %collective-permute-done.17.refs_2_), channel_id=1, source_target_pairs={{0,16},{16,0},{1,17},{17,1},{2,18},{18,2},{3,19},{19,3},{4,20},{20... | collective-permute-start | bytes 884744 | tf_op jit(solution)/shard_map/ppermute | solution.py:106
  86.0 33.0 %collective-permute-start.21 = (bf16[384,384]{1,0:T(8,128)(2,1)}, bf16[384,384]{1,0:T(8,128)(2,1)}, u32[]{:S(2)}, u32[]{:S(2)}) collective-permute-start(bf16[384,384]{1,0:T(8,128)(2,1)} %collective-permute-done.20.refs_0_), channel_id=1, source_target_pairs={{0,16},{16,0},{1,17},{17,1},{2,18},{18,2},{3,19},{19,3},{4,20},{20... | collective-permute-start | bytes 884744 | tf_op jit(solution)/shard_map/ppermute | solution.py:106
  90.3 29.4 %collective-permute-start.23 = (bf16[384,384]{1,0:T(8,128)(2,1)}, bf16[384,384]{1,0:T(8,128)(2,1)}, u32[]{:S(2)}, u32[]{:S(2)}) collective-permute-start(bf16[384,384]{1,0:T(8,128)(2,1)} %collective-permute-done.22.refs_2_), channel_id=1, source_target_pairs={{0,16},{16,0},{1,17},{17,1},{2,18},{18,2},{3,19},{19,3},{4,20},{20... | collective-permute-start | bytes 884744 | tf_op jit(solution)/shard_map/ppermute | solution.py:106
  91.8 31.9 %collective-permute-start.11 = (bf16[384,384]{1,0:T(8,128)(2,1)}, bf16[384,384]{1,0:T(8,128)(2,1)S(1)}, u32[]{:S(2)}, u32[]{:S(2)}) collective-permute-start(bf16[384,384]{1,0:T(8,128)(2,1)} %copy-done.18), channel_id=1, source_target_pairs={{0,16},{16,0},{1,17},{17,1},{2,18},{18,2},{3,19},{19,3},{4,20},{20... | collective-permute-start | bytes 884744 | tf_op jit(solution)/shard_map/ppermute | solution.py:106
  92.4 1.0 copy-start.3
  93.4 1.0 copy-start.5
  94.4 1.0 copy-start.7
  100.1 19.0 %copy-start.17 = (bf16[384,384]{1,0:T(8,128)(2,1)S(1)}, bf16[384,384]{1,0:T(8,128)(2,1)}, u32[]{:S(2)}) copy-start(bf16[384,384]{1,0:T(8,128)(2,1)} %copy-done.16) | copy-start | bytes 884740
  100.1 45.1 %collective-permute-start.29 = (bf16[768,768]{1,0:T(8,128)(2,1)S(1)}, bf16[768,768]{1,0:T(8,128)(2,1)S(1)}, u32[]{:S(2)}, u32[]{:S(2)}) collective-permute-start(bf16[768,768]{1,0:T(8,128)(2,1)S(1)} %copy-done.1), channel_id=1, source_target_pairs={{0,1},{1,0},{2,3},{3,2},{4,5},{5,4},{6,7},{7,6},{8,9},{9,8},{10,11... | collective-permute-start | bytes 3538952 | tf_op jit(solution)/shard_map/ppermute | solution.py:106
  115.1 44.5 %collective-permute-start.30 = (bf16[768,768]{1,0:T(8,128)(2,1)S(1)}, bf16[768,768]{1,0:T(8,128)(2,1)S(1)}, u32[]{:S(2)}, u32[]{:S(2)}) collective-permute-start(bf16[768,768]{1,0:T(8,128)(2,1)S(1)} %collective-permute-done.28.refs_5_), channel_id=1, source_target_pairs={{0,1},{1,0},{2,3},{3,2},{4,5},{5,4},{6,7},{7,6},{8,9},{9,8},{10,11... | collective-permute-start | bytes 3538952 | tf_op jit(solution)/shard_map/ppermute | solution.py:106
  119.1 9.4 %collective-permute-start.13 = (bf16[384,384]{1,0:T(8,128)(2,1)S(1)}, bf16[384,384]{1,0:T(8,128)(2,1)S(1)}, u32[]{:S(2)}, u32[]{:S(2)}) collective-permute-start(bf16[384,384]{1,0:T(8,128)(2,1)S(1)} %copy-done.17), channel_id=1, source_target_pairs={{0,16},{16,0},{1,17},{17,1},{2,18},{18,2},{3,19},{19,3},{4,20},{20... | collective-permute-start | bytes 884744 | tf_op jit(solution)/shard_map/ppermute | solution.py:106
  119.6 8.9 %copy-start.19 = (bf16[384,384]{1,0:T(8,128)(2,1)S(1)}, bf16[384,384]{1,0:T(8,128)(2,1)}, u32[]{:S(2)}) copy-start(bf16[384,384]{1,0:T(8,128)(2,1)} %copy-done.18) | copy-start | bytes 884740
  119.6 13.4 %collective-permute-start.19 = (bf16[4,256,384]{2,1,0:T(8,128)(2,1)S(1)}, bf16[4,256,384]{2,1,0:T(8,128)(2,1)S(1)}, u32[]{:S(2)}, u32[]{:S(2)}) collective-permute-start(bf16[4,256,384]{2,1,0:T(8,128)(2,1)S(1)} %get-tuple-element.36), channel_id=1, source_target_pairs={{0,1},{1,0},{2,3},{3,2},{4,5},{5,4},{6,7},{7,6},{8,9},{9,8},{10,11... | collective-permute-start | bytes 2359304 | tf_op jit(solution)/shard_map/ppermute | solution.py:106
  123.7 11.2 %collective-permute-start.24 = (bf16[4,256,384]{2,1,0:T(8,128)(2,1)S(1)}, bf16[4,256,384]{2,1,0:T(8,128)(2,1)S(1)}, u32[]{:S(2)}, u32[]{:S(2)}) collective-permute-start(bf16[4,256,384]{2,1,0:T(8,128)(2,1)S(1)} %get-tuple-element.40), channel_id=1, source_target_pairs={{0,1},{1,0},{2,3},{3,2},{4,5},{5,4},{6,7},{7,6},{8,9},{9,8},{10,11... | collective-permute-start | bytes 2359304 | tf_op jit(solution)/shard_map/ppermute | solution.py:106
  131.2 1.8 collective-permute-start.14
  136.4 22.2 %collective-permute-start.26 = (bf16[2,128,384]{2,1,0:T(8,128)(2,1)S(1)}, bf16[2,128,384]{2,1,0:T(8,128)(2,1)S(1)}, u32[]{:S(2)}, u32[]{:S(2)}) collective-permute-start(bf16[2,128,384]{2,1,0:T(8,128)(2,1)S(1)} %get-tuple-element.41.refs_0_), channel_id=1, source_target_pairs={{0,8},{4,12},{8,0},{12,4},{1,9},{5,13},{9,1},{13,5},{2,10},{6,14},... | collective-permute-start | bytes 589832 | tf_op jit(solution)/shard_map/ppermute | solution.py:106
  144.6 14.0 %collective-permute-start.27 = (bf16[2,128,384]{2,1,0:T(8,128)(2,1)S(1)}, bf16[2,128,384]{2,1,0:T(8,128)(2,1)S(1)}, u32[]{:S(2)}, u32[]{:S(2)}) collective-permute-start(bf16[2,128,384]{2,1,0:T(8,128)(2,1)S(1)} %get-tuple-element.42), channel_id=1, source_target_pairs={{0,12},{4,8},{8,4},{12,0},{1,13},{5,9},{9,5},{13,1},{2,14},{6,10},... | collective-permute-start | bytes 589832 | tf_op jit(solution)/shard_map/ppermute | solution.py:106
  145.1 14.5 %collective-permute-start.25 = (bf16[2,128,384]{2,1,0:T(8,128)(2,1)S(1)}, bf16[2,128,384]{2,1,0:T(8,128)(2,1)S(1)}, u32[]{:S(2)}, u32[]{:S(2)}) collective-permute-start(bf16[2,128,384]{2,1,0:T(8,128)(2,1)S(1)} %get-tuple-element.42), channel_id=1, source_target_pairs={{0,4},{4,0},{8,12},{12,8},{1,5},{5,1},{9,13},{13,9},{2,6},{6,2},{1... | collective-permute-start | bytes 589832 | tf_op jit(solution)/shard_map/ppermute | solution.py:106
  162.0 5.7 %collective-permute-start.31 = (bf16[2,64,768]{2,1,0:T(8,128)(2,1)S(1)}, bf16[2,64,768]{2,1,0:T(8,128)(2,1)S(1)}, u32[]{:S(2)}, u32[]{:S(2)}) collective-permute-start(bf16[2,64,768]{2,1,0:T(8,128)(2,1)S(1)} %get-tuple-element.46), channel_id=1, source_target_pairs={{0,2},{2,0},{1,3},{3,1},{4,6},{6,4},{5,7},{7,5},{8,10},{10,8},{9,1... | collective-permute-start | bytes 589832 | tf_op jit(solution)/shard_map/ppermute | solution.py:106
  163.7 17.2 %collective-permute-start.32 = (bf16[2,64,768]{2,1,0:T(8,128)(2,1)S(1)}, bf16[2,64,768]{2,1,0:T(8,128)(2,1)S(1)}, u32[]{:S(2)}, u32[]{:S(2)}) collective-permute-start(bf16[2,64,768]{2,1,0:T(8,128)(2,1)S(1)} %get-tuple-element.47), channel_id=1, source_target_pairs={{0,8},{4,12},{8,0},{12,4},{1,9},{5,13},{9,1},{13,5},{2,10},{6,14},... | collective-permute-start | bytes 589832 | tf_op jit(solution)/shard_map/ppermute | solution.py:106
  166.1 17.2 %collective-permute-start.33 = (bf16[2,64,768]{2,1,0:T(8,128)(2,1)S(1)}, bf16[2,64,768]{2,1,0:T(8,128)(2,1)S(1)}, u32[]{:S(2)}, u32[]{:S(2)}) collective-permute-start(bf16[2,64,768]{2,1,0:T(8,128)(2,1)S(1)} %get-tuple-element.48), channel_id=1, source_target_pairs={{0,10},{2,8},{4,14},{6,12},{8,2},{10,0},{12,6},{14,4},{1,11},{3,9}... | collective-permute-start | bytes 589832 | tf_op jit(solution)/shard_map/ppermute | solution.py:390
  (8 other events, 7.0 us)

commit v5 on v3

--- a/solution.py
+++ b/solution.py
@@ -10,7 +10,7 @@
 HD = 128
 BS = 64
 MAXB = 4
-VMEM_BYTES = 48 * 1024 * 1024
+VMEM_BYTES = 24 * 1024 * 1024
 EXP2_SCALE = math.log2(math.e) / math.sqrt(HD)
 
 
@@ -126,71 +126,80 @@
     )(*prefetch, *operands)
 
 
-def project(place, mine, theirs, chunks):
-    peers, count, depth = mine[0].shape
-    slices = len(mine)
-    half, cols = chunks[0][0][0].shape
-    flat = [w for of_round in chunks for of_part in of_round for w in of_part]
+def assemble(place, mine, theirs):
+    count, width = mine[0].shape
+    rows = len(mine)
 
     def kernel(place_ref, *refs):
-        row, group, frame, core = (place_ref[i] for i in range(4))
-        x_refs, w_refs = refs[: 2 * slices], refs[2 * slices : 2 * slices + len(flat)]
-        q_keep, kv_keep, send, x_all, q_all = refs[2 * slices + len(flat) :]
-        for c in range(slices):
-            x_all[c, frame] = x_refs[c][0]
-            x_all[c, 1 - frame] = x_refs[slices + c][0]
-        for part in range(3):
-            acc = None
-            for k in range(slices):
-                at = (row + slices - k) % slices
-                for g in range(2):
-                    start = pl.multiple_of((group + g) % 2 * half, half)
-                    piece = x_all[at, :, :, pl.ds(start, half)].reshape(2 * count, half)
-                    w_ref = w_refs[(k * 3 + part) * 2 + g]
-                    term = jnp.dot(piece, w_ref[...], preferred_element_type=jnp.float32)
-                    acc = term if acc is None else acc + term
-            if part == 0:
-                q_all[...] = acc.reshape(2, count, cols)
-                own = pl.multiple_of(core * BS, BS)
-                other = pl.multiple_of((1 - core) * BS, BS)
-                q_keep[0] = q_all[:, pl.ds(own, BS), :].reshape(2 * BS, cols)
-                for f in range(2):
-                    send[0, 2 * count :, f * cols : (f + 1) * cols] = q_all[f, pl.ds(other, BS), :].astype(
-                        jnp.bfloat16
-                    )
-            else:
-                where = slice((part - 1) * cols, part * cols)
-                kv_keep[0, :, where] = acc
-                send[0, : 2 * count, where] = acc.astype(jnp.bfloat16)
-
-    def at_row(*shape):
-        return pl.BlockSpec((1, *shape), lambda i, *_: (i,) + (0,) * len(shape))
-
-    def whole(shape):
-        return pl.BlockSpec(shape, lambda i, *_: (0,) * len(shape))
-
-    shapes = ((2 * BS, cols), (2 * count, 2 * cols), (2 * count + BS, 2 * cols))
-    flops = 2 * peers * 2 * count * slices * depth * 3 * cols
+        row, frame = place_ref[0], place_ref[2]
+        out_ref, sems = refs[2 * rows], refs[2 * rows + 1]
+        copies = []
+        for i in range(2 * rows):
+            place_at = out_ref.at[row ^ (i % rows), (frame + i // rows) % 2]
+            copies.append(pltpu.make_async_copy(refs[i], place_at, sems.at[i]))
+            copies[-1].start()
+        for copy in copies:
+            copy.wait()
+
     return pl.pallas_call(
         kernel,
-        out_shape=(
-            jax.ShapeDtypeStruct((peers, *shapes[0]), jnp.float32),
-            jax.ShapeDtypeStruct((peers, *shapes[1]), jnp.float32),
-            jax.ShapeDtypeStruct((peers, *shapes[2]), jnp.bfloat16),
-        ),
+        out_shape=jax.ShapeDtypeStruct((rows, 2, count, width), jnp.bfloat16),
         grid_spec=pltpu.PrefetchScalarGridSpec(
             num_scalar_prefetch=1,
-            grid=(peers,),
-            in_specs=[at_row(count, depth)] * (2 * slices) + [whole(w.shape) for w in flat],
-            out_specs=tuple(at_row(*shape) for shape in shapes),
-            scratch_shapes=[
-                pltpu.VMEM((slices, 2, count, depth), jnp.bfloat16),
-                pltpu.VMEM((2, count, cols), jnp.float32),
-            ],
+            grid=(),
+            in_specs=[pl.BlockSpec(memory_space=pl.ANY)] * (2 * rows),
+            out_specs=pl.BlockSpec(memory_space=pl.ANY),
+            scratch_shapes=[pltpu.SemaphoreType.DMA((2 * rows,))],
         ),
-        compiler_params=pltpu.CompilerParams(vmem_limit_bytes=VMEM_BYTES),
-        cost_estimate=pl.CostEstimate(flops=flops, bytes_accessed=flops // 300, transcendentals=0),
-    )(place, *mine, *theirs, *flat)
+        cost_estimate=pl.CostEstimate(flops=0, bytes_accessed=8 * rows * count * width, transcendentals=0),
+    )(place, *mine, *theirs)
+
+
+def project(place, tokens, chunks):
+    rows, _, count, width = tokens.shape
+    _, half, cols = chunks[0][0].shape
+    slices = len(chunks)
+    flat = [w for of_round in chunks for w in of_round]
+    total_rows = rows * 2 * count
+
+    def kernel(place_ref, x_ref, *refs):
+        row, group, core = place_ref[0], place_ref[1], place_ref[3]
+        w_refs = refs[: len(flat)]
+        q_keep, kv_keep, send, total = refs[len(flat) :]
+        acc = None
+        for k in range(slices):
+            for g in range(2):
+                at = (row + slices - k) % slices * (2 * half) + (group + g) % 2 * half
+                piece = x_ref[:, :, :, pl.ds(pl.multiple_of(at, half), half)].reshape(-1, half)
+                w_ref = w_refs[2 * k + g]
+                weight = jnp.concatenate([w_ref[part] for part in range(3)], axis=1)
+                term = jnp.dot(piece, weight, preferred_element_type=jnp.float32)
+                acc = term if acc is None else acc + term
+        kv_part = acc[:, cols:].reshape(rows, 2 * count, 2 * cols)
+        kv_keep[...] = kv_part
+        send[:, : 2 * count, :] = kv_part.astype(jnp.bfloat16)
+        total[...] = acc[:, :cols].reshape(rows, 2, count, cols)
+        own = pl.multiple_of(core * BS, BS)
+        other = pl.multiple_of((1 - core) * BS, BS)
+        q_keep[...] = total[:, :, pl.ds(own, BS), :].reshape(q_keep.shape)
+        for f in range(2):
+            at = slice(f * cols, (f + 1) * cols)
+            send[:, 2 * count :, at] = total[:, f, pl.ds(other, BS), :].astype(jnp.bfloat16)
+
+    flops = 2 * total_rows * width * 3 * cols
+    return call(
+        kernel,
+        (
+            jax.ShapeDtypeStruct((rows, 2 * BS, cols), jnp.float32),
+            jax.ShapeDtypeStruct((rows, 2 * count, 2 * cols), jnp.float32),
+            jax.ShapeDtypeStruct((rows, 2 * count + BS, 2 * cols), jnp.bfloat16),
+        ),
+        [place],
+        [tokens, *flat],
+        scratch=[pltpu.VMEM((rows, 2, count, cols), jnp.float32)],
+        flops=flops,
+        read=flops // 300,
+    )
 
 
 def attend_all(place, members, counts, queries, keyvals, more):
@@ -247,15 +256,19 @@
 
 
 def mix(place, attended, w_parts):
-    blocks, block_len, cols = attended[0].shape
+    blocks, block_len, _ = attended[0][0].shape
+    widths = [a.shape[2] for a in attended[0]]
+    cols, parts = sum(widths), len(widths)
     width = w_parts[0].shape[1]
 
     def kernel(place_ref, *refs):
         row, _, frame, core = (place_ref[i] for i in range(4))
-        a_refs, w_refs = refs[:4], refs[4:8]
-        keep, over_x, over_z, over_both, a_all, sums = refs[8:]
+        w_refs = refs[4 * parts : 4 * parts + 4]
+        keep, over_x, over_z, over_both, a_all, sums = refs[4 * parts + 4 :]
         for s in range(4):
-            a_all[s] = a_refs[s][...].reshape(blocks * block_len, cols)
+            for i, of_group in enumerate(widths):
+                at = slice(sum(widths[:i]), sum(widths[: i + 1]))
+                a_all[s, :, at] = refs[s * parts + i][...].reshape(blocks * block_len, of_group)
 
         def term(w_ref, side):
             first = a_all[(2 * side) ^ row]
@@ -279,7 +292,7 @@
         kernel,
         (jax.ShapeDtypeStruct(shape, jnp.float32), sent, sent, sent),
         [place],
-        [*attended, *w_parts],
+        [*(a for of_row in attended for a in of_row), *w_parts],
         scratch=[
             pltpu.VMEM((4, blocks * block_len, cols), jnp.bfloat16),
             pltpu.VMEM((blocks, 2, BS, width), jnp.float32),
@@ -321,13 +334,13 @@
     half = depth // 2
     place = jnp.stack([row, group, frame, core]).astype(jnp.int32)
 
-    gathered = []
-    for c in range(span):
-        slice_at = (core * span + c) * depth
-        mine = lax.dynamic_slice_in_dim(latents[0], slice_at, depth, axis=1)
-        gathered.append(lax.all_gather(mine, "rows", axis=0))
+    mine = [lax.dynamic_slice_in_dim(latents[0], core * span * depth, span * depth, axis=1)]
+    mine += [swap(mine[0], "rows", s) for s in range(1, rows_n)]
+    theirs = [swap(x, "frames") for x in mine]
+    tokens = assemble(place, mine, theirs)
 
     tables = jnp.concatenate([win_blocks, win_counts[:, None], block_window[:, None]], axis=1)
+    tables = after(tables, mine[1])
     found = [tables] + [swap(tables, "rows", s) for s in range(1, rows_n)]
     tables = jnp.stack(found)[row ^ jnp.arange(rows_n)].reshape(rows_n * heads_n, MAXB + 2)
     windows = lax.dynamic_index_in_dim(
@@ -336,34 +349,43 @@
     picked = tables[windows]
     members, counts = picked[:, :MAXB].reshape(-1), picked[:, MAXB]
 
+    across = swap(after(w_out, mine[1]), "heads")
+    beside = swap(after(w_out, mine[3]), "rows")
+
     by_part = w_qkv.transpose(1, 0, 2)
-    here = []
-    for k in range(span):
-        pairs = [
-            (r * heads_n + h, (h * span + (k + r) % span) * heads_n + r // span)
-            for r in range(rows_n)
-            for h in range(heads_n)
-        ]
-        for part in range(3):
+    last = cols // (3 * HD) * HD
+    waits = [[mine[1]], [mine[2]], [mine[3], theirs[0], members, counts], [theirs[1], across]]
+    here, there = [], []
+    for first, wide in ((0, cols - last), (cols - last, last)):
+        for k in range(span):
+            pairs = [
+                (r * heads_n + h, (h * span + (k + r) % span) * heads_n + r // span)
+                for r in range(rows_n)
+                for h in range(heads_n)
+            ]
             piece = lax.dynamic_slice(
-                by_part[part], (group * half, (k + row) % span * cols), (half, cols)
+                by_part, (0, group * half, (k + row) % span * cols + first), (3, half, wide)
             )
-            if len(here) >= 2:
-                piece = after(piece, here[-2])
-            if len(here) == 3 * span - 1:
-                piece = after(piece, members, counts)
+            piece = after(piece, *waits[len(here)], *here[-2:-1])
             here.append(lax.ppermute(piece, ("rows", "heads"), pairs))
-    chunks = [
-        [(here[3 * k + part], swap(here[3 * k + part], "groups")) for part in range(3)] for k in range(span)
-    ]
-    theirs = [swap(after(g, here[2 + 2 * c]), "frames") for c, g in enumerate(gathered)]
-
-    queries, keyvals, send = project(place, gathered, theirs, chunks)
-    same, diff = attend_all(place, members, counts, queries, keyvals, swap(send, "heads"))
-    attended = [same] + [swap(same if s % 2 == 0 else diff, "rows", s) for s in range(1, rows_n)]
-
-    across = swap(after(w_out, here[1]), "heads")
-    beside = swap(after(w_out, here[-1]), "rows")
+    for i, piece in enumerate(here):
+        there.append(swap(after(piece, tokens) if i == 2 else piece, "groups"))
+
+    attended = [[] for _ in range(rows_n)]
+    send = None
+    for part in range(2):
+        chunks = [[here[i], there[i]] for i in range(part * span, (part + 1) * span)]
+        if part:
+            chunks[-1][-1] = after(chunks[-1][-1], send)
+        queries, keyvals, send = project(place, tokens, chunks)
+        if part == 0:
+            keyvals = after(keyvals, beside)
+        else:
+            keyvals = after(keyvals, attended[0][0])
+        same, diff = attend_all(place, members, counts, queries, keyvals, swap(send, "heads"))
+        for s in range(rows_n):
+            attended[s].append(swap(same if s % 2 == 0 else diff, "rows", s) if s else same)
+
     keep, over_x, over_z, over_both = mix(
         place, attended, [w_out, beside, across, swap(beside, "heads")]
     )

time: 185 us -> 277 us (1.50)
  Pallas kernels: 22.6 us -> 116 us
  blocking collectives: 52.7 us -> 0 us
  starting transfers between devices: 38.1 us -> 65.4 us
  waiting for transfers between devices: 57.9 us -> 82.6 us
    pallas_call x1, Pallas kernels: 10.3 us -> 97.1 us  [assemble(): pl.pallas_call(kernel, out_shape=jax.ShapeDtypeStruct((rows, 2, count, wi...]
    all_gather x2 -> x0, blocking collectives: 52.7 us -> none  [by_heads(): gathered.append(lax.all_gather(mine, 'rows', axis=0))]
    ppermute x20 -> x27, waiting for transfers between devices: 41.2 us -> 78.6 us  [swap(): return lax.ppermute(value, axis, [(i, i ^ step) for i in range(peers)])]
    ppermute x20 -> x27, starting transfers between devices: 30.9 us -> 51.1 us  [swap(): return lax.ppermute(value, axis, [(i, i ^ step) for i in range(peers)])]
    ppermute x6 -> x4, waiting for transfers between devices: 12.4 us -> 0.01 us  [by_heads(): here.append(lax.ppermute(piece, ('rows', 'heads'), pairs))]
    ppermute x6 -> x4, starting transfers between devices: 6.08 us -> 14.2 us  [by_heads(): here.append(lax.ppermute(piece, ('rows', 'heads'), pairs))]
    pallas_call x3 -> x6, Pallas kernels: 12.3 us -> 19.3 us  [call(): pl.pallas_call(kernel, out_shape=out_shape, grid_spec=pltpu.PrefetchScala...]
  transfers between devices with their start and end apart: 27 -> 32, of which waited for: 13 -> 14; matrix products, arithmetic and copies ran while one was open for 4% -> 3% of each run, Pallas kernels for 9% -> 40%
where the time goes in v5:
time: 277 us
  Pallas kernels  116 us (42%)
  waiting for transfers between devices  82.6 us (30%)
  starting transfers between devices  65.4 us (24%)
  local copies, waits for them, and re-layouts  10.5 us (4%)
    pallas_call x1, Pallas kernels, assemble(): pl.pallas_call(kernel, out_shape=jax.ShapeDtypeStruct((rows, 2, count, wi...  97.1 us
    ppermute x27, waiting for transfers between devices, swap(): return lax.ppermute(value, axis, [(i, i ^ step) for i in range(peers)])  78.6 us
    ppermute x27, starting transfers between devices, swap(): return lax.ppermute(value, axis, [(i, i ^ step) for i in range(peers)])  51.1 us
    pallas_call x6, Pallas kernels, call(): pl.pallas_call(kernel, out_shape=out_shape, grid_spec=pltpu.PrefetchScala...  19.3 us
    ppermute x4, starting transfers between devices, by_heads(): here.append(lax.ppermute(piece, ('rows', 'heads'), pairs))  14.2 us
  transfers between devices with their start and end apart: 32, of which 14 were waited for; matrix products, arithmetic and copies ran while one was open for 3% of the time, Pallas kernels for 40%

profile of v5, /device:TPU:0, one launch (start us, length us, event | category | flops | bytes accessed | tf_op | source)
XLA Modules:
  0.0 276.8 jit_solution(8408307135711495765)
XLA Ops:
  0.0 1.1 copy-done
  1.2 3.1 %collective-permute-start = (bf16[128,1536]{1,0:T(8,128)(2,1)S(1)}, bf16[128,1536]{1,0:T(8,128)(2,1)}, u32[]{:S(2)}, u32[]{:S(2)}) collective-permute-start(bf16[128,1536]{1,0:T(8,128)(2,1)S(1)} %dynamic-slice_bitcast_fusion.2.refs_0_), channel_id=1, source_target_pairs={{0,4},{4,0},{8,12},{12,8},{1,5},{5,1},{9,13},{13,9},{2,6},{6,2},{1... | collective-permute-start | bytes 1179656 | tf_op jit(solution)/shard_map/ppermute | solution.py:106
  4.3 2.6 collective-permute-start.4
  6.9 2.4 dynamic-slice_bitcast_fusion
  9.3 11.9 %collective-permute-done.refs_1_ = bf16[128,1536]{1,0:T(8,128)(2,1)} collective-permute-done((bf16[128,1536]{1,0:T(8,128)(2,1)S(1)}, bf16[128,1536]{1,0:T(8,128)(2,1)}, u32[]{:S(2)}, u32[]{:S(2)}) %collective-permute-start) | collective-permute-done | bytes 393248 | tf_op jit(solution)/shard_map/ppermute | solution.py:106
  21.2 6.0 %collective-permute-start.10 = (bf16[3,384,256]{2,1,0:T(8,128)(2,1)}, bf16[3,384,256]{2,1,0:T(8,128)(2,1)}, u32[]{:S(2)}, u32[]{:S(2)}) collective-permute-start(bf16[3,384,256]{2,1,0:T(8,128)(2,1)} %get-tuple-element.31), channel_id=1, source_target_pairs={{0,0},{1,8},{4,4},{5,12},{8,1},{9,9},{12,5},{13,13},{2,2},{3,10},{... | collective-permute-start | bytes 1769480 | tf_op jit(solution)/shard_map/ppermute | solution.py:370
  27.1 7.4 %collective-permute-done.4.refs_2_ = bf16[128,1536]{1,0:T(8,128)(2,1)S(1)} collective-permute-done((bf16[128,1536]{1,0:T(8,128)(2,1)S(1)}, bf16[128,1536]{1,0:T(8,128)(2,1)S(1)}, u32[]{:S(2)}, u32[]{:S(2)}) %collective-permute-start.4) | collective-permute-done | bytes 393248 | tf_op jit(solution)/shard_map/ppermute | solution.py:106
  34.6 5.5 %collective-permute-start.12 = (bf16[3,384,256]{2,1,0:T(8,128)(2,1)}, bf16[3,384,256]{2,1,0:T(8,128)(2,1)}, u32[]{:S(2)}, u32[]{:S(2)}) collective-permute-start(bf16[3,384,256]{2,1,0:T(8,128)(2,1)} %get-tuple-element.32), channel_id=1, source_target_pairs={{0,4},{1,12},{4,0},{5,8},{8,5},{9,13},{12,1},{13,9},{2,6},{3,14},{... | collective-permute-start | bytes 1769480 | tf_op jit(solution)/shard_map/ppermute | solution.py:370
  40.1 1.5 collective-permute-start.6
  42.1 2.4 collective-permute-start.18
  44.8 5.3 %collective-permute-done.6.refs_4_ = bf16[128,1536]{1,0:T(8,128)(2,1)} collective-permute-done((bf16[128,1536]{1,0:T(8,128)(2,1)S(1)}, bf16[128,1536]{1,0:T(8,128)(2,1)}, u32[]{:S(2)}, u32[]{:S(2)}) %collective-permute-start.6) | collective-permute-done | bytes 393248 | tf_op jit(solution)/shard_map/ppermute | solution.py:106
  50.8 4.8 %collective-permute-done.3 = s32[2,6]{1,0:T(2,128)S(1)} collective-permute-done((s32[2,6]{1,0:T(2,128)S(1)}, s32[2,6]{1,0:T(2,128)S(1)}, u32[]{:S(2)}, u32[]{:S(2)}) %collective-permute-start.3) | collective-permute-done | bytes 80 | tf_op jit(solution)/shard_map/ppermute | solution.py:106
  55.6 11.5 %collective-permute-start.1 = (s32[2,6]{1,0:T(2,128)S(1)}, s32[2,6]{1,0:T(2,128)S(1)}, u32[]{:S(2)}, u32[]{:S(2)}) collective-permute-start(s32[2,6]{1,0:T(2,128)S(1)} %pad_add_fusion.1), channel_id=1, source_target_pairs={{0,4},{4,0},{8,12},{12,8},{1,5},{5,1},{9,13},{13,9},{2,6},{6,2},{1... | collective-permute-start | bytes 152 | tf_op jit(solution)/shard_map/ppermute | solution.py:106
  67.0 1.5 collective-permute-done.1
  68.6 1.1 collective-permute-start.2
  69.7 3.4 %collective-permute-done.2 = s32[2,6]{1,0:T(2,128)S(1)} collective-permute-done((s32[2,6]{1,0:T(2,128)S(1)}, s32[2,6]{1,0:T(2,128)S(1)}, u32[]{:S(2)}, u32[]{:S(2)}) %collective-permute-start.2) | collective-permute-done | bytes 80 | tf_op jit(solution)/shard_map/ppermute | solution.py:106
  73.6 1.5 collective-permute-start.9
  75.2 2.1 collective-permute-start.14
  77.3 1.6 collective-permute-start.11
  80.0 1.9 dynamic-slice_bitcast_fusion.3
  81.9 1.3 collective-permute-done.9.refs_7_
  83.2 1.5 collective-permute-start.8
  87.2 4.5 %collective-permute-done.8.refs_6_ = bf16[128,1536]{1,0:T(8,128)(2,1)S(1)} collective-permute-done((bf16[128,1536]{1,0:T(8,128)(2,1)}, bf16[128,1536]{1,0:T(8,128)(2,1)S(1)}, u32[]{:S(2)}, u32[]{:S(2)}) %collective-permute-start.8) | collective-permute-done | bytes 393248 | tf_op jit(solution)/shard_map/ppermute | solution.py:106
  92.5 97.1 %shard_map.64.x_ref = bf16[4,2,128,1536]{3,2,1,0:T(8,128)(2,1)} custom-call(s32[4]{0:T(128)} %pad_add_fusion.2.place_ref, bf16[128,1536]{1,0:T(8,128)(2,1)} %copy-done.4, bf16[128,1536]{1,0:T(8,128)(2,1)} %collective-permute-done.refs_1_, bf16[128,1536]{1,0:T(8,128)(2,1)} %copy-done.5, bf16[128,1536]{1,0:T(8,128)(2,1)} %collective-permute-done.5.refs_3_, ...), custom_call_target="tpu_custom_call" | custom-call | bytes 6291456 | tf_op jit(solution)/shard_map/pallas_call | solution.py:144
  189.7 1.6 collective-permute-start.16
  191.3 1.1 collective-permute-start.19
  192.4 1.9 copy-done.1
  194.3 5.6 %shard_map.65 = (f32[4,128,256]{2,1,0:T(8,128)S(1)}, f32[4,256,512]{2,1,0:T(8,128)S(1)}, bf16[4,320,512]{2,1,0:T(8,128)(2,1)S(1)}) custom-call(s32[4]{0:T(128)S(1)} %copy-done.3, bf16[4,2,128,1536]{3,2,1,0:T(8,128)(2,1)S(1)} %copy-done.1, bf16[3,384,256]{2,1,0:T(8,128)(2,1)} %collective-permute-done.10.refs_0_, ...), custom_call_target="tpu_custom_call" | custom-call | flops 2415919104 | bytes 8053063 | tf_op jit(solution)/shard_map/pallas_call | solution.py:114
  199.9 3.7 %collective-permute-start.15 = (bf16[4,320,512]{2,1,0:T(8,128)(2,1)S(1)}, bf16[4,320,512]{2,1,0:T(8,128)(2,1)S(1)}, u32[]{:S(2)}, u32[]{:S(2)}) collective-permute-start(bf16[4,320,512]{2,1,0:T(8,128)(2,1)S(1)} %get-tuple-element.37), channel_id=1, source_target_pairs={{0,1},{1,0},{2,3},{3,2},{4,5},{5,4},{6,7},{7,6},{8,9},{9,8},{10,11... | collective-permute-start | bytes 3932168 | tf_op jit(solution)/shard_map/ppermute | solution.py:106
  203.7 1.6 collective-permute-start.20
  205.8 6.2 %collective-permute-done.20.refs_3_ = bf16[3,384,128]{2,1,0:T(8,128)(2,1)S(1)} collective-permute-done((bf16[3,384,128]{2,1,0:T(8,128)(2,1)S(1)}, bf16[3,384,128]{2,1,0:T(8,128)(2,1)S(1)}, u32[]{:S(2)}, u32[]{:S(2)}) %collective-permute-start.20) | collective-permute-done | bytes 294944 | tf_op jit(solution)/shard_map/ppermute | solution.py:106
  211.9 6.3 %collective-permute-done.17.refs_1_ = bf16[3,384,128]{2,1,0:T(8,128)(2,1)S(1)} collective-permute-done((bf16[3,384,128]{2,1,0:T(8,128)(2,1)S(1)}, bf16[3,384,128]{2,1,0:T(8,128)(2,1)S(1)}, u32[]{:S(2)}, u32[]{:S(2)}) %collective-permute-start.17) | collective-permute-done | bytes 294944 | tf_op jit(solution)/shard_map/ppermute | solution.py:106
  218.2 2.6 shard_map.67
  220.9 1.6 collective-permute-start.21
  222.5 3.8 %shard_map.66 = (bf16[2,128,256]{2,1,0:T(8,128)(2,1)S(1)}, bf16[2,128,256]{2,1,0:T(8,128)(2,1)S(1)}) custom-call(s32[4]{0:T(128)S(1)} %copy-done.3, s32[16]{0:T(128)S(1)} %reshape.24.members_ref, s32[4]{0:T(128)S(1)} %slice_reduce_fusion.1.counts_ref, f32[4,128,256]{2,1,0:T(8,128)S(1)} %get-tuple-element.33.q_ref, ...), custom_call_target="tpu_custom_call" | custom-call | flops 268435456 | bytes 2097152 | tf_op jit(solution)/shard_map/pallas_call | solution.py:114
  226.3 2.2 shard_map.68
  229.1 1.4 collective-permute-start.22
  230.6 1.8 collective-permute-start.24
  232.4 1.4 collective-permute-start.26
  233.8 2.0 collective-permute-start.25
  235.8 0.9 collective-permute-start.27
  236.7 13.0 %collective-permute-done.25.refs_5_ = bf16[2,128,128]{2,1,0:T(8,128)(2,1)S(1)} collective-permute-done((bf16[2,128,128]{2,1,0:T(8,128)(2,1)S(1)}, bf16[2,128,128]{2,1,0:T(8,128)(2,1)S(1)}, u32[]{:S(2)}, u32[]{:S(2)}) %collective-permute-start.25) | collective-permute-done | bytes 65568 | tf_op jit(solution)/shard_map/ppermute | solution.py:106
  249.7 3.7 %shard_map.69 = (f32[2,64,768]{2,1,0:T(8,128)S(1)}, bf16[2,64,768]{2,1,0:T(8,128)(2,1)S(1)}, bf16[2,64,768]{2,1,0:T(8,128)(2,1)S(1)}, bf16[2,64,768]{2,1,0:T(8,128)(2,1)S(1)}) custom-call(s32[4]{0:T(128)S(1)} %copy-done.3, bf16[2,128,256]{2,1,0:T(8,128)(2,1)S(1)} %get-tuple-element.38.refs_0_, bf16[2,128,128]{2,1,0:T(8,128)(2,1)S(1)} %get-tuple-element.48.refs_1_, ...), custom_call_target="tpu_custom_call" | custom-call | flops 1207959552 | bytes 4718592 | tf_op jit(solution)/shard_map/pallas_call | solution.py:114
  253.4 1.5 collective-permute-start.29
  255.0 3.5 %collective-permute-start.30 = (bf16[2,64,768]{2,1,0:T(8,128)(2,1)S(1)}, bf16[2,64,768]{2,1,0:T(8,128)(2,1)S(1)}, u32[]{:S(2)}, u32[]{:S(2)}) collective-permute-start(bf16[2,64,768]{2,1,0:T(8,128)(2,1)S(1)} %get-tuple-element.53), channel_id=1, source_target_pairs={{0,8},{4,12},{8,0},{12,4},{1,9},{5,13},{9,1},{13,5},{2,10},{6,14},... | collective-permute-start | bytes 589832 | tf_op jit(solution)/shard_map/ppermute | solution.py:106
  259.2 12.3 %collective-permute-done.30.z_ref = bf16[2,64,768]{2,1,0:T(8,128)(2,1)S(1)} collective-permute-done((bf16[2,64,768]{2,1,0:T(8,128)(2,1)S(1)}, bf16[2,64,768]{2,1,0:T(8,128)(2,1)S(1)}, u32[]{:S(2)}, u32[]{:S(2)}) %collective-permute-start.30) | collective-permute-done | bytes 196640 | tf_op jit(solution)/shard_map/ppermute | solution.py:106
  271.5 3.9 %collective-permute-done.31.both_ref = bf16[2,64,768]{2,1,0:T(8,128)(2,1)S(1)} collective-permute-done((bf16[2,64,768]{2,1,0:T(8,128)(2,1)S(1)}, bf16[2,64,768]{2,1,0:T(8,128)(2,1)S(1)}, u32[]{:S(2)}, u32[]{:S(2)}) %collective-permute-start.31) | collective-permute-done | bytes 196640 | tf_op jit(solution)/shard_map/ppermute | solution.py:394
  275.4 1.4 shard_map.70
  (69 shorter events, 8.6 us)
Async XLA Ops:
  0.0 1.1 copy-start
  1.2 80.8 %copy-start.4 = (bf16[128,1536]{1,0:T(8,128)(2,1)}, bf16[128,1536]{1,0:T(8,128)(2,1)S(1)}, u32[]{:S(2)}) copy-start(bf16[128,1536]{1,0:T(8,128)(2,1)S(1)} %dynamic-slice_bitcast_fusion.2.refs_0_) | copy-start | bytes 1179652
  1.2 40.9 %copy-start.2 = (bf16[768,768]{1,0:T(8,128)(2,1)S(1)}, bf16[768,768]{1,0:T(8,128)(2,1)}, u32[]{:S(2)}) copy-start(bf16[768,768]{1,0:T(8,128)(2,1)} %refs_8_.1) | copy-start | bytes 3538948
  1.2 43.4 %copy-start.12 = (s32[2]{0:T(128)S(1)}, s32[2]{0:T(128)}, u32[]{:S(2)}) copy-start(s32[2]{0:T(128)} %param.11) | copy-start | bytes 28
  1.2 43.5 %copy-start.13 = (s32[2]{0:T(128)S(1)}, s32[2]{0:T(128)}, u32[]{:S(2)}) copy-start(s32[2]{0:T(128)} %param.10) | copy-start | bytes 28
  1.2 43.5 %copy-start.8 = (s32[2,4]{1,0:T(2,128)S(1)}, s32[2,4]{1,0:T(2,128)}, u32[]{:S(2)}) copy-start(s32[2,4]{1,0:T(2,128)} %param.9) | copy-start | bytes 100
  1.2 20.0 %collective-permute-start = (bf16[128,1536]{1,0:T(8,128)(2,1)S(1)}, bf16[128,1536]{1,0:T(8,128)(2,1)}, u32[]{:S(2)}, u32[]{:S(2)}) collective-permute-start(bf16[128,1536]{1,0:T(8,128)(2,1)S(1)} %dynamic-slice_bitcast_fusion.2.refs_0_), channel_id=1, source_target_pairs={{0,4},{4,0},{8,12},{12,8},{1,5},{5,1},{9,13},{13,9},{2,6},{6,2},{1... | collective-permute-start | bytes 1179656 | tf_op jit(solution)/shard_map/ppermute | solution.py:106
  4.3 30.2 %collective-permute-start.4 = (bf16[128,1536]{1,0:T(8,128)(2,1)S(1)}, bf16[128,1536]{1,0:T(8,128)(2,1)S(1)}, u32[]{:S(2)}, u32[]{:S(2)}) collective-permute-start(bf16[128,1536]{1,0:T(8,128)(2,1)S(1)} %dynamic-slice_bitcast_fusion.2.refs_0_), channel_id=1, source_target_pairs={{0,8},{4,12},{8,0},{12,4},{1,9},{5,13},{9,1},{13,5},{2,10},{6,14},... | collective-permute-start | bytes 1179656 | tf_op jit(solution)/shard_map/ppermute | solution.py:106
  6.9 35.2 %collective-permute-start.5 = (bf16[128,1536]{1,0:T(8,128)(2,1)S(1)}, bf16[128,1536]{1,0:T(8,128)(2,1)}, u32[]{:S(2)}, u32[]{:S(2)}) collective-permute-start(bf16[128,1536]{1,0:T(8,128)(2,1)S(1)} %dynamic-slice_bitcast_fusion.2.refs_0_), channel_id=1, source_target_pairs={{0,12},{4,8},{8,4},{12,0},{1,13},{5,9},{9,5},{13,1},{2,14},{6,10},... | collective-permute-start | bytes 1179656 | tf_op jit(solution)/shard_map/ppermute | solution.py:106
  21.2 56.1 %collective-permute-start.10 = (bf16[3,384,256]{2,1,0:T(8,128)(2,1)}, bf16[3,384,256]{2,1,0:T(8,128)(2,1)}, u32[]{:S(2)}, u32[]{:S(2)}) collective-permute-start(bf16[3,384,256]{2,1,0:T(8,128)(2,1)} %get-tuple-element.31), channel_id=1, source_target_pairs={{0,0},{1,8},{4,4},{5,12},{8,1},{9,9},{12,5},{13,13},{2,2},{3,10},{... | collective-permute-start | bytes 1769480 | tf_op jit(solution)/shard_map/ppermute | solution.py:370
  34.6 7.6 %copy-start.5 = (bf16[128,1536]{1,0:T(8,128)(2,1)}, bf16[128,1536]{1,0:T(8,128)(2,1)S(1)}, u32[]{:S(2)}) copy-start(bf16[128,1536]{1,0:T(8,128)(2,1)S(1)} %collective-permute-done.4.refs_2_) | copy-start | bytes 1179652
  34.6 44.3 %collective-permute-start.12 = (bf16[3,384,256]{2,1,0:T(8,128)(2,1)}, bf16[3,384,256]{2,1,0:T(8,128)(2,1)}, u32[]{:S(2)}, u32[]{:S(2)}) collective-permute-start(bf16[3,384,256]{2,1,0:T(8,128)(2,1)} %get-tuple-element.32), channel_id=1, source_target_pairs={{0,4},{1,12},{4,0},{5,8},{8,5},{9,13},{12,1},{13,9},{2,6},{3,14},{... | collective-permute-start | bytes 1769480 | tf_op jit(solution)/shard_map/ppermute | solution.py:370
  40.1 10.1 %collective-permute-start.6 = (bf16[128,1536]{1,0:T(8,128)(2,1)S(1)}, bf16[128,1536]{1,0:T(8,128)(2,1)}, u32[]{:S(2)}, u32[]{:S(2)}) collective-permute-start(bf16[128,1536]{1,0:T(8,128)(2,1)S(1)} %dynamic-slice_bitcast_fusion.2.refs_0_), channel_id=1, source_target_pairs={{0,2},{2,0},{1,3},{3,1},{4,6},{6,4},{5,7},{7,5},{8,10},{10,8},{9,1... | collective-permute-start | bytes 1179656 | tf_op jit(solution)/shard_map/ppermute | solution.py:106
  41.6 33.6 %collective-permute-start.7 = (bf16[128,1536]{1,0:T(8,128)(2,1)}, bf16[128,1536]{1,0:T(8,128)(2,1)}, u32[]{:S(2)}, u32[]{:S(2)}) collective-permute-start(bf16[128,1536]{1,0:T(8,128)(2,1)} %collective-permute-done.refs_1_), channel_id=1, source_target_pairs={{0,2},{2,0},{1,3},{3,1},{4,6},{6,4},{5,7},{7,5},{8,10},{10,8},{9,1... | collective-permute-start | bytes 1179656 | tf_op jit(solution)/shard_map/ppermute | solution.py:106
  42.1 149.2 %collective-permute-start.18 = (bf16[768,768]{1,0:T(8,128)(2,1)S(1)}, bf16[768,768]{1,0:T(8,128)(2,1)S(1)}, u32[]{:S(2)}, u32[]{:S(2)}) collective-permute-start(bf16[768,768]{1,0:T(8,128)(2,1)S(1)} %copy-done.2), channel_id=1, source_target_pairs={{0,1},{1,0},{2,3},{3,2},{4,5},{5,4},{6,7},{7,6},{8,9},{9,8},{10,11... | collective-permute-start | bytes 3538952 | tf_op jit(solution)/shard_map/ppermute | solution.py:106
  44.8 30.4 %copy-start.7 = (s32[2,6]{1,0:T(2,128)}, s32[2,6]{1,0:T(2,128)S(1)}, u32[]{:S(2)}) copy-start(s32[2,6]{1,0:T(2,128)S(1)} %pad_add_fusion.1) | copy-start | bytes 148
  50.2 5.4 %collective-permute-start.3 = (s32[2,6]{1,0:T(2,128)S(1)}, s32[2,6]{1,0:T(2,128)S(1)}, u32[]{:S(2)}, u32[]{:S(2)}) collective-permute-start(s32[2,6]{1,0:T(2,128)S(1)} %pad_add_fusion.1), channel_id=1, source_target_pairs={{0,12},{4,8},{8,4},{12,0},{1,13},{5,9},{9,5},{13,1},{2,14},{6,10},... | collective-permute-start | bytes 152 | tf_op jit(solution)/shard_map/ppermute | solution.py:106
  55.6 17.5 %copy-start.9 = (s32[2,6]{1,0:T(2,128)}, s32[2,6]{1,0:T(2,128)S(1)}, u32[]{:S(2)}) copy-start(s32[2,6]{1,0:T(2,128)S(1)} %collective-permute-done.3) | copy-start | bytes 148
  55.6 13.0 %collective-permute-start.1 = (s32[2,6]{1,0:T(2,128)S(1)}, s32[2,6]{1,0:T(2,128)S(1)}, u32[]{:S(2)}, u32[]{:S(2)}) collective-permute-start(s32[2,6]{1,0:T(2,128)S(1)} %pad_add_fusion.1), channel_id=1, source_target_pairs={{0,4},{4,0},{8,12},{12,8},{1,5},{5,1},{9,13},{13,9},{2,6},{6,2},{1... | collective-permute-start | bytes 152 | tf_op jit(solution)/shard_map/ppermute | solution.py:106
  68.6 4.5 %copy-start.10 = (s32[2,6]{1,0:T(2,128)}, s32[2,6]{1,0:T(2,128)S(1)}, u32[]{:S(2)}) copy-start(s32[2,6]{1,0:T(2,128)S(1)} %collective-permute-done.1) | copy-start | bytes 148
  68.6 4.5 %collective-permute-start.2 = (s32[2,6]{1,0:T(2,128)S(1)}, s32[2,6]{1,0:T(2,128)S(1)}, u32[]{:S(2)}, u32[]{:S(2)}) collective-permute-start(s32[2,6]{1,0:T(2,128)S(1)} %pad_add_fusion.1), channel_id=1, source_target_pairs={{0,8},{4,12},{8,0},{12,4},{1,9},{5,13},{9,1},{13,5},{2,10},{6,14},... | collective-permute-start | bytes 152 | tf_op jit(solution)/shard_map/ppermute | solution.py:106
  73.1 0.5 copy-start.11
  73.6 9.6 %collective-permute-start.9 = (bf16[128,1536]{1,0:T(8,128)(2,1)}, bf16[128,1536]{1,0:T(8,128)(2,1)}, u32[]{:S(2)}, u32[]{:S(2)}) collective-permute-start(bf16[128,1536]{1,0:T(8,128)(2,1)} %collective-permute-done.5.refs_3_), channel_id=1, source_target_pairs={{0,2},{2,0},{1,3},{3,1},{4,6},{6,4},{5,7},{7,5},{8,10},{10,8},{9,1... | collective-permute-start | bytes 1179656 | tf_op jit(solution)/shard_map/ppermute | solution.py:106
  75.2 128.4 %collective-permute-start.14 = (bf16[768,768]{1,0:T(8,128)(2,1)S(1)}, bf16[768,768]{1,0:T(8,128)(2,1)}, u32[]{:S(2)}, u32[]{:S(2)}) collective-permute-start(bf16[768,768]{1,0:T(8,128)(2,1)S(1)} %copy-done.2), channel_id=1, source_target_pairs={{0,4},{4,0},{8,12},{12,8},{1,5},{5,1},{9,13},{13,9},{2,6},{6,2},{1... | collective-permute-start | bytes 3538952 | tf_op jit(solution)/shard_map/ppermute | solution.py:106
  77.3 115.1 %collective-permute-start.11 = (bf16[3,384,256]{2,1,0:T(8,128)(2,1)}, bf16[3,384,256]{2,1,0:T(8,128)(2,1)}, u32[]{:S(2)}, u32[]{:S(2)}) collective-permute-start(bf16[3,384,256]{2,1,0:T(8,128)(2,1)} %collective-permute-done.10.refs_0_), channel_id=1, source_target_pairs={{0,16},{16,0},{1,17},{17,1},{2,18},{18,2},{3,19},{19,3},{4,20},{20... | collective-permute-start | bytes 1769480 | tf_op jit(solution)/shard_map/ppermute | solution.py:106
  78.9 113.5 %collective-permute-start.13 = (bf16[3,384,256]{2,1,0:T(8,128)(2,1)}, bf16[3,384,256]{2,1,0:T(8,128)(2,1)}, u32[]{:S(2)}, u32[]{:S(2)}) collective-permute-start(bf16[3,384,256]{2,1,0:T(8,128)(2,1)} %collective-permute-done.12.refs_2_), channel_id=1, source_target_pairs={{0,16},{16,0},{1,17},{17,1},{2,18},{18,2},{3,19},{19,3},{4,20},{20... | collective-permute-start | bytes 1769480 | tf_op jit(solution)/shard_map/ppermute | solution.py:106
  83.2 8.6 %collective-permute-start.8 = (bf16[128,1536]{1,0:T(8,128)(2,1)}, bf16[128,1536]{1,0:T(8,128)(2,1)S(1)}, u32[]{:S(2)}, u32[]{:S(2)}) collective-permute-start(bf16[128,1536]{1,0:T(8,128)(2,1)} %copy-done.5), channel_id=1, source_target_pairs={{0,2},{2,0},{1,3},{3,1},{4,6},{6,4},{5,7},{7,5},{8,10},{10,8},{9,1... | collective-permute-start | bytes 1179656 | tf_op jit(solution)/shard_map/ppermute | solution.py:106
  87.2 105.2 %copy-start.3 = (s32[4]{0:T(128)S(1)}, s32[4]{0:T(128)}, u32[]{:S(2)}) copy-start(s32[4]{0:T(128)} %pad_add_fusion.2.place_ref) | copy-start | bytes 52
  91.8 0.8 copy-start.6
  189.7 14.1 %collective-permute-start.16 = (bf16[3,384,128]{2,1,0:T(8,128)(2,1)}, bf16[3,384,128]{2,1,0:T(8,128)(2,1)S(1)}, u32[]{:S(2)}, u32[]{:S(2)}) collective-permute-start(bf16[3,384,128]{2,1,0:T(8,128)(2,1)} %get-tuple-element.39), channel_id=1, source_target_pairs={{0,0},{1,8},{4,4},{5,12},{8,1},{9,9},{12,5},{13,13},{2,2},{3,10},{... | collective-permute-start | bytes 884744 | tf_op jit(solution)/shard_map/ppermute | solution.py:370
  191.3 12.4 %collective-permute-start.19 = (bf16[3,384,128]{2,1,0:T(8,128)(2,1)}, bf16[3,384,128]{2,1,0:T(8,128)(2,1)S(1)}, u32[]{:S(2)}, u32[]{:S(2)}) collective-permute-start(bf16[3,384,128]{2,1,0:T(8,128)(2,1)} %get-tuple-element.42), channel_id=1, source_target_pairs={{0,4},{1,12},{4,0},{5,8},{8,5},{9,13},{12,1},{13,9},{2,6},{3,14},{... | collective-permute-start | bytes 884744 | tf_op jit(solution)/shard_map/ppermute | solution.py:370
  192.4 1.9 copy-start.1
  199.9 22.5 %collective-permute-start.15 = (bf16[4,320,512]{2,1,0:T(8,128)(2,1)S(1)}, bf16[4,320,512]{2,1,0:T(8,128)(2,1)S(1)}, u32[]{:S(2)}, u32[]{:S(2)}) collective-permute-start(bf16[4,320,512]{2,1,0:T(8,128)(2,1)S(1)} %get-tuple-element.37), channel_id=1, source_target_pairs={{0,1},{1,0},{2,3},{3,2},{4,5},{5,4},{6,7},{7,6},{8,9},{9,8},{10,11... | collective-permute-start | bytes 3932168 | tf_op jit(solution)/shard_map/ppermute | solution.py:106
  203.6 30.1 %collective-permute-start.28 = (bf16[768,768]{1,0:T(8,128)(2,1)}, bf16[768,768]{1,0:T(8,128)(2,1)S(1)}, u32[]{:S(2)}, u32[]{:S(2)}) collective-permute-start(bf16[768,768]{1,0:T(8,128)(2,1)} %collective-permute-done.14.refs_9_), channel_id=1, source_target_pairs={{0,1},{1,0},{2,3},{3,2},{4,5},{5,4},{6,7},{7,6},{8,9},{9,8},{10,11... | collective-permute-start | bytes 3538952 | tf_op jit(solution)/shard_map/ppermute | solution.py:106
  203.7 8.2 %collective-permute-start.20 = (bf16[3,384,128]{2,1,0:T(8,128)(2,1)S(1)}, bf16[3,384,128]{2,1,0:T(8,128)(2,1)S(1)}, u32[]{:S(2)}, u32[]{:S(2)}) collective-permute-start(bf16[3,384,128]{2,1,0:T(8,128)(2,1)S(1)} %collective-permute-done.19.refs_2_), channel_id=1, source_target_pairs={{0,16},{16,0},{1,17},{17,1},{2,18},{18,2},{3,19},{19,3},{4,20},{20... | collective-permute-start | bytes 884744 | tf_op jit(solution)/shard_map/ppermute | solution.py:106
  205.3 13.0 %collective-permute-start.17 = (bf16[3,384,128]{2,1,0:T(8,128)(2,1)S(1)}, bf16[3,384,128]{2,1,0:T(8,128)(2,1)S(1)}, u32[]{:S(2)}, u32[]{:S(2)}) collective-permute-start(bf16[3,384,128]{2,1,0:T(8,128)(2,1)S(1)} %collective-permute-done.16.refs_0_), channel_id=1, source_target_pairs={{0,16},{16,0},{1,17},{17,1},{2,18},{18,2},{3,19},{19,3},{4,20},{20... | collective-permute-start | bytes 884744 | tf_op jit(solution)/shard_map/ppermute | solution.py:106
  220.9 5.4 %collective-permute-start.21 = (bf16[4,320,256]{2,1,0:T(8,128)(2,1)S(1)}, bf16[4,320,256]{2,1,0:T(8,128)(2,1)S(1)}, u32[]{:S(2)}, u32[]{:S(2)}) collective-permute-start(bf16[4,320,256]{2,1,0:T(8,128)(2,1)S(1)} %get-tuple-element.47), channel_id=1, source_target_pairs={{0,1},{1,0},{2,3},{3,2},{4,5},{5,4},{6,7},{7,6},{8,9},{9,8},{10,11... | collective-permute-start | bytes 1966088 | tf_op jit(solution)/shard_map/ppermute | solution.py:106
  228.5 7.3 %collective-permute-start.23 = (bf16[2,128,128]{2,1,0:T(8,128)(2,1)S(1)}, bf16[2,128,128]{2,1,0:T(8,128)(2,1)S(1)}, u32[]{:S(2)}, u32[]{:S(2)}) collective-permute-start(bf16[2,128,128]{2,1,0:T(8,128)(2,1)S(1)} %get-tuple-element.50), channel_id=1, source_target_pairs={{0,4},{4,0},{8,12},{12,8},{1,5},{5,1},{9,13},{13,9},{2,6},{6,2},{1... | collective-permute-start | bytes 196616 | tf_op jit(solution)/shard_map/ppermute | solution.py:106
  229.1 20.5 %collective-permute-start.22 = (bf16[2,128,256]{2,1,0:T(8,128)(2,1)S(1)}, bf16[2,128,256]{2,1,0:T(8,128)(2,1)S(1)}, u32[]{:S(2)}, u32[]{:S(2)}) collective-permute-start(bf16[2,128,256]{2,1,0:T(8,128)(2,1)S(1)} %get-tuple-element.49), channel_id=1, source_target_pairs={{0,4},{4,0},{8,12},{12,8},{1,5},{5,1},{9,13},{13,9},{2,6},{6,2},{1... | collective-permute-start | bytes 393224 | tf_op jit(solution)/shard_map/ppermute | solution.py:106
  230.6 19.1 %collective-permute-start.24 = (bf16[2,128,256]{2,1,0:T(8,128)(2,1)S(1)}, bf16[2,128,256]{2,1,0:T(8,128)(2,1)S(1)}, u32[]{:S(2)}, u32[]{:S(2)}) collective-permute-start(bf16[2,128,256]{2,1,0:T(8,128)(2,1)S(1)} %get-tuple-element.38.refs_0_), channel_id=1, source_target_pairs={{0,8},{4,12},{8,0},{12,4},{1,9},{5,13},{9,1},{13,5},{2,10},{6,14},... | collective-permute-start | bytes 393224 | tf_op jit(solution)/shard_map/ppermute | solution.py:106
  232.4 17.3 %collective-permute-start.26 = (bf16[2,128,256]{2,1,0:T(8,128)(2,1)S(1)}, bf16[2,128,256]{2,1,0:T(8,128)(2,1)S(1)}, u32[]{:S(2)}, u32[]{:S(2)}) collective-permute-start(bf16[2,128,256]{2,1,0:T(8,128)(2,1)S(1)} %get-tuple-element.49), channel_id=1, source_target_pairs={{0,12},{4,8},{8,4},{12,0},{1,13},{5,9},{9,5},{13,1},{2,14},{6,10},... | collective-permute-start | bytes 393224 | tf_op jit(solution)/shard_map/ppermute | solution.py:106
  233.8 15.9 %collective-permute-start.25 = (bf16[2,128,128]{2,1,0:T(8,128)(2,1)S(1)}, bf16[2,128,128]{2,1,0:T(8,128)(2,1)S(1)}, u32[]{:S(2)}, u32[]{:S(2)}) collective-permute-start(bf16[2,128,128]{2,1,0:T(8,128)(2,1)S(1)} %get-tuple-element.48.refs_1_), channel_id=1, source_target_pairs={{0,8},{4,12},{8,0},{12,4},{1,9},{5,13},{9,1},{13,5},{2,10},{6,14},... | collective-permute-start | bytes 196616 | tf_op jit(solution)/shard_map/ppermute | solution.py:106
  235.8 13.9 %collective-permute-start.27 = (bf16[2,128,128]{2,1,0:T(8,128)(2,1)S(1)}, bf16[2,128,128]{2,1,0:T(8,128)(2,1)S(1)}, u32[]{:S(2)}, u32[]{:S(2)}) collective-permute-start(bf16[2,128,128]{2,1,0:T(8,128)(2,1)S(1)} %get-tuple-element.50), channel_id=1, source_target_pairs={{0,12},{4,8},{8,4},{12,0},{1,13},{5,9},{9,5},{13,1},{2,14},{6,10},... | collective-permute-start | bytes 196616 | tf_op jit(solution)/shard_map/ppermute | solution.py:106
  253.4 5.8 %collective-permute-start.29 = (bf16[2,64,768]{2,1,0:T(8,128)(2,1)S(1)}, bf16[2,64,768]{2,1,0:T(8,128)(2,1)S(1)}, u32[]{:S(2)}, u32[]{:S(2)}) collective-permute-start(bf16[2,64,768]{2,1,0:T(8,128)(2,1)S(1)} %get-tuple-element.52), channel_id=1, source_target_pairs={{0,2},{2,0},{1,3},{3,1},{4,6},{6,4},{5,7},{7,5},{8,10},{10,8},{9,1... | collective-permute-start | bytes 589832 | tf_op jit(solution)/shard_map/ppermute | solution.py:106
  255.0 16.5 %collective-permute-start.30 = (bf16[2,64,768]{2,1,0:T(8,128)(2,1)S(1)}, bf16[2,64,768]{2,1,0:T(8,128)(2,1)S(1)}, u32[]{:S(2)}, u32[]{:S(2)}) collective-permute-start(bf16[2,64,768]{2,1,0:T(8,128)(2,1)S(1)} %get-tuple-element.53), channel_id=1, source_target_pairs={{0,8},{4,12},{8,0},{12,4},{1,9},{5,13},{9,1},{13,5},{2,10},{6,14},... | collective-permute-start | bytes 589832 | tf_op jit(solution)/shard_map/ppermute | solution.py:106
  258.4 17.0 %collective-permute-start.31 = (bf16[2,64,768]{2,1,0:T(8,128)(2,1)S(1)}, bf16[2,64,768]{2,1,0:T(8,128)(2,1)S(1)}, u32[]{:S(2)}, u32[]{:S(2)}) collective-permute-start(bf16[2,64,768]{2,1,0:T(8,128)(2,1)S(1)} %get-tuple-element.54), channel_id=1, source_target_pairs={{0,10},{2,8},{4,14},{6,12},{8,2},{10,0},{12,6},{14,4},{1,11},{3,9}... | collective-permute-start | bytes 589832 | tf_op jit(solution)/shard_map/ppermute | solution.py:394

commit v6 on v5

--- a/solution.py
+++ b/solution.py
@@ -11,6 +11,7 @@
 BS = 64
 MAXB = 4
 VMEM_BYTES = 24 * 1024 * 1024
+WHOLE_VMEM_BYTES = 56 * 1024 * 1024
 EXP2_SCALE = math.log2(math.e) / math.sqrt(HD)
 
 
@@ -110,7 +111,7 @@
     return lax.optimization_barrier((value, *others))[0]
 
 
-def call(kernel, out_shape, prefetch, operands, scratch=(), flops=0, read=0):
+def call(kernel, out_shape, prefetch, operands, scratch=(), flops=0, read=0, limit=VMEM_BYTES):
     return pl.pallas_call(
         kernel,
         out_shape=out_shape,
@@ -121,7 +122,7 @@
             out_specs=jax.tree.map(lambda _: pl.BlockSpec(memory_space=pltpu.VMEM), out_shape),
             scratch_shapes=scratch,
         ),
-        compiler_params=pltpu.CompilerParams(vmem_limit_bytes=VMEM_BYTES),
+        compiler_params=pltpu.CompilerParams(vmem_limit_bytes=limit),
         cost_estimate=pl.CostEstimate(flops=flops, bytes_accessed=read, transcendentals=0),
     )(*prefetch, *operands)
 
@@ -132,27 +133,18 @@
 
     def kernel(place_ref, *refs):
         row, frame = place_ref[0], place_ref[2]
-        out_ref, sems = refs[2 * rows], refs[2 * rows + 1]
-        copies = []
-        for i in range(2 * rows):
-            place_at = out_ref.at[row ^ (i % rows), (frame + i // rows) % 2]
-            copies.append(pltpu.make_async_copy(refs[i], place_at, sems.at[i]))
-            copies[-1].start()
-        for copy in copies:
-            copy.wait()
-
-    return pl.pallas_call(
-        kernel,
-        out_shape=jax.ShapeDtypeStruct((rows, 2, count, width), jnp.bfloat16),
-        grid_spec=pltpu.PrefetchScalarGridSpec(
-            num_scalar_prefetch=1,
-            grid=(),
-            in_specs=[pl.BlockSpec(memory_space=pl.ANY)] * (2 * rows),
-            out_specs=pl.BlockSpec(memory_space=pl.ANY),
-            scratch_shapes=[pltpu.SemaphoreType.DMA((2 * rows,))],
-        ),
-        cost_estimate=pl.CostEstimate(flops=0, bytes_accessed=8 * rows * count * width, transcendentals=0),
-    )(place, *mine, *theirs)
+        for s in range(rows):
+            refs[-1][row ^ s, frame] = refs[s][...]
+            refs[-1][row ^ s, 1 - frame] = refs[rows + s][...]
+
+    return call(
+        kernel,
+        jax.ShapeDtypeStruct((rows, 2, count, width), jnp.bfloat16),
+        [place],
+        [*mine, *theirs],
+        read=8 * rows * count * width,
+        limit=WHOLE_VMEM_BYTES,
+    )
 
 
 def project(place, tokens, chunks):
@@ -334,13 +326,7 @@
     half = depth // 2
     place = jnp.stack([row, group, frame, core]).astype(jnp.int32)
 
-    mine = [lax.dynamic_slice_in_dim(latents[0], core * span * depth, span * depth, axis=1)]
-    mine += [swap(mine[0], "rows", s) for s in range(1, rows_n)]
-    theirs = [swap(x, "frames") for x in mine]
-    tokens = assemble(place, mine, theirs)
-
     tables = jnp.concatenate([win_blocks, win_counts[:, None], block_window[:, None]], axis=1)
-    tables = after(tables, mine[1])
     found = [tables] + [swap(tables, "rows", s) for s in range(1, rows_n)]
     tables = jnp.stack(found)[row ^ jnp.arange(rows_n)].reshape(rows_n * heads_n, MAXB + 2)
     windows = lax.dynamic_index_in_dim(
@@ -349,12 +335,18 @@
     picked = tables[windows]
     members, counts = picked[:, :MAXB].reshape(-1), picked[:, MAXB]
 
+    mine = [lax.dynamic_slice_in_dim(latents[0], core * span * depth, span * depth, axis=1)]
+    mine = [after(mine[0], members, counts)]
+    mine += [swap(mine[0], "rows", s) for s in range(1, rows_n)]
+    theirs = [swap(x, "frames") for x in mine]
+    tokens = assemble(place, mine, theirs)
+
     across = swap(after(w_out, mine[1]), "heads")
     beside = swap(after(w_out, mine[3]), "rows")
 
     by_part = w_qkv.transpose(1, 0, 2)
     last = cols // (3 * HD) * HD
-    waits = [[mine[1]], [mine[2]], [mine[3], theirs[0], members, counts], [theirs[1], across]]
+    waits = [[mine[1]], [mine[2]], [mine[3], theirs[0]], [theirs[1], across]]
     here, there = [], []
     for first, wide in ((0, cols - last), (cols - last, last)):
         for k in range(span):

time: 277 us -> 178 us (0.64)
  Pallas kernels: 116 us -> 23.8 us
  starting transfers between devices: 65.4 us -> 54.7 us
  waiting for transfers between devices: 82.6 us -> 86.7 us
    pallas_call x1 -> x0, Pallas kernels: 97.1 us -> none  [assemble(): pl.pallas_call(kernel, out_shape=jax.ShapeDtypeStruct((rows, 2, count, wi...]
    ppermute x27, starting transfers between devices: 51.1 us -> 41.8 us  [swap(): return lax.ppermute(value, axis, [(i, i ^ step) for i in range(peers)])]
    ppermute x27, waiting for transfers between devices: 78.6 us -> 84 us  [swap(): return lax.ppermute(value, axis, [(i, i ^ step) for i in range(peers)])]
    pallas_call x6 -> x7, Pallas kernels: 19.3 us -> 23.8 us  [call(): pl.pallas_call(kernel, out_shape=out_shape, grid_spec=pltpu.PrefetchScala...]
    ppermute x4, starting transfers between devices: 14.2 us -> 10.7 us  [by_heads(): here.append(lax.ppermute(piece, ('rows', 'heads'), pairs))]
  transfers between devices with their start and end apart: 32 -> 32, of which waited for: 14 -> 13; matrix products, arithmetic and copies ran while one was open for 3% -> 3% of each run, Pallas kernels for 40% -> 11%
where the time goes in v6:
time: 178 us
  waiting for transfers between devices  86.7 us (49%)
  starting transfers between devices  54.7 us (31%)
  Pallas kernels  23.8 us (13%)
  local copies, waits for them, and re-layouts  9.99 us (6%)
  other arithmetic  2.43 us (1%)
    ppermute x27, waiting for transfers between devices, swap(): return lax.ppermute(value, axis, [(i, i ^ step) for i in range(peers)])  84 us
    ppermute x27, starting transfers between devices, swap(): return lax.ppermute(value, axis, [(i, i ^ step) for i in range(peers)])  41.8 us
    pallas_call x7, Pallas kernels, call(): pl.pallas_call(kernel, out_shape=out_shape, grid_spec=pltpu.PrefetchScala...  23.8 us
    ppermute x4, starting transfers between devices, by_heads(): here.append(lax.ppermute(piece, ('rows', 'heads'), pairs))  10.7 us
  transfers between devices with their start and end apart: 32, of which 13 were waited for; matrix products, arithmetic and copies ran while one was open for 3% of the time, Pallas kernels for 11%

profile of v6, /device:TPU:0, one launch (start us, length us, event | category | flops | bytes accessed | tf_op | source)
XLA Modules:
  0.0 177.7 jit_solution(1138709490462110316)
XLA Ops:
  0.0 0.8 copy.10
  0.8 0.7 copy.9
  1.6 0.8 pad_add_fusion.1
  2.3 3.0 %collective-permute-start = (s32[2,6]{1,0:T(2,128)S(1)}, s32[2,6]{1,0:T(2,128)S(1)}, u32[]{:S(2)}, u32[]{:S(2)}) collective-permute-start(s32[2,6]{1,0:T(2,128)S(1)} %pad_add_fusion.1), channel_id=1, source_target_pairs={{0,4},{4,0},{8,12},{12,8},{1,5},{5,1},{9,13},{13,9},{2,6},{6,2},{1... | collective-permute-start | bytes 152 | tf_op jit(solution)/shard_map/ppermute | solution.py:107
  5.3 2.6 %collective-permute-start.1 = (s32[2,6]{1,0:T(2,128)S(1)}, s32[2,6]{1,0:T(2,128)S(1)}, u32[]{:S(2)}, u32[]{:S(2)}) collective-permute-start(s32[2,6]{1,0:T(2,128)S(1)} %pad_add_fusion.1), channel_id=1, source_target_pairs={{0,8},{4,12},{8,0},{12,4},{1,9},{5,13},{9,1},{13,5},{2,10},{6,14},... | collective-permute-start | bytes 152 | tf_op jit(solution)/shard_map/ppermute | solution.py:107
  7.9 0.8 fusion.2
  8.9 0.9 collective-permute-done.1
  9.8 3.5 %collective-permute-done.2 = s32[2,6]{1,0:T(2,128)S(1)} collective-permute-done((s32[2,6]{1,0:T(2,128)S(1)}, s32[2,6]{1,0:T(2,128)S(1)}, u32[]{:S(2)}, u32[]{:S(2)}) %collective-permute-start.2) | collective-permute-done | bytes 80 | tf_op jit(solution)/shard_map/ppermute | solution.py:107
  15.8 3.8 %collective-permute-start.5 = (bf16[128,1536]{1,0:T(8,128)(2,1)S(1)}, bf16[128,1536]{1,0:T(8,128)(2,1)}, u32[]{:S(2)}, u32[]{:S(2)}) collective-permute-start(bf16[128,1536]{1,0:T(8,128)(2,1)S(1)} %dynamic-slice_bitcast_fusion.2.refs_0_), channel_id=1, source_target_pairs={{0,12},{4,8},{8,4},{12,0},{1,13},{5,9},{9,5},{13,1},{2,14},{6,10},... | collective-permute-start | bytes 1179656 | tf_op jit(solution)/shard_map/ppermute | solution.py:107
  19.6 1.3 dynamic-slice_bitcast_fusion
  20.9 1.6 collective-permute-start.6
  22.5 9.0 %collective-permute-done.3.refs_1_ = bf16[128,1536]{1,0:T(8,128)(2,1)S(1)} collective-permute-done((bf16[128,1536]{1,0:T(8,128)(2,1)S(1)}, bf16[128,1536]{1,0:T(8,128)(2,1)S(1)}, u32[]{:S(2)}, u32[]{:S(2)}) %collective-permute-start.3) | collective-permute-done | bytes 393248 | tf_op jit(solution)/shard_map/ppermute | solution.py:107
  31.5 0.8 copy-done.5
  32.3 1.5 collective-permute-start.10
  33.8 13.8 %collective-permute-done.4.refs_2_ = bf16[128,1536]{1,0:T(8,128)(2,1)} collective-permute-done((bf16[128,1536]{1,0:T(8,128)(2,1)S(1)}, bf16[128,1536]{1,0:T(8,128)(2,1)}, u32[]{:S(2)}, u32[]{:S(2)}) %collective-permute-start.4) | collective-permute-done | bytes 393248 | tf_op jit(solution)/shard_map/ppermute | solution.py:107
  47.5 2.5 %collective-permute-start.12 = (bf16[3,384,256]{2,1,0:T(8,128)(2,1)S(1)}, bf16[3,384,256]{2,1,0:T(8,128)(2,1)}, u32[]{:S(2)}, u32[]{:S(2)}) collective-permute-start(bf16[3,384,256]{2,1,0:T(8,128)(2,1)S(1)} %get-tuple-element.32), channel_id=1, source_target_pairs={{0,4},{1,12},{4,0},{5,8},{8,5},{9,13},{12,1},{13,9},{2,6},{3,14},{... | collective-permute-start | bytes 1769480 | tf_op jit(solution)/shard_map/ppermute | solution.py:362
  50.0 1.5 collective-permute-start.7
  52.0 8.0 %collective-permute-done.7.refs_5_ = bf16[128,1536]{1,0:T(8,128)(2,1)S(1)} collective-permute-done((bf16[128,1536]{1,0:T(8,128)(2,1)}, bf16[128,1536]{1,0:T(8,128)(2,1)S(1)}, u32[]{:S(2)}, u32[]{:S(2)}) %collective-permute-start.7) | collective-permute-done | bytes 393248 | tf_op jit(solution)/shard_map/ppermute | solution.py:107
  60.1 11.8 %collective-permute-start.14 = (bf16[768,768]{1,0:T(8,128)(2,1)S(1)}, bf16[768,768]{1,0:T(8,128)(2,1)}, u32[]{:S(2)}, u32[]{:S(2)}) collective-permute-start(bf16[768,768]{1,0:T(8,128)(2,1)S(1)} %copy-done.2), channel_id=1, source_target_pairs={{0,4},{4,0},{8,12},{12,8},{1,5},{5,1},{9,13},{13,9},{2,6},{6,2},{1... | collective-permute-start | bytes 3538952 | tf_op jit(solution)/shard_map/ppermute | solution.py:107
  71.9 1.5 collective-permute-start.11
  74.0 0.7 copy-done.8
  74.7 1.5 collective-permute-start.8
  76.8 1.9 %dynamic-slice_bitcast_fusion.3 = (bf16[3,384,128]{2,1,0:T(8,128)(2,1)}, bf16[3,384,128]{2,1,0:T(8,128)(2,1)}) fusion(bf16[768,3,768]{2,0,1:T(8,128)(2,1)} %param.7, s32[]{:T(128)S(6)} %select_n.58, s32[]{:T(128)S(6)} %select_n.64, s32[]{:T(128)S(6)} %select_n.63), kind=kLoop, calls=%fused_computation.5 | loop fusion | bytes 1179660 | tf_op jit(solution)/shard_map/dynamic_slice | solution.py:358
  78.7 4.4 %collective-permute-done.8.refs_6_ = bf16[128,1536]{1,0:T(8,128)(2,1)} collective-permute-done((bf16[128,1536]{1,0:T(8,128)(2,1)}, bf16[128,1536]{1,0:T(8,128)(2,1)}, u32[]{:S(2)}, u32[]{:S(2)}) %collective-permute-start.8) | collective-permute-done | bytes 393248 | tf_op jit(solution)/shard_map/ppermute | solution.py:107
  83.2 4.3 %shard_map.64.x_ref = bf16[4,2,128,1536]{3,2,1,0:T(8,128)(2,1)} custom-call(s32[4]{0:T(128)} %pad_add_fusion.2.place_ref, bf16[128,1536]{1,0:T(8,128)(2,1)} %copy-done.4, bf16[128,1536]{1,0:T(8,128)(2,1)} %copy-done.5, bf16[128,1536]{1,0:T(8,128)(2,1)} %collective-permute-done.4.refs_2_, bf16[128,1536]{1,0:T(8,128)(2,1)} %collective-permute-done.5.refs_3_, ...), custom_call_target="tpu_custom_call" | custom-call | bytes 6291456 | tf_op jit(solution)/shard_map/pallas_call | solution.py:115
  87.5 1.6 collective-permute-start.16
  89.1 5.1 %collective-permute-start.19 = (bf16[3,384,128]{2,1,0:T(8,128)(2,1)}, bf16[3,384,128]{2,1,0:T(8,128)(2,1)S(1)}, u32[]{:S(2)}, u32[]{:S(2)}) collective-permute-start(bf16[3,384,128]{2,1,0:T(8,128)(2,1)} %get-tuple-element.42), channel_id=1, source_target_pairs={{0,4},{1,12},{4,0},{5,8},{8,5},{9,13},{12,1},{13,9},{2,6},{3,14},{... | collective-permute-start | bytes 884744 | tf_op jit(solution)/shard_map/ppermute | solution.py:362
  94.3 3.5 %collective-permute-done.13.refs_3_ = bf16[3,384,256]{2,1,0:T(8,128)(2,1)} collective-permute-done((bf16[3,384,256]{2,1,0:T(8,128)(2,1)}, bf16[3,384,256]{2,1,0:T(8,128)(2,1)}, u32[]{:S(2)}, u32[]{:S(2)}) %collective-permute-start.13) | collective-permute-done | bytes 589856 | tf_op jit(solution)/shard_map/ppermute | solution.py:107
  97.8 1.9 %copy-done.1 = bf16[4,2,128,1536]{3,2,1,0:T(8,128)(2,1)S(1)} copy-done((bf16[4,2,128,1536]{3,2,1,0:T(8,128)(2,1)S(1)}, bf16[4,2,128,1536]{3,2,1,0:T(8,128)(2,1)}, u32[]{:S(2)}) %copy-start.1) | copy-done | bytes 3145752
  99.7 5.6 %shard_map.65 = (f32[4,128,256]{2,1,0:T(8,128)S(1)}, f32[4,256,512]{2,1,0:T(8,128)S(1)}, bf16[4,320,512]{2,1,0:T(8,128)(2,1)S(1)}) custom-call(s32[4]{0:T(128)S(1)} %copy-done.3, bf16[4,2,128,1536]{3,2,1,0:T(8,128)(2,1)S(1)} %copy-done.1, bf16[3,384,256]{2,1,0:T(8,128)(2,1)} %collective-permute-done.10.refs_0_, ...), custom_call_target="tpu_custom_call" | custom-call | flops 2415919104 | bytes 8053063 | tf_op jit(solution)/shard_map/pallas_call | solution.py:115
  105.9 1.6 collective-permute-start.20
  108.0 7.8 %collective-permute-done.20.refs_3_ = bf16[3,384,128]{2,1,0:T(8,128)(2,1)S(1)} collective-permute-done((bf16[3,384,128]{2,1,0:T(8,128)(2,1)S(1)}, bf16[3,384,128]{2,1,0:T(8,128)(2,1)S(1)}, u32[]{:S(2)}, u32[]{:S(2)}) %collective-permute-start.20) | collective-permute-done | bytes 294944 | tf_op jit(solution)/shard_map/ppermute | solution.py:107
  115.7 6.0 %collective-permute-done.17.refs_1_ = bf16[3,384,128]{2,1,0:T(8,128)(2,1)S(1)} collective-permute-done((bf16[3,384,128]{2,1,0:T(8,128)(2,1)S(1)}, bf16[3,384,128]{2,1,0:T(8,128)(2,1)S(1)}, u32[]{:S(2)}, u32[]{:S(2)}) %collective-permute-start.17) | collective-permute-done | bytes 294944 | tf_op jit(solution)/shard_map/ppermute | solution.py:107
  121.7 2.7 %shard_map.67 = (f32[4,128,128]{2,1,0:T(8,128)S(1)}, f32[4,256,256]{2,1,0:T(8,128)S(1)}, bf16[4,320,256]{2,1,0:T(8,128)(2,1)S(1)}) custom-call(s32[4]{0:T(128)S(1)} %copy-done.3, bf16[4,2,128,1536]{3,2,1,0:T(8,128)(2,1)S(1)} %copy-done.1, bf16[3,384,128]{2,1,0:T(8,128)(2,1)S(1)} %collective-permute-done.16.refs_0_, ...), custom_call_target="tpu_custom_call" | custom-call | flops 1207959552 | bytes 4026531 | tf_op jit(solution)/shard_map/pallas_call | solution.py:115
  124.5 3.8 %shard_map.66 = (bf16[2,128,256]{2,1,0:T(8,128)(2,1)S(1)}, bf16[2,128,256]{2,1,0:T(8,128)(2,1)S(1)}) custom-call(s32[4]{0:T(128)S(1)} %copy-done.3, s32[16]{0:T(128)S(1)} %reshape.24.members_ref, s32[4]{0:T(128)S(1)} %slice_reduce_fusion.1.counts_ref, f32[4,128,256]{2,1,0:T(8,128)S(1)} %get-tuple-element.33.q_ref, ...), custom_call_target="tpu_custom_call" | custom-call | flops 268435456 | bytes 2097152 | tf_op jit(solution)/shard_map/pallas_call | solution.py:115
  128.3 2.2 %shard_map.68 = (bf16[2,128,128]{2,1,0:T(8,128)(2,1)S(1)}, bf16[2,128,128]{2,1,0:T(8,128)(2,1)S(1)}) custom-call(s32[4]{0:T(128)S(1)} %copy-done.3, s32[16]{0:T(128)S(1)} %reshape.24.members_ref, s32[4]{0:T(128)S(1)} %slice_reduce_fusion.1.counts_ref, f32[4,128,128]{2,1,0:T(8,128)S(1)} %get-tuple-element.44.q_ref, ...), custom_call_target="tpu_custom_call" | custom-call | flops 134217728 | bytes 1048576 | tf_op jit(solution)/shard_map/pallas_call | solution.py:115
  130.6 2.0 %collective-permute-start.22 = (bf16[2,128,256]{2,1,0:T(8,128)(2,1)S(1)}, bf16[2,128,256]{2,1,0:T(8,128)(2,1)S(1)}, u32[]{:S(2)}, u32[]{:S(2)}) collective-permute-start(bf16[2,128,256]{2,1,0:T(8,128)(2,1)S(1)} %get-tuple-element.49), channel_id=1, source_target_pairs={{0,4},{4,0},{8,12},{12,8},{1,5},{5,1},{9,13},{13,9},{2,6},{6,2},{1... | collective-permute-start | bytes 393224 | tf_op jit(solution)/shard_map/ppermute | solution.py:107
  132.6 2.4 %collective-permute-start.26 = (bf16[2,128,256]{2,1,0:T(8,128)(2,1)S(1)}, bf16[2,128,256]{2,1,0:T(8,128)(2,1)S(1)}, u32[]{:S(2)}, u32[]{:S(2)}) collective-permute-start(bf16[2,128,256]{2,1,0:T(8,128)(2,1)S(1)} %get-tuple-element.49), channel_id=1, source_target_pairs={{0,12},{4,8},{8,4},{12,0},{1,13},{5,9},{9,5},{13,1},{2,14},{6,10},... | collective-permute-start | bytes 393224 | tf_op jit(solution)/shard_map/ppermute | solution.py:107
  135.5 2.9 %collective-permute-start.27 = (bf16[2,128,128]{2,1,0:T(8,128)(2,1)S(1)}, bf16[2,128,128]{2,1,0:T(8,128)(2,1)S(1)}, u32[]{:S(2)}, u32[]{:S(2)}) collective-permute-start(bf16[2,128,128]{2,1,0:T(8,128)(2,1)S(1)} %get-tuple-element.50), channel_id=1, source_target_pairs={{0,12},{4,8},{8,4},{12,0},{1,13},{5,9},{9,5},{13,1},{2,14},{6,10},... | collective-permute-start | bytes 196616 | tf_op jit(solution)/shard_map/ppermute | solution.py:107
  138.5 13.7 %collective-permute-done.25.refs_5_ = bf16[2,128,128]{2,1,0:T(8,128)(2,1)S(1)} collective-permute-done((bf16[2,128,128]{2,1,0:T(8,128)(2,1)S(1)}, bf16[2,128,128]{2,1,0:T(8,128)(2,1)S(1)}, u32[]{:S(2)}, u32[]{:S(2)}) %collective-permute-start.25) | collective-permute-done | bytes 65568 | tf_op jit(solution)/shard_map/ppermute | solution.py:107
  152.2 3.8 %shard_map.69 = (f32[2,64,768]{2,1,0:T(8,128)S(1)}, bf16[2,64,768]{2,1,0:T(8,128)(2,1)S(1)}, bf16[2,64,768]{2,1,0:T(8,128)(2,1)S(1)}, bf16[2,64,768]{2,1,0:T(8,128)(2,1)S(1)}) custom-call(s32[4]{0:T(128)S(1)} %copy-done.3, bf16[2,128,256]{2,1,0:T(8,128)(2,1)S(1)} %get-tuple-element.38.refs_0_, bf16[2,128,128]{2,1,0:T(8,128)(2,1)S(1)} %get-tuple-element.48.refs_1_, ...), custom_call_target="tpu_custom_call" | custom-call | flops 1207959552 | bytes 4718592 | tf_op jit(solution)/shard_map/pallas_call | solution.py:115
  155.9 1.5 collective-permute-start.29
  157.5 0.7 collective-permute-start.30
  158.2 2.2 %collective-permute-start.31 = (bf16[2,64,768]{2,1,0:T(8,128)(2,1)S(1)}, bf16[2,64,768]{2,1,0:T(8,128)(2,1)S(1)}, u32[]{:S(2)}, u32[]{:S(2)}) collective-permute-start(bf16[2,64,768]{2,1,0:T(8,128)(2,1)S(1)} %get-tuple-element.54), channel_id=1, source_target_pairs={{0,10},{2,8},{4,14},{6,12},{8,2},{10,0},{12,6},{14,4},{1,11},{3,9}... | collective-permute-start | bytes 589832 | tf_op jit(solution)/shard_map/ppermute | solution.py:386
  160.4 1.3 collective-permute-done.29.x_ref
  161.7 12.0 %collective-permute-done.30.z_ref = bf16[2,64,768]{2,1,0:T(8,128)(2,1)S(1)} collective-permute-done((bf16[2,64,768]{2,1,0:T(8,128)(2,1)S(1)}, bf16[2,64,768]{2,1,0:T(8,128)(2,1)S(1)}, u32[]{:S(2)}, u32[]{:S(2)}) %collective-permute-start.30) | collective-permute-done | bytes 196640 | tf_op jit(solution)/shard_map/ppermute | solution.py:107
  173.7 2.6 %collective-permute-done.31.both_ref = bf16[2,64,768]{2,1,0:T(8,128)(2,1)S(1)} collective-permute-done((bf16[2,64,768]{2,1,0:T(8,128)(2,1)S(1)}, bf16[2,64,768]{2,1,0:T(8,128)(2,1)S(1)}, u32[]{:S(2)}, u32[]{:S(2)}) %collective-permute-start.31) | collective-permute-done | bytes 196640 | tf_op jit(solution)/shard_map/ppermute | solution.py:386
  176.4 1.4 shard_map.70
  (60 shorter events, 6.0 us)
Async XLA Ops:
  0.0 8.8 %copy-start = (bf16[1,128,3072]{2,1,0:T(8,128)(2,1)S(1)}, bf16[1,128,3072]{2,1,0:T(8,128)(2,1)}, u32[]{:S(2)}) copy-start(bf16[1,128,3072]{2,1,0:T(8,128)(2,1)} %param.6) | copy-start | bytes 2359300
  2.3 6.6 %collective-permute-start = (s32[2,6]{1,0:T(2,128)S(1)}, s32[2,6]{1,0:T(2,128)S(1)}, u32[]{:S(2)}, u32[]{:S(2)}) collective-permute-start(s32[2,6]{1,0:T(2,128)S(1)} %pad_add_fusion.1), channel_id=1, source_target_pairs={{0,4},{4,0},{8,12},{12,8},{1,5},{5,1},{9,13},{13,9},{2,6},{6,2},{1... | collective-permute-start | bytes 152 | tf_op jit(solution)/shard_map/ppermute | solution.py:107
  5.3 4.5 %collective-permute-start.1 = (s32[2,6]{1,0:T(2,128)S(1)}, s32[2,6]{1,0:T(2,128)S(1)}, u32[]{:S(2)}, u32[]{:S(2)}) collective-permute-start(s32[2,6]{1,0:T(2,128)S(1)} %pad_add_fusion.1), channel_id=1, source_target_pairs={{0,8},{4,12},{8,0},{12,4},{1,9},{5,13},{9,1},{13,5},{2,10},{6,14},... | collective-permute-start | bytes 152 | tf_op jit(solution)/shard_map/ppermute | solution.py:107
  7.9 5.4 %collective-permute-start.2 = (s32[2,6]{1,0:T(2,128)S(1)}, s32[2,6]{1,0:T(2,128)S(1)}, u32[]{:S(2)}, u32[]{:S(2)}) collective-permute-start(s32[2,6]{1,0:T(2,128)S(1)} %pad_add_fusion.1), channel_id=1, source_target_pairs={{0,12},{4,8},{8,4},{12,0},{1,13},{5,9},{9,5},{13,1},{2,14},{6,10},... | collective-permute-start | bytes 152 | tf_op jit(solution)/shard_map/ppermute | solution.py:107
  8.9 69.9 %copy-start.4 = (bf16[128,1536]{1,0:T(8,128)(2,1)}, bf16[128,1536]{1,0:T(8,128)(2,1)S(1)}, u32[]{:S(2)}) copy-start(bf16[128,1536]{1,0:T(8,128)(2,1)S(1)} %dynamic-slice_bitcast_fusion.2.refs_0_) | copy-start | bytes 1179652
  8.9 24.9 %copy-start.2 = (bf16[768,768]{1,0:T(8,128)(2,1)S(1)}, bf16[768,768]{1,0:T(8,128)(2,1)}, u32[]{:S(2)}) copy-start(bf16[768,768]{1,0:T(8,128)(2,1)} %refs_8_.1) | copy-start | bytes 3538948
  15.2 16.3 %collective-permute-start.3 = (bf16[128,1536]{1,0:T(8,128)(2,1)S(1)}, bf16[128,1536]{1,0:T(8,128)(2,1)S(1)}, u32[]{:S(2)}, u32[]{:S(2)}) collective-permute-start(bf16[128,1536]{1,0:T(8,128)(2,1)S(1)} %dynamic-slice_bitcast_fusion.2.refs_0_), channel_id=1, source_target_pairs={{0,4},{4,0},{8,12},{12,8},{1,5},{5,1},{9,13},{13,9},{2,6},{6,2},{1... | collective-permute-start | bytes 1179656 | tf_op jit(solution)/shard_map/ppermute | solution.py:107
  15.2 32.3 %collective-permute-start.4 = (bf16[128,1536]{1,0:T(8,128)(2,1)S(1)}, bf16[128,1536]{1,0:T(8,128)(2,1)}, u32[]{:S(2)}, u32[]{:S(2)}) collective-permute-start(bf16[128,1536]{1,0:T(8,128)(2,1)S(1)} %dynamic-slice_bitcast_fusion.2.refs_0_), channel_id=1, source_target_pairs={{0,8},{4,12},{8,0},{12,4},{1,9},{5,13},{9,1},{13,5},{2,10},{6,14},... | collective-permute-start | bytes 1179656 | tf_op jit(solution)/shard_map/ppermute | solution.py:107
  15.8 34.2 %collective-permute-start.5 = (bf16[128,1536]{1,0:T(8,128)(2,1)S(1)}, bf16[128,1536]{1,0:T(8,128)(2,1)}, u32[]{:S(2)}, u32[]{:S(2)}) collective-permute-start(bf16[128,1536]{1,0:T(8,128)(2,1)S(1)} %dynamic-slice_bitcast_fusion.2.refs_0_), channel_id=1, source_target_pairs={{0,12},{4,8},{8,4},{12,0},{1,13},{5,9},{9,5},{13,1},{2,14},{6,10},... | collective-permute-start | bytes 1179656 | tf_op jit(solution)/shard_map/ppermute | solution.py:107
  20.9 30.6 %collective-permute-start.6 = (bf16[128,1536]{1,0:T(8,128)(2,1)S(1)}, bf16[128,1536]{1,0:T(8,128)(2,1)S(1)}, u32[]{:S(2)}, u32[]{:S(2)}) collective-permute-start(bf16[128,1536]{1,0:T(8,128)(2,1)S(1)} %dynamic-slice_bitcast_fusion.2.refs_0_), channel_id=1, source_target_pairs={{0,2},{2,0},{1,3},{3,1},{4,6},{6,4},{5,7},{7,5},{8,10},{10,8},{9,1... | collective-permute-start | bytes 1179656 | tf_op jit(solution)/shard_map/ppermute | solution.py:107
  31.5 0.8 copy-start.5
  32.3 39.6 %collective-permute-start.10 = (bf16[3,384,256]{2,1,0:T(8,128)(2,1)S(1)}, bf16[3,384,256]{2,1,0:T(8,128)(2,1)}, u32[]{:S(2)}, u32[]{:S(2)}) collective-permute-start(bf16[3,384,256]{2,1,0:T(8,128)(2,1)S(1)} %get-tuple-element.31), channel_id=1, source_target_pairs={{0,0},{1,8},{4,4},{5,12},{8,1},{9,9},{12,5},{13,13},{2,2},{3,10},{... | collective-permute-start | bytes 1769480 | tf_op jit(solution)/shard_map/ppermute | solution.py:362
  33.8 55.3 %collective-permute-start.18 = (bf16[768,768]{1,0:T(8,128)(2,1)S(1)}, bf16[768,768]{1,0:T(8,128)(2,1)S(1)}, u32[]{:S(2)}, u32[]{:S(2)}) collective-permute-start(bf16[768,768]{1,0:T(8,128)(2,1)S(1)} %copy-done.2), channel_id=1, source_target_pairs={{0,1},{1,0},{2,3},{3,2},{4,5},{5,4},{6,7},{7,6},{8,9},{9,8},{10,11... | collective-permute-start | bytes 3538952 | tf_op jit(solution)/shard_map/ppermute | solution.py:107
  47.5 25.9 %collective-permute-start.12 = (bf16[3,384,256]{2,1,0:T(8,128)(2,1)S(1)}, bf16[3,384,256]{2,1,0:T(8,128)(2,1)}, u32[]{:S(2)}, u32[]{:S(2)}) collective-permute-start(bf16[3,384,256]{2,1,0:T(8,128)(2,1)S(1)} %get-tuple-element.32), channel_id=1, source_target_pairs={{0,4},{1,12},{4,0},{5,8},{8,5},{9,13},{12,1},{13,9},{2,6},{3,14},{... | collective-permute-start | bytes 1769480 | tf_op jit(solution)/shard_map/ppermute | solution.py:362
  50.0 10.1 %collective-permute-start.7 = (bf16[128,1536]{1,0:T(8,128)(2,1)}, bf16[128,1536]{1,0:T(8,128)(2,1)S(1)}, u32[]{:S(2)}, u32[]{:S(2)}) collective-permute-start(bf16[128,1536]{1,0:T(8,128)(2,1)} %copy-done.5), channel_id=1, source_target_pairs={{0,2},{2,0},{1,3},{3,1},{4,6},{6,4},{5,7},{7,5},{8,10},{10,8},{9,1... | collective-permute-start | bytes 1179656 | tf_op jit(solution)/shard_map/ppermute | solution.py:107
  51.5 21.9 %copy-start.6 = (bf16[128,1536]{1,0:T(8,128)(2,1)}, bf16[128,1536]{1,0:T(8,128)(2,1)S(1)}, u32[]{:S(2)}) copy-start(bf16[128,1536]{1,0:T(8,128)(2,1)S(1)} %collective-permute-done.6.refs_4_) | copy-start | bytes 1179652
  51.5 22.5 %collective-permute-start.9 = (bf16[128,1536]{1,0:T(8,128)(2,1)}, bf16[128,1536]{1,0:T(8,128)(2,1)S(1)}, u32[]{:S(2)}, u32[]{:S(2)}) collective-permute-start(bf16[128,1536]{1,0:T(8,128)(2,1)} %collective-permute-done.5.refs_3_), channel_id=1, source_target_pairs={{0,2},{2,0},{1,3},{3,1},{4,6},{6,4},{5,7},{7,5},{8,10},{10,8},{9,1... | collective-permute-start | bytes 1179656 | tf_op jit(solution)/shard_map/ppermute | solution.py:107
  60.1 13.9 %copy-start.7 = (bf16[128,1536]{1,0:T(8,128)(2,1)}, bf16[128,1536]{1,0:T(8,128)(2,1)S(1)}, u32[]{:S(2)}) copy-start(bf16[128,1536]{1,0:T(8,128)(2,1)S(1)} %collective-permute-done.7.refs_5_) | copy-start | bytes 1179652
  60.1 45.4 %collective-permute-start.14 = (bf16[768,768]{1,0:T(8,128)(2,1)S(1)}, bf16[768,768]{1,0:T(8,128)(2,1)}, u32[]{:S(2)}, u32[]{:S(2)}) collective-permute-start(bf16[768,768]{1,0:T(8,128)(2,1)S(1)} %copy-done.2), channel_id=1, source_target_pairs={{0,4},{4,0},{8,12},{12,8},{1,5},{5,1},{9,13},{13,9},{2,6},{6,2},{1... | collective-permute-start | bytes 3538952 | tf_op jit(solution)/shard_map/ppermute | solution.py:107
  71.9 22.3 %collective-permute-start.11 = (bf16[3,384,256]{2,1,0:T(8,128)(2,1)}, bf16[3,384,256]{2,1,0:T(8,128)(2,1)}, u32[]{:S(2)}, u32[]{:S(2)}) collective-permute-start(bf16[3,384,256]{2,1,0:T(8,128)(2,1)} %collective-permute-done.10.refs_0_), channel_id=1, source_target_pairs={{0,16},{16,0},{1,17},{17,1},{2,18},{18,2},{3,19},{19,3},{4,20},{20... | collective-permute-start | bytes 1769480 | tf_op jit(solution)/shard_map/ppermute | solution.py:107
  73.4 24.4 %collective-permute-start.13 = (bf16[3,384,256]{2,1,0:T(8,128)(2,1)}, bf16[3,384,256]{2,1,0:T(8,128)(2,1)}, u32[]{:S(2)}, u32[]{:S(2)}) collective-permute-start(bf16[3,384,256]{2,1,0:T(8,128)(2,1)} %collective-permute-done.12.refs_2_), channel_id=1, source_target_pairs={{0,16},{16,0},{1,17},{17,1},{2,18},{18,2},{3,19},{19,3},{4,20},{20... | collective-permute-start | bytes 1769480 | tf_op jit(solution)/shard_map/ppermute | solution.py:107
  74.0 0.7 copy-start.8
  74.7 8.5 %collective-permute-start.8 = (bf16[128,1536]{1,0:T(8,128)(2,1)}, bf16[128,1536]{1,0:T(8,128)(2,1)}, u32[]{:S(2)}, u32[]{:S(2)}) collective-permute-start(bf16[128,1536]{1,0:T(8,128)(2,1)} %collective-permute-done.4.refs_2_), channel_id=1, source_target_pairs={{0,2},{2,0},{1,3},{3,1},{4,6},{6,4},{5,7},{7,5},{8,10},{10,8},{9,1... | collective-permute-start | bytes 1179656 | tf_op jit(solution)/shard_map/ppermute | solution.py:107
  78.7 19.1 %copy-start.3 = (s32[4]{0:T(128)S(1)}, s32[4]{0:T(128)}, u32[]{:S(2)}) copy-start(s32[4]{0:T(128)} %pad_add_fusion.2.place_ref) | copy-start | bytes 52
  87.5 18.4 %collective-permute-start.16 = (bf16[3,384,128]{2,1,0:T(8,128)(2,1)}, bf16[3,384,128]{2,1,0:T(8,128)(2,1)S(1)}, u32[]{:S(2)}, u32[]{:S(2)}) collective-permute-start(bf16[3,384,128]{2,1,0:T(8,128)(2,1)} %get-tuple-element.39), channel_id=1, source_target_pairs={{0,0},{1,8},{4,4},{5,12},{8,1},{9,9},{12,5},{13,13},{2,2},{3,10},{... | collective-permute-start | bytes 884744 | tf_op jit(solution)/shard_map/ppermute | solution.py:362
  89.1 16.8 %collective-permute-start.19 = (bf16[3,384,128]{2,1,0:T(8,128)(2,1)}, bf16[3,384,128]{2,1,0:T(8,128)(2,1)S(1)}, u32[]{:S(2)}, u32[]{:S(2)}) collective-permute-start(bf16[3,384,128]{2,1,0:T(8,128)(2,1)} %get-tuple-element.42), channel_id=1, source_target_pairs={{0,4},{1,12},{4,0},{5,8},{8,5},{9,13},{12,1},{13,9},{2,6},{3,14},{... | collective-permute-start | bytes 884744 | tf_op jit(solution)/shard_map/ppermute | solution.py:362
  97.8 1.9 %copy-start.1 = (bf16[4,2,128,1536]{3,2,1,0:T(8,128)(2,1)S(1)}, bf16[4,2,128,1536]{3,2,1,0:T(8,128)(2,1)}, u32[]{:S(2)}) copy-start(bf16[4,2,128,1536]{3,2,1,0:T(8,128)(2,1)} %shard_map.64.x_ref) | copy-start | bytes 9437188
  105.3 19.1 %collective-permute-start.15 = (bf16[4,320,512]{2,1,0:T(8,128)(2,1)S(1)}, bf16[4,320,512]{2,1,0:T(8,128)(2,1)S(1)}, u32[]{:S(2)}, u32[]{:S(2)}) collective-permute-start(bf16[4,320,512]{2,1,0:T(8,128)(2,1)S(1)} %get-tuple-element.37), channel_id=1, source_target_pairs={{0,1},{1,0},{2,3},{3,2},{4,5},{5,4},{6,7},{7,6},{8,9},{9,8},{10,11... | collective-permute-start | bytes 3932168 | tf_op jit(solution)/shard_map/ppermute | solution.py:107
  105.4 29.6 %collective-permute-start.28 = (bf16[768,768]{1,0:T(8,128)(2,1)}, bf16[768,768]{1,0:T(8,128)(2,1)S(1)}, u32[]{:S(2)}, u32[]{:S(2)}) collective-permute-start(bf16[768,768]{1,0:T(8,128)(2,1)} %collective-permute-done.14.refs_9_), channel_id=1, source_target_pairs={{0,1},{1,0},{2,3},{3,2},{4,5},{5,4},{6,7},{7,6},{8,9},{9,8},{10,11... | collective-permute-start | bytes 3538952 | tf_op jit(solution)/shard_map/ppermute | solution.py:107
  105.9 9.8 %collective-permute-start.20 = (bf16[3,384,128]{2,1,0:T(8,128)(2,1)S(1)}, bf16[3,384,128]{2,1,0:T(8,128)(2,1)S(1)}, u32[]{:S(2)}, u32[]{:S(2)}) collective-permute-start(bf16[3,384,128]{2,1,0:T(8,128)(2,1)S(1)} %collective-permute-done.19.refs_2_), channel_id=1, source_target_pairs={{0,16},{16,0},{1,17},{17,1},{2,18},{18,2},{3,19},{19,3},{4,20},{20... | collective-permute-start | bytes 884744 | tf_op jit(solution)/shard_map/ppermute | solution.py:107
  107.5 14.2 %collective-permute-start.17 = (bf16[3,384,128]{2,1,0:T(8,128)(2,1)S(1)}, bf16[3,384,128]{2,1,0:T(8,128)(2,1)S(1)}, u32[]{:S(2)}, u32[]{:S(2)}) collective-permute-start(bf16[3,384,128]{2,1,0:T(8,128)(2,1)S(1)} %collective-permute-done.16.refs_0_), channel_id=1, source_target_pairs={{0,16},{16,0},{1,17},{17,1},{2,18},{18,2},{3,19},{19,3},{4,20},{20... | collective-permute-start | bytes 884744 | tf_op jit(solution)/shard_map/ppermute | solution.py:107
  124.4 3.9 %collective-permute-start.21 = (bf16[4,320,256]{2,1,0:T(8,128)(2,1)S(1)}, bf16[4,320,256]{2,1,0:T(8,128)(2,1)S(1)}, u32[]{:S(2)}, u32[]{:S(2)}) collective-permute-start(bf16[4,320,256]{2,1,0:T(8,128)(2,1)S(1)} %get-tuple-element.47), channel_id=1, source_target_pairs={{0,1},{1,0},{2,3},{3,2},{4,5},{5,4},{6,7},{7,6},{8,9},{9,8},{10,11... | collective-permute-start | bytes 1966088 | tf_op jit(solution)/shard_map/ppermute | solution.py:107
  130.5 5.0 %collective-permute-start.23 = (bf16[2,128,128]{2,1,0:T(8,128)(2,1)S(1)}, bf16[2,128,128]{2,1,0:T(8,128)(2,1)S(1)}, u32[]{:S(2)}, u32[]{:S(2)}) collective-permute-start(bf16[2,128,128]{2,1,0:T(8,128)(2,1)S(1)} %get-tuple-element.50), channel_id=1, source_target_pairs={{0,4},{4,0},{8,12},{12,8},{1,5},{5,1},{9,13},{13,9},{2,6},{6,2},{1... | collective-permute-start | bytes 196616 | tf_op jit(solution)/shard_map/ppermute | solution.py:107
  130.6 21.5 %collective-permute-start.22 = (bf16[2,128,256]{2,1,0:T(8,128)(2,1)S(1)}, bf16[2,128,256]{2,1,0:T(8,128)(2,1)S(1)}, u32[]{:S(2)}, u32[]{:S(2)}) collective-permute-start(bf16[2,128,256]{2,1,0:T(8,128)(2,1)S(1)} %get-tuple-element.49), channel_id=1, source_target_pairs={{0,4},{4,0},{8,12},{12,8},{1,5},{5,1},{9,13},{13,9},{2,6},{6,2},{1... | collective-permute-start | bytes 393224 | tf_op jit(solution)/shard_map/ppermute | solution.py:107
  132.6 19.5 %collective-permute-start.24 = (bf16[2,128,256]{2,1,0:T(8,128)(2,1)S(1)}, bf16[2,128,256]{2,1,0:T(8,128)(2,1)S(1)}, u32[]{:S(2)}, u32[]{:S(2)}) collective-permute-start(bf16[2,128,256]{2,1,0:T(8,128)(2,1)S(1)} %get-tuple-element.38.refs_0_), channel_id=1, source_target_pairs={{0,8},{4,12},{8,0},{12,4},{1,9},{5,13},{9,1},{13,5},{2,10},{6,14},... | collective-permute-start | bytes 393224 | tf_op jit(solution)/shard_map/ppermute | solution.py:107
  132.6 19.5 %collective-permute-start.26 = (bf16[2,128,256]{2,1,0:T(8,128)(2,1)S(1)}, bf16[2,128,256]{2,1,0:T(8,128)(2,1)S(1)}, u32[]{:S(2)}, u32[]{:S(2)}) collective-permute-start(bf16[2,128,256]{2,1,0:T(8,128)(2,1)S(1)} %get-tuple-element.49), channel_id=1, source_target_pairs={{0,12},{4,8},{8,4},{12,0},{1,13},{5,9},{9,5},{13,1},{2,14},{6,10},... | collective-permute-start | bytes 393224 | tf_op jit(solution)/shard_map/ppermute | solution.py:107
  135.1 17.1 %collective-permute-start.25 = (bf16[2,128,128]{2,1,0:T(8,128)(2,1)S(1)}, bf16[2,128,128]{2,1,0:T(8,128)(2,1)S(1)}, u32[]{:S(2)}, u32[]{:S(2)}) collective-permute-start(bf16[2,128,128]{2,1,0:T(8,128)(2,1)S(1)} %get-tuple-element.48.refs_1_), channel_id=1, source_target_pairs={{0,8},{4,12},{8,0},{12,4},{1,9},{5,13},{9,1},{13,5},{2,10},{6,14},... | collective-permute-start | bytes 196616 | tf_op jit(solution)/shard_map/ppermute | solution.py:107
  135.5 16.6 %collective-permute-start.27 = (bf16[2,128,128]{2,1,0:T(8,128)(2,1)S(1)}, bf16[2,128,128]{2,1,0:T(8,128)(2,1)S(1)}, u32[]{:S(2)}, u32[]{:S(2)}) collective-permute-start(bf16[2,128,128]{2,1,0:T(8,128)(2,1)S(1)} %get-tuple-element.50), channel_id=1, source_target_pairs={{0,12},{4,8},{8,4},{12,0},{1,13},{5,9},{9,5},{13,1},{2,14},{6,10},... | collective-permute-start | bytes 196616 | tf_op jit(solution)/shard_map/ppermute | solution.py:107
  155.9 5.7 %collective-permute-start.29 = (bf16[2,64,768]{2,1,0:T(8,128)(2,1)S(1)}, bf16[2,64,768]{2,1,0:T(8,128)(2,1)S(1)}, u32[]{:S(2)}, u32[]{:S(2)}) collective-permute-start(bf16[2,64,768]{2,1,0:T(8,128)(2,1)S(1)} %get-tuple-element.52), channel_id=1, source_target_pairs={{0,2},{2,0},{1,3},{3,1},{4,6},{6,4},{5,7},{7,5},{8,10},{10,8},{9,1... | collective-permute-start | bytes 589832 | tf_op jit(solution)/shard_map/ppermute | solution.py:107
  157.5 16.2 %collective-permute-start.30 = (bf16[2,64,768]{2,1,0:T(8,128)(2,1)S(1)}, bf16[2,64,768]{2,1,0:T(8,128)(2,1)S(1)}, u32[]{:S(2)}, u32[]{:S(2)}) collective-permute-start(bf16[2,64,768]{2,1,0:T(8,128)(2,1)S(1)} %get-tuple-element.53), channel_id=1, source_target_pairs={{0,8},{4,12},{8,0},{12,4},{1,9},{5,13},{9,1},{13,5},{2,10},{6,14},... | collective-permute-start | bytes 589832 | tf_op jit(solution)/shard_map/ppermute | solution.py:107
  158.2 18.2 %collective-permute-start.31 = (bf16[2,64,768]{2,1,0:T(8,128)(2,1)S(1)}, bf16[2,64,768]{2,1,0:T(8,128)(2,1)S(1)}, u32[]{:S(2)}, u32[]{:S(2)}) collective-permute-start(bf16[2,64,768]{2,1,0:T(8,128)(2,1)S(1)} %get-tuple-element.54), channel_id=1, source_target_pairs={{0,10},{2,8},{4,14},{6,12},{8,2},{10,0},{12,6},{14,4},{1,11},{3,9}... | collective-permute-start | bytes 589832 | tf_op jit(solution)/shard_map/ppermute | solution.py:386

commit v7 on v6

--- a/solution.py
+++ b/solution.py
@@ -127,22 +127,30 @@
     )(*prefetch, *operands)
 
 
-def assemble(place, mine, theirs):
-    count, width = mine[0].shape
-    rows = len(mine)
+def assemble(place, near, inward, outward):
+    count, width = near[0][0].shape
+    pieces = [x for pair in near + inward + outward for x in pair]
 
     def kernel(place_ref, *refs):
         row, frame = place_ref[0], place_ref[2]
-        for s in range(rows):
-            refs[-1][row ^ s, frame] = refs[s][...]
-            refs[-1][row ^ s, 1 - frame] = refs[rows + s][...]
+        out_ref = refs[-1]
+
+        def put(first, steps):
+            for i, s in enumerate(steps):
+                for f in range(2):
+                    out_ref[row ^ s, (frame + f) % 2] = refs[2 * (first + i) + f][...]
+
+        middle = (row == 1) | (row == 2)
+        put(0, (0, 1))
+        pl.when(middle)(lambda: put(2, (3, 2)))
+        pl.when(jnp.logical_not(middle))(lambda: put(4, (2, 3)))
 
     return call(
         kernel,
-        jax.ShapeDtypeStruct((rows, 2, count, width), jnp.bfloat16),
+        jax.ShapeDtypeStruct((4, 2, count, width), jnp.bfloat16),
         [place],
-        [*mine, *theirs],
-        read=8 * rows * count * width,
+        pieces,
+        read=40 * count * width,
         limit=WHOLE_VMEM_BYTES,
     )
 
@@ -326,27 +334,33 @@
     half = depth // 2
     place = jnp.stack([row, group, frame, core]).astype(jnp.int32)
 
-    tables = jnp.concatenate([win_blocks, win_counts[:, None], block_window[:, None]], axis=1)
-    found = [tables] + [swap(tables, "rows", s) for s in range(1, rows_n)]
-    tables = jnp.stack(found)[row ^ jnp.arange(rows_n)].reshape(rows_n * heads_n, MAXB + 2)
-    windows = lax.dynamic_index_in_dim(
-        tables[:, MAXB + 1].reshape(rows_n, heads_n), core, axis=1, keepdims=False
-    )
-    picked = tables[windows]
-    members, counts = picked[:, :MAXB].reshape(-1), picked[:, MAXB]
-
-    mine = [lax.dynamic_slice_in_dim(latents[0], core * span * depth, span * depth, axis=1)]
-    mine = [after(mine[0], members, counts)]
-    mine += [swap(mine[0], "rows", s) for s in range(1, rows_n)]
-    theirs = [swap(x, "frames") for x in mine]
-    tokens = assemble(place, mine, theirs)
-
-    across = swap(after(w_out, mine[1]), "heads")
-    beside = swap(after(w_out, mine[3]), "rows")
+    mine = lax.dynamic_slice_in_dim(latents[0], core * span * depth, span * depth, axis=1)
+
+    def over_frames(value, rows):
+        pairs = [(2 * r + f, 2 * r + 1 - f) for r in rows for f in range(2)]
+        return lax.ppermute(value, ("rows", "frames"), pairs)
+
+    mine_x = swap(mine, "frames")
+    beside_1 = swap(mine, "rows")
+    in_1 = lax.ppermute(mine, "rows", [(1, 2), (2, 1)])
+    beside_1x = swap(beside_1, "frames")
+    in_2 = lax.ppermute(after(beside_1, in_1), "rows", [(1, 2), (2, 1)])
+    out_1 = lax.ppermute(in_1, "rows", [(1, 0), (2, 3)])
+    in_1x = over_frames(in_1, (1, 2))
+    out_2 = lax.ppermute(in_2, "rows", [(1, 0), (2, 3)])
+    in_2x = over_frames(in_2, (1, 2))
+    out_1x = over_frames(out_1, (0, 3))
+    out_2x = over_frames(out_2, (0, 3))
+    tokens = assemble(
+        place,
+        [(mine, mine_x), (beside_1, beside_1x)],
+        [(in_1, in_1x), (in_2, in_2x)],
+        [(out_1, out_1x), (out_2, out_2x)],
+    )
 
     by_part = w_qkv.transpose(1, 0, 2)
     last = cols // (3 * HD) * HD
-    waits = [[mine[1]], [mine[2]], [mine[3], theirs[0]], [theirs[1], across]]
+    waits = [[beside_1, in_1, mine_x], [in_2, beside_1x], [out_1, in_1x], [out_2, in_2x, out_1x]]
     here, there = [], []
     for first, wide in ((0, cols - last), (cols - last, last)):
         for k in range(span):
@@ -358,10 +372,21 @@
             piece = lax.dynamic_slice(
                 by_part, (0, group * half, (k + row) % span * cols + first), (3, half, wide)
             )
-            piece = after(piece, *waits[len(here)], *here[-2:-1])
+            piece = after(piece, *waits[len(here)], *here[-2:-1], *there[-3:-2])
             here.append(lax.ppermute(piece, ("rows", "heads"), pairs))
-    for i, piece in enumerate(here):
-        there.append(swap(after(piece, tokens) if i == 2 else piece, "groups"))
+            there.append(swap(here[-1], "groups"))
+    across = swap(after(w_out, here[0]), "heads")
+    beside = swap(after(w_out, here[1]), "rows")
+
+    tables = jnp.concatenate([win_blocks, win_counts[:, None], block_window[:, None]], axis=1)
+    tables = after(tables, here[0])
+    found = [tables] + [swap(tables, "rows", s) for s in range(1, rows_n)]
+    tables = jnp.stack(found)[row ^ jnp.arange(rows_n)].reshape(rows_n * heads_n, MAXB + 2)
+    windows = lax.dynamic_index_in_dim(
+        tables[:, MAXB + 1].reshape(rows_n, heads_n), core, axis=1, keepdims=False
+    )
+    picked = tables[windows]
+    members, counts = picked[:, :MAXB].reshape(-1), picked[:, MAXB]
 
     attended = [[] for _ in range(rows_n)]
     send = None
@@ -369,11 +394,11 @@
         chunks = [[here[i], there[i]] for i in range(part * span, (part + 1) * span)]
         if part:
             chunks[-1][-1] = after(chunks[-1][-1], send)
+        else:
+            chunks[-1][-1] = after(chunks[-1][-1], there[2], members, counts)
         queries, keyvals, send = project(place, tokens, chunks)
-        if part == 0:
-            keyvals = after(keyvals, beside)
-        else:
-            keyvals = after(keyvals, attended[0][0])
+        if part:
+            keyvals = after(keyvals, attended[0][0], beside)
         same, diff = attend_all(place, members, counts, queries, keyvals, swap(send, "heads"))
         for s in range(rows_n):
             attended[s].append(swap(same if s % 2 == 0 else diff, "rows", s) if s else same)

time: 178 us -> 172 us (0.966)
  waiting for transfers between devices: 86.7 us -> 79.5 us
  starting transfers between devices: 54.7 us -> 56.5 us
    ppermute x27 -> x23, waiting for transfers between devices: 84 us -> 59.6 us  [swap(): return lax.ppermute(value, axis, [(i, i ^ step) for i in range(peers)])]
    ppermute x27 -> x23, starting transfers between devices: 41.8 us -> 26.8 us  [swap(): return lax.ppermute(value, axis, [(i, i ^ step) for i in range(peers)])]
    ppermute x0 -> x8, starting transfers between devices: none -> 14.6 us  [the longest x4 9.82 us: over_frames(): return lax.ppermute(value, ('rows', 'frames'), pairs)]
    ppermute x4, waiting for transfers between devices: 0.01 us -> 11.4 us  [by_heads(): here.append(lax.ppermute(piece, ('rows', 'heads'), pairs))]
    ppermute x0 -> x8, waiting for transfers between devices: none -> 6.49 us  [the longest x4 6.48 us: over_frames(): return lax.ppermute(value, ('rows', 'frames'), pairs)]
  transfers between devices with their start and end apart: 32 -> 36, of which waited for: 13 -> 12; matrix products, arithmetic and copies ran while one was open for 3% -> 4% of each run, Pallas kernels for 11% -> 12%
where the time goes in v7:
time: 172 us; the launch traced here: 171 us
  waiting for transfers between devices  79.5 us (46%)
  starting transfers between devices  56.5 us (33%)
  Pallas kernels  23.9 us (14%)
  local copies, waits for them, and re-layouts  9.71 us (6%)
    ppermute x23, waiting for transfers between devices, swap(): return lax.ppermute(value, axis, [(i, i ^ step) for i in range(peers)])  59.6 us
    ppermute x23, starting transfers between devices, swap(): return lax.ppermute(value, axis, [(i, i ^ step) for i in range(peers)])  26.8 us
    pallas_call x7, Pallas kernels, call(): pl.pallas_call(kernel, out_shape=out_shape, grid_spec=pltpu.PrefetchScala...  23.9 us
    ppermute x4, starting transfers between devices, by_heads(): here.append(lax.ppermute(piece, ('rows', 'heads'), pairs))  12.2 us
    ppermute x4, waiting for transfers between devices, by_heads(): here.append(lax.ppermute(piece, ('rows', 'heads'), pairs))  11.4 us
    ppermute x4, starting transfers between devices, over_frames(): return lax.ppermute(value, ('rows', 'frames'), pairs)  9.82 us
    ppermute x4, waiting for transfers between devices, over_frames(): return lax.ppermute(value, ('rows', 'frames'), pairs)  6.48 us
    dynamic_slice x2, local copies, waits for them, and re-layouts, by_heads(): lax.dynamic_slice(by_part, (0, group * half, (k + row) % span * cols + fi...  4.13 us
  transfers between devices with their start and end apart: 36, of which 12 were waited for; matrix products, arithmetic and copies ran while one was open for 4% of the time, Pallas kernels for 12%

profile of v7, /device:TPU:0, one launch (start us, length us, event | category | flops | bytes accessed | tf_op | source)
XLA Modules:
  0.0 171.0 jit_solution(571703246401813273)
XLA Ops:
  0.0 1.1 copy-done
  1.2 0.8 collective-permute-start.1
  2.0 5.9 %collective-permute-start = (bf16[128,1536]{1,0:T(8,128)(2,1)S(1)}, bf16[128,1536]{1,0:T(8,128)(2,1)}, u32[]{:S(2)}, u32[]{:S(2)}) collective-permute-start(bf16[128,1536]{1,0:T(8,128)(2,1)S(1)} %dynamic-slice_bitcast_fusion.2.refs_0_), channel_id=1, source_target_pairs={{0,4},{4,0},{8,12},{12,8},{1,5},{5,1},{9,13},{13,9},{2,6},{6,2},{1... | collective-permute-start | bytes 1179656 | tf_op jit(solution)/shard_map/ppermute | solution.py:107
  7.9 1.5 collective-permute-start.2
  9.4 7.4 %collective-permute-done.refs_2_ = bf16[128,1536]{1,0:T(8,128)(2,1)} collective-permute-done((bf16[128,1536]{1,0:T(8,128)(2,1)S(1)}, bf16[128,1536]{1,0:T(8,128)(2,1)}, u32[]{:S(2)}, u32[]{:S(2)}) %collective-permute-start) | collective-permute-done | bytes 393248 | tf_op jit(solution)/shard_map/ppermute | solution.py:107
  16.9 1.4 collective-permute-start.9
  18.3 1.5 collective-permute-start.7
  19.8 1.3 collective-permute-start.11
  21.1 1.6 collective-permute-start.8
  22.7 2.2 %dynamic-slice_bitcast_fusion = (bf16[3,384,256]{2,1,0:T(8,128)(2,1)S(1)}, bf16[3,384,256]{2,1,0:T(8,128)(2,1)}) fusion(bf16[768,3,768]{2,0,1:T(8,128)(2,1)} %param.7, s32[]{:T(128)S(6)} %select_n.54, s32[]{:T(128)S(6)} %select_n.62, s32[]{:T(128)S(6)} %select_n.56), kind=kLoop, calls=%fused_computation.2 | loop fusion | bytes 2359308 | tf_op jit(solution)/shard_map/dynamic_slice | solution.py:372
  24.9 6.0 %collective-permute-start.3 = (bf16[3,384,256]{2,1,0:T(8,128)(2,1)}, bf16[3,384,256]{2,1,0:T(8,128)(2,1)}, u32[]{:S(2)}, u32[]{:S(2)}) collective-permute-start(bf16[3,384,256]{2,1,0:T(8,128)(2,1)} %get-tuple-element.30), channel_id=1, source_target_pairs={{0,0},{1,8},{4,4},{5,12},{8,1},{9,9},{12,5},{13,13},{2,2},{3,10},{... | collective-permute-start | bytes 1769480 | tf_op jit(solution)/shard_map/ppermute | solution.py:376
  30.8 4.6 %collective-permute-start.16 = (bf16[3,384,256]{2,1,0:T(8,128)(2,1)S(1)}, bf16[3,384,256]{2,1,0:T(8,128)(2,1)S(1)}, u32[]{:S(2)}, u32[]{:S(2)}) collective-permute-start(bf16[3,384,256]{2,1,0:T(8,128)(2,1)S(1)} %get-tuple-element.33), channel_id=1, source_target_pairs={{0,4},{1,12},{4,0},{5,8},{8,5},{9,13},{12,1},{13,9},{2,6},{3,14},{... | collective-permute-start | bytes 1769480 | tf_op jit(solution)/shard_map/ppermute | solution.py:376
  35.4 1.3 collective-permute-start.13
  36.7 1.4 collective-permute-start.10
  38.2 0.7 copy.9
  39.0 3.4 %collective-permute-start.12 = (bf16[128,1536]{1,0:T(8,128)(2,1)}, bf16[128,1536]{1,0:T(8,128)(2,1)}, u32[]{:S(2)}, u32[]{:S(2)}) collective-permute-start(bf16[128,1536]{1,0:T(8,128)(2,1)} %collective-permute-done.11.refs_8_), channel_id=1, source_target_pairs={{0,2},{2,0},{12,14},{14,12},{1,3},{3,1},{13,15},{15,13},{16,18},{1... | collective-permute-start | bytes 1179656 | tf_op jit(solution)/shard_map/ppermute | solution.py:341
  42.5 1.9 %dynamic-slice_bitcast_fusion.3 = (bf16[3,384,128]{2,1,0:T(8,128)(2,1)}, bf16[3,384,128]{2,1,0:T(8,128)(2,1)}) fusion(bf16[768,3,768]{2,0,1:T(8,128)(2,1)} %param.7, s32[]{:T(128)S(6)} %select_n.54, s32[]{:T(128)S(6)} %select_n.64, s32[]{:T(128)S(6)} %select_n.63), kind=kLoop, calls=%fused_computation.5 | loop fusion | bytes 1179660 | tf_op jit(solution)/shard_map/dynamic_slice | solution.py:372
  44.4 4.0 %collective-permute-start.5 = (s32[2,6]{1,0:T(2,128)S(1)}, s32[2,6]{1,0:T(2,128)S(1)}, u32[]{:S(2)}, u32[]{:S(2)}) collective-permute-start(s32[2,6]{1,0:T(2,128)S(1)} %pad_add_fusion.1), channel_id=1, source_target_pairs={{0,8},{4,12},{8,0},{12,4},{1,9},{5,13},{9,1},{13,5},{2,10},{6,14},... | collective-permute-start | bytes 152 | tf_op jit(solution)/shard_map/ppermute | solution.py:107
  48.5 11.3 %collective-permute-done.16.refs_2_ = bf16[3,384,256]{2,1,0:T(8,128)(2,1)S(1)} collective-permute-done((bf16[3,384,256]{2,1,0:T(8,128)(2,1)S(1)}, bf16[3,384,256]{2,1,0:T(8,128)(2,1)S(1)}, u32[]{:S(2)}, u32[]{:S(2)}) %collective-permute-start.16) | collective-permute-done | bytes 589856 | tf_op jit(solution)/shard_map/ppermute | solution.py:376
  59.9 5.3 %collective-permute-done.6 = s32[2,6]{1,0:T(2,128)S(1)} collective-permute-done((s32[2,6]{1,0:T(2,128)S(1)}, s32[2,6]{1,0:T(2,128)S(1)}, u32[]{:S(2)}, u32[]{:S(2)}) %collective-permute-start.6) | collective-permute-done | bytes 80 | tf_op jit(solution)/shard_map/ppermute | solution.py:107
  65.2 1.6 collective-permute-start.18
  66.8 1.5 collective-permute-start.15
  69.0 0.6 pad_add_fusion.2.place_ref
  69.7 3.4 %collective-permute-start.14 = (bf16[128,1536]{1,0:T(8,128)(2,1)}, bf16[128,1536]{1,0:T(8,128)(2,1)}, u32[]{:S(2)}, u32[]{:S(2)}) collective-permute-start(bf16[128,1536]{1,0:T(8,128)(2,1)} %collective-permute-done.13.refs_10_), channel_id=1, source_target_pairs={{0,2},{2,0},{12,14},{14,12},{1,3},{3,1},{13,15},{15,13},{16,18},{1... | collective-permute-start | bytes 1179656 | tf_op jit(solution)/shard_map/ppermute | solution.py:341
  73.7 1.6 collective-permute-start.19
  76.6 6.5 %collective-permute-done.14.refs_11_ = bf16[128,1536]{1,0:T(8,128)(2,1)} collective-permute-done((bf16[128,1536]{1,0:T(8,128)(2,1)}, bf16[128,1536]{1,0:T(8,128)(2,1)}, u32[]{:S(2)}, u32[]{:S(2)}) %collective-permute-start.14) | collective-permute-done | bytes 393248 | tf_op jit(solution)/shard_map/ppermute | solution.py:341
  83.1 5.0 %shard_map.64.x_ref = bf16[4,2,128,1536]{3,2,1,0:T(8,128)(2,1)} custom-call(s32[4]{0:T(128)} %pad_add_fusion.2.place_ref, bf16[128,1536]{1,0:T(8,128)(2,1)} %copy-done.6, bf16[128,1536]{1,0:T(8,128)(2,1)} %collective-permute-done.2.refs_1_, bf16[128,1536]{1,0:T(8,128)(2,1)} %collective-permute-done.refs_2_, ...), custom_call_target="tpu_custom_call" | custom-call | bytes 7864320 | tf_op jit(solution)/shard_map/pallas_call | solution.py:115
  88.2 12.6 %collective-permute-done.19.refs_1_ = bf16[3,384,128]{2,1,0:T(8,128)(2,1)} collective-permute-done((bf16[3,384,128]{2,1,0:T(8,128)(2,1)S(1)}, bf16[3,384,128]{2,1,0:T(8,128)(2,1)}, u32[]{:S(2)}, u32[]{:S(2)}) %collective-permute-start.19) | collective-permute-done | bytes 294944 | tf_op jit(solution)/shard_map/ppermute | solution.py:107
  100.9 1.9 %copy-done.1 = bf16[4,2,128,1536]{3,2,1,0:T(8,128)(2,1)S(1)} copy-done((bf16[4,2,128,1536]{3,2,1,0:T(8,128)(2,1)S(1)}, bf16[4,2,128,1536]{3,2,1,0:T(8,128)(2,1)}, u32[]{:S(2)}) %copy-start.1) | copy-done | bytes 3145752
  102.7 5.5 %shard_map.65 = (f32[4,128,256]{2,1,0:T(8,128)S(1)}, f32[4,256,512]{2,1,0:T(8,128)S(1)}, bf16[4,320,512]{2,1,0:T(8,128)(2,1)S(1)}) custom-call(s32[4]{0:T(128)S(1)} %copy-done.3, bf16[4,2,128,1536]{3,2,1,0:T(8,128)(2,1)S(1)} %copy-done.1, bf16[3,384,256]{2,1,0:T(8,128)(2,1)} %collective-permute-done.3.refs_0_, ...), custom_call_target="tpu_custom_call" | custom-call | flops 2415919104 | bytes 8053063 | tf_op jit(solution)/shard_map/pallas_call | solution.py:115
  108.8 1.5 collective-permute-start.22
  110.3 7.5 %collective-permute-done.22.refs_3_ = bf16[3,384,128]{2,1,0:T(8,128)(2,1)S(1)} collective-permute-done((bf16[3,384,128]{2,1,0:T(8,128)(2,1)S(1)}, bf16[3,384,128]{2,1,0:T(8,128)(2,1)S(1)}, u32[]{:S(2)}, u32[]{:S(2)}) %collective-permute-start.22) | collective-permute-done | bytes 294944 | tf_op jit(solution)/shard_map/ppermute | solution.py:107
  117.8 3.6 %shard_map.67 = (f32[4,128,128]{2,1,0:T(8,128)S(1)}, f32[4,256,256]{2,1,0:T(8,128)S(1)}, bf16[4,320,256]{2,1,0:T(8,128)(2,1)S(1)}) custom-call(s32[4]{0:T(128)S(1)} %copy-done.3, bf16[4,2,128,1536]{3,2,1,0:T(8,128)(2,1)S(1)} %copy-done.1, bf16[3,384,128]{2,1,0:T(8,128)(2,1)S(1)} %collective-permute-done.18.refs_0_, ...), custom_call_target="tpu_custom_call" | custom-call | flops 1207959552 | bytes 4026531 | tf_op jit(solution)/shard_map/pallas_call | solution.py:115
  121.5 3.8 %shard_map.66 = (bf16[2,128,256]{2,1,0:T(8,128)(2,1)S(1)}, bf16[2,128,256]{2,1,0:T(8,128)(2,1)S(1)}) custom-call(s32[4]{0:T(128)S(1)} %copy-done.3, s32[16]{0:T(128)S(1)} %reshape.24.members_ref, s32[4]{0:T(128)S(1)} %slice_reduce_fusion.1.counts_ref, f32[4,128,256]{2,1,0:T(8,128)S(1)} %get-tuple-element.36.q_ref, ...), custom_call_target="tpu_custom_call" | custom-call | flops 268435456 | bytes 2097152 | tf_op jit(solution)/shard_map/pallas_call | solution.py:115
  125.3 2.2 %shard_map.68 = (bf16[2,128,128]{2,1,0:T(8,128)(2,1)S(1)}, bf16[2,128,128]{2,1,0:T(8,128)(2,1)S(1)}) custom-call(s32[4]{0:T(128)S(1)} %copy-done.3, s32[16]{0:T(128)S(1)} %reshape.24.members_ref, s32[4]{0:T(128)S(1)} %slice_reduce_fusion.1.counts_ref, f32[4,128,128]{2,1,0:T(8,128)S(1)} %get-tuple-element.42.q_ref, ...), custom_call_target="tpu_custom_call" | custom-call | flops 134217728 | bytes 1048576 | tf_op jit(solution)/shard_map/pallas_call | solution.py:115
  127.6 2.9 %collective-permute-start.28 = (bf16[2,128,128]{2,1,0:T(8,128)(2,1)S(1)}, bf16[2,128,128]{2,1,0:T(8,128)(2,1)S(1)}, u32[]{:S(2)}, u32[]{:S(2)}) collective-permute-start(bf16[2,128,128]{2,1,0:T(8,128)(2,1)S(1)} %get-tuple-element.47.refs_1_), channel_id=1, source_target_pairs={{0,8},{4,12},{8,0},{12,4},{1,9},{5,13},{9,1},{13,5},{2,10},{6,14},... | collective-permute-start | bytes 196616 | tf_op jit(solution)/shard_map/ppermute | solution.py:107
  130.6 1.9 %collective-permute-start.25 = (bf16[2,128,256]{2,1,0:T(8,128)(2,1)S(1)}, bf16[2,128,256]{2,1,0:T(8,128)(2,1)S(1)}, u32[]{:S(2)}, u32[]{:S(2)}) collective-permute-start(bf16[2,128,256]{2,1,0:T(8,128)(2,1)S(1)} %get-tuple-element.48), channel_id=1, source_target_pairs={{0,4},{4,0},{8,12},{12,8},{1,5},{5,1},{9,13},{13,9},{2,6},{6,2},{1... | collective-permute-start | bytes 393224 | tf_op jit(solution)/shard_map/ppermute | solution.py:107
  132.5 0.7 collective-permute-done.26.refs_3_
  133.2 10.1 %collective-permute-done.28.refs_5_ = bf16[2,128,128]{2,1,0:T(8,128)(2,1)S(1)} collective-permute-done((bf16[2,128,128]{2,1,0:T(8,128)(2,1)S(1)}, bf16[2,128,128]{2,1,0:T(8,128)(2,1)S(1)}, u32[]{:S(2)}, u32[]{:S(2)}) %collective-permute-start.28) | collective-permute-done | bytes 65568 | tf_op jit(solution)/shard_map/ppermute | solution.py:107
  143.3 1.3 collective-permute-start.30
  144.6 4.7 %collective-permute-done.30.refs_7_ = bf16[2,128,128]{2,1,0:T(8,128)(2,1)S(1)} collective-permute-done((bf16[2,128,128]{2,1,0:T(8,128)(2,1)S(1)}, bf16[2,128,128]{2,1,0:T(8,128)(2,1)S(1)}, u32[]{:S(2)}, u32[]{:S(2)}) %collective-permute-start.30) | collective-permute-done | bytes 65568 | tf_op jit(solution)/shard_map/ppermute | solution.py:107
  149.4 2.5 %shard_map.69 = (f32[2,64,768]{2,1,0:T(8,128)S(1)}, bf16[2,64,768]{2,1,0:T(8,128)(2,1)S(1)}, bf16[2,64,768]{2,1,0:T(8,128)(2,1)S(1)}, bf16[2,64,768]{2,1,0:T(8,128)(2,1)S(1)}) custom-call(s32[4]{0:T(128)S(1)} %copy-done.3, bf16[2,128,256]{2,1,0:T(8,128)(2,1)S(1)} %get-tuple-element.39.refs_0_, bf16[2,128,128]{2,1,0:T(8,128)(2,1)S(1)} %get-tuple-element.47.refs_1_, ...), custom_call_target="tpu_custom_call" | custom-call | flops 1207959552 | bytes 4718592 | tf_op jit(solution)/shard_map/pallas_call | solution.py:115
  151.9 1.5 collective-permute-start.33
  153.4 2.9 %collective-permute-start.35 = (bf16[2,64,768]{2,1,0:T(8,128)(2,1)S(1)}, bf16[2,64,768]{2,1,0:T(8,128)(2,1)S(1)}, u32[]{:S(2)}, u32[]{:S(2)}) collective-permute-start(bf16[2,64,768]{2,1,0:T(8,128)(2,1)S(1)} %get-tuple-element.54), channel_id=1, source_target_pairs={{0,10},{2,8},{4,14},{6,12},{8,2},{10,0},{12,6},{14,4},{1,11},{3,9}... | collective-permute-start | bytes 589832 | tf_op jit(solution)/shard_map/ppermute | solution.py:411
  156.3 1.3 collective-permute-done.33.x_ref
  157.6 9.9 %collective-permute-done.34.z_ref = bf16[2,64,768]{2,1,0:T(8,128)(2,1)S(1)} collective-permute-done((bf16[2,64,768]{2,1,0:T(8,128)(2,1)S(1)}, bf16[2,64,768]{2,1,0:T(8,128)(2,1)S(1)}, u32[]{:S(2)}, u32[]{:S(2)}) %collective-permute-start.34) | collective-permute-done | bytes 196640 | tf_op jit(solution)/shard_map/ppermute | solution.py:107
  167.5 2.1 %collective-permute-done.35.both_ref = bf16[2,64,768]{2,1,0:T(8,128)(2,1)S(1)} collective-permute-done((bf16[2,64,768]{2,1,0:T(8,128)(2,1)S(1)}, bf16[2,64,768]{2,1,0:T(8,128)(2,1)S(1)}, u32[]{:S(2)}, u32[]{:S(2)}) %collective-permute-start.35) | collective-permute-done | bytes 196640 | tf_op jit(solution)/shard_map/ppermute | solution.py:411
  169.6 1.4 shard_map.70
  (71 shorter events, 3.9 us)
Async XLA Ops:
  0.0 1.1 copy-start
  1.2 29.7 %copy-start.6 = (bf16[128,1536]{1,0:T(8,128)(2,1)}, bf16[128,1536]{1,0:T(8,128)(2,1)S(1)}, u32[]{:S(2)}) copy-start(bf16[128,1536]{1,0:T(8,128)(2,1)S(1)} %dynamic-slice_bitcast_fusion.2.refs_0_) | copy-start | bytes 1179652
  1.2 37.0 %copy-start.10 = (s32[2]{0:T(128)S(1)}, s32[2]{0:T(128)}, u32[]{:S(2)}) copy-start(s32[2]{0:T(128)} %param.11) | copy-start | bytes 28
  1.2 41.2 %copy-start.9 = (s32[2,4]{1,0:T(2,128)S(1)}, s32[2,4]{1,0:T(2,128)}, u32[]{:S(2)}) copy-start(s32[2,4]{1,0:T(2,128)} %param.9) | copy-start | bytes 100
  1.2 8.2 %collective-permute-start.1 = (bf16[128,1536]{1,0:T(8,128)(2,1)S(1)}, bf16[128,1536]{1,0:T(8,128)(2,1)S(1)}, u32[]{:S(2)}, u32[]{:S(2)}) collective-permute-start(bf16[128,1536]{1,0:T(8,128)(2,1)S(1)} %dynamic-slice_bitcast_fusion.2.refs_0_), channel_id=1, source_target_pairs={{4,8},{8,4},{5,9},{9,5},{6,10},{10,6},{7,11},{11,7},{20,24},{24,20... | collective-permute-start | bytes 1179656 | tf_op jit(solution)/shard_map/ppermute | solution.py:345
  2.0 14.8 %collective-permute-start = (bf16[128,1536]{1,0:T(8,128)(2,1)S(1)}, bf16[128,1536]{1,0:T(8,128)(2,1)}, u32[]{:S(2)}, u32[]{:S(2)}) collective-permute-start(bf16[128,1536]{1,0:T(8,128)(2,1)S(1)} %dynamic-slice_bitcast_fusion.2.refs_0_), channel_id=1, source_target_pairs={{0,4},{4,0},{8,12},{12,8},{1,5},{5,1},{9,13},{13,9},{2,6},{6,2},{1... | collective-permute-start | bytes 1179656 | tf_op jit(solution)/shard_map/ppermute | solution.py:107
  7.9 16.9 %collective-permute-start.2 = (bf16[128,1536]{1,0:T(8,128)(2,1)S(1)}, bf16[128,1536]{1,0:T(8,128)(2,1)}, u32[]{:S(2)}, u32[]{:S(2)}) collective-permute-start(bf16[128,1536]{1,0:T(8,128)(2,1)S(1)} %dynamic-slice_bitcast_fusion.2.refs_0_), channel_id=1, source_target_pairs={{0,2},{2,0},{1,3},{3,1},{4,6},{6,4},{5,7},{7,5},{8,10},{10,8},{9,1... | collective-permute-start | bytes 1179656 | tf_op jit(solution)/shard_map/ppermute | solution.py:107
  9.4 35.0 %copy-start.7 = (bf16[128,1536]{1,0:T(8,128)(2,1)}, bf16[128,1536]{1,0:T(8,128)(2,1)S(1)}, u32[]{:S(2)}) copy-start(bf16[128,1536]{1,0:T(8,128)(2,1)S(1)} %collective-permute-done.1.refs_4_) | copy-start | bytes 1179652
  16.9 14.0 %collective-permute-start.9 = (bf16[128,1536]{1,0:T(8,128)(2,1)}, bf16[128,1536]{1,0:T(8,128)(2,1)}, u32[]{:S(2)}, u32[]{:S(2)}) collective-permute-start(bf16[128,1536]{1,0:T(8,128)(2,1)} %collective-permute-done.refs_2_), channel_id=1, source_target_pairs={{4,8},{8,4},{5,9},{9,5},{6,10},{10,6},{7,11},{11,7},{20,24},{24,20... | collective-permute-start | bytes 1179656 | tf_op jit(solution)/shard_map/ppermute | solution.py:347
  18.3 12.6 %collective-permute-start.7 = (bf16[128,1536]{1,0:T(8,128)(2,1)}, bf16[128,1536]{1,0:T(8,128)(2,1)}, u32[]{:S(2)}, u32[]{:S(2)}) collective-permute-start(bf16[128,1536]{1,0:T(8,128)(2,1)} %collective-permute-done.refs_2_), channel_id=1, source_target_pairs={{0,2},{2,0},{1,3},{3,1},{4,6},{6,4},{5,7},{7,5},{8,10},{10,8},{9,1... | collective-permute-start | bytes 1179656 | tf_op jit(solution)/shard_map/ppermute | solution.py:107
  19.8 16.9 %collective-permute-start.11 = (bf16[128,1536]{1,0:T(8,128)(2,1)S(1)}, bf16[128,1536]{1,0:T(8,128)(2,1)}, u32[]{:S(2)}, u32[]{:S(2)}) collective-permute-start(bf16[128,1536]{1,0:T(8,128)(2,1)S(1)} %collective-permute-done.1.refs_4_), channel_id=1, source_target_pairs={{4,0},{8,12},{5,1},{9,13},{6,2},{10,14},{7,3},{11,15},{20,16},{24,... | collective-permute-start | bytes 1179656 | tf_op jit(solution)/shard_map/ppermute | solution.py:348
  21.1 47.3 %copy-start.2 = (bf16[768,768]{1,0:T(8,128)(2,1)S(1)}, bf16[768,768]{1,0:T(8,128)(2,1)}, u32[]{:S(2)}) copy-start(bf16[768,768]{1,0:T(8,128)(2,1)} %refs_8_.1) | copy-start | bytes 3538948
  21.1 17.9 %collective-permute-start.8 = (bf16[128,1536]{1,0:T(8,128)(2,1)S(1)}, bf16[128,1536]{1,0:T(8,128)(2,1)}, u32[]{:S(2)}, u32[]{:S(2)}) collective-permute-start(bf16[128,1536]{1,0:T(8,128)(2,1)S(1)} %collective-permute-done.1.refs_4_), channel_id=1, source_target_pairs={{4,6},{6,4},{8,10},{10,8},{5,7},{7,5},{9,11},{11,9},{20,22},{22,20... | collective-permute-start | bytes 1179656 | tf_op jit(solution)/shard_map/ppermute | solution.py:341
  24.9 19.6 %collective-permute-start.3 = (bf16[3,384,256]{2,1,0:T(8,128)(2,1)}, bf16[3,384,256]{2,1,0:T(8,128)(2,1)}, u32[]{:S(2)}, u32[]{:S(2)}) collective-permute-start(bf16[3,384,256]{2,1,0:T(8,128)(2,1)} %get-tuple-element.30), channel_id=1, source_target_pairs={{0,0},{1,8},{4,4},{5,12},{8,1},{9,9},{12,5},{13,13},{2,2},{3,10},{... | collective-permute-start | bytes 1769480 | tf_op jit(solution)/shard_map/ppermute | solution.py:376
  30.8 29.0 %collective-permute-start.16 = (bf16[3,384,256]{2,1,0:T(8,128)(2,1)S(1)}, bf16[3,384,256]{2,1,0:T(8,128)(2,1)S(1)}, u32[]{:S(2)}, u32[]{:S(2)}) collective-permute-start(bf16[3,384,256]{2,1,0:T(8,128)(2,1)S(1)} %get-tuple-element.33), channel_id=1, source_target_pairs={{0,4},{1,12},{4,0},{5,8},{8,5},{9,13},{12,1},{13,9},{2,6},{3,14},{... | collective-permute-start | bytes 1769480 | tf_op jit(solution)/shard_map/ppermute | solution.py:376
  35.4 32.9 %collective-permute-start.13 = (bf16[128,1536]{1,0:T(8,128)(2,1)}, bf16[128,1536]{1,0:T(8,128)(2,1)}, u32[]{:S(2)}, u32[]{:S(2)}) collective-permute-start(bf16[128,1536]{1,0:T(8,128)(2,1)} %collective-permute-done.9.refs_6_), channel_id=1, source_target_pairs={{4,0},{8,12},{5,1},{9,13},{6,2},{10,14},{7,3},{11,15},{20,16},{24,... | collective-permute-start | bytes 1179656 | tf_op jit(solution)/shard_map/ppermute | solution.py:350
  36.7 31.7 %collective-permute-start.10 = (bf16[128,1536]{1,0:T(8,128)(2,1)}, bf16[128,1536]{1,0:T(8,128)(2,1)}, u32[]{:S(2)}, u32[]{:S(2)}) collective-permute-start(bf16[128,1536]{1,0:T(8,128)(2,1)} %collective-permute-done.9.refs_6_), channel_id=1, source_target_pairs={{4,6},{6,4},{8,10},{10,8},{5,7},{7,5},{9,11},{11,9},{20,22},{22,20... | collective-permute-start | bytes 1179656 | tf_op jit(solution)/shard_map/ppermute | solution.py:341
  39.0 30.7 %collective-permute-start.12 = (bf16[128,1536]{1,0:T(8,128)(2,1)}, bf16[128,1536]{1,0:T(8,128)(2,1)}, u32[]{:S(2)}, u32[]{:S(2)}) collective-permute-start(bf16[128,1536]{1,0:T(8,128)(2,1)} %collective-permute-done.11.refs_8_), channel_id=1, source_target_pairs={{0,2},{2,0},{12,14},{14,12},{1,3},{3,1},{13,15},{15,13},{16,18},{1... | collective-permute-start | bytes 1179656 | tf_op jit(solution)/shard_map/ppermute | solution.py:341
  44.4 15.4 %collective-permute-start.5 = (s32[2,6]{1,0:T(2,128)S(1)}, s32[2,6]{1,0:T(2,128)S(1)}, u32[]{:S(2)}, u32[]{:S(2)}) collective-permute-start(s32[2,6]{1,0:T(2,128)S(1)} %pad_add_fusion.1), channel_id=1, source_target_pairs={{0,8},{4,12},{8,0},{12,4},{1,9},{5,13},{9,1},{13,5},{2,10},{6,14},... | collective-permute-start | bytes 152 | tf_op jit(solution)/shard_map/ppermute | solution.py:107
  59.8 8.5 %copy-start.4 = (bf16[3,384,256]{2,1,0:T(8,128)(2,1)}, bf16[3,384,256]{2,1,0:T(8,128)(2,1)S(1)}, u32[]{:S(2)}) copy-start(bf16[3,384,256]{2,1,0:T(8,128)(2,1)S(1)} %collective-permute-done.16.refs_2_) | copy-start | bytes 1769476
  59.8 5.4 %collective-permute-start.6 = (s32[2,6]{1,0:T(2,128)S(1)}, s32[2,6]{1,0:T(2,128)S(1)}, u32[]{:S(2)}, u32[]{:S(2)}) collective-permute-start(s32[2,6]{1,0:T(2,128)S(1)} %pad_add_fusion.1), channel_id=1, source_target_pairs={{0,12},{4,8},{8,4},{12,0},{1,13},{5,9},{9,5},{13,1},{2,14},{6,10},... | collective-permute-start | bytes 152 | tf_op jit(solution)/shard_map/ppermute | solution.py:107
  59.8 7.0 %collective-permute-start.4 = (s32[2,6]{1,0:T(2,128)S(1)}, s32[2,6]{1,0:T(2,128)S(1)}, u32[]{:S(2)}, u32[]{:S(2)}) collective-permute-start(s32[2,6]{1,0:T(2,128)S(1)} %pad_add_fusion.1), channel_id=1, source_target_pairs={{0,4},{4,0},{8,12},{12,8},{1,5},{5,1},{9,13},{13,9},{2,6},{6,2},{1... | collective-permute-start | bytes 152 | tf_op jit(solution)/shard_map/ppermute | solution.py:107
  65.2 8.5 %collective-permute-start.18 = (bf16[3,384,128]{2,1,0:T(8,128)(2,1)}, bf16[3,384,128]{2,1,0:T(8,128)(2,1)S(1)}, u32[]{:S(2)}, u32[]{:S(2)}) collective-permute-start(bf16[3,384,128]{2,1,0:T(8,128)(2,1)} %get-tuple-element.34), channel_id=1, source_target_pairs={{0,0},{1,8},{4,4},{5,12},{8,1},{9,9},{12,5},{13,13},{2,2},{3,10},{... | collective-permute-start | bytes 884744 | tf_op jit(solution)/shard_map/ppermute | solution.py:376
  66.8 21.3 %collective-permute-start.15 = (bf16[3,384,256]{2,1,0:T(8,128)(2,1)}, bf16[3,384,256]{2,1,0:T(8,128)(2,1)}, u32[]{:S(2)}, u32[]{:S(2)}) collective-permute-start(bf16[3,384,256]{2,1,0:T(8,128)(2,1)} %collective-permute-done.3.refs_0_), channel_id=1, source_target_pairs={{0,16},{16,0},{1,17},{17,1},{2,18},{18,2},{3,19},{19,3},{4,20},{20... | collective-permute-start | bytes 1769480 | tf_op jit(solution)/shard_map/ppermute | solution.py:107
  68.3 42.0 %collective-permute-start.23 = (bf16[768,768]{1,0:T(8,128)(2,1)S(1)}, bf16[768,768]{1,0:T(8,128)(2,1)S(1)}, u32[]{:S(2)}, u32[]{:S(2)}) collective-permute-start(bf16[768,768]{1,0:T(8,128)(2,1)S(1)} %copy-done.2), channel_id=1, source_target_pairs={{0,4},{4,0},{8,12},{12,8},{1,5},{5,1},{9,13},{13,9},{2,6},{6,2},{1... | collective-permute-start | bytes 3538952 | tf_op jit(solution)/shard_map/ppermute | solution.py:107
  68.4 32.4 %collective-permute-start.17 = (bf16[3,384,256]{2,1,0:T(8,128)(2,1)}, bf16[3,384,256]{2,1,0:T(8,128)(2,1)}, u32[]{:S(2)}, u32[]{:S(2)}) collective-permute-start(bf16[3,384,256]{2,1,0:T(8,128)(2,1)} %copy-done.4), channel_id=1, source_target_pairs={{0,16},{16,0},{1,17},{17,1},{2,18},{18,2},{3,19},{19,3},{4,20},{20... | collective-permute-start | bytes 1769480 | tf_op jit(solution)/shard_map/ppermute | solution.py:107
  69.7 13.4 %collective-permute-start.14 = (bf16[128,1536]{1,0:T(8,128)(2,1)}, bf16[128,1536]{1,0:T(8,128)(2,1)}, u32[]{:S(2)}, u32[]{:S(2)}) collective-permute-start(bf16[128,1536]{1,0:T(8,128)(2,1)} %collective-permute-done.13.refs_10_), channel_id=1, source_target_pairs={{0,2},{2,0},{12,14},{14,12},{1,3},{3,1},{13,15},{15,13},{16,18},{1... | collective-permute-start | bytes 1179656 | tf_op jit(solution)/shard_map/ppermute | solution.py:341
  73.7 27.1 %collective-permute-start.19 = (bf16[3,384,128]{2,1,0:T(8,128)(2,1)S(1)}, bf16[3,384,128]{2,1,0:T(8,128)(2,1)}, u32[]{:S(2)}, u32[]{:S(2)}) collective-permute-start(bf16[3,384,128]{2,1,0:T(8,128)(2,1)S(1)} %collective-permute-done.18.refs_0_), channel_id=1, source_target_pairs={{0,16},{16,0},{1,17},{17,1},{2,18},{18,2},{3,19},{19,3},{4,20},{20... | collective-permute-start | bytes 884744 | tf_op jit(solution)/shard_map/ppermute | solution.py:107
  76.6 11.5 %copy-start.8 = (bf16[3,384,128]{2,1,0:T(8,128)(2,1)S(1)}, bf16[3,384,128]{2,1,0:T(8,128)(2,1)}, u32[]{:S(2)}) copy-start(bf16[3,384,128]{2,1,0:T(8,128)(2,1)} %get-tuple-element.40) | copy-start | bytes 884740
  76.6 24.2 %copy-start.3 = (s32[4]{0:T(128)S(1)}, s32[4]{0:T(128)}, u32[]{:S(2)}) copy-start(s32[4]{0:T(128)} %pad_add_fusion.2.place_ref) | copy-start | bytes 52
  76.6 24.2 %copy-start.5 = (bf16[3,384,256]{2,1,0:T(8,128)(2,1)S(1)}, bf16[3,384,256]{2,1,0:T(8,128)(2,1)}, u32[]{:S(2)}) copy-start(bf16[3,384,256]{2,1,0:T(8,128)(2,1)} %copy-done.4) | copy-start | bytes 1769476
  88.1 20.7 %collective-permute-start.21 = (bf16[3,384,128]{2,1,0:T(8,128)(2,1)S(1)}, bf16[3,384,128]{2,1,0:T(8,128)(2,1)S(1)}, u32[]{:S(2)}, u32[]{:S(2)}) collective-permute-start(bf16[3,384,128]{2,1,0:T(8,128)(2,1)S(1)} %copy-done.8), channel_id=1, source_target_pairs={{0,4},{1,12},{4,0},{5,8},{8,5},{9,13},{12,1},{13,9},{2,6},{3,14},{... | collective-permute-start | bytes 884744 | tf_op jit(solution)/shard_map/ppermute | solution.py:376
  100.9 1.9 %copy-start.1 = (bf16[4,2,128,1536]{3,2,1,0:T(8,128)(2,1)S(1)}, bf16[4,2,128,1536]{3,2,1,0:T(8,128)(2,1)}, u32[]{:S(2)}) copy-start(bf16[4,2,128,1536]{3,2,1,0:T(8,128)(2,1)} %shard_map.64.x_ref) | copy-start | bytes 9437188
  108.2 13.3 %collective-permute-start.20 = (bf16[4,320,512]{2,1,0:T(8,128)(2,1)S(1)}, bf16[4,320,512]{2,1,0:T(8,128)(2,1)S(1)}, u32[]{:S(2)}, u32[]{:S(2)}) collective-permute-start(bf16[4,320,512]{2,1,0:T(8,128)(2,1)S(1)} %get-tuple-element.38), channel_id=1, source_target_pairs={{0,1},{1,0},{2,3},{3,2},{4,5},{5,4},{6,7},{7,6},{8,9},{9,8},{10,11... | collective-permute-start | bytes 3932168 | tf_op jit(solution)/shard_map/ppermute | solution.py:107
  108.3 22.3 %collective-permute-start.31 = (bf16[768,768]{1,0:T(8,128)(2,1)S(1)}, bf16[768,768]{1,0:T(8,128)(2,1)S(1)}, u32[]{:S(2)}, u32[]{:S(2)}) collective-permute-start(bf16[768,768]{1,0:T(8,128)(2,1)S(1)} %copy-done.2), channel_id=1, source_target_pairs={{0,1},{1,0},{2,3},{3,2},{4,5},{5,4},{6,7},{7,6},{8,9},{9,8},{10,11... | collective-permute-start | bytes 3538952 | tf_op jit(solution)/shard_map/ppermute | solution.py:107
  108.8 9.0 %collective-permute-start.22 = (bf16[3,384,128]{2,1,0:T(8,128)(2,1)S(1)}, bf16[3,384,128]{2,1,0:T(8,128)(2,1)S(1)}, u32[]{:S(2)}, u32[]{:S(2)}) collective-permute-start(bf16[3,384,128]{2,1,0:T(8,128)(2,1)S(1)} %collective-permute-done.21.refs_2_), channel_id=1, source_target_pairs={{0,16},{16,0},{1,17},{17,1},{2,18},{18,2},{3,19},{19,3},{4,20},{20... | collective-permute-start | bytes 884744 | tf_op jit(solution)/shard_map/ppermute | solution.py:107
  110.3 39.1 %collective-permute-start.32 = (bf16[768,768]{1,0:T(8,128)(2,1)S(1)}, bf16[768,768]{1,0:T(8,128)(2,1)S(1)}, u32[]{:S(2)}, u32[]{:S(2)}) collective-permute-start(bf16[768,768]{1,0:T(8,128)(2,1)S(1)} %collective-permute-done.23.refs_9_), channel_id=1, source_target_pairs={{0,1},{1,0},{2,3},{3,2},{4,5},{5,4},{6,7},{7,6},{8,9},{9,8},{10,11... | collective-permute-start | bytes 3538952 | tf_op jit(solution)/shard_map/ppermute | solution.py:107
  121.4 3.9 %collective-permute-start.24 = (bf16[4,320,256]{2,1,0:T(8,128)(2,1)S(1)}, bf16[4,320,256]{2,1,0:T(8,128)(2,1)S(1)}, u32[]{:S(2)}, u32[]{:S(2)}) collective-permute-start(bf16[4,320,256]{2,1,0:T(8,128)(2,1)S(1)} %get-tuple-element.46), channel_id=1, source_target_pairs={{0,1},{1,0},{2,3},{3,2},{4,5},{5,4},{6,7},{7,6},{8,9},{9,8},{10,11... | collective-permute-start | bytes 1966088 | tf_op jit(solution)/shard_map/ppermute | solution.py:107
  127.5 5.7 %collective-permute-start.26 = (bf16[2,128,128]{2,1,0:T(8,128)(2,1)S(1)}, bf16[2,128,128]{2,1,0:T(8,128)(2,1)S(1)}, u32[]{:S(2)}, u32[]{:S(2)}) collective-permute-start(bf16[2,128,128]{2,1,0:T(8,128)(2,1)S(1)} %get-tuple-element.49), channel_id=1, source_target_pairs={{0,4},{4,0},{8,12},{12,8},{1,5},{5,1},{9,13},{13,9},{2,6},{6,2},{1... | collective-permute-start | bytes 196616 | tf_op jit(solution)/shard_map/ppermute | solution.py:107
  127.6 21.8 %collective-permute-start.27 = (bf16[2,128,256]{2,1,0:T(8,128)(2,1)S(1)}, bf16[2,128,256]{2,1,0:T(8,128)(2,1)S(1)}, u32[]{:S(2)}, u32[]{:S(2)}) collective-permute-start(bf16[2,128,256]{2,1,0:T(8,128)(2,1)S(1)} %get-tuple-element.39.refs_0_), channel_id=1, source_target_pairs={{0,8},{4,12},{8,0},{12,4},{1,9},{5,13},{9,1},{13,5},{2,10},{6,14},... | collective-permute-start | bytes 393224 | tf_op jit(solution)/shard_map/ppermute | solution.py:107
  127.6 15.7 %collective-permute-start.28 = (bf16[2,128,128]{2,1,0:T(8,128)(2,1)S(1)}, bf16[2,128,128]{2,1,0:T(8,128)(2,1)S(1)}, u32[]{:S(2)}, u32[]{:S(2)}) collective-permute-start(bf16[2,128,128]{2,1,0:T(8,128)(2,1)S(1)} %get-tuple-element.47.refs_1_), channel_id=1, source_target_pairs={{0,8},{4,12},{8,0},{12,4},{1,9},{5,13},{9,1},{13,5},{2,10},{6,14},... | collective-permute-start | bytes 196616 | tf_op jit(solution)/shard_map/ppermute | solution.py:107
  130.6 18.8 %collective-permute-start.25 = (bf16[2,128,256]{2,1,0:T(8,128)(2,1)S(1)}, bf16[2,128,256]{2,1,0:T(8,128)(2,1)S(1)}, u32[]{:S(2)}, u32[]{:S(2)}) collective-permute-start(bf16[2,128,256]{2,1,0:T(8,128)(2,1)S(1)} %get-tuple-element.48), channel_id=1, source_target_pairs={{0,4},{4,0},{8,12},{12,8},{1,5},{5,1},{9,13},{13,9},{2,6},{6,2},{1... | collective-permute-start | bytes 393224 | tf_op jit(solution)/shard_map/ppermute | solution.py:107
  133.2 16.2 %collective-permute-start.29 = (bf16[2,128,256]{2,1,0:T(8,128)(2,1)S(1)}, bf16[2,128,256]{2,1,0:T(8,128)(2,1)S(1)}, u32[]{:S(2)}, u32[]{:S(2)}) collective-permute-start(bf16[2,128,256]{2,1,0:T(8,128)(2,1)S(1)} %get-tuple-element.48), channel_id=1, source_target_pairs={{0,12},{4,8},{8,4},{12,0},{1,13},{5,9},{9,5},{13,1},{2,14},{6,10},... | collective-permute-start | bytes 393224 | tf_op jit(solution)/shard_map/ppermute | solution.py:107
  143.3 6.1 %collective-permute-start.30 = (bf16[2,128,128]{2,1,0:T(8,128)(2,1)S(1)}, bf16[2,128,128]{2,1,0:T(8,128)(2,1)S(1)}, u32[]{:S(2)}, u32[]{:S(2)}) collective-permute-start(bf16[2,128,128]{2,1,0:T(8,128)(2,1)S(1)} %get-tuple-element.49), channel_id=1, source_target_pairs={{0,12},{4,8},{8,4},{12,0},{1,13},{5,9},{9,5},{13,1},{2,14},{6,10},... | collective-permute-start | bytes 196616 | tf_op jit(solution)/shard_map/ppermute | solution.py:107
  151.9 5.8 %collective-permute-start.33 = (bf16[2,64,768]{2,1,0:T(8,128)(2,1)S(1)}, bf16[2,64,768]{2,1,0:T(8,128)(2,1)S(1)}, u32[]{:S(2)}, u32[]{:S(2)}) collective-permute-start(bf16[2,64,768]{2,1,0:T(8,128)(2,1)S(1)} %get-tuple-element.52), channel_id=1, source_target_pairs={{0,2},{2,0},{1,3},{3,1},{4,6},{6,4},{5,7},{7,5},{8,10},{10,8},{9,1... | collective-permute-start | bytes 589832 | tf_op jit(solution)/shard_map/ppermute | solution.py:107
  153.4 14.1 %collective-permute-start.34 = (bf16[2,64,768]{2,1,0:T(8,128)(2,1)S(1)}, bf16[2,64,768]{2,1,0:T(8,128)(2,1)S(1)}, u32[]{:S(2)}, u32[]{:S(2)}) collective-permute-start(bf16[2,64,768]{2,1,0:T(8,128)(2,1)S(1)} %get-tuple-element.53), channel_id=1, source_target_pairs={{0,8},{4,12},{8,0},{12,4},{1,9},{5,13},{9,1},{13,5},{2,10},{6,14},... | collective-permute-start | bytes 589832 | tf_op jit(solution)/shard_map/ppermute | solution.py:107
  153.4 16.2 %collective-permute-start.35 = (bf16[2,64,768]{2,1,0:T(8,128)(2,1)S(1)}, bf16[2,64,768]{2,1,0:T(8,128)(2,1)S(1)}, u32[]{:S(2)}, u32[]{:S(2)}) collective-permute-start(bf16[2,64,768]{2,1,0:T(8,128)(2,1)S(1)} %get-tuple-element.54), channel_id=1, source_target_pairs={{0,10},{2,8},{4,14},{6,12},{8,2},{10,0},{12,6},{14,4},{1,11},{3,9}... | collective-permute-start | bytes 589832 | tf_op jit(solution)/shard_map/ppermute | solution.py:411

commit v8 on v7

--- a/solution.py
+++ b/solution.py
@@ -107,8 +107,8 @@
     return lax.ppermute(value, axis, [(i, i ^ step) for i in range(peers)])
 
 
-def after(value, *others):
-    return lax.optimization_barrier((value, *others))[0]
+def settle(*values):
+    return lax.optimization_barrier(values)
 
 
 def call(kernel, out_shape, prefetch, operands, scratch=(), flops=0, read=0, limit=VMEM_BYTES):
@@ -157,9 +157,9 @@
 
 def project(place, tokens, chunks):
     rows, _, count, width = tokens.shape
-    _, half, cols = chunks[0][0].shape
-    slices = len(chunks)
-    flat = [w for of_round in chunks for w in of_round]
+    half, cols = chunks[0][0][0].shape[1], len(chunks) * HD
+    slices = len(chunks[0])
+    flat = [w for of_head in chunks for of_round in of_head for w in of_round]
     total_rows = rows * 2 * count
 
     def kernel(place_ref, x_ref, *refs):
@@ -171,8 +171,8 @@
             for g in range(2):
                 at = (row + slices - k) % slices * (2 * half) + (group + g) % 2 * half
                 piece = x_ref[:, :, :, pl.ds(pl.multiple_of(at, half), half)].reshape(-1, half)
-                w_ref = w_refs[2 * k + g]
-                weight = jnp.concatenate([w_ref[part] for part in range(3)], axis=1)
+                of_heads = w_refs[2 * k + g :: 2 * slices]
+                weight = jnp.concatenate([w_ref[part] for part in range(3) for w_ref in of_heads], axis=1)
                 term = jnp.dot(piece, weight, preferred_element_type=jnp.float32)
                 acc = term if acc is None else acc + term
         kv_part = acc[:, cols:].reshape(rows, 2 * count, 2 * cols)
@@ -202,12 +202,14 @@
     )
 
 
-def attend_all(place, members, counts, queries, keyvals, more):
+def attend_all(place, members, counts, queries, keyvals, more, earlier=()):
     blocks, block_len, cols = queries.shape
+    first = earlier[0].shape[2] if earlier else 0
     rows = keyvals.shape[1]
     per_row = rows // block_len
 
-    def kernel(place_ref, members_ref, counts_ref, q_ref, kv_ref, more_ref, same_ref, diff_ref, q_sum, kv_sum, out):
+    def kernel(place_ref, members_ref, counts_ref, q_ref, kv_ref, more_ref, *refs):
+        same_ref, diff_ref, q_sum, kv_sum, out = refs[len(earlier) :]
         for r in range(blocks):
             added = more_ref[r, rows:, :].astype(jnp.float32)
             added = jnp.concatenate([added[:, :cols], added[:, cols:]], axis=0)
@@ -236,15 +238,17 @@
                     weights.astype(jnp.bfloat16), values, preferred_element_type=jnp.float32
                 )
                 out[(b + place_ref[0]) % 2, b // 2, :, at] = blended.astype(jnp.bfloat16)
-        same_ref[...] = out[0]
-        diff_ref[...] = out[1]
-
-    half = jax.ShapeDtypeStruct((blocks // 2, block_len, cols), jnp.bfloat16)
+        for i, out_ref in enumerate((same_ref, diff_ref)):
+            if earlier:
+                out_ref[:, :, :first] = refs[i][...]
+            out_ref[:, :, first:] = out[i]
+
+    half = jax.ShapeDtypeStruct((blocks // 2, block_len, first + cols), jnp.bfloat16)
     return call(
         kernel,
         (half, half),
         [place, members, counts],
-        [queries, keyvals, more],
+        [queries, keyvals, more, *earlier],
         scratch=[
             pltpu.VMEM((blocks, block_len, cols), jnp.bfloat16),
             pltpu.VMEM((blocks * per_row, block_len, 2 * cols), jnp.bfloat16),
@@ -256,29 +260,25 @@
 
 
 def mix(place, attended, w_parts):
-    blocks, block_len, _ = attended[0][0].shape
-    widths = [a.shape[2] for a in attended[0]]
-    cols, parts = sum(widths), len(widths)
+    blocks, block_len, cols = attended[0].shape
     width = w_parts[0].shape[1]
 
     def kernel(place_ref, *refs):
         row, _, frame, core = (place_ref[i] for i in range(4))
-        w_refs = refs[4 * parts : 4 * parts + 4]
-        keep, over_x, over_z, over_both, a_all, sums = refs[4 * parts + 4 :]
+        w_refs = refs[4:12]
+        keep, over_x, over_z, over_both, a_all, sums = refs[12:]
         for s in range(4):
-            for i, of_group in enumerate(widths):
-                at = slice(sum(widths[:i]), sum(widths[: i + 1]))
-                a_all[s, :, at] = refs[s * parts + i][...].reshape(blocks * block_len, of_group)
-
-        def term(w_ref, side):
-            first = a_all[(2 * side) ^ row]
-            second = a_all[(2 * side + 1) ^ row]
-            acc = jnp.dot(first, w_ref[:cols], preferred_element_type=jnp.float32)
-            acc = acc + jnp.dot(second, w_ref[cols:], preferred_element_type=jnp.float32)
+            a_all[s] = refs[s][...].reshape(blocks * block_len, cols)
+
+        def term(first, side):
+            acc = jnp.dot(a_all[(2 * side) ^ row], w_refs[first][...], preferred_element_type=jnp.float32)
+            acc = acc + jnp.dot(
+                a_all[(2 * side + 1) ^ row], w_refs[first + 1][...], preferred_element_type=jnp.float32
+            )
             return acc.astype(jnp.bfloat16).astype(jnp.float32)
 
         for c in range(2):
-            total = term(w_refs[c], core) + term(w_refs[2 + c], 1 - core)
+            total = term(2 * c, core) + term(4 + 2 * c, 1 - core)
             sums[...] = total.reshape(blocks, 2, BS, width)
             at = (row + c) % 2
             keep[at] = sums[row // 2, frame]
@@ -292,7 +292,7 @@
         kernel,
         (jax.ShapeDtypeStruct(shape, jnp.float32), sent, sent, sent),
         [place],
-        [*(a for of_row in attended for a in of_row), *w_parts],
+        [*attended, *w_parts],
         scratch=[
             pltpu.VMEM((4, blocks * block_len, cols), jnp.bfloat16),
             pltpu.VMEM((blocks, 2, BS, width), jnp.float32),
@@ -334,52 +334,68 @@
     half = depth // 2
     place = jnp.stack([row, group, frame, core]).astype(jnp.int32)
 
-    mine = lax.dynamic_slice_in_dim(latents[0], core * span * depth, span * depth, axis=1)
-
     def over_frames(value, rows):
         pairs = [(2 * r + f, 2 * r + 1 - f) for r in rows for f in range(2)]
         return lax.ppermute(value, ("rows", "frames"), pairs)
 
+    def inward(value):
+        return lax.ppermute(value, "rows", [(1, 2), (2, 1)])
+
+    def outward(value):
+        return lax.ppermute(value, "rows", [(1, 0), (2, 3)])
+
+    def piece(weights, i):
+        at = (0, group * half, (i % span + row) % span * cols + i // span * HD)
+        return lax.dynamic_slice(weights.transpose(1, 0, 2), at, (3, half, HD))
+
+    def reshard(value, i):
+        pairs = [
+            (r * heads_n + h, (h * span + (i % span + r) % span) * heads_n + r // span)
+            for r in range(rows_n)
+            for h in range(heads_n)
+        ]
+        return lax.ppermute(value, ("rows", "heads"), pairs)
+
+    here, there = {}, {}
+    mine = lax.dynamic_slice_in_dim(latents[0], core * span * depth, span * depth, axis=1)
+    here[0] = reshard(piece(w_qkv, 0), 0)
     mine_x = swap(mine, "frames")
-    beside_1 = swap(mine, "rows")
-    in_1 = lax.ppermute(mine, "rows", [(1, 2), (2, 1)])
-    beside_1x = swap(beside_1, "frames")
-    in_2 = lax.ppermute(after(beside_1, in_1), "rows", [(1, 2), (2, 1)])
-    out_1 = lax.ppermute(in_1, "rows", [(1, 0), (2, 3)])
+    near = swap(mine, "rows")
+    in_1 = inward(mine)
+    ready = piece(w_qkv, 1)
+    here, mine_x, near, in_1, ready, w_qkv, w_out = settle(here, mine_x, near, in_1, ready, w_qkv, w_out)
+
+    here[1] = reshard(ready, 1)
+    there[0] = swap(here[0], "groups")
+    near_x = swap(near, "frames")
     in_1x = over_frames(in_1, (1, 2))
-    out_2 = lax.ppermute(in_2, "rows", [(1, 0), (2, 3)])
+    in_2 = inward(near)
+    out_1 = outward(in_1)
+    ready = [piece(w_qkv, 2), piece(w_qkv, 3)]
+    here, there, near_x, in_1x, in_2, out_1, ready, w_qkv, w_out = settle(
+        here, there, near_x, in_1x, in_2, out_1, ready, w_qkv, w_out
+    )
+
+    here[2], here[3] = reshard(ready[0], 2), reshard(ready[1], 3)
+    there[1] = swap(here[1], "groups")
     in_2x = over_frames(in_2, (1, 2))
+    out_2 = outward(in_2)
     out_1x = over_frames(out_1, (0, 3))
+    across = swap(w_out, "heads")
+    ready = [piece(w_qkv, 4), piece(w_qkv, 5)]
+    here, there, in_2x, out_2, out_1x, across, ready, w_qkv, w_out = settle(
+        here, there, in_2x, out_2, out_1x, across, ready, w_qkv, w_out
+    )
+
+    here[4], here[5] = reshard(ready[0], 4), reshard(ready[1], 5)
+    there[2], there[3] = swap(here[2], "groups"), swap(here[3], "groups")
     out_2x = over_frames(out_2, (0, 3))
-    tokens = assemble(
-        place,
-        [(mine, mine_x), (beside_1, beside_1x)],
-        [(in_1, in_1x), (in_2, in_2x)],
-        [(out_1, out_1x), (out_2, out_2x)],
-    )
-
-    by_part = w_qkv.transpose(1, 0, 2)
-    last = cols // (3 * HD) * HD
-    waits = [[beside_1, in_1, mine_x], [in_2, beside_1x], [out_1, in_1x], [out_2, in_2x, out_1x]]
-    here, there = [], []
-    for first, wide in ((0, cols - last), (cols - last, last)):
-        for k in range(span):
-            pairs = [
-                (r * heads_n + h, (h * span + (k + r) % span) * heads_n + r // span)
-                for r in range(rows_n)
-                for h in range(heads_n)
-            ]
-            piece = lax.dynamic_slice(
-                by_part, (0, group * half, (k + row) % span * cols + first), (3, half, wide)
-            )
-            piece = after(piece, *waits[len(here)], *here[-2:-1], *there[-3:-2])
-            here.append(lax.ppermute(piece, ("rows", "heads"), pairs))
-            there.append(swap(here[-1], "groups"))
-    across = swap(after(w_out, here[0]), "heads")
-    beside = swap(after(w_out, here[1]), "rows")
-
+    upper, lower = w_out[:cols], w_out[cols:]
     tables = jnp.concatenate([win_blocks, win_counts[:, None], block_window[:, None]], axis=1)
-    tables = after(tables, here[0])
+    here, there, out_2x, upper, lower, w_out, tables = settle(here, there, out_2x, upper, lower, w_out, tables)
+
+    there[4], there[5] = swap(here[4], "groups"), swap(here[5], "groups")
+    beside_upper = swap(upper, "rows")
     found = [tables] + [swap(tables, "rows", s) for s in range(1, rows_n)]
     tables = jnp.stack(found)[row ^ jnp.arange(rows_n)].reshape(rows_n * heads_n, MAXB + 2)
     windows = lax.dynamic_index_in_dim(
@@ -387,24 +403,31 @@
     )
     picked = tables[windows]
     members, counts = picked[:, :MAXB].reshape(-1), picked[:, MAXB]
-
-    attended = [[] for _ in range(rows_n)]
-    send = None
-    for part in range(2):
-        chunks = [[here[i], there[i]] for i in range(part * span, (part + 1) * span)]
-        if part:
-            chunks[-1][-1] = after(chunks[-1][-1], send)
-        else:
-            chunks[-1][-1] = after(chunks[-1][-1], there[2], members, counts)
-        queries, keyvals, send = project(place, tokens, chunks)
-        if part:
-            keyvals = after(keyvals, attended[0][0], beside)
-        same, diff = attend_all(place, members, counts, queries, keyvals, swap(send, "heads"))
-        for s in range(rows_n):
-            attended[s].append(swap(same if s % 2 == 0 else diff, "rows", s) if s else same)
-
+    tokens = assemble(
+        place, [(mine, mine_x), (near, near_x)], [(in_1, in_1x), (in_2, in_2x)], [(out_1, out_1x), (out_2, out_2x)]
+    )
+    heads = len(here) // span
+    chunks = [[(here[h * span + k], there[h * span + k]) for k in range(span)] for h in range(heads)]
+    first = project(place, tokens, chunks[:-1])
+    beside_upper, tokens, first, chunks, members, counts, lower = settle(
+        beside_upper, tokens, first, chunks, members, counts, lower
+    )
+
+    beside_lower = swap(lower, "rows")
+    first_more = swap(first[2], "heads")
+    second = project(place, tokens, chunks[-1:])
+    second_more = swap(second[2], "heads")
+    attended = attend_all(place, members, counts, *first[:2], first_more)
+    attended, second, second_more, beside_upper, beside_lower = settle(
+        attended, second, second_more, beside_upper, beside_lower
+    )
+
+    same, diff = attend_all(place, members, counts, *second[:2], second_more, attended)
+    attended = [same] + [swap(same if s % 2 == 0 else diff, "rows", s) for s in range(1, rows_n)]
+    beside = [beside_upper, beside_lower]
+    beside_across = [swap(part, "heads") for part in beside]
     keep, over_x, over_z, over_both = mix(
-        place, attended, [w_out, beside, across, swap(beside, "heads")]
+        place, attended, [upper, lower, *beside, across[:cols], across[cols:], *beside_across]
     )
     from_x = swap(over_x, "frames")
     from_z = swap(over_z, "rows", 2)
@@ -421,7 +444,7 @@
     rows_n = lax.axis_size("rows")
     pairs = all(lax.axis_size(axis) == 2 for axis in ("groups", "frames", "heads"))
     heads_here = w_qkv.shape[2] // HD
-    if pairs and rows_n == 4 and heads_here % 2 == 0 and latents.shape[:2] == (1, 2 * BS):
+    if pairs and rows_n == 4 and heads_here == 6 and latents.shape[:2] == (1, 2 * BS):
         plan = by_heads
     else:
         plan = by_tokens

time: 172 us -> 187 us (1.087)
  local copies, waits for them, and re-layouts: 9.71 us -> 17.1 us
  starting transfers between devices: 56.5 us -> 60.9 us
  waiting for transfers between devices: 79.5 us -> 82.7 us
    ppermute x4, waiting for transfers between devices: 6.48 us -> 0.01 us  [over_frames(): return lax.ppermute(value, ('rows', 'frames'), pairs)]
    ppermute x23 -> x24, starting transfers between devices: 26.8 us -> 33.2 us  [swap(): return lax.ppermute(value, axis, [(i, i ^ step) for i in range(peers)])]
    ppermute x8 -> x10, waiting for transfers between devices: 11.4 us -> 17.8 us  [the longest x2 12.7 us: outward(): return lax.ppermute(value, 'rows', [(1, 0), (2, 3)])]
    unnamed x22 -> x50, local copies, waits for them, and re-layouts: 3.06 us -> 8.4 us
    slice x0 -> x2, local copies, waits for them, and re-layouts: none -> 2.64 us  [the longest x1 1.32 us: by_heads(): upper, lower = (w_out[:cols], w_out[cols:])]
    ppermute x23 -> x24, waiting for transfers between devices: 59.6 us -> 61 us  [swap(): return lax.ppermute(value, axis, [(i, i ^ step) for i in range(peers)])]
    ppermute x8 -> x10, starting transfers between devices: 17 us -> 16.9 us  [the longest x6 12.2 us: reshard(): return lax.ppermute(value, ('rows', 'heads'), pairs)]
    dynamic_slice x2 -> x3, local copies, waits for them, and re-layouts: 4.13 us -> 4.17 us  [piece(): return lax.dynamic_slice(weights.transpose(1, 0, 2), at, (3, half, HD))]
  transfers between devices with their start and end apart: 36 -> 39, of which waited for: 12 -> 14; matrix products, arithmetic and copies ran while one was open for 4% -> 5% of each run, Pallas kernels for 12% -> 11%
where the time goes in v8:
time: 187 us; the launch traced here: 186 us
  waiting for transfers between devices  82.7 us (44%)
  starting transfers between devices  60.9 us (33%)
  Pallas kernels  23.8 us (13%)
  local copies, waits for them, and re-layouts  17.1 us (9%)
    ppermute x24, waiting for transfers between devices, swap(): return lax.ppermute(value, axis, [(i, i ^ step) for i in range(peers)])  61 us
    ppermute x24, starting transfers between devices, swap(): return lax.ppermute(value, axis, [(i, i ^ step) for i in range(peers)])  33.2 us
    pallas_call x7, Pallas kernels, call(): pl.pallas_call(kernel, out_shape=out_shape, grid_spec=pltpu.PrefetchScala...  23.8 us
    ppermute x2, waiting for transfers between devices, outward(): return lax.ppermute(value, 'rows', [(1, 0), (2, 3)])  12.7 us
    ppermute x6, starting transfers between devices, reshard(): return lax.ppermute(value, ('rows', 'heads'), pairs)  12.2 us
    unnamed x50, local copies, waits for them, and re-layouts  8.4 us
    ppermute x4, starting transfers between devices, over_frames(): return lax.ppermute(value, ('rows', 'frames'), pairs)  8.34 us
    ppermute x6, waiting for transfers between devices, reshard(): return lax.ppermute(value, ('rows', 'heads'), pairs)  5.08 us
  transfers between devices with their start and end apart: 39, of which 14 were waited for; matrix products, arithmetic and copies ran while one was open for 5% of the time, Pallas kernels for 11%

profile of v8, /device:TPU:0, one launch (start us, length us, event | category | flops | bytes accessed | tf_op | source)
XLA Modules:
  0.0 185.9 jit_solution(14901381106108806178)
XLA Ops:
  1.9 5.9 %collective-permute-start.2 = (bf16[128,1536]{1,0:T(8,128)(2,1)S(1)}, bf16[128,1536]{1,0:T(8,128)(2,1)S(1)}, u32[]{:S(2)}, u32[]{:S(2)}) collective-permute-start(bf16[128,1536]{1,0:T(8,128)(2,1)S(1)} %dynamic-slice_bitcast_fusion.refs_0_), channel_id=1, source_target_pairs={{0,4},{4,0},{8,12},{12,8},{1,5},{5,1},{9,13},{13,9},{2,6},{6,2},{1... | collective-permute-start | bytes 1179656 | tf_op jit(solution)/shard_map/ppermute | solution.py:107
  7.8 1.5 collective-permute-start.1
  11.1 6.8 %collective-permute-done.2.refs_2_ = bf16[128,1536]{1,0:T(8,128)(2,1)S(1)} collective-permute-done((bf16[128,1536]{1,0:T(8,128)(2,1)S(1)}, bf16[128,1536]{1,0:T(8,128)(2,1)S(1)}, u32[]{:S(2)}, u32[]{:S(2)}) %collective-permute-start.2) | collective-permute-done | bytes 393248 | tf_op jit(solution)/shard_map/ppermute | solution.py:107
  18.1 1.8 collective-permute-start.4
  19.9 1.5 collective-permute-start.8
  21.3 1.5 collective-permute-start.6
  24.1 1.4 collective-permute-start.7
  25.6 1.5 collective-permute-start.5
  28.2 4.1 %collective-permute-done.5.refs_1_ = bf16[3,384,128]{2,1,0:T(8,128)(2,1)S(1)} collective-permute-done((bf16[3,384,128]{2,1,0:T(8,128)(2,1)S(1)}, bf16[3,384,128]{2,1,0:T(8,128)(2,1)S(1)}, u32[]{:S(2)}, u32[]{:S(2)}) %collective-permute-start.5) | collective-permute-done | bytes 294944 | tf_op jit(solution)/shard_map/ppermute | solution.py:107
  32.3 5.6 %collective-permute-done.9.refs_8_ = bf16[128,1536]{1,0:T(8,128)(2,1)} collective-permute-done((bf16[128,1536]{1,0:T(8,128)(2,1)S(1)}, bf16[128,1536]{1,0:T(8,128)(2,1)}, u32[]{:S(2)}, u32[]{:S(2)}) %collective-permute-start.9) | collective-permute-done | bytes 393248 | tf_op jit(solution)/shard_map/ppermute | solution.py:345
  37.9 1.6 collective-permute-start.16
  40.1 5.3 %collective-permute-start.11 = (bf16[3,384,128]{2,1,0:T(8,128)(2,1)S(1)}, bf16[3,384,128]{2,1,0:T(8,128)(2,1)S(1)}, u32[]{:S(2)}, u32[]{:S(2)}) collective-permute-start(bf16[3,384,128]{2,1,0:T(8,128)(2,1)S(1)} %get-tuple-element.92), channel_id=1, source_target_pairs={{0,4},{1,12},{4,0},{5,8},{8,5},{9,13},{12,1},{13,9},{2,6},{3,14},{... | collective-permute-start | bytes 884744 | tf_op jit(solution)/shard_map/ppermute | solution.py:357
  45.4 3.6 %collective-permute-start.15 = (bf16[128,1536]{1,0:T(8,128)(2,1)}, bf16[128,1536]{1,0:T(8,128)(2,1)}, u32[]{:S(2)}, u32[]{:S(2)}) collective-permute-start(bf16[128,1536]{1,0:T(8,128)(2,1)} %collective-permute-done.9.refs_8_), channel_id=1, source_target_pairs={{0,2},{2,0},{12,14},{14,12},{1,3},{3,1},{13,15},{15,13},{16,18},{1... | collective-permute-start | bytes 1179656 | tf_op jit(solution)/shard_map/ppermute | solution.py:339
  50.3 1.4 collective-permute-start.13
  51.7 1.5 collective-permute-start.12
  53.6 1.9 %dynamic-slice_bitcast_fusion.1 = (bf16[3,384,128]{2,1,0:T(8,128)(2,1)}, bf16[3,384,128]{2,1,0:T(8,128)(2,1)}) fusion(bf16[768,3,768]{2,0,1:T(8,128)(2,1)} %param.7, s32[]{:T(128)S(6)} %select_n.66, s32[]{:T(128)S(6)} %select_n.75, s32[]{:T(128)S(6)} %select_n.74), kind=kLoop, calls=%fused_computation.3 | loop fusion | bytes 1179660 | tf_op jit(solution)/shard_map/dynamic_slice | solution.py:349
  55.5 2.9 %collective-permute-done.12.refs_3_ = bf16[3,384,128]{2,1,0:T(8,128)(2,1)S(1)} collective-permute-done((bf16[3,384,128]{2,1,0:T(8,128)(2,1)S(1)}, bf16[3,384,128]{2,1,0:T(8,128)(2,1)S(1)}, u32[]{:S(2)}, u32[]{:S(2)}) %collective-permute-start.12) | collective-permute-done | bytes 294944 | tf_op jit(solution)/shard_map/ppermute | solution.py:107
  58.5 7.1 %collective-permute-done.14.refs_10_ = bf16[128,1536]{1,0:T(8,128)(2,1)} collective-permute-done((bf16[128,1536]{1,0:T(8,128)(2,1)}, bf16[128,1536]{1,0:T(8,128)(2,1)}, u32[]{:S(2)}, u32[]{:S(2)}) %collective-permute-start.14) | collective-permute-done | bytes 393248 | tf_op jit(solution)/shard_map/ppermute | solution.py:345
  65.6 1.9 %collective-permute-start.21 = (bf16[128,1536]{1,0:T(8,128)(2,1)}, bf16[128,1536]{1,0:T(8,128)(2,1)}, u32[]{:S(2)}, u32[]{:S(2)}) collective-permute-start(bf16[128,1536]{1,0:T(8,128)(2,1)} %collective-permute-done.14.refs_10_), channel_id=1, source_target_pairs={{0,2},{2,0},{12,14},{14,12},{1,3},{3,1},{13,15},{15,13},{16,18},{1... | collective-permute-start | bytes 1179656 | tf_op jit(solution)/shard_map/ppermute | solution.py:339
  67.6 3.8 %collective-permute-start.17 = (bf16[3,384,128]{2,1,0:T(8,128)(2,1)}, bf16[3,384,128]{2,1,0:T(8,128)(2,1)}, u32[]{:S(2)}, u32[]{:S(2)}) collective-permute-start(bf16[3,384,128]{2,1,0:T(8,128)(2,1)} %get-tuple-element.102), channel_id=1, source_target_pairs={{0,0},{1,8},{4,4},{5,12},{8,1},{9,9},{12,5},{13,13},{2,2},{3,10},{... | collective-permute-start | bytes 884744 | tf_op jit(solution)/shard_map/ppermute | solution.py:357
  71.4 1.5 collective-permute-start.19
  74.0 1.3 fusion.3
  75.4 5.1 %collective-permute-done.18.refs_2_ = bf16[3,384,128]{2,1,0:T(8,128)(2,1)} collective-permute-done((bf16[3,384,128]{2,1,0:T(8,128)(2,1)}, bf16[3,384,128]{2,1,0:T(8,128)(2,1)}, u32[]{:S(2)}, u32[]{:S(2)}) %collective-permute-start.18) | collective-permute-done | bytes 294944 | tf_op jit(solution)/shard_map/ppermute | solution.py:357
  80.4 5.4 %collective-permute-done.20.refs_7_ = bf16[3,384,128]{2,1,0:T(8,128)(2,1)} collective-permute-done((bf16[3,384,128]{2,1,0:T(8,128)(2,1)S(1)}, bf16[3,384,128]{2,1,0:T(8,128)(2,1)}, u32[]{:S(2)}, u32[]{:S(2)}) %collective-permute-start.20) | collective-permute-done | bytes 294944 | tf_op jit(solution)/shard_map/ppermute | solution.py:107
  85.9 2.6 %collective-permute-start.27 = (s32[2,6]{1,0:T(2,128)S(1)}, s32[2,6]{1,0:T(2,128)S(1)}, u32[]{:S(2)}, u32[]{:S(2)}) collective-permute-start(s32[2,6]{1,0:T(2,128)S(1)} %pad_add_fusion.1), channel_id=1, source_target_pairs={{0,12},{4,8},{8,4},{12,0},{1,13},{5,9},{9,5},{13,1},{2,14},{6,10},... | collective-permute-start | bytes 152 | tf_op jit(solution)/shard_map/ppermute | solution.py:107
  88.4 2.8 %collective-permute-start.26 = (s32[2,6]{1,0:T(2,128)S(1)}, s32[2,6]{1,0:T(2,128)S(1)}, u32[]{:S(2)}, u32[]{:S(2)}) collective-permute-start(s32[2,6]{1,0:T(2,128)S(1)} %pad_add_fusion.1), channel_id=1, source_target_pairs={{0,8},{4,12},{8,0},{12,4},{1,9},{5,13},{9,1},{13,5},{2,10},{6,14},... | collective-permute-start | bytes 152 | tf_op jit(solution)/shard_map/ppermute | solution.py:107
  91.2 1.6 collective-permute-start.23
  92.8 2.0 %collective-permute-start.22 = (bf16[384,768]{1,0:T(8,128)(2,1)S(1)}, bf16[384,768]{1,0:T(8,128)(2,1)S(1)}, u32[]{:S(2)}, u32[]{:S(2)}) collective-permute-start(bf16[384,768]{1,0:T(8,128)(2,1)S(1)} %get-tuple-element.108.refs_4_), channel_id=1, source_target_pairs={{0,4},{4,0},{8,12},{12,8},{1,5},{5,1},{9,13},{13,9},{2,6},{6,2},{1... | collective-permute-start | bytes 1769480 | tf_op jit(solution)/shard_map/ppermute | solution.py:107
  94.8 5.0 %shard_map.64.x_ref = bf16[4,2,128,1536]{3,2,1,0:T(8,128)(2,1)} custom-call(s32[4]{0:T(128)} %pad_add_fusion.2.place_ref, bf16[128,1536]{1,0:T(8,128)(2,1)} %copy-done.17, bf16[128,1536]{1,0:T(8,128)(2,1)} %copy-done.20, bf16[128,1536]{1,0:T(8,128)(2,1)} %copy-done.19, bf16[128,1536]{1,0:T(8,128)(2,1)} %copy-done.21, bf16[128,1536]{1,0:T(8,128)(2,1)} %copy-done.18, ...), custom_call_target="tpu_custom_call" | custom-call | bytes 7864320 | tf_op jit(solution)/shard_map/pallas_call | solution.py:115
  99.8 1.9 %copy-done.1 = bf16[4,2,128,1536]{3,2,1,0:T(8,128)(2,1)S(1)} copy-done((bf16[4,2,128,1536]{3,2,1,0:T(8,128)(2,1)S(1)}, bf16[4,2,128,1536]{3,2,1,0:T(8,128)(2,1)}, u32[]{:S(2)}) %copy-start.1) | copy-done | bytes 3145752
  102.7 5.1 %shard_map.65 = (f32[4,128,256]{2,1,0:T(8,128)S(1)}, f32[4,256,512]{2,1,0:T(8,128)S(1)}, bf16[4,320,512]{2,1,0:T(8,128)(2,1)S(1)}) custom-call(s32[4]{0:T(128)S(1)} %copy-done.5, bf16[4,2,128,1536]{3,2,1,0:T(8,128)(2,1)S(1)} %copy-done.1, bf16[3,384,128]{2,1,0:T(8,128)(2,1)S(1)} %collective-permute-done.refs_0_, bf16[3,384,128]{2,1,0:T(8,128)(2,1)S(1)} %copy-done.10, ...), custom_call_target="tpu_custom_call" | custom-call | flops 2415919104 | bytes 8053063 | tf_op jit(solution)/shard_map/pallas_call | solution.py:115
  107.8 1.4 copy-done.3
  112.6 5.4 %collective-permute-done.24.refs_3_ = bf16[3,384,128]{2,1,0:T(8,128)(2,1)S(1)} collective-permute-done((bf16[3,384,128]{2,1,0:T(8,128)(2,1)}, bf16[3,384,128]{2,1,0:T(8,128)(2,1)S(1)}, u32[]{:S(2)}, u32[]{:S(2)}) %collective-permute-start.24) | collective-permute-done | bytes 294944 | tf_op jit(solution)/shard_map/ppermute | solution.py:107
  118.0 1.9 %copy-done.2 = bf16[4,2,128,1536]{3,2,1,0:T(8,128)(2,1)S(1)} copy-done((bf16[4,2,128,1536]{3,2,1,0:T(8,128)(2,1)S(1)}, bf16[4,2,128,1536]{3,2,1,0:T(8,128)(2,1)}, u32[]{:S(2)}) %copy-start.2) | copy-done | bytes 3145752
  119.9 3.9 %shard_map.67 = (f32[4,128,128]{2,1,0:T(8,128)S(1)}, f32[4,256,256]{2,1,0:T(8,128)S(1)}, bf16[4,320,256]{2,1,0:T(8,128)(2,1)S(1)}) custom-call(s32[4]{0:T(128)S(1)} %copy-done.5, bf16[4,2,128,1536]{3,2,1,0:T(8,128)(2,1)S(1)} %copy-done.2, bf16[3,384,128]{2,1,0:T(8,128)(2,1)} %collective-permute-done.17.refs_0_, ...), custom_call_target="tpu_custom_call" | custom-call | flops 1207959552 | bytes 4026531 | tf_op jit(solution)/shard_map/pallas_call | solution.py:115
  125.1 3.8 %shard_map.66 = (bf16[2,128,256]{2,1,0:T(8,128)(2,1)S(1)}, bf16[2,128,256]{2,1,0:T(8,128)(2,1)S(1)}) custom-call(s32[4]{0:T(128)S(1)} %copy-done.5, s32[16]{0:T(128)S(1)} %reshape.24.members_ref, s32[4]{0:T(128)S(1)} %slice_reduce_fusion.1.counts_ref, f32[4,128,256]{2,1,0:T(8,128)S(1)} %get-tuple-element.132.q_ref, f32[4,256,512]{2,1,0:T(8,128)S(1)} %copy-done.4, ...), custom_call_target="tpu_custom_call" | custom-call | flops 268435456 | bytes 2097152 | tf_op jit(solution)/shard_map/pallas_call | solution.py:115
  128.9 10.8 %collective-permute-done.30.refs_7_ = bf16[384,768]{1,0:T(8,128)(2,1)S(1)} collective-permute-done((bf16[384,768]{1,0:T(8,128)(2,1)S(1)}, bf16[384,768]{1,0:T(8,128)(2,1)S(1)}, u32[]{:S(2)}, u32[]{:S(2)}) %collective-permute-start.30) | collective-permute-done | bytes 589856 | tf_op jit(solution)/shard_map/ppermute | solution.py:107
  140.2 2.2 %shard_map.68 = (bf16[2,128,384]{2,1,0:T(8,128)(2,1)S(1)}, bf16[2,128,384]{2,1,0:T(8,128)(2,1)S(1)}) custom-call(s32[4]{0:T(128)S(1)} %copy-done.5, s32[16]{0:T(128)S(1)} %reshape.24.members_ref, s32[4]{0:T(128)S(1)} %slice_reduce_fusion.1.counts_ref, f32[4,128,128]{2,1,0:T(8,128)S(1)} %get-tuple-element.147.q_ref, ...), custom_call_target="tpu_custom_call" | custom-call | flops 134217728 | bytes 1048576 | tf_op jit(solution)/shard_map/pallas_call | solution.py:115
  142.4 1.3 collective-permute-start.33
  143.8 3.1 %collective-permute-start.32 = (bf16[2,128,384]{2,1,0:T(8,128)(2,1)S(1)}, bf16[2,128,384]{2,1,0:T(8,128)(2,1)S(1)}, u32[]{:S(2)}, u32[]{:S(2)}) collective-permute-start(bf16[2,128,384]{2,1,0:T(8,128)(2,1)S(1)} %get-tuple-element.152.refs_0_), channel_id=1, source_target_pairs={{0,8},{4,12},{8,0},{12,4},{1,9},{5,13},{9,1},{13,5},{2,10},{6,14},... | collective-permute-start | bytes 589832 | tf_op jit(solution)/shard_map/ppermute | solution.py:107
  148.2 13.9 %collective-permute-done.32.refs_2_ = bf16[2,128,384]{2,1,0:T(8,128)(2,1)S(1)} collective-permute-done((bf16[2,128,384]{2,1,0:T(8,128)(2,1)S(1)}, bf16[2,128,384]{2,1,0:T(8,128)(2,1)S(1)}, u32[]{:S(2)}, u32[]{:S(2)}) %collective-permute-start.32) | collective-permute-done | bytes 196640 | tf_op jit(solution)/shard_map/ppermute | solution.py:107
  162.1 2.5 %shard_map.69 = (f32[2,64,768]{2,1,0:T(8,128)S(1)}, bf16[2,64,768]{2,1,0:T(8,128)(2,1)S(1)}, bf16[2,64,768]{2,1,0:T(8,128)(2,1)S(1)}, bf16[2,64,768]{2,1,0:T(8,128)(2,1)S(1)}) custom-call(s32[4]{0:T(128)S(1)} %copy-done.5, bf16[2,128,384]{2,1,0:T(8,128)(2,1)S(1)} %get-tuple-element.152.refs_0_, bf16[2,128,384]{2,1,0:T(8,128)(2,1)S(1)} %collective-permute-done.31.refs_1_, ...), custom_call_target="tpu_custom_call" | custom-call | flops 1207959552 | bytes 4718592 | tf_op jit(solution)/shard_map/pallas_call | solution.py:115
  164.6 2.1 %collective-permute-start.36 = (bf16[2,64,768]{2,1,0:T(8,128)(2,1)S(1)}, bf16[2,64,768]{2,1,0:T(8,128)(2,1)S(1)}, u32[]{:S(2)}, u32[]{:S(2)}) collective-permute-start(bf16[2,64,768]{2,1,0:T(8,128)(2,1)S(1)} %get-tuple-element.158), channel_id=1, source_target_pairs={{0,2},{2,0},{1,3},{3,1},{4,6},{6,4},{5,7},{7,5},{8,10},{10,8},{9,1... | collective-permute-start | bytes 589832 | tf_op jit(solution)/shard_map/ppermute | solution.py:107
  166.7 2.4 %collective-permute-start.38 = (bf16[2,64,768]{2,1,0:T(8,128)(2,1)S(1)}, bf16[2,64,768]{2,1,0:T(8,128)(2,1)S(1)}, u32[]{:S(2)}, u32[]{:S(2)}) collective-permute-start(bf16[2,64,768]{2,1,0:T(8,128)(2,1)S(1)} %get-tuple-element.160), channel_id=1, source_target_pairs={{0,10},{2,8},{4,14},{6,12},{8,2},{10,0},{12,6},{14,4},{1,11},{3,9}... | collective-permute-start | bytes 589832 | tf_op jit(solution)/shard_map/ppermute | solution.py:434
  169.1 1.8 collective-permute-done.36.x_ref
  170.9 9.7 %collective-permute-done.37.z_ref = bf16[2,64,768]{2,1,0:T(8,128)(2,1)S(1)} collective-permute-done((bf16[2,64,768]{2,1,0:T(8,128)(2,1)S(1)}, bf16[2,64,768]{2,1,0:T(8,128)(2,1)S(1)}, u32[]{:S(2)}, u32[]{:S(2)}) %collective-permute-start.37) | collective-permute-done | bytes 196640 | tf_op jit(solution)/shard_map/ppermute | solution.py:107
  180.6 3.9 %collective-permute-done.38.both_ref = bf16[2,64,768]{2,1,0:T(8,128)(2,1)S(1)} collective-permute-done((bf16[2,64,768]{2,1,0:T(8,128)(2,1)S(1)}, bf16[2,64,768]{2,1,0:T(8,128)(2,1)S(1)}, u32[]{:S(2)}, u32[]{:S(2)}) %collective-permute-start.38) | collective-permute-done | bytes 196640 | tf_op jit(solution)/shard_map/ppermute | solution.py:434
  184.5 1.4 shard_map.70
  (108 shorter events, 17.3 us)
Async XLA Ops:
  0.0 53.3 %copy-start.23 = (s32[2]{0:T(128)S(1)}, s32[2]{0:T(128)}, u32[]{:S(2)}) copy-start(s32[2]{0:T(128)} %param.10) | copy-start | bytes 28
  0.0 53.3 %copy-start.24 = (s32[2]{0:T(128)S(1)}, s32[2]{0:T(128)}, u32[]{:S(2)}) copy-start(s32[2]{0:T(128)} %param.11) | copy-start | bytes 28
  1.1 66.4 %copy-start.22 = (s32[2,4]{1,0:T(2,128)S(1)}, s32[2,4]{1,0:T(2,128)}, u32[]{:S(2)}) copy-start(s32[2,4]{1,0:T(2,128)} %param.9) | copy-start | bytes 100
  1.2 9.9 %collective-permute-start.3 = (bf16[128,1536]{1,0:T(8,128)(2,1)S(1)}, bf16[128,1536]{1,0:T(8,128)(2,1)S(1)}, u32[]{:S(2)}, u32[]{:S(2)}) collective-permute-start(bf16[128,1536]{1,0:T(8,128)(2,1)S(1)} %dynamic-slice_bitcast_fusion.refs_0_), channel_id=1, source_target_pairs={{4,8},{8,4},{5,9},{9,5},{6,10},{10,6},{7,11},{11,7},{20,24},{24,20... | collective-permute-start | bytes 1179656 | tf_op jit(solution)/shard_map/ppermute | solution.py:342
  1.9 16.0 %collective-permute-start.2 = (bf16[128,1536]{1,0:T(8,128)(2,1)S(1)}, bf16[128,1536]{1,0:T(8,128)(2,1)S(1)}, u32[]{:S(2)}, u32[]{:S(2)}) collective-permute-start(bf16[128,1536]{1,0:T(8,128)(2,1)S(1)} %dynamic-slice_bitcast_fusion.refs_0_), channel_id=1, source_target_pairs={{0,4},{4,0},{8,12},{12,8},{1,5},{5,1},{9,13},{13,9},{2,6},{6,2},{1... | collective-permute-start | bytes 1179656 | tf_op jit(solution)/shard_map/ppermute | solution.py:107
  7.8 10.3 %collective-permute-start.1 = (bf16[128,1536]{1,0:T(8,128)(2,1)S(1)}, bf16[128,1536]{1,0:T(8,128)(2,1)S(1)}, u32[]{:S(2)}, u32[]{:S(2)}) collective-permute-start(bf16[128,1536]{1,0:T(8,128)(2,1)S(1)} %dynamic-slice_bitcast_fusion.refs_0_), channel_id=1, source_target_pairs={{0,2},{2,0},{1,3},{3,1},{4,6},{6,4},{5,7},{7,5},{8,10},{10,8},{9,1... | collective-permute-start | bytes 1179656 | tf_op jit(solution)/shard_map/ppermute | solution.py:107
  10.4 0.7 collective-permute-start
  11.1 64.3 %copy-start.18 = (bf16[128,1536]{1,0:T(8,128)(2,1)}, bf16[128,1536]{1,0:T(8,128)(2,1)S(1)}, u32[]{:S(2)}) copy-start(bf16[128,1536]{1,0:T(8,128)(2,1)S(1)} %collective-permute-done.3.refs_4_) | copy-start | bytes 1179652
  17.9 56.1 %copy-start.19 = (bf16[128,1536]{1,0:T(8,128)(2,1)}, bf16[128,1536]{1,0:T(8,128)(2,1)S(1)}, u32[]{:S(2)}) copy-start(bf16[128,1536]{1,0:T(8,128)(2,1)S(1)} %collective-permute-done.2.refs_2_) | copy-start | bytes 1179652
  18.1 7.5 %collective-permute-start.4 = (bf16[3,384,128]{2,1,0:T(8,128)(2,1)S(1)}, bf16[3,384,128]{2,1,0:T(8,128)(2,1)S(1)}, u32[]{:S(2)}, u32[]{:S(2)}) collective-permute-start(bf16[3,384,128]{2,1,0:T(8,128)(2,1)S(1)} %get-tuple-element.84), channel_id=1, source_target_pairs={{0,4},{1,12},{4,0},{5,8},{8,5},{9,13},{12,1},{13,9},{2,6},{3,14},{... | collective-permute-start | bytes 884744 | tf_op jit(solution)/shard_map/ppermute | solution.py:357
  19.9 12.4 %collective-permute-start.8 = (bf16[128,1536]{1,0:T(8,128)(2,1)S(1)}, bf16[128,1536]{1,0:T(8,128)(2,1)}, u32[]{:S(2)}, u32[]{:S(2)}) collective-permute-start(bf16[128,1536]{1,0:T(8,128)(2,1)S(1)} %collective-permute-done.2.refs_2_), channel_id=1, source_target_pairs={{4,8},{8,4},{5,9},{9,5},{6,10},{10,6},{7,11},{11,7},{20,24},{24,20... | collective-permute-start | bytes 1179656 | tf_op jit(solution)/shard_map/ppermute | solution.py:342
  21.3 10.9 %collective-permute-start.6 = (bf16[128,1536]{1,0:T(8,128)(2,1)S(1)}, bf16[128,1536]{1,0:T(8,128)(2,1)S(1)}, u32[]{:S(2)}, u32[]{:S(2)}) collective-permute-start(bf16[128,1536]{1,0:T(8,128)(2,1)S(1)} %collective-permute-done.2.refs_2_), channel_id=1, source_target_pairs={{0,2},{2,0},{1,3},{3,1},{4,6},{6,4},{5,7},{7,5},{8,10},{10,8},{9,1... | collective-permute-start | bytes 1179656 | tf_op jit(solution)/shard_map/ppermute | solution.py:107
  22.8 15.0 %collective-permute-start.9 = (bf16[128,1536]{1,0:T(8,128)(2,1)S(1)}, bf16[128,1536]{1,0:T(8,128)(2,1)}, u32[]{:S(2)}, u32[]{:S(2)}) collective-permute-start(bf16[128,1536]{1,0:T(8,128)(2,1)S(1)} %collective-permute-done.3.refs_4_), channel_id=1, source_target_pairs={{4,0},{8,12},{5,1},{9,13},{6,2},{10,14},{7,3},{11,15},{20,16},{24,... | collective-permute-start | bytes 1179656 | tf_op jit(solution)/shard_map/ppermute | solution.py:345
  24.1 13.7 %collective-permute-start.7 = (bf16[128,1536]{1,0:T(8,128)(2,1)S(1)}, bf16[128,1536]{1,0:T(8,128)(2,1)}, u32[]{:S(2)}, u32[]{:S(2)}) collective-permute-start(bf16[128,1536]{1,0:T(8,128)(2,1)S(1)} %collective-permute-done.3.refs_4_), channel_id=1, source_target_pairs={{4,6},{6,4},{8,10},{10,8},{5,7},{7,5},{9,11},{11,9},{20,22},{22,20... | collective-permute-start | bytes 1179656 | tf_op jit(solution)/shard_map/ppermute | solution.py:339
  25.6 48.5 %copy-start.7 = (bf16[3,384,128]{2,1,0:T(8,128)(2,1)}, bf16[3,384,128]{2,1,0:T(8,128)(2,1)S(1)}, u32[]{:S(2)}) copy-start(bf16[3,384,128]{2,1,0:T(8,128)(2,1)S(1)} %collective-permute-done.4.refs_2_) | copy-start | bytes 884740
  25.6 6.7 %collective-permute-start.5 = (bf16[3,384,128]{2,1,0:T(8,128)(2,1)S(1)}, bf16[3,384,128]{2,1,0:T(8,128)(2,1)S(1)}, u32[]{:S(2)}, u32[]{:S(2)}) collective-permute-start(bf16[3,384,128]{2,1,0:T(8,128)(2,1)S(1)} %collective-permute-done.refs_0_), channel_id=1, source_target_pairs={{0,16},{16,0},{1,17},{17,1},{2,18},{18,2},{3,19},{19,3},{4,20},{20... | collective-permute-start | bytes 884744 | tf_op jit(solution)/shard_map/ppermute | solution.py:107
  32.3 41.8 %copy-start.9 = (bf16[3,384,128]{2,1,0:T(8,128)(2,1)}, bf16[3,384,128]{2,1,0:T(8,128)(2,1)S(1)}, u32[]{:S(2)}) copy-start(bf16[3,384,128]{2,1,0:T(8,128)(2,1)S(1)} %collective-permute-done.5.refs_1_) | copy-start | bytes 884740
  37.9 27.7 %collective-permute-start.16 = (bf16[768,768]{1,0:T(8,128)(2,1)}, bf16[768,768]{1,0:T(8,128)(2,1)}, u32[]{:S(2)}, u32[]{:S(2)}) collective-permute-start(bf16[768,768]{1,0:T(8,128)(2,1)} %param.8), channel_id=1, source_target_pairs={{0,1},{1,0},{2,3},{3,2},{4,5},{5,4},{6,7},{7,6},{8,9},{9,8},{10,11... | collective-permute-start | bytes 3538952 | tf_op jit(solution)/shard_map/ppermute | solution.py:107
  39.5 10.8 %collective-permute-start.10 = (bf16[3,384,128]{2,1,0:T(8,128)(2,1)S(1)}, bf16[3,384,128]{2,1,0:T(8,128)(2,1)S(1)}, u32[]{:S(2)}, u32[]{:S(2)}) collective-permute-start(bf16[3,384,128]{2,1,0:T(8,128)(2,1)S(1)} %get-tuple-element.91), channel_id=1, source_target_pairs={{0,0},{1,8},{4,4},{5,12},{8,1},{9,9},{12,5},{13,13},{2,2},{3,10},{... | collective-permute-start | bytes 884744 | tf_op jit(solution)/shard_map/ppermute | solution.py:357
  40.1 11.6 %collective-permute-start.11 = (bf16[3,384,128]{2,1,0:T(8,128)(2,1)S(1)}, bf16[3,384,128]{2,1,0:T(8,128)(2,1)S(1)}, u32[]{:S(2)}, u32[]{:S(2)}) collective-permute-start(bf16[3,384,128]{2,1,0:T(8,128)(2,1)S(1)} %get-tuple-element.92), channel_id=1, source_target_pairs={{0,4},{1,12},{4,0},{5,8},{8,5},{9,13},{12,1},{13,9},{2,6},{3,14},{... | collective-permute-start | bytes 884744 | tf_op jit(solution)/shard_map/ppermute | solution.py:357
  45.4 13.1 %collective-permute-start.15 = (bf16[128,1536]{1,0:T(8,128)(2,1)}, bf16[128,1536]{1,0:T(8,128)(2,1)}, u32[]{:S(2)}, u32[]{:S(2)}) collective-permute-start(bf16[128,1536]{1,0:T(8,128)(2,1)} %collective-permute-done.9.refs_8_), channel_id=1, source_target_pairs={{0,2},{2,0},{12,14},{14,12},{1,3},{3,1},{13,15},{15,13},{16,18},{1... | collective-permute-start | bytes 1179656 | tf_op jit(solution)/shard_map/ppermute | solution.py:339
  49.0 16.6 %collective-permute-start.14 = (bf16[128,1536]{1,0:T(8,128)(2,1)}, bf16[128,1536]{1,0:T(8,128)(2,1)}, u32[]{:S(2)}, u32[]{:S(2)}) collective-permute-start(bf16[128,1536]{1,0:T(8,128)(2,1)} %collective-permute-done.8.refs_6_), channel_id=1, source_target_pairs={{4,0},{8,12},{5,1},{9,13},{6,2},{10,14},{7,3},{11,15},{20,16},{24,... | collective-permute-start | bytes 1179656 | tf_op jit(solution)/shard_map/ppermute | solution.py:345
  50.3 40.9 %copy-start.11 = (bf16[3,384,128]{2,1,0:T(8,128)(2,1)}, bf16[3,384,128]{2,1,0:T(8,128)(2,1)S(1)}, u32[]{:S(2)}) copy-start(bf16[3,384,128]{2,1,0:T(8,128)(2,1)S(1)} %collective-permute-done.10.refs_4_) | copy-start | bytes 884740
  50.3 15.3 %collective-permute-start.13 = (bf16[128,1536]{1,0:T(8,128)(2,1)}, bf16[128,1536]{1,0:T(8,128)(2,1)}, u32[]{:S(2)}, u32[]{:S(2)}) collective-permute-start(bf16[128,1536]{1,0:T(8,128)(2,1)} %collective-permute-done.8.refs_6_), channel_id=1, source_target_pairs={{4,6},{6,4},{8,10},{10,8},{5,7},{7,5},{9,11},{11,9},{20,22},{22,20... | collective-permute-start | bytes 1179656 | tf_op jit(solution)/shard_map/ppermute | solution.py:339
  51.7 39.5 %copy-start.13 = (bf16[3,384,128]{2,1,0:T(8,128)(2,1)}, bf16[3,384,128]{2,1,0:T(8,128)(2,1)S(1)}, u32[]{:S(2)}) copy-start(bf16[3,384,128]{2,1,0:T(8,128)(2,1)S(1)} %collective-permute-done.11.refs_6_) | copy-start | bytes 884740
  51.7 6.7 %collective-permute-start.12 = (bf16[3,384,128]{2,1,0:T(8,128)(2,1)S(1)}, bf16[3,384,128]{2,1,0:T(8,128)(2,1)S(1)}, u32[]{:S(2)}, u32[]{:S(2)}) collective-permute-start(bf16[3,384,128]{2,1,0:T(8,128)(2,1)S(1)} %collective-permute-done.4.refs_2_), channel_id=1, source_target_pairs={{0,16},{16,0},{1,17},{17,1},{2,18},{18,2},{3,19},{19,3},{4,20},{20... | collective-permute-start | bytes 884744 | tf_op jit(solution)/shard_map/ppermute | solution.py:107
  65.6 20.2 %collective-permute-start.21 = (bf16[128,1536]{1,0:T(8,128)(2,1)}, bf16[128,1536]{1,0:T(8,128)(2,1)}, u32[]{:S(2)}, u32[]{:S(2)}) collective-permute-start(bf16[128,1536]{1,0:T(8,128)(2,1)} %collective-permute-done.14.refs_10_), channel_id=1, source_target_pairs={{0,2},{2,0},{12,14},{14,12},{1,3},{3,1},{13,15},{15,13},{16,18},{1... | collective-permute-start | bytes 1179656 | tf_op jit(solution)/shard_map/ppermute | solution.py:339
  67.6 7.8 %collective-permute-start.17 = (bf16[3,384,128]{2,1,0:T(8,128)(2,1)}, bf16[3,384,128]{2,1,0:T(8,128)(2,1)}, u32[]{:S(2)}, u32[]{:S(2)}) collective-permute-start(bf16[3,384,128]{2,1,0:T(8,128)(2,1)} %get-tuple-element.102), channel_id=1, source_target_pairs={{0,0},{1,8},{4,4},{5,12},{8,1},{9,9},{12,5},{13,13},{2,2},{3,10},{... | collective-permute-start | bytes 884744 | tf_op jit(solution)/shard_map/ppermute | solution.py:357
  71.4 9.1 %collective-permute-start.18 = (bf16[3,384,128]{2,1,0:T(8,128)(2,1)}, bf16[3,384,128]{2,1,0:T(8,128)(2,1)}, u32[]{:S(2)}, u32[]{:S(2)}) collective-permute-start(bf16[3,384,128]{2,1,0:T(8,128)(2,1)} %get-tuple-element.103), channel_id=1, source_target_pairs={{0,4},{1,12},{4,0},{5,8},{8,5},{9,13},{12,1},{13,9},{2,6},{3,14},{... | collective-permute-start | bytes 884744 | tf_op jit(solution)/shard_map/ppermute | solution.py:357
  71.4 9.1 %collective-permute-start.19 = (bf16[3,384,128]{2,1,0:T(8,128)(2,1)S(1)}, bf16[3,384,128]{2,1,0:T(8,128)(2,1)}, u32[]{:S(2)}, u32[]{:S(2)}) collective-permute-start(bf16[3,384,128]{2,1,0:T(8,128)(2,1)S(1)} %collective-permute-done.10.refs_4_), channel_id=1, source_target_pairs={{0,16},{16,0},{1,17},{17,1},{2,18},{18,2},{3,19},{19,3},{4,20},{20... | collective-permute-start | bytes 884744 | tf_op jit(solution)/shard_map/ppermute | solution.py:107
  72.9 13.0 %collective-permute-start.20 = (bf16[3,384,128]{2,1,0:T(8,128)(2,1)S(1)}, bf16[3,384,128]{2,1,0:T(8,128)(2,1)}, u32[]{:S(2)}, u32[]{:S(2)}) collective-permute-start(bf16[3,384,128]{2,1,0:T(8,128)(2,1)S(1)} %collective-permute-done.11.refs_6_), channel_id=1, source_target_pairs={{0,16},{16,0},{1,17},{17,1},{2,18},{18,2},{3,19},{19,3},{4,20},{20... | collective-permute-start | bytes 884744 | tf_op jit(solution)/shard_map/ppermute | solution.py:107
  85.9 24.3 %collective-permute-start.27 = (s32[2,6]{1,0:T(2,128)S(1)}, s32[2,6]{1,0:T(2,128)S(1)}, u32[]{:S(2)}, u32[]{:S(2)}) collective-permute-start(s32[2,6]{1,0:T(2,128)S(1)} %pad_add_fusion.1), channel_id=1, source_target_pairs={{0,12},{4,8},{8,4},{12,0},{1,13},{5,9},{9,5},{13,1},{2,14},{6,10},... | collective-permute-start | bytes 152 | tf_op jit(solution)/shard_map/ppermute | solution.py:107
  88.4 22.3 %collective-permute-start.26 = (s32[2,6]{1,0:T(2,128)S(1)}, s32[2,6]{1,0:T(2,128)S(1)}, u32[]{:S(2)}, u32[]{:S(2)}) collective-permute-start(s32[2,6]{1,0:T(2,128)S(1)} %pad_add_fusion.1), channel_id=1, source_target_pairs={{0,8},{4,12},{8,0},{12,4},{1,9},{5,13},{9,1},{13,5},{2,10},{6,14},... | collective-permute-start | bytes 152 | tf_op jit(solution)/shard_map/ppermute | solution.py:107
  91.2 19.6 %collective-permute-start.25 = (s32[2,6]{1,0:T(2,128)S(1)}, s32[2,6]{1,0:T(2,128)S(1)}, u32[]{:S(2)}, u32[]{:S(2)}) collective-permute-start(s32[2,6]{1,0:T(2,128)S(1)} %pad_add_fusion.1), channel_id=1, source_target_pairs={{0,4},{4,0},{8,12},{12,8},{1,5},{5,1},{9,13},{13,9},{2,6},{6,2},{1... | collective-permute-start | bytes 152 | tf_op jit(solution)/shard_map/ppermute | solution.py:107
  91.2 21.4 %collective-permute-start.23 = (bf16[3,384,128]{2,1,0:T(8,128)(2,1)}, bf16[3,384,128]{2,1,0:T(8,128)(2,1)}, u32[]{:S(2)}, u32[]{:S(2)}) collective-permute-start(bf16[3,384,128]{2,1,0:T(8,128)(2,1)} %collective-permute-done.17.refs_0_), channel_id=1, source_target_pairs={{0,16},{16,0},{1,17},{17,1},{2,18},{18,2},{3,19},{19,3},{4,20},{20... | collective-permute-start | bytes 884744 | tf_op jit(solution)/shard_map/ppermute | solution.py:107
  92.8 25.2 %collective-permute-start.22 = (bf16[384,768]{1,0:T(8,128)(2,1)S(1)}, bf16[384,768]{1,0:T(8,128)(2,1)S(1)}, u32[]{:S(2)}, u32[]{:S(2)}) collective-permute-start(bf16[384,768]{1,0:T(8,128)(2,1)S(1)} %get-tuple-element.108.refs_4_), channel_id=1, source_target_pairs={{0,4},{4,0},{8,12},{12,8},{1,5},{5,1},{9,13},{13,9},{2,6},{6,2},{1... | collective-permute-start | bytes 1769480 | tf_op jit(solution)/shard_map/ppermute | solution.py:107
  110.2 7.8 %collective-permute-start.24 = (bf16[3,384,128]{2,1,0:T(8,128)(2,1)}, bf16[3,384,128]{2,1,0:T(8,128)(2,1)S(1)}, u32[]{:S(2)}, u32[]{:S(2)}) collective-permute-start(bf16[3,384,128]{2,1,0:T(8,128)(2,1)} %collective-permute-done.18.refs_2_), channel_id=1, source_target_pairs={{0,16},{16,0},{1,17},{17,1},{2,18},{18,2},{3,19},{19,3},{4,20},{20... | collective-permute-start | bytes 884744 | tf_op jit(solution)/shard_map/ppermute | solution.py:107
  118.0 7.1 %collective-permute-start.28 = (bf16[4,320,512]{2,1,0:T(8,128)(2,1)}, bf16[4,320,512]{2,1,0:T(8,128)(2,1)S(1)}, u32[]{:S(2)}, u32[]{:S(2)}) collective-permute-start(bf16[4,320,512]{2,1,0:T(8,128)(2,1)} %copy-done.6), channel_id=1, source_target_pairs={{0,1},{1,0},{2,3},{3,2},{4,5},{5,4},{6,7},{7,6},{8,9},{9,8},{10,11... | collective-permute-start | bytes 3932168 | tf_op jit(solution)/shard_map/ppermute | solution.py:107
  123.8 15.9 %collective-permute-start.29 = (bf16[4,320,256]{2,1,0:T(8,128)(2,1)S(1)}, bf16[4,320,256]{2,1,0:T(8,128)(2,1)S(1)}, u32[]{:S(2)}, u32[]{:S(2)}) collective-permute-start(bf16[4,320,256]{2,1,0:T(8,128)(2,1)S(1)} %get-tuple-element.144), channel_id=1, source_target_pairs={{0,1},{1,0},{2,3},{3,2},{4,5},{5,4},{6,7},{7,6},{8,9},{9,8},{10,11... | collective-permute-start | bytes 1966088 | tf_op jit(solution)/shard_map/ppermute | solution.py:107
  124.4 15.3 %collective-permute-start.30 = (bf16[384,768]{1,0:T(8,128)(2,1)S(1)}, bf16[384,768]{1,0:T(8,128)(2,1)S(1)}, u32[]{:S(2)}, u32[]{:S(2)}) collective-permute-start(bf16[384,768]{1,0:T(8,128)(2,1)S(1)} %get-tuple-element.146.refs_5_), channel_id=1, source_target_pairs={{0,4},{4,0},{8,12},{12,8},{1,5},{5,1},{9,13},{13,9},{2,6},{6,2},{1... | collective-permute-start | bytes 1769480 | tf_op jit(solution)/shard_map/ppermute | solution.py:107
  139.7 22.4 %collective-permute-start.34 = (bf16[384,768]{1,0:T(8,128)(2,1)S(1)}, bf16[384,768]{1,0:T(8,128)(2,1)S(1)}, u32[]{:S(2)}, u32[]{:S(2)}) collective-permute-start(bf16[384,768]{1,0:T(8,128)(2,1)S(1)} %collective-permute-done.22.refs_6_), channel_id=1, source_target_pairs={{0,1},{1,0},{2,3},{3,2},{4,5},{5,4},{6,7},{7,6},{8,9},{9,8},{10,11... | collective-permute-start | bytes 1769480 | tf_op jit(solution)/shard_map/ppermute | solution.py:107
  139.7 22.4 %collective-permute-start.35 = (bf16[384,768]{1,0:T(8,128)(2,1)S(1)}, bf16[384,768]{1,0:T(8,128)(2,1)S(1)}, u32[]{:S(2)}, u32[]{:S(2)}) collective-permute-start(bf16[384,768]{1,0:T(8,128)(2,1)S(1)} %collective-permute-done.30.refs_7_), channel_id=1, source_target_pairs={{0,1},{1,0},{2,3},{3,2},{4,5},{5,4},{6,7},{7,6},{8,9},{9,8},{10,11... | collective-permute-start | bytes 1769480 | tf_op jit(solution)/shard_map/ppermute | solution.py:107
  142.4 19.6 %collective-permute-start.33 = (bf16[2,128,384]{2,1,0:T(8,128)(2,1)S(1)}, bf16[2,128,384]{2,1,0:T(8,128)(2,1)S(1)}, u32[]{:S(2)}, u32[]{:S(2)}) collective-permute-start(bf16[2,128,384]{2,1,0:T(8,128)(2,1)S(1)} %get-tuple-element.153), channel_id=1, source_target_pairs={{0,12},{4,8},{8,4},{12,0},{1,13},{5,9},{9,5},{13,1},{2,14},{6,10},... | collective-permute-start | bytes 589832 | tf_op jit(solution)/shard_map/ppermute | solution.py:107
  143.8 18.3 %collective-permute-start.31 = (bf16[2,128,384]{2,1,0:T(8,128)(2,1)S(1)}, bf16[2,128,384]{2,1,0:T(8,128)(2,1)S(1)}, u32[]{:S(2)}, u32[]{:S(2)}) collective-permute-start(bf16[2,128,384]{2,1,0:T(8,128)(2,1)S(1)} %get-tuple-element.153), channel_id=1, source_target_pairs={{0,4},{4,0},{8,12},{12,8},{1,5},{5,1},{9,13},{13,9},{2,6},{6,2},{1... | collective-permute-start | bytes 589832 | tf_op jit(solution)/shard_map/ppermute | solution.py:107
  143.8 18.3 %collective-permute-start.32 = (bf16[2,128,384]{2,1,0:T(8,128)(2,1)S(1)}, bf16[2,128,384]{2,1,0:T(8,128)(2,1)S(1)}, u32[]{:S(2)}, u32[]{:S(2)}) collective-permute-start(bf16[2,128,384]{2,1,0:T(8,128)(2,1)S(1)} %get-tuple-element.152.refs_0_), channel_id=1, source_target_pairs={{0,8},{4,12},{8,0},{12,4},{1,9},{5,13},{9,1},{13,5},{2,10},{6,14},... | collective-permute-start | bytes 589832 | tf_op jit(solution)/shard_map/ppermute | solution.py:107
  164.6 6.3 %collective-permute-start.36 = (bf16[2,64,768]{2,1,0:T(8,128)(2,1)S(1)}, bf16[2,64,768]{2,1,0:T(8,128)(2,1)S(1)}, u32[]{:S(2)}, u32[]{:S(2)}) collective-permute-start(bf16[2,64,768]{2,1,0:T(8,128)(2,1)S(1)} %get-tuple-element.158), channel_id=1, source_target_pairs={{0,2},{2,0},{1,3},{3,1},{4,6},{6,4},{5,7},{7,5},{8,10},{10,8},{9,1... | collective-permute-start | bytes 589832 | tf_op jit(solution)/shard_map/ppermute | solution.py:107
  166.6 14.0 %collective-permute-start.37 = (bf16[2,64,768]{2,1,0:T(8,128)(2,1)S(1)}, bf16[2,64,768]{2,1,0:T(8,128)(2,1)S(1)}, u32[]{:S(2)}, u32[]{:S(2)}) collective-permute-start(bf16[2,64,768]{2,1,0:T(8,128)(2,1)S(1)} %get-tuple-element.159), channel_id=1, source_target_pairs={{0,8},{4,12},{8,0},{12,4},{1,9},{5,13},{9,1},{13,5},{2,10},{6,14},... | collective-permute-start | bytes 589832 | tf_op jit(solution)/shard_map/ppermute | solution.py:107
  166.7 17.9 %collective-permute-start.38 = (bf16[2,64,768]{2,1,0:T(8,128)(2,1)S(1)}, bf16[2,64,768]{2,1,0:T(8,128)(2,1)S(1)}, u32[]{:S(2)}, u32[]{:S(2)}) collective-permute-start(bf16[2,64,768]{2,1,0:T(8,128)(2,1)S(1)} %get-tuple-element.160), channel_id=1, source_target_pairs={{0,10},{2,8},{4,14},{6,12},{8,2},{10,0},{12,6},{14,4},{1,11},{3,9}... | collective-permute-start | bytes 589832 | tf_op jit(solution)/shard_map/ppermute | solution.py:434
  (16 other events, 147.8 us)

commit v9 on v8

--- a/solution.py
+++ b/solution.py
@@ -107,8 +107,8 @@
     return lax.ppermute(value, axis, [(i, i ^ step) for i in range(peers)])
 
 
-def settle(*values):
-    return lax.optimization_barrier(values)
+def after(value, *others):
+    return lax.optimization_barrier((value, *others))[0]
 
 
 def call(kernel, out_shape, prefetch, operands, scratch=(), flops=0, read=0, limit=VMEM_BYTES):
@@ -157,9 +157,9 @@
 
 def project(place, tokens, chunks):
     rows, _, count, width = tokens.shape
-    half, cols = chunks[0][0][0].shape[1], len(chunks) * HD
-    slices = len(chunks[0])
-    flat = [w for of_head in chunks for of_round in of_head for w in of_round]
+    _, half, cols = chunks[0][0].shape
+    slices = len(chunks)
+    flat = [w for of_round in chunks for w in of_round]
     total_rows = rows * 2 * count
 
     def kernel(place_ref, x_ref, *refs):
@@ -171,8 +171,8 @@
             for g in range(2):
                 at = (row + slices - k) % slices * (2 * half) + (group + g) % 2 * half
                 piece = x_ref[:, :, :, pl.ds(pl.multiple_of(at, half), half)].reshape(-1, half)
-                of_heads = w_refs[2 * k + g :: 2 * slices]
-                weight = jnp.concatenate([w_ref[part] for part in range(3) for w_ref in of_heads], axis=1)
+                w_ref = w_refs[2 * k + g]
+                weight = jnp.concatenate([w_ref[part] for part in range(3)], axis=1)
                 term = jnp.dot(piece, weight, preferred_element_type=jnp.float32)
                 acc = term if acc is None else acc + term
         kv_part = acc[:, cols:].reshape(rows, 2 * count, 2 * cols)
@@ -264,21 +264,22 @@
     width = w_parts[0].shape[1]
 
     def kernel(place_ref, *refs):
-        row, _, frame, core = (place_ref[i] for i in range(4))
+        row, group, frame, core = (place_ref[i] for i in range(4))
         w_refs = refs[4:12]
         keep, over_x, over_z, over_both, a_all, sums = refs[12:]
         for s in range(4):
             a_all[s] = refs[s][...].reshape(blocks * block_len, cols)
 
-        def term(first, side):
-            acc = jnp.dot(a_all[(2 * side) ^ row], w_refs[first][...], preferred_element_type=jnp.float32)
-            acc = acc + jnp.dot(
-                a_all[(2 * side + 1) ^ row], w_refs[first + 1][...], preferred_element_type=jnp.float32
-            )
+        def term(c, first, side):
+            acc = None
+            for i in range(2):
+                at = 2 * side + (i if c == 0 else (i + group) % 2)
+                part = jnp.dot(a_all[at ^ row], w_refs[first + i][...], preferred_element_type=jnp.float32)
+                acc = part if acc is None else acc + part
             return acc.astype(jnp.bfloat16).astype(jnp.float32)
 
         for c in range(2):
-            total = term(2 * c, core) + term(4 + 2 * c, 1 - core)
+            total = term(c, 2 * c, core) + term(c, 4 + 2 * c, 1 - core)
             sums[...] = total.reshape(blocks, 2, BS, width)
             at = (row + c) % 2
             keep[at] = sums[row // 2, frame]
@@ -344,58 +345,43 @@
     def outward(value):
         return lax.ppermute(value, "rows", [(1, 0), (2, 3)])
 
-    def piece(weights, i):
-        at = (0, group * half, (i % span + row) % span * cols + i // span * HD)
-        return lax.dynamic_slice(weights.transpose(1, 0, 2), at, (3, half, HD))
-
-    def reshard(value, i):
+    last = cols // (3 * HD) * HD
+
+    def reshard(i, *others):
+        k = i % span
+        at, wide = (0, cols - last) if i < span else (cols - last, last)
+        value = lax.dynamic_slice(
+            w_qkv.transpose(1, 0, 2), (0, group * half, (k + row) % span * cols + at), (3, half, wide)
+        )
         pairs = [
-            (r * heads_n + h, (h * span + (i % span + r) % span) * heads_n + r // span)
+            (r * heads_n + h, (h * span + (k + r) % span) * heads_n + r // span)
             for r in range(rows_n)
             for h in range(heads_n)
         ]
-        return lax.ppermute(value, ("rows", "heads"), pairs)
-
-    here, there = {}, {}
+        return lax.ppermute(after(value, *others) if others else value, ("rows", "heads"), pairs)
+
     mine = lax.dynamic_slice_in_dim(latents[0], core * span * depth, span * depth, axis=1)
-    here[0] = reshard(piece(w_qkv, 0), 0)
-    mine_x = swap(mine, "frames")
-    near = swap(mine, "rows")
-    in_1 = inward(mine)
-    ready = piece(w_qkv, 1)
-    here, mine_x, near, in_1, ready, w_qkv, w_out = settle(here, mine_x, near, in_1, ready, w_qkv, w_out)
-
-    here[1] = reshard(ready, 1)
-    there[0] = swap(here[0], "groups")
+    in_1, near, mine_x = inward(mine), swap(mine, "rows"), swap(mine, "frames")
+    here, there = [reshard(0)], []
     near_x = swap(near, "frames")
-    in_1x = over_frames(in_1, (1, 2))
-    in_2 = inward(near)
-    out_1 = outward(in_1)
-    ready = [piece(w_qkv, 2), piece(w_qkv, 3)]
-    here, there, near_x, in_1x, in_2, out_1, ready, w_qkv, w_out = settle(
-        here, there, near_x, in_1x, in_2, out_1, ready, w_qkv, w_out
-    )
-
-    here[2], here[3] = reshard(ready[0], 2), reshard(ready[1], 3)
-    there[1] = swap(here[1], "groups")
-    in_2x = over_frames(in_2, (1, 2))
-    out_2 = outward(in_2)
+    out_1, in_1x = outward(in_1), over_frames(in_1, (1, 2))
+    here.append(reshard(1, in_1, near))
+    there.append(swap(here[0], "groups"))
+    across = swap(after(w_out, near), "heads")
+    in_2 = inward(after(near, here[0]))
     out_1x = over_frames(out_1, (0, 3))
-    across = swap(w_out, "heads")
-    ready = [piece(w_qkv, 4), piece(w_qkv, 5)]
-    here, there, in_2x, out_2, out_1x, across, ready, w_qkv, w_out = settle(
-        here, there, in_2x, out_2, out_1x, across, ready, w_qkv, w_out
-    )
-
-    here[4], here[5] = reshard(ready[0], 4), reshard(ready[1], 5)
-    there[2], there[3] = swap(here[2], "groups"), swap(here[3], "groups")
+    here.append(reshard(2, here[1], there[0], mine_x, near_x, in_1x, out_1, across))
+    there.append(swap(here[1], "groups"))
+    out_2, in_2x = outward(in_2), over_frames(in_2, (1, 2))
+    here.append(reshard(3, here[1], there[1], in_2, in_2x, out_1x))
+    there += [swap(here[2], "groups"), swap(here[3], "groups")]
     out_2x = over_frames(out_2, (0, 3))
-    upper, lower = w_out[:cols], w_out[cols:]
+    tokens = assemble(
+        place, [(mine, mine_x), (near, near_x)], [(in_1, in_1x), (in_2, in_2x)], [(out_1, out_1x), (out_2, out_2x)]
+    )
+
     tables = jnp.concatenate([win_blocks, win_counts[:, None], block_window[:, None]], axis=1)
-    here, there, out_2x, upper, lower, w_out, tables = settle(here, there, out_2x, upper, lower, w_out, tables)
-
-    there[4], there[5] = swap(here[4], "groups"), swap(here[5], "groups")
-    beside_upper = swap(upper, "rows")
+    tables = after(tables, there[2])
     found = [tables] + [swap(tables, "rows", s) for s in range(1, rows_n)]
     tables = jnp.stack(found)[row ^ jnp.arange(rows_n)].reshape(rows_n * heads_n, MAXB + 2)
     windows = lax.dynamic_index_in_dim(
@@ -403,31 +389,23 @@
     )
     picked = tables[windows]
     members, counts = picked[:, :MAXB].reshape(-1), picked[:, MAXB]
-    tokens = assemble(
-        place, [(mine, mine_x), (near, near_x)], [(in_1, in_1x), (in_2, in_2x)], [(out_1, out_1x), (out_2, out_2x)]
-    )
-    heads = len(here) // span
-    chunks = [[(here[h * span + k], there[h * span + k]) for k in range(span)] for h in range(heads)]
-    first = project(place, tokens, chunks[:-1])
-    beside_upper, tokens, first, chunks, members, counts, lower = settle(
-        beside_upper, tokens, first, chunks, members, counts, lower
-    )
-
-    beside_lower = swap(lower, "rows")
+
+    out_half = lax.dynamic_slice_in_dim(w_out, group * cols, cols, axis=0)
+    beside = [swap(after(out_half, here[2]), "rows")]
+    beside.append(swap(beside[0], "groups"))
+
+    chunks = [(here[0], there[0]), (here[1], after(there[1], there[2], there[3], members, counts))]
+    first = project(place, tokens, chunks)
     first_more = swap(first[2], "heads")
-    second = project(place, tokens, chunks[-1:])
+    second = project(place, tokens, [(here[2], there[2]), (here[3], after(there[3], first[2], beside[0]))])
     second_more = swap(second[2], "heads")
     attended = attend_all(place, members, counts, *first[:2], first_more)
-    attended, second, second_more, beside_upper, beside_lower = settle(
-        attended, second, second_more, beside_upper, beside_lower
-    )
-
     same, diff = attend_all(place, members, counts, *second[:2], second_more, attended)
     attended = [same] + [swap(same if s % 2 == 0 else diff, "rows", s) for s in range(1, rows_n)]
-    beside = [beside_upper, beside_lower]
-    beside_across = [swap(part, "heads") for part in beside]
+    halves = [w_out[:cols], w_out[cols:], *beside]
+    beside_across = [swap(part, "heads") for part in (beside[0], after(beside[1], attended[1]))]
     keep, over_x, over_z, over_both = mix(
-        place, attended, [upper, lower, *beside, across[:cols], across[cols:], *beside_across]
+        place, attended, [*halves, across[:cols], across[cols:], *beside_across]
     )
     from_x = swap(over_x, "frames")
     from_z = swap(over_z, "rows", 2)

time: 187 us -> 181 us (0.968)
  starting transfers between devices: 60.9 us -> 55.1 us
  waiting for transfers between devices: 82.7 us -> 86.4 us
  local copies, waits for them, and re-layouts: 17.1 us -> 15.2 us
    ppermute x24 -> x22, starting transfers between devices: 33.2 us -> 21.6 us  [swap(): return lax.ppermute(value, axis, [(i, i ^ step) for i in range(peers)])]
    ppermute x24 -> x22, waiting for transfers between devices: 61 us -> 51.5 us  [swap(): return lax.ppermute(value, axis, [(i, i ^ step) for i in range(peers)])]
    ppermute x2, waiting for transfers between devices: 12.7 us -> 19.6 us  [outward(): return lax.ppermute(value, 'rows', [(1, 0), (2, 3)])]
    ppermute x4, waiting for transfers between devices: 0.01 us -> 5.2 us  [over_frames(): return lax.ppermute(value, ('rows', 'frames'), pairs)]
    unnamed x50 -> x30, local copies, waits for them, and re-layouts: 8.4 us -> 6.25 us
    ppermute x6 -> x4, starting transfers between devices: 12.2 us -> 14.2 us  [reshard(): lax.ppermute(after(value, *others) if others else value, ('rows', 'heads'...]
    dynamic_slice x3 -> x2, local copies, waits for them, and re-layouts: 4.17 us -> 3.32 us  [reshard(): lax.dynamic_slice(w_qkv.transpose(1, 0, 2), (0, group * half, (k + row) %...]
    ppermute x6 -> x4, waiting for transfers between devices: 5.08 us -> 4.82 us  [reshard(): lax.ppermute(after(value, *others) if others else value, ('rows', 'heads'...]
  transfers between devices with their start and end apart: 39 -> 35, of which waited for: 14 -> 11; matrix products, arithmetic and copies ran while one was open for 5% -> 5% of each run, Pallas kernels for 11% -> 10%
where the time goes in v9:
time: 181 us
  waiting for transfers between devices  86.4 us (48%)
  starting transfers between devices  55.1 us (30%)
  Pallas kernels  22.7 us (13%)
  local copies, waits for them, and re-layouts  15.2 us (8%)
    ppermute x22, waiting for transfers between devices, swap(): return lax.ppermute(value, axis, [(i, i ^ step) for i in range(peers)])  51.5 us
    pallas_call x7, Pallas kernels, call(): pl.pallas_call(kernel, out_shape=out_shape, grid_spec=pltpu.PrefetchScala...  22.7 us
    ppermute x22, starting transfers between devices, swap(): return lax.ppermute(value, axis, [(i, i ^ step) for i in range(peers)])  21.6 us
    ppermute x2, waiting for transfers between devices, outward(): return lax.ppermute(value, 'rows', [(1, 0), (2, 3)])  19.6 us
    ppermute x4, starting transfers between devices, reshard(): lax.ppermute(after(value, *others) if others else value, ('rows', 'heads'...  14.2 us
    ppermute x4, starting transfers between devices, over_frames(): return lax.ppermute(value, ('rows', 'frames'), pairs)  9.65 us
    unnamed x30, local copies, waits for them, and re-layouts  6.25 us
    ppermute x1, waiting for transfers between devices, by_heads(): lax.ppermute(over_both, ('rows', 'frames'), [(2 * r + f, 2 * (r ^ 2) + 1...  5.22 us
  transfers between devices with their start and end apart: 35, of which 11 were waited for; matrix products, arithmetic and copies ran while one was open for 5% of the time, Pallas kernels for 10%

profile of v9, /device:TPU:0, one launch (start us, length us, event | category | flops | bytes accessed | tf_op | source)
XLA Modules:
  0.0 180.6 jit_solution(7854380642448904614)
XLA Ops:
  0.0 1.1 copy-done
  1.2 3.1 %collective-permute-start.1 = (bf16[128,1536]{1,0:T(8,128)(2,1)S(1)}, bf16[128,1536]{1,0:T(8,128)(2,1)S(1)}, u32[]{:S(2)}, u32[]{:S(2)}) collective-permute-start(bf16[128,1536]{1,0:T(8,128)(2,1)S(1)} %dynamic-slice_bitcast_fusion.2.refs_0_), channel_id=1, source_target_pairs={{0,4},{4,0},{8,12},{12,8},{1,5},{5,1},{9,13},{13,9},{2,6},{6,2},{1... | collective-permute-start | bytes 1179656 | tf_op jit(solution)/shard_map/ppermute | solution.py:107
  4.3 1.4 collective-permute-start
  5.7 1.4 dynamic-slice_bitcast_fusion
  7.8 1.6 collective-permute-start.5
  9.3 4.1 %collective-permute-done.1.refs_2_ = bf16[128,1536]{1,0:T(8,128)(2,1)S(1)} collective-permute-done((bf16[128,1536]{1,0:T(8,128)(2,1)S(1)}, bf16[128,1536]{1,0:T(8,128)(2,1)S(1)}, u32[]{:S(2)}, u32[]{:S(2)}) %collective-permute-start.1) | collective-permute-done | bytes 393248 | tf_op jit(solution)/shard_map/ppermute | solution.py:107
  13.5 1.5 collective-permute-start.6
  15.0 1.3 collective-permute-start.8
  16.4 10.9 %collective-permute-start.2 = (bf16[3,384,256]{2,1,0:T(8,128)(2,1)S(1)}, bf16[3,384,256]{2,1,0:T(8,128)(2,1)S(1)}, u32[]{:S(2)}, u32[]{:S(2)}) collective-permute-start(bf16[3,384,256]{2,1,0:T(8,128)(2,1)S(1)} %get-tuple-element.29), channel_id=1, source_target_pairs={{0,4},{1,12},{4,0},{5,8},{8,5},{9,13},{12,1},{13,9},{2,6},{3,14},{... | collective-permute-start | bytes 1769480 | tf_op jit(solution)/shard_map/ppermute | solution.py:361
  27.2 1.5 collective-permute-start.4
  28.8 1.5 collective-permute-start.7
  30.2 14.9 %collective-permute-done.8.refs_8_ = bf16[128,1536]{1,0:T(8,128)(2,1)} collective-permute-done((bf16[128,1536]{1,0:T(8,128)(2,1)}, bf16[128,1536]{1,0:T(8,128)(2,1)}, u32[]{:S(2)}, u32[]{:S(2)}) %collective-permute-start.8) | collective-permute-done | bytes 393248 | tf_op jit(solution)/shard_map/ppermute | solution.py:346
  45.1 1.4 collective-permute-start.15
  46.5 4.8 %collective-permute-done.2.refs_2_ = bf16[3,384,256]{2,1,0:T(8,128)(2,1)S(1)} collective-permute-done((bf16[3,384,256]{2,1,0:T(8,128)(2,1)S(1)}, bf16[3,384,256]{2,1,0:T(8,128)(2,1)S(1)}, u32[]{:S(2)}, u32[]{:S(2)}) %collective-permute-start.2) | collective-permute-done | bytes 589856 | tf_op jit(solution)/shard_map/ppermute | solution.py:361
  51.3 1.5 collective-permute-start.20
  52.8 3.4 %collective-permute-start.17 = (bf16[128,1536]{1,0:T(8,128)(2,1)}, bf16[128,1536]{1,0:T(8,128)(2,1)}, u32[]{:S(2)}, u32[]{:S(2)}) collective-permute-start(bf16[128,1536]{1,0:T(8,128)(2,1)} %collective-permute-done.8.refs_8_), channel_id=1, source_target_pairs={{0,2},{2,0},{12,14},{14,12},{1,3},{3,1},{13,15},{15,13},{16,18},{1... | collective-permute-start | bytes 1179656 | tf_op jit(solution)/shard_map/ppermute | solution.py:340
  56.2 1.3 collective-permute-start.18
  57.5 1.4 collective-permute-start.16
  59.0 1.9 %dynamic-slice_bitcast_fusion.3 = (bf16[3,384,128]{2,1,0:T(8,128)(2,1)}, bf16[3,384,128]{2,1,0:T(8,128)(2,1)}) fusion(bf16[768,3,768]{2,0,1:T(8,128)(2,1)} %param.7, s32[]{:T(128)S(6)} %select_n.55, s32[]{:T(128)S(6)} %select_n.65, s32[]{:T(128)S(6)} %select_n.57), kind=kLoop, calls=%fused_computation.5 | loop fusion | bytes 1179660 | tf_op jit(solution)/shard_map/dynamic_slice | solution.py:353
  60.9 1.6 collective-permute-start.10
  62.9 4.8 %collective-permute-done.18.refs_10_ = bf16[128,1536]{1,0:T(8,128)(2,1)} collective-permute-done((bf16[128,1536]{1,0:T(8,128)(2,1)}, bf16[128,1536]{1,0:T(8,128)(2,1)}, u32[]{:S(2)}, u32[]{:S(2)}) %collective-permute-start.18) | collective-permute-done | bytes 393248 | tf_op jit(solution)/shard_map/ppermute | solution.py:346
  67.7 3.4 %collective-permute-start.19 = (bf16[128,1536]{1,0:T(8,128)(2,1)}, bf16[128,1536]{1,0:T(8,128)(2,1)}, u32[]{:S(2)}, u32[]{:S(2)}) collective-permute-start(bf16[128,1536]{1,0:T(8,128)(2,1)} %collective-permute-done.18.refs_10_), channel_id=1, source_target_pairs={{0,2},{2,0},{12,14},{14,12},{1,3},{3,1},{13,15},{15,13},{16,18},{1... | collective-permute-start | bytes 1179656 | tf_op jit(solution)/shard_map/ppermute | solution.py:340
  71.1 1.0 collective-permute-start.21
  72.1 1.5 collective-permute-start.11
  74.2 2.4 %fusion.3 = (bf16[384,768]{1,0:T(8,128)(2,1)S(1)}, bf16[384,768]{1,0:T(8,128)(2,1)}, bf16[384,768]{1,0:T(8,128)(2,1)S(1)}) fusion(bf16[768,768]{1,0:T(8,128)(2,1)} %param.8, s32[]{:T(128)S(6)} %select_n.55), kind=kLoop, calls=%fused_computation.20 | loop fusion | bytes 3538948 | tf_op jit(solution)/shard_map/slice | solution.py:405
  76.6 5.2 %collective-permute-done.19.refs_11_ = bf16[128,1536]{1,0:T(8,128)(2,1)} collective-permute-done((bf16[128,1536]{1,0:T(8,128)(2,1)}, bf16[128,1536]{1,0:T(8,128)(2,1)}, u32[]{:S(2)}, u32[]{:S(2)}) %collective-permute-start.19) | collective-permute-done | bytes 393248 | tf_op jit(solution)/shard_map/ppermute | solution.py:340
  81.8 5.0 %shard_map.64.x_ref = bf16[4,2,128,1536]{3,2,1,0:T(8,128)(2,1)} custom-call(s32[4]{0:T(128)} %pad_add_fusion.2.place_ref, bf16[128,1536]{1,0:T(8,128)(2,1)} %copy-done.9, bf16[128,1536]{1,0:T(8,128)(2,1)} %collective-permute-done.5.refs_1_, bf16[128,1536]{1,0:T(8,128)(2,1)} %copy-done.10, bf16[128,1536]{1,0:T(8,128)(2,1)} %copy-done.11, ...), custom_call_target="tpu_custom_call" | custom-call | bytes 7864320 | tf_op jit(solution)/shard_map/pallas_call | solution.py:115
  86.8 1.6 collective-permute-start.22
  88.4 4.7 %collective-permute-start.14 = (s32[2,6]{1,0:T(2,128)S(1)}, s32[2,6]{1,0:T(2,128)S(1)}, u32[]{:S(2)}, u32[]{:S(2)}) collective-permute-start(s32[2,6]{1,0:T(2,128)S(1)} %pad_add_fusion.1), channel_id=1, source_target_pairs={{0,12},{4,8},{8,4},{12,0},{1,13},{5,9},{9,5},{13,1},{2,14},{6,10},... | collective-permute-start | bytes 152 | tf_op jit(solution)/shard_map/ppermute | solution.py:107
  94.2 11.6 %collective-permute-done.14 = s32[2,6]{1,0:T(2,128)S(1)} collective-permute-done((s32[2,6]{1,0:T(2,128)S(1)}, s32[2,6]{1,0:T(2,128)S(1)}, u32[]{:S(2)}, u32[]{:S(2)}) %collective-permute-start.14) | collective-permute-done | bytes 80 | tf_op jit(solution)/shard_map/ppermute | solution.py:107
  107.7 1.9 %copy-done.1 = bf16[4,2,128,1536]{3,2,1,0:T(8,128)(2,1)S(1)} copy-done((bf16[4,2,128,1536]{3,2,1,0:T(8,128)(2,1)S(1)}, bf16[4,2,128,1536]{3,2,1,0:T(8,128)(2,1)}, u32[]{:S(2)}) %copy-start.1) | copy-done | bytes 3145752
  109.5 1.1 copy-done.4
  110.6 1.1 copy-done.6
  111.7 1.1 copy-done.8
  112.7 4.1 %shard_map.65 = (f32[4,128,256]{2,1,0:T(8,128)S(1)}, f32[4,256,512]{2,1,0:T(8,128)S(1)}, bf16[4,320,512]{2,1,0:T(8,128)(2,1)S(1)}) custom-call(s32[4]{0:T(128)S(1)} %copy-done.2, bf16[4,2,128,1536]{3,2,1,0:T(8,128)(2,1)S(1)} %copy-done.1, bf16[3,384,256]{2,1,0:T(8,128)(2,1)S(1)} %collective-permute-done.3.refs_0_, bf16[3,384,256]{2,1,0:T(8,128)(2,1)S(1)} %copy-done.6, ...), custom_call_target="tpu_custom_call" | custom-call | flops 2415919104 | bytes 8053063 | tf_op jit(solution)/shard_map/pallas_call | solution.py:115
  116.9 3.8 %shard_map.66 = (f32[4,128,128]{2,1,0:T(8,128)S(1)}, f32[4,256,256]{2,1,0:T(8,128)S(1)}, bf16[4,320,256]{2,1,0:T(8,128)(2,1)S(1)}) custom-call(s32[4]{0:T(128)S(1)} %copy-done.2, bf16[4,2,128,1536]{3,2,1,0:T(8,128)(2,1)S(1)} %copy-done.1, bf16[3,384,128]{2,1,0:T(8,128)(2,1)S(1)} %collective-permute-done.10.refs_0_, ...), custom_call_target="tpu_custom_call" | custom-call | flops 1207959552 | bytes 4026531 | tf_op jit(solution)/shard_map/pallas_call | solution.py:115
  121.3 3.8 %shard_map.67 = (bf16[2,128,256]{2,1,0:T(8,128)(2,1)S(1)}, bf16[2,128,256]{2,1,0:T(8,128)(2,1)S(1)}) custom-call(s32[4]{0:T(128)S(1)} %copy-done.2, s32[16]{0:T(128)S(1)} %reshape.24.members_ref, s32[4]{0:T(128)S(1)} %slice_reduce_fusion.1.counts_ref, f32[4,128,256]{2,1,0:T(8,128)S(1)} %get-tuple-element.42.q_ref, ...), custom_call_target="tpu_custom_call" | custom-call | flops 268435456 | bytes 2097152 | tf_op jit(solution)/shard_map/pallas_call | solution.py:115
  125.1 2.2 %shard_map.68 = (bf16[2,128,384]{2,1,0:T(8,128)(2,1)S(1)}, bf16[2,128,384]{2,1,0:T(8,128)(2,1)S(1)}) custom-call(s32[4]{0:T(128)S(1)} %copy-done.2, s32[16]{0:T(128)S(1)} %reshape.24.members_ref, s32[4]{0:T(128)S(1)} %slice_reduce_fusion.1.counts_ref, f32[4,128,128]{2,1,0:T(8,128)S(1)} %get-tuple-element.39.q_ref, ...), custom_call_target="tpu_custom_call" | custom-call | flops 134217728 | bytes 1048576 | tf_op jit(solution)/shard_map/pallas_call | solution.py:115
  127.9 8.7 %collective-permute-done.29.refs_7_ = bf16[384,768]{1,0:T(8,128)(2,1)S(1)} collective-permute-done((bf16[384,768]{1,0:T(8,128)(2,1)S(1)}, bf16[384,768]{1,0:T(8,128)(2,1)S(1)}, u32[]{:S(2)}, u32[]{:S(2)}) %collective-permute-start.29) | collective-permute-done | bytes 589856 | tf_op jit(solution)/shard_map/ppermute | solution.py:107
  136.6 1.8 collective-permute-start.28
  138.6 1.3 fusion.2
  139.9 16.6 %collective-permute-done.27.refs_2_ = bf16[2,128,384]{2,1,0:T(8,128)(2,1)S(1)} collective-permute-done((bf16[2,128,384]{2,1,0:T(8,128)(2,1)S(1)}, bf16[2,128,384]{2,1,0:T(8,128)(2,1)S(1)}, u32[]{:S(2)}, u32[]{:S(2)}) %collective-permute-start.27) | collective-permute-done | bytes 196640 | tf_op jit(solution)/shard_map/ppermute | solution.py:107
  156.5 2.5 %shard_map.69 = (f32[2,64,768]{2,1,0:T(8,128)S(1)}, bf16[2,64,768]{2,1,0:T(8,128)(2,1)S(1)}, bf16[2,64,768]{2,1,0:T(8,128)(2,1)S(1)}, bf16[2,64,768]{2,1,0:T(8,128)(2,1)S(1)}) custom-call(s32[4]{0:T(128)S(1)} %copy-done.2, bf16[2,128,384]{2,1,0:T(8,128)(2,1)S(1)} %get-tuple-element.46.refs_0_, bf16[2,128,384]{2,1,0:T(8,128)(2,1)S(1)} %collective-permute-done.26.refs_1_, ...), custom_call_target="tpu_custom_call" | custom-call | flops 1207959552 | bytes 4718592 | tf_op jit(solution)/shard_map/pallas_call | solution.py:115
  159.1 4.3 %collective-permute-start.34 = (bf16[2,64,768]{2,1,0:T(8,128)(2,1)S(1)}, bf16[2,64,768]{2,1,0:T(8,128)(2,1)S(1)}, u32[]{:S(2)}, u32[]{:S(2)}) collective-permute-start(bf16[2,64,768]{2,1,0:T(8,128)(2,1)S(1)} %get-tuple-element.52), channel_id=1, source_target_pairs={{0,10},{2,8},{4,14},{6,12},{8,2},{10,0},{12,6},{14,4},{1,11},{3,9}... | collective-permute-start | bytes 589832 | tf_op jit(solution)/shard_map/ppermute | solution.py:412
  163.4 2.1 %collective-permute-done.32.x_ref = bf16[2,64,768]{2,1,0:T(8,128)(2,1)S(1)} collective-permute-done((bf16[2,64,768]{2,1,0:T(8,128)(2,1)S(1)}, bf16[2,64,768]{2,1,0:T(8,128)(2,1)S(1)}, u32[]{:S(2)}, u32[]{:S(2)}) %collective-permute-start.32) | collective-permute-done | bytes 196640 | tf_op jit(solution)/shard_map/ppermute | solution.py:107
  165.6 8.4 %collective-permute-done.33.z_ref = bf16[2,64,768]{2,1,0:T(8,128)(2,1)S(1)} collective-permute-done((bf16[2,64,768]{2,1,0:T(8,128)(2,1)S(1)}, bf16[2,64,768]{2,1,0:T(8,128)(2,1)S(1)}, u32[]{:S(2)}, u32[]{:S(2)}) %collective-permute-start.33) | collective-permute-done | bytes 196640 | tf_op jit(solution)/shard_map/ppermute | solution.py:107
  174.0 5.2 %collective-permute-done.34.both_ref = bf16[2,64,768]{2,1,0:T(8,128)(2,1)S(1)} collective-permute-done((bf16[2,64,768]{2,1,0:T(8,128)(2,1)S(1)}, bf16[2,64,768]{2,1,0:T(8,128)(2,1)S(1)}, u32[]{:S(2)}, u32[]{:S(2)}) %collective-permute-start.34) | collective-permute-done | bytes 196640 | tf_op jit(solution)/shard_map/ppermute | solution.py:412
  179.2 1.4 shard_map.70
  (79 shorter events, 6.5 us)
Async XLA Ops:
  0.0 1.1 copy-start
  1.2 15.2 %copy-start.9 = (bf16[128,1536]{1,0:T(8,128)(2,1)}, bf16[128,1536]{1,0:T(8,128)(2,1)S(1)}, u32[]{:S(2)}) copy-start(bf16[128,1536]{1,0:T(8,128)(2,1)S(1)} %dynamic-slice_bitcast_fusion.2.refs_0_) | copy-start | bytes 1179652
  1.2 12.2 %collective-permute-start.1 = (bf16[128,1536]{1,0:T(8,128)(2,1)S(1)}, bf16[128,1536]{1,0:T(8,128)(2,1)S(1)}, u32[]{:S(2)}, u32[]{:S(2)}) collective-permute-start(bf16[128,1536]{1,0:T(8,128)(2,1)S(1)} %dynamic-slice_bitcast_fusion.2.refs_0_), channel_id=1, source_target_pairs={{0,4},{4,0},{8,12},{12,8},{1,5},{5,1},{9,13},{13,9},{2,6},{6,2},{1... | collective-permute-start | bytes 1179656 | tf_op jit(solution)/shard_map/ppermute | solution.py:107
  4.3 10.8 %collective-permute-start = (bf16[128,1536]{1,0:T(8,128)(2,1)S(1)}, bf16[128,1536]{1,0:T(8,128)(2,1)}, u32[]{:S(2)}, u32[]{:S(2)}) collective-permute-start(bf16[128,1536]{1,0:T(8,128)(2,1)S(1)} %dynamic-slice_bitcast_fusion.2.refs_0_), channel_id=1, source_target_pairs={{4,8},{8,4},{5,9},{9,5},{6,10},{10,6},{7,11},{11,7},{20,24},{24,20... | collective-permute-start | bytes 1179656 | tf_op jit(solution)/shard_map/ppermute | solution.py:343
  5.7 56.8 %copy-start.13 = (s32[2]{0:T(128)S(1)}, s32[2]{0:T(128)}, u32[]{:S(2)}) copy-start(s32[2]{0:T(128)} %param.10) | copy-start | bytes 28
  5.7 56.9 %copy-start.14 = (s32[2]{0:T(128)S(1)}, s32[2]{0:T(128)}, u32[]{:S(2)}) copy-start(s32[2]{0:T(128)} %param.11) | copy-start | bytes 28
  5.7 57.2 %copy-start.12 = (s32[2,4]{1,0:T(2,128)S(1)}, s32[2,4]{1,0:T(2,128)}, u32[]{:S(2)}) copy-start(s32[2,4]{1,0:T(2,128)} %param.9) | copy-start | bytes 100
  7.1 20.2 %collective-permute-start.3 = (bf16[3,384,256]{2,1,0:T(8,128)(2,1)S(1)}, bf16[3,384,256]{2,1,0:T(8,128)(2,1)S(1)}, u32[]{:S(2)}, u32[]{:S(2)}) collective-permute-start(bf16[3,384,256]{2,1,0:T(8,128)(2,1)S(1)} %get-tuple-element.55), channel_id=1, source_target_pairs={{0,0},{1,8},{4,4},{5,12},{8,1},{9,9},{12,5},{13,13},{2,2},{3,10},{... | collective-permute-start | bytes 1769480 | tf_op jit(solution)/shard_map/ppermute | solution.py:361
  7.8 8.6 %collective-permute-start.5 = (bf16[128,1536]{1,0:T(8,128)(2,1)S(1)}, bf16[128,1536]{1,0:T(8,128)(2,1)}, u32[]{:S(2)}, u32[]{:S(2)}) collective-permute-start(bf16[128,1536]{1,0:T(8,128)(2,1)S(1)} %dynamic-slice_bitcast_fusion.2.refs_0_), channel_id=1, source_target_pairs={{0,2},{2,0},{1,3},{3,1},{4,6},{6,4},{5,7},{7,5},{8,10},{10,8},{9,1... | collective-permute-start | bytes 1179656 | tf_op jit(solution)/shard_map/ppermute | solution.py:107
  13.4 47.5 %copy-start.10 = (bf16[128,1536]{1,0:T(8,128)(2,1)}, bf16[128,1536]{1,0:T(8,128)(2,1)S(1)}, u32[]{:S(2)}) copy-start(bf16[128,1536]{1,0:T(8,128)(2,1)S(1)} %collective-permute-done.1.refs_2_) | copy-start | bytes 1179652
  13.4 47.5 %collective-permute-start.9 = (bf16[768,768]{1,0:T(8,128)(2,1)}, bf16[768,768]{1,0:T(8,128)(2,1)}, u32[]{:S(2)}, u32[]{:S(2)}) collective-permute-start(bf16[768,768]{1,0:T(8,128)(2,1)} %param.8), channel_id=1, source_target_pairs={{0,1},{1,0},{2,3},{3,2},{4,5},{5,4},{6,7},{7,6},{8,9},{9,8},{10,11... | collective-permute-start | bytes 3538952 | tf_op jit(solution)/shard_map/ppermute | solution.py:107
  13.5 15.2 %collective-permute-start.6 = (bf16[128,1536]{1,0:T(8,128)(2,1)S(1)}, bf16[128,1536]{1,0:T(8,128)(2,1)S(1)}, u32[]{:S(2)}, u32[]{:S(2)}) collective-permute-start(bf16[128,1536]{1,0:T(8,128)(2,1)S(1)} %collective-permute-done.1.refs_2_), channel_id=1, source_target_pairs={{0,2},{2,0},{1,3},{3,1},{4,6},{6,4},{5,7},{7,5},{8,10},{10,8},{9,1... | collective-permute-start | bytes 1179656 | tf_op jit(solution)/shard_map/ppermute | solution.py:107
  15.0 30.0 %collective-permute-start.8 = (bf16[128,1536]{1,0:T(8,128)(2,1)}, bf16[128,1536]{1,0:T(8,128)(2,1)}, u32[]{:S(2)}, u32[]{:S(2)}) collective-permute-start(bf16[128,1536]{1,0:T(8,128)(2,1)} %collective-permute-done.refs_4_), channel_id=1, source_target_pairs={{4,0},{8,12},{5,1},{9,13},{6,2},{10,14},{7,3},{11,15},{20,16},{24,... | collective-permute-start | bytes 1179656 | tf_op jit(solution)/shard_map/ppermute | solution.py:346
  16.4 34.9 %collective-permute-start.2 = (bf16[3,384,256]{2,1,0:T(8,128)(2,1)S(1)}, bf16[3,384,256]{2,1,0:T(8,128)(2,1)S(1)}, u32[]{:S(2)}, u32[]{:S(2)}) collective-permute-start(bf16[3,384,256]{2,1,0:T(8,128)(2,1)S(1)} %get-tuple-element.29), channel_id=1, source_target_pairs={{0,4},{1,12},{4,0},{5,8},{8,5},{9,13},{12,1},{13,9},{2,6},{3,14},{... | collective-permute-start | bytes 1769480 | tf_op jit(solution)/shard_map/ppermute | solution.py:361
  27.2 30.3 %collective-permute-start.4 = (bf16[3,384,256]{2,1,0:T(8,128)(2,1)S(1)}, bf16[3,384,256]{2,1,0:T(8,128)(2,1)S(1)}, u32[]{:S(2)}, u32[]{:S(2)}) collective-permute-start(bf16[3,384,256]{2,1,0:T(8,128)(2,1)S(1)} %collective-permute-done.3.refs_0_), channel_id=1, source_target_pairs={{0,16},{16,0},{1,17},{17,1},{2,18},{18,2},{3,19},{19,3},{4,20},{20... | collective-permute-start | bytes 1769480 | tf_op jit(solution)/shard_map/ppermute | solution.py:107
  28.8 17.7 %copy-start.11 = (bf16[128,1536]{1,0:T(8,128)(2,1)}, bf16[128,1536]{1,0:T(8,128)(2,1)S(1)}, u32[]{:S(2)}) copy-start(bf16[128,1536]{1,0:T(8,128)(2,1)S(1)} %collective-permute-done.6.refs_3_) | copy-start | bytes 1179652
  28.8 24.0 %collective-permute-start.7 = (bf16[128,1536]{1,0:T(8,128)(2,1)}, bf16[128,1536]{1,0:T(8,128)(2,1)}, u32[]{:S(2)}, u32[]{:S(2)}) collective-permute-start(bf16[128,1536]{1,0:T(8,128)(2,1)} %collective-permute-done.refs_4_), channel_id=1, source_target_pairs={{4,6},{6,4},{8,10},{10,8},{5,7},{7,5},{9,11},{11,9},{20,22},{22,20... | collective-permute-start | bytes 1179656 | tf_op jit(solution)/shard_map/ppermute | solution.py:340
  45.1 11.1 %collective-permute-start.15 = (bf16[128,1536]{1,0:T(8,128)(2,1)S(1)}, bf16[128,1536]{1,0:T(8,128)(2,1)}, u32[]{:S(2)}, u32[]{:S(2)}) collective-permute-start(bf16[128,1536]{1,0:T(8,128)(2,1)S(1)} %collective-permute-done.1.refs_2_), channel_id=1, source_target_pairs={{4,8},{8,4},{5,9},{9,5},{6,10},{10,6},{7,11},{11,7},{20,24},{24,20... | collective-permute-start | bytes 1179656 | tf_op jit(solution)/shard_map/ppermute | solution.py:343
  51.3 22.9 %copy-start.3 = (bf16[3,384,256]{2,1,0:T(8,128)(2,1)}, bf16[3,384,256]{2,1,0:T(8,128)(2,1)S(1)}, u32[]{:S(2)}) copy-start(bf16[3,384,256]{2,1,0:T(8,128)(2,1)S(1)} %collective-permute-done.2.refs_2_) | copy-start | bytes 1769476
  51.3 19.8 %collective-permute-start.20 = (bf16[3,384,256]{2,1,0:T(8,128)(2,1)S(1)}, bf16[3,384,256]{2,1,0:T(8,128)(2,1)S(1)}, u32[]{:S(2)}, u32[]{:S(2)}) collective-permute-start(bf16[3,384,256]{2,1,0:T(8,128)(2,1)S(1)} %collective-permute-done.2.refs_2_), channel_id=1, source_target_pairs={{0,16},{16,0},{1,17},{17,1},{2,18},{18,2},{3,19},{19,3},{4,20},{20... | collective-permute-start | bytes 1769480 | tf_op jit(solution)/shard_map/ppermute | solution.py:107
  52.8 18.3 %collective-permute-start.17 = (bf16[128,1536]{1,0:T(8,128)(2,1)}, bf16[128,1536]{1,0:T(8,128)(2,1)}, u32[]{:S(2)}, u32[]{:S(2)}) collective-permute-start(bf16[128,1536]{1,0:T(8,128)(2,1)} %collective-permute-done.8.refs_8_), channel_id=1, source_target_pairs={{0,2},{2,0},{12,14},{14,12},{1,3},{3,1},{13,15},{15,13},{16,18},{1... | collective-permute-start | bytes 1179656 | tf_op jit(solution)/shard_map/ppermute | solution.py:340
  56.2 11.5 %collective-permute-start.18 = (bf16[128,1536]{1,0:T(8,128)(2,1)}, bf16[128,1536]{1,0:T(8,128)(2,1)}, u32[]{:S(2)}, u32[]{:S(2)}) collective-permute-start(bf16[128,1536]{1,0:T(8,128)(2,1)} %collective-permute-done.15.refs_6_), channel_id=1, source_target_pairs={{4,0},{8,12},{5,1},{9,13},{6,2},{10,14},{7,3},{11,15},{20,16},{24,... | collective-permute-start | bytes 1179656 | tf_op jit(solution)/shard_map/ppermute | solution.py:346
  57.5 16.7 %copy-start.5 = (bf16[3,384,256]{2,1,0:T(8,128)(2,1)}, bf16[3,384,256]{2,1,0:T(8,128)(2,1)S(1)}, u32[]{:S(2)}) copy-start(bf16[3,384,256]{2,1,0:T(8,128)(2,1)S(1)} %collective-permute-done.4.refs_1_) | copy-start | bytes 1769476
  57.5 13.5 %collective-permute-start.16 = (bf16[128,1536]{1,0:T(8,128)(2,1)}, bf16[128,1536]{1,0:T(8,128)(2,1)}, u32[]{:S(2)}, u32[]{:S(2)}) collective-permute-start(bf16[128,1536]{1,0:T(8,128)(2,1)} %collective-permute-done.15.refs_6_), channel_id=1, source_target_pairs={{4,6},{6,4},{8,10},{10,8},{5,7},{7,5},{9,11},{11,9},{20,22},{22,20... | collective-permute-start | bytes 1179656 | tf_op jit(solution)/shard_map/ppermute | solution.py:340
  60.9 11.2 %collective-permute-start.10 = (bf16[3,384,128]{2,1,0:T(8,128)(2,1)}, bf16[3,384,128]{2,1,0:T(8,128)(2,1)S(1)}, u32[]{:S(2)}, u32[]{:S(2)}) collective-permute-start(bf16[3,384,128]{2,1,0:T(8,128)(2,1)} %get-tuple-element.31), channel_id=1, source_target_pairs={{0,0},{1,8},{4,4},{5,12},{8,1},{9,9},{12,5},{13,13},{2,2},{3,10},{... | collective-permute-start | bytes 884744 | tf_op jit(solution)/shard_map/ppermute | solution.py:361
  67.7 14.2 %collective-permute-start.19 = (bf16[128,1536]{1,0:T(8,128)(2,1)}, bf16[128,1536]{1,0:T(8,128)(2,1)}, u32[]{:S(2)}, u32[]{:S(2)}) collective-permute-start(bf16[128,1536]{1,0:T(8,128)(2,1)} %collective-permute-done.18.refs_10_), channel_id=1, source_target_pairs={{0,2},{2,0},{12,14},{14,12},{1,3},{3,1},{13,15},{15,13},{16,18},{1... | collective-permute-start | bytes 1179656 | tf_op jit(solution)/shard_map/ppermute | solution.py:340
  71.1 5.5 %copy-start.7 = (bf16[3,384,256]{2,1,0:T(8,128)(2,1)}, bf16[3,384,256]{2,1,0:T(8,128)(2,1)S(1)}, u32[]{:S(2)}) copy-start(bf16[3,384,256]{2,1,0:T(8,128)(2,1)S(1)} %collective-permute-done.20.refs_3_) | copy-start | bytes 1769476
  71.1 15.7 %collective-permute-start.21 = (bf16[3,384,128]{2,1,0:T(8,128)(2,1)}, bf16[3,384,128]{2,1,0:T(8,128)(2,1)}, u32[]{:S(2)}, u32[]{:S(2)}) collective-permute-start(bf16[3,384,128]{2,1,0:T(8,128)(2,1)} %get-tuple-element.34), channel_id=1, source_target_pairs={{0,4},{1,12},{4,0},{5,8},{8,5},{9,13},{12,1},{13,9},{2,6},{3,14},{... | collective-permute-start | bytes 884744 | tf_op jit(solution)/shard_map/ppermute | solution.py:361
  72.1 16.3 %collective-permute-start.11 = (bf16[3,384,128]{2,1,0:T(8,128)(2,1)S(1)}, bf16[3,384,128]{2,1,0:T(8,128)(2,1)}, u32[]{:S(2)}, u32[]{:S(2)}) collective-permute-start(bf16[3,384,128]{2,1,0:T(8,128)(2,1)S(1)} %collective-permute-done.10.refs_0_), channel_id=1, source_target_pairs={{0,16},{16,0},{1,17},{17,1},{2,18},{18,2},{3,19},{19,3},{4,20},{20... | collective-permute-start | bytes 884744 | tf_op jit(solution)/shard_map/ppermute | solution.py:107
  76.6 31.0 %copy-start.2 = (s32[4]{0:T(128)S(1)}, s32[4]{0:T(128)}, u32[]{:S(2)}) copy-start(s32[4]{0:T(128)} %pad_add_fusion.2.place_ref) | copy-start | bytes 52
  86.8 30.1 %collective-permute-start.23 = (bf16[384,768]{1,0:T(8,128)(2,1)}, bf16[384,768]{1,0:T(8,128)(2,1)S(1)}, u32[]{:S(2)}, u32[]{:S(2)}) collective-permute-start(bf16[384,768]{1,0:T(8,128)(2,1)} %get-tuple-element.37), channel_id=1, source_target_pairs={{0,4},{4,0},{8,12},{12,8},{1,5},{5,1},{9,13},{13,9},{2,6},{6,2},{1... | collective-permute-start | bytes 1769480 | tf_op jit(solution)/shard_map/ppermute | solution.py:107
  86.8 20.8 %collective-permute-start.22 = (bf16[3,384,128]{2,1,0:T(8,128)(2,1)}, bf16[3,384,128]{2,1,0:T(8,128)(2,1)}, u32[]{:S(2)}, u32[]{:S(2)}) collective-permute-start(bf16[3,384,128]{2,1,0:T(8,128)(2,1)} %collective-permute-done.21.refs_2_), channel_id=1, source_target_pairs={{0,16},{16,0},{1,17},{17,1},{2,18},{18,2},{3,19},{19,3},{4,20},{20... | collective-permute-start | bytes 884744 | tf_op jit(solution)/shard_map/ppermute | solution.py:107
  88.4 17.3 %collective-permute-start.14 = (s32[2,6]{1,0:T(2,128)S(1)}, s32[2,6]{1,0:T(2,128)S(1)}, u32[]{:S(2)}, u32[]{:S(2)}) collective-permute-start(s32[2,6]{1,0:T(2,128)S(1)} %pad_add_fusion.1), channel_id=1, source_target_pairs={{0,12},{4,8},{8,4},{12,0},{1,13},{5,9},{9,5},{13,1},{2,14},{6,10},... | collective-permute-start | bytes 152 | tf_op jit(solution)/shard_map/ppermute | solution.py:107
  93.1 12.6 %collective-permute-start.13 = (s32[2,6]{1,0:T(2,128)S(1)}, s32[2,6]{1,0:T(2,128)S(1)}, u32[]{:S(2)}, u32[]{:S(2)}) collective-permute-start(s32[2,6]{1,0:T(2,128)S(1)} %pad_add_fusion.1), channel_id=1, source_target_pairs={{0,8},{4,12},{8,0},{12,4},{1,9},{5,13},{9,1},{13,5},{2,10},{6,14},... | collective-permute-start | bytes 152 | tf_op jit(solution)/shard_map/ppermute | solution.py:107
  93.7 12.1 %collective-permute-start.12 = (s32[2,6]{1,0:T(2,128)S(1)}, s32[2,6]{1,0:T(2,128)S(1)}, u32[]{:S(2)}, u32[]{:S(2)}) collective-permute-start(s32[2,6]{1,0:T(2,128)S(1)} %pad_add_fusion.1), channel_id=1, source_target_pairs={{0,4},{4,0},{8,12},{12,8},{1,5},{5,1},{9,13},{13,9},{2,6},{6,2},{1... | collective-permute-start | bytes 152 | tf_op jit(solution)/shard_map/ppermute | solution.py:107
  107.7 1.9 %copy-start.1 = (bf16[4,2,128,1536]{3,2,1,0:T(8,128)(2,1)S(1)}, bf16[4,2,128,1536]{3,2,1,0:T(8,128)(2,1)}, u32[]{:S(2)}) copy-start(bf16[4,2,128,1536]{3,2,1,0:T(8,128)(2,1)} %shard_map.64.x_ref) | copy-start | bytes 9437188
  109.5 1.1 copy-start.4
  116.8 4.5 %collective-permute-start.25 = (bf16[4,320,512]{2,1,0:T(8,128)(2,1)S(1)}, bf16[4,320,512]{2,1,0:T(8,128)(2,1)S(1)}, u32[]{:S(2)}, u32[]{:S(2)}) collective-permute-start(bf16[4,320,512]{2,1,0:T(8,128)(2,1)S(1)} %get-tuple-element.36), channel_id=1, source_target_pairs={{0,1},{1,0},{2,3},{3,2},{4,5},{5,4},{6,7},{7,6},{8,9},{9,8},{10,11... | collective-permute-start | bytes 3932168 | tf_op jit(solution)/shard_map/ppermute | solution.py:107
  120.7 4.4 %collective-permute-start.24 = (bf16[4,320,256]{2,1,0:T(8,128)(2,1)S(1)}, bf16[4,320,256]{2,1,0:T(8,128)(2,1)S(1)}, u32[]{:S(2)}, u32[]{:S(2)}) collective-permute-start(bf16[4,320,256]{2,1,0:T(8,128)(2,1)S(1)} %get-tuple-element.41), channel_id=1, source_target_pairs={{0,1},{1,0},{2,3},{3,2},{4,5},{5,4},{6,7},{7,6},{8,9},{9,8},{10,11... | collective-permute-start | bytes 1966088 | tf_op jit(solution)/shard_map/ppermute | solution.py:107
  121.3 15.3 %collective-permute-start.29 = (bf16[384,768]{1,0:T(8,128)(2,1)S(1)}, bf16[384,768]{1,0:T(8,128)(2,1)S(1)}, u32[]{:S(2)}, u32[]{:S(2)}) collective-permute-start(bf16[384,768]{1,0:T(8,128)(2,1)S(1)} %collective-permute-done.23.refs_6_), channel_id=1, source_target_pairs={{0,16},{16,0},{1,17},{17,1},{2,18},{18,2},{3,19},{19,3},{4,20},{20... | collective-permute-start | bytes 1769480 | tf_op jit(solution)/shard_map/ppermute | solution.py:107
  127.3 9.3 %collective-permute-start.26 = (bf16[2,128,384]{2,1,0:T(8,128)(2,1)S(1)}, bf16[2,128,384]{2,1,0:T(8,128)(2,1)S(1)}, u32[]{:S(2)}, u32[]{:S(2)}) collective-permute-start(bf16[2,128,384]{2,1,0:T(8,128)(2,1)S(1)} %get-tuple-element.47), channel_id=1, source_target_pairs={{0,4},{4,0},{8,12},{12,8},{1,5},{5,1},{9,13},{13,9},{2,6},{6,2},{1... | collective-permute-start | bytes 589832 | tf_op jit(solution)/shard_map/ppermute | solution.py:107
  127.9 12.0 %collective-permute-start.30 = (bf16[384,768]{1,0:T(8,128)(2,1)S(1)}, bf16[384,768]{1,0:T(8,128)(2,1)S(1)}, u32[]{:S(2)}, u32[]{:S(2)}) collective-permute-start(bf16[384,768]{1,0:T(8,128)(2,1)S(1)} %collective-permute-done.23.refs_6_), channel_id=1, source_target_pairs={{0,1},{1,0},{2,3},{3,2},{4,5},{5,4},{6,7},{7,6},{8,9},{9,8},{10,11... | collective-permute-start | bytes 1769480 | tf_op jit(solution)/shard_map/ppermute | solution.py:107
  136.6 19.9 %collective-permute-start.31 = (bf16[384,768]{1,0:T(8,128)(2,1)S(1)}, bf16[384,768]{1,0:T(8,128)(2,1)S(1)}, u32[]{:S(2)}, u32[]{:S(2)}) collective-permute-start(bf16[384,768]{1,0:T(8,128)(2,1)S(1)} %collective-permute-done.29.refs_7_), channel_id=1, source_target_pairs={{0,1},{1,0},{2,3},{3,2},{4,5},{5,4},{6,7},{7,6},{8,9},{9,8},{10,11... | collective-permute-start | bytes 1769480 | tf_op jit(solution)/shard_map/ppermute | solution.py:107
  136.6 19.9 %collective-permute-start.28 = (bf16[2,128,384]{2,1,0:T(8,128)(2,1)S(1)}, bf16[2,128,384]{2,1,0:T(8,128)(2,1)S(1)}, u32[]{:S(2)}, u32[]{:S(2)}) collective-permute-start(bf16[2,128,384]{2,1,0:T(8,128)(2,1)S(1)} %get-tuple-element.47), channel_id=1, source_target_pairs={{0,12},{4,8},{8,4},{12,0},{1,13},{5,9},{9,5},{13,1},{2,14},{6,10},... | collective-permute-start | bytes 589832 | tf_op jit(solution)/shard_map/ppermute | solution.py:107
  138.3 18.2 %collective-permute-start.27 = (bf16[2,128,384]{2,1,0:T(8,128)(2,1)S(1)}, bf16[2,128,384]{2,1,0:T(8,128)(2,1)S(1)}, u32[]{:S(2)}, u32[]{:S(2)}) collective-permute-start(bf16[2,128,384]{2,1,0:T(8,128)(2,1)S(1)} %get-tuple-element.46.refs_0_), channel_id=1, source_target_pairs={{0,8},{4,12},{8,0},{12,4},{1,9},{5,13},{9,1},{13,5},{2,10},{6,14},... | collective-permute-start | bytes 589832 | tf_op jit(solution)/shard_map/ppermute | solution.py:107
  159.0 6.6 %collective-permute-start.32 = (bf16[2,64,768]{2,1,0:T(8,128)(2,1)S(1)}, bf16[2,64,768]{2,1,0:T(8,128)(2,1)S(1)}, u32[]{:S(2)}, u32[]{:S(2)}) collective-permute-start(bf16[2,64,768]{2,1,0:T(8,128)(2,1)S(1)} %get-tuple-element.50), channel_id=1, source_target_pairs={{0,2},{2,0},{1,3},{3,1},{4,6},{6,4},{5,7},{7,5},{8,10},{10,8},{9,1... | collective-permute-start | bytes 589832 | tf_op jit(solution)/shard_map/ppermute | solution.py:107
  159.1 14.9 %collective-permute-start.33 = (bf16[2,64,768]{2,1,0:T(8,128)(2,1)S(1)}, bf16[2,64,768]{2,1,0:T(8,128)(2,1)S(1)}, u32[]{:S(2)}, u32[]{:S(2)}) collective-permute-start(bf16[2,64,768]{2,1,0:T(8,128)(2,1)S(1)} %get-tuple-element.51), channel_id=1, source_target_pairs={{0,8},{4,12},{8,0},{12,4},{1,9},{5,13},{9,1},{13,5},{2,10},{6,14},... | collective-permute-start | bytes 589832 | tf_op jit(solution)/shard_map/ppermute | solution.py:107
  159.1 20.1 %collective-permute-start.34 = (bf16[2,64,768]{2,1,0:T(8,128)(2,1)S(1)}, bf16[2,64,768]{2,1,0:T(8,128)(2,1)S(1)}, u32[]{:S(2)}, u32[]{:S(2)}) collective-permute-start(bf16[2,64,768]{2,1,0:T(8,128)(2,1)S(1)} %get-tuple-element.52), channel_id=1, source_target_pairs={{0,10},{2,8},{4,14},{6,12},{8,2},{10,0},{12,6},{14,4},{1,11},{3,9}... | collective-permute-start | bytes 589832 | tf_op jit(solution)/shard_map/ppermute | solution.py:412
  (2 other events, 2.1 us)

commit v10 on v9

--- a/solution.py
+++ b/solution.py
@@ -127,30 +127,21 @@
     )(*prefetch, *operands)
 
 
-def assemble(place, near, inward, outward):
-    count, width = near[0][0].shape
-    pieces = [x for pair in near + inward + outward for x in pair]
+def assemble(place, mine, theirs, count):
+    width, rows = mine[0].shape[1], len(mine)
 
     def kernel(place_ref, *refs):
         row, frame = place_ref[0], place_ref[2]
-        out_ref = refs[-1]
-
-        def put(first, steps):
-            for i, s in enumerate(steps):
-                for f in range(2):
-                    out_ref[row ^ s, (frame + f) % 2] = refs[2 * (first + i) + f][...]
-
-        middle = (row == 1) | (row == 2)
-        put(0, (0, 1))
-        pl.when(middle)(lambda: put(2, (3, 2)))
-        pl.when(jnp.logical_not(middle))(lambda: put(4, (2, 3)))
+        for s in range(rows):
+            refs[-1][row ^ s, frame] = refs[s][:count]
+            refs[-1][row ^ s, 1 - frame] = refs[rows + s][:count]
 
     return call(
         kernel,
-        jax.ShapeDtypeStruct((4, 2, count, width), jnp.bfloat16),
+        jax.ShapeDtypeStruct((rows, 2, count, width), jnp.bfloat16),
         [place],
-        pieces,
-        read=40 * count * width,
+        [*mine, *theirs],
+        read=8 * rows * count * width,
         limit=WHOLE_VMEM_BYTES,
     )
 
@@ -197,8 +188,9 @@
         [place],
         [tokens, *flat],
         scratch=[pltpu.VMEM((rows, 2, count, cols), jnp.float32)],
-        flops=flops,
+        flops=8 * flops,
         read=flops // 300,
+        limit=WHOLE_VMEM_BYTES,
     )
 
 
@@ -256,6 +248,7 @@
         ],
         flops=4 * blocks * block_len * MAXB * block_len * cols,
         read=16 * blocks * block_len * cols,
+        limit=WHOLE_VMEM_BYTES,
     )
 
 
@@ -329,21 +322,12 @@
     rows_n, heads_n = lax.axis_size("rows"), lax.axis_size("heads")
     group, row = lax.axis_index("groups"), lax.axis_index("rows")
     frame, core = lax.axis_index("frames"), lax.axis_index("heads")
+    count = latents.shape[1]
     depth, _, local_cols = w_qkv.shape
     span = rows_n // heads_n
     cols = local_cols // span
     half = depth // 2
     place = jnp.stack([row, group, frame, core]).astype(jnp.int32)
-
-    def over_frames(value, rows):
-        pairs = [(2 * r + f, 2 * r + 1 - f) for r in rows for f in range(2)]
-        return lax.ppermute(value, ("rows", "frames"), pairs)
-
-    def inward(value):
-        return lax.ppermute(value, "rows", [(1, 2), (2, 1)])
-
-    def outward(value):
-        return lax.ppermute(value, "rows", [(1, 0), (2, 3)])
 
     last = cols // (3 * HD) * HD
 
@@ -360,50 +344,49 @@
         ]
         return lax.ppermute(after(value, *others) if others else value, ("rows", "heads"), pairs)
 
+    tables = jnp.concatenate([win_blocks, win_counts[:, None], block_window[:, None]], axis=1)
+    tables = jnp.pad(tables, ((0, 6), (0, span * depth - MAXB - 2))).astype(latents.dtype)
     mine = lax.dynamic_slice_in_dim(latents[0], core * span * depth, span * depth, axis=1)
-    in_1, near, mine_x = inward(mine), swap(mine, "rows"), swap(mine, "frames")
+    mine = jnp.concatenate([mine, tables], axis=0)
+
+    near, mine_x = swap(mine, "rows"), swap(mine, "frames")
     here, there = [reshard(0)], []
     near_x = swap(near, "frames")
-    out_1, in_1x = outward(in_1), over_frames(in_1, (1, 2))
-    here.append(reshard(1, in_1, near))
+    across = swap(after(w_out, near), "heads")
+    here.append(reshard(1, near, mine_x))
     there.append(swap(here[0], "groups"))
-    across = swap(after(w_out, near), "heads")
-    in_2 = inward(after(near, here[0]))
-    out_1x = over_frames(out_1, (0, 3))
-    here.append(reshard(2, here[1], there[0], mine_x, near_x, in_1x, out_1, across))
+    far_2 = swap(after(mine, here[0]), "rows", 2)
     there.append(swap(here[1], "groups"))
-    out_2, in_2x = outward(in_2), over_frames(in_2, (1, 2))
-    here.append(reshard(3, here[1], there[1], in_2, in_2x, out_1x))
+    far_3 = swap(after(mine, here[1], near_x), "rows", 3)
+    far_2x = swap(far_2, "frames")
+    out_half = lax.dynamic_slice_in_dim(w_out, group * cols, cols, axis=0)
+    beside = [swap(after(out_half, here[0]), "rows")]
+    beside.append(swap(beside[0], "groups"))
+    here.append(reshard(2, far_2, there[0], there[1], across, beside[0]))
+    far_3x = swap(far_3, "frames")
+    here.append(reshard(3, far_3, far_2x, beside[1]))
     there += [swap(here[2], "groups"), swap(here[3], "groups")]
-    out_2x = over_frames(out_2, (0, 3))
-    tokens = assemble(
-        place, [(mine, mine_x), (near, near_x)], [(in_1, in_1x), (in_2, in_2x)], [(out_1, out_1x), (out_2, out_2x)]
-    )
-
-    tables = jnp.concatenate([win_blocks, win_counts[:, None], block_window[:, None]], axis=1)
-    tables = after(tables, there[2])
-    found = [tables] + [swap(tables, "rows", s) for s in range(1, rows_n)]
-    tables = jnp.stack(found)[row ^ jnp.arange(rows_n)].reshape(rows_n * heads_n, MAXB + 2)
+    pieces = [mine, near, far_2, far_3]
+    tokens = assemble(place, pieces, [mine_x, near_x, far_2x, far_3x], count)
+
+    found = jnp.stack([x[count : count + heads_n, : MAXB + 2] for x in pieces]).astype(jnp.int32)
+    tables = found[row ^ jnp.arange(rows_n)].reshape(rows_n * heads_n, MAXB + 2)
     windows = lax.dynamic_index_in_dim(
         tables[:, MAXB + 1].reshape(rows_n, heads_n), core, axis=1, keepdims=False
     )
     picked = tables[windows]
     members, counts = picked[:, :MAXB].reshape(-1), picked[:, MAXB]
 
-    out_half = lax.dynamic_slice_in_dim(w_out, group * cols, cols, axis=0)
-    beside = [swap(after(out_half, here[2]), "rows")]
-    beside.append(swap(beside[0], "groups"))
-
-    chunks = [(here[0], there[0]), (here[1], after(there[1], there[2], there[3], members, counts))]
+    chunks = [(here[0], there[0]), (here[1], after(there[1], there[2], here[3]))]
     first = project(place, tokens, chunks)
     first_more = swap(first[2], "heads")
-    second = project(place, tokens, [(here[2], there[2]), (here[3], after(there[3], first[2], beside[0]))])
+    second = project(place, tokens, [(here[2], there[2]), (here[3], after(there[3], first[2]))])
     second_more = swap(second[2], "heads")
     attended = attend_all(place, members, counts, *first[:2], first_more)
     same, diff = attend_all(place, members, counts, *second[:2], second_more, attended)
     attended = [same] + [swap(same if s % 2 == 0 else diff, "rows", s) for s in range(1, rows_n)]
     halves = [w_out[:cols], w_out[cols:], *beside]
-    beside_across = [swap(part, "heads") for part in (beside[0], after(beside[1], attended[1]))]
+    beside_across = [swap(part, "heads") for part in beside]
     keep, over_x, over_z, over_both = mix(
         place, attended, [*halves, across[:cols], across[cols:], *beside_across]
     )

time: 181 us -> 183 us (1.011)
  Pallas kernels: 22.7 us -> 35.4 us
  waiting for transfers between devices: 86.4 us -> 77.6 us
  local copies, waits for them, and re-layouts: 15.2 us -> 11.8 us
  other arithmetic: 0.96 us -> 3.97 us
    ppermute x8 -> x0, waiting for transfers between devices: 24.8 us -> none  [the longest x2 19.6 us: outward(): return lax.ppermute(value, 'rows', [(1, 0), (2, 3)])]
    ppermute x8 -> x0, starting transfers between devices: 15 us -> none  [the longest x4 9.65 us: over_frames(): return lax.ppermute(value, ('rows', 'frames'), pairs)]
    ppermute x22 -> x23, starting transfers between devices: 21.6 us -> 34.9 us  [swap(): return lax.ppermute(value, axis, [(i, i ^ step) for i in range(peers)])]
    pallas_call x7, Pallas kernels: 22.7 us -> 35.4 us  [call(): pl.pallas_call(kernel, out_shape=out_shape, grid_spec=pltpu.PrefetchScala...]
    ppermute x22 -> x23, waiting for transfers between devices: 51.5 us -> 60.4 us  [swap(): return lax.ppermute(value, axis, [(i, i ^ step) for i in range(peers)])]
    ppermute x4, waiting for transfers between devices: 4.82 us -> 13.3 us  [reshard(): lax.ppermute(after(value, *others) if others else value, ('rows', 'heads'...]
    unnamed x30 -> x26, local copies, waits for them, and re-layouts: 6.25 us -> 1.55 us
    another operation x0 -> x3, local copies, waits for them, and re-layouts: none -> 1.98 us  [by_heads(): jnp.stack([x[count:count + heads_n, :MAXB + 2] for x in pieces])]
  transfers between devices with their start and end apart: 35 -> 28, of which waited for: 11 -> 11; matrix products, arithmetic and copies ran while one was open for 5% -> 6% of each run, Pallas kernels for 10% -> 17%
where the time goes in v10:
time: 183 us
  waiting for transfers between devices  77.6 us (42%)
  starting transfers between devices  53.6 us (29%)
  Pallas kernels  35.4 us (19%)
  local copies, waits for them, and re-layouts  11.8 us (6%)
  other arithmetic  3.97 us (2%)
    ppermute x23, waiting for transfers between devices, swap(): return lax.ppermute(value, axis, [(i, i ^ step) for i in range(peers)])  60.4 us
    pallas_call x7, Pallas kernels, call(): pl.pallas_call(kernel, out_shape=out_shape, grid_spec=pltpu.PrefetchScala...  35.4 us
    ppermute x23, starting transfers between devices, swap(): return lax.ppermute(value, axis, [(i, i ^ step) for i in range(peers)])  34.9 us
    ppermute x4, starting transfers between devices, reshard(): lax.ppermute(after(value, *others) if others else value, ('rows', 'heads'...  16.1 us
    ppermute x4, waiting for transfers between devices, reshard(): lax.ppermute(after(value, *others) if others else value, ('rows', 'heads'...  13.3 us
    ppermute x1, waiting for transfers between devices, by_heads(): lax.ppermute(over_both, ('rows', 'frames'), [(2 * r + f, 2 * (r ^ 2) + 1...  3.92 us
  transfers between devices with their start and end apart: 28, of which 11 were waited for; matrix products, arithmetic and copies ran while one was open for 6% of the time, Pallas kernels for 17%

profile of v10, /device:TPU:0, one launch (start us, length us, event | category | flops | bytes accessed | tf_op | source)
XLA Modules:
  0.0 182.6 jit_solution(11996624228694454350)
XLA Ops:
  0.0 0.7 convert_bitcast_fusion
  0.8 0.7 convert_bitcast_fusion.1
  1.6 0.7 convert.13
  2.4 0.8 fusion.1.refs_0_
  3.2 3.0 %collective-permute-start = (bf16[136,1536]{1,0:T(8,128)(2,1)}, bf16[136,1536]{1,0:T(8,128)(2,1)S(1)}, u32[]{:S(2)}, u32[]{:S(2)}) collective-permute-start(bf16[136,1536]{1,0:T(8,128)(2,1)} %fusion.1.refs_0_), channel_id=1, source_target_pairs={{0,4},{4,0},{8,12},{12,8},{1,5},{5,1},{9,13},{13,9},{2,6},{6,2},{1... | collective-permute-start | bytes 1253384 | tf_op jit(solution)/shard_map/ppermute | solution.py:107
  6.2 1.5 collective-permute-start.3
  7.7 1.3 dynamic-slice_bitcast_fusion.1
  9.1 1.5 collective-permute-start.1
  10.5 8.8 %collective-permute-done.refs_1_ = bf16[136,1536]{1,0:T(8,128)(2,1)S(1)} collective-permute-done((bf16[136,1536]{1,0:T(8,128)(2,1)}, bf16[136,1536]{1,0:T(8,128)(2,1)S(1)}, u32[]{:S(2)}, u32[]{:S(2)}) %collective-permute-start) | collective-permute-done | bytes 417824 | tf_op jit(solution)/shard_map/ppermute | solution.py:107
  19.4 3.0 %collective-permute-start.11 = (bf16[768,768]{1,0:T(8,128)(2,1)}, bf16[768,768]{1,0:T(8,128)(2,1)}, u32[]{:S(2)}, u32[]{:S(2)}) collective-permute-start(bf16[768,768]{1,0:T(8,128)(2,1)} %param.8), channel_id=1, source_target_pairs={{0,1},{1,0},{2,3},{3,2},{4,5},{5,4},{6,7},{7,6},{8,9},{9,8},{10,11... | collective-permute-start | bytes 3538952 | tf_op jit(solution)/shard_map/ppermute | solution.py:107
  22.4 2.5 %collective-permute-start.5 = (bf16[136,1536]{1,0:T(8,128)(2,1)S(1)}, bf16[136,1536]{1,0:T(8,128)(2,1)S(1)}, u32[]{:S(2)}, u32[]{:S(2)}) collective-permute-start(bf16[136,1536]{1,0:T(8,128)(2,1)S(1)} %collective-permute-done.refs_1_), channel_id=1, source_target_pairs={{0,2},{2,0},{1,3},{3,1},{4,6},{6,4},{5,7},{7,5},{8,10},{10,8},{9,1... | collective-permute-start | bytes 1253384 | tf_op jit(solution)/shard_map/ppermute | solution.py:107
  24.8 1.6 fusion.5
  26.5 1.5 collective-permute-start.9
  28.1 13.3 %collective-permute-done.4.refs_2_ = bf16[3,384,256]{2,1,0:T(8,128)(2,1)} collective-permute-done((bf16[3,384,256]{2,1,0:T(8,128)(2,1)S(1)}, bf16[3,384,256]{2,1,0:T(8,128)(2,1)}, u32[]{:S(2)}, u32[]{:S(2)}) %collective-permute-start.4) | collective-permute-done | bytes 589856 | tf_op jit(solution)/shard_map/ppermute | solution.py:345
  41.4 1.7 collective-permute-start.10
  43.4 13.0 %collective-permute-done.12.refs_6_ = bf16[384,768]{1,0:T(8,128)(2,1)S(1)} collective-permute-done((bf16[384,768]{1,0:T(8,128)(2,1)S(1)}, bf16[384,768]{1,0:T(8,128)(2,1)S(1)}, u32[]{:S(2)}, u32[]{:S(2)}) %collective-permute-start.12) | collective-permute-done | bytes 589856 | tf_op jit(solution)/shard_map/ppermute | solution.py:107
  56.5 2.6 %collective-permute-start.15 = (bf16[384,768]{1,0:T(8,128)(2,1)S(1)}, bf16[384,768]{1,0:T(8,128)(2,1)S(1)}, u32[]{:S(2)}, u32[]{:S(2)}) collective-permute-start(bf16[384,768]{1,0:T(8,128)(2,1)S(1)} %collective-permute-done.12.refs_6_), channel_id=1, source_target_pairs={{0,16},{16,0},{1,17},{17,1},{2,18},{18,2},{3,19},{19,3},{4,20},{20... | collective-permute-start | bytes 1769480 | tf_op jit(solution)/shard_map/ppermute | solution.py:107
  59.2 3.4 %collective-permute-done.2.refs_2_ = bf16[136,1536]{1,0:T(8,128)(2,1)} collective-permute-done((bf16[136,1536]{1,0:T(8,128)(2,1)}, bf16[136,1536]{1,0:T(8,128)(2,1)}, u32[]{:S(2)}, u32[]{:S(2)}) %collective-permute-start.2) | collective-permute-done | bytes 417824 | tf_op jit(solution)/shard_map/ppermute | solution.py:107
  62.6 0.7 collective-permute-start.6
  63.3 2.6 %collective-permute-start.7 = (bf16[136,1536]{1,0:T(8,128)(2,1)}, bf16[136,1536]{1,0:T(8,128)(2,1)S(1)}, u32[]{:S(2)}, u32[]{:S(2)}) collective-permute-start(bf16[136,1536]{1,0:T(8,128)(2,1)} %collective-permute-done.2.refs_2_), channel_id=1, source_target_pairs={{0,2},{2,0},{1,3},{3,1},{4,6},{6,4},{5,7},{7,5},{8,10},{10,8},{9,1... | collective-permute-start | bytes 1253384 | tf_op jit(solution)/shard_map/ppermute | solution.py:107
  65.9 1.1 dynamic-slice_bitcast_fusion.3
  67.1 0.7 collective-permute-start.13
  68.4 6.2 %collective-permute-done.6.refs_3_ = bf16[136,1536]{1,0:T(8,128)(2,1)S(1)} collective-permute-done((bf16[136,1536]{1,0:T(8,128)(2,1)}, bf16[136,1536]{1,0:T(8,128)(2,1)S(1)}, u32[]{:S(2)}, u32[]{:S(2)}) %collective-permute-start.6) | collective-permute-done | bytes 417824 | tf_op jit(solution)/shard_map/ppermute | solution.py:107
  74.6 2.5 %collective-permute-start.8 = (bf16[136,1536]{1,0:T(8,128)(2,1)S(1)}, bf16[136,1536]{1,0:T(8,128)(2,1)S(1)}, u32[]{:S(2)}, u32[]{:S(2)}) collective-permute-start(bf16[136,1536]{1,0:T(8,128)(2,1)S(1)} %collective-permute-done.6.refs_3_), channel_id=1, source_target_pairs={{0,2},{2,0},{1,3},{3,1},{4,6},{6,4},{5,7},{7,5},{8,10},{10,8},{9,1... | collective-permute-start | bytes 1253384 | tf_op jit(solution)/shard_map/ppermute | solution.py:107
  77.1 13.8 %collective-permute-start.16 = (bf16[3,384,128]{2,1,0:T(8,128)(2,1)S(1)}, bf16[3,384,128]{2,1,0:T(8,128)(2,1)S(1)}, u32[]{:S(2)}, u32[]{:S(2)}) collective-permute-start(bf16[3,384,128]{2,1,0:T(8,128)(2,1)S(1)} %get-tuple-element.34), channel_id=1, source_target_pairs={{0,4},{1,12},{4,0},{5,8},{8,5},{9,13},{12,1},{13,9},{2,6},{3,14},{... | collective-permute-start | bytes 884744 | tf_op jit(solution)/shard_map/ppermute | solution.py:345
  92.1 0.7 slice_bitcast_fusion.1
  92.8 0.8 copy-done.8
  93.5 4.4 %shard_map.64.x_ref = bf16[4,2,128,1536]{3,2,1,0:T(8,128)(2,1)} custom-call(s32[4]{0:T(128)} %pad_add_fusion.place_ref, bf16[136,1536]{1,0:T(8,128)(2,1)} %fusion.1.refs_0_, bf16[136,1536]{1,0:T(8,128)(2,1)} %copy-done.3, bf16[136,1536]{1,0:T(8,128)(2,1)} %collective-permute-done.2.refs_2_, bf16[136,1536]{1,0:T(8,128)(2,1)} %copy-done.6, ...), custom_call_target="tpu_custom_call" | custom-call | bytes 6291456 | tf_op jit(solution)/shard_map/pallas_call | solution.py:115
  97.9 1.6 collective-permute-start.17
  100.0 8.5 %shard_map.65 = (f32[4,128,256]{2,1,0:T(8,128)}, f32[4,256,512]{2,1,0:T(8,128)}, bf16[4,320,512]{2,1,0:T(8,128)(2,1)}) custom-call(s32[4]{0:T(128)} %pad_add_fusion.place_ref, bf16[4,2,128,1536]{3,2,1,0:T(8,128)(2,1)} %shard_map.64.x_ref, bf16[3,384,256]{2,1,0:T(8,128)(2,1)} %collective-permute-done.1.refs_0_, ...), custom_call_target="tpu_custom_call" | custom-call | flops 19327352832 | bytes 8053063 | tf_op jit(solution)/shard_map/pallas_call | solution.py:115
  108.6 0.7 copy-done.12
  109.3 6.2 %shard_map.66 = (f32[4,128,128]{2,1,0:T(8,128)}, f32[4,256,256]{2,1,0:T(8,128)}, bf16[4,320,256]{2,1,0:T(8,128)(2,1)}) custom-call(s32[4]{0:T(128)} %pad_add_fusion.place_ref, bf16[4,2,128,1536]{3,2,1,0:T(8,128)(2,1)} %shard_map.64.x_ref, bf16[3,384,128]{2,1,0:T(8,128)(2,1)} %copy-done.9, bf16[3,384,128]{2,1,0:T(8,128)(2,1)} %copy-done.11, ...), custom_call_target="tpu_custom_call" | custom-call | flops 9663676416 | bytes 4026531 | tf_op jit(solution)/shard_map/pallas_call | solution.py:115
  116.0 0.7 slice_bitcast_fusion
  118.9 0.7 slice_reduce_fusion.1.counts_ref
  119.6 6.7 %shard_map.67 = (bf16[2,128,256]{2,1,0:T(8,128)(2,1)}, bf16[2,128,256]{2,1,0:T(8,128)(2,1)}) custom-call(s32[4]{0:T(128)} %pad_add_fusion.place_ref, s32[16]{0:T(128)} %reshape.24.members_ref, s32[4]{0:T(128)} %slice_reduce_fusion.1.counts_ref, f32[4,128,256]{2,1,0:T(8,128)} %get-tuple-element.41.q_ref, f32[4,256,512]{2,1,0:T(8,128)} %get-tuple-element.42.kv_ref, ...), custom_call_target="tpu_custom_call" | custom-call | flops 268435456 | bytes 2097152 | tf_op jit(solution)/shard_map/pallas_call | solution.py:115
  126.3 4.6 %shard_map.68 = (bf16[2,128,384]{2,1,0:T(8,128)(2,1)}, bf16[2,128,384]{2,1,0:T(8,128)(2,1)}) custom-call(s32[4]{0:T(128)} %pad_add_fusion.place_ref, s32[16]{0:T(128)} %reshape.24.members_ref, s32[4]{0:T(128)} %slice_reduce_fusion.1.counts_ref, f32[4,128,128]{2,1,0:T(8,128)} %get-tuple-element.38.q_ref, f32[4,256,256]{2,1,0:T(8,128)} %get-tuple-element.39.kv_ref, ...), custom_call_target="tpu_custom_call" | custom-call | flops 134217728 | bytes 1048576 | tf_op jit(solution)/shard_map/pallas_call | solution.py:115
  130.9 6.8 %collective-permute-start.20 = (bf16[2,128,384]{2,1,0:T(8,128)(2,1)}, bf16[2,128,384]{2,1,0:T(8,128)(2,1)S(1)}, u32[]{:S(2)}, u32[]{:S(2)}) collective-permute-start(bf16[2,128,384]{2,1,0:T(8,128)(2,1)} %get-tuple-element.46), channel_id=1, source_target_pairs={{0,4},{4,0},{8,12},{12,8},{1,5},{5,1},{9,13},{13,9},{2,6},{6,2},{1... | collective-permute-start | bytes 589832 | tf_op jit(solution)/shard_map/ppermute | solution.py:107
  137.7 1.4 collective-permute-start.22
  139.3 1.3 fusion.4
  140.6 2.9 %collective-permute-done.20.refs_1_ = bf16[2,128,384]{2,1,0:T(8,128)(2,1)S(1)} collective-permute-done((bf16[2,128,384]{2,1,0:T(8,128)(2,1)}, bf16[2,128,384]{2,1,0:T(8,128)(2,1)S(1)}, u32[]{:S(2)}, u32[]{:S(2)}) %collective-permute-start.20) | collective-permute-done | bytes 196640 | tf_op jit(solution)/shard_map/ppermute | solution.py:107
  143.5 13.9 %collective-permute-done.21.refs_2_ = bf16[2,128,384]{2,1,0:T(8,128)(2,1)S(1)} collective-permute-done((bf16[2,128,384]{2,1,0:T(8,128)(2,1)}, bf16[2,128,384]{2,1,0:T(8,128)(2,1)S(1)}, u32[]{:S(2)}, u32[]{:S(2)}) %collective-permute-start.21) | collective-permute-done | bytes 196640 | tf_op jit(solution)/shard_map/ppermute | solution.py:107
  157.4 3.7 %shard_map.69 = (f32[2,64,768]{2,1,0:T(8,128)S(1)}, bf16[2,64,768]{2,1,0:T(8,128)(2,1)S(1)}, bf16[2,64,768]{2,1,0:T(8,128)(2,1)S(1)}, bf16[2,64,768]{2,1,0:T(8,128)(2,1)S(1)}) custom-call(s32[4]{0:T(128)S(1)} %copy-done.2, bf16[2,128,384]{2,1,0:T(8,128)(2,1)S(1)} %copy-done.1, bf16[2,128,384]{2,1,0:T(8,128)(2,1)S(1)} %collective-permute-done.20.refs_1_, ...), custom_call_target="tpu_custom_call" | custom-call | flops 1207959552 | bytes 4718592 | tf_op jit(solution)/shard_map/pallas_call | solution.py:115
  161.1 1.8 collective-permute-start.25
  162.9 2.6 %collective-permute-start.27 = (bf16[2,64,768]{2,1,0:T(8,128)(2,1)S(1)}, bf16[2,64,768]{2,1,0:T(8,128)(2,1)S(1)}, u32[]{:S(2)}, u32[]{:S(2)}) collective-permute-start(bf16[2,64,768]{2,1,0:T(8,128)(2,1)S(1)} %get-tuple-element.50), channel_id=1, source_target_pairs={{0,10},{2,8},{4,14},{6,12},{8,2},{10,0},{12,6},{14,4},{1,11},{3,9}... | collective-permute-start | bytes 589832 | tf_op jit(solution)/shard_map/ppermute | solution.py:395
  165.5 2.1 %collective-permute-done.25.x_ref = bf16[2,64,768]{2,1,0:T(8,128)(2,1)S(1)} collective-permute-done((bf16[2,64,768]{2,1,0:T(8,128)(2,1)S(1)}, bf16[2,64,768]{2,1,0:T(8,128)(2,1)S(1)}, u32[]{:S(2)}, u32[]{:S(2)}) %collective-permute-start.25) | collective-permute-done | bytes 196640 | tf_op jit(solution)/shard_map/ppermute | solution.py:107
  167.7 9.6 %collective-permute-done.26.z_ref = bf16[2,64,768]{2,1,0:T(8,128)(2,1)S(1)} collective-permute-done((bf16[2,64,768]{2,1,0:T(8,128)(2,1)S(1)}, bf16[2,64,768]{2,1,0:T(8,128)(2,1)S(1)}, u32[]{:S(2)}, u32[]{:S(2)}) %collective-permute-start.26) | collective-permute-done | bytes 196640 | tf_op jit(solution)/shard_map/ppermute | solution.py:107
  177.3 3.9 %collective-permute-done.27.both_ref = bf16[2,64,768]{2,1,0:T(8,128)(2,1)S(1)} collective-permute-done((bf16[2,64,768]{2,1,0:T(8,128)(2,1)S(1)}, bf16[2,64,768]{2,1,0:T(8,128)(2,1)S(1)}, u32[]{:S(2)}, u32[]{:S(2)}) %collective-permute-start.27) | collective-permute-done | bytes 196640 | tf_op jit(solution)/shard_map/ppermute | solution.py:395
  181.2 1.4 shard_map.70
  (69 shorter events, 6.4 us)
Async XLA Ops:
  0.0 2.3 %copy-start = (bf16[1,128,3072]{2,1,0:T(8,128)(2,1)S(1)}, bf16[1,128,3072]{2,1,0:T(8,128)(2,1)}, u32[]{:S(2)}) copy-start(bf16[1,128,3072]{2,1,0:T(8,128)(2,1)} %param.6) | copy-start | bytes 2359300
  3.2 16.1 %collective-permute-start = (bf16[136,1536]{1,0:T(8,128)(2,1)}, bf16[136,1536]{1,0:T(8,128)(2,1)S(1)}, u32[]{:S(2)}, u32[]{:S(2)}) collective-permute-start(bf16[136,1536]{1,0:T(8,128)(2,1)} %fusion.1.refs_0_), channel_id=1, source_target_pairs={{0,4},{4,0},{8,12},{12,8},{1,5},{5,1},{9,13},{13,9},{2,6},{6,2},{1... | collective-permute-start | bytes 1253384 | tf_op jit(solution)/shard_map/ppermute | solution.py:107
  6.2 13.1 %collective-permute-start.3 = (bf16[136,1536]{1,0:T(8,128)(2,1)}, bf16[136,1536]{1,0:T(8,128)(2,1)S(1)}, u32[]{:S(2)}, u32[]{:S(2)}) collective-permute-start(bf16[136,1536]{1,0:T(8,128)(2,1)} %fusion.1.refs_0_), channel_id=1, source_target_pairs={{0,2},{2,0},{1,3},{3,1},{4,6},{6,4},{5,7},{7,5},{8,10},{10,8},{9,1... | collective-permute-start | bytes 1253384 | tf_op jit(solution)/shard_map/ppermute | solution.py:107
  9.1 17.4 %collective-permute-start.1 = (bf16[3,384,256]{2,1,0:T(8,128)(2,1)S(1)}, bf16[3,384,256]{2,1,0:T(8,128)(2,1)}, u32[]{:S(2)}, u32[]{:S(2)}) collective-permute-start(bf16[3,384,256]{2,1,0:T(8,128)(2,1)S(1)} %get-tuple-element.53), channel_id=1, source_target_pairs={{0,0},{1,8},{4,4},{5,12},{8,1},{9,9},{12,5},{13,13},{2,2},{3,10},{... | collective-permute-start | bytes 1769480 | tf_op jit(solution)/shard_map/ppermute | solution.py:345
  19.3 7.1 %copy-start.3 = (bf16[136,1536]{1,0:T(8,128)(2,1)}, bf16[136,1536]{1,0:T(8,128)(2,1)S(1)}, u32[]{:S(2)}) copy-start(bf16[136,1536]{1,0:T(8,128)(2,1)S(1)} %collective-permute-done.refs_1_) | copy-start | bytes 1253380
  19.3 3.1 %copy-start.4 = (bf16[136,1536]{1,0:T(8,128)(2,1)}, bf16[136,1536]{1,0:T(8,128)(2,1)S(1)}, u32[]{:S(2)}) copy-start(bf16[136,1536]{1,0:T(8,128)(2,1)S(1)} %collective-permute-done.3.refs_4_) | copy-start | bytes 1253380
  19.3 22.1 %collective-permute-start.4 = (bf16[3,384,256]{2,1,0:T(8,128)(2,1)S(1)}, bf16[3,384,256]{2,1,0:T(8,128)(2,1)}, u32[]{:S(2)}, u32[]{:S(2)}) collective-permute-start(bf16[3,384,256]{2,1,0:T(8,128)(2,1)S(1)} %get-tuple-element.29), channel_id=1, source_target_pairs={{0,4},{1,12},{4,0},{5,8},{8,5},{9,13},{12,1},{13,9},{2,6},{3,14},{... | collective-permute-start | bytes 1769480 | tf_op jit(solution)/shard_map/ppermute | solution.py:345
  19.4 47.7 %collective-permute-start.11 = (bf16[768,768]{1,0:T(8,128)(2,1)}, bf16[768,768]{1,0:T(8,128)(2,1)}, u32[]{:S(2)}, u32[]{:S(2)}) collective-permute-start(bf16[768,768]{1,0:T(8,128)(2,1)} %param.8), channel_id=1, source_target_pairs={{0,1},{1,0},{2,3},{3,2},{4,5},{5,4},{6,7},{7,6},{8,9},{9,8},{10,11... | collective-permute-start | bytes 3538952 | tf_op jit(solution)/shard_map/ppermute | solution.py:107
  22.4 20.7 %collective-permute-start.5 = (bf16[136,1536]{1,0:T(8,128)(2,1)S(1)}, bf16[136,1536]{1,0:T(8,128)(2,1)S(1)}, u32[]{:S(2)}, u32[]{:S(2)}) collective-permute-start(bf16[136,1536]{1,0:T(8,128)(2,1)S(1)} %collective-permute-done.refs_1_), channel_id=1, source_target_pairs={{0,2},{2,0},{1,3},{3,1},{4,6},{6,4},{5,7},{7,5},{8,10},{10,8},{9,1... | collective-permute-start | bytes 1253384 | tf_op jit(solution)/shard_map/ppermute | solution.py:107
  26.5 30.0 %collective-permute-start.12 = (bf16[384,768]{1,0:T(8,128)(2,1)S(1)}, bf16[384,768]{1,0:T(8,128)(2,1)S(1)}, u32[]{:S(2)}, u32[]{:S(2)}) collective-permute-start(bf16[384,768]{1,0:T(8,128)(2,1)S(1)} %get-tuple-element.32), channel_id=1, source_target_pairs={{0,4},{4,0},{8,12},{12,8},{1,5},{5,1},{9,13},{13,9},{2,6},{6,2},{1... | collective-permute-start | bytes 1769480 | tf_op jit(solution)/shard_map/ppermute | solution.py:107
  26.5 36.8 %collective-permute-start.9 = (bf16[3,384,256]{2,1,0:T(8,128)(2,1)}, bf16[3,384,256]{2,1,0:T(8,128)(2,1)}, u32[]{:S(2)}, u32[]{:S(2)}) collective-permute-start(bf16[3,384,256]{2,1,0:T(8,128)(2,1)} %collective-permute-done.1.refs_0_), channel_id=1, source_target_pairs={{0,16},{16,0},{1,17},{17,1},{2,18},{18,2},{3,19},{19,3},{4,20},{20... | collective-permute-start | bytes 1769480 | tf_op jit(solution)/shard_map/ppermute | solution.py:107
  41.4 25.7 %collective-permute-start.10 = (bf16[3,384,256]{2,1,0:T(8,128)(2,1)}, bf16[3,384,256]{2,1,0:T(8,128)(2,1)}, u32[]{:S(2)}, u32[]{:S(2)}) collective-permute-start(bf16[3,384,256]{2,1,0:T(8,128)(2,1)} %collective-permute-done.4.refs_2_), channel_id=1, source_target_pairs={{0,16},{16,0},{1,17},{17,1},{2,18},{18,2},{3,19},{19,3},{4,20},{20... | collective-permute-start | bytes 1769480 | tf_op jit(solution)/shard_map/ppermute | solution.py:107
  43.1 13.4 %copy-start.5 = (bf16[136,1536]{1,0:T(8,128)(2,1)}, bf16[136,1536]{1,0:T(8,128)(2,1)S(1)}, u32[]{:S(2)}) copy-start(bf16[136,1536]{1,0:T(8,128)(2,1)S(1)} %collective-permute-done.5.refs_5_) | copy-start | bytes 1253380
  43.1 19.5 %collective-permute-start.2 = (bf16[136,1536]{1,0:T(8,128)(2,1)}, bf16[136,1536]{1,0:T(8,128)(2,1)}, u32[]{:S(2)}, u32[]{:S(2)}) collective-permute-start(bf16[136,1536]{1,0:T(8,128)(2,1)} %fusion.1.refs_0_), channel_id=1, source_target_pairs={{0,8},{4,12},{8,0},{12,4},{1,9},{5,13},{9,1},{13,5},{2,10},{6,14},... | collective-permute-start | bytes 1253384 | tf_op jit(solution)/shard_map/ppermute | solution.py:107
  56.5 20.6 %collective-permute-start.15 = (bf16[384,768]{1,0:T(8,128)(2,1)S(1)}, bf16[384,768]{1,0:T(8,128)(2,1)S(1)}, u32[]{:S(2)}, u32[]{:S(2)}) collective-permute-start(bf16[384,768]{1,0:T(8,128)(2,1)S(1)} %collective-permute-done.12.refs_6_), channel_id=1, source_target_pairs={{0,16},{16,0},{1,17},{17,1},{2,18},{18,2},{3,19},{19,3},{4,20},{20... | collective-permute-start | bytes 1769480 | tf_op jit(solution)/shard_map/ppermute | solution.py:107
  62.6 12.0 %collective-permute-start.6 = (bf16[136,1536]{1,0:T(8,128)(2,1)}, bf16[136,1536]{1,0:T(8,128)(2,1)S(1)}, u32[]{:S(2)}, u32[]{:S(2)}) collective-permute-start(bf16[136,1536]{1,0:T(8,128)(2,1)} %fusion.1.refs_0_), channel_id=1, source_target_pairs={{0,12},{4,8},{8,4},{12,0},{1,13},{5,9},{9,5},{13,1},{2,14},{6,10},... | collective-permute-start | bytes 1253384 | tf_op jit(solution)/shard_map/ppermute | solution.py:107
  63.3 13.7 %collective-permute-start.7 = (bf16[136,1536]{1,0:T(8,128)(2,1)}, bf16[136,1536]{1,0:T(8,128)(2,1)S(1)}, u32[]{:S(2)}, u32[]{:S(2)}) collective-permute-start(bf16[136,1536]{1,0:T(8,128)(2,1)} %collective-permute-done.2.refs_2_), channel_id=1, source_target_pairs={{0,2},{2,0},{1,3},{3,1},{4,6},{6,4},{5,7},{7,5},{8,10},{10,8},{9,1... | collective-permute-start | bytes 1253384 | tf_op jit(solution)/shard_map/ppermute | solution.py:107
  67.1 23.9 %collective-permute-start.13 = (bf16[3,384,128]{2,1,0:T(8,128)(2,1)S(1)}, bf16[3,384,128]{2,1,0:T(8,128)(2,1)S(1)}, u32[]{:S(2)}, u32[]{:S(2)}) collective-permute-start(bf16[3,384,128]{2,1,0:T(8,128)(2,1)S(1)} %get-tuple-element.33), channel_id=1, source_target_pairs={{0,0},{1,8},{4,4},{5,12},{8,1},{9,9},{12,5},{13,13},{2,2},{3,10},{... | collective-permute-start | bytes 884744 | tf_op jit(solution)/shard_map/ppermute | solution.py:345
  74.6 18.1 %copy-start.6 = (bf16[136,1536]{1,0:T(8,128)(2,1)}, bf16[136,1536]{1,0:T(8,128)(2,1)S(1)}, u32[]{:S(2)}) copy-start(bf16[136,1536]{1,0:T(8,128)(2,1)S(1)} %collective-permute-done.6.refs_3_) | copy-start | bytes 1253380
  74.6 18.1 %collective-permute-start.8 = (bf16[136,1536]{1,0:T(8,128)(2,1)S(1)}, bf16[136,1536]{1,0:T(8,128)(2,1)S(1)}, u32[]{:S(2)}, u32[]{:S(2)}) collective-permute-start(bf16[136,1536]{1,0:T(8,128)(2,1)S(1)} %collective-permute-done.6.refs_3_), channel_id=1, source_target_pairs={{0,2},{2,0},{1,3},{3,1},{4,6},{6,4},{5,7},{7,5},{8,10},{10,8},{9,1... | collective-permute-start | bytes 1253384 | tf_op jit(solution)/shard_map/ppermute | solution.py:107
  77.1 15.7 %copy-start.7 = (bf16[136,1536]{1,0:T(8,128)(2,1)}, bf16[136,1536]{1,0:T(8,128)(2,1)S(1)}, u32[]{:S(2)}) copy-start(bf16[136,1536]{1,0:T(8,128)(2,1)S(1)} %collective-permute-done.7.refs_6_) | copy-start | bytes 1253380
  77.1 20.9 %collective-permute-start.16 = (bf16[3,384,128]{2,1,0:T(8,128)(2,1)S(1)}, bf16[3,384,128]{2,1,0:T(8,128)(2,1)S(1)}, u32[]{:S(2)}, u32[]{:S(2)}) collective-permute-start(bf16[3,384,128]{2,1,0:T(8,128)(2,1)S(1)} %get-tuple-element.34), channel_id=1, source_target_pairs={{0,4},{1,12},{4,0},{5,8},{8,5},{9,13},{12,1},{13,9},{2,6},{3,14},{... | collective-permute-start | bytes 884744 | tf_op jit(solution)/shard_map/ppermute | solution.py:345
  90.9 17.6 %copy-start.9 = (bf16[3,384,128]{2,1,0:T(8,128)(2,1)}, bf16[3,384,128]{2,1,0:T(8,128)(2,1)S(1)}, u32[]{:S(2)}) copy-start(bf16[3,384,128]{2,1,0:T(8,128)(2,1)S(1)} %collective-permute-done.13.refs_0_) | copy-start | bytes 884740
  90.9 9.1 %collective-permute-start.14 = (bf16[3,384,128]{2,1,0:T(8,128)(2,1)S(1)}, bf16[3,384,128]{2,1,0:T(8,128)(2,1)S(1)}, u32[]{:S(2)}, u32[]{:S(2)}) collective-permute-start(bf16[3,384,128]{2,1,0:T(8,128)(2,1)S(1)} %collective-permute-done.13.refs_0_), channel_id=1, source_target_pairs={{0,16},{16,0},{1,17},{17,1},{2,18},{18,2},{3,19},{19,3},{4,20},{20... | collective-permute-start | bytes 884744 | tf_op jit(solution)/shard_map/ppermute | solution.py:107
  92.7 47.8 %collective-permute-start.23 = (bf16[384,768]{1,0:T(8,128)(2,1)S(1)}, bf16[384,768]{1,0:T(8,128)(2,1)}, u32[]{:S(2)}, u32[]{:S(2)}) collective-permute-start(bf16[384,768]{1,0:T(8,128)(2,1)S(1)} %collective-permute-done.12.refs_6_), channel_id=1, source_target_pairs={{0,1},{1,0},{2,3},{3,2},{4,5},{5,4},{6,7},{7,6},{8,9},{9,8},{10,11... | collective-permute-start | bytes 1769480 | tf_op jit(solution)/shard_map/ppermute | solution.py:107
  92.8 0.8 copy-start.8
  97.9 10.5 %copy-start.10 = (bf16[3,384,128]{2,1,0:T(8,128)(2,1)}, bf16[3,384,128]{2,1,0:T(8,128)(2,1)S(1)}, u32[]{:S(2)}) copy-start(bf16[3,384,128]{2,1,0:T(8,128)(2,1)S(1)} %collective-permute-done.16.refs_2_) | copy-start | bytes 884740
  97.9 10.6 %collective-permute-start.17 = (bf16[3,384,128]{2,1,0:T(8,128)(2,1)S(1)}, bf16[3,384,128]{2,1,0:T(8,128)(2,1)S(1)}, u32[]{:S(2)}, u32[]{:S(2)}) collective-permute-start(bf16[3,384,128]{2,1,0:T(8,128)(2,1)S(1)} %collective-permute-done.16.refs_2_), channel_id=1, source_target_pairs={{0,16},{16,0},{1,17},{17,1},{2,18},{18,2},{3,19},{19,3},{4,20},{20... | collective-permute-start | bytes 884744 | tf_op jit(solution)/shard_map/ppermute | solution.py:107
  100.0 8.5 %copy-start.11 = (bf16[3,384,128]{2,1,0:T(8,128)(2,1)}, bf16[3,384,128]{2,1,0:T(8,128)(2,1)S(1)}, u32[]{:S(2)}) copy-start(bf16[3,384,128]{2,1,0:T(8,128)(2,1)S(1)} %collective-permute-done.14.refs_1_) | copy-start | bytes 884740
  108.5 11.1 %collective-permute-start.19 = (bf16[4,320,512]{2,1,0:T(8,128)(2,1)}, bf16[4,320,512]{2,1,0:T(8,128)(2,1)}, u32[]{:S(2)}, u32[]{:S(2)}) collective-permute-start(bf16[4,320,512]{2,1,0:T(8,128)(2,1)} %get-tuple-element.36), channel_id=1, source_target_pairs={{0,1},{1,0},{2,3},{3,2},{4,5},{5,4},{6,7},{7,6},{8,9},{9,8},{10,11... | collective-permute-start | bytes 3932168 | tf_op jit(solution)/shard_map/ppermute | solution.py:107
  108.6 0.7 copy-start.12
  115.5 10.8 %collective-permute-start.18 = (bf16[4,320,256]{2,1,0:T(8,128)(2,1)}, bf16[4,320,256]{2,1,0:T(8,128)(2,1)}, u32[]{:S(2)}, u32[]{:S(2)}) collective-permute-start(bf16[4,320,256]{2,1,0:T(8,128)(2,1)} %get-tuple-element.40), channel_id=1, source_target_pairs={{0,1},{1,0},{2,3},{3,2},{4,5},{5,4},{6,7},{7,6},{8,9},{9,8},{10,11... | collective-permute-start | bytes 1966088 | tf_op jit(solution)/shard_map/ppermute | solution.py:107
  117.2 23.3 %collective-permute-start.24 = (bf16[384,768]{1,0:T(8,128)(2,1)S(1)}, bf16[384,768]{1,0:T(8,128)(2,1)}, u32[]{:S(2)}, u32[]{:S(2)}) collective-permute-start(bf16[384,768]{1,0:T(8,128)(2,1)S(1)} %collective-permute-done.15.refs_7_), channel_id=1, source_target_pairs={{0,1},{1,0},{2,3},{3,2},{4,5},{5,4},{6,7},{7,6},{8,9},{9,8},{10,11... | collective-permute-start | bytes 1769480 | tf_op jit(solution)/shard_map/ppermute | solution.py:107
  130.9 26.5 %copy-start.1 = (bf16[2,128,384]{2,1,0:T(8,128)(2,1)S(1)}, bf16[2,128,384]{2,1,0:T(8,128)(2,1)}, u32[]{:S(2)}) copy-start(bf16[2,128,384]{2,1,0:T(8,128)(2,1)} %get-tuple-element.45.refs_0_) | copy-start | bytes 589828
  130.9 26.5 %copy-start.2 = (s32[4]{0:T(128)S(1)}, s32[4]{0:T(128)}, u32[]{:S(2)}) copy-start(s32[4]{0:T(128)} %pad_add_fusion.place_ref) | copy-start | bytes 52
  130.9 12.6 %collective-permute-start.20 = (bf16[2,128,384]{2,1,0:T(8,128)(2,1)}, bf16[2,128,384]{2,1,0:T(8,128)(2,1)S(1)}, u32[]{:S(2)}, u32[]{:S(2)}) collective-permute-start(bf16[2,128,384]{2,1,0:T(8,128)(2,1)} %get-tuple-element.46), channel_id=1, source_target_pairs={{0,4},{4,0},{8,12},{12,8},{1,5},{5,1},{9,13},{13,9},{2,6},{6,2},{1... | collective-permute-start | bytes 589832 | tf_op jit(solution)/shard_map/ppermute | solution.py:107
  137.7 19.7 %collective-permute-start.22 = (bf16[2,128,384]{2,1,0:T(8,128)(2,1)}, bf16[2,128,384]{2,1,0:T(8,128)(2,1)S(1)}, u32[]{:S(2)}, u32[]{:S(2)}) collective-permute-start(bf16[2,128,384]{2,1,0:T(8,128)(2,1)} %get-tuple-element.46), channel_id=1, source_target_pairs={{0,12},{4,8},{8,4},{12,0},{1,13},{5,9},{9,5},{13,1},{2,14},{6,10},... | collective-permute-start | bytes 589832 | tf_op jit(solution)/shard_map/ppermute | solution.py:107
  139.1 18.3 %collective-permute-start.21 = (bf16[2,128,384]{2,1,0:T(8,128)(2,1)}, bf16[2,128,384]{2,1,0:T(8,128)(2,1)S(1)}, u32[]{:S(2)}, u32[]{:S(2)}) collective-permute-start(bf16[2,128,384]{2,1,0:T(8,128)(2,1)} %get-tuple-element.45.refs_0_), channel_id=1, source_target_pairs={{0,8},{4,12},{8,0},{12,4},{1,9},{5,13},{9,1},{13,5},{2,10},{6,14},... | collective-permute-start | bytes 589832 | tf_op jit(solution)/shard_map/ppermute | solution.py:107
  161.1 6.6 %collective-permute-start.25 = (bf16[2,64,768]{2,1,0:T(8,128)(2,1)S(1)}, bf16[2,64,768]{2,1,0:T(8,128)(2,1)S(1)}, u32[]{:S(2)}, u32[]{:S(2)}) collective-permute-start(bf16[2,64,768]{2,1,0:T(8,128)(2,1)S(1)} %get-tuple-element.48), channel_id=1, source_target_pairs={{0,2},{2,0},{1,3},{3,1},{4,6},{6,4},{5,7},{7,5},{8,10},{10,8},{9,1... | collective-permute-start | bytes 589832 | tf_op jit(solution)/shard_map/ppermute | solution.py:107
  162.9 14.4 %collective-permute-start.26 = (bf16[2,64,768]{2,1,0:T(8,128)(2,1)S(1)}, bf16[2,64,768]{2,1,0:T(8,128)(2,1)S(1)}, u32[]{:S(2)}, u32[]{:S(2)}) collective-permute-start(bf16[2,64,768]{2,1,0:T(8,128)(2,1)S(1)} %get-tuple-element.49), channel_id=1, source_target_pairs={{0,8},{4,12},{8,0},{12,4},{1,9},{5,13},{9,1},{13,5},{2,10},{6,14},... | collective-permute-start | bytes 589832 | tf_op jit(solution)/shard_map/ppermute | solution.py:107
  162.9 18.3 %collective-permute-start.27 = (bf16[2,64,768]{2,1,0:T(8,128)(2,1)S(1)}, bf16[2,64,768]{2,1,0:T(8,128)(2,1)S(1)}, u32[]{:S(2)}, u32[]{:S(2)}) collective-permute-start(bf16[2,64,768]{2,1,0:T(8,128)(2,1)S(1)} %get-tuple-element.50), channel_id=1, source_target_pairs={{0,10},{2,8},{4,14},{6,12},{8,2},{10,0},{12,6},{14,4},{1,11},{3,9}... | collective-permute-start | bytes 589832 | tf_op jit(solution)/shard_map/ppermute | solution.py:395

commit v11 on v9

--- a/solution.py
+++ b/solution.py
@@ -197,7 +197,7 @@
         [place],
         [tokens, *flat],
         scratch=[pltpu.VMEM((rows, 2, count, cols), jnp.float32)],
-        flops=flops,
+        flops=8 * flops,
         read=flops // 300,
     )
 
@@ -363,18 +363,18 @@
     mine = lax.dynamic_slice_in_dim(latents[0], core * span * depth, span * depth, axis=1)
     in_1, near, mine_x = inward(mine), swap(mine, "rows"), swap(mine, "frames")
     here, there = [reshard(0)], []
+    here.append(reshard(1, in_1, near, mine_x))
+    in_2 = inward(after(near, in_1))
     near_x = swap(near, "frames")
-    out_1, in_1x = outward(in_1), over_frames(in_1, (1, 2))
-    here.append(reshard(1, in_1, near))
+    out_1, in_1x = outward(after(in_1, near_x)), over_frames(in_1, (1, 2))
+    across = swap(after(w_out, near), "heads")
     there.append(swap(here[0], "groups"))
-    across = swap(after(w_out, near), "heads")
-    in_2 = inward(after(near, here[0]))
+    here.append(reshard(2, in_2, out_1, near_x, in_1x, there[0], across))
+    there.append(swap(here[1], "groups"))
+    out_2, in_2x = outward(after(in_2, there[0])), over_frames(in_2, (1, 2))
     out_1x = over_frames(out_1, (0, 3))
-    here.append(reshard(2, here[1], there[0], mine_x, near_x, in_1x, out_1, across))
-    there.append(swap(here[1], "groups"))
-    out_2, in_2x = outward(in_2), over_frames(in_2, (1, 2))
-    here.append(reshard(3, here[1], there[1], in_2, in_2x, out_1x))
-    there += [swap(here[2], "groups"), swap(here[3], "groups")]
+    here.append(reshard(3, here[1], in_2x, out_1x))
+    there += [swap(after(here[2], there[1]), "groups"), swap(here[3], "groups")]
     out_2x = over_frames(out_2, (0, 3))
     tokens = assemble(
         place, [(mine, mine_x), (near, near_x)], [(in_1, in_1x), (in_2, in_2x)], [(out_1, out_1x), (out_2, out_2x)]
@@ -391,10 +391,10 @@
     members, counts = picked[:, :MAXB].reshape(-1), picked[:, MAXB]
 
     out_half = lax.dynamic_slice_in_dim(w_out, group * cols, cols, axis=0)
-    beside = [swap(after(out_half, here[2]), "rows")]
+    beside = [swap(after(out_half, members, counts), "rows")]
     beside.append(swap(beside[0], "groups"))
 
-    chunks = [(here[0], there[0]), (here[1], after(there[1], there[2], there[3], members, counts))]
+    chunks = [(here[0], there[0]), (here[1], after(there[1], there[2]))]
     first = project(place, tokens, chunks)
     first_more = swap(first[2], "heads")
     second = project(place, tokens, [(here[2], there[2]), (here[3], after(there[3], first[2], beside[0]))])
@@ -403,7 +403,7 @@
     same, diff = attend_all(place, members, counts, *second[:2], second_more, attended)
     attended = [same] + [swap(same if s % 2 == 0 else diff, "rows", s) for s in range(1, rows_n)]
     halves = [w_out[:cols], w_out[cols:], *beside]
-    beside_across = [swap(part, "heads") for part in (beside[0], after(beside[1], attended[1]))]
+    beside_across = [swap(part, "heads") for part in (beside[0], after(beside[1], *attended[1:]))]
     keep, over_x, over_z, over_both = mix(
         place, attended, [*halves, across[:cols], across[cols:], *beside_across]
     )

time: 181 us -> 174 us (0.961)
  waiting for transfers between devices: 86.4 us -> 67.5 us
  starting transfers between devices: 55.1 us -> 66 us
    ppermute x2, waiting for transfers between devices: 19.6 us -> 3.8 us  [outward(): return lax.ppermute(value, 'rows', [(1, 0), (2, 3)])]
    ppermute x4, starting transfers between devices: 14.2 us -> 24 us  [reshard(): lax.ppermute(after(value, *others) if others else value, ('rows', 'heads'...]
    ppermute x22, starting transfers between devices: 21.6 us -> 27.5 us  [swap(): return lax.ppermute(value, axis, [(i, i ^ step) for i in range(peers)])]
    ppermute x1, starting transfers between devices: 4.3 us -> 0.01 us  [by_heads(): lax.ppermute(over_both, ('rows', 'frames'), [(2 * r + f, 2 * (r ^ 2) + 1...]
    ppermute x22, waiting for transfers between devices: 51.5 us -> 49.4 us  [swap(): return lax.ppermute(value, axis, [(i, i ^ step) for i in range(peers)])]
    ppermute x4, waiting for transfers between devices: 4.82 us -> 6.86 us  [reshard(): lax.ppermute(after(value, *others) if others else value, ('rows', 'heads'...]
    ppermute x1, waiting for transfers between devices: 5.22 us -> 3.21 us  [by_heads(): lax.ppermute(over_both, ('rows', 'frames'), [(2 * r + f, 2 * (r ^ 2) + 1...]
  transfers between devices with their start and end apart: 35 -> 35, of which waited for: 11 -> 16; matrix products, arithmetic and copies ran while one was open for 5% -> 6% of each run, Pallas kernels for 10% -> 11%
where the time goes in v11:
time: 174 us; the launch traced here: 173 us
  waiting for transfers between devices  67.5 us (39%)
  starting transfers between devices  66 us (38%)
  Pallas kernels  22.6 us (13%)
  local copies, waits for them, and re-layouts  15.7 us (9%)
    ppermute x22, waiting for transfers between devices, swap(): return lax.ppermute(value, axis, [(i, i ^ step) for i in range(peers)])  49.4 us
    ppermute x22, starting transfers between devices, swap(): return lax.ppermute(value, axis, [(i, i ^ step) for i in range(peers)])  27.5 us
    ppermute x4, starting transfers between devices, reshard(): lax.ppermute(after(value, *others) if others else value, ('rows', 'heads'...  24 us
    pallas_call x7, Pallas kernels, call(): pl.pallas_call(kernel, out_shape=out_shape, grid_spec=pltpu.PrefetchScala...  22.6 us
    ppermute x4, starting transfers between devices, over_frames(): return lax.ppermute(value, ('rows', 'frames'), pairs)  9.75 us
    ppermute x4, waiting for transfers between devices, reshard(): lax.ppermute(after(value, *others) if others else value, ('rows', 'heads'...  6.86 us
    unnamed x30, local copies, waits for them, and re-layouts  6.76 us
    ppermute x4, waiting for transfers between devices, over_frames(): return lax.ppermute(value, ('rows', 'frames'), pairs)  4.32 us
  transfers between devices with their start and end apart: 35, of which 16 were waited for; matrix products, arithmetic and copies ran while one was open for 6% of the time, Pallas kernels for 11%

profile of v11, /device:TPU:0, one launch (start us, length us, event | category | flops | bytes accessed | tf_op | source)
XLA Modules:
  0.0 173.1 jit_solution(6319655210078459500)
XLA Ops:
  0.0 1.1 copy-done
  1.2 3.1 %collective-permute-start = (bf16[128,1536]{1,0:T(8,128)(2,1)S(1)}, bf16[128,1536]{1,0:T(8,128)(2,1)S(1)}, u32[]{:S(2)}, u32[]{:S(2)}) collective-permute-start(bf16[128,1536]{1,0:T(8,128)(2,1)S(1)} %dynamic-slice_bitcast_fusion.2.refs_0_), channel_id=1, source_target_pairs={{0,4},{4,0},{8,12},{12,8},{1,5},{5,1},{9,13},{13,9},{2,6},{6,2},{1... | collective-permute-start | bytes 1179656 | tf_op jit(solution)/shard_map/ppermute | solution.py:107
  4.3 1.4 dynamic-slice_bitcast_fusion
  7.1 1.6 collective-permute-start.10
  8.6 8.2 %collective-permute-done.refs_2_ = bf16[128,1536]{1,0:T(8,128)(2,1)S(1)} collective-permute-done((bf16[128,1536]{1,0:T(8,128)(2,1)S(1)}, bf16[128,1536]{1,0:T(8,128)(2,1)S(1)}, u32[]{:S(2)}, u32[]{:S(2)}) %collective-permute-start) | collective-permute-done | bytes 393248 | tf_op jit(solution)/shard_map/ppermute | solution.py:107
  16.8 1.6 collective-permute-start.3
  18.5 1.5 collective-permute-start.2
  20.7 21.7 %collective-permute-start.11 = (bf16[3,384,256]{2,1,0:T(8,128)(2,1)S(1)}, bf16[3,384,256]{2,1,0:T(8,128)(2,1)S(1)}, u32[]{:S(2)}, u32[]{:S(2)}) collective-permute-start(bf16[3,384,256]{2,1,0:T(8,128)(2,1)S(1)} %get-tuple-element.36), channel_id=1, source_target_pairs={{0,4},{1,12},{4,0},{5,8},{8,5},{9,13},{12,1},{13,9},{2,6},{3,14},{... | collective-permute-start | bytes 1769480 | tf_op jit(solution)/shard_map/ppermute | solution.py:361
  42.4 1.5 collective-permute-start.7
  43.9 1.5 collective-permute-start.5
  45.4 1.3 collective-permute-start.4
  46.7 3.6 %collective-permute-done.11.refs_2_ = bf16[3,384,256]{2,1,0:T(8,128)(2,1)S(1)} collective-permute-done((bf16[3,384,256]{2,1,0:T(8,128)(2,1)S(1)}, bf16[3,384,256]{2,1,0:T(8,128)(2,1)S(1)}, u32[]{:S(2)}, u32[]{:S(2)}) %collective-permute-start.11) | collective-permute-done | bytes 589856 | tf_op jit(solution)/shard_map/ppermute | solution.py:361
  50.2 1.5 collective-permute-start.12
  51.8 3.6 %collective-permute-done.7.refs_1_ = bf16[3,384,256]{2,1,0:T(8,128)(2,1)S(1)} collective-permute-done((bf16[3,384,256]{2,1,0:T(8,128)(2,1)S(1)}, bf16[3,384,256]{2,1,0:T(8,128)(2,1)S(1)}, u32[]{:S(2)}, u32[]{:S(2)}) %collective-permute-start.7) | collective-permute-done | bytes 589856 | tf_op jit(solution)/shard_map/ppermute | solution.py:107
  55.4 1.4 collective-permute-start.17
  56.8 1.3 collective-permute-start.19
  58.1 3.8 %collective-permute-done.4.refs_8_ = bf16[128,1536]{1,0:T(8,128)(2,1)} collective-permute-done((bf16[128,1536]{1,0:T(8,128)(2,1)S(1)}, bf16[128,1536]{1,0:T(8,128)(2,1)}, u32[]{:S(2)}, u32[]{:S(2)}) %collective-permute-start.4) | collective-permute-done | bytes 393248 | tf_op jit(solution)/shard_map/ppermute | solution.py:346
  61.9 3.4 %collective-permute-start.18 = (bf16[128,1536]{1,0:T(8,128)(2,1)}, bf16[128,1536]{1,0:T(8,128)(2,1)}, u32[]{:S(2)}, u32[]{:S(2)}) collective-permute-start(bf16[128,1536]{1,0:T(8,128)(2,1)} %collective-permute-done.4.refs_8_), channel_id=1, source_target_pairs={{0,2},{2,0},{12,14},{14,12},{1,3},{3,1},{13,15},{15,13},{16,18},{1... | collective-permute-start | bytes 1179656 | tf_op jit(solution)/shard_map/ppermute | solution.py:340
  65.3 1.9 %dynamic-slice_bitcast_fusion.3 = (bf16[3,384,128]{2,1,0:T(8,128)(2,1)}, bf16[3,384,128]{2,1,0:T(8,128)(2,1)}) fusion(bf16[768,3,768]{2,0,1:T(8,128)(2,1)} %param.7, s32[]{:T(128)S(6)} %select_n.55, s32[]{:T(128)S(6)} %select_n.65, s32[]{:T(128)S(6)} %select_n.57), kind=kLoop, calls=%fused_computation.5 | loop fusion | bytes 1179660 | tf_op jit(solution)/shard_map/dynamic_slice | solution.py:353
  67.3 1.6 collective-permute-start.9
  69.3 4.3 %collective-permute-done.18.refs_9_ = bf16[128,1536]{1,0:T(8,128)(2,1)} collective-permute-done((bf16[128,1536]{1,0:T(8,128)(2,1)}, bf16[128,1536]{1,0:T(8,128)(2,1)}, u32[]{:S(2)}, u32[]{:S(2)}) %collective-permute-start.18) | collective-permute-done | bytes 393248 | tf_op jit(solution)/shard_map/ppermute | solution.py:340
  73.6 3.5 %collective-permute-start.20 = (bf16[128,1536]{1,0:T(8,128)(2,1)}, bf16[128,1536]{1,0:T(8,128)(2,1)}, u32[]{:S(2)}, u32[]{:S(2)}) collective-permute-start(bf16[128,1536]{1,0:T(8,128)(2,1)} %collective-permute-done.19.refs_10_), channel_id=1, source_target_pairs={{0,2},{2,0},{12,14},{14,12},{1,3},{3,1},{13,15},{15,13},{16,18},{1... | collective-permute-start | bytes 1179656 | tf_op jit(solution)/shard_map/ppermute | solution.py:340
  77.9 1.5 collective-permute-start.13
  80.1 2.4 %fusion.3 = (bf16[384,768]{1,0:T(8,128)(2,1)S(1)}, bf16[384,768]{1,0:T(8,128)(2,1)}, bf16[384,768]{1,0:T(8,128)(2,1)S(1)}) fusion(bf16[768,768]{1,0:T(8,128)(2,1)} %param.8, s32[]{:T(128)S(6)} %select_n.55), kind=kLoop, calls=%fused_computation.20 | loop fusion | bytes 3538948 | tf_op jit(solution)/shard_map/slice | solution.py:405
  82.6 3.3 %collective-permute-done.21.refs_2_ = bf16[3,384,128]{2,1,0:T(8,128)(2,1)} collective-permute-done((bf16[3,384,128]{2,1,0:T(8,128)(2,1)}, bf16[3,384,128]{2,1,0:T(8,128)(2,1)}, u32[]{:S(2)}, u32[]{:S(2)}) %collective-permute-start.21) | collective-permute-done | bytes 294944 | tf_op jit(solution)/shard_map/ppermute | solution.py:361
  86.5 5.0 %shard_map.64.x_ref = bf16[4,2,128,1536]{3,2,1,0:T(8,128)(2,1)} custom-call(s32[4]{0:T(128)} %pad_add_fusion.2.place_ref, bf16[128,1536]{1,0:T(8,128)(2,1)} %copy-done.7, bf16[128,1536]{1,0:T(8,128)(2,1)} %copy-done.10, bf16[128,1536]{1,0:T(8,128)(2,1)} %copy-done.8, bf16[128,1536]{1,0:T(8,128)(2,1)} %copy-done.11, bf16[128,1536]{1,0:T(8,128)(2,1)} %copy-done.9, ...), custom_call_target="tpu_custom_call" | custom-call | bytes 7864320 | tf_op jit(solution)/shard_map/pallas_call | solution.py:115
  91.5 4.0 %collective-permute-start.16 = (s32[2,6]{1,0:T(2,128)S(1)}, s32[2,6]{1,0:T(2,128)S(1)}, u32[]{:S(2)}, u32[]{:S(2)}) collective-permute-start(s32[2,6]{1,0:T(2,128)S(1)} %pad_add_fusion.1), channel_id=1, source_target_pairs={{0,12},{4,8},{8,4},{12,0},{1,13},{5,9},{9,5},{13,1},{2,14},{6,10},... | collective-permute-start | bytes 152 | tf_op jit(solution)/shard_map/ppermute | solution.py:107
  97.0 2.9 %collective-permute-done.15 = s32[2,6]{1,0:T(2,128)S(1)} collective-permute-done((s32[2,6]{1,0:T(2,128)S(1)}, s32[2,6]{1,0:T(2,128)S(1)}, u32[]{:S(2)}, u32[]{:S(2)}) %collective-permute-start.15) | collective-permute-done | bytes 80 | tf_op jit(solution)/shard_map/ppermute | solution.py:107
  101.9 1.9 %copy-done.1 = bf16[4,2,128,1536]{3,2,1,0:T(8,128)(2,1)S(1)} copy-done((bf16[4,2,128,1536]{3,2,1,0:T(8,128)(2,1)S(1)}, bf16[4,2,128,1536]{3,2,1,0:T(8,128)(2,1)}, u32[]{:S(2)}) %copy-start.1) | copy-done | bytes 3145752
  103.7 1.1 copy-done.4
  105.9 4.0 %shard_map.65 = (f32[4,128,256]{2,1,0:T(8,128)S(1)}, f32[4,256,512]{2,1,0:T(8,128)S(1)}, bf16[4,320,512]{2,1,0:T(8,128)(2,1)S(1)}) custom-call(s32[4]{0:T(128)S(1)} %copy-done.2, bf16[4,2,128,1536]{3,2,1,0:T(8,128)(2,1)S(1)} %copy-done.1, bf16[3,384,256]{2,1,0:T(8,128)(2,1)S(1)} %collective-permute-done.6.refs_0_, bf16[3,384,256]{2,1,0:T(8,128)(2,1)S(1)} %copy-done.4, ...), custom_call_target="tpu_custom_call" | custom-call | flops 19327352832 | bytes 8053063 | tf_op jit(solution)/shard_map/pallas_call | solution.py:115
  110.0 5.0 %collective-permute-done.23.refs_6_ = bf16[384,768]{1,0:T(8,128)(2,1)S(1)} collective-permute-done((bf16[384,768]{1,0:T(8,128)(2,1)}, bf16[384,768]{1,0:T(8,128)(2,1)S(1)}, u32[]{:S(2)}, u32[]{:S(2)}) %collective-permute-start.23) | collective-permute-done | bytes 589856 | tf_op jit(solution)/shard_map/ppermute | solution.py:107
  115.0 3.8 %shard_map.66 = (f32[4,128,128]{2,1,0:T(8,128)S(1)}, f32[4,256,256]{2,1,0:T(8,128)S(1)}, bf16[4,320,256]{2,1,0:T(8,128)(2,1)S(1)}) custom-call(s32[4]{0:T(128)S(1)} %copy-done.2, bf16[4,2,128,1536]{3,2,1,0:T(8,128)(2,1)S(1)} %copy-done.1, bf16[3,384,128]{2,1,0:T(8,128)(2,1)S(1)} %collective-permute-done.9.refs_0_, ...), custom_call_target="tpu_custom_call" | custom-call | flops 9663676416 | bytes 4026531 | tf_op jit(solution)/shard_map/pallas_call | solution.py:115
  118.9 1.5 collective-permute-start.29
  120.4 3.8 %shard_map.67 = (bf16[2,128,256]{2,1,0:T(8,128)(2,1)S(1)}, bf16[2,128,256]{2,1,0:T(8,128)(2,1)S(1)}) custom-call(s32[4]{0:T(128)S(1)} %copy-done.2, s32[16]{0:T(128)S(1)} %reshape.24.members_ref, s32[4]{0:T(128)S(1)} %slice_reduce_fusion.1.counts_ref, f32[4,128,256]{2,1,0:T(8,128)S(1)} %get-tuple-element.48.q_ref, ...), custom_call_target="tpu_custom_call" | custom-call | flops 268435456 | bytes 2097152 | tf_op jit(solution)/shard_map/pallas_call | solution.py:115
  124.2 2.2 %shard_map.68 = (bf16[2,128,384]{2,1,0:T(8,128)(2,1)S(1)}, bf16[2,128,384]{2,1,0:T(8,128)(2,1)S(1)}) custom-call(s32[4]{0:T(128)S(1)} %copy-done.2, s32[16]{0:T(128)S(1)} %reshape.24.members_ref, s32[4]{0:T(128)S(1)} %slice_reduce_fusion.1.counts_ref, f32[4,128,128]{2,1,0:T(8,128)S(1)} %get-tuple-element.45.q_ref, ...), custom_call_target="tpu_custom_call" | custom-call | flops 134217728 | bytes 1048576 | tf_op jit(solution)/shard_map/pallas_call | solution.py:115
  126.4 2.1 %collective-permute-start.27 = (bf16[2,128,384]{2,1,0:T(8,128)(2,1)S(1)}, bf16[2,128,384]{2,1,0:T(8,128)(2,1)S(1)}, u32[]{:S(2)}, u32[]{:S(2)}) collective-permute-start(bf16[2,128,384]{2,1,0:T(8,128)(2,1)S(1)} %get-tuple-element.52.refs_0_), channel_id=1, source_target_pairs={{0,8},{4,12},{8,0},{12,4},{1,9},{5,13},{9,1},{13,5},{2,10},{6,14},... | collective-permute-start | bytes 589832 | tf_op jit(solution)/shard_map/ppermute | solution.py:107
  128.5 1.8 %collective-permute-start.28 = (bf16[2,128,384]{2,1,0:T(8,128)(2,1)S(1)}, bf16[2,128,384]{2,1,0:T(8,128)(2,1)S(1)}, u32[]{:S(2)}, u32[]{:S(2)}) collective-permute-start(bf16[2,128,384]{2,1,0:T(8,128)(2,1)S(1)} %get-tuple-element.53), channel_id=1, source_target_pairs={{0,12},{4,8},{8,4},{12,0},{1,13},{5,9},{9,5},{13,1},{2,14},{6,10},... | collective-permute-start | bytes 589832 | tf_op jit(solution)/shard_map/ppermute | solution.py:107
  130.3 4.3 %collective-permute-done.29.refs_7_ = bf16[384,768]{1,0:T(8,128)(2,1)S(1)} collective-permute-done((bf16[384,768]{1,0:T(8,128)(2,1)S(1)}, bf16[384,768]{1,0:T(8,128)(2,1)S(1)}, u32[]{:S(2)}, u32[]{:S(2)}) %collective-permute-start.29) | collective-permute-done | bytes 589856 | tf_op jit(solution)/shard_map/ppermute | solution.py:107
  134.6 8.9 %collective-permute-done.27.refs_2_ = bf16[2,128,384]{2,1,0:T(8,128)(2,1)S(1)} collective-permute-done((bf16[2,128,384]{2,1,0:T(8,128)(2,1)S(1)}, bf16[2,128,384]{2,1,0:T(8,128)(2,1)S(1)}, u32[]{:S(2)}, u32[]{:S(2)}) %collective-permute-start.27) | collective-permute-done | bytes 196640 | tf_op jit(solution)/shard_map/ppermute | solution.py:107
  144.1 1.3 fusion.2
  146.1 2.4 %shard_map.69 = (f32[2,64,768]{2,1,0:T(8,128)S(1)}, bf16[2,64,768]{2,1,0:T(8,128)(2,1)S(1)}, bf16[2,64,768]{2,1,0:T(8,128)(2,1)S(1)}, bf16[2,64,768]{2,1,0:T(8,128)(2,1)S(1)}) custom-call(s32[4]{0:T(128)S(1)} %copy-done.2, bf16[2,128,384]{2,1,0:T(8,128)(2,1)S(1)} %get-tuple-element.52.refs_0_, bf16[2,128,384]{2,1,0:T(8,128)(2,1)S(1)} %collective-permute-done.26.refs_1_, ...), custom_call_target="tpu_custom_call" | custom-call | flops 1207959552 | bytes 4718592 | tf_op jit(solution)/shard_map/pallas_call | solution.py:115
  148.6 1.5 collective-permute-start.32
  150.1 4.4 %collective-permute-start.33 = (bf16[2,64,768]{2,1,0:T(8,128)(2,1)S(1)}, bf16[2,64,768]{2,1,0:T(8,128)(2,1)S(1)}, u32[]{:S(2)}, u32[]{:S(2)}) collective-permute-start(bf16[2,64,768]{2,1,0:T(8,128)(2,1)S(1)} %get-tuple-element.57), channel_id=1, source_target_pairs={{0,8},{4,12},{8,0},{12,4},{1,9},{5,13},{9,1},{13,5},{2,10},{6,14},... | collective-permute-start | bytes 589832 | tf_op jit(solution)/shard_map/ppermute | solution.py:107
  154.4 1.2 collective-permute-done.32.x_ref
  155.6 13.0 %collective-permute-done.33.z_ref = bf16[2,64,768]{2,1,0:T(8,128)(2,1)S(1)} collective-permute-done((bf16[2,64,768]{2,1,0:T(8,128)(2,1)S(1)}, bf16[2,64,768]{2,1,0:T(8,128)(2,1)S(1)}, u32[]{:S(2)}, u32[]{:S(2)}) %collective-permute-start.33) | collective-permute-done | bytes 196640 | tf_op jit(solution)/shard_map/ppermute | solution.py:107
  168.6 3.2 %collective-permute-done.34.both_ref = bf16[2,64,768]{2,1,0:T(8,128)(2,1)S(1)} collective-permute-done((bf16[2,64,768]{2,1,0:T(8,128)(2,1)S(1)}, bf16[2,64,768]{2,1,0:T(8,128)(2,1)S(1)}, u32[]{:S(2)}, u32[]{:S(2)}) %collective-permute-start.34) | collective-permute-done | bytes 196640 | tf_op jit(solution)/shard_map/ppermute | solution.py:412
  171.8 1.4 shard_map.70
  (79 shorter events, 10.6 us)
Async XLA Ops:
  0.0 1.1 copy-start
  1.2 41.2 %copy-start.7 = (bf16[128,1536]{1,0:T(8,128)(2,1)}, bf16[128,1536]{1,0:T(8,128)(2,1)S(1)}, u32[]{:S(2)}) copy-start(bf16[128,1536]{1,0:T(8,128)(2,1)S(1)} %dynamic-slice_bitcast_fusion.2.refs_0_) | copy-start | bytes 1179652
  1.2 15.7 %collective-permute-start = (bf16[128,1536]{1,0:T(8,128)(2,1)S(1)}, bf16[128,1536]{1,0:T(8,128)(2,1)S(1)}, u32[]{:S(2)}, u32[]{:S(2)}) collective-permute-start(bf16[128,1536]{1,0:T(8,128)(2,1)S(1)} %dynamic-slice_bitcast_fusion.2.refs_0_), channel_id=1, source_target_pairs={{0,4},{4,0},{8,12},{12,8},{1,5},{5,1},{9,13},{13,9},{2,6},{6,2},{1... | collective-permute-start | bytes 1179656 | tf_op jit(solution)/shard_map/ppermute | solution.py:107
  4.3 64.6 %copy-start.13 = (s32[2]{0:T(128)S(1)}, s32[2]{0:T(128)}, u32[]{:S(2)}) copy-start(s32[2]{0:T(128)} %param.10) | copy-start | bytes 28
  4.3 64.7 %copy-start.14 = (s32[2]{0:T(128)S(1)}, s32[2]{0:T(128)}, u32[]{:S(2)}) copy-start(s32[2]{0:T(128)} %param.11) | copy-start | bytes 28
  4.3 64.9 %copy-start.12 = (s32[2,4]{1,0:T(2,128)S(1)}, s32[2,4]{1,0:T(2,128)}, u32[]{:S(2)}) copy-start(s32[2,4]{1,0:T(2,128)} %param.9) | copy-start | bytes 100
  5.7 36.7 %collective-permute-start.6 = (bf16[3,384,256]{2,1,0:T(8,128)(2,1)S(1)}, bf16[3,384,256]{2,1,0:T(8,128)(2,1)S(1)}, u32[]{:S(2)}, u32[]{:S(2)}) collective-permute-start(bf16[3,384,256]{2,1,0:T(8,128)(2,1)S(1)} %get-tuple-element.62), channel_id=1, source_target_pairs={{0,0},{1,8},{4,4},{5,12},{8,1},{9,9},{12,5},{13,13},{2,2},{3,10},{... | collective-permute-start | bytes 1769480 | tf_op jit(solution)/shard_map/ppermute | solution.py:361
  6.4 12.1 %collective-permute-start.1 = (bf16[128,1536]{1,0:T(8,128)(2,1)S(1)}, bf16[128,1536]{1,0:T(8,128)(2,1)S(1)}, u32[]{:S(2)}, u32[]{:S(2)}) collective-permute-start(bf16[128,1536]{1,0:T(8,128)(2,1)S(1)} %dynamic-slice_bitcast_fusion.2.refs_0_), channel_id=1, source_target_pairs={{4,8},{8,4},{5,9},{9,5},{6,10},{10,6},{7,11},{11,7},{20,24},{24,20... | collective-permute-start | bytes 1179656 | tf_op jit(solution)/shard_map/ppermute | solution.py:343
  7.1 12.9 %collective-permute-start.10 = (bf16[128,1536]{1,0:T(8,128)(2,1)S(1)}, bf16[128,1536]{1,0:T(8,128)(2,1)S(1)}, u32[]{:S(2)}, u32[]{:S(2)}) collective-permute-start(bf16[128,1536]{1,0:T(8,128)(2,1)S(1)} %dynamic-slice_bitcast_fusion.2.refs_0_), channel_id=1, source_target_pairs={{0,2},{2,0},{1,3},{3,1},{4,6},{6,4},{5,7},{7,5},{8,10},{10,8},{9,1... | collective-permute-start | bytes 1179656 | tf_op jit(solution)/shard_map/ppermute | solution.py:107
  16.8 29.8 %copy-start.8 = (bf16[128,1536]{1,0:T(8,128)(2,1)}, bf16[128,1536]{1,0:T(8,128)(2,1)S(1)}, u32[]{:S(2)}) copy-start(bf16[128,1536]{1,0:T(8,128)(2,1)S(1)} %collective-permute-done.refs_2_) | copy-start | bytes 1179652
  16.8 50.4 %collective-permute-start.8 = (bf16[768,768]{1,0:T(8,128)(2,1)}, bf16[768,768]{1,0:T(8,128)(2,1)}, u32[]{:S(2)}, u32[]{:S(2)}) collective-permute-start(bf16[768,768]{1,0:T(8,128)(2,1)} %param.8), channel_id=1, source_target_pairs={{0,1},{1,0},{2,3},{3,2},{4,5},{5,4},{6,7},{7,6},{8,9},{9,8},{10,11... | collective-permute-start | bytes 3538952 | tf_op jit(solution)/shard_map/ppermute | solution.py:107
  16.8 27.1 %collective-permute-start.3 = (bf16[128,1536]{1,0:T(8,128)(2,1)S(1)}, bf16[128,1536]{1,0:T(8,128)(2,1)S(1)}, u32[]{:S(2)}, u32[]{:S(2)}) collective-permute-start(bf16[128,1536]{1,0:T(8,128)(2,1)S(1)} %collective-permute-done.refs_2_), channel_id=1, source_target_pairs={{0,2},{2,0},{1,3},{3,1},{4,6},{6,4},{5,7},{7,5},{8,10},{10,8},{9,1... | collective-permute-start | bytes 1179656 | tf_op jit(solution)/shard_map/ppermute | solution.py:107
  18.5 48.8 %copy-start.9 = (bf16[128,1536]{1,0:T(8,128)(2,1)}, bf16[128,1536]{1,0:T(8,128)(2,1)S(1)}, u32[]{:S(2)}) copy-start(bf16[128,1536]{1,0:T(8,128)(2,1)S(1)} %collective-permute-done.1.refs_4_) | copy-start | bytes 1179652
  18.5 26.9 %collective-permute-start.2 = (bf16[128,1536]{1,0:T(8,128)(2,1)S(1)}, bf16[128,1536]{1,0:T(8,128)(2,1)}, u32[]{:S(2)}, u32[]{:S(2)}) collective-permute-start(bf16[128,1536]{1,0:T(8,128)(2,1)S(1)} %collective-permute-done.refs_2_), channel_id=1, source_target_pairs={{4,8},{8,4},{5,9},{9,5},{6,10},{10,6},{7,11},{11,7},{20,24},{24,20... | collective-permute-start | bytes 1179656 | tf_op jit(solution)/shard_map/ppermute | solution.py:343
  20.7 29.5 %collective-permute-start.11 = (bf16[3,384,256]{2,1,0:T(8,128)(2,1)S(1)}, bf16[3,384,256]{2,1,0:T(8,128)(2,1)S(1)}, u32[]{:S(2)}, u32[]{:S(2)}) collective-permute-start(bf16[3,384,256]{2,1,0:T(8,128)(2,1)S(1)} %get-tuple-element.36), channel_id=1, source_target_pairs={{0,4},{1,12},{4,0},{5,8},{8,5},{9,13},{12,1},{13,9},{2,6},{3,14},{... | collective-permute-start | bytes 1769480 | tf_op jit(solution)/shard_map/ppermute | solution.py:361
  42.4 13.0 %collective-permute-start.7 = (bf16[3,384,256]{2,1,0:T(8,128)(2,1)S(1)}, bf16[3,384,256]{2,1,0:T(8,128)(2,1)S(1)}, u32[]{:S(2)}, u32[]{:S(2)}) collective-permute-start(bf16[3,384,256]{2,1,0:T(8,128)(2,1)S(1)} %collective-permute-done.6.refs_0_), channel_id=1, source_target_pairs={{0,16},{16,0},{1,17},{17,1},{2,18},{18,2},{3,19},{19,3},{4,20},{20... | collective-permute-start | bytes 1769480 | tf_op jit(solution)/shard_map/ppermute | solution.py:107
  43.9 6.3 %copy-start.11 = (bf16[128,1536]{1,0:T(8,128)(2,1)}, bf16[128,1536]{1,0:T(8,128)(2,1)S(1)}, u32[]{:S(2)}) copy-start(bf16[128,1536]{1,0:T(8,128)(2,1)S(1)} %collective-permute-done.3.refs_3_) | copy-start | bytes 1179652
  43.9 12.9 %collective-permute-start.5 = (bf16[128,1536]{1,0:T(8,128)(2,1)S(1)}, bf16[128,1536]{1,0:T(8,128)(2,1)}, u32[]{:S(2)}, u32[]{:S(2)}) collective-permute-start(bf16[128,1536]{1,0:T(8,128)(2,1)S(1)} %collective-permute-done.1.refs_4_), channel_id=1, source_target_pairs={{4,6},{6,4},{8,10},{10,8},{5,7},{7,5},{9,11},{11,9},{20,22},{22,20... | collective-permute-start | bytes 1179656 | tf_op jit(solution)/shard_map/ppermute | solution.py:340
  45.4 16.5 %collective-permute-start.4 = (bf16[128,1536]{1,0:T(8,128)(2,1)S(1)}, bf16[128,1536]{1,0:T(8,128)(2,1)}, u32[]{:S(2)}, u32[]{:S(2)}) collective-permute-start(bf16[128,1536]{1,0:T(8,128)(2,1)S(1)} %collective-permute-done.1.refs_4_), channel_id=1, source_target_pairs={{4,0},{8,12},{5,1},{9,13},{6,2},{10,14},{7,3},{11,15},{20,16},{24,... | collective-permute-start | bytes 1179656 | tf_op jit(solution)/shard_map/ppermute | solution.py:346
  50.2 26.9 %collective-permute-start.12 = (bf16[3,384,256]{2,1,0:T(8,128)(2,1)S(1)}, bf16[3,384,256]{2,1,0:T(8,128)(2,1)S(1)}, u32[]{:S(2)}, u32[]{:S(2)}) collective-permute-start(bf16[3,384,256]{2,1,0:T(8,128)(2,1)S(1)} %collective-permute-done.11.refs_2_), channel_id=1, source_target_pairs={{0,16},{16,0},{1,17},{17,1},{2,18},{18,2},{3,19},{19,3},{4,20},{20... | collective-permute-start | bytes 1769480 | tf_op jit(solution)/shard_map/ppermute | solution.py:107
  55.4 24.7 %copy-start.3 = (bf16[3,384,256]{2,1,0:T(8,128)(2,1)}, bf16[3,384,256]{2,1,0:T(8,128)(2,1)S(1)}, u32[]{:S(2)}) copy-start(bf16[3,384,256]{2,1,0:T(8,128)(2,1)S(1)} %collective-permute-done.7.refs_1_) | copy-start | bytes 1769476
  55.4 13.9 %collective-permute-start.17 = (bf16[128,1536]{1,0:T(8,128)(2,1)}, bf16[128,1536]{1,0:T(8,128)(2,1)}, u32[]{:S(2)}, u32[]{:S(2)}) collective-permute-start(bf16[128,1536]{1,0:T(8,128)(2,1)} %collective-permute-done.2.refs_6_), channel_id=1, source_target_pairs={{4,6},{6,4},{8,10},{10,8},{5,7},{7,5},{9,11},{11,9},{20,22},{22,20... | collective-permute-start | bytes 1179656 | tf_op jit(solution)/shard_map/ppermute | solution.py:340
  56.8 16.8 %collective-permute-start.19 = (bf16[128,1536]{1,0:T(8,128)(2,1)}, bf16[128,1536]{1,0:T(8,128)(2,1)}, u32[]{:S(2)}, u32[]{:S(2)}) collective-permute-start(bf16[128,1536]{1,0:T(8,128)(2,1)} %collective-permute-done.2.refs_6_), channel_id=1, source_target_pairs={{4,0},{8,12},{5,1},{9,13},{6,2},{10,14},{7,3},{11,15},{20,16},{24,... | collective-permute-start | bytes 1179656 | tf_op jit(solution)/shard_map/ppermute | solution.py:346
  61.9 11.7 %collective-permute-start.18 = (bf16[128,1536]{1,0:T(8,128)(2,1)}, bf16[128,1536]{1,0:T(8,128)(2,1)}, u32[]{:S(2)}, u32[]{:S(2)}) collective-permute-start(bf16[128,1536]{1,0:T(8,128)(2,1)} %collective-permute-done.4.refs_8_), channel_id=1, source_target_pairs={{0,2},{2,0},{12,14},{14,12},{1,3},{3,1},{13,15},{15,13},{16,18},{1... | collective-permute-start | bytes 1179656 | tf_op jit(solution)/shard_map/ppermute | solution.py:340
  67.3 10.7 %collective-permute-start.9 = (bf16[3,384,128]{2,1,0:T(8,128)(2,1)}, bf16[3,384,128]{2,1,0:T(8,128)(2,1)S(1)}, u32[]{:S(2)}, u32[]{:S(2)}) collective-permute-start(bf16[3,384,128]{2,1,0:T(8,128)(2,1)} %get-tuple-element.35), channel_id=1, source_target_pairs={{0,0},{1,8},{4,4},{5,12},{8,1},{9,9},{12,5},{13,13},{2,2},{3,10},{... | collective-permute-start | bytes 884744 | tf_op jit(solution)/shard_map/ppermute | solution.py:361
  73.6 12.2 %collective-permute-start.21 = (bf16[3,384,128]{2,1,0:T(8,128)(2,1)}, bf16[3,384,128]{2,1,0:T(8,128)(2,1)}, u32[]{:S(2)}, u32[]{:S(2)}) collective-permute-start(bf16[3,384,128]{2,1,0:T(8,128)(2,1)} %get-tuple-element.40), channel_id=1, source_target_pairs={{0,4},{1,12},{4,0},{5,8},{8,5},{9,13},{12,1},{13,9},{2,6},{3,14},{... | collective-permute-start | bytes 884744 | tf_op jit(solution)/shard_map/ppermute | solution.py:361
  73.6 12.9 %collective-permute-start.20 = (bf16[128,1536]{1,0:T(8,128)(2,1)}, bf16[128,1536]{1,0:T(8,128)(2,1)}, u32[]{:S(2)}, u32[]{:S(2)}) collective-permute-start(bf16[128,1536]{1,0:T(8,128)(2,1)} %collective-permute-done.19.refs_10_), channel_id=1, source_target_pairs={{0,2},{2,0},{12,14},{14,12},{1,3},{3,1},{13,15},{15,13},{16,18},{1... | collective-permute-start | bytes 1179656 | tf_op jit(solution)/shard_map/ppermute | solution.py:340
  77.9 13.5 %collective-permute-start.13 = (bf16[3,384,128]{2,1,0:T(8,128)(2,1)S(1)}, bf16[3,384,128]{2,1,0:T(8,128)(2,1)}, u32[]{:S(2)}, u32[]{:S(2)}) collective-permute-start(bf16[3,384,128]{2,1,0:T(8,128)(2,1)S(1)} %collective-permute-done.9.refs_0_), channel_id=1, source_target_pairs={{0,16},{16,0},{1,17},{17,1},{2,18},{18,2},{3,19},{19,3},{4,20},{20... | collective-permute-start | bytes 884744 | tf_op jit(solution)/shard_map/ppermute | solution.py:107
  82.6 19.3 %copy-start.2 = (s32[4]{0:T(128)S(1)}, s32[4]{0:T(128)}, u32[]{:S(2)}) copy-start(s32[4]{0:T(128)} %pad_add_fusion.2.place_ref) | copy-start | bytes 52
  85.8 24.2 %collective-permute-start.22 = (bf16[3,384,128]{2,1,0:T(8,128)(2,1)}, bf16[3,384,128]{2,1,0:T(8,128)(2,1)}, u32[]{:S(2)}, u32[]{:S(2)}) collective-permute-start(bf16[3,384,128]{2,1,0:T(8,128)(2,1)} %collective-permute-done.21.refs_2_), channel_id=1, source_target_pairs={{0,16},{16,0},{1,17},{17,1},{2,18},{18,2},{3,19},{19,3},{4,20},{20... | collective-permute-start | bytes 884744 | tf_op jit(solution)/shard_map/ppermute | solution.py:107
  91.5 5.6 %collective-permute-start.16 = (s32[2,6]{1,0:T(2,128)S(1)}, s32[2,6]{1,0:T(2,128)S(1)}, u32[]{:S(2)}, u32[]{:S(2)}) collective-permute-start(s32[2,6]{1,0:T(2,128)S(1)} %pad_add_fusion.1), channel_id=1, source_target_pairs={{0,12},{4,8},{8,4},{12,0},{1,13},{5,9},{9,5},{13,1},{2,14},{6,10},... | collective-permute-start | bytes 152 | tf_op jit(solution)/shard_map/ppermute | solution.py:107
  95.5 4.5 %collective-permute-start.15 = (s32[2,6]{1,0:T(2,128)S(1)}, s32[2,6]{1,0:T(2,128)S(1)}, u32[]{:S(2)}, u32[]{:S(2)}) collective-permute-start(s32[2,6]{1,0:T(2,128)S(1)} %pad_add_fusion.1), channel_id=1, source_target_pairs={{0,8},{4,12},{8,0},{12,4},{1,9},{5,13},{9,1},{13,5},{2,10},{6,14},... | collective-permute-start | bytes 152 | tf_op jit(solution)/shard_map/ppermute | solution.py:107
  95.5 4.5 %collective-permute-start.14 = (s32[2,6]{1,0:T(2,128)S(1)}, s32[2,6]{1,0:T(2,128)S(1)}, u32[]{:S(2)}, u32[]{:S(2)}) collective-permute-start(s32[2,6]{1,0:T(2,128)S(1)} %pad_add_fusion.1), channel_id=1, source_target_pairs={{0,4},{4,0},{8,12},{12,8},{1,5},{5,1},{9,13},{13,9},{2,6},{6,2},{1... | collective-permute-start | bytes 152 | tf_op jit(solution)/shard_map/ppermute | solution.py:107
  101.8 13.2 %collective-permute-start.23 = (bf16[384,768]{1,0:T(8,128)(2,1)}, bf16[384,768]{1,0:T(8,128)(2,1)S(1)}, u32[]{:S(2)}, u32[]{:S(2)}) collective-permute-start(bf16[384,768]{1,0:T(8,128)(2,1)} %get-tuple-element.43), channel_id=1, source_target_pairs={{0,4},{4,0},{8,12},{12,8},{1,5},{5,1},{9,13},{13,9},{2,6},{6,2},{1... | collective-permute-start | bytes 1769480 | tf_op jit(solution)/shard_map/ppermute | solution.py:107
  101.9 1.9 %copy-start.1 = (bf16[4,2,128,1536]{3,2,1,0:T(8,128)(2,1)S(1)}, bf16[4,2,128,1536]{3,2,1,0:T(8,128)(2,1)}, u32[]{:S(2)}) copy-start(bf16[4,2,128,1536]{3,2,1,0:T(8,128)(2,1)} %shard_map.64.x_ref) | copy-start | bytes 9437188
  103.7 1.1 copy-start.4
  104.8 1.1 copy-start.6
  109.9 10.5 %collective-permute-start.25 = (bf16[4,320,512]{2,1,0:T(8,128)(2,1)S(1)}, bf16[4,320,512]{2,1,0:T(8,128)(2,1)S(1)}, u32[]{:S(2)}, u32[]{:S(2)}) collective-permute-start(bf16[4,320,512]{2,1,0:T(8,128)(2,1)S(1)} %get-tuple-element.42), channel_id=1, source_target_pairs={{0,1},{1,0},{2,3},{3,2},{4,5},{5,4},{6,7},{7,6},{8,9},{9,8},{10,11... | collective-permute-start | bytes 3932168 | tf_op jit(solution)/shard_map/ppermute | solution.py:107
  118.8 5.4 %collective-permute-start.24 = (bf16[4,320,256]{2,1,0:T(8,128)(2,1)S(1)}, bf16[4,320,256]{2,1,0:T(8,128)(2,1)S(1)}, u32[]{:S(2)}, u32[]{:S(2)}) collective-permute-start(bf16[4,320,256]{2,1,0:T(8,128)(2,1)S(1)} %get-tuple-element.47), channel_id=1, source_target_pairs={{0,1},{1,0},{2,3},{3,2},{4,5},{5,4},{6,7},{7,6},{8,9},{9,8},{10,11... | collective-permute-start | bytes 1966088 | tf_op jit(solution)/shard_map/ppermute | solution.py:107
  118.9 15.7 %collective-permute-start.29 = (bf16[384,768]{1,0:T(8,128)(2,1)S(1)}, bf16[384,768]{1,0:T(8,128)(2,1)S(1)}, u32[]{:S(2)}, u32[]{:S(2)}) collective-permute-start(bf16[384,768]{1,0:T(8,128)(2,1)S(1)} %collective-permute-done.23.refs_6_), channel_id=1, source_target_pairs={{0,16},{16,0},{1,17},{17,1},{2,18},{18,2},{3,19},{19,3},{4,20},{20... | collective-permute-start | bytes 1769480 | tf_op jit(solution)/shard_map/ppermute | solution.py:107
  126.4 17.2 %collective-permute-start.27 = (bf16[2,128,384]{2,1,0:T(8,128)(2,1)S(1)}, bf16[2,128,384]{2,1,0:T(8,128)(2,1)S(1)}, u32[]{:S(2)}, u32[]{:S(2)}) collective-permute-start(bf16[2,128,384]{2,1,0:T(8,128)(2,1)S(1)} %get-tuple-element.52.refs_0_), channel_id=1, source_target_pairs={{0,8},{4,12},{8,0},{12,4},{1,9},{5,13},{9,1},{13,5},{2,10},{6,14},... | collective-permute-start | bytes 589832 | tf_op jit(solution)/shard_map/ppermute | solution.py:107
  128.5 15.1 %collective-permute-start.28 = (bf16[2,128,384]{2,1,0:T(8,128)(2,1)S(1)}, bf16[2,128,384]{2,1,0:T(8,128)(2,1)S(1)}, u32[]{:S(2)}, u32[]{:S(2)}) collective-permute-start(bf16[2,128,384]{2,1,0:T(8,128)(2,1)S(1)} %get-tuple-element.53), channel_id=1, source_target_pairs={{0,12},{4,8},{8,4},{12,0},{1,13},{5,9},{9,5},{13,1},{2,14},{6,10},... | collective-permute-start | bytes 589832 | tf_op jit(solution)/shard_map/ppermute | solution.py:107
  130.3 13.8 %collective-permute-start.26 = (bf16[2,128,384]{2,1,0:T(8,128)(2,1)S(1)}, bf16[2,128,384]{2,1,0:T(8,128)(2,1)S(1)}, u32[]{:S(2)}, u32[]{:S(2)}) collective-permute-start(bf16[2,128,384]{2,1,0:T(8,128)(2,1)S(1)} %get-tuple-element.53), channel_id=1, source_target_pairs={{0,4},{4,0},{8,12},{12,8},{1,5},{5,1},{9,13},{13,9},{2,6},{6,2},{1... | collective-permute-start | bytes 589832 | tf_op jit(solution)/shard_map/ppermute | solution.py:107
  130.3 15.1 %collective-permute-start.30 = (bf16[384,768]{1,0:T(8,128)(2,1)S(1)}, bf16[384,768]{1,0:T(8,128)(2,1)S(1)}, u32[]{:S(2)}, u32[]{:S(2)}) collective-permute-start(bf16[384,768]{1,0:T(8,128)(2,1)S(1)} %collective-permute-done.23.refs_6_), channel_id=1, source_target_pairs={{0,1},{1,0},{2,3},{3,2},{4,5},{5,4},{6,7},{7,6},{8,9},{9,8},{10,11... | collective-permute-start | bytes 1769480 | tf_op jit(solution)/shard_map/ppermute | solution.py:107
  144.1 2.0 %collective-permute-start.31 = (bf16[384,768]{1,0:T(8,128)(2,1)S(1)}, bf16[384,768]{1,0:T(8,128)(2,1)S(1)}, u32[]{:S(2)}, u32[]{:S(2)}) collective-permute-start(bf16[384,768]{1,0:T(8,128)(2,1)S(1)} %collective-permute-done.29.refs_7_), channel_id=1, source_target_pairs={{0,1},{1,0},{2,3},{3,2},{4,5},{5,4},{6,7},{7,6},{8,9},{9,8},{10,11... | collective-permute-start | bytes 1769480 | tf_op jit(solution)/shard_map/ppermute | solution.py:107
  148.6 7.0 %collective-permute-start.32 = (bf16[2,64,768]{2,1,0:T(8,128)(2,1)S(1)}, bf16[2,64,768]{2,1,0:T(8,128)(2,1)S(1)}, u32[]{:S(2)}, u32[]{:S(2)}) collective-permute-start(bf16[2,64,768]{2,1,0:T(8,128)(2,1)S(1)} %get-tuple-element.56), channel_id=1, source_target_pairs={{0,2},{2,0},{1,3},{3,1},{4,6},{6,4},{5,7},{7,5},{8,10},{10,8},{9,1... | collective-permute-start | bytes 589832 | tf_op jit(solution)/shard_map/ppermute | solution.py:107
  150.1 18.5 %collective-permute-start.33 = (bf16[2,64,768]{2,1,0:T(8,128)(2,1)S(1)}, bf16[2,64,768]{2,1,0:T(8,128)(2,1)S(1)}, u32[]{:S(2)}, u32[]{:S(2)}) collective-permute-start(bf16[2,64,768]{2,1,0:T(8,128)(2,1)S(1)} %get-tuple-element.57), channel_id=1, source_target_pairs={{0,8},{4,12},{8,0},{12,4},{1,9},{5,13},{9,1},{13,5},{2,10},{6,14},... | collective-permute-start | bytes 589832 | tf_op jit(solution)/shard_map/ppermute | solution.py:107
  154.4 17.4 %collective-permute-start.34 = (bf16[2,64,768]{2,1,0:T(8,128)(2,1)S(1)}, bf16[2,64,768]{2,1,0:T(8,128)(2,1)S(1)}, u32[]{:S(2)}, u32[]{:S(2)}) collective-permute-start(bf16[2,64,768]{2,1,0:T(8,128)(2,1)S(1)} %get-tuple-element.58), channel_id=1, source_target_pairs={{0,10},{2,8},{4,14},{6,12},{8,2},{10,0},{12,6},{14,4},{1,11},{3,9}... | collective-permute-start | bytes 589832 | tf_op jit(solution)/shard_map/ppermute | solution.py:412
  (2 other events, 1.6 us)

commit v12 on v10

--- a/solution.py
+++ b/solution.py
@@ -127,41 +127,28 @@
     )(*prefetch, *operands)
 
 
-def assemble(place, mine, theirs, count):
-    width, rows = mine[0].shape[1], len(mine)
-
-    def kernel(place_ref, *refs):
-        row, frame = place_ref[0], place_ref[2]
-        for s in range(rows):
-            refs[-1][row ^ s, frame] = refs[s][:count]
-            refs[-1][row ^ s, 1 - frame] = refs[rows + s][:count]
-
-    return call(
-        kernel,
-        jax.ShapeDtypeStruct((rows, 2, count, width), jnp.bfloat16),
-        [place],
-        [*mine, *theirs],
-        read=8 * rows * count * width,
-        limit=WHOLE_VMEM_BYTES,
-    )
-
-
-def project(place, tokens, chunks):
-    rows, _, count, width = tokens.shape
+def project(place, mine, theirs, chunks):
+    rows, (count, width) = len(mine), mine[0].shape
     _, half, cols = chunks[0][0].shape
     slices = len(chunks)
     flat = [w for of_round in chunks for w in of_round]
-    total_rows = rows * 2 * count
-
-    def kernel(place_ref, x_ref, *refs):
-        row, group, core = place_ref[0], place_ref[1], place_ref[3]
-        w_refs = refs[: len(flat)]
-        q_keep, kv_keep, send, total = refs[len(flat) :]
+
+    def kernel(place_ref, *refs):
+        row, group, frame, core = (place_ref[i] for i in range(4))
+        x_refs, w_refs = refs[: 2 * rows], refs[2 * rows : 2 * rows + len(flat)]
+        q_keep, kv_keep, send, x_all, total, sems = refs[2 * rows + len(flat) :]
+        copies = []
+        for i, x_ref in enumerate(x_refs):
+            to = x_all.at[row ^ (i % rows), (frame + i // rows) % 2]
+            copies.append(pltpu.make_async_copy(x_ref, to, sems.at[i]))
+            copies[-1].start()
+        for copy in copies:
+            copy.wait()
         acc = None
         for k in range(slices):
             for g in range(2):
                 at = (row + slices - k) % slices * (2 * half) + (group + g) % 2 * half
-                piece = x_ref[:, :, :, pl.ds(pl.multiple_of(at, half), half)].reshape(-1, half)
+                piece = x_all[:, :, :, pl.ds(pl.multiple_of(at, half), half)].reshape(-1, half)
                 w_ref = w_refs[2 * k + g]
                 weight = jnp.concatenate([w_ref[part] for part in range(3)], axis=1)
                 term = jnp.dot(piece, weight, preferred_element_type=jnp.float32)
@@ -177,21 +164,29 @@
             at = slice(f * cols, (f + 1) * cols)
             send[:, 2 * count :, at] = total[:, f, pl.ds(other, BS), :].astype(jnp.bfloat16)
 
-    flops = 2 * total_rows * width * 3 * cols
-    return call(
+    vmem, anywhere = pl.BlockSpec(memory_space=pltpu.VMEM), pl.BlockSpec(memory_space=pl.ANY)
+    flops = 2 * rows * 2 * count * width * 3 * cols
+    return pl.pallas_call(
         kernel,
-        (
+        out_shape=(
             jax.ShapeDtypeStruct((rows, 2 * BS, cols), jnp.float32),
             jax.ShapeDtypeStruct((rows, 2 * count, 2 * cols), jnp.float32),
             jax.ShapeDtypeStruct((rows, 2 * count + BS, 2 * cols), jnp.bfloat16),
         ),
-        [place],
-        [tokens, *flat],
-        scratch=[pltpu.VMEM((rows, 2, count, cols), jnp.float32)],
-        flops=8 * flops,
-        read=flops // 300,
-        limit=WHOLE_VMEM_BYTES,
-    )
+        grid_spec=pltpu.PrefetchScalarGridSpec(
+            num_scalar_prefetch=1,
+            grid=(),
+            in_specs=[anywhere] * (2 * rows) + [vmem] * len(flat),
+            out_specs=(vmem, vmem, vmem),
+            scratch_shapes=[
+                pltpu.VMEM((rows, 2, count, width), jnp.bfloat16),
+                pltpu.VMEM((rows, 2, count, cols), jnp.float32),
+                pltpu.SemaphoreType.DMA((2 * rows,)),
+            ],
+        ),
+        compiler_params=pltpu.CompilerParams(vmem_limit_bytes=VMEM_BYTES),
+        cost_estimate=pl.CostEstimate(flops=8 * flops, bytes_accessed=flops // 300, transcendentals=0),
+    )(place, *mine, *theirs, *flat)
 
 
 def attend_all(place, members, counts, queries, keyvals, more, earlier=()):
@@ -248,7 +243,6 @@
         ],
         flops=4 * blocks * block_len * MAXB * block_len * cols,
         read=16 * blocks * block_len * cols,
-        limit=WHOLE_VMEM_BYTES,
     )
 
 
@@ -322,7 +316,6 @@
     rows_n, heads_n = lax.axis_size("rows"), lax.axis_size("heads")
     group, row = lax.axis_index("groups"), lax.axis_index("rows")
     frame, core = lax.axis_index("frames"), lax.axis_index("heads")
-    count = latents.shape[1]
     depth, _, local_cols = w_qkv.shape
     span = rows_n // heads_n
     cols = local_cols // span
@@ -345,48 +338,44 @@
         return lax.ppermute(after(value, *others) if others else value, ("rows", "heads"), pairs)
 
     tables = jnp.concatenate([win_blocks, win_counts[:, None], block_window[:, None]], axis=1)
-    tables = jnp.pad(tables, ((0, 6), (0, span * depth - MAXB - 2))).astype(latents.dtype)
+    found = [tables] + [swap(tables, "rows", s) for s in range(1, rows_n)]
+    tables = jnp.stack(found)[row ^ jnp.arange(rows_n)].reshape(rows_n * heads_n, MAXB + 2)
+    windows = lax.dynamic_index_in_dim(
+        tables[:, MAXB + 1].reshape(rows_n, heads_n), core, axis=1, keepdims=False
+    )
+    picked = tables[windows]
+    members, counts = picked[:, :MAXB].reshape(-1), picked[:, MAXB]
+
     mine = lax.dynamic_slice_in_dim(latents[0], core * span * depth, span * depth, axis=1)
-    mine = jnp.concatenate([mine, tables], axis=0)
-
     near, mine_x = swap(mine, "rows"), swap(mine, "frames")
     here, there = [reshard(0)], []
+    far_2 = swap(after(mine, members, counts), "rows", 2)
+    here.append(reshard(1, near, mine_x, here[0]))
     near_x = swap(near, "frames")
     across = swap(after(w_out, near), "heads")
-    here.append(reshard(1, near, mine_x))
     there.append(swap(here[0], "groups"))
-    far_2 = swap(after(mine, here[0]), "rows", 2)
+    far_3 = swap(after(mine, here[0], near_x), "rows", 3)
+    here.append(reshard(2, far_2, across))
+    far_2x = swap(far_2, "frames")
+    here.append(reshard(3, here[1], there[0], far_2x))
     there.append(swap(here[1], "groups"))
-    far_3 = swap(after(mine, here[1], near_x), "rows", 3)
-    far_2x = swap(far_2, "frames")
+    far_3x = swap(far_3, "frames")
+    there += [swap(here[2], "groups"), swap(here[3], "groups")]
+
     out_half = lax.dynamic_slice_in_dim(w_out, group * cols, cols, axis=0)
-    beside = [swap(after(out_half, here[0]), "rows")]
-    beside.append(swap(beside[0], "groups"))
-    here.append(reshard(2, far_2, there[0], there[1], across, beside[0]))
-    far_3x = swap(far_3, "frames")
-    here.append(reshard(3, far_3, far_2x, beside[1]))
-    there += [swap(here[2], "groups"), swap(here[3], "groups")]
-    pieces = [mine, near, far_2, far_3]
-    tokens = assemble(place, pieces, [mine_x, near_x, far_2x, far_3x], count)
-
-    found = jnp.stack([x[count : count + heads_n, : MAXB + 2] for x in pieces]).astype(jnp.int32)
-    tables = found[row ^ jnp.arange(rows_n)].reshape(rows_n * heads_n, MAXB + 2)
-    windows = lax.dynamic_index_in_dim(
-        tables[:, MAXB + 1].reshape(rows_n, heads_n), core, axis=1, keepdims=False
-    )
-    picked = tables[windows]
-    members, counts = picked[:, :MAXB].reshape(-1), picked[:, MAXB]
-
-    chunks = [(here[0], there[0]), (here[1], after(there[1], there[2], here[3]))]
-    first = project(place, tokens, chunks)
+    beside = [swap(after(out_half, here[3]), "rows")]
+
+    pieces = [mine, near, far_2, far_3], [mine_x, near_x, far_2x, far_3x]
+    first = project(place, *pieces, [(here[0], there[0]), (here[1], after(there[1], there[2]))])
     first_more = swap(first[2], "heads")
-    second = project(place, tokens, [(here[2], there[2]), (here[3], after(there[3], first[2]))])
+    second = project(place, *pieces, [(here[2], there[2]), (here[3], after(there[3], first[2]))])
     second_more = swap(second[2], "heads")
-    attended = attend_all(place, members, counts, *first[:2], first_more)
+    attended = attend_all(place, members, counts, first[0], after(first[1], beside[0]), first_more)
+    beside.append(swap(after(beside[0], attended[0]), "groups"))
     same, diff = attend_all(place, members, counts, *second[:2], second_more, attended)
     attended = [same] + [swap(same if s % 2 == 0 else diff, "rows", s) for s in range(1, rows_n)]
     halves = [w_out[:cols], w_out[cols:], *beside]
-    beside_across = [swap(part, "heads") for part in beside]
+    beside_across = [swap(part, "heads") for part in (beside[0], after(beside[1], *attended[1:]))]
     keep, over_x, over_z, over_both = mix(
         place, attended, [*halves, across[:cols], across[cols:], *beside_across]
     )

time: 183 us -> 181 us (0.989)
  waiting for transfers between devices: 77.6 us -> 107 us
  starting transfers between devices: 53.6 us -> 35.6 us
  Pallas kernels: 35.4 us -> 21.8 us
  local copies, waits for them, and re-layouts: 11.8 us -> 15.4 us
  other arithmetic: 3.97 us -> 0.55 us
    ppermute x23 -> x26, waiting for transfers between devices: 60.4 us -> 96.1 us  [swap(): return lax.ppermute(value, axis, [(i, i ^ step) for i in range(peers)])]
    pallas_call x7 -> x4, Pallas kernels: 35.4 us -> 9.84 us  [call(): pl.pallas_call(kernel, out_shape=out_shape, grid_spec=pltpu.PrefetchScala...]
    ppermute x4, starting transfers between devices: 16.1 us -> 2.08 us  [reshard(): lax.ppermute(after(value, *others) if others else value, ('rows', 'heads'...]
    pallas_call x0 -> x2, Pallas kernels: none -> 12 us  [project(): pl.pallas_call(kernel, out_shape=(jax.ShapeDtypeStruct((rows, 2 * BS, col...]
    unnamed x26 -> x28, local copies, waits for them, and re-layouts: 1.55 us -> 8.07 us
    ppermute x4, waiting for transfers between devices: 13.3 us -> 7.49 us  [reshard(): lax.ppermute(after(value, *others) if others else value, ('rows', 'heads'...]
    ppermute x1, starting transfers between devices: 2.63 us -> 0.01 us  [by_heads(): lax.ppermute(over_both, ('rows', 'frames'), [(2 * r + f, 2 * (r ^ 2) + 1...]
    another operation x3 -> x0, local copies, waits for them, and re-layouts: 1.98 us -> none  [by_heads(): jnp.stack([x[count:count + heads_n, :MAXB + 2] for x in pieces])]
  transfers between devices with their start and end apart: 28 -> 31, of which waited for: 11 -> 15; matrix products, arithmetic and copies ran while one was open for 6% -> 4% of each run, Pallas kernels for 17% -> 10%
where the time goes in v12:
time: 181 us
  waiting for transfers between devices  107 us (59%)
  starting transfers between devices  35.6 us (20%)
  Pallas kernels  21.8 us (12%)
  local copies, waits for them, and re-layouts  15.4 us (9%)
    ppermute x26, waiting for transfers between devices, swap(): return lax.ppermute(value, axis, [(i, i ^ step) for i in range(peers)])  96.1 us
    ppermute x26, starting transfers between devices, swap(): return lax.ppermute(value, axis, [(i, i ^ step) for i in range(peers)])  33.5 us
    pallas_call x2, Pallas kernels, project(): pl.pallas_call(kernel, out_shape=(jax.ShapeDtypeStruct((rows, 2 * BS, col...  12 us
    pallas_call x4, Pallas kernels, call(): pl.pallas_call(kernel, out_shape=out_shape, grid_spec=pltpu.PrefetchScala...  9.84 us
    unnamed x28, local copies, waits for them, and re-layouts  8.07 us
    ppermute x4, waiting for transfers between devices, reshard(): lax.ppermute(after(value, *others) if others else value, ('rows', 'heads'...  7.49 us
    dynamic_slice x2, local copies, waits for them, and re-layouts, reshard(): lax.dynamic_slice(w_qkv.transpose(1, 0, 2), (0, group * half, (k + row) %...  4 us
  transfers between devices with their start and end apart: 31, of which 15 were waited for; matrix products, arithmetic and copies ran while one was open for 4% of the time, Pallas kernels for 10%

profile of v12, /device:TPU:0, one launch (start us, length us, event | category | flops | bytes accessed | tf_op | source)
XLA Modules:
  0.0 180.6 jit_solution(14944275080572889571)
XLA Ops:
  0.0 1.1 copy-done
  1.2 3.1 %collective-permute-start.3 = (bf16[128,1536]{1,0:T(8,128)(2,1)S(1)}, bf16[128,1536]{1,0:T(8,128)(2,1)S(1)}, u32[]{:S(2)}, u32[]{:S(2)}) collective-permute-start(bf16[128,1536]{1,0:T(8,128)(2,1)S(1)} %dynamic-slice_bitcast_fusion.2.refs_0_), channel_id=1, source_target_pairs={{0,4},{4,0},{8,12},{12,8},{1,5},{5,1},{9,13},{13,9},{2,6},{6,2},{1... | collective-permute-start | bytes 1179656 | tf_op jit(solution)/shard_map/ppermute | solution.py:107
  4.3 2.2 %dynamic-slice_bitcast_fusion = (bf16[3,384,256]{2,1,0:T(8,128)(2,1)}, bf16[3,384,256]{2,1,0:T(8,128)(2,1)S(1)}) fusion(bf16[768,3,768]{2,0,1:T(8,128)(2,1)} %param.7, s32[]{:T(128)S(6)} %select_n.59, s32[]{:T(128)S(6)} %select_n.65, s32[]{:T(128)S(6)} %select_n.61), kind=kLoop, calls=%fused_computation.2 | loop fusion | bytes 2359308 | tf_op jit(solution)/shard_map/dynamic_slice | solution.py:330
  7.4 3.8 %collective-permute-start.1 = (s32[2,6]{1,0:T(2,128)S(1)}, s32[2,6]{1,0:T(2,128)S(1)}, u32[]{:S(2)}, u32[]{:S(2)}) collective-permute-start(s32[2,6]{1,0:T(2,128)S(1)} %pad_add_fusion.1), channel_id=1, source_target_pairs={{0,8},{4,12},{8,0},{12,4},{1,9},{5,13},{9,1},{13,5},{2,10},{6,14},... | collective-permute-start | bytes 152 | tf_op jit(solution)/shard_map/ppermute | solution.py:107
  11.7 1.5 collective-permute-start.8
  13.3 3.3 %collective-permute-done.3.refs_1_ = bf16[128,1536]{1,0:T(8,128)(2,1)S(1)} collective-permute-done((bf16[128,1536]{1,0:T(8,128)(2,1)S(1)}, bf16[128,1536]{1,0:T(8,128)(2,1)S(1)}, u32[]{:S(2)}, u32[]{:S(2)}) %collective-permute-start.3) | collective-permute-done | bytes 393248 | tf_op jit(solution)/shard_map/ppermute | solution.py:107
  16.7 8.5 %collective-permute-done.1 = s32[2,6]{1,0:T(2,128)S(1)} collective-permute-done((s32[2,6]{1,0:T(2,128)S(1)}, s32[2,6]{1,0:T(2,128)S(1)}, u32[]{:S(2)}, u32[]{:S(2)}) %collective-permute-start.1) | collective-permute-done | bytes 80 | tf_op jit(solution)/shard_map/ppermute | solution.py:107
  25.2 5.4 %collective-permute-done.2 = s32[2,6]{1,0:T(2,128)S(1)} collective-permute-done((s32[2,6]{1,0:T(2,128)S(1)}, s32[2,6]{1,0:T(2,128)S(1)}, u32[]{:S(2)}, u32[]{:S(2)}) %collective-permute-start.2) | collective-permute-done | bytes 80 | tf_op jit(solution)/shard_map/ppermute | solution.py:107
  32.3 1.5 collective-permute-start.6
  33.8 0.8 copy-done.4
  34.8 1.6 collective-permute-start.15
  36.4 4.6 %collective-permute-done.6.refs_5_ = bf16[128,1536]{1,0:T(8,128)(2,1)S(1)} collective-permute-done((bf16[128,1536]{1,0:T(8,128)(2,1)S(1)}, bf16[128,1536]{1,0:T(8,128)(2,1)S(1)}, u32[]{:S(2)}, u32[]{:S(2)}) %collective-permute-start.6) | collective-permute-done | bytes 393248 | tf_op jit(solution)/shard_map/ppermute | solution.py:107
  40.9 0.7 copy-done.6
  41.7 3.1 %collective-permute-start.7 = (bf16[128,1536]{1,0:T(8,128)(2,1)S(1)}, bf16[128,1536]{1,0:T(8,128)(2,1)}, u32[]{:S(2)}, u32[]{:S(2)}) collective-permute-start(bf16[128,1536]{1,0:T(8,128)(2,1)S(1)} %dynamic-slice_bitcast_fusion.2.refs_0_), channel_id=1, source_target_pairs={{0,12},{4,8},{8,4},{12,0},{1,13},{5,9},{9,5},{13,1},{2,14},{6,10},... | collective-permute-start | bytes 1179656 | tf_op jit(solution)/shard_map/ppermute | solution.py:107
  44.8 29.9 %collective-permute-done.4.refs_2_ = bf16[128,1536]{1,0:T(8,128)(2,1)} collective-permute-done((bf16[128,1536]{1,0:T(8,128)(2,1)S(1)}, bf16[128,1536]{1,0:T(8,128)(2,1)}, u32[]{:S(2)}, u32[]{:S(2)}) %collective-permute-start.4) | collective-permute-done | bytes 393248 | tf_op jit(solution)/shard_map/ppermute | solution.py:107
  75.2 1.8 %dynamic-slice_bitcast_fusion.3 = (bf16[3,384,128]{2,1,0:T(8,128)(2,1)}, bf16[3,384,128]{2,1,0:T(8,128)(2,1)S(1)}) fusion(bf16[768,3,768]{2,0,1:T(8,128)(2,1)} %param.7, s32[]{:T(128)S(6)} %select_n.59, s32[]{:T(128)S(6)} %select_n.64, s32[]{:T(128)S(6)} %select_n.62), kind=kLoop, calls=%fused_computation.5 | loop fusion | bytes 1179660 | tf_op jit(solution)/shard_map/dynamic_slice | solution.py:330
  77.0 1.4 collective-permute-start.12
  78.4 1.5 collective-permute-start.18
  80.0 1.5 collective-permute-start.10
  81.5 1.2 collective-permute-done.9.refs_6_
  82.7 0.7 copy-done.8
  83.4 2.5 %collective-permute-start.13 = (bf16[3,384,128]{2,1,0:T(8,128)(2,1)}, bf16[3,384,128]{2,1,0:T(8,128)(2,1)}, u32[]{:S(2)}, u32[]{:S(2)}) collective-permute-start(bf16[3,384,128]{2,1,0:T(8,128)(2,1)} %collective-permute-done.12.refs_8_), channel_id=1, source_target_pairs={{0,16},{16,0},{1,17},{17,1},{2,18},{18,2},{3,19},{19,3},{4,20},{20... | collective-permute-start | bytes 884744 | tf_op jit(solution)/shard_map/ppermute | solution.py:107
  86.0 7.5 %collective-permute-done.16.refs_10_ = bf16[3,384,128]{2,1,0:T(8,128)(2,1)} collective-permute-done((bf16[3,384,128]{2,1,0:T(8,128)(2,1)}, bf16[3,384,128]{2,1,0:T(8,128)(2,1)}, u32[]{:S(2)}, u32[]{:S(2)}) %collective-permute-start.16) | collective-permute-done | bytes 294944 | tf_op jit(solution)/shard_map/ppermute | solution.py:338
  93.5 1.4 collective-permute-start.17
  95.0 6.1 %collective-permute-done.13.refs_9_ = bf16[3,384,128]{2,1,0:T(8,128)(2,1)} collective-permute-done((bf16[3,384,128]{2,1,0:T(8,128)(2,1)}, bf16[3,384,128]{2,1,0:T(8,128)(2,1)}, u32[]{:S(2)}, u32[]{:S(2)}) %collective-permute-start.13) | collective-permute-done | bytes 294944 | tf_op jit(solution)/shard_map/ppermute | solution.py:107
  101.0 1.0 copy-done.2
  102.0 1.0 copy-done.5
  103.0 1.0 copy-done.7
  104.0 1.0 copy-done.9
  105.0 6.1 %shard_map.64 = (f32[4,128,256]{2,1,0:T(8,128)S(1)}, f32[4,256,512]{2,1,0:T(8,128)S(1)}, bf16[4,320,512]{2,1,0:T(8,128)(2,1)S(1)}) custom-call(s32[4]{0:T(128)S(1)} %pad_add_fusion.2.place_ref, bf16[128,1536]{1,0:T(8,128)(2,1)S(1)} %dynamic-slice_bitcast_fusion.2.refs_0_, bf16[128,1536]{1,0:T(8,128)(2,1)S(1)} %copy-done.2, ...), custom_call_target="tpu_custom_call" | custom-call | flops 19327352832 | bytes 8053063 | tf_op jit(solution)/shard_map/pallas_call | solution.py:169
  112.2 5.9 %shard_map.65 = (f32[4,128,128]{2,1,0:T(8,128)S(1)}, f32[4,256,256]{2,1,0:T(8,128)S(1)}, bf16[4,320,256]{2,1,0:T(8,128)(2,1)S(1)}) custom-call(s32[4]{0:T(128)S(1)} %pad_add_fusion.2.place_ref, bf16[128,1536]{1,0:T(8,128)(2,1)S(1)} %dynamic-slice_bitcast_fusion.2.refs_0_, bf16[128,1536]{1,0:T(8,128)(2,1)S(1)} %copy-done.3, ...), custom_call_target="tpu_custom_call" | custom-call | flops 9663676416 | bytes 4026531 | tf_op jit(solution)/shard_map/pallas_call | solution.py:169
  118.1 9.0 %collective-permute-done.20.refs_6_ = bf16[384,768]{1,0:T(8,128)(2,1)S(1)} collective-permute-done((bf16[384,768]{1,0:T(8,128)(2,1)S(1)}, bf16[384,768]{1,0:T(8,128)(2,1)S(1)}, u32[]{:S(2)}, u32[]{:S(2)}) %collective-permute-start.20) | collective-permute-done | bytes 589856 | tf_op jit(solution)/shard_map/ppermute | solution.py:107
  127.2 3.8 %shard_map.66 = (bf16[2,128,256]{2,1,0:T(8,128)(2,1)S(1)}, bf16[2,128,256]{2,1,0:T(8,128)(2,1)S(1)}) custom-call(s32[4]{0:T(128)S(1)} %pad_add_fusion.2.place_ref, s32[16]{0:T(128)S(1)} %reshape.24.members_ref, s32[4]{0:T(128)S(1)} %slice_reduce_fusion.1.counts_ref, f32[4,128,256]{2,1,0:T(8,128)S(1)} %get-tuple-element.43.q_ref, ...), custom_call_target="tpu_custom_call" | custom-call | flops 268435456 | bytes 2097152 | tf_op jit(solution)/shard_map/pallas_call | solution.py:115
  131.0 1.6 collective-permute-start.25
  132.6 2.2 %shard_map.67 = (bf16[2,128,384]{2,1,0:T(8,128)(2,1)S(1)}, bf16[2,128,384]{2,1,0:T(8,128)(2,1)S(1)}) custom-call(s32[4]{0:T(128)S(1)} %pad_add_fusion.2.place_ref, s32[16]{0:T(128)S(1)} %reshape.24.members_ref, s32[4]{0:T(128)S(1)} %slice_reduce_fusion.1.counts_ref, f32[4,128,128]{2,1,0:T(8,128)S(1)} %get-tuple-element.40.q_ref, ...), custom_call_target="tpu_custom_call" | custom-call | flops 134217728 | bytes 1048576 | tf_op jit(solution)/shard_map/pallas_call | solution.py:115
  134.8 0.9 collective-permute-start.23
  135.7 1.8 %collective-permute-start.24 = (bf16[2,128,384]{2,1,0:T(8,128)(2,1)S(1)}, bf16[2,128,384]{2,1,0:T(8,128)(2,1)S(1)}, u32[]{:S(2)}, u32[]{:S(2)}) collective-permute-start(bf16[2,128,384]{2,1,0:T(8,128)(2,1)S(1)} %get-tuple-element.50), channel_id=1, source_target_pairs={{0,12},{4,8},{8,4},{12,0},{1,13},{5,9},{9,5},{13,1},{2,14},{6,10},... | collective-permute-start | bytes 589832 | tf_op jit(solution)/shard_map/ppermute | solution.py:107
  137.5 0.8 collective-permute-start.22
  138.3 12.1 %collective-permute-done.23.refs_2_ = bf16[2,128,384]{2,1,0:T(8,128)(2,1)S(1)} collective-permute-done((bf16[2,128,384]{2,1,0:T(8,128)(2,1)S(1)}, bf16[2,128,384]{2,1,0:T(8,128)(2,1)S(1)}, u32[]{:S(2)}, u32[]{:S(2)}) %collective-permute-start.23) | collective-permute-done | bytes 196640 | tf_op jit(solution)/shard_map/ppermute | solution.py:107
  150.5 1.2 collective-permute-done.22.refs_1_
  151.7 1.3 fusion.2
  153.7 2.5 %shard_map.68 = (f32[2,64,768]{2,1,0:T(8,128)S(1)}, bf16[2,64,768]{2,1,0:T(8,128)(2,1)S(1)}, bf16[2,64,768]{2,1,0:T(8,128)(2,1)S(1)}, bf16[2,64,768]{2,1,0:T(8,128)(2,1)S(1)}) custom-call(s32[4]{0:T(128)S(1)} %pad_add_fusion.2.place_ref, bf16[2,128,384]{2,1,0:T(8,128)(2,1)S(1)} %get-tuple-element.49.refs_0_, ...), custom_call_target="tpu_custom_call" | custom-call | flops 1207959552 | bytes 4718592 | tf_op jit(solution)/shard_map/pallas_call | solution.py:115
  156.2 1.6 collective-permute-start.28
  157.7 4.0 %collective-permute-start.29 = (bf16[2,64,768]{2,1,0:T(8,128)(2,1)S(1)}, bf16[2,64,768]{2,1,0:T(8,128)(2,1)S(1)}, u32[]{:S(2)}, u32[]{:S(2)}) collective-permute-start(bf16[2,64,768]{2,1,0:T(8,128)(2,1)S(1)} %get-tuple-element.55), channel_id=1, source_target_pairs={{0,8},{4,12},{8,0},{12,4},{1,9},{5,13},{9,1},{13,5},{2,10},{6,14},... | collective-permute-start | bytes 589832 | tf_op jit(solution)/shard_map/ppermute | solution.py:107
  161.7 1.5 collective-permute-done.28.x_ref
  163.2 12.7 %collective-permute-done.29.z_ref = bf16[2,64,768]{2,1,0:T(8,128)(2,1)S(1)} collective-permute-done((bf16[2,64,768]{2,1,0:T(8,128)(2,1)S(1)}, bf16[2,64,768]{2,1,0:T(8,128)(2,1)S(1)}, u32[]{:S(2)}, u32[]{:S(2)}) %collective-permute-start.29) | collective-permute-done | bytes 196640 | tf_op jit(solution)/shard_map/ppermute | solution.py:107
  175.9 3.4 %collective-permute-done.30.both_ref = bf16[2,64,768]{2,1,0:T(8,128)(2,1)S(1)} collective-permute-done((bf16[2,64,768]{2,1,0:T(8,128)(2,1)S(1)}, bf16[2,64,768]{2,1,0:T(8,128)(2,1)S(1)}, u32[]{:S(2)}, u32[]{:S(2)}) %collective-permute-start.30) | collective-permute-done | bytes 196640 | tf_op jit(solution)/shard_map/ppermute | solution.py:384
  179.3 1.4 shard_map.69
  (69 shorter events, 6.0 us)
Async XLA Ops:
  0.0 1.1 copy-start
  1.2 6.0 %copy-start.12 = (s32[2]{0:T(128)S(1)}, s32[2]{0:T(128)}, u32[]{:S(2)}) copy-start(s32[2]{0:T(128)} %param.10) | copy-start | bytes 28
  1.2 6.1 %copy-start.13 = (s32[2]{0:T(128)S(1)}, s32[2]{0:T(128)}, u32[]{:S(2)}) copy-start(s32[2]{0:T(128)} %param.11) | copy-start | bytes 28
  1.2 6.2 %copy-start.11 = (s32[2,4]{1,0:T(2,128)S(1)}, s32[2,4]{1,0:T(2,128)}, u32[]{:S(2)}) copy-start(s32[2,4]{1,0:T(2,128)} %param.9) | copy-start | bytes 100
  1.2 15.4 %collective-permute-start.3 = (bf16[128,1536]{1,0:T(8,128)(2,1)S(1)}, bf16[128,1536]{1,0:T(8,128)(2,1)S(1)}, u32[]{:S(2)}, u32[]{:S(2)}) collective-permute-start(bf16[128,1536]{1,0:T(8,128)(2,1)S(1)} %dynamic-slice_bitcast_fusion.2.refs_0_), channel_id=1, source_target_pairs={{0,4},{4,0},{8,12},{12,8},{1,5},{5,1},{9,13},{13,9},{2,6},{6,2},{1... | collective-permute-start | bytes 1179656 | tf_op jit(solution)/shard_map/ppermute | solution.py:107
  6.5 28.1 %collective-permute-start.5 = (bf16[3,384,256]{2,1,0:T(8,128)(2,1)S(1)}, bf16[3,384,256]{2,1,0:T(8,128)(2,1)S(1)}, u32[]{:S(2)}, u32[]{:S(2)}) collective-permute-start(bf16[3,384,256]{2,1,0:T(8,128)(2,1)S(1)} %get-tuple-element.58), channel_id=1, source_target_pairs={{0,0},{1,8},{4,4},{5,12},{8,1},{9,9},{12,5},{13,13},{2,2},{3,10},{... | collective-permute-start | bytes 1769480 | tf_op jit(solution)/shard_map/ppermute | solution.py:338
  7.4 17.8 %collective-permute-start.1 = (s32[2,6]{1,0:T(2,128)S(1)}, s32[2,6]{1,0:T(2,128)S(1)}, u32[]{:S(2)}, u32[]{:S(2)}) collective-permute-start(s32[2,6]{1,0:T(2,128)S(1)} %pad_add_fusion.1), channel_id=1, source_target_pairs={{0,8},{4,12},{8,0},{12,4},{1,9},{5,13},{9,1},{13,5},{2,10},{6,14},... | collective-permute-start | bytes 152 | tf_op jit(solution)/shard_map/ppermute | solution.py:107
  11.2 14.0 %collective-permute-start = (s32[2,6]{1,0:T(2,128)S(1)}, s32[2,6]{1,0:T(2,128)S(1)}, u32[]{:S(2)}, u32[]{:S(2)}) collective-permute-start(s32[2,6]{1,0:T(2,128)S(1)} %pad_add_fusion.1), channel_id=1, source_target_pairs={{0,4},{4,0},{8,12},{12,8},{1,5},{5,1},{9,13},{13,9},{2,6},{6,2},{1... | collective-permute-start | bytes 152 | tf_op jit(solution)/shard_map/ppermute | solution.py:107
  11.7 22.1 %collective-permute-start.8 = (bf16[128,1536]{1,0:T(8,128)(2,1)S(1)}, bf16[128,1536]{1,0:T(8,128)(2,1)S(1)}, u32[]{:S(2)}, u32[]{:S(2)}) collective-permute-start(bf16[128,1536]{1,0:T(8,128)(2,1)S(1)} %dynamic-slice_bitcast_fusion.2.refs_0_), channel_id=1, source_target_pairs={{0,2},{2,0},{1,3},{3,1},{4,6},{6,4},{5,7},{7,5},{8,10},{10,8},{9,1... | collective-permute-start | bytes 1179656 | tf_op jit(solution)/shard_map/ppermute | solution.py:107
  16.6 61.8 %copy-start.1 = (bf16[128,1536]{1,0:T(8,128)(2,1)}, bf16[128,1536]{1,0:T(8,128)(2,1)S(1)}, u32[]{:S(2)}) copy-start(bf16[128,1536]{1,0:T(8,128)(2,1)S(1)} %collective-permute-done.3.refs_1_) | copy-start | bytes 1179652
  16.6 60.5 %collective-permute-start.11 = (bf16[768,768]{1,0:T(8,128)(2,1)}, bf16[768,768]{1,0:T(8,128)(2,1)}, u32[]{:S(2)}, u32[]{:S(2)}) collective-permute-start(bf16[768,768]{1,0:T(8,128)(2,1)} %param.8), channel_id=1, source_target_pairs={{0,1},{1,0},{2,3},{3,2},{4,5},{5,4},{6,7},{7,6},{8,9},{9,8},{10,11... | collective-permute-start | bytes 3538952 | tf_op jit(solution)/shard_map/ppermute | solution.py:107
  25.2 5.4 %collective-permute-start.2 = (s32[2,6]{1,0:T(2,128)S(1)}, s32[2,6]{1,0:T(2,128)S(1)}, u32[]{:S(2)}, u32[]{:S(2)}) collective-permute-start(s32[2,6]{1,0:T(2,128)S(1)} %pad_add_fusion.1), channel_id=1, source_target_pairs={{0,12},{4,8},{8,4},{12,0},{1,13},{5,9},{9,5},{13,1},{2,14},{6,10},... | collective-permute-start | bytes 152 | tf_op jit(solution)/shard_map/ppermute | solution.py:107
  32.3 8.7 %collective-permute-start.6 = (bf16[128,1536]{1,0:T(8,128)(2,1)S(1)}, bf16[128,1536]{1,0:T(8,128)(2,1)S(1)}, u32[]{:S(2)}, u32[]{:S(2)}) collective-permute-start(bf16[128,1536]{1,0:T(8,128)(2,1)S(1)} %collective-permute-done.3.refs_1_), channel_id=1, source_target_pairs={{0,2},{2,0},{1,3},{3,1},{4,6},{6,4},{5,7},{7,5},{8,10},{10,8},{9,1... | collective-permute-start | bytes 1179656 | tf_op jit(solution)/shard_map/ppermute | solution.py:107
  33.8 0.8 copy-start.4
  34.5 43.9 %collective-permute-start.14 = (bf16[3,384,256]{2,1,0:T(8,128)(2,1)}, bf16[3,384,256]{2,1,0:T(8,128)(2,1)S(1)}, u32[]{:S(2)}, u32[]{:S(2)}) collective-permute-start(bf16[3,384,256]{2,1,0:T(8,128)(2,1)} %get-tuple-element.35), channel_id=1, source_target_pairs={{0,4},{1,12},{4,0},{5,8},{8,5},{9,13},{12,1},{13,9},{2,6},{3,14},{... | collective-permute-start | bytes 1769480 | tf_op jit(solution)/shard_map/ppermute | solution.py:338
  34.7 40.0 %collective-permute-start.4 = (bf16[128,1536]{1,0:T(8,128)(2,1)S(1)}, bf16[128,1536]{1,0:T(8,128)(2,1)}, u32[]{:S(2)}, u32[]{:S(2)}) collective-permute-start(bf16[128,1536]{1,0:T(8,128)(2,1)S(1)} %dynamic-slice_bitcast_fusion.2.refs_0_), channel_id=1, source_target_pairs={{0,8},{4,12},{8,0},{12,4},{1,9},{5,13},{9,1},{13,5},{2,10},{6,14},... | collective-permute-start | bytes 1179656 | tf_op jit(solution)/shard_map/ppermute | solution.py:107
  34.8 48.6 %collective-permute-start.15 = (bf16[3,384,256]{2,1,0:T(8,128)(2,1)S(1)}, bf16[3,384,256]{2,1,0:T(8,128)(2,1)S(1)}, u32[]{:S(2)}, u32[]{:S(2)}) collective-permute-start(bf16[3,384,256]{2,1,0:T(8,128)(2,1)S(1)} %collective-permute-done.5.refs_8_), channel_id=1, source_target_pairs={{0,16},{16,0},{1,17},{17,1},{2,18},{18,2},{3,19},{19,3},{4,20},{20... | collective-permute-start | bytes 1769480 | tf_op jit(solution)/shard_map/ppermute | solution.py:107
  40.9 0.7 copy-start.6
  41.7 38.3 %collective-permute-start.7 = (bf16[128,1536]{1,0:T(8,128)(2,1)S(1)}, bf16[128,1536]{1,0:T(8,128)(2,1)}, u32[]{:S(2)}, u32[]{:S(2)}) collective-permute-start(bf16[128,1536]{1,0:T(8,128)(2,1)S(1)} %dynamic-slice_bitcast_fusion.2.refs_0_), channel_id=1, source_target_pairs={{0,12},{4,8},{8,4},{12,0},{1,13},{5,9},{9,5},{13,1},{2,14},{6,10},... | collective-permute-start | bytes 1179656 | tf_op jit(solution)/shard_map/ppermute | solution.py:107
  74.7 8.0 %collective-permute-start.9 = (bf16[128,1536]{1,0:T(8,128)(2,1)}, bf16[128,1536]{1,0:T(8,128)(2,1)S(1)}, u32[]{:S(2)}, u32[]{:S(2)}) collective-permute-start(bf16[128,1536]{1,0:T(8,128)(2,1)} %collective-permute-done.4.refs_2_), channel_id=1, source_target_pairs={{0,2},{2,0},{1,3},{3,1},{4,6},{6,4},{5,7},{7,5},{8,10},{10,8},{9,1... | collective-permute-start | bytes 1179656 | tf_op jit(solution)/shard_map/ppermute | solution.py:107
  77.0 6.4 %collective-permute-start.12 = (bf16[3,384,128]{2,1,0:T(8,128)(2,1)S(1)}, bf16[3,384,128]{2,1,0:T(8,128)(2,1)}, u32[]{:S(2)}, u32[]{:S(2)}) collective-permute-start(bf16[3,384,128]{2,1,0:T(8,128)(2,1)S(1)} %get-tuple-element.34), channel_id=1, source_target_pairs={{0,0},{1,8},{4,4},{5,12},{8,1},{9,9},{12,5},{13,13},{2,2},{3,10},{... | collective-permute-start | bytes 884744 | tf_op jit(solution)/shard_map/ppermute | solution.py:338
  78.4 16.5 %collective-permute-start.18 = (bf16[3,384,256]{2,1,0:T(8,128)(2,1)S(1)}, bf16[3,384,256]{2,1,0:T(8,128)(2,1)S(1)}, u32[]{:S(2)}, u32[]{:S(2)}) collective-permute-start(bf16[3,384,256]{2,1,0:T(8,128)(2,1)S(1)} %collective-permute-done.14.refs_10_), channel_id=1, source_target_pairs={{0,16},{16,0},{1,17},{17,1},{2,18},{18,2},{3,19},{19,3},{4,20},{20... | collective-permute-start | bytes 1769480 | tf_op jit(solution)/shard_map/ppermute | solution.py:107
  80.0 21.1 %collective-permute-start.10 = (bf16[128,1536]{1,0:T(8,128)(2,1)}, bf16[128,1536]{1,0:T(8,128)(2,1)}, u32[]{:S(2)}, u32[]{:S(2)}) collective-permute-start(bf16[128,1536]{1,0:T(8,128)(2,1)} %collective-permute-done.7.refs_3_), channel_id=1, source_target_pairs={{0,2},{2,0},{1,3},{3,1},{4,6},{6,4},{5,7},{7,5},{8,10},{10,8},{9,1... | collective-permute-start | bytes 1179656 | tf_op jit(solution)/shard_map/ppermute | solution.py:107
  82.7 0.7 copy-start.8
  83.4 10.1 %collective-permute-start.16 = (bf16[3,384,128]{2,1,0:T(8,128)(2,1)}, bf16[3,384,128]{2,1,0:T(8,128)(2,1)}, u32[]{:S(2)}, u32[]{:S(2)}) collective-permute-start(bf16[3,384,128]{2,1,0:T(8,128)(2,1)} %get-tuple-element.36), channel_id=1, source_target_pairs={{0,4},{1,12},{4,0},{5,8},{8,5},{9,13},{12,1},{13,9},{2,6},{3,14},{... | collective-permute-start | bytes 884744 | tf_op jit(solution)/shard_map/ppermute | solution.py:338
  83.4 17.6 %collective-permute-start.13 = (bf16[3,384,128]{2,1,0:T(8,128)(2,1)}, bf16[3,384,128]{2,1,0:T(8,128)(2,1)}, u32[]{:S(2)}, u32[]{:S(2)}) collective-permute-start(bf16[3,384,128]{2,1,0:T(8,128)(2,1)} %collective-permute-done.12.refs_8_), channel_id=1, source_target_pairs={{0,16},{16,0},{1,17},{17,1},{2,18},{18,2},{3,19},{19,3},{4,20},{20... | collective-permute-start | bytes 884744 | tf_op jit(solution)/shard_map/ppermute | solution.py:107
  93.5 18.0 %collective-permute-start.17 = (bf16[3,384,128]{2,1,0:T(8,128)(2,1)}, bf16[3,384,128]{2,1,0:T(8,128)(2,1)S(1)}, u32[]{:S(2)}, u32[]{:S(2)}) collective-permute-start(bf16[3,384,128]{2,1,0:T(8,128)(2,1)} %collective-permute-done.16.refs_10_), channel_id=1, source_target_pairs={{0,16},{16,0},{1,17},{17,1},{2,18},{18,2},{3,19},{19,3},{4,20},{20... | collective-permute-start | bytes 884744 | tf_op jit(solution)/shard_map/ppermute | solution.py:107
  101.0 1.0 copy-start.2
  102.0 1.0 copy-start.5
  103.0 1.0 copy-start.7
  104.0 1.0 copy-start.9
  105.0 6.2 %copy-start.10 = (bf16[768,768]{1,0:T(8,128)(2,1)S(1)}, bf16[768,768]{1,0:T(8,128)(2,1)}, u32[]{:S(2)}) copy-start(bf16[768,768]{1,0:T(8,128)(2,1)} %param.8) | copy-start | bytes 3538948
  111.2 1.0 copy-start.3
  111.2 16.0 %collective-permute-start.21 = (bf16[4,320,512]{2,1,0:T(8,128)(2,1)S(1)}, bf16[4,320,512]{2,1,0:T(8,128)(2,1)S(1)}, u32[]{:S(2)}, u32[]{:S(2)}) collective-permute-start(bf16[4,320,512]{2,1,0:T(8,128)(2,1)S(1)} %get-tuple-element.38), channel_id=1, source_target_pairs={{0,1},{1,0},{2,3},{3,2},{4,5},{5,4},{6,7},{7,6},{8,9},{9,8},{10,11... | collective-permute-start | bytes 3932168 | tf_op jit(solution)/shard_map/ppermute | solution.py:107
  111.4 15.8 %collective-permute-start.20 = (bf16[384,768]{1,0:T(8,128)(2,1)S(1)}, bf16[384,768]{1,0:T(8,128)(2,1)S(1)}, u32[]{:S(2)}, u32[]{:S(2)}) collective-permute-start(bf16[384,768]{1,0:T(8,128)(2,1)S(1)} %get-tuple-element.45), channel_id=1, source_target_pairs={{0,4},{4,0},{8,12},{12,8},{1,5},{5,1},{9,13},{13,9},{2,6},{6,2},{1... | collective-permute-start | bytes 1769480 | tf_op jit(solution)/shard_map/ppermute | solution.py:107
  118.1 14.5 %collective-permute-start.19 = (bf16[4,320,256]{2,1,0:T(8,128)(2,1)S(1)}, bf16[4,320,256]{2,1,0:T(8,128)(2,1)S(1)}, u32[]{:S(2)}, u32[]{:S(2)}) collective-permute-start(bf16[4,320,256]{2,1,0:T(8,128)(2,1)S(1)} %get-tuple-element.42), channel_id=1, source_target_pairs={{0,1},{1,0},{2,3},{3,2},{4,5},{5,4},{6,7},{7,6},{8,9},{9,8},{10,11... | collective-permute-start | bytes 1966088 | tf_op jit(solution)/shard_map/ppermute | solution.py:107
  131.0 20.7 %collective-permute-start.25 = (bf16[384,768]{1,0:T(8,128)(2,1)S(1)}, bf16[384,768]{1,0:T(8,128)(2,1)S(1)}, u32[]{:S(2)}, u32[]{:S(2)}) collective-permute-start(bf16[384,768]{1,0:T(8,128)(2,1)S(1)} %collective-permute-done.20.refs_6_), channel_id=1, source_target_pairs={{0,16},{16,0},{1,17},{17,1},{2,18},{18,2},{3,19},{19,3},{4,20},{20... | collective-permute-start | bytes 1769480 | tf_op jit(solution)/shard_map/ppermute | solution.py:107
  134.8 15.7 %collective-permute-start.23 = (bf16[2,128,384]{2,1,0:T(8,128)(2,1)S(1)}, bf16[2,128,384]{2,1,0:T(8,128)(2,1)S(1)}, u32[]{:S(2)}, u32[]{:S(2)}) collective-permute-start(bf16[2,128,384]{2,1,0:T(8,128)(2,1)S(1)} %get-tuple-element.49.refs_0_), channel_id=1, source_target_pairs={{0,8},{4,12},{8,0},{12,4},{1,9},{5,13},{9,1},{13,5},{2,10},{6,14},... | collective-permute-start | bytes 589832 | tf_op jit(solution)/shard_map/ppermute | solution.py:107
  135.7 14.8 %collective-permute-start.24 = (bf16[2,128,384]{2,1,0:T(8,128)(2,1)S(1)}, bf16[2,128,384]{2,1,0:T(8,128)(2,1)S(1)}, u32[]{:S(2)}, u32[]{:S(2)}) collective-permute-start(bf16[2,128,384]{2,1,0:T(8,128)(2,1)S(1)} %get-tuple-element.50), channel_id=1, source_target_pairs={{0,12},{4,8},{8,4},{12,0},{1,13},{5,9},{9,5},{13,1},{2,14},{6,10},... | collective-permute-start | bytes 589832 | tf_op jit(solution)/shard_map/ppermute | solution.py:107
  137.5 14.2 %collective-permute-start.22 = (bf16[2,128,384]{2,1,0:T(8,128)(2,1)S(1)}, bf16[2,128,384]{2,1,0:T(8,128)(2,1)S(1)}, u32[]{:S(2)}, u32[]{:S(2)}) collective-permute-start(bf16[2,128,384]{2,1,0:T(8,128)(2,1)S(1)} %get-tuple-element.50), channel_id=1, source_target_pairs={{0,4},{4,0},{8,12},{12,8},{1,5},{5,1},{9,13},{13,9},{2,6},{6,2},{1... | collective-permute-start | bytes 589832 | tf_op jit(solution)/shard_map/ppermute | solution.py:107
  138.3 14.7 %collective-permute-start.26 = (bf16[384,768]{1,0:T(8,128)(2,1)S(1)}, bf16[384,768]{1,0:T(8,128)(2,1)S(1)}, u32[]{:S(2)}, u32[]{:S(2)}) collective-permute-start(bf16[384,768]{1,0:T(8,128)(2,1)S(1)} %collective-permute-done.20.refs_6_), channel_id=1, source_target_pairs={{0,1},{1,0},{2,3},{3,2},{4,5},{5,4},{6,7},{7,6},{8,9},{9,8},{10,11... | collective-permute-start | bytes 1769480 | tf_op jit(solution)/shard_map/ppermute | solution.py:107
  151.7 2.0 %collective-permute-start.27 = (bf16[384,768]{1,0:T(8,128)(2,1)S(1)}, bf16[384,768]{1,0:T(8,128)(2,1)S(1)}, u32[]{:S(2)}, u32[]{:S(2)}) collective-permute-start(bf16[384,768]{1,0:T(8,128)(2,1)S(1)} %collective-permute-done.25.refs_7_), channel_id=1, source_target_pairs={{0,1},{1,0},{2,3},{3,2},{4,5},{5,4},{6,7},{7,6},{8,9},{9,8},{10,11... | collective-permute-start | bytes 1769480 | tf_op jit(solution)/shard_map/ppermute | solution.py:107
  156.2 7.0 %collective-permute-start.28 = (bf16[2,64,768]{2,1,0:T(8,128)(2,1)S(1)}, bf16[2,64,768]{2,1,0:T(8,128)(2,1)S(1)}, u32[]{:S(2)}, u32[]{:S(2)}) collective-permute-start(bf16[2,64,768]{2,1,0:T(8,128)(2,1)S(1)} %get-tuple-element.54), channel_id=1, source_target_pairs={{0,2},{2,0},{1,3},{3,1},{4,6},{6,4},{5,7},{7,5},{8,10},{10,8},{9,1... | collective-permute-start | bytes 589832 | tf_op jit(solution)/shard_map/ppermute | solution.py:107
  157.7 18.1 %collective-permute-start.29 = (bf16[2,64,768]{2,1,0:T(8,128)(2,1)S(1)}, bf16[2,64,768]{2,1,0:T(8,128)(2,1)S(1)}, u32[]{:S(2)}, u32[]{:S(2)}) collective-permute-start(bf16[2,64,768]{2,1,0:T(8,128)(2,1)S(1)} %get-tuple-element.55), channel_id=1, source_target_pairs={{0,8},{4,12},{8,0},{12,4},{1,9},{5,13},{9,1},{13,5},{2,10},{6,14},... | collective-permute-start | bytes 589832 | tf_op jit(solution)/shard_map/ppermute | solution.py:107
  161.7 17.5 %collective-permute-start.30 = (bf16[2,64,768]{2,1,0:T(8,128)(2,1)S(1)}, bf16[2,64,768]{2,1,0:T(8,128)(2,1)S(1)}, u32[]{:S(2)}, u32[]{:S(2)}) collective-permute-start(bf16[2,64,768]{2,1,0:T(8,128)(2,1)S(1)} %get-tuple-element.56), channel_id=1, source_target_pairs={{0,10},{2,8},{4,14},{6,12},{8,2},{10,0},{12,6},{14,4},{1,11},{3,9}... | collective-permute-start | bytes 589832 | tf_op jit(solution)/shard_map/ppermute | solution.py:384

commit v13 on v10

--- a/solution.py
+++ b/solution.py
@@ -127,25 +127,6 @@
     )(*prefetch, *operands)
 
 
-def assemble(place, mine, theirs, count):
-    width, rows = mine[0].shape[1], len(mine)
-
-    def kernel(place_ref, *refs):
-        row, frame = place_ref[0], place_ref[2]
-        for s in range(rows):
-            refs[-1][row ^ s, frame] = refs[s][:count]
-            refs[-1][row ^ s, 1 - frame] = refs[rows + s][:count]
-
-    return call(
-        kernel,
-        jax.ShapeDtypeStruct((rows, 2, count, width), jnp.bfloat16),
-        [place],
-        [*mine, *theirs],
-        read=8 * rows * count * width,
-        limit=WHOLE_VMEM_BYTES,
-    )
-
-
 def project(place, tokens, chunks):
     rows, _, count, width = tokens.shape
     _, half, cols = chunks[0][0].shape
@@ -190,7 +171,6 @@
         scratch=[pltpu.VMEM((rows, 2, count, cols), jnp.float32)],
         flops=8 * flops,
         read=flops // 300,
-        limit=WHOLE_VMEM_BYTES,
     )
 
 
@@ -248,7 +228,6 @@
         ],
         flops=4 * blocks * block_len * MAXB * block_len * cols,
         read=16 * blocks * block_len * cols,
-        limit=WHOLE_VMEM_BYTES,
     )
 
 
@@ -344,41 +323,31 @@
         ]
         return lax.ppermute(after(value, *others) if others else value, ("rows", "heads"), pairs)
 
+    mine = lax.dynamic_slice_in_dim(latents[0], core * span * depth, span * depth, axis=1)
+    tokens = lax.all_gather(mine, ("rows", "frames"), axis=0).reshape(rows_n, 2, count, span * depth)
+
     tables = jnp.concatenate([win_blocks, win_counts[:, None], block_window[:, None]], axis=1)
-    tables = jnp.pad(tables, ((0, 6), (0, span * depth - MAXB - 2))).astype(latents.dtype)
-    mine = lax.dynamic_slice_in_dim(latents[0], core * span * depth, span * depth, axis=1)
-    mine = jnp.concatenate([mine, tables], axis=0)
-
-    near, mine_x = swap(mine, "rows"), swap(mine, "frames")
-    here, there = [reshard(0)], []
-    near_x = swap(near, "frames")
-    across = swap(after(w_out, near), "heads")
-    here.append(reshard(1, near, mine_x))
-    there.append(swap(here[0], "groups"))
-    far_2 = swap(after(mine, here[0]), "rows", 2)
-    there.append(swap(here[1], "groups"))
-    far_3 = swap(after(mine, here[1], near_x), "rows", 3)
-    far_2x = swap(far_2, "frames")
-    out_half = lax.dynamic_slice_in_dim(w_out, group * cols, cols, axis=0)
-    beside = [swap(after(out_half, here[0]), "rows")]
-    beside.append(swap(beside[0], "groups"))
-    here.append(reshard(2, far_2, there[0], there[1], across, beside[0]))
-    far_3x = swap(far_3, "frames")
-    here.append(reshard(3, far_3, far_2x, beside[1]))
-    there += [swap(here[2], "groups"), swap(here[3], "groups")]
-    pieces = [mine, near, far_2, far_3]
-    tokens = assemble(place, pieces, [mine_x, near_x, far_2x, far_3x], count)
-
-    found = jnp.stack([x[count : count + heads_n, : MAXB + 2] for x in pieces]).astype(jnp.int32)
-    tables = found[row ^ jnp.arange(rows_n)].reshape(rows_n * heads_n, MAXB + 2)
+    found = [tables] + [swap(tables, "rows", s) for s in range(1, rows_n)]
+    tables = jnp.stack(found)[row ^ jnp.arange(rows_n)].reshape(rows_n * heads_n, MAXB + 2)
     windows = lax.dynamic_index_in_dim(
         tables[:, MAXB + 1].reshape(rows_n, heads_n), core, axis=1, keepdims=False
     )
     picked = tables[windows]
     members, counts = picked[:, :MAXB].reshape(-1), picked[:, MAXB]
 
-    chunks = [(here[0], there[0]), (here[1], after(there[1], there[2], here[3]))]
-    first = project(place, tokens, chunks)
+    here, there = [reshard(0), reshard(1)], []
+    there += [swap(here[0], "groups"), swap(here[1], "groups")]
+    across = swap(w_out, "heads")
+    here.append(reshard(2, here[0], here[1], members, counts))
+    here.append(reshard(3, there[0], across))
+    there += [swap(here[2], "groups"), swap(here[3], "groups")]
+    out_half = lax.dynamic_slice_in_dim(w_out, group * cols, cols, axis=0)
+    beside = [swap(after(out_half, here[2]), "rows")]
+    beside.append(swap(beside[0], "groups"))
+    beside_across = [swap(part, "heads") for part in beside]
+
+    tokens = after(tokens, *there, *beside, *beside_across)
+    first = project(place, tokens, [(here[0], there[0]), (here[1], there[1])])
     first_more = swap(first[2], "heads")
     second = project(place, tokens, [(here[2], there[2]), (here[3], after(there[3], first[2]))])
     second_more = swap(second[2], "heads")
@@ -386,7 +355,6 @@
     same, diff = attend_all(place, members, counts, *second[:2], second_more, attended)
     attended = [same] + [swap(same if s % 2 == 0 else diff, "rows", s) for s in range(1, rows_n)]
     halves = [w_out[:cols], w_out[cols:], *beside]
-    beside_across = [swap(part, "heads") for part in beside]
     keep, over_x, over_z, over_both = mix(
         place, attended, [*halves, across[:cols], across[cols:], *beside_across]
     )

time: 183 us -> 214 us (1.17)
  starting transfers between devices: 53.6 us -> 77.1 us
  Pallas kernels: 35.4 us -> 20.3 us
  between operations: 0.2 us -> 13.5 us
  waiting for transfers between devices: 77.6 us -> 88 us
  other arithmetic: 3.97 us -> 1.23 us
    ppermute x23 -> x19, starting transfers between devices: 34.9 us -> 68.9 us  [swap(): return lax.ppermute(value, axis, [(i, i ^ step) for i in range(peers)])]
    pallas_call x7 -> x6, Pallas kernels: 35.4 us -> 20.3 us  [call(): pl.pallas_call(kernel, out_shape=out_shape, grid_spec=pltpu.PrefetchScala...]
    ppermute x4, starting transfers between devices: 16.1 us -> 4.84 us  [reshard(): lax.ppermute(after(value, *others) if others else value, ('rows', 'heads'...]
    ppermute x4, waiting for transfers between devices: 13.3 us -> 22.4 us  [reshard(): lax.ppermute(after(value, *others) if others else value, ('rows', 'heads'...]
    unnamed x26 -> x16, local copies, waits for them, and re-layouts: 1.55 us -> 4.94 us
    ppermute x23 -> x19, waiting for transfers between devices: 60.4 us -> 60.9 us  [swap(): return lax.ppermute(value, axis, [(i, i ^ step) for i in range(peers)])]
  transfers between devices with their start and end apart: 28 -> 25, of which waited for: 11 -> 11; matrix products, arithmetic and copies ran while one was open for 6% -> 4% of each run, Pallas kernels for 17% -> 4%
where the time goes in v13:
time: 214 us
  waiting for transfers between devices  88 us (41%)
  starting transfers between devices  77.1 us (36%)
  Pallas kernels  20.3 us (9%)
  local copies, waits for them, and re-layouts  13.7 us (6%)
  between operations  13.5 us (6%)
    ppermute x19, starting transfers between devices, swap(): return lax.ppermute(value, axis, [(i, i ^ step) for i in range(peers)])  68.9 us
    ppermute x19, waiting for transfers between devices, swap(): return lax.ppermute(value, axis, [(i, i ^ step) for i in range(peers)])  60.9 us
    ppermute x4, waiting for transfers between devices, reshard(): lax.ppermute(after(value, *others) if others else value, ('rows', 'heads'...  22.4 us
    pallas_call x6, Pallas kernels, call(): pl.pallas_call(kernel, out_shape=out_shape, grid_spec=pltpu.PrefetchScala...  20.3 us
    unnamed x16, local copies, waits for them, and re-layouts  4.94 us
    ppermute x4, starting transfers between devices, reshard(): lax.ppermute(after(value, *others) if others else value, ('rows', 'heads'...  4.84 us
    ppermute x1, waiting for transfers between devices, by_heads(): lax.ppermute(over_both, ('rows', 'frames'), [(2 * r + f, 2 * (r ^ 2) + 1...  4.62 us
  transfers between devices with their start and end apart: 25, of which 11 were waited for; matrix products, arithmetic and copies ran while one was open for 4% of the time, Pallas kernels for 4%

profile of v13, /device:TPU:0, one launch (start us, length us, event | category | flops | bytes accessed | tf_op | source)
XLA Modules:
  0.0 213.8 jit_solution(15004891974625150483)
XLA Ops:
  6.5 1.1 copy-done
  7.7 0.8 constant_dynamic-slice_fusion.1
  8.5 0.7 copy.11
  9.2 0.7 copy.12
  10.0 0.8 pad_add_fusion.1
  10.7 4.0 %collective-permute-start.1 = (s32[2,6]{1,0:T(2,128)S(1)}, s32[2,6]{1,0:T(2,128)S(1)}, u32[]{:S(2)}, u32[]{:S(2)}) collective-permute-start(s32[2,6]{1,0:T(2,128)S(1)} %pad_add_fusion.1), channel_id=1, source_target_pairs={{0,8},{4,12},{8,0},{12,4},{1,9},{5,13},{9,1},{13,5},{2,10},{6,14},... | collective-permute-start | bytes 152 | tf_op jit(solution)/shard_map/ppermute | solution.py:107
  14.8 1.6 collective-permute-start
  16.3 1.3 dynamic-slice_bitcast_fusion
  17.7 1.0 collective-permute-start.5
  18.6 1.5 collective-permute-start.3
  20.3 1.9 dynamic-slice_bitcast_fusion.2
  24.1 22.4 %collective-permute-done.5.refs_2_ = bf16[3,384,256]{2,1,0:T(8,128)(2,1)} collective-permute-done((bf16[3,384,256]{2,1,0:T(8,128)(2,1)S(1)}, bf16[3,384,256]{2,1,0:T(8,128)(2,1)}, u32[]{:S(2)}, u32[]{:S(2)}) %collective-permute-start.5) | collective-permute-done | bytes 589856 | tf_op jit(solution)/shard_map/ppermute | solution.py:324
  46.5 0.8 collective-permute-start.7
  47.3 33.4 %collective-permute-start.9 = (bf16[768,768]{1,0:T(8,128)(2,1)}, bf16[768,768]{1,0:T(8,128)(2,1)S(1)}, u32[]{:S(2)}, u32[]{:S(2)}) collective-permute-start(bf16[768,768]{1,0:T(8,128)(2,1)} %param.8), channel_id=1, source_target_pairs={{0,1},{1,0},{2,3},{3,2},{4,5},{5,4},{6,7},{7,6},{8,9},{9,8},{10,11... | collective-permute-start | bytes 3538952 | tf_op jit(solution)/shard_map/ppermute | solution.py:107
  80.7 1.5 fusion.3
  82.3 7.6 %collective-permute-start.12 = (bf16[384,768]{1,0:T(8,128)(2,1)S(1)}, bf16[384,768]{1,0:T(8,128)(2,1)S(1)}, u32[]{:S(2)}, u32[]{:S(2)}) collective-permute-start(bf16[384,768]{1,0:T(8,128)(2,1)S(1)} %get-tuple-element.26), channel_id=1, source_target_pairs={{0,4},{4,0},{8,12},{12,8},{1,5},{5,1},{9,13},{13,9},{2,6},{6,2},{1... | collective-permute-start | bytes 1769480 | tf_op jit(solution)/shard_map/ppermute | solution.py:107
  89.9 1.1 collective-permute-start.4
  91.0 9.4 %collective-permute-done.12.refs_6_ = bf16[384,768]{1,0:T(8,128)(2,1)S(1)} collective-permute-done((bf16[384,768]{1,0:T(8,128)(2,1)S(1)}, bf16[384,768]{1,0:T(8,128)(2,1)S(1)}, u32[]{:S(2)}, u32[]{:S(2)}) %collective-permute-start.12) | collective-permute-done | bytes 589856 | tf_op jit(solution)/shard_map/ppermute | solution.py:107
  100.4 1.2 collective-permute-start.13
  101.7 0.8 collective-permute-start.6
  102.5 0.8 collective-permute-done.4.refs_1_
  103.2 0.8 copy-done.2
  104.1 1.6 collective-permute-start.10
  105.7 4.6 %collective-permute-start.14 = (bf16[384,768]{1,0:T(8,128)(2,1)S(1)}, bf16[384,768]{1,0:T(8,128)(2,1)}, u32[]{:S(2)}, u32[]{:S(2)}) collective-permute-start(bf16[384,768]{1,0:T(8,128)(2,1)S(1)} %collective-permute-done.12.refs_6_), channel_id=1, source_target_pairs={{0,1},{1,0},{2,3},{3,2},{4,5},{5,4},{6,7},{7,6},{8,9},{9,8},{10,11... | collective-permute-start | bytes 1769480 | tf_op jit(solution)/shard_map/ppermute | solution.py:107
  110.3 6.4 %collective-permute-done.13.refs_7_ = bf16[384,768]{1,0:T(8,128)(2,1)S(1)} collective-permute-done((bf16[384,768]{1,0:T(8,128)(2,1)S(1)}, bf16[384,768]{1,0:T(8,128)(2,1)S(1)}, u32[]{:S(2)}, u32[]{:S(2)}) %collective-permute-start.13) | collective-permute-done | bytes 589856 | tf_op jit(solution)/shard_map/ppermute | solution.py:107
  116.7 4.7 %collective-permute-start.15 = (bf16[384,768]{1,0:T(8,128)(2,1)S(1)}, bf16[384,768]{1,0:T(8,128)(2,1)}, u32[]{:S(2)}, u32[]{:S(2)}) collective-permute-start(bf16[384,768]{1,0:T(8,128)(2,1)S(1)} %collective-permute-done.13.refs_7_), channel_id=1, source_target_pairs={{0,1},{1,0},{2,3},{3,2},{4,5},{5,4},{6,7},{7,6},{8,9},{9,8},{10,11... | collective-permute-start | bytes 1769480 | tf_op jit(solution)/shard_map/ppermute | solution.py:107
  121.4 1.0 collective-permute-start.8
  122.4 1.0 collective-permute-start.11
  123.5 5.9 %collective-permute-done.6.refs_3_ = bf16[3,384,256]{2,1,0:T(8,128)(2,1)} collective-permute-done((bf16[3,384,256]{2,1,0:T(8,128)(2,1)}, bf16[3,384,256]{2,1,0:T(8,128)(2,1)}, u32[]{:S(2)}, u32[]{:S(2)}) %collective-permute-start.6) | collective-permute-done | bytes 589856 | tf_op jit(solution)/shard_map/ppermute | solution.py:107
  129.4 6.3 %collective-permute-done.8.refs_1_ = bf16[3,384,128]{2,1,0:T(8,128)(2,1)} collective-permute-done((bf16[3,384,128]{2,1,0:T(8,128)(2,1)S(1)}, bf16[3,384,128]{2,1,0:T(8,128)(2,1)}, u32[]{:S(2)}, u32[]{:S(2)}) %collective-permute-start.8) | collective-permute-done | bytes 294944 | tf_op jit(solution)/shard_map/ppermute | solution.py:107
  135.8 6.3 %collective-permute-done.11.refs_3_ = bf16[3,384,128]{2,1,0:T(8,128)(2,1)} collective-permute-done((bf16[3,384,128]{2,1,0:T(8,128)(2,1)}, bf16[3,384,128]{2,1,0:T(8,128)(2,1)}, u32[]{:S(2)}, u32[]{:S(2)}) %collective-permute-start.11) | collective-permute-done | bytes 294944 | tf_op jit(solution)/shard_map/ppermute | solution.py:107
  142.1 1.9 copy-done.1
  144.0 1.1 copy-done.3
  145.1 5.5 %shard_map.64 = (f32[4,128,256]{2,1,0:T(8,128)S(1)}, f32[4,256,512]{2,1,0:T(8,128)S(1)}, bf16[4,320,512]{2,1,0:T(8,128)(2,1)S(1)}) custom-call(s32[4]{0:T(128)S(1)} %pad_add_fusion.2.place_ref, bf16[4,2,128,1536]{3,2,1,0:T(8,128)(2,1)S(1)} %bitcast.23, bf16[3,384,256]{2,1,0:T(8,128)(2,1)} %collective-permute-done.3.refs_0_, ...), custom_call_target="tpu_custom_call" | custom-call | flops 19327352832 | bytes 8053063 | tf_op jit(solution)/shard_map/pallas_call | solution.py:115
  150.5 2.1 %collective-permute-start.17 = (bf16[4,320,512]{2,1,0:T(8,128)(2,1)S(1)}, bf16[4,320,512]{2,1,0:T(8,128)(2,1)S(1)}, u32[]{:S(2)}, u32[]{:S(2)}) collective-permute-start(bf16[4,320,512]{2,1,0:T(8,128)(2,1)S(1)} %get-tuple-element.28), channel_id=1, source_target_pairs={{0,1},{1,0},{2,3},{3,2},{4,5},{5,4},{6,7},{7,6},{8,9},{9,8},{10,11... | collective-permute-start | bytes 3932168 | tf_op jit(solution)/shard_map/ppermute | solution.py:107
  152.7 3.8 %shard_map.65 = (f32[4,128,128]{2,1,0:T(8,128)S(1)}, f32[4,256,256]{2,1,0:T(8,128)S(1)}, bf16[4,320,256]{2,1,0:T(8,128)(2,1)S(1)}) custom-call(s32[4]{0:T(128)S(1)} %pad_add_fusion.2.place_ref, bf16[4,2,128,1536]{3,2,1,0:T(8,128)(2,1)S(1)} %bitcast.24, bf16[3,384,128]{2,1,0:T(8,128)(2,1)S(1)} %collective-permute-done.7.refs_0_, ...), custom_call_target="tpu_custom_call" | custom-call | flops 9663676416 | bytes 4026531 | tf_op jit(solution)/shard_map/pallas_call | solution.py:115
  156.6 3.8 %shard_map.66 = (bf16[2,128,256]{2,1,0:T(8,128)(2,1)S(1)}, bf16[2,128,256]{2,1,0:T(8,128)(2,1)S(1)}) custom-call(s32[4]{0:T(128)S(1)} %pad_add_fusion.2.place_ref, s32[16]{0:T(128)S(1)} %reshape.28.members_ref, s32[4]{0:T(128)S(1)} %slice_reduce_fusion.1.counts_ref, f32[4,128,256]{2,1,0:T(8,128)S(1)} %get-tuple-element.33.q_ref, ...), custom_call_target="tpu_custom_call" | custom-call | flops 268435456 | bytes 2097152 | tf_op jit(solution)/shard_map/pallas_call | solution.py:115
  160.3 2.2 %shard_map.67 = (bf16[2,128,384]{2,1,0:T(8,128)(2,1)S(1)}, bf16[2,128,384]{2,1,0:T(8,128)(2,1)S(1)}) custom-call(s32[4]{0:T(128)S(1)} %pad_add_fusion.2.place_ref, s32[16]{0:T(128)S(1)} %reshape.28.members_ref, s32[4]{0:T(128)S(1)} %slice_reduce_fusion.1.counts_ref, f32[4,128,128]{2,1,0:T(8,128)S(1)} %get-tuple-element.30.q_ref, ...), custom_call_target="tpu_custom_call" | custom-call | flops 134217728 | bytes 1048576 | tf_op jit(solution)/shard_map/pallas_call | solution.py:115
  162.6 0.6 collective-permute-start.20
  163.2 3.8 %collective-permute-start.19 = (bf16[2,128,384]{2,1,0:T(8,128)(2,1)S(1)}, bf16[2,128,384]{2,1,0:T(8,128)(2,1)S(1)}, u32[]{:S(2)}, u32[]{:S(2)}) collective-permute-start(bf16[2,128,384]{2,1,0:T(8,128)(2,1)S(1)} %get-tuple-element.37.refs_0_), channel_id=1, source_target_pairs={{0,8},{4,12},{8,0},{12,4},{1,9},{5,13},{9,1},{13,5},{2,10},{6,14},... | collective-permute-start | bytes 589832 | tf_op jit(solution)/shard_map/ppermute | solution.py:107
  167.1 15.0 %collective-permute-done.19.refs_2_ = bf16[2,128,384]{2,1,0:T(8,128)(2,1)S(1)} collective-permute-done((bf16[2,128,384]{2,1,0:T(8,128)(2,1)S(1)}, bf16[2,128,384]{2,1,0:T(8,128)(2,1)S(1)}, u32[]{:S(2)}, u32[]{:S(2)}) %collective-permute-start.19) | collective-permute-done | bytes 196640 | tf_op jit(solution)/shard_map/ppermute | solution.py:107
  182.1 3.7 %shard_map.68 = (f32[2,64,768]{2,1,0:T(8,128)S(1)}, bf16[2,64,768]{2,1,0:T(8,128)(2,1)S(1)}, bf16[2,64,768]{2,1,0:T(8,128)(2,1)S(1)}, bf16[2,64,768]{2,1,0:T(8,128)(2,1)S(1)}) custom-call(s32[4]{0:T(128)S(1)} %pad_add_fusion.2.place_ref, bf16[2,128,384]{2,1,0:T(8,128)(2,1)S(1)} %get-tuple-element.37.refs_0_, ...), custom_call_target="tpu_custom_call" | custom-call | flops 1207959552 | bytes 4718592 | tf_op jit(solution)/shard_map/pallas_call | solution.py:115
  185.8 1.0 collective-permute-start.21
  186.9 3.4 %collective-permute-start.23 = (bf16[2,64,768]{2,1,0:T(8,128)(2,1)S(1)}, bf16[2,64,768]{2,1,0:T(8,128)(2,1)S(1)}, u32[]{:S(2)}, u32[]{:S(2)}) collective-permute-start(bf16[2,64,768]{2,1,0:T(8,128)(2,1)S(1)} %get-tuple-element.42), channel_id=1, source_target_pairs={{0,10},{2,8},{4,14},{6,12},{8,2},{10,0},{12,6},{14,4},{1,11},{3,9}... | collective-permute-start | bytes 589832 | tf_op jit(solution)/shard_map/ppermute | solution.py:363
  190.3 2.1 collective-permute-done.21.x_ref
  192.4 8.6 %collective-permute-done.22.z_ref = bf16[2,64,768]{2,1,0:T(8,128)(2,1)S(1)} collective-permute-done((bf16[2,64,768]{2,1,0:T(8,128)(2,1)S(1)}, bf16[2,64,768]{2,1,0:T(8,128)(2,1)S(1)}, u32[]{:S(2)}, u32[]{:S(2)}) %collective-permute-start.22) | collective-permute-done | bytes 196640 | tf_op jit(solution)/shard_map/ppermute | solution.py:107
  201.0 4.6 %collective-permute-done.23.both_ref = bf16[2,64,768]{2,1,0:T(8,128)(2,1)S(1)} collective-permute-done((bf16[2,64,768]{2,1,0:T(8,128)(2,1)S(1)}, bf16[2,64,768]{2,1,0:T(8,128)(2,1)S(1)}, u32[]{:S(2)}, u32[]{:S(2)}) %collective-permute-start.23) | collective-permute-done | bytes 196640 | tf_op jit(solution)/shard_map/ppermute | solution.py:363
  205.6 1.4 shard_map.69
  (46 shorter events, 2.4 us)
Async XLA Ops:
  6.5 1.1 copy-start
  6.5 135.6 %all-gather.2.cloned.1.call-start = ((), (), s32[]{:S(2)}) async-start(), calls=%async_computation | async-start | bytes 3538944 | tf_op jit(solution)/shard_map/all_gather | solution.py:327
  8.5 11.8 %copy-start.7 = (s32[2,4]{1,0:T(2,128)S(1)}, s32[2,4]{1,0:T(2,128)}, u32[]{:S(2)}) copy-start(s32[2,4]{1,0:T(2,128)} %param.9) | copy-start | bytes 100
  10.7 11.5 %collective-permute-start.1 = (s32[2,6]{1,0:T(2,128)S(1)}, s32[2,6]{1,0:T(2,128)S(1)}, u32[]{:S(2)}, u32[]{:S(2)}) collective-permute-start(s32[2,6]{1,0:T(2,128)S(1)} %pad_add_fusion.1), channel_id=1, source_target_pairs={{0,8},{4,12},{8,0},{12,4},{1,9},{5,13},{9,1},{13,5},{2,10},{6,14},... | collective-permute-start | bytes 152 | tf_op jit(solution)/shard_map/ppermute | solution.py:107
  14.8 7.5 %collective-permute-start = (s32[2,6]{1,0:T(2,128)S(1)}, s32[2,6]{1,0:T(2,128)S(1)}, u32[]{:S(2)}, u32[]{:S(2)}) collective-permute-start(s32[2,6]{1,0:T(2,128)S(1)} %pad_add_fusion.1), channel_id=1, source_target_pairs={{0,4},{4,0},{8,12},{12,8},{1,5},{5,1},{9,13},{13,9},{2,6},{6,2},{1... | collective-permute-start | bytes 152 | tf_op jit(solution)/shard_map/ppermute | solution.py:107
  16.3 5.9 %collective-permute-start.2 = (s32[2,6]{1,0:T(2,128)S(1)}, s32[2,6]{1,0:T(2,128)S(1)}, u32[]{:S(2)}, u32[]{:S(2)}) collective-permute-start(s32[2,6]{1,0:T(2,128)S(1)} %pad_add_fusion.1), channel_id=1, source_target_pairs={{0,12},{4,8},{8,4},{12,0},{1,13},{5,9},{9,5},{13,1},{2,14},{6,10},... | collective-permute-start | bytes 152 | tf_op jit(solution)/shard_map/ppermute | solution.py:107
  17.7 28.8 %collective-permute-start.5 = (bf16[3,384,256]{2,1,0:T(8,128)(2,1)S(1)}, bf16[3,384,256]{2,1,0:T(8,128)(2,1)}, u32[]{:S(2)}, u32[]{:S(2)}) collective-permute-start(bf16[3,384,256]{2,1,0:T(8,128)(2,1)S(1)} %get-tuple-element.45), channel_id=1, source_target_pairs={{0,4},{1,12},{4,0},{5,8},{8,5},{9,13},{12,1},{13,9},{2,6},{3,14},{... | collective-permute-start | bytes 1769480 | tf_op jit(solution)/shard_map/ppermute | solution.py:324
  18.6 27.9 %collective-permute-start.3 = (bf16[3,384,256]{2,1,0:T(8,128)(2,1)S(1)}, bf16[3,384,256]{2,1,0:T(8,128)(2,1)}, u32[]{:S(2)}, u32[]{:S(2)}) collective-permute-start(bf16[3,384,256]{2,1,0:T(8,128)(2,1)S(1)} %get-tuple-element.46), channel_id=1, source_target_pairs={{0,0},{1,8},{4,4},{5,12},{8,1},{9,9},{12,5},{13,13},{2,2},{3,10},{... | collective-permute-start | bytes 1769480 | tf_op jit(solution)/shard_map/ppermute | solution.py:324
  46.5 57.6 %copy-start.6 = (bf16[3,384,128]{2,1,0:T(8,128)(2,1)S(1)}, bf16[3,384,128]{2,1,0:T(8,128)(2,1)}, u32[]{:S(2)}) copy-start(bf16[3,384,128]{2,1,0:T(8,128)(2,1)} %get-tuple-element.25) | copy-start | bytes 884740
  46.5 35.8 %collective-permute-start.7 = (bf16[3,384,128]{2,1,0:T(8,128)(2,1)S(1)}, bf16[3,384,128]{2,1,0:T(8,128)(2,1)S(1)}, u32[]{:S(2)}, u32[]{:S(2)}) collective-permute-start(bf16[3,384,128]{2,1,0:T(8,128)(2,1)S(1)} %get-tuple-element.24), channel_id=1, source_target_pairs={{0,0},{1,8},{4,4},{5,12},{8,1},{9,9},{12,5},{13,13},{2,2},{3,10},{... | collective-permute-start | bytes 884744 | tf_op jit(solution)/shard_map/ppermute | solution.py:324
  47.3 56.7 %collective-permute-start.9 = (bf16[768,768]{1,0:T(8,128)(2,1)}, bf16[768,768]{1,0:T(8,128)(2,1)S(1)}, u32[]{:S(2)}, u32[]{:S(2)}) collective-permute-start(bf16[768,768]{1,0:T(8,128)(2,1)} %param.8), channel_id=1, source_target_pairs={{0,1},{1,0},{2,3},{3,2},{4,5},{5,4},{6,7},{7,6},{8,9},{9,8},{10,11... | collective-permute-start | bytes 3538952 | tf_op jit(solution)/shard_map/ppermute | solution.py:107
  82.3 18.1 %collective-permute-start.12 = (bf16[384,768]{1,0:T(8,128)(2,1)S(1)}, bf16[384,768]{1,0:T(8,128)(2,1)S(1)}, u32[]{:S(2)}, u32[]{:S(2)}) collective-permute-start(bf16[384,768]{1,0:T(8,128)(2,1)S(1)} %get-tuple-element.26), channel_id=1, source_target_pairs={{0,4},{4,0},{8,12},{12,8},{1,5},{5,1},{9,13},{13,9},{2,6},{6,2},{1... | collective-permute-start | bytes 1769480 | tf_op jit(solution)/shard_map/ppermute | solution.py:107
  89.9 13.3 %collective-permute-start.4 = (bf16[3,384,256]{2,1,0:T(8,128)(2,1)}, bf16[3,384,256]{2,1,0:T(8,128)(2,1)S(1)}, u32[]{:S(2)}, u32[]{:S(2)}) collective-permute-start(bf16[3,384,256]{2,1,0:T(8,128)(2,1)} %collective-permute-done.3.refs_0_), channel_id=1, source_target_pairs={{0,16},{16,0},{1,17},{17,1},{2,18},{18,2},{3,19},{19,3},{4,20},{20... | collective-permute-start | bytes 1769480 | tf_op jit(solution)/shard_map/ppermute | solution.py:107
  100.4 16.3 %collective-permute-start.13 = (bf16[384,768]{1,0:T(8,128)(2,1)S(1)}, bf16[384,768]{1,0:T(8,128)(2,1)S(1)}, u32[]{:S(2)}, u32[]{:S(2)}) collective-permute-start(bf16[384,768]{1,0:T(8,128)(2,1)S(1)} %collective-permute-done.12.refs_6_), channel_id=1, source_target_pairs={{0,16},{16,0},{1,17},{17,1},{2,18},{18,2},{3,19},{19,3},{4,20},{20... | collective-permute-start | bytes 1769480 | tf_op jit(solution)/shard_map/ppermute | solution.py:107
  101.7 27.8 %collective-permute-start.6 = (bf16[3,384,256]{2,1,0:T(8,128)(2,1)}, bf16[3,384,256]{2,1,0:T(8,128)(2,1)}, u32[]{:S(2)}, u32[]{:S(2)}) collective-permute-start(bf16[3,384,256]{2,1,0:T(8,128)(2,1)} %collective-permute-done.5.refs_2_), channel_id=1, source_target_pairs={{0,16},{16,0},{1,17},{17,1},{2,18},{18,2},{3,19},{19,3},{4,20},{20... | collective-permute-start | bytes 1769480 | tf_op jit(solution)/shard_map/ppermute | solution.py:107
  103.2 0.8 copy-start.2
  104.1 12.6 %copy-start.4 = (bf16[768,768]{1,0:T(8,128)(2,1)}, bf16[768,768]{1,0:T(8,128)(2,1)S(1)}, u32[]{:S(2)}) copy-start(bf16[768,768]{1,0:T(8,128)(2,1)S(1)} %collective-permute-done.9) | copy-start | bytes 3538948
  104.1 18.4 %collective-permute-start.10 = (bf16[3,384,128]{2,1,0:T(8,128)(2,1)S(1)}, bf16[3,384,128]{2,1,0:T(8,128)(2,1)}, u32[]{:S(2)}, u32[]{:S(2)}) collective-permute-start(bf16[3,384,128]{2,1,0:T(8,128)(2,1)S(1)} %copy-done.6), channel_id=1, source_target_pairs={{0,4},{1,12},{4,0},{5,8},{8,5},{9,13},{12,1},{13,9},{2,6},{3,14},{... | collective-permute-start | bytes 884744 | tf_op jit(solution)/shard_map/ppermute | solution.py:324
  105.7 36.4 %collective-permute-start.14 = (bf16[384,768]{1,0:T(8,128)(2,1)S(1)}, bf16[384,768]{1,0:T(8,128)(2,1)}, u32[]{:S(2)}, u32[]{:S(2)}) collective-permute-start(bf16[384,768]{1,0:T(8,128)(2,1)S(1)} %collective-permute-done.12.refs_6_), channel_id=1, source_target_pairs={{0,1},{1,0},{2,3},{3,2},{4,5},{5,4},{6,7},{7,6},{8,9},{9,8},{10,11... | collective-permute-start | bytes 1769480 | tf_op jit(solution)/shard_map/ppermute | solution.py:107
  116.7 25.4 %collective-permute-start.15 = (bf16[384,768]{1,0:T(8,128)(2,1)S(1)}, bf16[384,768]{1,0:T(8,128)(2,1)}, u32[]{:S(2)}, u32[]{:S(2)}) collective-permute-start(bf16[384,768]{1,0:T(8,128)(2,1)S(1)} %collective-permute-done.13.refs_7_), channel_id=1, source_target_pairs={{0,1},{1,0},{2,3},{3,2},{4,5},{5,4},{6,7},{7,6},{8,9},{9,8},{10,11... | collective-permute-start | bytes 1769480 | tf_op jit(solution)/shard_map/ppermute | solution.py:107
  121.4 14.3 %collective-permute-start.8 = (bf16[3,384,128]{2,1,0:T(8,128)(2,1)S(1)}, bf16[3,384,128]{2,1,0:T(8,128)(2,1)}, u32[]{:S(2)}, u32[]{:S(2)}) collective-permute-start(bf16[3,384,128]{2,1,0:T(8,128)(2,1)S(1)} %collective-permute-done.7.refs_0_), channel_id=1, source_target_pairs={{0,16},{16,0},{1,17},{17,1},{2,18},{18,2},{3,19},{19,3},{4,20},{20... | collective-permute-start | bytes 884744 | tf_op jit(solution)/shard_map/ppermute | solution.py:107
  122.4 19.6 %collective-permute-start.11 = (bf16[3,384,128]{2,1,0:T(8,128)(2,1)}, bf16[3,384,128]{2,1,0:T(8,128)(2,1)}, u32[]{:S(2)}, u32[]{:S(2)}) collective-permute-start(bf16[3,384,128]{2,1,0:T(8,128)(2,1)} %collective-permute-done.10.refs_2_), channel_id=1, source_target_pairs={{0,16},{16,0},{1,17},{17,1},{2,18},{18,2},{3,19},{19,3},{4,20},{20... | collective-permute-start | bytes 884744 | tf_op jit(solution)/shard_map/ppermute | solution.py:107
  142.1 1.9 copy-start.1
  144.0 1.1 copy-start.3
  150.5 6.0 %collective-permute-start.17 = (bf16[4,320,512]{2,1,0:T(8,128)(2,1)S(1)}, bf16[4,320,512]{2,1,0:T(8,128)(2,1)S(1)}, u32[]{:S(2)}, u32[]{:S(2)}) collective-permute-start(bf16[4,320,512]{2,1,0:T(8,128)(2,1)S(1)} %get-tuple-element.28), channel_id=1, source_target_pairs={{0,1},{1,0},{2,3},{3,2},{4,5},{5,4},{6,7},{7,6},{8,9},{9,8},{10,11... | collective-permute-start | bytes 3932168 | tf_op jit(solution)/shard_map/ppermute | solution.py:107
  156.5 3.9 %collective-permute-start.16 = (bf16[4,320,256]{2,1,0:T(8,128)(2,1)S(1)}, bf16[4,320,256]{2,1,0:T(8,128)(2,1)S(1)}, u32[]{:S(2)}, u32[]{:S(2)}) collective-permute-start(bf16[4,320,256]{2,1,0:T(8,128)(2,1)S(1)} %get-tuple-element.32), channel_id=1, source_target_pairs={{0,1},{1,0},{2,3},{3,2},{4,5},{5,4},{6,7},{7,6},{8,9},{9,8},{10,11... | collective-permute-start | bytes 1966088 | tf_op jit(solution)/shard_map/ppermute | solution.py:107
  160.3 6.7 %copy-start.5 = (bf16[768,768]{1,0:T(8,128)(2,1)S(1)}, bf16[768,768]{1,0:T(8,128)(2,1)}, u32[]{:S(2)}) copy-start(bf16[768,768]{1,0:T(8,128)(2,1)} %copy-done.4) | copy-start | bytes 3538948
  162.6 19.6 %collective-permute-start.20 = (bf16[2,128,384]{2,1,0:T(8,128)(2,1)S(1)}, bf16[2,128,384]{2,1,0:T(8,128)(2,1)S(1)}, u32[]{:S(2)}, u32[]{:S(2)}) collective-permute-start(bf16[2,128,384]{2,1,0:T(8,128)(2,1)S(1)} %get-tuple-element.38), channel_id=1, source_target_pairs={{0,12},{4,8},{8,4},{12,0},{1,13},{5,9},{9,5},{13,1},{2,14},{6,10},... | collective-permute-start | bytes 589832 | tf_op jit(solution)/shard_map/ppermute | solution.py:107
  163.2 19.0 %collective-permute-start.18 = (bf16[2,128,384]{2,1,0:T(8,128)(2,1)S(1)}, bf16[2,128,384]{2,1,0:T(8,128)(2,1)S(1)}, u32[]{:S(2)}, u32[]{:S(2)}) collective-permute-start(bf16[2,128,384]{2,1,0:T(8,128)(2,1)S(1)} %get-tuple-element.38), channel_id=1, source_target_pairs={{0,4},{4,0},{8,12},{12,8},{1,5},{5,1},{9,13},{13,9},{2,6},{6,2},{1... | collective-permute-start | bytes 589832 | tf_op jit(solution)/shard_map/ppermute | solution.py:107
  163.2 19.0 %collective-permute-start.19 = (bf16[2,128,384]{2,1,0:T(8,128)(2,1)S(1)}, bf16[2,128,384]{2,1,0:T(8,128)(2,1)S(1)}, u32[]{:S(2)}, u32[]{:S(2)}) collective-permute-start(bf16[2,128,384]{2,1,0:T(8,128)(2,1)S(1)} %get-tuple-element.37.refs_0_), channel_id=1, source_target_pairs={{0,8},{4,12},{8,0},{12,4},{1,9},{5,13},{9,1},{13,5},{2,10},{6,14},... | collective-permute-start | bytes 589832 | tf_op jit(solution)/shard_map/ppermute | solution.py:107
  185.8 6.6 %collective-permute-start.21 = (bf16[2,64,768]{2,1,0:T(8,128)(2,1)S(1)}, bf16[2,64,768]{2,1,0:T(8,128)(2,1)S(1)}, u32[]{:S(2)}, u32[]{:S(2)}) collective-permute-start(bf16[2,64,768]{2,1,0:T(8,128)(2,1)S(1)} %get-tuple-element.40), channel_id=1, source_target_pairs={{0,2},{2,0},{1,3},{3,1},{4,6},{6,4},{5,7},{7,5},{8,10},{10,8},{9,1... | collective-permute-start | bytes 589832 | tf_op jit(solution)/shard_map/ppermute | solution.py:107
  186.9 14.1 %collective-permute-start.22 = (bf16[2,64,768]{2,1,0:T(8,128)(2,1)S(1)}, bf16[2,64,768]{2,1,0:T(8,128)(2,1)S(1)}, u32[]{:S(2)}, u32[]{:S(2)}) collective-permute-start(bf16[2,64,768]{2,1,0:T(8,128)(2,1)S(1)} %get-tuple-element.41), channel_id=1, source_target_pairs={{0,8},{4,12},{8,0},{12,4},{1,9},{5,13},{9,1},{13,5},{2,10},{6,14},... | collective-permute-start | bytes 589832 | tf_op jit(solution)/shard_map/ppermute | solution.py:107
  186.9 18.8 %collective-permute-start.23 = (bf16[2,64,768]{2,1,0:T(8,128)(2,1)S(1)}, bf16[2,64,768]{2,1,0:T(8,128)(2,1)S(1)}, u32[]{:S(2)}, u32[]{:S(2)}) collective-permute-start(bf16[2,64,768]{2,1,0:T(8,128)(2,1)S(1)} %get-tuple-element.42), channel_id=1, source_target_pairs={{0,10},{2,8},{4,14},{6,12},{8,2},{10,0},{12,6},{14,4},{1,11},{3,9}... | collective-permute-start | bytes 589832 | tf_op jit(solution)/shard_map/ppermute | solution.py:363
Sparse Core Ops, SparseCore 0:
  9.5 75.4 all-gather.1

commit v14 on v12

--- a/solution.py
+++ b/solution.py
@@ -128,7 +128,7 @@
 
 
 def project(place, mine, theirs, chunks):
-    rows, (count, width) = len(mine), mine[0].shape
+    rows, (count, width) = len(mine), theirs[0].shape
     _, half, cols = chunks[0][0].shape
     slices = len(chunks)
     flat = [w for of_round in chunks for w in of_round]
@@ -136,23 +136,21 @@
     def kernel(place_ref, *refs):
         row, group, frame, core = (place_ref[i] for i in range(4))
         x_refs, w_refs = refs[: 2 * rows], refs[2 * rows : 2 * rows + len(flat)]
-        q_keep, kv_keep, send, x_all, total, sems = refs[2 * rows + len(flat) :]
+        q_keep, kv_keep, send, x_all, w_all, total, sems = refs[2 * rows + len(flat) :]
         copies = []
         for i, x_ref in enumerate(x_refs):
             to = x_all.at[row ^ (i % rows), (frame + i // rows) % 2]
-            copies.append(pltpu.make_async_copy(x_ref, to, sems.at[i]))
+            copies.append(pltpu.make_async_copy(x_ref.at[pl.ds(0, count)], to, sems.at[i]))
             copies[-1].start()
-        for copy in copies:
-            copy.wait()
-        acc = None
         for k in range(slices):
             for g in range(2):
                 at = (row + slices - k) % slices * (2 * half) + (group + g) % 2 * half
-                piece = x_all[:, :, :, pl.ds(pl.multiple_of(at, half), half)].reshape(-1, half)
-                w_ref = w_refs[2 * k + g]
-                weight = jnp.concatenate([w_ref[part] for part in range(3)], axis=1)
-                term = jnp.dot(piece, weight, preferred_element_type=jnp.float32)
-                acc = term if acc is None else acc + term
+                for part in range(3):
+                    into = w_all.at[pl.ds(pl.multiple_of(at, half), half), part * cols : (part + 1) * cols]
+                    into[...] = w_refs[2 * k + g][part]
+        for copy in copies:
+            copy.wait()
+        acc = jnp.dot(x_all[...].reshape(-1, width), w_all[...], preferred_element_type=jnp.float32)
         kv_part = acc[:, cols:].reshape(rows, 2 * count, 2 * cols)
         kv_keep[...] = kv_part
         send[:, : 2 * count, :] = kv_part.astype(jnp.bfloat16)
@@ -164,7 +162,7 @@
             at = slice(f * cols, (f + 1) * cols)
             send[:, 2 * count :, at] = total[:, f, pl.ds(other, BS), :].astype(jnp.bfloat16)
 
-    vmem, anywhere = pl.BlockSpec(memory_space=pltpu.VMEM), pl.BlockSpec(memory_space=pl.ANY)
+    vmem, hbm = pl.BlockSpec(memory_space=pltpu.VMEM), pl.BlockSpec(memory_space=pltpu.HBM)
     flops = 2 * rows * 2 * count * width * 3 * cols
     return pl.pallas_call(
         kernel,
@@ -176,10 +174,11 @@
         grid_spec=pltpu.PrefetchScalarGridSpec(
             num_scalar_prefetch=1,
             grid=(),
-            in_specs=[anywhere] * (2 * rows) + [vmem] * len(flat),
+            in_specs=[hbm] * (2 * rows) + [vmem] * len(flat),
             out_specs=(vmem, vmem, vmem),
             scratch_shapes=[
                 pltpu.VMEM((rows, 2, count, width), jnp.bfloat16),
+                pltpu.VMEM((width, 3 * cols), jnp.bfloat16),
                 pltpu.VMEM((rows, 2, count, cols), jnp.float32),
                 pltpu.SemaphoreType.DMA((2 * rows,)),
             ],
@@ -246,41 +245,44 @@
     )
 
 
-def mix(place, attended, w_parts):
+def mix(place, attended, w_own, w_across, beside, beside_across):
     blocks, block_len, cols = attended[0].shape
-    width = w_parts[0].shape[1]
+    width = w_own.shape[1]
 
     def kernel(place_ref, *refs):
         row, group, frame, core = (place_ref[i] for i in range(4))
-        w_refs = refs[4:12]
-        keep, over_x, over_z, over_both, a_all, sums = refs[12:]
+        w_refs = refs[4:10]
+        near_keep, near_send, far_keep, far_send, a_all, sums = refs[10:]
         for s in range(4):
             a_all[s] = refs[s][...].reshape(blocks * block_len, cols)
 
-        def term(c, first, side):
+        def term(c, other):
+            side = 1 - core if other else core
             acc = None
             for i in range(2):
-                at = 2 * side + (i if c == 0 else (i + group) % 2)
-                part = jnp.dot(a_all[at ^ row], w_refs[first + i][...], preferred_element_type=jnp.float32)
+                if c == 0:
+                    weight, half = w_refs[other][i * cols : (i + 1) * cols, :], i
+                else:
+                    weight, half = w_refs[2 + 2 * other + i][...], (i + group) % 2
+                part = jnp.dot(a_all[(2 * side + half) ^ row], weight, preferred_element_type=jnp.float32)
                 acc = part if acc is None else acc + part
             return acc.astype(jnp.bfloat16).astype(jnp.float32)
 
         for c in range(2):
-            total = term(c, 2 * c, core) + term(c, 4 + 2 * c, 1 - core)
-            sums[...] = total.reshape(blocks, 2, BS, width)
+            sums[...] = (term(c, 0) + term(c, 1)).reshape(blocks, 2, BS, width)
             at = (row + c) % 2
-            keep[at] = sums[row // 2, frame]
-            over_x[at] = sums[row // 2, 1 - frame].astype(jnp.bfloat16)
-            over_z[at] = sums[1 - row // 2, frame].astype(jnp.bfloat16)
-            over_both[at] = sums[1 - row // 2, 1 - frame].astype(jnp.bfloat16)
-
-    shape = (2, BS, width)
-    sent = jax.ShapeDtypeStruct(shape, jnp.bfloat16)
+            near_keep[at] = sums[row // 2, frame]
+            near_send[at] = sums[row // 2, 1 - frame].astype(jnp.bfloat16)
+            far_keep[at] = sums[1 - row // 2, frame]
+            far_send[at] = sums[1 - row // 2, 1 - frame].astype(jnp.bfloat16)
+
+    kept = jax.ShapeDtypeStruct((2, BS, width), jnp.float32)
+    sent = jax.ShapeDtypeStruct((2, BS, width), jnp.bfloat16)
     return call(
         kernel,
-        (jax.ShapeDtypeStruct(shape, jnp.float32), sent, sent, sent),
+        (kept, sent, kept, sent),
         [place],
-        [*attended, *w_parts],
+        [*attended, w_own, w_across, *beside, *beside_across],
         scratch=[
             pltpu.VMEM((4, blocks * block_len, cols), jnp.bfloat16),
             pltpu.VMEM((blocks, 2, BS, width), jnp.float32),
@@ -290,25 +292,23 @@
     )
 
 
-def finish(place, keep, from_x, from_z, from_both):
-    halves, rows, width = keep.shape
-
-    def kernel(place_ref, keep_ref, x_ref, z_ref, both_ref, out_ref):
+def finish(place, near_keep, near_more, far):
+    halves, rows, width = near_keep.shape
+
+    def kernel(place_ref, keep_ref, more_ref, far_ref, out_ref):
         pair = place_ref[0] // 2
         for c in range(halves):
-            near = pl.multiple_of((pair * halves + c) * width, width)
-            far = pl.multiple_of(((1 - pair) * halves + c) * width, width)
-            out_ref[:, pl.ds(near, width)] = (keep_ref[c] + x_ref[c].astype(jnp.float32)).astype(jnp.bfloat16)
-            out_ref[:, pl.ds(far, width)] = (
-                z_ref[c].astype(jnp.float32) + both_ref[c].astype(jnp.float32)
-            ).astype(jnp.bfloat16)
+            here = pl.multiple_of((pair * halves + c) * width, width)
+            there = pl.multiple_of(((1 - pair) * halves + c) * width, width)
+            out_ref[:, pl.ds(here, width)] = (keep_ref[c] + more_ref[c].astype(jnp.float32)).astype(jnp.bfloat16)
+            out_ref[:, pl.ds(there, width)] = far_ref[c]
 
     return call(
         kernel,
         jax.ShapeDtypeStruct((rows, 2 * halves * width), jnp.bfloat16),
         [place],
-        [keep, from_x, from_z, from_both],
-        read=16 * rows * halves * width,
+        [near_keep, near_more, far],
+        read=12 * rows * halves * width,
     )
 
 
@@ -316,6 +316,7 @@
     rows_n, heads_n = lax.axis_size("rows"), lax.axis_size("heads")
     group, row = lax.axis_index("groups"), lax.axis_index("rows")
     frame, core = lax.axis_index("frames"), lax.axis_index("heads")
+    count = latents.shape[1]
     depth, _, local_cols = w_qkv.shape
     span = rows_n // heads_n
     cols = local_cols // span
@@ -337,57 +338,51 @@
         ]
         return lax.ppermute(after(value, *others) if others else value, ("rows", "heads"), pairs)
 
+    mine = lax.dynamic_slice_in_dim(latents[0], core * span * depth, span * depth, axis=1)
+    mine_x = swap(mine, "frames")
+    here, there = [reshard(0)], []
     tables = jnp.concatenate([win_blocks, win_counts[:, None], block_window[:, None]], axis=1)
-    found = [tables] + [swap(tables, "rows", s) for s in range(1, rows_n)]
-    tables = jnp.stack(found)[row ^ jnp.arange(rows_n)].reshape(rows_n * heads_n, MAXB + 2)
-    windows = lax.dynamic_index_in_dim(
-        tables[:, MAXB + 1].reshape(rows_n, heads_n), core, axis=1, keepdims=False
-    )
-    picked = tables[windows]
-    members, counts = picked[:, :MAXB].reshape(-1), picked[:, MAXB]
-
-    mine = lax.dynamic_slice_in_dim(latents[0], core * span * depth, span * depth, axis=1)
-    near, mine_x = swap(mine, "rows"), swap(mine, "frames")
-    here, there = [reshard(0)], []
-    far_2 = swap(after(mine, members, counts), "rows", 2)
-    here.append(reshard(1, near, mine_x, here[0]))
+    tables = jnp.pad(tables, ((0, 8 - heads_n), (0, span * depth - MAXB - 2))).astype(mine.dtype)
+    joined = jnp.concatenate([mine, tables], axis=0)
+    near = swap(joined, "rows")
     near_x = swap(near, "frames")
     across = swap(after(w_out, near), "heads")
     there.append(swap(here[0], "groups"))
-    far_3 = swap(after(mine, here[0], near_x), "rows", 3)
-    here.append(reshard(2, far_2, across))
+    here.append(reshard(1, near, mine_x, here[0]))
+    far_2 = swap(after(joined, here[0]), "rows", 2)
+    there.append(swap(here[1], "groups"))
     far_2x = swap(far_2, "frames")
-    here.append(reshard(3, here[1], there[0], far_2x))
-    there.append(swap(here[1], "groups"))
-    far_3x = swap(far_3, "frames")
-    there += [swap(here[2], "groups"), swap(here[3], "groups")]
-
+    far_3 = swap(after(joined, far_2), "rows", 3)
+    here.append(reshard(2, far_2, near_x, there[0], across))
     out_half = lax.dynamic_slice_in_dim(w_out, group * cols, cols, axis=0)
-    beside = [swap(after(out_half, here[3]), "rows")]
-
-    pieces = [mine, near, far_2, far_3], [mine_x, near_x, far_2x, far_3x]
-    first = project(place, *pieces, [(here[0], there[0]), (here[1], after(there[1], there[2]))])
+    beside = [swap(after(out_half, far_2), "rows")]
+    here.append(reshard(3, here[1]))
+    far_3x = swap(after(far_3, here[2], there[1]), "frames")
+    there += [swap(here[2], "groups"), swap(after(here[3], beside[0]), "groups")]
+
+    found = jnp.stack([x[count : count + heads_n, : MAXB + 2] for x in (joined, near, far_2, far_3)])
+    tables = found.astype(jnp.int32)[row ^ jnp.arange(rows_n)].reshape(rows_n * heads_n, MAXB + 2)
+    windows = lax.dynamic_index_in_dim(
+        tables[:, MAXB + 1].reshape(rows_n, heads_n), core, axis=1, keepdims=False
+    )
+    picked = tables[windows]
+    members, counts = picked[:, :MAXB].reshape(-1), picked[:, MAXB]
+
+    pieces = [joined, near, far_2, far_3], [mine_x, near_x, far_2x, far_3x]
+    first = project(place, *pieces, [(here[0], there[0]), (here[1], after(there[1], there[2], members, counts))])
+    beside.append(swap(after(beside[0], first[2]), "groups"))
     first_more = swap(first[2], "heads")
     second = project(place, *pieces, [(here[2], there[2]), (here[3], after(there[3], first[2]))])
     second_more = swap(second[2], "heads")
-    attended = attend_all(place, members, counts, first[0], after(first[1], beside[0]), first_more)
-    beside.append(swap(after(beside[0], attended[0]), "groups"))
+    attended = attend_all(place, members, counts, *first[:2], first_more)
     same, diff = attend_all(place, members, counts, *second[:2], second_more, attended)
     attended = [same] + [swap(same if s % 2 == 0 else diff, "rows", s) for s in range(1, rows_n)]
-    halves = [w_out[:cols], w_out[cols:], *beside]
     beside_across = [swap(part, "heads") for part in (beside[0], after(beside[1], *attended[1:]))]
-    keep, over_x, over_z, over_both = mix(
-        place, attended, [*halves, across[:cols], across[cols:], *beside_across]
-    )
-    from_x = swap(over_x, "frames")
-    from_z = swap(over_z, "rows", 2)
-    from_both = lax.ppermute(
-        over_both,
-        ("rows", "frames"),
-        [(2 * r + f, 2 * (r ^ 2) + 1 - f) for r in range(rows_n) for f in range(2)],
-    )
-    out = finish(place, keep, from_x, from_z, from_both)
-    return out[None]
+    near_keep, near_send, far_keep, far_send = mix(place, attended, w_out, across, beside, beside_across)
+    far_more = swap(far_send, "frames")
+    far = swap((far_keep + far_more.astype(jnp.float32)).astype(jnp.bfloat16), "rows", 2)
+    near_more = swap(after(near_send, far_more), "frames")
+    return finish(place, near_keep, near_more, far)[None]
 
 
 def local(latents, w_qkv, w_out, win_blocks, win_counts, block_window):

time: 181 us -> 171 us (0.945)
  waiting for transfers between devices: 107 us -> 76.6 us
  starting transfers between devices: 35.6 us -> 50.7 us
  other arithmetic: 0.55 us -> 4.36 us
    ppermute x26 -> x24, waiting for transfers between devices: 96.1 us -> 72.2 us  [swap(): return lax.ppermute(value, axis, [(i, i ^ step) for i in range(peers)])]
    ppermute x26 -> x24, starting transfers between devices: 33.5 us -> 42.9 us  [swap(): return lax.ppermute(value, axis, [(i, i ^ step) for i in range(peers)])]
    ppermute x4, starting transfers between devices: 2.08 us -> 7.74 us  [reshard(): lax.ppermute(after(value, *others) if others else value, ('rows', 'heads'...]
    ppermute x1 -> x0, waiting for transfers between devices: 3.39 us -> none  [by_heads(): lax.ppermute(over_both, ('rows', 'frames'), [(2 * r + f, 2 * (r ^ 2) + 1...]
    ppermute x4, waiting for transfers between devices: 7.49 us -> 4.44 us  [reshard(): lax.ppermute(after(value, *others) if others else value, ('rows', 'heads'...]
    another operation x0 -> x3, local copies, waits for them, and re-layouts: none -> 2.03 us  [by_heads(): jnp.stack([x[count:count + heads_n, :MAXB + 2] for x in (joined, near, fa...]
  transfers between devices with their start and end apart: 31 -> 28, of which waited for: 15 -> 11; matrix products, arithmetic and copies ran while one was open for 4% -> 6% of each run, Pallas kernels for 10% -> 10%
where the time goes in v14:
time: 171 us
  waiting for transfers between devices  76.6 us (45%)
  starting transfers between devices  50.7 us (30%)
  Pallas kernels  22.6 us (13%)
  local copies, waits for them, and re-layouts  16.1 us (9%)
  other arithmetic  4.36 us (3%)
    ppermute x24, waiting for transfers between devices, swap(): return lax.ppermute(value, axis, [(i, i ^ step) for i in range(peers)])  72.2 us
    ppermute x24, starting transfers between devices, swap(): return lax.ppermute(value, axis, [(i, i ^ step) for i in range(peers)])  42.9 us
    pallas_call x2, Pallas kernels, project(): pl.pallas_call(kernel, out_shape=(jax.ShapeDtypeStruct((rows, 2 * BS, col...  11.8 us
    pallas_call x4, Pallas kernels, call(): pl.pallas_call(kernel, out_shape=out_shape, grid_spec=pltpu.PrefetchScala...  10.8 us
    ppermute x4, starting transfers between devices, reshard(): lax.ppermute(after(value, *others) if others else value, ('rows', 'heads'...  7.74 us
    unnamed x28, local copies, waits for them, and re-layouts  6.57 us
    ppermute x4, waiting for transfers between devices, reshard(): lax.ppermute(after(value, *others) if others else value, ('rows', 'heads'...  4.44 us
    dynamic_slice x2, local copies, waits for them, and re-layouts, reshard(): lax.dynamic_slice(w_qkv.transpose(1, 0, 2), (0, group * half, (k + row) %...  3.99 us
  transfers between devices with their start and end apart: 28, of which 11 were waited for; matrix products, arithmetic and copies ran while one was open for 6% of the time, Pallas kernels for 10%

profile of v14, /device:TPU:0, one launch (start us, length us, event | category | flops | bytes accessed | tf_op | source)
XLA Modules:
  0.0 170.5 jit_solution(11349442138057047481)
XLA Ops:
  2.3 0.8 dynamic-slice_bitcast_fusion.2
  3.1 1.0 fusion.1.refs_0_
  4.2 3.1 %collective-permute-start = (bf16[136,1536]{1,0:T(8,128)(2,1)S(1)}, bf16[136,1536]{1,0:T(8,128)(2,1)}, u32[]{:S(2)}, u32[]{:S(2)}) collective-permute-start(bf16[136,1536]{1,0:T(8,128)(2,1)S(1)} %fusion.1.refs_0_), channel_id=1, source_target_pairs={{0,4},{4,0},{8,12},{12,8},{1,5},{5,1},{9,13},{13,9},{2,6},{6,2},{1... | collective-permute-start | bytes 1253384 | tf_op jit(solution)/shard_map/ppermute | solution.py:107
  7.3 2.2 %dynamic-slice_bitcast_fusion = (bf16[3,384,256]{2,1,0:T(8,128)(2,1)}, bf16[3,384,256]{2,1,0:T(8,128)(2,1)S(1)}) fusion(bf16[768,3,768]{2,0,1:T(8,128)(2,1)} %param.7, s32[]{:T(128)S(6)} %select_n.56, s32[]{:T(128)S(6)} %select_n.64, s32[]{:T(128)S(6)} %select_n.58), kind=kLoop, calls=%fused_computation.4 | loop fusion | bytes 2359308 | tf_op jit(solution)/shard_map/dynamic_slice | solution.py:331
  9.4 1.5 collective-permute-start.1
  11.0 1.5 collective-permute-start.4
  12.4 8.3 %collective-permute-done.refs_1_ = bf16[136,1536]{1,0:T(8,128)(2,1)} collective-permute-done((bf16[136,1536]{1,0:T(8,128)(2,1)S(1)}, bf16[136,1536]{1,0:T(8,128)(2,1)}, u32[]{:S(2)}, u32[]{:S(2)}) %collective-permute-start) | collective-permute-done | bytes 417824 | tf_op jit(solution)/shard_map/ppermute | solution.py:107
  21.0 7.8 %collective-permute-start.2 = (bf16[136,1536]{1,0:T(8,128)(2,1)}, bf16[136,1536]{1,0:T(8,128)(2,1)}, u32[]{:S(2)}, u32[]{:S(2)}) collective-permute-start(bf16[136,1536]{1,0:T(8,128)(2,1)} %copy-done.2), channel_id=1, source_target_pairs={{0,8},{4,12},{8,0},{12,4},{1,9},{5,13},{9,1},{13,5},{2,10},{6,14},... | collective-permute-start | bytes 1253384 | tf_op jit(solution)/shard_map/ppermute | solution.py:107
  29.5 1.6 collective-permute-start.7
  31.1 0.9 constant_dynamic-slice_fusion
  32.0 1.5 collective-permute-start.5
  33.5 1.8 %dynamic-slice_bitcast_fusion.3 = (bf16[3,384,128]{2,1,0:T(8,128)(2,1)}, bf16[3,384,128]{2,1,0:T(8,128)(2,1)S(1)}) fusion(bf16[768,3,768]{2,0,1:T(8,128)(2,1)} %param.7, s32[]{:T(128)S(6)} %select_n.56, s32[]{:T(128)S(6)} %select_n.65, s32[]{:T(128)S(6)} %select_n.62), kind=kLoop, calls=%fused_computation.9 | loop fusion | bytes 1179660 | tf_op jit(solution)/shard_map/dynamic_slice | solution.py:331
  35.4 25.8 %collective-permute-done.2.refs_2_ = bf16[136,1536]{1,0:T(8,128)(2,1)} collective-permute-done((bf16[136,1536]{1,0:T(8,128)(2,1)}, bf16[136,1536]{1,0:T(8,128)(2,1)}, u32[]{:S(2)}, u32[]{:S(2)}) %collective-permute-start.2) | collective-permute-done | bytes 417824 | tf_op jit(solution)/shard_map/ppermute | solution.py:107
  61.2 1.6 collective-permute-start.11
  63.5 0.8 copy-done.10
  64.3 0.8 copy-done.6
  65.1 1.4 collective-permute-start.9
  67.1 1.5 collective-permute-start.6
  68.6 7.0 %collective-permute-done.3.refs_3_ = bf16[136,1536]{1,0:T(8,128)(2,1)} collective-permute-done((bf16[136,1536]{1,0:T(8,128)(2,1)S(1)}, bf16[136,1536]{1,0:T(8,128)(2,1)}, u32[]{:S(2)}, u32[]{:S(2)}) %collective-permute-start.3) | collective-permute-done | bytes 417824 | tf_op jit(solution)/shard_map/ppermute | solution.py:107
  75.7 4.7 %collective-permute-start.14 = (bf16[3,384,128]{2,1,0:T(8,128)(2,1)}, bf16[3,384,128]{2,1,0:T(8,128)(2,1)}, u32[]{:S(2)}, u32[]{:S(2)}) collective-permute-start(bf16[3,384,128]{2,1,0:T(8,128)(2,1)} %get-tuple-element.39), channel_id=1, source_target_pairs={{0,4},{1,12},{4,0},{5,8},{8,5},{9,13},{12,1},{13,9},{2,6},{3,14},{... | collective-permute-start | bytes 884744 | tf_op jit(solution)/shard_map/ppermute | solution.py:339
  81.1 0.8 copy-done.8
  81.9 1.5 collective-permute-start.12
  84.0 1.6 collective-permute-start.13
  86.9 4.4 %collective-permute-done.14.refs_10_ = bf16[3,384,128]{2,1,0:T(8,128)(2,1)} collective-permute-done((bf16[3,384,128]{2,1,0:T(8,128)(2,1)}, bf16[3,384,128]{2,1,0:T(8,128)(2,1)}, u32[]{:S(2)}, u32[]{:S(2)}) %collective-permute-start.14) | collective-permute-done | bytes 294944 | tf_op jit(solution)/shard_map/ppermute | solution.py:339
  91.3 1.5 collective-permute-start.16
  92.8 1.0 copy-done.4
  93.8 1.1 copy-done.7
  94.9 1.1 copy-done.9
  96.0 1.0 copy-done.11
  97.0 6.3 %shard_map.64 = (f32[4,128,256]{2,1,0:T(8,128)S(1)}, f32[4,256,512]{2,1,0:T(8,128)S(1)}, bf16[4,320,512]{2,1,0:T(8,128)(2,1)S(1)}) custom-call(s32[4]{0:T(128)S(1)} %pad_add_fusion.place_ref, bf16[136,1536]{1,0:T(8,128)(2,1)S(1)} %copy-done.4, bf16[136,1536]{1,0:T(8,128)(2,1)} %collective-permute-done.refs_1_, ...), custom_call_target="tpu_custom_call" | custom-call | flops 19327352832 | bytes 8053063 | tf_op jit(solution)/shard_map/pallas_call | solution.py:167
  103.3 8.7 %collective-permute-start.18 = (bf16[4,320,512]{2,1,0:T(8,128)(2,1)S(1)}, bf16[4,320,512]{2,1,0:T(8,128)(2,1)S(1)}, u32[]{:S(2)}, u32[]{:S(2)}) collective-permute-start(bf16[4,320,512]{2,1,0:T(8,128)(2,1)S(1)} %get-tuple-element.43), channel_id=1, source_target_pairs={{0,1},{1,0},{2,3},{3,2},{4,5},{5,4},{6,7},{7,6},{8,9},{9,8},{10,11... | collective-permute-start | bytes 3932168 | tf_op jit(solution)/shard_map/ppermute | solution.py:107
  112.0 5.5 %shard_map.65 = (f32[4,128,128]{2,1,0:T(8,128)S(1)}, f32[4,256,256]{2,1,0:T(8,128)S(1)}, bf16[4,320,256]{2,1,0:T(8,128)(2,1)S(1)}) custom-call(s32[4]{0:T(128)S(1)} %pad_add_fusion.place_ref, bf16[136,1536]{1,0:T(8,128)(2,1)S(1)} %copy-done.5, bf16[136,1536]{1,0:T(8,128)(2,1)} %collective-permute-done.refs_1_, ...), custom_call_target="tpu_custom_call" | custom-call | flops 9663676416 | bytes 4026531 | tf_op jit(solution)/shard_map/pallas_call | solution.py:167
  117.6 1.6 collective-permute-start.22
  119.2 3.8 %shard_map.66 = (bf16[2,128,256]{2,1,0:T(8,128)(2,1)S(1)}, bf16[2,128,256]{2,1,0:T(8,128)(2,1)S(1)}) custom-call(s32[4]{0:T(128)S(1)} %pad_add_fusion.place_ref, s32[16]{0:T(128)S(1)} %reshape.24.members_ref, s32[4]{0:T(128)S(1)} %slice_reduce_fusion.1.counts_ref, f32[4,128,256]{2,1,0:T(8,128)S(1)} %get-tuple-element.48.q_ref, ...), custom_call_target="tpu_custom_call" | custom-call | flops 268435456 | bytes 2097152 | tf_op jit(solution)/shard_map/pallas_call | solution.py:115
  123.0 2.2 %shard_map.67 = (bf16[2,128,384]{2,1,0:T(8,128)(2,1)S(1)}, bf16[2,128,384]{2,1,0:T(8,128)(2,1)S(1)}) custom-call(s32[4]{0:T(128)S(1)} %pad_add_fusion.place_ref, s32[16]{0:T(128)S(1)} %reshape.24.members_ref, s32[4]{0:T(128)S(1)} %slice_reduce_fusion.1.counts_ref, f32[4,128,128]{2,1,0:T(8,128)S(1)} %get-tuple-element.45.q_ref, ...), custom_call_target="tpu_custom_call" | custom-call | flops 134217728 | bytes 1048576 | tf_op jit(solution)/shard_map/pallas_call | solution.py:115
  125.2 1.1 collective-permute-start.19
  126.3 0.9 collective-permute-start.20
  127.2 2.4 %collective-permute-start.21 = (bf16[2,128,384]{2,1,0:T(8,128)(2,1)S(1)}, bf16[2,128,384]{2,1,0:T(8,128)(2,1)S(1)}, u32[]{:S(2)}, u32[]{:S(2)}) collective-permute-start(bf16[2,128,384]{2,1,0:T(8,128)(2,1)S(1)} %get-tuple-element.53), channel_id=1, source_target_pairs={{0,12},{4,8},{8,4},{12,0},{1,13},{5,9},{9,5},{13,1},{2,14},{6,10},... | collective-permute-start | bytes 589832 | tf_op jit(solution)/shard_map/ppermute | solution.py:107
  129.6 3.9 %collective-permute-done.22.refs_7_ = bf16[384,768]{1,0:T(8,128)(2,1)S(1)} collective-permute-done((bf16[384,768]{1,0:T(8,128)(2,1)}, bf16[384,768]{1,0:T(8,128)(2,1)S(1)}, u32[]{:S(2)}, u32[]{:S(2)}) %collective-permute-start.22) | collective-permute-done | bytes 589856 | tf_op jit(solution)/shard_map/ppermute | solution.py:107
  133.5 2.1 %collective-permute-done.19.refs_1_ = bf16[2,128,384]{2,1,0:T(8,128)(2,1)S(1)} collective-permute-done((bf16[2,128,384]{2,1,0:T(8,128)(2,1)S(1)}, bf16[2,128,384]{2,1,0:T(8,128)(2,1)S(1)}, u32[]{:S(2)}, u32[]{:S(2)}) %collective-permute-start.19) | collective-permute-done | bytes 196640 | tf_op jit(solution)/shard_map/ppermute | solution.py:107
  135.6 7.8 %collective-permute-done.20.refs_2_ = bf16[2,128,384]{2,1,0:T(8,128)(2,1)S(1)} collective-permute-done((bf16[2,128,384]{2,1,0:T(8,128)(2,1)S(1)}, bf16[2,128,384]{2,1,0:T(8,128)(2,1)S(1)}, u32[]{:S(2)}, u32[]{:S(2)}) %collective-permute-start.20) | collective-permute-done | bytes 196640 | tf_op jit(solution)/shard_map/ppermute | solution.py:107
  143.4 2.0 %collective-permute-done.24.refs_9_ = bf16[384,768]{1,0:T(8,128)(2,1)S(1)} collective-permute-done((bf16[384,768]{1,0:T(8,128)(2,1)S(1)}, bf16[384,768]{1,0:T(8,128)(2,1)S(1)}, u32[]{:S(2)}, u32[]{:S(2)}) %collective-permute-start.24) | collective-permute-done | bytes 589856 | tf_op jit(solution)/shard_map/ppermute | solution.py:107
  145.4 3.5 %shard_map.68 = (f32[2,64,768]{2,1,0:T(8,128)S(1)}, bf16[2,64,768]{2,1,0:T(8,128)(2,1)S(1)}, f32[2,64,768]{2,1,0:T(8,128)S(1)}, bf16[2,64,768]{2,1,0:T(8,128)(2,1)S(1)}) custom-call(s32[4]{0:T(128)S(1)} %pad_add_fusion.place_ref, bf16[2,128,384]{2,1,0:T(8,128)(2,1)S(1)} %get-tuple-element.52.refs_0_, ...), custom_call_target="tpu_custom_call" | custom-call | flops 1207959552 | bytes 4718592 | tf_op jit(solution)/shard_map/pallas_call | solution.py:115
  149.0 6.9 %collective-permute-done.25 = bf16[2,64,768]{2,1,0:T(8,128)(2,1)S(1)} collective-permute-done((bf16[2,64,768]{2,1,0:T(8,128)(2,1)S(1)}, bf16[2,64,768]{2,1,0:T(8,128)(2,1)S(1)}, u32[]{:S(2)}, u32[]{:S(2)}) %collective-permute-start.25) | collective-permute-done | bytes 196640 | tf_op jit(solution)/shard_map/ppermute | solution.py:107
  156.3 4.7 %collective-permute-start.27 = (bf16[2,64,768]{2,1,0:T(8,128)(2,1)S(1)}, bf16[2,64,768]{2,1,0:T(8,128)(2,1)S(1)}, u32[]{:S(2)}, u32[]{:S(2)}) collective-permute-start(bf16[2,64,768]{2,1,0:T(8,128)(2,1)S(1)} %add_convert_fusion), channel_id=1, source_target_pairs={{0,8},{4,12},{8,0},{12,4},{1,9},{5,13},{9,1},{13,5},{2,10},{6,14},... | collective-permute-start | bytes 589832 | tf_op jit(solution)/shard_map/ppermute | solution.py:107
  160.9 1.1 collective-permute-done.26.more_ref
  162.1 7.2 %collective-permute-done.27.far_ref = bf16[2,64,768]{2,1,0:T(8,128)(2,1)S(1)} collective-permute-done((bf16[2,64,768]{2,1,0:T(8,128)(2,1)S(1)}, bf16[2,64,768]{2,1,0:T(8,128)(2,1)S(1)}, u32[]{:S(2)}, u32[]{:S(2)}) %collective-permute-start.27) | collective-permute-done | bytes 196640 | tf_op jit(solution)/shard_map/ppermute | solution.py:107
  169.2 1.3 shard_map.69
  (70 shorter events, 8.0 us)
Async XLA Ops:
  0.0 2.3 %copy-start = (bf16[1,128,3072]{2,1,0:T(8,128)(2,1)S(1)}, bf16[1,128,3072]{2,1,0:T(8,128)(2,1)}, u32[]{:S(2)}) copy-start(bf16[1,128,3072]{2,1,0:T(8,128)(2,1)} %param.6) | copy-start | bytes 2359300
  2.3 7.2 %copy-start.13 = (bf16[2,4]{1,0:T(2,128)(2,1)}, bf16[2,4]{1,0:T(2,128)(2,1)S(1)}, u32[]{:S(2)}) copy-start(bf16[2,4]{1,0:T(2,128)(2,1)S(1)} %convert.13) | copy-start | bytes 52
  4.2 8.3 %copy-start.2 = (bf16[136,1536]{1,0:T(8,128)(2,1)}, bf16[136,1536]{1,0:T(8,128)(2,1)S(1)}, u32[]{:S(2)}) copy-start(bf16[136,1536]{1,0:T(8,128)(2,1)S(1)} %fusion.1.refs_0_) | copy-start | bytes 1253380
  4.2 16.6 %copy-start.1 = (bf16[768,768]{1,0:T(8,128)(2,1)S(1)}, bf16[768,768]{1,0:T(8,128)(2,1)}, u32[]{:S(2)}) copy-start(bf16[768,768]{1,0:T(8,128)(2,1)} %refs_4_.1) | copy-start | bytes 3538948
  4.2 16.5 %collective-permute-start = (bf16[136,1536]{1,0:T(8,128)(2,1)S(1)}, bf16[136,1536]{1,0:T(8,128)(2,1)}, u32[]{:S(2)}, u32[]{:S(2)}) collective-permute-start(bf16[136,1536]{1,0:T(8,128)(2,1)S(1)} %fusion.1.refs_0_), channel_id=1, source_target_pairs={{0,4},{4,0},{8,12},{12,8},{1,5},{5,1},{9,13},{13,9},{2,6},{6,2},{1... | collective-permute-start | bytes 1253384 | tf_op jit(solution)/shard_map/ppermute | solution.py:107
  9.4 11.4 %collective-permute-start.1 = (bf16[3,384,256]{2,1,0:T(8,128)(2,1)S(1)}, bf16[3,384,256]{2,1,0:T(8,128)(2,1)}, u32[]{:S(2)}, u32[]{:S(2)}) collective-permute-start(bf16[3,384,256]{2,1,0:T(8,128)(2,1)S(1)} %get-tuple-element.64), channel_id=1, source_target_pairs={{0,0},{1,8},{4,4},{5,12},{8,1},{9,9},{12,5},{13,13},{2,2},{3,10},{... | collective-permute-start | bytes 1769480 | tf_op jit(solution)/shard_map/ppermute | solution.py:339
  11.0 9.9 %collective-permute-start.4 = (bf16[128,1536]{1,0:T(8,128)(2,1)}, bf16[128,1536]{1,0:T(8,128)(2,1)S(1)}, u32[]{:S(2)}, u32[]{:S(2)}) collective-permute-start(bf16[128,1536]{1,0:T(8,128)(2,1)} %dynamic-slice_bitcast_fusion.2), channel_id=1, source_target_pairs={{0,2},{2,0},{1,3},{3,1},{4,6},{6,4},{5,7},{7,5},{8,10},{10,8},{9,1... | collective-permute-start | bytes 1179656 | tf_op jit(solution)/shard_map/ppermute | solution.py:107
  20.7 44.4 %collective-permute-start.8 = (bf16[768,768]{1,0:T(8,128)(2,1)S(1)}, bf16[768,768]{1,0:T(8,128)(2,1)S(1)}, u32[]{:S(2)}, u32[]{:S(2)}) collective-permute-start(bf16[768,768]{1,0:T(8,128)(2,1)S(1)} %copy-done.1), channel_id=1, source_target_pairs={{0,1},{1,0},{2,3},{3,2},{4,5},{5,4},{6,7},{7,6},{8,9},{9,8},{10,11... | collective-permute-start | bytes 3538952 | tf_op jit(solution)/shard_map/ppermute | solution.py:107
  20.9 40.3 %collective-permute-start.10 = (bf16[3,384,256]{2,1,0:T(8,128)(2,1)}, bf16[3,384,256]{2,1,0:T(8,128)(2,1)}, u32[]{:S(2)}, u32[]{:S(2)}) collective-permute-start(bf16[3,384,256]{2,1,0:T(8,128)(2,1)} %get-tuple-element.37), channel_id=1, source_target_pairs={{0,4},{1,12},{4,0},{5,8},{8,5},{9,13},{12,1},{13,9},{2,6},{3,14},{... | collective-permute-start | bytes 1769480 | tf_op jit(solution)/shard_map/ppermute | solution.py:339
  21.0 40.2 %collective-permute-start.2 = (bf16[136,1536]{1,0:T(8,128)(2,1)}, bf16[136,1536]{1,0:T(8,128)(2,1)}, u32[]{:S(2)}, u32[]{:S(2)}) collective-permute-start(bf16[136,1536]{1,0:T(8,128)(2,1)} %copy-done.2), channel_id=1, source_target_pairs={{0,8},{4,12},{8,0},{12,4},{1,9},{5,13},{9,1},{13,5},{2,10},{6,14},... | collective-permute-start | bytes 1253384 | tf_op jit(solution)/shard_map/ppermute | solution.py:107
  29.5 31.6 %copy-start.3 = (bf16[136,1536]{1,0:T(8,128)(2,1)S(1)}, bf16[136,1536]{1,0:T(8,128)(2,1)}, u32[]{:S(2)}) copy-start(bf16[136,1536]{1,0:T(8,128)(2,1)} %copy-done.2) | copy-start | bytes 1253380
  29.5 34.7 %collective-permute-start.7 = (bf16[3,384,256]{2,1,0:T(8,128)(2,1)}, bf16[3,384,256]{2,1,0:T(8,128)(2,1)S(1)}, u32[]{:S(2)}, u32[]{:S(2)}) collective-permute-start(bf16[3,384,256]{2,1,0:T(8,128)(2,1)} %collective-permute-done.1.refs_8_), channel_id=1, source_target_pairs={{0,16},{16,0},{1,17},{17,1},{2,18},{18,2},{3,19},{19,3},{4,20},{20... | collective-permute-start | bytes 1769480 | tf_op jit(solution)/shard_map/ppermute | solution.py:107
  32.0 31.5 %collective-permute-start.5 = (bf16[136,1536]{1,0:T(8,128)(2,1)}, bf16[136,1536]{1,0:T(8,128)(2,1)S(1)}, u32[]{:S(2)}, u32[]{:S(2)}) collective-permute-start(bf16[136,1536]{1,0:T(8,128)(2,1)} %collective-permute-done.refs_1_), channel_id=1, source_target_pairs={{0,2},{2,0},{1,3},{3,1},{4,6},{6,4},{5,7},{7,5},{8,10},{10,8},{9,1... | collective-permute-start | bytes 1253384 | tf_op jit(solution)/shard_map/ppermute | solution.py:107
  61.2 14.5 %collective-permute-start.3 = (bf16[136,1536]{1,0:T(8,128)(2,1)S(1)}, bf16[136,1536]{1,0:T(8,128)(2,1)}, u32[]{:S(2)}, u32[]{:S(2)}) collective-permute-start(bf16[136,1536]{1,0:T(8,128)(2,1)S(1)} %copy-done.3), channel_id=1, source_target_pairs={{0,12},{4,8},{8,4},{12,0},{1,13},{5,9},{9,5},{13,1},{2,14},{6,10},... | collective-permute-start | bytes 1253384 | tf_op jit(solution)/shard_map/ppermute | solution.py:107
  61.2 19.9 %collective-permute-start.11 = (bf16[3,384,256]{2,1,0:T(8,128)(2,1)}, bf16[3,384,256]{2,1,0:T(8,128)(2,1)S(1)}, u32[]{:S(2)}, u32[]{:S(2)}) collective-permute-start(bf16[3,384,256]{2,1,0:T(8,128)(2,1)} %collective-permute-done.10.refs_10_), channel_id=1, source_target_pairs={{0,16},{16,0},{1,17},{17,1},{2,18},{18,2},{3,19},{19,3},{4,20},{20... | collective-permute-start | bytes 1769480 | tf_op jit(solution)/shard_map/ppermute | solution.py:107
  63.5 0.8 copy-start.10
  64.2 27.1 %collective-permute-start.15 = (bf16[384,768]{1,0:T(8,128)(2,1)}, bf16[384,768]{1,0:T(8,128)(2,1)}, u32[]{:S(2)}, u32[]{:S(2)}) collective-permute-start(bf16[384,768]{1,0:T(8,128)(2,1)} %constant_dynamic-slice_fusion), channel_id=1, source_target_pairs={{0,4},{4,0},{8,12},{12,8},{1,5},{5,1},{9,13},{13,9},{2,6},{6,2},{1... | collective-permute-start | bytes 1769480 | tf_op jit(solution)/shard_map/ppermute | solution.py:107
  64.3 0.8 copy-start.6
  65.1 16.8 %collective-permute-start.9 = (bf16[3,384,128]{2,1,0:T(8,128)(2,1)S(1)}, bf16[3,384,128]{2,1,0:T(8,128)(2,1)}, u32[]{:S(2)}, u32[]{:S(2)}) collective-permute-start(bf16[3,384,128]{2,1,0:T(8,128)(2,1)S(1)} %get-tuple-element.36), channel_id=1, source_target_pairs={{0,0},{1,8},{4,4},{5,12},{8,1},{9,9},{12,5},{13,13},{2,2},{3,10},{... | collective-permute-start | bytes 884744 | tf_op jit(solution)/shard_map/ppermute | solution.py:339
  67.1 25.7 %collective-permute-start.6 = (bf16[136,1536]{1,0:T(8,128)(2,1)}, bf16[136,1536]{1,0:T(8,128)(2,1)}, u32[]{:S(2)}, u32[]{:S(2)}) collective-permute-start(bf16[136,1536]{1,0:T(8,128)(2,1)} %collective-permute-done.2.refs_2_), channel_id=1, source_target_pairs={{0,2},{2,0},{1,3},{3,1},{4,6},{6,4},{5,7},{7,5},{8,10},{10,8},{9,1... | collective-permute-start | bytes 1253384 | tf_op jit(solution)/shard_map/ppermute | solution.py:107
  75.7 15.6 %collective-permute-start.14 = (bf16[3,384,128]{2,1,0:T(8,128)(2,1)}, bf16[3,384,128]{2,1,0:T(8,128)(2,1)}, u32[]{:S(2)}, u32[]{:S(2)}) collective-permute-start(bf16[3,384,128]{2,1,0:T(8,128)(2,1)} %get-tuple-element.39), channel_id=1, source_target_pairs={{0,4},{1,12},{4,0},{5,8},{8,5},{9,13},{12,1},{13,9},{2,6},{3,14},{... | collective-permute-start | bytes 884744 | tf_op jit(solution)/shard_map/ppermute | solution.py:339
  81.1 0.8 copy-start.8
  81.9 10.9 %collective-permute-start.12 = (bf16[136,1536]{1,0:T(8,128)(2,1)}, bf16[136,1536]{1,0:T(8,128)(2,1)}, u32[]{:S(2)}, u32[]{:S(2)}) collective-permute-start(bf16[136,1536]{1,0:T(8,128)(2,1)} %collective-permute-done.3.refs_3_), channel_id=1, source_target_pairs={{0,2},{2,0},{1,3},{3,1},{4,6},{6,4},{5,7},{7,5},{8,10},{10,8},{9,1... | collective-permute-start | bytes 1253384 | tf_op jit(solution)/shard_map/ppermute | solution.py:107
  84.0 8.8 %collective-permute-start.13 = (bf16[3,384,128]{2,1,0:T(8,128)(2,1)}, bf16[3,384,128]{2,1,0:T(8,128)(2,1)}, u32[]{:S(2)}, u32[]{:S(2)}) collective-permute-start(bf16[3,384,128]{2,1,0:T(8,128)(2,1)} %collective-permute-done.9.refs_8_), channel_id=1, source_target_pairs={{0,16},{16,0},{1,17},{17,1},{2,18},{18,2},{3,19},{19,3},{4,20},{20... | collective-permute-start | bytes 884744 | tf_op jit(solution)/shard_map/ppermute | solution.py:107
  91.3 20.7 %collective-permute-start.16 = (bf16[3,384,128]{2,1,0:T(8,128)(2,1)}, bf16[3,384,128]{2,1,0:T(8,128)(2,1)S(1)}, u32[]{:S(2)}, u32[]{:S(2)}) collective-permute-start(bf16[3,384,128]{2,1,0:T(8,128)(2,1)} %collective-permute-done.14.refs_10_), channel_id=1, source_target_pairs={{0,16},{16,0},{1,17},{17,1},{2,18},{18,2},{3,19},{19,3},{4,20},{20... | collective-permute-start | bytes 884744 | tf_op jit(solution)/shard_map/ppermute | solution.py:107
  92.8 1.0 copy-start.4
  93.8 1.1 copy-start.7
  94.9 1.1 copy-start.9
  96.0 1.0 copy-start.11
  97.0 15.1 %copy-start.5 = (bf16[136,1536]{1,0:T(8,128)(2,1)S(1)}, bf16[136,1536]{1,0:T(8,128)(2,1)}, u32[]{:S(2)}) copy-start(bf16[136,1536]{1,0:T(8,128)(2,1)} %copy-done.2) | copy-start | bytes 1253380
  97.0 15.1 %copy-start.12 = (bf16[136,1536]{1,0:T(8,128)(2,1)S(1)}, bf16[136,1536]{1,0:T(8,128)(2,1)}, u32[]{:S(2)}) copy-start(bf16[136,1536]{1,0:T(8,128)(2,1)} %copy-done.10) | copy-start | bytes 1253380
  103.3 15.8 %collective-permute-start.18 = (bf16[4,320,512]{2,1,0:T(8,128)(2,1)S(1)}, bf16[4,320,512]{2,1,0:T(8,128)(2,1)S(1)}, u32[]{:S(2)}, u32[]{:S(2)}) collective-permute-start(bf16[4,320,512]{2,1,0:T(8,128)(2,1)S(1)} %get-tuple-element.43), channel_id=1, source_target_pairs={{0,1},{1,0},{2,3},{3,2},{4,5},{5,4},{6,7},{7,6},{8,9},{9,8},{10,11... | collective-permute-start | bytes 3932168 | tf_op jit(solution)/shard_map/ppermute | solution.py:107
  117.5 5.5 %collective-permute-start.17 = (bf16[4,320,256]{2,1,0:T(8,128)(2,1)S(1)}, bf16[4,320,256]{2,1,0:T(8,128)(2,1)S(1)}, u32[]{:S(2)}, u32[]{:S(2)}) collective-permute-start(bf16[4,320,256]{2,1,0:T(8,128)(2,1)S(1)} %get-tuple-element.47), channel_id=1, source_target_pairs={{0,1},{1,0},{2,3},{3,2},{4,5},{5,4},{6,7},{7,6},{8,9},{9,8},{10,11... | collective-permute-start | bytes 1966088 | tf_op jit(solution)/shard_map/ppermute | solution.py:107
  117.6 15.9 %collective-permute-start.22 = (bf16[384,768]{1,0:T(8,128)(2,1)}, bf16[384,768]{1,0:T(8,128)(2,1)S(1)}, u32[]{:S(2)}, u32[]{:S(2)}) collective-permute-start(bf16[384,768]{1,0:T(8,128)(2,1)} %collective-permute-done.15.refs_6_), channel_id=1, source_target_pairs={{0,16},{16,0},{1,17},{17,1},{2,18},{18,2},{3,19},{19,3},{4,20},{20... | collective-permute-start | bytes 1769480 | tf_op jit(solution)/shard_map/ppermute | solution.py:107
  125.2 10.4 %collective-permute-start.19 = (bf16[2,128,384]{2,1,0:T(8,128)(2,1)S(1)}, bf16[2,128,384]{2,1,0:T(8,128)(2,1)S(1)}, u32[]{:S(2)}, u32[]{:S(2)}) collective-permute-start(bf16[2,128,384]{2,1,0:T(8,128)(2,1)S(1)} %get-tuple-element.53), channel_id=1, source_target_pairs={{0,4},{4,0},{8,12},{12,8},{1,5},{5,1},{9,13},{13,9},{2,6},{6,2},{1... | collective-permute-start | bytes 589832 | tf_op jit(solution)/shard_map/ppermute | solution.py:107
  126.3 17.1 %collective-permute-start.20 = (bf16[2,128,384]{2,1,0:T(8,128)(2,1)S(1)}, bf16[2,128,384]{2,1,0:T(8,128)(2,1)S(1)}, u32[]{:S(2)}, u32[]{:S(2)}) collective-permute-start(bf16[2,128,384]{2,1,0:T(8,128)(2,1)S(1)} %get-tuple-element.52.refs_0_), channel_id=1, source_target_pairs={{0,8},{4,12},{8,0},{12,4},{1,9},{5,13},{9,1},{13,5},{2,10},{6,14},... | collective-permute-start | bytes 589832 | tf_op jit(solution)/shard_map/ppermute | solution.py:107
  127.2 16.2 %collective-permute-start.21 = (bf16[2,128,384]{2,1,0:T(8,128)(2,1)S(1)}, bf16[2,128,384]{2,1,0:T(8,128)(2,1)S(1)}, u32[]{:S(2)}, u32[]{:S(2)}) collective-permute-start(bf16[2,128,384]{2,1,0:T(8,128)(2,1)S(1)} %get-tuple-element.53), channel_id=1, source_target_pairs={{0,12},{4,8},{8,4},{12,0},{1,13},{5,9},{9,5},{13,1},{2,14},{6,10},... | collective-permute-start | bytes 589832 | tf_op jit(solution)/shard_map/ppermute | solution.py:107
  129.6 13.8 %collective-permute-start.23 = (bf16[384,768]{1,0:T(8,128)(2,1)}, bf16[384,768]{1,0:T(8,128)(2,1)S(1)}, u32[]{:S(2)}, u32[]{:S(2)}) collective-permute-start(bf16[384,768]{1,0:T(8,128)(2,1)} %collective-permute-done.15.refs_6_), channel_id=1, source_target_pairs={{0,1},{1,0},{2,3},{3,2},{4,5},{5,4},{6,7},{7,6},{8,9},{9,8},{10,11... | collective-permute-start | bytes 1769480 | tf_op jit(solution)/shard_map/ppermute | solution.py:107
  143.4 2.0 %collective-permute-start.24 = (bf16[384,768]{1,0:T(8,128)(2,1)S(1)}, bf16[384,768]{1,0:T(8,128)(2,1)S(1)}, u32[]{:S(2)}, u32[]{:S(2)}) collective-permute-start(bf16[384,768]{1,0:T(8,128)(2,1)S(1)} %collective-permute-done.22.refs_7_), channel_id=1, source_target_pairs={{0,1},{1,0},{2,3},{3,2},{4,5},{5,4},{6,7},{7,6},{8,9},{9,8},{10,11... | collective-permute-start | bytes 1769480 | tf_op jit(solution)/shard_map/ppermute | solution.py:107
  148.9 7.0 %collective-permute-start.25 = (bf16[2,64,768]{2,1,0:T(8,128)(2,1)S(1)}, bf16[2,64,768]{2,1,0:T(8,128)(2,1)S(1)}, u32[]{:S(2)}, u32[]{:S(2)}) collective-permute-start(bf16[2,64,768]{2,1,0:T(8,128)(2,1)S(1)} %get-tuple-element.58), channel_id=1, source_target_pairs={{0,2},{2,0},{1,3},{3,1},{4,6},{6,4},{5,7},{7,5},{8,10},{10,8},{9,1... | collective-permute-start | bytes 589832 | tf_op jit(solution)/shard_map/ppermute | solution.py:107
  155.9 6.1 %collective-permute-start.26 = (bf16[2,64,768]{2,1,0:T(8,128)(2,1)S(1)}, bf16[2,64,768]{2,1,0:T(8,128)(2,1)S(1)}, u32[]{:S(2)}, u32[]{:S(2)}) collective-permute-start(bf16[2,64,768]{2,1,0:T(8,128)(2,1)S(1)} %get-tuple-element.59), channel_id=1, source_target_pairs={{0,2},{2,0},{1,3},{3,1},{4,6},{6,4},{5,7},{7,5},{8,10},{10,8},{9,1... | collective-permute-start | bytes 589832 | tf_op jit(solution)/shard_map/ppermute | solution.py:107
  156.3 13.0 %collective-permute-start.27 = (bf16[2,64,768]{2,1,0:T(8,128)(2,1)S(1)}, bf16[2,64,768]{2,1,0:T(8,128)(2,1)S(1)}, u32[]{:S(2)}, u32[]{:S(2)}) collective-permute-start(bf16[2,64,768]{2,1,0:T(8,128)(2,1)S(1)} %add_convert_fusion), channel_id=1, source_target_pairs={{0,8},{4,12},{8,0},{12,4},{1,9},{5,13},{9,1},{13,5},{2,10},{6,14},... | collective-permute-start | bytes 589832 | tf_op jit(solution)/shard_map/ppermute | solution.py:107

commit v15 on v14

--- a/solution.py
+++ b/solution.py
@@ -128,26 +128,38 @@
 
 
 def project(place, mine, theirs, chunks):
-    rows, (count, width) = len(mine), theirs[0].shape
+    rows, (count, width) = len(mine) - 1, theirs[0].shape
     _, half, cols = chunks[0][0].shape
     slices = len(chunks)
     flat = [w for of_round in chunks for w in of_round]
+    fetched = 2 * len(mine) + len(flat)
 
     def kernel(place_ref, *refs):
         row, group, frame, core = (place_ref[i] for i in range(4))
-        x_refs, w_refs = refs[: 2 * rows], refs[2 * rows : 2 * rows + len(flat)]
-        q_keep, kv_keep, send, x_all, w_all, total, sems = refs[2 * rows + len(flat) :]
+        w_refs = refs[2 * len(mine) : fetched]
+        q_keep, kv_keep, send, x_all, w_all, total, sems = refs[fetched:]
+        middle = (row == 1) | (row == 2)
         copies = []
-        for i, x_ref in enumerate(x_refs):
-            to = x_all.at[row ^ (i % rows), (frame + i // rows) % 2]
-            copies.append(pltpu.make_async_copy(x_ref.at[pl.ds(0, count)], to, sems.at[i]))
-            copies[-1].start()
         for k in range(slices):
             for g in range(2):
-                at = (row + slices - k) % slices * (2 * half) + (group + g) % 2 * half
+                at = pl.multiple_of((row + slices - k) % slices * (2 * half) + (group + g) % 2 * half, half)
                 for part in range(3):
-                    into = w_all.at[pl.ds(pl.multiple_of(at, half), half), part * cols : (part + 1) * cols]
-                    into[...] = w_refs[2 * k + g][part]
+                    into = w_all.at[pl.ds(at, half), part * cols : (part + 1) * cols]
+                    copy = pltpu.make_async_copy(w_refs[2 * k + g].at[part], into, sems.at[len(copies)])
+                    copy.start()
+                    copies.append(copy)
+        for f in range(2):
+            x_refs = refs[f * len(mine) : (f + 1) * len(mine)]
+            for s in range(rows):
+                to, sem = x_all.at[row ^ s, (frame + f) % 2], sems.at[len(copies)]
+                copy = pltpu.make_async_copy(x_refs[s].at[pl.ds(0, count)], to, sem)
+                copies.append(copy)
+                if s < rows - 1:
+                    copy.start()
+                else:
+                    other = pltpu.make_async_copy(x_refs[rows].at[pl.ds(0, count)], to, sem)
+                    pl.when(middle)(copy.start)
+                    pl.when(jnp.logical_not(middle))(other.start)
         for copy in copies:
             copy.wait()
         acc = jnp.dot(x_all[...].reshape(-1, width), w_all[...], preferred_element_type=jnp.float32)
@@ -174,13 +186,13 @@
         grid_spec=pltpu.PrefetchScalarGridSpec(
             num_scalar_prefetch=1,
             grid=(),
-            in_specs=[hbm] * (2 * rows) + [vmem] * len(flat),
+            in_specs=[hbm] * fetched,
             out_specs=(vmem, vmem, vmem),
             scratch_shapes=[
                 pltpu.VMEM((rows, 2, count, width), jnp.bfloat16),
                 pltpu.VMEM((width, 3 * cols), jnp.bfloat16),
                 pltpu.VMEM((rows, 2, count, cols), jnp.float32),
-                pltpu.SemaphoreType.DMA((2 * rows,)),
+                pltpu.SemaphoreType.DMA((2 * rows + 3 * len(flat),)),
             ],
         ),
         compiler_params=pltpu.CompilerParams(vmem_limit_bytes=VMEM_BYTES),
@@ -323,6 +335,10 @@
     half = depth // 2
     place = jnp.stack([row, group, frame, core]).astype(jnp.int32)
 
+    def over_frames(value, rows):
+        pairs = [(2 * r + f, 2 * r + 1 - f) for r in rows for f in range(2)]
+        return lax.ppermute(value, ("rows", "frames"), pairs)
+
     last = cols // (3 * HD) * HD
 
     def reshard(i, *others):
@@ -344,23 +360,27 @@
     tables = jnp.concatenate([win_blocks, win_counts[:, None], block_window[:, None]], axis=1)
     tables = jnp.pad(tables, ((0, 8 - heads_n), (0, span * depth - MAXB - 2))).astype(mine.dtype)
     joined = jnp.concatenate([mine, tables], axis=0)
+    in_3 = lax.ppermute(joined, "rows", [(1, 2), (2, 1)])
     near = swap(joined, "rows")
     near_x = swap(near, "frames")
     across = swap(after(w_out, near), "heads")
     there.append(swap(here[0], "groups"))
-    here.append(reshard(1, near, mine_x, here[0]))
-    far_2 = swap(after(joined, here[0]), "rows", 2)
+    in_3x = over_frames(after(in_3, there[0]), (1, 2))
+    here.append(reshard(1, near, mine_x, in_3, here[0]))
+    far_2 = swap(after(joined, near), "rows", 2)
     there.append(swap(here[1], "groups"))
     far_2x = swap(far_2, "frames")
-    far_3 = swap(after(joined, far_2), "rows", 3)
-    here.append(reshard(2, far_2, near_x, there[0], across))
+    out_3 = lax.ppermute(far_2, "rows", [(1, 0), (2, 3)])
+    here.append(reshard(2, far_2, near_x, in_3x, there[0], across))
     out_half = lax.dynamic_slice_in_dim(w_out, group * cols, cols, axis=0)
     beside = [swap(after(out_half, far_2), "rows")]
     here.append(reshard(3, here[1]))
-    far_3x = swap(after(far_3, here[2], there[1]), "frames")
+    out_3x = over_frames(after(out_3, there[1]), (0, 3))
     there += [swap(here[2], "groups"), swap(after(here[3], beside[0]), "groups")]
 
-    found = jnp.stack([x[count : count + heads_n, : MAXB + 2] for x in (joined, near, far_2, far_3)])
+    extra = jnp.where((row == 1) | (row == 2), in_3[count:], out_3[count:])
+    found = [joined[count:], near[count:], far_2[count:], extra]
+    found = jnp.stack([x[:heads_n, : MAXB + 2] for x in found])
     tables = found.astype(jnp.int32)[row ^ jnp.arange(rows_n)].reshape(rows_n * heads_n, MAXB + 2)
     windows = lax.dynamic_index_in_dim(
         tables[:, MAXB + 1].reshape(rows_n, heads_n), core, axis=1, keepdims=False
@@ -368,7 +388,7 @@
     picked = tables[windows]
     members, counts = picked[:, :MAXB].reshape(-1), picked[:, MAXB]
 
-    pieces = [joined, near, far_2, far_3], [mine_x, near_x, far_2x, far_3x]
+    pieces = [joined, near, far_2, in_3, out_3], [mine_x, near_x, far_2x, in_3x, out_3x]
     first = project(place, *pieces, [(here[0], there[0]), (here[1], after(there[1], there[2], members, counts))])
     beside.append(swap(after(beside[0], first[2]), "groups"))
     first_more = swap(first[2], "heads")

time: 171 us -> 173 us (1.012)
  starting transfers between devices: 50.7 us -> 54.4 us
  other arithmetic: 4.36 us -> 2.39 us
    ppermute x24 -> x22, starting transfers between devices: 42.9 us -> 30.8 us  [swap(): return lax.ppermute(value, axis, [(i, i ^ step) for i in range(peers)])]
    ppermute x4, starting transfers between devices: 7.74 us -> 16.8 us  [reshard(): lax.ppermute(after(value, *others) if others else value, ('rows', 'heads'...]
    ppermute x0 -> x4, waiting for transfers between devices: none -> 6.96 us  [the longest x1 6.95 us: by_heads(): out_3 = lax.ppermute(far_2, 'rows', [(1, 0), (2, 3)])]
    ppermute x0 -> x4, starting transfers between devices: none -> 6.77 us  [the longest x2 4.08 us: over_frames(): return lax.ppermute(value, ('rows', 'frames'), pairs)]
    ppermute x24 -> x22, waiting for transfers between devices: 72.2 us -> 68.5 us  [swap(): return lax.ppermute(value, axis, [(i, i ^ step) for i in range(peers)])]
    ppermute x4, waiting for transfers between devices: 4.44 us -> 2.17 us  [reshard(): lax.ppermute(after(value, *others) if others else value, ('rows', 'heads'...]
    unnamed x28 -> x22, local copies, waits for them, and re-layouts: 6.57 us -> 5.4 us
  transfers between devices with their start and end apart: 28 -> 30, of which waited for: 11 -> 11; matrix products, arithmetic and copies ran while one was open for 6% -> 6% of each run, Pallas kernels for 10% -> 10%
where the time goes in v15:
time: 173 us; the launch traced here: 172 us
  waiting for transfers between devices  77.6 us (45%)
  starting transfers between devices  54.4 us (31%)
  Pallas kernels  21.2 us (12%)
  local copies, waits for them, and re-layouts  16.2 us (9%)
  other arithmetic  2.39 us (1%)
    ppermute x22, waiting for transfers between devices, swap(): return lax.ppermute(value, axis, [(i, i ^ step) for i in range(peers)])  68.5 us
    ppermute x22, starting transfers between devices, swap(): return lax.ppermute(value, axis, [(i, i ^ step) for i in range(peers)])  30.8 us
    ppermute x4, starting transfers between devices, reshard(): lax.ppermute(after(value, *others) if others else value, ('rows', 'heads'...  16.8 us
    pallas_call x4, Pallas kernels, call(): pl.pallas_call(kernel, out_shape=out_shape, grid_spec=pltpu.PrefetchScala...  10.9 us
    pallas_call x2, Pallas kernels, project(): pl.pallas_call(kernel, out_shape=(jax.ShapeDtypeStruct((rows, 2 * BS, col...  10.3 us
    ppermute x1, waiting for transfers between devices, by_heads(): out_3 = lax.ppermute(far_2, 'rows', [(1, 0), (2, 3)])  6.95 us
    unnamed x22, local copies, waits for them, and re-layouts  5.4 us
    dynamic_slice x2, local copies, waits for them, and re-layouts, reshard(): lax.dynamic_slice(w_qkv.transpose(1, 0, 2), (0, group * half, (k + row) %...  4.45 us
  transfers between devices with their start and end apart: 30, of which 11 were waited for; matrix products, arithmetic and copies ran while one was open for 6% of the time, Pallas kernels for 10%

profile of v15, /device:TPU:0, one launch (start us, length us, event | category | flops | bytes accessed | tf_op | source)
XLA Modules:
  0.0 172.1 jit_solution(3940947450952751575)
XLA Ops:
  0.0 2.5 %dynamic-slice_bitcast_fusion = (bf16[3,384,256]{2,1,0:T(8,128)(2,1)}, bf16[3,384,256]{2,1,0:T(8,128)(2,1)}) fusion(bf16[768,3,768]{2,0,1:T(8,128)(2,1)} %param.7, s32[]{:T(128)S(6)} %select_n.69, s32[]{:T(128)S(6)} %select_n.73, s32[]{:T(128)S(6)} %select_n.71), kind=kLoop, calls=%fused_computation.4 | loop fusion | bytes 2359308 | tf_op jit(solution)/shard_map/dynamic_slice | solution.py:347
  2.5 6.1 %collective-permute-start.7 = (bf16[3,384,256]{2,1,0:T(8,128)(2,1)}, bf16[3,384,256]{2,1,0:T(8,128)(2,1)}, u32[]{:S(2)}, u32[]{:S(2)}) collective-permute-start(bf16[3,384,256]{2,1,0:T(8,128)(2,1)} %get-tuple-element.64), channel_id=1, source_target_pairs={{0,0},{1,8},{4,4},{5,12},{8,1},{9,9},{12,5},{13,13},{2,2},{3,10},{... | collective-permute-start | bytes 1769480 | tf_op jit(solution)/shard_map/ppermute | solution.py:355
  8.9 0.8 dynamic-slice_bitcast_fusion.2
  9.7 1.8 %fusion.1.refs_0_ = bf16[136,1536]{1,0:T(8,128)(2,1)} fusion(bf16[2,6]{1,0:T(2,128)(2,1)S(1)} %pad_maximum_fusion, bf16[128,1536]{1,0:T(8,128)(2,1)} %dynamic-slice_bitcast_fusion.2), kind=kLoop, calls=%fused_computation.6 | loop fusion | flops 1253376 | bytes 811032 | tf_op jit(solution)/shard_map/concatenate | solution.py:362
  11.5 3.0 %collective-permute-start = (bf16[136,1536]{1,0:T(8,128)(2,1)}, bf16[136,1536]{1,0:T(8,128)(2,1)}, u32[]{:S(2)}, u32[]{:S(2)}) collective-permute-start(bf16[136,1536]{1,0:T(8,128)(2,1)} %fusion.1.refs_0_), channel_id=1, source_target_pairs={{0,4},{4,0},{8,12},{12,8},{1,5},{5,1},{9,13},{13,9},{2,6},{6,2},{1... | collective-permute-start | bytes 1253384 | tf_op jit(solution)/shard_map/ppermute | solution.py:107
  14.5 1.4 collective-permute-start.2
  15.9 1.5 collective-permute-start.4
  17.4 11.2 %collective-permute-done.refs_1_ = bf16[136,1536]{1,0:T(8,128)(2,1)} collective-permute-done((bf16[136,1536]{1,0:T(8,128)(2,1)}, bf16[136,1536]{1,0:T(8,128)(2,1)}, u32[]{:S(2)}, u32[]{:S(2)}) %collective-permute-start) | collective-permute-done | bytes 417824 | tf_op jit(solution)/shard_map/ppermute | solution.py:107
  28.7 3.9 %collective-permute-start.10 = (bf16[3,384,256]{2,1,0:T(8,128)(2,1)}, bf16[3,384,256]{2,1,0:T(8,128)(2,1)}, u32[]{:S(2)}, u32[]{:S(2)}) collective-permute-start(bf16[3,384,256]{2,1,0:T(8,128)(2,1)} %get-tuple-element.35), channel_id=1, source_target_pairs={{0,4},{1,12},{4,0},{5,8},{8,5},{9,13},{12,1},{13,9},{2,6},{3,14},{... | collective-permute-start | bytes 1769480 | tf_op jit(solution)/shard_map/ppermute | solution.py:355
  32.6 1.5 collective-permute-start.8
  34.2 1.0 collective-permute-start.1
  35.5 0.9 constant_dynamic-slice_fusion
  36.4 2.0 %dynamic-slice_bitcast_fusion.3 = (bf16[3,384,128]{2,1,0:T(8,128)(2,1)}, bf16[3,384,128]{2,1,0:T(8,128)(2,1)}) fusion(bf16[768,3,768]{2,0,1:T(8,128)(2,1)} %param.7, s32[]{:T(128)S(6)} %select_n.69, s32[]{:T(128)S(6)} %select_n.75, s32[]{:T(128)S(6)} %select_n.74), kind=kLoop, calls=%fused_computation.9 | loop fusion | bytes 1179660 | tf_op jit(solution)/shard_map/dynamic_slice | solution.py:347
  38.3 1.5 collective-permute-start.5
  40.6 24.5 %collective-permute-done.1.refs_2_ = bf16[136,1536]{1,0:T(8,128)(2,1)} collective-permute-done((bf16[136,1536]{1,0:T(8,128)(2,1)}, bf16[136,1536]{1,0:T(8,128)(2,1)}, u32[]{:S(2)}, u32[]{:S(2)}) %collective-permute-start.1) | collective-permute-done | bytes 417824 | tf_op jit(solution)/shard_map/ppermute | solution.py:107
  65.1 1.3 collective-permute-start.3
  67.1 1.6 collective-permute-start.11
  70.1 6.9 %collective-permute-done.3.refs_4_ = bf16[136,1536]{1,0:T(8,128)(2,1)} collective-permute-done((bf16[136,1536]{1,0:T(8,128)(2,1)}, bf16[136,1536]{1,0:T(8,128)(2,1)}, u32[]{:S(2)}, u32[]{:S(2)}) %collective-permute-start.3) | collective-permute-done | bytes 417824 | tf_op jit(solution)/shard_map/ppermute | solution.py:373
  78.5 1.5 collective-permute-start.6
  80.8 3.0 %collective-permute-start.16 = (bf16[3,384,128]{2,1,0:T(8,128)(2,1)}, bf16[3,384,128]{2,1,0:T(8,128)(2,1)}, u32[]{:S(2)}, u32[]{:S(2)}) collective-permute-start(bf16[3,384,128]{2,1,0:T(8,128)(2,1)} %get-tuple-element.39), channel_id=1, source_target_pairs={{0,4},{1,12},{4,0},{5,8},{8,5},{9,13},{12,1},{13,9},{2,6},{3,14},{... | collective-permute-start | bytes 884744 | tf_op jit(solution)/shard_map/ppermute | solution.py:355
  83.8 3.8 %collective-permute-start.14 = (bf16[3,384,128]{2,1,0:T(8,128)(2,1)}, bf16[3,384,128]{2,1,0:T(8,128)(2,1)}, u32[]{:S(2)}, u32[]{:S(2)}) collective-permute-start(bf16[3,384,128]{2,1,0:T(8,128)(2,1)} %get-tuple-element.38), channel_id=1, source_target_pairs={{0,0},{1,8},{4,4},{5,12},{8,1},{9,9},{12,5},{13,13},{2,2},{3,10},{... | collective-permute-start | bytes 884744 | tf_op jit(solution)/shard_map/ppermute | solution.py:355
  87.6 0.8 copy-done.2
  88.4 3.4 %collective-permute-start.12 = (bf16[136,1536]{1,0:T(8,128)(2,1)}, bf16[136,1536]{1,0:T(8,128)(2,1)}, u32[]{:S(2)}, u32[]{:S(2)}) collective-permute-start(bf16[136,1536]{1,0:T(8,128)(2,1)} %collective-permute-done.3.refs_4_), channel_id=1, source_target_pairs={{0,2},{2,0},{12,14},{14,12},{1,3},{3,1},{13,15},{15,13},{16,18},{1... | collective-permute-start | bytes 1253384 | tf_op jit(solution)/shard_map/ppermute | solution.py:340
  92.4 1.6 collective-permute-start.15
  95.3 2.2 %collective-permute-done.16.refs_12_ = bf16[3,384,128]{2,1,0:T(8,128)(2,1)} collective-permute-done((bf16[3,384,128]{2,1,0:T(8,128)(2,1)}, bf16[3,384,128]{2,1,0:T(8,128)(2,1)}, u32[]{:S(2)}, u32[]{:S(2)}) %collective-permute-start.16) | collective-permute-done | bytes 294944 | tf_op jit(solution)/shard_map/ppermute | solution.py:355
  97.5 1.6 collective-permute-start.18
  99.0 3.6 %collective-permute-done.15.refs_11_ = bf16[3,384,128]{2,1,0:T(8,128)(2,1)} collective-permute-done((bf16[3,384,128]{2,1,0:T(8,128)(2,1)}, bf16[3,384,128]{2,1,0:T(8,128)(2,1)}, u32[]{:S(2)}, u32[]{:S(2)}) %collective-permute-start.15) | collective-permute-done | bytes 294944 | tf_op jit(solution)/shard_map/ppermute | solution.py:107
  102.7 1.1 copy-done.3
  103.7 1.0 copy-done.5
  104.7 1.0 copy-done.7
  105.7 5.7 %shard_map.64 = (f32[4,128,256]{2,1,0:T(8,128)S(1)}, f32[4,256,512]{2,1,0:T(8,128)S(1)}, bf16[4,320,512]{2,1,0:T(8,128)(2,1)S(1)}) custom-call(s32[4]{0:T(128)S(1)} %pad_add_fusion.place_ref, bf16[136,1536]{1,0:T(8,128)(2,1)} %fusion.1.refs_0_, bf16[136,1536]{1,0:T(8,128)(2,1)} %collective-permute-done.refs_1_, ...), custom_call_target="tpu_custom_call" | custom-call | flops 19327352832 | bytes 8053063 | tf_op jit(solution)/shard_map/pallas_call | solution.py:179
  111.6 4.6 %shard_map.65 = (f32[4,128,128]{2,1,0:T(8,128)S(1)}, f32[4,256,256]{2,1,0:T(8,128)S(1)}, bf16[4,320,256]{2,1,0:T(8,128)(2,1)S(1)}) custom-call(s32[4]{0:T(128)S(1)} %pad_add_fusion.place_ref, bf16[136,1536]{1,0:T(8,128)(2,1)} %fusion.1.refs_0_, bf16[136,1536]{1,0:T(8,128)(2,1)} %collective-permute-done.refs_1_, ...), custom_call_target="tpu_custom_call" | custom-call | flops 9663676416 | bytes 4026531 | tf_op jit(solution)/shard_map/pallas_call | solution.py:179
  116.7 1.5 collective-permute-start.24
  118.3 3.8 %shard_map.66 = (bf16[2,128,256]{2,1,0:T(8,128)(2,1)S(1)}, bf16[2,128,256]{2,1,0:T(8,128)(2,1)S(1)}) custom-call(s32[4]{0:T(128)S(1)} %pad_add_fusion.place_ref, s32[16]{0:T(128)S(1)} %reshape.24.members_ref, s32[4]{0:T(128)S(1)} %slice_reduce_fusion.1.counts_ref, f32[4,128,256]{2,1,0:T(8,128)S(1)} %get-tuple-element.48.q_ref, ...), custom_call_target="tpu_custom_call" | custom-call | flops 268435456 | bytes 2097152 | tf_op jit(solution)/shard_map/pallas_call | solution.py:115
  122.1 2.2 %shard_map.67 = (bf16[2,128,384]{2,1,0:T(8,128)(2,1)S(1)}, bf16[2,128,384]{2,1,0:T(8,128)(2,1)S(1)}) custom-call(s32[4]{0:T(128)S(1)} %pad_add_fusion.place_ref, s32[16]{0:T(128)S(1)} %reshape.24.members_ref, s32[4]{0:T(128)S(1)} %slice_reduce_fusion.1.counts_ref, f32[4,128,128]{2,1,0:T(8,128)S(1)} %get-tuple-element.45.q_ref, ...), custom_call_target="tpu_custom_call" | custom-call | flops 134217728 | bytes 1048576 | tf_op jit(solution)/shard_map/pallas_call | solution.py:115
  124.3 3.8 %collective-permute-start.21 = (bf16[2,128,384]{2,1,0:T(8,128)(2,1)S(1)}, bf16[2,128,384]{2,1,0:T(8,128)(2,1)S(1)}, u32[]{:S(2)}, u32[]{:S(2)}) collective-permute-start(bf16[2,128,384]{2,1,0:T(8,128)(2,1)S(1)} %get-tuple-element.53), channel_id=1, source_target_pairs={{0,4},{4,0},{8,12},{12,8},{1,5},{5,1},{9,13},{13,9},{2,6},{6,2},{1... | collective-permute-start | bytes 589832 | tf_op jit(solution)/shard_map/ppermute | solution.py:107
  128.1 2.6 %collective-permute-start.22 = (bf16[2,128,384]{2,1,0:T(8,128)(2,1)S(1)}, bf16[2,128,384]{2,1,0:T(8,128)(2,1)S(1)}, u32[]{:S(2)}, u32[]{:S(2)}) collective-permute-start(bf16[2,128,384]{2,1,0:T(8,128)(2,1)S(1)} %get-tuple-element.52.refs_0_), channel_id=1, source_target_pairs={{0,8},{4,12},{8,0},{12,4},{1,9},{5,13},{9,1},{13,5},{2,10},{6,14},... | collective-permute-start | bytes 589832 | tf_op jit(solution)/shard_map/ppermute | solution.py:107
  130.7 1.6 collective-permute-done.24.refs_7_
  132.3 4.4 %collective-permute-done.21.refs_1_ = bf16[2,128,384]{2,1,0:T(8,128)(2,1)S(1)} collective-permute-done((bf16[2,128,384]{2,1,0:T(8,128)(2,1)S(1)}, bf16[2,128,384]{2,1,0:T(8,128)(2,1)S(1)}, u32[]{:S(2)}, u32[]{:S(2)}) %collective-permute-start.21) | collective-permute-done | bytes 196640 | tf_op jit(solution)/shard_map/ppermute | solution.py:107
  136.7 8.5 %collective-permute-done.22.refs_2_ = bf16[2,128,384]{2,1,0:T(8,128)(2,1)S(1)} collective-permute-done((bf16[2,128,384]{2,1,0:T(8,128)(2,1)S(1)}, bf16[2,128,384]{2,1,0:T(8,128)(2,1)S(1)}, u32[]{:S(2)}, u32[]{:S(2)}) %collective-permute-start.22) | collective-permute-done | bytes 196640 | tf_op jit(solution)/shard_map/ppermute | solution.py:107
  145.2 2.0 %collective-permute-done.26.refs_9_ = bf16[384,768]{1,0:T(8,128)(2,1)S(1)} collective-permute-done((bf16[384,768]{1,0:T(8,128)(2,1)S(1)}, bf16[384,768]{1,0:T(8,128)(2,1)S(1)}, u32[]{:S(2)}, u32[]{:S(2)}) %collective-permute-start.26) | collective-permute-done | bytes 589856 | tf_op jit(solution)/shard_map/ppermute | solution.py:107
  147.2 3.5 %shard_map.68 = (f32[2,64,768]{2,1,0:T(8,128)S(1)}, bf16[2,64,768]{2,1,0:T(8,128)(2,1)S(1)}, f32[2,64,768]{2,1,0:T(8,128)S(1)}, bf16[2,64,768]{2,1,0:T(8,128)(2,1)S(1)}) custom-call(s32[4]{0:T(128)S(1)} %pad_add_fusion.place_ref, bf16[2,128,384]{2,1,0:T(8,128)(2,1)S(1)} %get-tuple-element.52.refs_0_, ...), custom_call_target="tpu_custom_call" | custom-call | flops 1207959552 | bytes 4718592 | tf_op jit(solution)/shard_map/pallas_call | solution.py:115
  150.8 1.6 collective-permute-start.27
  152.3 5.4 %collective-permute-done.27 = bf16[2,64,768]{2,1,0:T(8,128)(2,1)S(1)} collective-permute-done((bf16[2,64,768]{2,1,0:T(8,128)(2,1)S(1)}, bf16[2,64,768]{2,1,0:T(8,128)(2,1)S(1)}, u32[]{:S(2)}, u32[]{:S(2)}) %collective-permute-start.27) | collective-permute-done | bytes 196640 | tf_op jit(solution)/shard_map/ppermute | solution.py:107
  157.8 4.3 %collective-permute-start.29 = (bf16[2,64,768]{2,1,0:T(8,128)(2,1)S(1)}, bf16[2,64,768]{2,1,0:T(8,128)(2,1)S(1)}, u32[]{:S(2)}, u32[]{:S(2)}) collective-permute-start(bf16[2,64,768]{2,1,0:T(8,128)(2,1)S(1)} %add_convert_fusion), channel_id=1, source_target_pairs={{0,8},{4,12},{8,0},{12,4},{1,9},{5,13},{9,1},{13,5},{2,10},{6,14},... | collective-permute-start | bytes 589832 | tf_op jit(solution)/shard_map/ppermute | solution.py:107
  162.2 1.5 collective-permute-start.28
  163.6 7.1 %collective-permute-done.29.far_ref = bf16[2,64,768]{2,1,0:T(8,128)(2,1)S(1)} collective-permute-done((bf16[2,64,768]{2,1,0:T(8,128)(2,1)S(1)}, bf16[2,64,768]{2,1,0:T(8,128)(2,1)S(1)}, u32[]{:S(2)}, u32[]{:S(2)}) %collective-permute-start.29) | collective-permute-done | bytes 196640 | tf_op jit(solution)/shard_map/ppermute | solution.py:107
  170.7 1.3 shard_map.69
  (70 shorter events, 8.3 us)
Async XLA Ops:
  0.0 8.9 %copy-start = (bf16[1,128,3072]{2,1,0:T(8,128)(2,1)S(1)}, bf16[1,128,3072]{2,1,0:T(8,128)(2,1)}, u32[]{:S(2)}) copy-start(bf16[1,128,3072]{2,1,0:T(8,128)(2,1)} %param.6) | copy-start | bytes 2359300
  0.0 8.6 %copy-start.9 = (s32[2]{0:T(128)S(1)}, s32[2]{0:T(128)}, u32[]{:S(2)}) copy-start(s32[2]{0:T(128)} %param.11) | copy-start | bytes 28
  0.0 8.7 %copy-start.10 = (s32[2]{0:T(128)S(1)}, s32[2]{0:T(128)}, u32[]{:S(2)}) copy-start(s32[2]{0:T(128)} %param.10) | copy-start | bytes 28
  0.0 8.8 %copy-start.8 = (s32[2,4]{1,0:T(2,128)S(1)}, s32[2,4]{1,0:T(2,128)}, u32[]{:S(2)}) copy-start(s32[2,4]{1,0:T(2,128)} %param.9) | copy-start | bytes 100
  2.5 26.2 %copy-start.1 = (bf16[768,768]{1,0:T(8,128)(2,1)S(1)}, bf16[768,768]{1,0:T(8,128)(2,1)}, u32[]{:S(2)}) copy-start(bf16[768,768]{1,0:T(8,128)(2,1)} %refs_4_.1) | copy-start | bytes 3538948
  2.5 26.2 %collective-permute-start.7 = (bf16[3,384,256]{2,1,0:T(8,128)(2,1)}, bf16[3,384,256]{2,1,0:T(8,128)(2,1)}, u32[]{:S(2)}, u32[]{:S(2)}) collective-permute-start(bf16[3,384,256]{2,1,0:T(8,128)(2,1)} %get-tuple-element.64), channel_id=1, source_target_pairs={{0,0},{1,8},{4,4},{5,12},{8,1},{9,9},{12,5},{13,13},{2,2},{3,10},{... | collective-permute-start | bytes 1769480 | tf_op jit(solution)/shard_map/ppermute | solution.py:355
  11.5 17.2 %collective-permute-start = (bf16[136,1536]{1,0:T(8,128)(2,1)}, bf16[136,1536]{1,0:T(8,128)(2,1)}, u32[]{:S(2)}, u32[]{:S(2)}) collective-permute-start(bf16[136,1536]{1,0:T(8,128)(2,1)} %fusion.1.refs_0_), channel_id=1, source_target_pairs={{0,4},{4,0},{8,12},{12,8},{1,5},{5,1},{9,13},{13,9},{2,6},{6,2},{1... | collective-permute-start | bytes 1253384 | tf_op jit(solution)/shard_map/ppermute | solution.py:107
  14.5 14.2 %collective-permute-start.2 = (bf16[136,1536]{1,0:T(8,128)(2,1)}, bf16[136,1536]{1,0:T(8,128)(2,1)}, u32[]{:S(2)}, u32[]{:S(2)}) collective-permute-start(bf16[136,1536]{1,0:T(8,128)(2,1)} %fusion.1.refs_0_), channel_id=1, source_target_pairs={{4,8},{8,4},{5,9},{9,5},{6,10},{10,6},{7,11},{11,7},{20,24},{24,20... | collective-permute-start | bytes 1253384 | tf_op jit(solution)/shard_map/ppermute | solution.py:363
  15.9 12.7 %collective-permute-start.4 = (bf16[128,1536]{1,0:T(8,128)(2,1)}, bf16[128,1536]{1,0:T(8,128)(2,1)S(1)}, u32[]{:S(2)}, u32[]{:S(2)}) collective-permute-start(bf16[128,1536]{1,0:T(8,128)(2,1)} %dynamic-slice_bitcast_fusion.2), channel_id=1, source_target_pairs={{0,2},{2,0},{1,3},{3,1},{4,6},{6,4},{5,7},{7,5},{8,10},{10,8},{9,1... | collective-permute-start | bytes 1179656 | tf_op jit(solution)/shard_map/ppermute | solution.py:107
  28.7 55.1 %collective-permute-start.13 = (bf16[768,768]{1,0:T(8,128)(2,1)S(1)}, bf16[768,768]{1,0:T(8,128)(2,1)S(1)}, u32[]{:S(2)}, u32[]{:S(2)}) collective-permute-start(bf16[768,768]{1,0:T(8,128)(2,1)S(1)} %copy-done.1), channel_id=1, source_target_pairs={{0,1},{1,0},{2,3},{3,2},{4,5},{5,4},{6,7},{7,6},{8,9},{9,8},{10,11... | collective-permute-start | bytes 3538952 | tf_op jit(solution)/shard_map/ppermute | solution.py:107
  28.7 38.4 %collective-permute-start.10 = (bf16[3,384,256]{2,1,0:T(8,128)(2,1)}, bf16[3,384,256]{2,1,0:T(8,128)(2,1)}, u32[]{:S(2)}, u32[]{:S(2)}) collective-permute-start(bf16[3,384,256]{2,1,0:T(8,128)(2,1)} %get-tuple-element.35), channel_id=1, source_target_pairs={{0,4},{1,12},{4,0},{5,8},{8,5},{9,13},{12,1},{13,9},{2,6},{3,14},{... | collective-permute-start | bytes 1769480 | tf_op jit(solution)/shard_map/ppermute | solution.py:355
  32.6 33.7 %collective-permute-start.8 = (bf16[3,384,256]{2,1,0:T(8,128)(2,1)}, bf16[3,384,256]{2,1,0:T(8,128)(2,1)}, u32[]{:S(2)}, u32[]{:S(2)}) collective-permute-start(bf16[3,384,256]{2,1,0:T(8,128)(2,1)} %collective-permute-done.7.refs_10_), channel_id=1, source_target_pairs={{0,16},{16,0},{1,17},{17,1},{2,18},{18,2},{3,19},{19,3},{4,20},{20... | collective-permute-start | bytes 1769480 | tf_op jit(solution)/shard_map/ppermute | solution.py:107
  34.2 30.9 %collective-permute-start.1 = (bf16[136,1536]{1,0:T(8,128)(2,1)}, bf16[136,1536]{1,0:T(8,128)(2,1)}, u32[]{:S(2)}, u32[]{:S(2)}) collective-permute-start(bf16[136,1536]{1,0:T(8,128)(2,1)} %fusion.1.refs_0_), channel_id=1, source_target_pairs={{0,8},{4,12},{8,0},{12,4},{1,9},{5,13},{9,1},{13,5},{2,10},{6,14},... | collective-permute-start | bytes 1253384 | tf_op jit(solution)/shard_map/ppermute | solution.py:107
  38.3 39.4 %collective-permute-start.5 = (bf16[136,1536]{1,0:T(8,128)(2,1)}, bf16[136,1536]{1,0:T(8,128)(2,1)S(1)}, u32[]{:S(2)}, u32[]{:S(2)}) collective-permute-start(bf16[136,1536]{1,0:T(8,128)(2,1)} %collective-permute-done.refs_1_), channel_id=1, source_target_pairs={{0,2},{2,0},{1,3},{3,1},{4,6},{6,4},{5,7},{7,5},{8,10},{10,8},{9,1... | collective-permute-start | bytes 1253384 | tf_op jit(solution)/shard_map/ppermute | solution.py:107
  65.1 11.9 %collective-permute-start.3 = (bf16[136,1536]{1,0:T(8,128)(2,1)}, bf16[136,1536]{1,0:T(8,128)(2,1)}, u32[]{:S(2)}, u32[]{:S(2)}) collective-permute-start(bf16[136,1536]{1,0:T(8,128)(2,1)} %collective-permute-done.1.refs_2_), channel_id=1, source_target_pairs={{4,0},{8,12},{5,1},{9,13},{6,2},{10,14},{7,3},{11,15},{20,16},{24,... | collective-permute-start | bytes 1253384 | tf_op jit(solution)/shard_map/ppermute | solution.py:373
  66.4 13.7 %collective-permute-start.9 = (bf16[136,1536]{1,0:T(8,128)(2,1)}, bf16[136,1536]{1,0:T(8,128)(2,1)S(1)}, u32[]{:S(2)}, u32[]{:S(2)}) collective-permute-start(bf16[136,1536]{1,0:T(8,128)(2,1)} %collective-permute-done.2.refs_3_), channel_id=1, source_target_pairs={{4,6},{6,4},{8,10},{10,8},{5,7},{7,5},{9,11},{11,9},{20,22},{22,20... | collective-permute-start | bytes 1253384 | tf_op jit(solution)/shard_map/ppermute | solution.py:340
  67.1 20.5 %collective-permute-start.11 = (bf16[3,384,256]{2,1,0:T(8,128)(2,1)}, bf16[3,384,256]{2,1,0:T(8,128)(2,1)S(1)}, u32[]{:S(2)}, u32[]{:S(2)}) collective-permute-start(bf16[3,384,256]{2,1,0:T(8,128)(2,1)} %collective-permute-done.10.refs_12_), channel_id=1, source_target_pairs={{0,16},{16,0},{1,17},{17,1},{2,18},{18,2},{3,19},{19,3},{4,20},{20... | collective-permute-start | bytes 1769480 | tf_op jit(solution)/shard_map/ppermute | solution.py:107
  77.0 18.3 %collective-permute-start.17 = (bf16[384,768]{1,0:T(8,128)(2,1)}, bf16[384,768]{1,0:T(8,128)(2,1)}, u32[]{:S(2)}, u32[]{:S(2)}) collective-permute-start(bf16[384,768]{1,0:T(8,128)(2,1)} %constant_dynamic-slice_fusion), channel_id=1, source_target_pairs={{0,4},{4,0},{8,12},{12,8},{1,5},{5,1},{9,13},{13,9},{2,6},{6,2},{1... | collective-permute-start | bytes 1769480 | tf_op jit(solution)/shard_map/ppermute | solution.py:107
  77.8 0.8 copy-start.4
  78.5 24.1 %collective-permute-start.6 = (bf16[136,1536]{1,0:T(8,128)(2,1)}, bf16[136,1536]{1,0:T(8,128)(2,1)}, u32[]{:S(2)}, u32[]{:S(2)}) collective-permute-start(bf16[136,1536]{1,0:T(8,128)(2,1)} %collective-permute-done.1.refs_2_), channel_id=1, source_target_pairs={{0,2},{2,0},{1,3},{3,1},{4,6},{6,4},{5,7},{7,5},{8,10},{10,8},{9,1... | collective-permute-start | bytes 1253384 | tf_op jit(solution)/shard_map/ppermute | solution.py:107
  80.1 0.7 copy-start.6
  80.8 16.7 %collective-permute-start.16 = (bf16[3,384,128]{2,1,0:T(8,128)(2,1)}, bf16[3,384,128]{2,1,0:T(8,128)(2,1)}, u32[]{:S(2)}, u32[]{:S(2)}) collective-permute-start(bf16[3,384,128]{2,1,0:T(8,128)(2,1)} %get-tuple-element.39), channel_id=1, source_target_pairs={{0,4},{1,12},{4,0},{5,8},{8,5},{9,13},{12,1},{13,9},{2,6},{3,14},{... | collective-permute-start | bytes 884744 | tf_op jit(solution)/shard_map/ppermute | solution.py:355
  83.8 8.6 %collective-permute-start.14 = (bf16[3,384,128]{2,1,0:T(8,128)(2,1)}, bf16[3,384,128]{2,1,0:T(8,128)(2,1)}, u32[]{:S(2)}, u32[]{:S(2)}) collective-permute-start(bf16[3,384,128]{2,1,0:T(8,128)(2,1)} %get-tuple-element.38), channel_id=1, source_target_pairs={{0,0},{1,8},{4,4},{5,12},{8,1},{9,9},{12,5},{13,13},{2,2},{3,10},{... | collective-permute-start | bytes 884744 | tf_op jit(solution)/shard_map/ppermute | solution.py:355
  87.6 0.8 copy-start.2
  88.4 14.2 %collective-permute-start.12 = (bf16[136,1536]{1,0:T(8,128)(2,1)}, bf16[136,1536]{1,0:T(8,128)(2,1)}, u32[]{:S(2)}, u32[]{:S(2)}) collective-permute-start(bf16[136,1536]{1,0:T(8,128)(2,1)} %collective-permute-done.3.refs_4_), channel_id=1, source_target_pairs={{0,2},{2,0},{12,14},{14,12},{1,3},{3,1},{13,15},{15,13},{16,18},{1... | collective-permute-start | bytes 1253384 | tf_op jit(solution)/shard_map/ppermute | solution.py:340
  92.4 10.2 %collective-permute-start.15 = (bf16[3,384,128]{2,1,0:T(8,128)(2,1)}, bf16[3,384,128]{2,1,0:T(8,128)(2,1)}, u32[]{:S(2)}, u32[]{:S(2)}) collective-permute-start(bf16[3,384,128]{2,1,0:T(8,128)(2,1)} %collective-permute-done.14.refs_10_), channel_id=1, source_target_pairs={{0,16},{16,0},{1,17},{17,1},{2,18},{18,2},{3,19},{19,3},{4,20},{20... | collective-permute-start | bytes 884744 | tf_op jit(solution)/shard_map/ppermute | solution.py:107
  97.5 14.2 %collective-permute-start.18 = (bf16[3,384,128]{2,1,0:T(8,128)(2,1)}, bf16[3,384,128]{2,1,0:T(8,128)(2,1)S(1)}, u32[]{:S(2)}, u32[]{:S(2)}) collective-permute-start(bf16[3,384,128]{2,1,0:T(8,128)(2,1)} %collective-permute-done.16.refs_12_), channel_id=1, source_target_pairs={{0,16},{16,0},{1,17},{17,1},{2,18},{18,2},{3,19},{19,3},{4,20},{20... | collective-permute-start | bytes 884744 | tf_op jit(solution)/shard_map/ppermute | solution.py:107
  102.7 1.1 copy-start.3
  103.7 1.0 copy-start.5
  104.7 1.0 copy-start.7
  111.5 6.8 %collective-permute-start.20 = (bf16[4,320,512]{2,1,0:T(8,128)(2,1)S(1)}, bf16[4,320,512]{2,1,0:T(8,128)(2,1)S(1)}, u32[]{:S(2)}, u32[]{:S(2)}) collective-permute-start(bf16[4,320,512]{2,1,0:T(8,128)(2,1)S(1)} %get-tuple-element.43), channel_id=1, source_target_pairs={{0,1},{1,0},{2,3},{3,2},{4,5},{5,4},{6,7},{7,6},{8,9},{9,8},{10,11... | collective-permute-start | bytes 3932168 | tf_op jit(solution)/shard_map/ppermute | solution.py:107
  116.3 5.8 %collective-permute-start.19 = (bf16[4,320,256]{2,1,0:T(8,128)(2,1)S(1)}, bf16[4,320,256]{2,1,0:T(8,128)(2,1)S(1)}, u32[]{:S(2)}, u32[]{:S(2)}) collective-permute-start(bf16[4,320,256]{2,1,0:T(8,128)(2,1)S(1)} %get-tuple-element.47), channel_id=1, source_target_pairs={{0,1},{1,0},{2,3},{3,2},{4,5},{5,4},{6,7},{7,6},{8,9},{9,8},{10,11... | collective-permute-start | bytes 1966088 | tf_op jit(solution)/shard_map/ppermute | solution.py:107
  116.7 15.6 %collective-permute-start.24 = (bf16[384,768]{1,0:T(8,128)(2,1)}, bf16[384,768]{1,0:T(8,128)(2,1)S(1)}, u32[]{:S(2)}, u32[]{:S(2)}) collective-permute-start(bf16[384,768]{1,0:T(8,128)(2,1)} %collective-permute-done.17.refs_6_), channel_id=1, source_target_pairs={{0,16},{16,0},{1,17},{17,1},{2,18},{18,2},{3,19},{19,3},{4,20},{20... | collective-permute-start | bytes 1769480 | tf_op jit(solution)/shard_map/ppermute | solution.py:107
  124.3 12.4 %collective-permute-start.21 = (bf16[2,128,384]{2,1,0:T(8,128)(2,1)S(1)}, bf16[2,128,384]{2,1,0:T(8,128)(2,1)S(1)}, u32[]{:S(2)}, u32[]{:S(2)}) collective-permute-start(bf16[2,128,384]{2,1,0:T(8,128)(2,1)S(1)} %get-tuple-element.53), channel_id=1, source_target_pairs={{0,4},{4,0},{8,12},{12,8},{1,5},{5,1},{9,13},{13,9},{2,6},{6,2},{1... | collective-permute-start | bytes 589832 | tf_op jit(solution)/shard_map/ppermute | solution.py:107
  128.1 17.1 %collective-permute-start.22 = (bf16[2,128,384]{2,1,0:T(8,128)(2,1)S(1)}, bf16[2,128,384]{2,1,0:T(8,128)(2,1)S(1)}, u32[]{:S(2)}, u32[]{:S(2)}) collective-permute-start(bf16[2,128,384]{2,1,0:T(8,128)(2,1)S(1)} %get-tuple-element.52.refs_0_), channel_id=1, source_target_pairs={{0,8},{4,12},{8,0},{12,4},{1,9},{5,13},{9,1},{13,5},{2,10},{6,14},... | collective-permute-start | bytes 589832 | tf_op jit(solution)/shard_map/ppermute | solution.py:107
  130.7 14.5 %collective-permute-start.23 = (bf16[2,128,384]{2,1,0:T(8,128)(2,1)S(1)}, bf16[2,128,384]{2,1,0:T(8,128)(2,1)S(1)}, u32[]{:S(2)}, u32[]{:S(2)}) collective-permute-start(bf16[2,128,384]{2,1,0:T(8,128)(2,1)S(1)} %get-tuple-element.53), channel_id=1, source_target_pairs={{0,12},{4,8},{8,4},{12,0},{1,13},{5,9},{9,5},{13,1},{2,14},{6,10},... | collective-permute-start | bytes 589832 | tf_op jit(solution)/shard_map/ppermute | solution.py:107
  130.7 14.5 %collective-permute-start.25 = (bf16[384,768]{1,0:T(8,128)(2,1)}, bf16[384,768]{1,0:T(8,128)(2,1)S(1)}, u32[]{:S(2)}, u32[]{:S(2)}) collective-permute-start(bf16[384,768]{1,0:T(8,128)(2,1)} %collective-permute-done.17.refs_6_), channel_id=1, source_target_pairs={{0,1},{1,0},{2,3},{3,2},{4,5},{5,4},{6,7},{7,6},{8,9},{9,8},{10,11... | collective-permute-start | bytes 1769480 | tf_op jit(solution)/shard_map/ppermute | solution.py:107
  145.2 2.0 %collective-permute-start.26 = (bf16[384,768]{1,0:T(8,128)(2,1)S(1)}, bf16[384,768]{1,0:T(8,128)(2,1)S(1)}, u32[]{:S(2)}, u32[]{:S(2)}) collective-permute-start(bf16[384,768]{1,0:T(8,128)(2,1)S(1)} %collective-permute-done.24.refs_7_), channel_id=1, source_target_pairs={{0,1},{1,0},{2,3},{3,2},{4,5},{5,4},{6,7},{7,6},{8,9},{9,8},{10,11... | collective-permute-start | bytes 1769480 | tf_op jit(solution)/shard_map/ppermute | solution.py:107
  150.8 7.0 %collective-permute-start.27 = (bf16[2,64,768]{2,1,0:T(8,128)(2,1)S(1)}, bf16[2,64,768]{2,1,0:T(8,128)(2,1)S(1)}, u32[]{:S(2)}, u32[]{:S(2)}) collective-permute-start(bf16[2,64,768]{2,1,0:T(8,128)(2,1)S(1)} %get-tuple-element.58), channel_id=1, source_target_pairs={{0,2},{2,0},{1,3},{3,1},{4,6},{6,4},{5,7},{7,5},{8,10},{10,8},{9,1... | collective-permute-start | bytes 589832 | tf_op jit(solution)/shard_map/ppermute | solution.py:107
  157.8 12.9 %collective-permute-start.29 = (bf16[2,64,768]{2,1,0:T(8,128)(2,1)S(1)}, bf16[2,64,768]{2,1,0:T(8,128)(2,1)S(1)}, u32[]{:S(2)}, u32[]{:S(2)}) collective-permute-start(bf16[2,64,768]{2,1,0:T(8,128)(2,1)S(1)} %add_convert_fusion), channel_id=1, source_target_pairs={{0,8},{4,12},{8,0},{12,4},{1,9},{5,13},{9,1},{13,5},{2,10},{6,14},... | collective-permute-start | bytes 589832 | tf_op jit(solution)/shard_map/ppermute | solution.py:107
  162.2 8.6 %collective-permute-start.28 = (bf16[2,64,768]{2,1,0:T(8,128)(2,1)S(1)}, bf16[2,64,768]{2,1,0:T(8,128)(2,1)S(1)}, u32[]{:S(2)}, u32[]{:S(2)}) collective-permute-start(bf16[2,64,768]{2,1,0:T(8,128)(2,1)S(1)} %get-tuple-element.59), channel_id=1, source_target_pairs={{0,2},{2,0},{1,3},{3,1},{4,6},{6,4},{5,7},{7,5},{8,10},{10,8},{9,1... | collective-permute-start | bytes 589832 | tf_op jit(solution)/shard_map/ppermute | solution.py:107

commit v16 on v14

--- a/solution.py
+++ b/solution.py
@@ -127,27 +127,30 @@
     )(*prefetch, *operands)
 
 
-def project(place, mine, theirs, chunks):
+def project(place, mine, theirs, chunks, first, cols):
     rows, (count, width) = len(mine), theirs[0].shape
-    _, half, cols = chunks[0][0].shape
+    half = chunks[0][0].shape[1]
     slices = len(chunks)
     flat = [w for of_round in chunks for w in of_round]
+    fetched = 2 * rows + len(flat)
 
     def kernel(place_ref, *refs):
         row, group, frame, core = (place_ref[i] for i in range(4))
-        x_refs, w_refs = refs[: 2 * rows], refs[2 * rows : 2 * rows + len(flat)]
-        q_keep, kv_keep, send, x_all, w_all, total, sems = refs[2 * rows + len(flat) :]
+        w_refs = refs[2 * rows : fetched]
+        q_keep, kv_keep, send, x_all, w_all, total, sems = refs[fetched:]
         copies = []
-        for i, x_ref in enumerate(x_refs):
-            to = x_all.at[row ^ (i % rows), (frame + i // rows) % 2]
-            copies.append(pltpu.make_async_copy(x_ref.at[pl.ds(0, count)], to, sems.at[i]))
-            copies[-1].start()
         for k in range(slices):
             for g in range(2):
-                at = (row + slices - k) % slices * (2 * half) + (group + g) % 2 * half
+                at = pl.multiple_of((row + slices - k) % slices * (2 * half) + (group + g) % 2 * half, half)
                 for part in range(3):
-                    into = w_all.at[pl.ds(pl.multiple_of(at, half), half), part * cols : (part + 1) * cols]
-                    into[...] = w_refs[2 * k + g][part]
+                    source = w_refs[2 * k + g].at[part, :, first : first + cols]
+                    into = w_all.at[pl.ds(at, half), part * cols : (part + 1) * cols]
+                    copies.append(pltpu.make_async_copy(source, into, sems.at[len(copies)]))
+        for i in range(2 * rows):
+            to = x_all.at[row ^ (i % rows), (frame + i // rows) % 2]
+            copies.append(pltpu.make_async_copy(refs[i].at[pl.ds(0, count)], to, sems.at[len(copies)]))
+        for copy in copies:
+            copy.start()
         for copy in copies:
             copy.wait()
         acc = jnp.dot(x_all[...].reshape(-1, width), w_all[...], preferred_element_type=jnp.float32)
@@ -174,13 +177,13 @@
         grid_spec=pltpu.PrefetchScalarGridSpec(
             num_scalar_prefetch=1,
             grid=(),
-            in_specs=[hbm] * (2 * rows) + [vmem] * len(flat),
+            in_specs=[hbm] * fetched,
             out_specs=(vmem, vmem, vmem),
             scratch_shapes=[
                 pltpu.VMEM((rows, 2, count, width), jnp.bfloat16),
                 pltpu.VMEM((width, 3 * cols), jnp.bfloat16),
                 pltpu.VMEM((rows, 2, count, cols), jnp.float32),
-                pltpu.SemaphoreType.DMA((2 * rows,)),
+                pltpu.SemaphoreType.DMA((2 * rows + 3 * len(flat),)),
             ],
         ),
         compiler_params=pltpu.CompilerParams(vmem_limit_bytes=VMEM_BYTES),
@@ -323,13 +326,9 @@
     half = depth // 2
     place = jnp.stack([row, group, frame, core]).astype(jnp.int32)
 
-    last = cols // (3 * HD) * HD
-
-    def reshard(i, *others):
-        k = i % span
-        at, wide = (0, cols - last) if i < span else (cols - last, last)
+    def reshard(k, *others):
         value = lax.dynamic_slice(
-            w_qkv.transpose(1, 0, 2), (0, group * half, (k + row) % span * cols + at), (3, half, wide)
+            w_qkv.transpose(1, 0, 2), (0, group * half, (k + row) % span * cols), (3, half, cols)
         )
         pairs = [
             (r * heads_n + h, (h * span + (k + r) % span) * heads_n + r // span)
@@ -350,15 +349,12 @@
     there.append(swap(here[0], "groups"))
     here.append(reshard(1, near, mine_x, here[0]))
     far_2 = swap(after(joined, here[0]), "rows", 2)
+    out_half = lax.dynamic_slice_in_dim(w_out, group * cols, cols, axis=0)
+    beside = [swap(after(out_half, here[0]), "rows")]
     there.append(swap(here[1], "groups"))
     far_2x = swap(far_2, "frames")
-    far_3 = swap(after(joined, far_2), "rows", 3)
-    here.append(reshard(2, far_2, near_x, there[0], across))
-    out_half = lax.dynamic_slice_in_dim(w_out, group * cols, cols, axis=0)
-    beside = [swap(after(out_half, far_2), "rows")]
-    here.append(reshard(3, here[1]))
-    far_3x = swap(after(far_3, here[2], there[1]), "frames")
-    there += [swap(here[2], "groups"), swap(after(here[3], beside[0]), "groups")]
+    far_3 = swap(after(joined, far_2, near_x, there[0], across), "rows", 3)
+    far_3x = swap(far_3, "frames")
 
     found = jnp.stack([x[count : count + heads_n, : MAXB + 2] for x in (joined, near, far_2, far_3)])
     tables = found.astype(jnp.int32)[row ^ jnp.arange(rows_n)].reshape(rows_n * heads_n, MAXB + 2)
@@ -369,15 +365,18 @@
     members, counts = picked[:, :MAXB].reshape(-1), picked[:, MAXB]
 
     pieces = [joined, near, far_2, far_3], [mine_x, near_x, far_2x, far_3x]
-    first = project(place, *pieces, [(here[0], there[0]), (here[1], after(there[1], there[2], members, counts))])
-    beside.append(swap(after(beside[0], first[2]), "groups"))
+    chunks = [(here[0], there[0]), (here[1], after(there[1], members, counts, beside[0]))]
+    last = cols // (3 * HD) * HD
+    first = project(place, *pieces, chunks, 0, cols - last)
     first_more = swap(first[2], "heads")
-    second = project(place, *pieces, [(here[2], there[2]), (here[3], after(there[3], first[2]))])
+    beside.append(swap(after(beside[0], there[1]), "groups"))
+    chunks[1] = (here[1], after(there[1], first[2]))
+    second = project(place, *pieces, chunks, cols - last, last)
     second_more = swap(second[2], "heads")
     attended = attend_all(place, members, counts, *first[:2], first_more)
     same, diff = attend_all(place, members, counts, *second[:2], second_more, attended)
     attended = [same] + [swap(same if s % 2 == 0 else diff, "rows", s) for s in range(1, rows_n)]
-    beside_across = [swap(part, "heads") for part in (beside[0], after(beside[1], *attended[1:]))]
+    beside_across = [swap(part, "heads") for part in (beside[0], after(beside[1], same))]
     near_keep, near_send, far_keep, far_send = mix(place, attended, w_out, across, beside, beside_across)
     far_more = swap(far_send, "frames")
     far = swap((far_keep + far_more.astype(jnp.float32)).astype(jnp.bfloat16), "rows", 2)

time: 171 us -> 184 us (1.076)
  waiting for transfers between devices: 76.6 us -> 103 us
  starting transfers between devices: 50.7 us -> 45.3 us
  other arithmetic: 4.36 us -> 0.64 us
  local copies, waits for them, and re-layouts: 16.1 us -> 12.4 us
    ppermute x24 -> x22, waiting for transfers between devices: 72.2 us -> 103 us  [swap(): return lax.ppermute(value, axis, [(i, i ^ step) for i in range(peers)])]
    ppermute x24 -> x22, starting transfers between devices: 42.9 us -> 34.7 us  [swap(): return lax.ppermute(value, axis, [(i, i ^ step) for i in range(peers)])]
    ppermute x4 -> x2, waiting for transfers between devices: 4.44 us -> 0.01 us  [reshard(): lax.ppermute(after(value, *others) if others else value, ('rows', 'heads'...]
    ppermute x4 -> x2, starting transfers between devices: 7.74 us -> 10.6 us  [reshard(): lax.ppermute(after(value, *others) if others else value, ('rows', 'heads'...]
    unnamed x28, local copies, waits for them, and re-layouts: 6.57 us -> 4.58 us
    dynamic_slice x2 -> x1, local copies, waits for them, and re-layouts: 3.99 us -> 2.92 us  [reshard(): lax.dynamic_slice(w_qkv.transpose(1, 0, 2), (0, group * half, (k + row) %...]
  transfers between devices with their start and end apart: 28 -> 24, of which waited for: 11 -> 11; matrix products, arithmetic and copies ran while one was open for 6% -> 3% of each run, Pallas kernels for 10% -> 6%
where the time goes in v16:
time: 184 us; the launch traced here: 183 us
  waiting for transfers between devices  103 us (56%)
  starting transfers between devices  45.3 us (25%)
  Pallas kernels  21.2 us (12%)
  local copies, waits for them, and re-layouts  12.4 us (7%)
    ppermute x22, waiting for transfers between devices, swap(): return lax.ppermute(value, axis, [(i, i ^ step) for i in range(peers)])  103 us
    ppermute x22, starting transfers between devices, swap(): return lax.ppermute(value, axis, [(i, i ^ step) for i in range(peers)])  34.7 us
    pallas_call x4, Pallas kernels, call(): pl.pallas_call(kernel, out_shape=out_shape, grid_spec=pltpu.PrefetchScala...  10.8 us
    ppermute x2, starting transfers between devices, reshard(): lax.ppermute(after(value, *others) if others else value, ('rows', 'heads'...  10.6 us
    pallas_call x2, Pallas kernels, project(): pl.pallas_call(kernel, out_shape=(jax.ShapeDtypeStruct((rows, 2 * BS, col...  10.4 us
    unnamed x28, local copies, waits for them, and re-layouts  4.58 us
  transfers between devices with their start and end apart: 24, of which 11 were waited for; matrix products, arithmetic and copies ran while one was open for 3% of the time, Pallas kernels for 6%

profile of v16, /device:TPU:0, one launch (start us, length us, event | category | flops | bytes accessed | tf_op | source)
XLA Modules:
  0.0 182.7 jit_solution(3058529435344111719)
XLA Ops:
  0.0 2.9 %dynamic-slice_bitcast_fusion = (bf16[3,384,384]{2,1,0:T(8,128)(2,1)}, bf16[3,384,384]{2,1,0:T(8,128)(2,1)}) fusion(bf16[768,3,768]{2,0,1:T(8,128)(2,1)} %param.7, s32[]{:T(128)S(6)} %select_n.44, s32[]{:T(128)S(6)} %select_n.51, s32[]{:T(128)S(6)} %select_n.46), kind=kLoop, calls=%fused_computation.2 | loop fusion | bytes 3538956 | tf_op jit(solution)/shard_map/dynamic_slice | solution.py:330
  2.9 8.4 %collective-permute-start.1 = (bf16[3,384,384]{2,1,0:T(8,128)(2,1)}, bf16[3,384,384]{2,1,0:T(8,128)(2,1)}, u32[]{:S(2)}, u32[]{:S(2)}) collective-permute-start(bf16[3,384,384]{2,1,0:T(8,128)(2,1)} %get-tuple-element.54), channel_id=1, source_target_pairs={{0,0},{1,8},{4,4},{5,12},{8,1},{9,9},{12,5},{13,13},{2,2},{3,10},{... | collective-permute-start | bytes 2654216 | tf_op jit(solution)/shard_map/ppermute | solution.py:338
  11.7 3.1 %collective-permute-start = (bf16[136,1536]{1,0:T(8,128)(2,1)S(1)}, bf16[136,1536]{1,0:T(8,128)(2,1)S(1)}, u32[]{:S(2)}, u32[]{:S(2)}) collective-permute-start(bf16[136,1536]{1,0:T(8,128)(2,1)S(1)} %fusion.1.refs_0_), channel_id=1, source_target_pairs={{0,4},{4,0},{8,12},{12,8},{1,5},{5,1},{9,13},{13,9},{2,6},{6,2},{1... | collective-permute-start | bytes 1253384 | tf_op jit(solution)/shard_map/ppermute | solution.py:107
  14.8 10.1 %collective-permute-done.refs_1_ = bf16[136,1536]{1,0:T(8,128)(2,1)S(1)} collective-permute-done((bf16[136,1536]{1,0:T(8,128)(2,1)S(1)}, bf16[136,1536]{1,0:T(8,128)(2,1)S(1)}, u32[]{:S(2)}, u32[]{:S(2)}) %collective-permute-start) | collective-permute-done | bytes 417824 | tf_op jit(solution)/shard_map/ppermute | solution.py:107
  24.9 0.8 copy-done.5
  25.7 3.4 %collective-permute-start.5 = (bf16[768,768]{1,0:T(8,128)(2,1)S(1)}, bf16[768,768]{1,0:T(8,128)(2,1)S(1)}, u32[]{:S(2)}, u32[]{:S(2)}) collective-permute-start(bf16[768,768]{1,0:T(8,128)(2,1)S(1)} %copy-done.1), channel_id=1, source_target_pairs={{0,1},{1,0},{2,3},{3,2},{4,5},{5,4},{6,7},{7,6},{8,9},{9,8},{10,11... | collective-permute-start | bytes 3538952 | tf_op jit(solution)/shard_map/ppermute | solution.py:107
  29.1 1.5 collective-permute-start.7
  30.6 1.5 collective-permute-start.4
  32.1 8.0 %collective-permute-done.7.refs_4_ = bf16[128,1536]{1,0:T(8,128)(2,1)S(1)} collective-permute-done((bf16[128,1536]{1,0:T(8,128)(2,1)S(1)}, bf16[128,1536]{1,0:T(8,128)(2,1)S(1)}, u32[]{:S(2)}, u32[]{:S(2)}) %collective-permute-start.7) | collective-permute-done | bytes 393248 | tf_op jit(solution)/shard_map/ppermute | solution.py:107
  40.1 2.2 %collective-permute-start.10 = (bf16[3,384,384]{2,1,0:T(8,128)(2,1)}, bf16[3,384,384]{2,1,0:T(8,128)(2,1)}, u32[]{:S(2)}, u32[]{:S(2)}) collective-permute-start(bf16[3,384,384]{2,1,0:T(8,128)(2,1)} %get-tuple-element.32), channel_id=1, source_target_pairs={{0,4},{1,12},{4,0},{5,8},{8,5},{9,13},{12,1},{13,9},{2,6},{3,14},{... | collective-permute-start | bytes 2654216 | tf_op jit(solution)/shard_map/ppermute | solution.py:338
  42.4 1.5 collective-permute-start.3
  44.0 0.8 collective-permute-start.2
  45.0 0.9 constant_dynamic-slice_fusion
  45.8 7.4 %collective-permute-done.3.refs_5_ = bf16[136,1536]{1,0:T(8,128)(2,1)S(1)} collective-permute-done((bf16[136,1536]{1,0:T(8,128)(2,1)}, bf16[136,1536]{1,0:T(8,128)(2,1)S(1)}, u32[]{:S(2)}, u32[]{:S(2)}) %collective-permute-start.3) | collective-permute-done | bytes 417824 | tf_op jit(solution)/shard_map/ppermute | solution.py:107
  53.3 0.8 copy-done.8
  54.0 27.8 %collective-permute-done.2.refs_2_ = bf16[136,1536]{1,0:T(8,128)(2,1)} collective-permute-done((bf16[136,1536]{1,0:T(8,128)(2,1)}, bf16[136,1536]{1,0:T(8,128)(2,1)}, u32[]{:S(2)}, u32[]{:S(2)}) %collective-permute-start.2) | collective-permute-done | bytes 417824 | tf_op jit(solution)/shard_map/ppermute | solution.py:107
  81.9 0.7 slice_bitcast_fusion.2
  82.6 1.5 collective-permute-start.8
  84.1 1.5 collective-permute-start.11
  85.7 0.7 slice_bitcast_fusion.1
  86.3 10.3 %collective-permute-done.6.refs_3_ = bf16[136,1536]{1,0:T(8,128)(2,1)} collective-permute-done((bf16[136,1536]{1,0:T(8,128)(2,1)}, bf16[136,1536]{1,0:T(8,128)(2,1)}, u32[]{:S(2)}, u32[]{:S(2)}) %collective-permute-start.6) | collective-permute-done | bytes 417824 | tf_op jit(solution)/shard_map/ppermute | solution.py:107
  96.6 1.5 collective-permute-start.9
  98.1 0.7 slice_bitcast_fusion
  98.8 0.6 gather_fusion
  99.6 0.2 fusion.3
  99.8 0.6 gather_fusion.1
  100.7 6.1 %collective-permute-done.12.refs_6_ = bf16[384,768]{1,0:T(8,128)(2,1)} collective-permute-done((bf16[384,768]{1,0:T(8,128)(2,1)}, bf16[384,768]{1,0:T(8,128)(2,1)}, u32[]{:S(2)}, u32[]{:S(2)}) %collective-permute-start.12) | collective-permute-done | bytes 589856 | tf_op jit(solution)/shard_map/ppermute | solution.py:107
  106.8 1.0 copy-done.3
  107.8 1.0 copy-done.6
  108.8 1.0 copy-done.9
  109.8 5.7 %shard_map.64 = (f32[4,128,256]{2,1,0:T(8,128)S(1)}, f32[4,256,512]{2,1,0:T(8,128)S(1)}, bf16[4,320,512]{2,1,0:T(8,128)(2,1)S(1)}) custom-call(s32[4]{0:T(128)S(1)} %pad_add_fusion.place_ref, bf16[136,1536]{1,0:T(8,128)(2,1)S(1)} %copy-done.3, bf16[136,1536]{1,0:T(8,128)(2,1)S(1)} %copy-done.6, bf16[136,1536]{1,0:T(8,128)(2,1)} %collective-permute-done.2.refs_2_, ...), custom_call_target="tpu_custom_call" | custom-call | flops 19327352832 | bytes 8053063 | tf_op jit(solution)/shard_map/pallas_call | solution.py:170
  115.7 4.7 %shard_map.65 = (f32[4,128,128]{2,1,0:T(8,128)S(1)}, f32[4,256,256]{2,1,0:T(8,128)S(1)}, bf16[4,320,256]{2,1,0:T(8,128)(2,1)S(1)}) custom-call(s32[4]{0:T(128)S(1)} %pad_add_fusion.place_ref, bf16[136,1536]{1,0:T(8,128)(2,1)S(1)} %copy-done.4, bf16[136,1536]{1,0:T(8,128)(2,1)S(1)} %copy-done.7, bf16[136,1536]{1,0:T(8,128)(2,1)} %collective-permute-done.2.refs_2_, ...), custom_call_target="tpu_custom_call" | custom-call | flops 9663676416 | bytes 4026531 | tf_op jit(solution)/shard_map/pallas_call | solution.py:170
  120.4 0.5 collective-permute-start.13
  120.9 1.5 collective-permute-start.18
  122.4 3.8 %shard_map.66 = (bf16[2,128,256]{2,1,0:T(8,128)(2,1)S(1)}, bf16[2,128,256]{2,1,0:T(8,128)(2,1)S(1)}) custom-call(s32[4]{0:T(128)S(1)} %pad_add_fusion.place_ref, s32[16]{0:T(128)S(1)} %reshape.24.members_ref, s32[4]{0:T(128)S(1)} %slice_reduce_fusion.1.counts_ref, f32[4,128,256]{2,1,0:T(8,128)S(1)} %get-tuple-element.40.q_ref, ...), custom_call_target="tpu_custom_call" | custom-call | flops 268435456 | bytes 2097152 | tf_op jit(solution)/shard_map/pallas_call | solution.py:115
  126.2 2.2 %shard_map.67 = (bf16[2,128,384]{2,1,0:T(8,128)(2,1)S(1)}, bf16[2,128,384]{2,1,0:T(8,128)(2,1)S(1)}) custom-call(s32[4]{0:T(128)S(1)} %pad_add_fusion.place_ref, s32[16]{0:T(128)S(1)} %reshape.24.members_ref, s32[4]{0:T(128)S(1)} %slice_reduce_fusion.1.counts_ref, f32[4,128,128]{2,1,0:T(8,128)S(1)} %get-tuple-element.37.q_ref, ...), custom_call_target="tpu_custom_call" | custom-call | flops 134217728 | bytes 1048576 | tf_op jit(solution)/shard_map/pallas_call | solution.py:115
  128.4 8.0 %collective-permute-done.18.refs_7_ = bf16[384,768]{1,0:T(8,128)(2,1)S(1)} collective-permute-done((bf16[384,768]{1,0:T(8,128)(2,1)}, bf16[384,768]{1,0:T(8,128)(2,1)S(1)}, u32[]{:S(2)}, u32[]{:S(2)}) %collective-permute-start.18) | collective-permute-done | bytes 589856 | tf_op jit(solution)/shard_map/ppermute | solution.py:107
  136.5 6.9 %collective-permute-start.15 = (bf16[2,128,384]{2,1,0:T(8,128)(2,1)S(1)}, bf16[2,128,384]{2,1,0:T(8,128)(2,1)S(1)}, u32[]{:S(2)}, u32[]{:S(2)}) collective-permute-start(bf16[2,128,384]{2,1,0:T(8,128)(2,1)S(1)} %get-tuple-element.45), channel_id=1, source_target_pairs={{0,4},{4,0},{8,12},{12,8},{1,5},{5,1},{9,13},{13,9},{2,6},{6,2},{1... | collective-permute-start | bytes 589832 | tf_op jit(solution)/shard_map/ppermute | solution.py:107
  143.3 2.4 %collective-permute-start.17 = (bf16[2,128,384]{2,1,0:T(8,128)(2,1)S(1)}, bf16[2,128,384]{2,1,0:T(8,128)(2,1)S(1)}, u32[]{:S(2)}, u32[]{:S(2)}) collective-permute-start(bf16[2,128,384]{2,1,0:T(8,128)(2,1)S(1)} %get-tuple-element.45), channel_id=1, source_target_pairs={{0,12},{4,8},{8,4},{12,0},{1,13},{5,9},{9,5},{13,1},{2,14},{6,10},... | collective-permute-start | bytes 589832 | tf_op jit(solution)/shard_map/ppermute | solution.py:107
  145.7 5.4 %collective-permute-done.15.refs_1_ = bf16[2,128,384]{2,1,0:T(8,128)(2,1)S(1)} collective-permute-done((bf16[2,128,384]{2,1,0:T(8,128)(2,1)S(1)}, bf16[2,128,384]{2,1,0:T(8,128)(2,1)S(1)}, u32[]{:S(2)}, u32[]{:S(2)}) %collective-permute-start.15) | collective-permute-done | bytes 196640 | tf_op jit(solution)/shard_map/ppermute | solution.py:107
  151.1 9.3 %collective-permute-done.16.refs_2_ = bf16[2,128,384]{2,1,0:T(8,128)(2,1)S(1)} collective-permute-done((bf16[2,128,384]{2,1,0:T(8,128)(2,1)S(1)}, bf16[2,128,384]{2,1,0:T(8,128)(2,1)S(1)}, u32[]{:S(2)}, u32[]{:S(2)}) %collective-permute-start.16) | collective-permute-done | bytes 196640 | tf_op jit(solution)/shard_map/ppermute | solution.py:107
  160.4 3.5 %shard_map.68 = (f32[2,64,768]{2,1,0:T(8,128)S(1)}, bf16[2,64,768]{2,1,0:T(8,128)(2,1)S(1)}, f32[2,64,768]{2,1,0:T(8,128)S(1)}, bf16[2,64,768]{2,1,0:T(8,128)(2,1)S(1)}) custom-call(s32[4]{0:T(128)S(1)} %pad_add_fusion.place_ref, bf16[2,128,384]{2,1,0:T(8,128)(2,1)S(1)} %get-tuple-element.44.refs_0_, ...), custom_call_target="tpu_custom_call" | custom-call | flops 1207959552 | bytes 4718592 | tf_op jit(solution)/shard_map/pallas_call | solution.py:115
  164.0 1.6 collective-permute-start.21
  165.5 4.2 %collective-permute-done.21 = bf16[2,64,768]{2,1,0:T(8,128)(2,1)S(1)} collective-permute-done((bf16[2,64,768]{2,1,0:T(8,128)(2,1)S(1)}, bf16[2,64,768]{2,1,0:T(8,128)(2,1)S(1)}, u32[]{:S(2)}, u32[]{:S(2)}) %collective-permute-start.21) | collective-permute-done | bytes 196640 | tf_op jit(solution)/shard_map/ppermute | solution.py:107
  169.7 3.8 %collective-permute-start.23 = (bf16[2,64,768]{2,1,0:T(8,128)(2,1)S(1)}, bf16[2,64,768]{2,1,0:T(8,128)(2,1)S(1)}, u32[]{:S(2)}, u32[]{:S(2)}) collective-permute-start(bf16[2,64,768]{2,1,0:T(8,128)(2,1)S(1)} %add_convert_fusion), channel_id=1, source_target_pairs={{0,8},{4,12},{8,0},{12,4},{1,9},{5,13},{9,1},{13,5},{2,10},{6,14},... | collective-permute-start | bytes 589832 | tf_op jit(solution)/shard_map/ppermute | solution.py:107
  173.6 1.5 collective-permute-start.22
  175.0 6.4 %collective-permute-done.23.far_ref = bf16[2,64,768]{2,1,0:T(8,128)(2,1)S(1)} collective-permute-done((bf16[2,64,768]{2,1,0:T(8,128)(2,1)S(1)}, bf16[2,64,768]{2,1,0:T(8,128)(2,1)S(1)}, u32[]{:S(2)}, u32[]{:S(2)}) %collective-permute-start.23) | collective-permute-done | bytes 196640 | tf_op jit(solution)/shard_map/ppermute | solution.py:107
  181.4 1.3 shard_map.69
  (61 shorter events, 1.6 us)
Async XLA Ops:
  0.0 11.6 %copy-start = (bf16[1,128,3072]{2,1,0:T(8,128)(2,1)S(1)}, bf16[1,128,3072]{2,1,0:T(8,128)(2,1)}, u32[]{:S(2)}) copy-start(bf16[1,128,3072]{2,1,0:T(8,128)(2,1)} %param.6) | copy-start | bytes 2359300
  0.0 11.3 %copy-start.12 = (s32[2]{0:T(128)S(1)}, s32[2]{0:T(128)}, u32[]{:S(2)}) copy-start(s32[2]{0:T(128)} %param.11) | copy-start | bytes 28
  0.0 11.4 %copy-start.13 = (s32[2]{0:T(128)S(1)}, s32[2]{0:T(128)}, u32[]{:S(2)}) copy-start(s32[2]{0:T(128)} %param.10) | copy-start | bytes 28
  0.0 11.5 %copy-start.11 = (s32[2,4]{1,0:T(2,128)S(1)}, s32[2,4]{1,0:T(2,128)}, u32[]{:S(2)}) copy-start(s32[2,4]{1,0:T(2,128)} %param.9) | copy-start | bytes 100
  2.9 22.8 %copy-start.1 = (bf16[768,768]{1,0:T(8,128)(2,1)S(1)}, bf16[768,768]{1,0:T(8,128)(2,1)}, u32[]{:S(2)}) copy-start(bf16[768,768]{1,0:T(8,128)(2,1)} %refs_4_.1) | copy-start | bytes 3538948
  2.9 27.7 %collective-permute-start.1 = (bf16[3,384,384]{2,1,0:T(8,128)(2,1)}, bf16[3,384,384]{2,1,0:T(8,128)(2,1)}, u32[]{:S(2)}, u32[]{:S(2)}) collective-permute-start(bf16[3,384,384]{2,1,0:T(8,128)(2,1)} %get-tuple-element.54), channel_id=1, source_target_pairs={{0,0},{1,8},{4,4},{5,12},{8,1},{9,9},{12,5},{13,13},{2,2},{3,10},{... | collective-permute-start | bytes 2654216 | tf_op jit(solution)/shard_map/ppermute | solution.py:338
  11.7 3.1 %copy-start.2 = (bf16[136,1536]{1,0:T(8,128)(2,1)}, bf16[136,1536]{1,0:T(8,128)(2,1)S(1)}, u32[]{:S(2)}) copy-start(bf16[136,1536]{1,0:T(8,128)(2,1)S(1)} %fusion.1.refs_0_) | copy-start | bytes 1253380
  11.7 13.2 %collective-permute-start = (bf16[136,1536]{1,0:T(8,128)(2,1)S(1)}, bf16[136,1536]{1,0:T(8,128)(2,1)S(1)}, u32[]{:S(2)}, u32[]{:S(2)}) collective-permute-start(bf16[136,1536]{1,0:T(8,128)(2,1)S(1)} %fusion.1.refs_0_), channel_id=1, source_target_pairs={{0,4},{4,0},{8,12},{12,8},{1,5},{5,1},{9,13},{13,9},{2,6},{6,2},{1... | collective-permute-start | bytes 1253384 | tf_op jit(solution)/shard_map/ppermute | solution.py:107
  24.9 0.8 copy-start.5
  25.7 56.1 %collective-permute-start.5 = (bf16[768,768]{1,0:T(8,128)(2,1)S(1)}, bf16[768,768]{1,0:T(8,128)(2,1)S(1)}, u32[]{:S(2)}, u32[]{:S(2)}) collective-permute-start(bf16[768,768]{1,0:T(8,128)(2,1)S(1)} %copy-done.1), channel_id=1, source_target_pairs={{0,1},{1,0},{2,3},{3,2},{4,5},{5,4},{6,7},{7,6},{8,9},{9,8},{10,11... | collective-permute-start | bytes 3538952 | tf_op jit(solution)/shard_map/ppermute | solution.py:107
  29.1 11.0 %collective-permute-start.7 = (bf16[128,1536]{1,0:T(8,128)(2,1)S(1)}, bf16[128,1536]{1,0:T(8,128)(2,1)S(1)}, u32[]{:S(2)}, u32[]{:S(2)}) collective-permute-start(bf16[128,1536]{1,0:T(8,128)(2,1)S(1)} %dynamic-slice_bitcast_fusion.2), channel_id=1, source_target_pairs={{0,2},{2,0},{1,3},{3,1},{4,6},{6,4},{5,7},{7,5},{8,10},{10,8},{9,1... | collective-permute-start | bytes 1179656 | tf_op jit(solution)/shard_map/ppermute | solution.py:107
  30.6 51.3 %collective-permute-start.4 = (bf16[3,384,384]{2,1,0:T(8,128)(2,1)}, bf16[3,384,384]{2,1,0:T(8,128)(2,1)}, u32[]{:S(2)}, u32[]{:S(2)}) collective-permute-start(bf16[3,384,384]{2,1,0:T(8,128)(2,1)} %collective-permute-done.1.refs_8_), channel_id=1, source_target_pairs={{0,16},{16,0},{1,17},{17,1},{2,18},{18,2},{3,19},{19,3},{4,20},{20... | collective-permute-start | bytes 2654216 | tf_op jit(solution)/shard_map/ppermute | solution.py:107
  40.1 44.0 %collective-permute-start.10 = (bf16[3,384,384]{2,1,0:T(8,128)(2,1)}, bf16[3,384,384]{2,1,0:T(8,128)(2,1)}, u32[]{:S(2)}, u32[]{:S(2)}) collective-permute-start(bf16[3,384,384]{2,1,0:T(8,128)(2,1)} %get-tuple-element.32), channel_id=1, source_target_pairs={{0,4},{1,12},{4,0},{5,8},{8,5},{9,13},{12,1},{13,9},{2,6},{3,14},{... | collective-permute-start | bytes 2654216 | tf_op jit(solution)/shard_map/ppermute | solution.py:338
  42.4 10.8 %collective-permute-start.3 = (bf16[136,1536]{1,0:T(8,128)(2,1)}, bf16[136,1536]{1,0:T(8,128)(2,1)S(1)}, u32[]{:S(2)}, u32[]{:S(2)}) collective-permute-start(bf16[136,1536]{1,0:T(8,128)(2,1)} %copy-done.5), channel_id=1, source_target_pairs={{0,2},{2,0},{1,3},{3,1},{4,6},{6,4},{5,7},{7,5},{8,10},{10,8},{9,1... | collective-permute-start | bytes 1253384 | tf_op jit(solution)/shard_map/ppermute | solution.py:107
  44.0 37.9 %collective-permute-start.2 = (bf16[136,1536]{1,0:T(8,128)(2,1)}, bf16[136,1536]{1,0:T(8,128)(2,1)}, u32[]{:S(2)}, u32[]{:S(2)}) collective-permute-start(bf16[136,1536]{1,0:T(8,128)(2,1)} %copy-done.2), channel_id=1, source_target_pairs={{0,8},{4,12},{8,0},{12,4},{1,9},{5,13},{9,1},{13,5},{2,10},{6,14},... | collective-permute-start | bytes 1253384 | tf_op jit(solution)/shard_map/ppermute | solution.py:107
  53.3 0.8 copy-start.8
  81.9 14.7 %collective-permute-start.6 = (bf16[136,1536]{1,0:T(8,128)(2,1)}, bf16[136,1536]{1,0:T(8,128)(2,1)}, u32[]{:S(2)}, u32[]{:S(2)}) collective-permute-start(bf16[136,1536]{1,0:T(8,128)(2,1)} %copy-done.2), channel_id=1, source_target_pairs={{0,12},{4,8},{8,4},{12,0},{1,13},{5,9},{9,5},{13,1},{2,14},{6,10},... | collective-permute-start | bytes 1253384 | tf_op jit(solution)/shard_map/ppermute | solution.py:107
  82.5 24.3 %collective-permute-start.12 = (bf16[384,768]{1,0:T(8,128)(2,1)}, bf16[384,768]{1,0:T(8,128)(2,1)}, u32[]{:S(2)}, u32[]{:S(2)}) collective-permute-start(bf16[384,768]{1,0:T(8,128)(2,1)} %constant_dynamic-slice_fusion), channel_id=1, source_target_pairs={{0,4},{4,0},{8,12},{12,8},{1,5},{5,1},{9,13},{13,9},{2,6},{6,2},{1... | collective-permute-start | bytes 1769480 | tf_op jit(solution)/shard_map/ppermute | solution.py:107
  82.6 24.2 %collective-permute-start.8 = (bf16[136,1536]{1,0:T(8,128)(2,1)}, bf16[136,1536]{1,0:T(8,128)(2,1)}, u32[]{:S(2)}, u32[]{:S(2)}) collective-permute-start(bf16[136,1536]{1,0:T(8,128)(2,1)} %collective-permute-done.2.refs_2_), channel_id=1, source_target_pairs={{0,2},{2,0},{1,3},{3,1},{4,6},{6,4},{5,7},{7,5},{8,10},{10,8},{9,1... | collective-permute-start | bytes 1253384 | tf_op jit(solution)/shard_map/ppermute | solution.py:107
  84.1 22.7 %collective-permute-start.11 = (bf16[3,384,384]{2,1,0:T(8,128)(2,1)}, bf16[3,384,384]{2,1,0:T(8,128)(2,1)}, u32[]{:S(2)}, u32[]{:S(2)}) collective-permute-start(bf16[3,384,384]{2,1,0:T(8,128)(2,1)} %collective-permute-done.10.refs_10_), channel_id=1, source_target_pairs={{0,16},{16,0},{1,17},{17,1},{2,18},{18,2},{3,19},{19,3},{4,20},{20... | collective-permute-start | bytes 2654216 | tf_op jit(solution)/shard_map/ppermute | solution.py:107
  96.6 10.2 %collective-permute-start.9 = (bf16[136,1536]{1,0:T(8,128)(2,1)}, bf16[136,1536]{1,0:T(8,128)(2,1)}, u32[]{:S(2)}, u32[]{:S(2)}) collective-permute-start(bf16[136,1536]{1,0:T(8,128)(2,1)} %collective-permute-done.6.refs_3_), channel_id=1, source_target_pairs={{0,2},{2,0},{1,3},{3,1},{4,6},{6,4},{5,7},{7,5},{8,10},{10,8},{9,1... | collective-permute-start | bytes 1253384 | tf_op jit(solution)/shard_map/ppermute | solution.py:107
  106.8 1.0 copy-start.3
  107.8 1.0 copy-start.6
  108.8 1.0 copy-start.9
  109.8 5.9 %copy-start.4 = (bf16[136,1536]{1,0:T(8,128)(2,1)S(1)}, bf16[136,1536]{1,0:T(8,128)(2,1)}, u32[]{:S(2)}) copy-start(bf16[136,1536]{1,0:T(8,128)(2,1)} %copy-done.2) | copy-start | bytes 1253380
  109.8 5.9 %copy-start.7 = (bf16[136,1536]{1,0:T(8,128)(2,1)S(1)}, bf16[136,1536]{1,0:T(8,128)(2,1)}, u32[]{:S(2)}) copy-start(bf16[136,1536]{1,0:T(8,128)(2,1)} %copy-done.5) | copy-start | bytes 1253380
  109.8 5.9 %copy-start.10 = (bf16[136,1536]{1,0:T(8,128)(2,1)S(1)}, bf16[136,1536]{1,0:T(8,128)(2,1)}, u32[]{:S(2)}) copy-start(bf16[136,1536]{1,0:T(8,128)(2,1)} %copy-done.8) | copy-start | bytes 1253380
  115.5 6.9 %collective-permute-start.14 = (bf16[4,320,512]{2,1,0:T(8,128)(2,1)S(1)}, bf16[4,320,512]{2,1,0:T(8,128)(2,1)S(1)}, u32[]{:S(2)}, u32[]{:S(2)}) collective-permute-start(bf16[4,320,512]{2,1,0:T(8,128)(2,1)S(1)} %get-tuple-element.35), channel_id=1, source_target_pairs={{0,1},{1,0},{2,3},{3,2},{4,5},{5,4},{6,7},{7,6},{8,9},{9,8},{10,11... | collective-permute-start | bytes 3932168 | tf_op jit(solution)/shard_map/ppermute | solution.py:107
  120.4 5.8 %collective-permute-start.13 = (bf16[4,320,256]{2,1,0:T(8,128)(2,1)S(1)}, bf16[4,320,256]{2,1,0:T(8,128)(2,1)S(1)}, u32[]{:S(2)}, u32[]{:S(2)}) collective-permute-start(bf16[4,320,256]{2,1,0:T(8,128)(2,1)S(1)} %get-tuple-element.39), channel_id=1, source_target_pairs={{0,1},{1,0},{2,3},{3,2},{4,5},{5,4},{6,7},{7,6},{8,9},{9,8},{10,11... | collective-permute-start | bytes 1966088 | tf_op jit(solution)/shard_map/ppermute | solution.py:107
  120.9 15.6 %collective-permute-start.18 = (bf16[384,768]{1,0:T(8,128)(2,1)}, bf16[384,768]{1,0:T(8,128)(2,1)S(1)}, u32[]{:S(2)}, u32[]{:S(2)}) collective-permute-start(bf16[384,768]{1,0:T(8,128)(2,1)} %collective-permute-done.12.refs_6_), channel_id=1, source_target_pairs={{0,16},{16,0},{1,17},{17,1},{2,18},{18,2},{3,19},{19,3},{4,20},{20... | collective-permute-start | bytes 1769480 | tf_op jit(solution)/shard_map/ppermute | solution.py:107
  122.4 23.3 %collective-permute-start.19 = (bf16[384,768]{1,0:T(8,128)(2,1)}, bf16[384,768]{1,0:T(8,128)(2,1)S(1)}, u32[]{:S(2)}, u32[]{:S(2)}) collective-permute-start(bf16[384,768]{1,0:T(8,128)(2,1)} %collective-permute-done.12.refs_6_), channel_id=1, source_target_pairs={{0,1},{1,0},{2,3},{3,2},{4,5},{5,4},{6,7},{7,6},{8,9},{9,8},{10,11... | collective-permute-start | bytes 1769480 | tf_op jit(solution)/shard_map/ppermute | solution.py:107
  136.5 24.0 %collective-permute-start.20 = (bf16[384,768]{1,0:T(8,128)(2,1)S(1)}, bf16[384,768]{1,0:T(8,128)(2,1)S(1)}, u32[]{:S(2)}, u32[]{:S(2)}) collective-permute-start(bf16[384,768]{1,0:T(8,128)(2,1)S(1)} %collective-permute-done.18.refs_7_), channel_id=1, source_target_pairs={{0,1},{1,0},{2,3},{3,2},{4,5},{5,4},{6,7},{7,6},{8,9},{9,8},{10,11... | collective-permute-start | bytes 1769480 | tf_op jit(solution)/shard_map/ppermute | solution.py:107
  136.5 14.7 %collective-permute-start.15 = (bf16[2,128,384]{2,1,0:T(8,128)(2,1)S(1)}, bf16[2,128,384]{2,1,0:T(8,128)(2,1)S(1)}, u32[]{:S(2)}, u32[]{:S(2)}) collective-permute-start(bf16[2,128,384]{2,1,0:T(8,128)(2,1)S(1)} %get-tuple-element.45), channel_id=1, source_target_pairs={{0,4},{4,0},{8,12},{12,8},{1,5},{5,1},{9,13},{13,9},{2,6},{6,2},{1... | collective-permute-start | bytes 589832 | tf_op jit(solution)/shard_map/ppermute | solution.py:107
  143.3 17.1 %collective-permute-start.16 = (bf16[2,128,384]{2,1,0:T(8,128)(2,1)S(1)}, bf16[2,128,384]{2,1,0:T(8,128)(2,1)S(1)}, u32[]{:S(2)}, u32[]{:S(2)}) collective-permute-start(bf16[2,128,384]{2,1,0:T(8,128)(2,1)S(1)} %get-tuple-element.44.refs_0_), channel_id=1, source_target_pairs={{0,8},{4,12},{8,0},{12,4},{1,9},{5,13},{9,1},{13,5},{2,10},{6,14},... | collective-permute-start | bytes 589832 | tf_op jit(solution)/shard_map/ppermute | solution.py:107
  143.3 17.1 %collective-permute-start.17 = (bf16[2,128,384]{2,1,0:T(8,128)(2,1)S(1)}, bf16[2,128,384]{2,1,0:T(8,128)(2,1)S(1)}, u32[]{:S(2)}, u32[]{:S(2)}) collective-permute-start(bf16[2,128,384]{2,1,0:T(8,128)(2,1)S(1)} %get-tuple-element.45), channel_id=1, source_target_pairs={{0,12},{4,8},{8,4},{12,0},{1,13},{5,9},{9,5},{13,1},{2,14},{6,10},... | collective-permute-start | bytes 589832 | tf_op jit(solution)/shard_map/ppermute | solution.py:107
  164.0 5.7 %collective-permute-start.21 = (bf16[2,64,768]{2,1,0:T(8,128)(2,1)S(1)}, bf16[2,64,768]{2,1,0:T(8,128)(2,1)S(1)}, u32[]{:S(2)}, u32[]{:S(2)}) collective-permute-start(bf16[2,64,768]{2,1,0:T(8,128)(2,1)S(1)} %get-tuple-element.50), channel_id=1, source_target_pairs={{0,2},{2,0},{1,3},{3,1},{4,6},{6,4},{5,7},{7,5},{8,10},{10,8},{9,1... | collective-permute-start | bytes 589832 | tf_op jit(solution)/shard_map/ppermute | solution.py:107
  169.7 11.7 %collective-permute-start.23 = (bf16[2,64,768]{2,1,0:T(8,128)(2,1)S(1)}, bf16[2,64,768]{2,1,0:T(8,128)(2,1)S(1)}, u32[]{:S(2)}, u32[]{:S(2)}) collective-permute-start(bf16[2,64,768]{2,1,0:T(8,128)(2,1)S(1)} %add_convert_fusion), channel_id=1, source_target_pairs={{0,8},{4,12},{8,0},{12,4},{1,9},{5,13},{9,1},{13,5},{2,10},{6,14},... | collective-permute-start | bytes 589832 | tf_op jit(solution)/shard_map/ppermute | solution.py:107
  173.6 7.9 %collective-permute-start.22 = (bf16[2,64,768]{2,1,0:T(8,128)(2,1)S(1)}, bf16[2,64,768]{2,1,0:T(8,128)(2,1)S(1)}, u32[]{:S(2)}, u32[]{:S(2)}) collective-permute-start(bf16[2,64,768]{2,1,0:T(8,128)(2,1)S(1)} %get-tuple-element.51), channel_id=1, source_target_pairs={{0,2},{2,0},{1,3},{3,1},{4,6},{6,4},{5,7},{7,5},{8,10},{10,8},{9,1... | collective-permute-start | bytes 589832 | tf_op jit(solution)/shard_map/ppermute | solution.py:107

commit v17 on v16

--- a/solution.py
+++ b/solution.py
@@ -347,13 +347,13 @@
     near_x = swap(near, "frames")
     across = swap(after(w_out, near), "heads")
     there.append(swap(here[0], "groups"))
-    here.append(reshard(1, near, mine_x, here[0]))
-    far_2 = swap(after(joined, here[0]), "rows", 2)
+    here.append(reshard(1, near))
+    far_2 = swap(after(joined, near, mine_x), "rows", 2)
     out_half = lax.dynamic_slice_in_dim(w_out, group * cols, cols, axis=0)
     beside = [swap(after(out_half, here[0]), "rows")]
-    there.append(swap(here[1], "groups"))
-    far_2x = swap(far_2, "frames")
-    far_3 = swap(after(joined, far_2, near_x, there[0], across), "rows", 3)
+    there.append(swap(after(here[1], beside[0], there[0]), "groups"))
+    far_2x = swap(after(far_2, near_x), "frames")
+    far_3 = swap(after(joined, far_2, across), "rows", 3)
     far_3x = swap(far_3, "frames")
 
     found = jnp.stack([x[count : count + heads_n, : MAXB + 2] for x in (joined, near, far_2, far_3)])
@@ -365,7 +365,7 @@
     members, counts = picked[:, :MAXB].reshape(-1), picked[:, MAXB]
 
     pieces = [joined, near, far_2, far_3], [mine_x, near_x, far_2x, far_3x]
-    chunks = [(here[0], there[0]), (here[1], after(there[1], members, counts, beside[0]))]
+    chunks = [(here[0], there[0]), (here[1], after(there[1], members, counts))]
     last = cols // (3 * HD) * HD
     first = project(place, *pieces, chunks, 0, cols - last)
     first_more = swap(first[2], "heads")
@@ -374,9 +374,9 @@
     second = project(place, *pieces, chunks, cols - last, last)
     second_more = swap(second[2], "heads")
     attended = attend_all(place, members, counts, *first[:2], first_more)
+    beside_across = [swap(part, "heads") for part in (beside[0], after(beside[1], attended[0]))]
     same, diff = attend_all(place, members, counts, *second[:2], second_more, attended)
     attended = [same] + [swap(same if s % 2 == 0 else diff, "rows", s) for s in range(1, rows_n)]
-    beside_across = [swap(part, "heads") for part in (beside[0], after(beside[1], same))]
     near_keep, near_send, far_keep, far_send = mix(place, attended, w_out, across, beside, beside_across)
     far_more = swap(far_send, "frames")
     far = swap((far_keep + far_more.astype(jnp.float32)).astype(jnp.bfloat16), "rows", 2)

time: 184 us -> 170 us (0.924)
  waiting for transfers between devices: 103 us -> 92.7 us
  starting transfers between devices: 45.3 us -> 42 us
  local copies, waits for them, and re-layouts: 12.4 us -> 10.3 us
  other arithmetic: 0.64 us -> 2.7 us
    ppermute x22, waiting for transfers between devices: 103 us -> 92.7 us  [swap(): return lax.ppermute(value, axis, [(i, i ^ step) for i in range(peers)])]
    ppermute x2, starting transfers between devices: 10.6 us -> 1.58 us  [reshard(): lax.ppermute(after(value, *others) if others else value, ('rows', 'heads'...]
    ppermute x22, starting transfers between devices: 34.7 us -> 40.5 us  [swap(): return lax.ppermute(value, axis, [(i, i ^ step) for i in range(peers)])]
    unnamed x28 -> x20, local copies, waits for them, and re-layouts: 4.58 us -> 2.8 us
  transfers between devices with their start and end apart: 24 -> 24, of which waited for: 11 -> 11; matrix products, arithmetic and copies ran while one was open for 3% -> 5% of each run, Pallas kernels for 6% -> 6%
where the time goes in v17:
time: 170 us; the launch traced here: 169 us
  waiting for transfers between devices  92.7 us (55%)
  starting transfers between devices  42 us (25%)
  Pallas kernels  21.3 us (13%)
  local copies, waits for them, and re-layouts  10.3 us (6%)
  other arithmetic  2.7 us (2%)
    ppermute x22, waiting for transfers between devices, swap(): return lax.ppermute(value, axis, [(i, i ^ step) for i in range(peers)])  92.7 us
    ppermute x22, starting transfers between devices, swap(): return lax.ppermute(value, axis, [(i, i ^ step) for i in range(peers)])  40.5 us
    pallas_call x4, Pallas kernels, call(): pl.pallas_call(kernel, out_shape=out_shape, grid_spec=pltpu.PrefetchScala...  10.9 us
    pallas_call x2, Pallas kernels, project(): pl.pallas_call(kernel, out_shape=(jax.ShapeDtypeStruct((rows, 2 * BS, col...  10.4 us
  transfers between devices with their start and end apart: 24, of which 11 were waited for; matrix products, arithmetic and copies ran while one was open for 5% of the time, Pallas kernels for 6%

profile of v17, /device:TPU:0, one launch (start us, length us, event | category | flops | bytes accessed | tf_op | source)
XLA Modules:
  0.0 169.2 jit_solution(15580765217763082396)
XLA Ops:
  0.0 0.7 convert_bitcast_fusion
  0.8 0.7 convert_bitcast_fusion.1
  1.6 0.7 convert.13
  2.5 3.1 %collective-permute-start = (bf16[136,1536]{1,0:T(8,128)(2,1)S(1)}, bf16[136,1536]{1,0:T(8,128)(2,1)}, u32[]{:S(2)}, u32[]{:S(2)}) collective-permute-start(bf16[136,1536]{1,0:T(8,128)(2,1)S(1)} %fusion.1.refs_0_), channel_id=1, source_target_pairs={{0,4},{4,0},{8,12},{12,8},{1,5},{5,1},{9,13},{13,9},{2,6},{6,2},{1... | collective-permute-start | bytes 1253384 | tf_op jit(solution)/shard_map/ppermute | solution.py:107
  5.6 2.7 %dynamic-slice_bitcast_fusion = (bf16[3,384,384]{2,1,0:T(8,128)(2,1)}, bf16[3,384,384]{2,1,0:T(8,128)(2,1)S(1)}) fusion(bf16[768,3,768]{2,0,1:T(8,128)(2,1)} %param.7, s32[]{:T(128)S(6)} %select_n.47, s32[]{:T(128)S(6)} %select_n.51, s32[]{:T(128)S(6)} %select_n.49), kind=kLoop, calls=%fused_computation.2 | loop fusion | bytes 3538956 | tf_op jit(solution)/shard_map/dynamic_slice | solution.py:330
  8.2 1.6 collective-permute-start.8
  9.8 8.7 %collective-permute-done.refs_1_ = bf16[136,1536]{1,0:T(8,128)(2,1)} collective-permute-done((bf16[136,1536]{1,0:T(8,128)(2,1)S(1)}, bf16[136,1536]{1,0:T(8,128)(2,1)}, u32[]{:S(2)}, u32[]{:S(2)}) %collective-permute-start) | collective-permute-done | bytes 417824 | tf_op jit(solution)/shard_map/ppermute | solution.py:107
  18.5 1.7 %collective-permute-start.1 = (bf16[128,1536]{1,0:T(8,128)(2,1)S(1)}, bf16[128,1536]{1,0:T(8,128)(2,1)S(1)}, u32[]{:S(2)}, u32[]{:S(2)}) collective-permute-start(bf16[128,1536]{1,0:T(8,128)(2,1)S(1)} %copy-done.9), channel_id=1, source_target_pairs={{0,2},{2,0},{1,3},{3,1},{4,6},{6,4},{5,7},{7,5},{8,10},{10,8},{9,1... | collective-permute-start | bytes 1179656 | tf_op jit(solution)/shard_map/ppermute | solution.py:107
  20.2 1.5 collective-permute-start.9
  21.7 8.3 %collective-permute-done.1.refs_4_ = bf16[128,1536]{1,0:T(8,128)(2,1)S(1)} collective-permute-done((bf16[128,1536]{1,0:T(8,128)(2,1)S(1)}, bf16[128,1536]{1,0:T(8,128)(2,1)S(1)}, u32[]{:S(2)}, u32[]{:S(2)}) %collective-permute-start.1) | collective-permute-done | bytes 393248 | tf_op jit(solution)/shard_map/ppermute | solution.py:107
  30.0 7.7 %collective-permute-start.2 = (bf16[136,1536]{1,0:T(8,128)(2,1)}, bf16[136,1536]{1,0:T(8,128)(2,1)}, u32[]{:S(2)}, u32[]{:S(2)}) collective-permute-start(bf16[136,1536]{1,0:T(8,128)(2,1)} %copy-done.2), channel_id=1, source_target_pairs={{0,8},{4,12},{8,0},{12,4},{1,9},{5,13},{9,1},{13,5},{2,10},{6,14},... | collective-permute-start | bytes 1253384 | tf_op jit(solution)/shard_map/ppermute | solution.py:107
  37.8 0.9 constant_dynamic-slice_fusion
  38.6 5.2 %collective-permute-start.11 = (bf16[384,768]{1,0:T(8,128)(2,1)}, bf16[384,768]{1,0:T(8,128)(2,1)}, u32[]{:S(2)}, u32[]{:S(2)}) collective-permute-start(bf16[384,768]{1,0:T(8,128)(2,1)} %constant_dynamic-slice_fusion), channel_id=1, source_target_pairs={{0,4},{4,0},{8,12},{12,8},{1,5},{5,1},{9,13},{13,9},{2,6},{6,2},{1... | collective-permute-start | bytes 1769480 | tf_op jit(solution)/shard_map/ppermute | solution.py:107
  44.0 26.4 %collective-permute-done.2.refs_2_ = bf16[136,1536]{1,0:T(8,128)(2,1)} collective-permute-done((bf16[136,1536]{1,0:T(8,128)(2,1)}, bf16[136,1536]{1,0:T(8,128)(2,1)}, u32[]{:S(2)}, u32[]{:S(2)}) %collective-permute-start.2) | collective-permute-done | bytes 417824 | tf_op jit(solution)/shard_map/ppermute | solution.py:107
  70.4 1.4 collective-permute-start.5
  71.9 0.7 slice_bitcast_fusion.2
  72.6 6.7 %collective-permute-done.5.refs_5_ = bf16[136,1536]{1,0:T(8,128)(2,1)S(1)} collective-permute-done((bf16[136,1536]{1,0:T(8,128)(2,1)}, bf16[136,1536]{1,0:T(8,128)(2,1)S(1)}, u32[]{:S(2)}, u32[]{:S(2)}) %collective-permute-start.5) | collective-permute-done | bytes 417824 | tf_op jit(solution)/shard_map/ppermute | solution.py:107
  79.4 0.8 copy-done.5
  80.1 2.2 %collective-permute-start.6 = (bf16[136,1536]{1,0:T(8,128)(2,1)}, bf16[136,1536]{1,0:T(8,128)(2,1)}, u32[]{:S(2)}, u32[]{:S(2)}) collective-permute-start(bf16[136,1536]{1,0:T(8,128)(2,1)} %collective-permute-done.2.refs_2_), channel_id=1, source_target_pairs={{0,2},{2,0},{1,3},{3,1},{4,6},{6,4},{5,7},{7,5},{8,10},{10,8},{9,1... | collective-permute-start | bytes 1253384 | tf_op jit(solution)/shard_map/ppermute | solution.py:107
  82.4 1.6 collective-permute-start.12
  84.0 0.7 slice_bitcast_fusion.1
  84.7 0.7 slice_bitcast_fusion
  85.4 0.6 gather_fusion
  86.2 0.2 fusion.3
  86.4 0.6 gather_fusion.1
  87.3 10.0 %collective-permute-done.12.refs_11_ = bf16[3,384,384]{2,1,0:T(8,128)(2,1)} collective-permute-done((bf16[3,384,384]{2,1,0:T(8,128)(2,1)}, bf16[3,384,384]{2,1,0:T(8,128)(2,1)}, u32[]{:S(2)}, u32[]{:S(2)}) %collective-permute-start.12) | collective-permute-done | bytes 884768 | tf_op jit(solution)/shard_map/ppermute | solution.py:107
  97.3 0.4 collective-permute-done.7.refs_7_
  97.6 1.0 copy-done.3
  98.6 1.0 copy-done.6
  99.6 5.8 %shard_map.64 = (f32[4,128,256]{2,1,0:T(8,128)S(1)}, f32[4,256,512]{2,1,0:T(8,128)S(1)}, bf16[4,320,512]{2,1,0:T(8,128)(2,1)S(1)}) custom-call(s32[4]{0:T(128)S(1)} %pad_add_fusion.place_ref, bf16[136,1536]{1,0:T(8,128)(2,1)S(1)} %copy-done.3, bf16[136,1536]{1,0:T(8,128)(2,1)} %collective-permute-done.refs_1_, ...), custom_call_target="tpu_custom_call" | custom-call | flops 19327352832 | bytes 8053063 | tf_op jit(solution)/shard_map/pallas_call | solution.py:170
  105.5 1.6 collective-permute-start.18
  107.1 4.6 %shard_map.65 = (f32[4,128,128]{2,1,0:T(8,128)S(1)}, f32[4,256,256]{2,1,0:T(8,128)S(1)}, bf16[4,320,256]{2,1,0:T(8,128)(2,1)S(1)}) custom-call(s32[4]{0:T(128)S(1)} %pad_add_fusion.place_ref, bf16[136,1536]{1,0:T(8,128)(2,1)S(1)} %copy-done.4, bf16[136,1536]{1,0:T(8,128)(2,1)} %collective-permute-done.refs_1_, ...), custom_call_target="tpu_custom_call" | custom-call | flops 9663676416 | bytes 4026531 | tf_op jit(solution)/shard_map/pallas_call | solution.py:170
  111.8 0.2 collective-permute-start.13
  112.0 0.3 collective-permute-start.19
  112.3 3.8 %shard_map.66 = (bf16[2,128,256]{2,1,0:T(8,128)(2,1)S(1)}, bf16[2,128,256]{2,1,0:T(8,128)(2,1)S(1)}) custom-call(s32[4]{0:T(128)S(1)} %pad_add_fusion.place_ref, s32[16]{0:T(128)S(1)} %reshape.24.members_ref, s32[4]{0:T(128)S(1)} %slice_reduce_fusion.1.counts_ref, f32[4,128,256]{2,1,0:T(8,128)S(1)} %get-tuple-element.44.q_ref, ...), custom_call_target="tpu_custom_call" | custom-call | flops 268435456 | bytes 2097152 | tf_op jit(solution)/shard_map/pallas_call | solution.py:115
  116.1 5.3 %collective-permute-done.18.refs_7_ = bf16[384,768]{1,0:T(8,128)(2,1)S(1)} collective-permute-done((bf16[384,768]{1,0:T(8,128)(2,1)}, bf16[384,768]{1,0:T(8,128)(2,1)S(1)}, u32[]{:S(2)}, u32[]{:S(2)}) %collective-permute-start.18) | collective-permute-done | bytes 589856 | tf_op jit(solution)/shard_map/ppermute | solution.py:107
  121.5 2.2 %shard_map.67 = (bf16[2,128,384]{2,1,0:T(8,128)(2,1)S(1)}, bf16[2,128,384]{2,1,0:T(8,128)(2,1)S(1)}) custom-call(s32[4]{0:T(128)S(1)} %pad_add_fusion.place_ref, s32[16]{0:T(128)S(1)} %reshape.24.members_ref, s32[4]{0:T(128)S(1)} %slice_reduce_fusion.1.counts_ref, f32[4,128,128]{2,1,0:T(8,128)S(1)} %get-tuple-element.41.q_ref, ...), custom_call_target="tpu_custom_call" | custom-call | flops 134217728 | bytes 1048576 | tf_op jit(solution)/shard_map/pallas_call | solution.py:115
  123.7 6.1 %collective-permute-start.15 = (bf16[2,128,384]{2,1,0:T(8,128)(2,1)S(1)}, bf16[2,128,384]{2,1,0:T(8,128)(2,1)S(1)}, u32[]{:S(2)}, u32[]{:S(2)}) collective-permute-start(bf16[2,128,384]{2,1,0:T(8,128)(2,1)S(1)} %get-tuple-element.49), channel_id=1, source_target_pairs={{0,4},{4,0},{8,12},{12,8},{1,5},{5,1},{9,13},{13,9},{2,6},{6,2},{1... | collective-permute-start | bytes 589832 | tf_op jit(solution)/shard_map/ppermute | solution.py:107
  129.8 2.4 %collective-permute-start.17 = (bf16[2,128,384]{2,1,0:T(8,128)(2,1)S(1)}, bf16[2,128,384]{2,1,0:T(8,128)(2,1)S(1)}, u32[]{:S(2)}, u32[]{:S(2)}) collective-permute-start(bf16[2,128,384]{2,1,0:T(8,128)(2,1)S(1)} %get-tuple-element.49), channel_id=1, source_target_pairs={{0,12},{4,8},{8,4},{12,0},{1,13},{5,9},{9,5},{13,1},{2,14},{6,10},... | collective-permute-start | bytes 589832 | tf_op jit(solution)/shard_map/ppermute | solution.py:107
  132.3 5.3 %collective-permute-done.15.refs_1_ = bf16[2,128,384]{2,1,0:T(8,128)(2,1)S(1)} collective-permute-done((bf16[2,128,384]{2,1,0:T(8,128)(2,1)S(1)}, bf16[2,128,384]{2,1,0:T(8,128)(2,1)S(1)}, u32[]{:S(2)}, u32[]{:S(2)}) %collective-permute-start.15) | collective-permute-done | bytes 196640 | tf_op jit(solution)/shard_map/ppermute | solution.py:107
  137.5 9.4 %collective-permute-done.16.refs_2_ = bf16[2,128,384]{2,1,0:T(8,128)(2,1)S(1)} collective-permute-done((bf16[2,128,384]{2,1,0:T(8,128)(2,1)S(1)}, bf16[2,128,384]{2,1,0:T(8,128)(2,1)S(1)}, u32[]{:S(2)}, u32[]{:S(2)}) %collective-permute-start.16) | collective-permute-done | bytes 196640 | tf_op jit(solution)/shard_map/ppermute | solution.py:107
  146.9 3.5 %shard_map.68 = (f32[2,64,768]{2,1,0:T(8,128)S(1)}, bf16[2,64,768]{2,1,0:T(8,128)(2,1)S(1)}, f32[2,64,768]{2,1,0:T(8,128)S(1)}, bf16[2,64,768]{2,1,0:T(8,128)(2,1)S(1)}) custom-call(s32[4]{0:T(128)S(1)} %pad_add_fusion.place_ref, bf16[2,128,384]{2,1,0:T(8,128)(2,1)S(1)} %get-tuple-element.48.refs_0_, ...), custom_call_target="tpu_custom_call" | custom-call | flops 1207959552 | bytes 4718592 | tf_op jit(solution)/shard_map/pallas_call | solution.py:115
  150.5 0.8 collective-permute-start.21
  151.2 5.0 %collective-permute-done.21 = bf16[2,64,768]{2,1,0:T(8,128)(2,1)S(1)} collective-permute-done((bf16[2,64,768]{2,1,0:T(8,128)(2,1)S(1)}, bf16[2,64,768]{2,1,0:T(8,128)(2,1)S(1)}, u32[]{:S(2)}, u32[]{:S(2)}) %collective-permute-start.21) | collective-permute-done | bytes 196640 | tf_op jit(solution)/shard_map/ppermute | solution.py:107
  156.3 3.7 %collective-permute-start.23 = (bf16[2,64,768]{2,1,0:T(8,128)(2,1)S(1)}, bf16[2,64,768]{2,1,0:T(8,128)(2,1)S(1)}, u32[]{:S(2)}, u32[]{:S(2)}) collective-permute-start(bf16[2,64,768]{2,1,0:T(8,128)(2,1)S(1)} %add_convert_fusion), channel_id=1, source_target_pairs={{0,8},{4,12},{8,0},{12,4},{1,9},{5,13},{9,1},{13,5},{2,10},{6,14},... | collective-permute-start | bytes 589832 | tf_op jit(solution)/shard_map/ppermute | solution.py:107
  160.0 0.6 collective-permute-start.22
  160.6 7.3 %collective-permute-done.23.far_ref = bf16[2,64,768]{2,1,0:T(8,128)(2,1)S(1)} collective-permute-done((bf16[2,64,768]{2,1,0:T(8,128)(2,1)S(1)}, bf16[2,64,768]{2,1,0:T(8,128)(2,1)S(1)}, u32[]{:S(2)}, u32[]{:S(2)}) %collective-permute-start.23) | collective-permute-done | bytes 196640 | tf_op jit(solution)/shard_map/ppermute | solution.py:107
  167.8 1.3 shard_map.69
  (53 shorter events, 1.5 us)
Async XLA Ops:
  0.0 2.3 %copy-start = (bf16[1,128,3072]{2,1,0:T(8,128)(2,1)S(1)}, bf16[1,128,3072]{2,1,0:T(8,128)(2,1)}, u32[]{:S(2)}) copy-start(bf16[1,128,3072]{2,1,0:T(8,128)(2,1)} %param.6) | copy-start | bytes 2359300
  2.3 3.2 %copy-start.8 = (bf16[128,1536]{1,0:T(8,128)(2,1)}, bf16[128,1536]{1,0:T(8,128)(2,1)S(1)}, u32[]{:S(2)}) copy-start(bf16[128,1536]{1,0:T(8,128)(2,1)S(1)} %dynamic-slice_bitcast_fusion.2) | copy-start | bytes 1179652
  2.5 5.8 %copy-start.2 = (bf16[136,1536]{1,0:T(8,128)(2,1)}, bf16[136,1536]{1,0:T(8,128)(2,1)S(1)}, u32[]{:S(2)}) copy-start(bf16[136,1536]{1,0:T(8,128)(2,1)S(1)} %fusion.1.refs_0_) | copy-start | bytes 1253380
  2.5 16.0 %collective-permute-start = (bf16[136,1536]{1,0:T(8,128)(2,1)S(1)}, bf16[136,1536]{1,0:T(8,128)(2,1)}, u32[]{:S(2)}, u32[]{:S(2)}) collective-permute-start(bf16[136,1536]{1,0:T(8,128)(2,1)S(1)} %fusion.1.refs_0_), channel_id=1, source_target_pairs={{0,4},{4,0},{8,12},{12,8},{1,5},{5,1},{9,13},{13,9},{2,6},{6,2},{1... | collective-permute-start | bytes 1253384 | tf_op jit(solution)/shard_map/ppermute | solution.py:107
  5.6 12.9 %copy-start.1 = (bf16[768,768]{1,0:T(8,128)(2,1)S(1)}, bf16[768,768]{1,0:T(8,128)(2,1)}, u32[]{:S(2)}) copy-start(bf16[768,768]{1,0:T(8,128)(2,1)} %refs_4_.1) | copy-start | bytes 3538948
  5.6 12.9 %copy-start.9 = (bf16[128,1536]{1,0:T(8,128)(2,1)S(1)}, bf16[128,1536]{1,0:T(8,128)(2,1)}, u32[]{:S(2)}) copy-start(bf16[128,1536]{1,0:T(8,128)(2,1)} %copy-done.8) | copy-start | bytes 1179652
  8.2 12.0 %collective-permute-start.8 = (bf16[3,384,384]{2,1,0:T(8,128)(2,1)S(1)}, bf16[3,384,384]{2,1,0:T(8,128)(2,1)}, u32[]{:S(2)}, u32[]{:S(2)}) collective-permute-start(bf16[3,384,384]{2,1,0:T(8,128)(2,1)S(1)} %get-tuple-element.58), channel_id=1, source_target_pairs={{0,0},{1,8},{4,4},{5,12},{8,1},{9,9},{12,5},{13,13},{2,2},{3,10},{... | collective-permute-start | bytes 2654216 | tf_op jit(solution)/shard_map/ppermute | solution.py:338
  18.5 53.4 %collective-permute-start.3 = (bf16[768,768]{1,0:T(8,128)(2,1)S(1)}, bf16[768,768]{1,0:T(8,128)(2,1)S(1)}, u32[]{:S(2)}, u32[]{:S(2)}) collective-permute-start(bf16[768,768]{1,0:T(8,128)(2,1)S(1)} %copy-done.1), channel_id=1, source_target_pairs={{0,1},{1,0},{2,3},{3,2},{4,5},{5,4},{6,7},{7,6},{8,9},{9,8},{10,11... | collective-permute-start | bytes 3538952 | tf_op jit(solution)/shard_map/ppermute | solution.py:107
  18.5 11.5 %collective-permute-start.1 = (bf16[128,1536]{1,0:T(8,128)(2,1)S(1)}, bf16[128,1536]{1,0:T(8,128)(2,1)S(1)}, u32[]{:S(2)}, u32[]{:S(2)}) collective-permute-start(bf16[128,1536]{1,0:T(8,128)(2,1)S(1)} %copy-done.9), channel_id=1, source_target_pairs={{0,2},{2,0},{1,3},{3,1},{4,6},{6,4},{5,7},{7,5},{8,10},{10,8},{9,1... | collective-permute-start | bytes 1179656 | tf_op jit(solution)/shard_map/ppermute | solution.py:107
  20.2 62.1 %collective-permute-start.10 = (bf16[3,384,384]{2,1,0:T(8,128)(2,1)}, bf16[3,384,384]{2,1,0:T(8,128)(2,1)}, u32[]{:S(2)}, u32[]{:S(2)}) collective-permute-start(bf16[3,384,384]{2,1,0:T(8,128)(2,1)} %get-tuple-element.35), channel_id=1, source_target_pairs={{0,4},{1,12},{4,0},{5,8},{8,5},{9,13},{12,1},{13,9},{2,6},{3,14},{... | collective-permute-start | bytes 2654216 | tf_op jit(solution)/shard_map/ppermute | solution.py:338
  20.2 62.1 %collective-permute-start.9 = (bf16[3,384,384]{2,1,0:T(8,128)(2,1)}, bf16[3,384,384]{2,1,0:T(8,128)(2,1)}, u32[]{:S(2)}, u32[]{:S(2)}) collective-permute-start(bf16[3,384,384]{2,1,0:T(8,128)(2,1)} %collective-permute-done.8.refs_8_), channel_id=1, source_target_pairs={{0,16},{16,0},{1,17},{17,1},{2,18},{18,2},{3,19},{19,3},{4,20},{20... | collective-permute-start | bytes 2654216 | tf_op jit(solution)/shard_map/ppermute | solution.py:107
  30.0 40.4 %collective-permute-start.2 = (bf16[136,1536]{1,0:T(8,128)(2,1)}, bf16[136,1536]{1,0:T(8,128)(2,1)}, u32[]{:S(2)}, u32[]{:S(2)}) collective-permute-start(bf16[136,1536]{1,0:T(8,128)(2,1)} %copy-done.2), channel_id=1, source_target_pairs={{0,8},{4,12},{8,0},{12,4},{1,9},{5,13},{9,1},{13,5},{2,10},{6,14},... | collective-permute-start | bytes 1253384 | tf_op jit(solution)/shard_map/ppermute | solution.py:107
  38.6 43.7 %collective-permute-start.11 = (bf16[384,768]{1,0:T(8,128)(2,1)}, bf16[384,768]{1,0:T(8,128)(2,1)}, u32[]{:S(2)}, u32[]{:S(2)}) collective-permute-start(bf16[384,768]{1,0:T(8,128)(2,1)} %constant_dynamic-slice_fusion), channel_id=1, source_target_pairs={{0,4},{4,0},{8,12},{12,8},{1,5},{5,1},{9,13},{13,9},{2,6},{6,2},{1... | collective-permute-start | bytes 1769480 | tf_op jit(solution)/shard_map/ppermute | solution.py:107
  70.4 9.0 %collective-permute-start.5 = (bf16[136,1536]{1,0:T(8,128)(2,1)}, bf16[136,1536]{1,0:T(8,128)(2,1)S(1)}, u32[]{:S(2)}, u32[]{:S(2)}) collective-permute-start(bf16[136,1536]{1,0:T(8,128)(2,1)} %collective-permute-done.refs_1_), channel_id=1, source_target_pairs={{0,2},{2,0},{1,3},{3,1},{4,6},{6,4},{5,7},{7,5},{8,10},{10,8},{9,1... | collective-permute-start | bytes 1253384 | tf_op jit(solution)/shard_map/ppermute | solution.py:107
  71.9 12.8 %collective-permute-start.4 = (bf16[136,1536]{1,0:T(8,128)(2,1)}, bf16[136,1536]{1,0:T(8,128)(2,1)}, u32[]{:S(2)}, u32[]{:S(2)}) collective-permute-start(bf16[136,1536]{1,0:T(8,128)(2,1)} %copy-done.2), channel_id=1, source_target_pairs={{0,12},{4,8},{8,4},{12,0},{1,13},{5,9},{9,5},{13,1},{2,14},{6,10},... | collective-permute-start | bytes 1253384 | tf_op jit(solution)/shard_map/ppermute | solution.py:107
  79.4 0.8 copy-start.5
  80.1 17.1 %collective-permute-start.6 = (bf16[136,1536]{1,0:T(8,128)(2,1)}, bf16[136,1536]{1,0:T(8,128)(2,1)}, u32[]{:S(2)}, u32[]{:S(2)}) collective-permute-start(bf16[136,1536]{1,0:T(8,128)(2,1)} %collective-permute-done.2.refs_2_), channel_id=1, source_target_pairs={{0,2},{2,0},{1,3},{3,1},{4,6},{6,4},{5,7},{7,5},{8,10},{10,8},{9,1... | collective-permute-start | bytes 1253384 | tf_op jit(solution)/shard_map/ppermute | solution.py:107
  82.4 14.9 %collective-permute-start.12 = (bf16[3,384,384]{2,1,0:T(8,128)(2,1)}, bf16[3,384,384]{2,1,0:T(8,128)(2,1)}, u32[]{:S(2)}, u32[]{:S(2)}) collective-permute-start(bf16[3,384,384]{2,1,0:T(8,128)(2,1)} %collective-permute-done.10.refs_10_), channel_id=1, source_target_pairs={{0,16},{16,0},{1,17},{17,1},{2,18},{18,2},{3,19},{19,3},{4,20},{20... | collective-permute-start | bytes 2654216 | tf_op jit(solution)/shard_map/ppermute | solution.py:107
  84.6 13.0 %collective-permute-start.7 = (bf16[136,1536]{1,0:T(8,128)(2,1)}, bf16[136,1536]{1,0:T(8,128)(2,1)}, u32[]{:S(2)}, u32[]{:S(2)}) collective-permute-start(bf16[136,1536]{1,0:T(8,128)(2,1)} %collective-permute-done.4.refs_3_), channel_id=1, source_target_pairs={{0,2},{2,0},{1,3},{3,1},{4,6},{6,4},{5,7},{7,5},{8,10},{10,8},{9,1... | collective-permute-start | bytes 1253384 | tf_op jit(solution)/shard_map/ppermute | solution.py:107
  97.6 1.0 copy-start.3
  98.6 1.0 copy-start.6
  99.6 7.5 %copy-start.4 = (bf16[136,1536]{1,0:T(8,128)(2,1)S(1)}, bf16[136,1536]{1,0:T(8,128)(2,1)}, u32[]{:S(2)}) copy-start(bf16[136,1536]{1,0:T(8,128)(2,1)} %copy-done.2) | copy-start | bytes 1253380
  99.6 7.5 %copy-start.7 = (bf16[136,1536]{1,0:T(8,128)(2,1)S(1)}, bf16[136,1536]{1,0:T(8,128)(2,1)}, u32[]{:S(2)}) copy-start(bf16[136,1536]{1,0:T(8,128)(2,1)} %copy-done.5) | copy-start | bytes 1253380
  105.5 6.9 %collective-permute-start.14 = (bf16[4,320,512]{2,1,0:T(8,128)(2,1)S(1)}, bf16[4,320,512]{2,1,0:T(8,128)(2,1)S(1)}, u32[]{:S(2)}, u32[]{:S(2)}) collective-permute-start(bf16[4,320,512]{2,1,0:T(8,128)(2,1)S(1)} %get-tuple-element.39), channel_id=1, source_target_pairs={{0,1},{1,0},{2,3},{3,2},{4,5},{5,4},{6,7},{7,6},{8,9},{9,8},{10,11... | collective-permute-start | bytes 3932168 | tf_op jit(solution)/shard_map/ppermute | solution.py:107
  105.5 16.0 %collective-permute-start.18 = (bf16[384,768]{1,0:T(8,128)(2,1)}, bf16[384,768]{1,0:T(8,128)(2,1)S(1)}, u32[]{:S(2)}, u32[]{:S(2)}) collective-permute-start(bf16[384,768]{1,0:T(8,128)(2,1)} %collective-permute-done.11.refs_6_), channel_id=1, source_target_pairs={{0,16},{16,0},{1,17},{17,1},{2,18},{18,2},{3,19},{19,3},{4,20},{20... | collective-permute-start | bytes 1769480 | tf_op jit(solution)/shard_map/ppermute | solution.py:107
  111.8 9.7 %collective-permute-start.13 = (bf16[4,320,256]{2,1,0:T(8,128)(2,1)S(1)}, bf16[4,320,256]{2,1,0:T(8,128)(2,1)S(1)}, u32[]{:S(2)}, u32[]{:S(2)}) collective-permute-start(bf16[4,320,256]{2,1,0:T(8,128)(2,1)S(1)} %get-tuple-element.43), channel_id=1, source_target_pairs={{0,1},{1,0},{2,3},{3,2},{4,5},{5,4},{6,7},{7,6},{8,9},{9,8},{10,11... | collective-permute-start | bytes 1966088 | tf_op jit(solution)/shard_map/ppermute | solution.py:107
  112.0 20.3 %collective-permute-start.19 = (bf16[384,768]{1,0:T(8,128)(2,1)}, bf16[384,768]{1,0:T(8,128)(2,1)S(1)}, u32[]{:S(2)}, u32[]{:S(2)}) collective-permute-start(bf16[384,768]{1,0:T(8,128)(2,1)} %collective-permute-done.11.refs_6_), channel_id=1, source_target_pairs={{0,1},{1,0},{2,3},{3,2},{4,5},{5,4},{6,7},{7,6},{8,9},{9,8},{10,11... | collective-permute-start | bytes 1769480 | tf_op jit(solution)/shard_map/ppermute | solution.py:107
  121.5 25.5 %collective-permute-start.20 = (bf16[384,768]{1,0:T(8,128)(2,1)S(1)}, bf16[384,768]{1,0:T(8,128)(2,1)S(1)}, u32[]{:S(2)}, u32[]{:S(2)}) collective-permute-start(bf16[384,768]{1,0:T(8,128)(2,1)S(1)} %collective-permute-done.18.refs_7_), channel_id=1, source_target_pairs={{0,1},{1,0},{2,3},{3,2},{4,5},{5,4},{6,7},{7,6},{8,9},{9,8},{10,11... | collective-permute-start | bytes 1769480 | tf_op jit(solution)/shard_map/ppermute | solution.py:107
  123.7 13.8 %collective-permute-start.15 = (bf16[2,128,384]{2,1,0:T(8,128)(2,1)S(1)}, bf16[2,128,384]{2,1,0:T(8,128)(2,1)S(1)}, u32[]{:S(2)}, u32[]{:S(2)}) collective-permute-start(bf16[2,128,384]{2,1,0:T(8,128)(2,1)S(1)} %get-tuple-element.49), channel_id=1, source_target_pairs={{0,4},{4,0},{8,12},{12,8},{1,5},{5,1},{9,13},{13,9},{2,6},{6,2},{1... | collective-permute-start | bytes 589832 | tf_op jit(solution)/shard_map/ppermute | solution.py:107
  129.8 17.1 %collective-permute-start.16 = (bf16[2,128,384]{2,1,0:T(8,128)(2,1)S(1)}, bf16[2,128,384]{2,1,0:T(8,128)(2,1)S(1)}, u32[]{:S(2)}, u32[]{:S(2)}) collective-permute-start(bf16[2,128,384]{2,1,0:T(8,128)(2,1)S(1)} %get-tuple-element.48.refs_0_), channel_id=1, source_target_pairs={{0,8},{4,12},{8,0},{12,4},{1,9},{5,13},{9,1},{13,5},{2,10},{6,14},... | collective-permute-start | bytes 589832 | tf_op jit(solution)/shard_map/ppermute | solution.py:107
  129.8 17.1 %collective-permute-start.17 = (bf16[2,128,384]{2,1,0:T(8,128)(2,1)S(1)}, bf16[2,128,384]{2,1,0:T(8,128)(2,1)S(1)}, u32[]{:S(2)}, u32[]{:S(2)}) collective-permute-start(bf16[2,128,384]{2,1,0:T(8,128)(2,1)S(1)} %get-tuple-element.49), channel_id=1, source_target_pairs={{0,12},{4,8},{8,4},{12,0},{1,13},{5,9},{9,5},{13,1},{2,14},{6,10},... | collective-permute-start | bytes 589832 | tf_op jit(solution)/shard_map/ppermute | solution.py:107
  150.5 5.7 %collective-permute-start.21 = (bf16[2,64,768]{2,1,0:T(8,128)(2,1)S(1)}, bf16[2,64,768]{2,1,0:T(8,128)(2,1)S(1)}, u32[]{:S(2)}, u32[]{:S(2)}) collective-permute-start(bf16[2,64,768]{2,1,0:T(8,128)(2,1)S(1)} %get-tuple-element.54), channel_id=1, source_target_pairs={{0,2},{2,0},{1,3},{3,1},{4,6},{6,4},{5,7},{7,5},{8,10},{10,8},{9,1... | collective-permute-start | bytes 589832 | tf_op jit(solution)/shard_map/ppermute | solution.py:107
  156.3 11.6 %collective-permute-start.23 = (bf16[2,64,768]{2,1,0:T(8,128)(2,1)S(1)}, bf16[2,64,768]{2,1,0:T(8,128)(2,1)S(1)}, u32[]{:S(2)}, u32[]{:S(2)}) collective-permute-start(bf16[2,64,768]{2,1,0:T(8,128)(2,1)S(1)} %add_convert_fusion), channel_id=1, source_target_pairs={{0,8},{4,12},{8,0},{12,4},{1,9},{5,13},{9,1},{13,5},{2,10},{6,14},... | collective-permute-start | bytes 589832 | tf_op jit(solution)/shard_map/ppermute | solution.py:107
  160.0 7.9 %collective-permute-start.22 = (bf16[2,64,768]{2,1,0:T(8,128)(2,1)S(1)}, bf16[2,64,768]{2,1,0:T(8,128)(2,1)S(1)}, u32[]{:S(2)}, u32[]{:S(2)}) collective-permute-start(bf16[2,64,768]{2,1,0:T(8,128)(2,1)S(1)} %get-tuple-element.55), channel_id=1, source_target_pairs={{0,2},{2,0},{1,3},{3,1},{4,6},{6,4},{5,7},{7,5},{8,10},{10,8},{9,1... | collective-permute-start | bytes 589832 | tf_op jit(solution)/shard_map/ppermute | solution.py:107

commit v18 on v17

--- a/solution.py
+++ b/solution.py
@@ -127,16 +127,16 @@
     )(*prefetch, *operands)
 
 
-def project(place, mine, theirs, chunks, first, cols):
-    rows, (count, width) = len(mine), theirs[0].shape
+def project(place, mine, theirs, chunks, first, cols, weight):
+    rows, (count, width) = len(mine) - 1, theirs[0].shape
     half = chunks[0][0].shape[1]
     slices = len(chunks)
     flat = [w for of_round in chunks for w in of_round]
-    fetched = 2 * rows + len(flat)
+    fetched = 2 * len(mine) + len(flat)
 
     def kernel(place_ref, *refs):
         row, group, frame, core = (place_ref[i] for i in range(4))
-        w_refs = refs[2 * rows : fetched]
+        w_refs = refs[2 * len(mine) : fetched]
         q_keep, kv_keep, send, x_all, w_all, total, sems = refs[fetched:]
         copies = []
         for k in range(slices):
@@ -146,11 +146,20 @@
                     source = w_refs[2 * k + g].at[part, :, first : first + cols]
                     into = w_all.at[pl.ds(at, half), part * cols : (part + 1) * cols]
                     copies.append(pltpu.make_async_copy(source, into, sems.at[len(copies)]))
-        for i in range(2 * rows):
-            to = x_all.at[row ^ (i % rows), (frame + i // rows) % 2]
-            copies.append(pltpu.make_async_copy(refs[i].at[pl.ds(0, count)], to, sems.at[len(copies)]))
         for copy in copies:
             copy.start()
+        middle = (row == 1) | (row == 2)
+        for f in range(2):
+            x_refs = refs[f * len(mine) : (f + 1) * len(mine)]
+            for s in range(rows):
+                to, sem = x_all.at[row ^ s, (frame + f) % 2], sems.at[len(copies)]
+                copies.append(pltpu.make_async_copy(x_refs[s].at[pl.ds(0, count)], to, sem))
+                if s < rows - 1:
+                    copies[-1].start()
+                else:
+                    other = pltpu.make_async_copy(x_refs[rows].at[pl.ds(0, count)], to, sem)
+                    pl.when(middle)(copies[-1].start)
+                    pl.when(jnp.logical_not(middle))(other.start)
         for copy in copies:
             copy.wait()
         acc = jnp.dot(x_all[...].reshape(-1, width), w_all[...], preferred_element_type=jnp.float32)
@@ -187,7 +196,7 @@
             ],
         ),
         compiler_params=pltpu.CompilerParams(vmem_limit_bytes=VMEM_BYTES),
-        cost_estimate=pl.CostEstimate(flops=8 * flops, bytes_accessed=flops // 300, transcendentals=0),
+        cost_estimate=pl.CostEstimate(flops=weight * flops, bytes_accessed=flops // 300, transcendentals=0),
     )(place, *mine, *theirs, *flat)
 
 
@@ -326,6 +335,10 @@
     half = depth // 2
     place = jnp.stack([row, group, frame, core]).astype(jnp.int32)
 
+    def over_frames(value, rows):
+        pairs = [(2 * r + f, 2 * r + 1 - f) for r in rows for f in range(2)]
+        return lax.ppermute(value, ("rows", "frames"), pairs)
+
     def reshard(k, *others):
         value = lax.dynamic_slice(
             w_qkv.transpose(1, 0, 2), (0, group * half, (k + row) % span * cols), (3, half, cols)
@@ -344,19 +357,23 @@
     tables = jnp.pad(tables, ((0, 8 - heads_n), (0, span * depth - MAXB - 2))).astype(mine.dtype)
     joined = jnp.concatenate([mine, tables], axis=0)
     near = swap(joined, "rows")
+    in_3 = lax.ppermute(joined, "rows", [(1, 2), (2, 1)])
     near_x = swap(near, "frames")
     across = swap(after(w_out, near), "heads")
     there.append(swap(here[0], "groups"))
     here.append(reshard(1, near))
-    far_2 = swap(after(joined, near, mine_x), "rows", 2)
+    far_2 = swap(after(joined, near, mine_x, near_x), "rows", 2)
     out_half = lax.dynamic_slice_in_dim(w_out, group * cols, cols, axis=0)
     beside = [swap(after(out_half, here[0]), "rows")]
-    there.append(swap(after(here[1], beside[0], there[0]), "groups"))
-    far_2x = swap(after(far_2, near_x), "frames")
-    far_3 = swap(after(joined, far_2, across), "rows", 3)
-    far_3x = swap(far_3, "frames")
-
-    found = jnp.stack([x[count : count + heads_n, : MAXB + 2] for x in (joined, near, far_2, far_3)])
+    in_3x = over_frames(in_3, (1, 2))
+    there.append(swap(after(here[1], beside[0], there[0], across), "groups"))
+    far_2x = swap(after(far_2, in_3x), "frames")
+    out_3 = lax.ppermute(far_2, "rows", [(1, 0), (2, 3)])
+    out_3x = over_frames(out_3, (0, 3))
+
+    extra = jnp.where((row == 1) | (row == 2), in_3[count:], out_3[count:])
+    found = [joined[count:], near[count:], far_2[count:], extra]
+    found = jnp.stack([x[:heads_n, : MAXB + 2] for x in found])
     tables = found.astype(jnp.int32)[row ^ jnp.arange(rows_n)].reshape(rows_n * heads_n, MAXB + 2)
     windows = lax.dynamic_index_in_dim(
         tables[:, MAXB + 1].reshape(rows_n, heads_n), core, axis=1, keepdims=False
@@ -364,19 +381,19 @@
     picked = tables[windows]
     members, counts = picked[:, :MAXB].reshape(-1), picked[:, MAXB]
 
-    pieces = [joined, near, far_2, far_3], [mine_x, near_x, far_2x, far_3x]
+    pieces = [joined, near, far_2, in_3, out_3], [mine_x, near_x, far_2x, in_3x, out_3x]
     chunks = [(here[0], there[0]), (here[1], after(there[1], members, counts))]
     last = cols // (3 * HD) * HD
-    first = project(place, *pieces, chunks, 0, cols - last)
+    first = project(place, *pieces, chunks, 0, cols - last, 8)
     first_more = swap(first[2], "heads")
     beside.append(swap(after(beside[0], there[1]), "groups"))
     chunks[1] = (here[1], after(there[1], first[2]))
-    second = project(place, *pieces, chunks, cols - last, last)
+    second = project(place, *pieces, chunks, cols - last, last, 1)
     second_more = swap(second[2], "heads")
     attended = attend_all(place, members, counts, *first[:2], first_more)
-    beside_across = [swap(part, "heads") for part in (beside[0], after(beside[1], attended[0]))]
     same, diff = attend_all(place, members, counts, *second[:2], second_more, attended)
     attended = [same] + [swap(same if s % 2 == 0 else diff, "rows", s) for s in range(1, rows_n)]
+    beside_across = [swap(part, "heads") for part in (beside[0], after(beside[1], same))]
     near_keep, near_send, far_keep, far_send = mix(place, attended, w_out, across, beside, beside_across)
     far_more = swap(far_send, "frames")
     far = swap((far_keep + far_more.astype(jnp.float32)).astype(jnp.bfloat16), "rows", 2)

time: 170 us -> 184 us (1.082)
  starting transfers between devices: 42 us -> 65.9 us
  waiting for transfers between devices: 92.7 us -> 78.9 us
  local copies, waits for them, and re-layouts: 10.3 us -> 15.8 us
  other arithmetic: 2.7 us -> 0.65 us
    ppermute x2, starting transfers between devices: 1.58 us -> 23.9 us  [reshard(): lax.ppermute(after(value, *others) if others else value, ('rows', 'heads'...]
    ppermute x22 -> x20, waiting for transfers between devices: 92.7 us -> 72.2 us  [swap(): return lax.ppermute(value, axis, [(i, i ^ step) for i in range(peers)])]
    ppermute x0 -> x4, waiting for transfers between devices: none -> 6.67 us  [the longest x1 5.22 us: by_heads(): out_3 = lax.ppermute(far_2, 'rows', [(1, 0), (2, 3)])]
    ppermute x0 -> x4, starting transfers between devices: none -> 5.07 us  [the longest x2 3.11 us: over_frames(): return lax.ppermute(value, ('rows', 'frames'), pairs)]
    unnamed x20 -> x38, local copies, waits for them, and re-layouts: 2.8 us -> 7.32 us
    ppermute x22 -> x20, starting transfers between devices: 40.5 us -> 37 us  [swap(): return lax.ppermute(value, axis, [(i, i ^ step) for i in range(peers)])]
  transfers between devices with their start and end apart: 24 -> 26, of which waited for: 11 -> 11; matrix products, arithmetic and copies ran while one was open for 5% -> 3% of each run, Pallas kernels for 6% -> 6%
where the time goes in v18:
time: 184 us; the launch traced here: 183 us
  waiting for transfers between devices  78.9 us (43%)
  starting transfers between devices  65.9 us (36%)
  Pallas kernels  21.5 us (12%)
  local copies, waits for them, and re-layouts  15.8 us (9%)
    ppermute x20, waiting for transfers between devices, swap(): return lax.ppermute(value, axis, [(i, i ^ step) for i in range(peers)])  72.2 us
    ppermute x20, starting transfers between devices, swap(): return lax.ppermute(value, axis, [(i, i ^ step) for i in range(peers)])  37 us
    ppermute x2, starting transfers between devices, reshard(): lax.ppermute(after(value, *others) if others else value, ('rows', 'heads'...  23.9 us
    pallas_call x4, Pallas kernels, call(): pl.pallas_call(kernel, out_shape=out_shape, grid_spec=pltpu.PrefetchScala...  11.2 us
    pallas_call x2, Pallas kernels, project(): pl.pallas_call(kernel, out_shape=(jax.ShapeDtypeStruct((rows, 2 * BS, col...  10.3 us
    unnamed x38, local copies, waits for them, and re-layouts  7.32 us
    ppermute x1, waiting for transfers between devices, by_heads(): out_3 = lax.ppermute(far_2, 'rows', [(1, 0), (2, 3)])  5.22 us
  transfers between devices with their start and end apart: 26, of which 11 were waited for; matrix products, arithmetic and copies ran while one was open for 3% of the time, Pallas kernels for 6%

profile of v18, /device:TPU:0, one launch (start us, length us, event | category | flops | bytes accessed | tf_op | source)
XLA Modules:
  0.0 183.0 jit_solution(3004371185776387244)
XLA Ops:
  0.0 2.9 %dynamic-slice_bitcast_fusion = (bf16[3,384,384]{2,1,0:T(8,128)(2,1)}, bf16[3,384,384]{2,1,0:T(8,128)(2,1)}) fusion(bf16[768,3,768]{2,0,1:T(8,128)(2,1)} %param.7, s32[]{:T(128)S(6)} %select_n.57, s32[]{:T(128)S(6)} %select_n.61, s32[]{:T(128)S(6)} %select_n.59), kind=kLoop, calls=%fused_computation.2 | loop fusion | bytes 3538956 | tf_op jit(solution)/shard_map/dynamic_slice | solution.py:343
  2.9 1.9 %collective-permute-start.9 = (bf16[3,384,384]{2,1,0:T(8,128)(2,1)}, bf16[3,384,384]{2,1,0:T(8,128)(2,1)S(1)}, u32[]{:S(2)}, u32[]{:S(2)}) collective-permute-start(bf16[3,384,384]{2,1,0:T(8,128)(2,1)} %get-tuple-element.56), channel_id=1, source_target_pairs={{0,0},{1,8},{4,4},{5,12},{8,1},{9,9},{12,5},{13,13},{2,2},{3,10},{... | collective-permute-start | bytes 2654216 | tf_op jit(solution)/shard_map/ppermute | solution.py:351
  5.3 3.1 %collective-permute-start = (bf16[136,1536]{1,0:T(8,128)(2,1)S(1)}, bf16[136,1536]{1,0:T(8,128)(2,1)S(1)}, u32[]{:S(2)}, u32[]{:S(2)}) collective-permute-start(bf16[136,1536]{1,0:T(8,128)(2,1)S(1)} %fusion.1.refs_0_), channel_id=1, source_target_pairs={{0,4},{4,0},{8,12},{12,8},{1,5},{5,1},{9,13},{13,9},{2,6},{6,2},{1... | collective-permute-start | bytes 1253384 | tf_op jit(solution)/shard_map/ppermute | solution.py:107
  8.4 0.7 collective-permute-start.4
  9.1 1.6 collective-permute-start.1
  10.6 10.9 %collective-permute-done.refs_1_ = bf16[136,1536]{1,0:T(8,128)(2,1)S(1)} collective-permute-done((bf16[136,1536]{1,0:T(8,128)(2,1)S(1)}, bf16[136,1536]{1,0:T(8,128)(2,1)S(1)}, u32[]{:S(2)}, u32[]{:S(2)}) %collective-permute-start) | collective-permute-done | bytes 417824 | tf_op jit(solution)/shard_map/ppermute | solution.py:107
  21.5 6.5 %collective-permute-start.13 = (bf16[768,768]{1,0:T(8,128)(2,1)S(1)}, bf16[768,768]{1,0:T(8,128)(2,1)}, u32[]{:S(2)}, u32[]{:S(2)}) collective-permute-start(bf16[768,768]{1,0:T(8,128)(2,1)S(1)} %copy-done.1), channel_id=1, source_target_pairs={{0,1},{1,0},{2,3},{3,2},{4,5},{5,4},{6,7},{7,6},{8,9},{9,8},{10,11... | collective-permute-start | bytes 3538952 | tf_op jit(solution)/shard_map/ppermute | solution.py:107
  28.1 1.5 collective-permute-start.2
  29.6 0.7 collective-permute-start.6
  30.3 0.7 copy-done.14
  31.0 21.9 %collective-permute-start.11 = (bf16[3,384,384]{2,1,0:T(8,128)(2,1)}, bf16[3,384,384]{2,1,0:T(8,128)(2,1)}, u32[]{:S(2)}, u32[]{:S(2)}) collective-permute-start(bf16[3,384,384]{2,1,0:T(8,128)(2,1)} %get-tuple-element.32), channel_id=1, source_target_pairs={{0,4},{1,12},{4,0},{5,8},{8,5},{9,13},{12,1},{13,9},{2,6},{3,14},{... | collective-permute-start | bytes 2654216 | tf_op jit(solution)/shard_map/ppermute | solution.py:351
  52.9 1.5 collective-permute-start.10
  54.4 0.8 copy-done.8
  55.2 0.8 collective-permute-start.3
  56.0 0.9 constant_dynamic-slice_fusion
  56.8 0.8 copy-done.11
  57.6 5.3 %collective-permute-start.12 = (bf16[384,768]{1,0:T(8,128)(2,1)}, bf16[384,768]{1,0:T(8,128)(2,1)}, u32[]{:S(2)}, u32[]{:S(2)}) collective-permute-start(bf16[384,768]{1,0:T(8,128)(2,1)} %constant_dynamic-slice_fusion), channel_id=1, source_target_pairs={{0,4},{4,0},{8,12},{12,8},{1,5},{5,1},{9,13},{13,9},{2,6},{6,2},{1... | collective-permute-start | bytes 1769480 | tf_op jit(solution)/shard_map/ppermute | solution.py:107
  63.2 0.7 slice.43
  64.0 19.0 %collective-permute-done.3.refs_2_ = bf16[136,1536]{1,0:T(8,128)(2,1)} collective-permute-done((bf16[136,1536]{1,0:T(8,128)(2,1)S(1)}, bf16[136,1536]{1,0:T(8,128)(2,1)}, u32[]{:S(2)}, u32[]{:S(2)}) %collective-permute-start.3) | collective-permute-done | bytes 417824 | tf_op jit(solution)/shard_map/ppermute | solution.py:107
  83.0 1.3 collective-permute-start.5
  84.3 0.7 slice_bitcast_fusion.1
  85.5 1.9 %collective-permute-done.12.refs_6_ = bf16[384,768]{1,0:T(8,128)(2,1)} collective-permute-done((bf16[384,768]{1,0:T(8,128)(2,1)}, bf16[384,768]{1,0:T(8,128)(2,1)}, u32[]{:S(2)}, u32[]{:S(2)}) %collective-permute-start.12) | collective-permute-done | bytes 589856 | tf_op jit(solution)/shard_map/ppermute | solution.py:107
  87.4 1.5 collective-permute-start.14
  88.9 0.7 slice_bitcast_fusion
  89.6 5.2 %collective-permute-done.5.refs_4_ = bf16[136,1536]{1,0:T(8,128)(2,1)} collective-permute-done((bf16[136,1536]{1,0:T(8,128)(2,1)}, bf16[136,1536]{1,0:T(8,128)(2,1)}, u32[]{:S(2)}, u32[]{:S(2)}) %collective-permute-start.5) | collective-permute-done | bytes 417824 | tf_op jit(solution)/shard_map/ppermute | solution.py:371
  94.8 0.7 slice.44
  95.5 2.4 %collective-permute-start.8 = (bf16[136,1536]{1,0:T(8,128)(2,1)}, bf16[136,1536]{1,0:T(8,128)(2,1)}, u32[]{:S(2)}, u32[]{:S(2)}) collective-permute-start(bf16[136,1536]{1,0:T(8,128)(2,1)} %collective-permute-done.5.refs_4_), channel_id=1, source_target_pairs={{0,2},{2,0},{12,14},{14,12},{1,3},{3,1},{13,15},{15,13},{16,18},{1... | collective-permute-start | bytes 1253384 | tf_op jit(solution)/shard_map/ppermute | solution.py:340
  99.9 5.1 %collective-permute-done.14.refs_13_ = bf16[3,384,384]{2,1,0:T(8,128)(2,1)} collective-permute-done((bf16[3,384,384]{2,1,0:T(8,128)(2,1)}, bf16[3,384,384]{2,1,0:T(8,128)(2,1)}, u32[]{:S(2)}, u32[]{:S(2)}) %collective-permute-start.14) | collective-permute-done | bytes 884768 | tf_op jit(solution)/shard_map/ppermute | solution.py:107
  105.0 1.4 collective-permute-done.8.refs_9_
  106.4 1.0 copy-done.3
  107.4 1.0 copy-done.6
  108.4 1.0 copy-done.9
  109.4 1.0 copy-done.12
  110.4 1.0 copy-done.15
  111.4 5.6 %shard_map.64 = (f32[4,128,256]{2,1,0:T(8,128)S(1)}, f32[4,256,512]{2,1,0:T(8,128)S(1)}, bf16[4,320,512]{2,1,0:T(8,128)(2,1)S(1)}) custom-call(s32[4]{0:T(128)S(1)} %pad_add_fusion.place_ref, bf16[136,1536]{1,0:T(8,128)(2,1)S(1)} %fusion.1.refs_0_, bf16[136,1536]{1,0:T(8,128)(2,1)S(1)} %copy-done.6, bf16[136,1536]{1,0:T(8,128)(2,1)} %collective-permute-done.3.refs_2_, ...), custom_call_target="tpu_custom_call" | custom-call | flops 19327352832 | bytes 8053063 | tf_op jit(solution)/shard_map/pallas_call | solution.py:179
  117.2 4.7 %shard_map.65 = (f32[4,128,128]{2,1,0:T(8,128)S(1)}, f32[4,256,256]{2,1,0:T(8,128)S(1)}, bf16[4,320,256]{2,1,0:T(8,128)(2,1)S(1)}) custom-call(s32[4]{0:T(128)S(1)} %pad_add_fusion.place_ref, bf16[136,1536]{1,0:T(8,128)(2,1)S(1)} %fusion.1.refs_0_, bf16[136,1536]{1,0:T(8,128)(2,1)S(1)} %copy-done.7, bf16[136,1536]{1,0:T(8,128)(2,1)} %collective-permute-done.3.refs_2_, ...), custom_call_target="tpu_custom_call" | custom-call | flops 1207959552 | bytes 4026531 | tf_op jit(solution)/shard_map/pallas_call | solution.py:179
  122.4 1.5 collective-permute-start.20
  123.9 3.8 %shard_map.66 = (bf16[2,128,256]{2,1,0:T(8,128)(2,1)S(1)}, bf16[2,128,256]{2,1,0:T(8,128)(2,1)S(1)}) custom-call(s32[4]{0:T(128)S(1)} %pad_add_fusion.place_ref, s32[16]{0:T(128)S(1)} %reshape.24.members_ref, s32[4]{0:T(128)S(1)} %slice_reduce_fusion.1.counts_ref, f32[4,128,256]{2,1,0:T(8,128)S(1)} %get-tuple-element.42.q_ref, ...), custom_call_target="tpu_custom_call" | custom-call | flops 268435456 | bytes 2097152 | tf_op jit(solution)/shard_map/pallas_call | solution.py:115
  127.7 2.2 %shard_map.67 = (bf16[2,128,384]{2,1,0:T(8,128)(2,1)S(1)}, bf16[2,128,384]{2,1,0:T(8,128)(2,1)S(1)}) custom-call(s32[4]{0:T(128)S(1)} %pad_add_fusion.place_ref, s32[16]{0:T(128)S(1)} %reshape.24.members_ref, s32[4]{0:T(128)S(1)} %slice_reduce_fusion.1.counts_ref, f32[4,128,128]{2,1,0:T(8,128)S(1)} %get-tuple-element.39.q_ref, ...), custom_call_target="tpu_custom_call" | custom-call | flops 134217728 | bytes 1048576 | tf_op jit(solution)/shard_map/pallas_call | solution.py:115
  129.9 8.0 %collective-permute-done.20.refs_7_ = bf16[384,768]{1,0:T(8,128)(2,1)S(1)} collective-permute-done((bf16[384,768]{1,0:T(8,128)(2,1)}, bf16[384,768]{1,0:T(8,128)(2,1)S(1)}, u32[]{:S(2)}, u32[]{:S(2)}) %collective-permute-start.20) | collective-permute-done | bytes 589856 | tf_op jit(solution)/shard_map/ppermute | solution.py:107
  138.2 5.3 %collective-permute-start.18 = (bf16[2,128,384]{2,1,0:T(8,128)(2,1)S(1)}, bf16[2,128,384]{2,1,0:T(8,128)(2,1)S(1)}, u32[]{:S(2)}, u32[]{:S(2)}) collective-permute-start(bf16[2,128,384]{2,1,0:T(8,128)(2,1)S(1)} %get-tuple-element.46.refs_0_), channel_id=1, source_target_pairs={{0,8},{4,12},{8,0},{12,4},{1,9},{5,13},{9,1},{13,5},{2,10},{6,14},... | collective-permute-start | bytes 589832 | tf_op jit(solution)/shard_map/ppermute | solution.py:107
  143.5 5.6 %collective-permute-done.17.refs_1_ = bf16[2,128,384]{2,1,0:T(8,128)(2,1)S(1)} collective-permute-done((bf16[2,128,384]{2,1,0:T(8,128)(2,1)S(1)}, bf16[2,128,384]{2,1,0:T(8,128)(2,1)S(1)}, u32[]{:S(2)}, u32[]{:S(2)}) %collective-permute-start.17) | collective-permute-done | bytes 196640 | tf_op jit(solution)/shard_map/ppermute | solution.py:107
  149.1 8.6 %collective-permute-done.18.refs_2_ = bf16[2,128,384]{2,1,0:T(8,128)(2,1)S(1)} collective-permute-done((bf16[2,128,384]{2,1,0:T(8,128)(2,1)S(1)}, bf16[2,128,384]{2,1,0:T(8,128)(2,1)S(1)}, u32[]{:S(2)}, u32[]{:S(2)}) %collective-permute-start.18) | collective-permute-done | bytes 196640 | tf_op jit(solution)/shard_map/ppermute | solution.py:107
  157.7 3.9 %shard_map.68 = (f32[2,64,768]{2,1,0:T(8,128)S(1)}, bf16[2,64,768]{2,1,0:T(8,128)(2,1)S(1)}, f32[2,64,768]{2,1,0:T(8,128)S(1)}, bf16[2,64,768]{2,1,0:T(8,128)(2,1)S(1)}) custom-call(s32[4]{0:T(128)S(1)} %pad_add_fusion.place_ref, bf16[2,128,384]{2,1,0:T(8,128)(2,1)S(1)} %get-tuple-element.46.refs_0_, ...), custom_call_target="tpu_custom_call" | custom-call | flops 1207959552 | bytes 4718592 | tf_op jit(solution)/shard_map/pallas_call | solution.py:115
  162.2 5.5 %collective-permute-done.23 = bf16[2,64,768]{2,1,0:T(8,128)(2,1)S(1)} collective-permute-done((bf16[2,64,768]{2,1,0:T(8,128)(2,1)S(1)}, bf16[2,64,768]{2,1,0:T(8,128)(2,1)S(1)}, u32[]{:S(2)}, u32[]{:S(2)}) %collective-permute-start.23) | collective-permute-done | bytes 196640 | tf_op jit(solution)/shard_map/ppermute | solution.py:107
  167.7 5.8 %collective-permute-start.25 = (bf16[2,64,768]{2,1,0:T(8,128)(2,1)S(1)}, bf16[2,64,768]{2,1,0:T(8,128)(2,1)S(1)}, u32[]{:S(2)}, u32[]{:S(2)}) collective-permute-start(bf16[2,64,768]{2,1,0:T(8,128)(2,1)S(1)} %add_convert_fusion), channel_id=1, source_target_pairs={{0,8},{4,12},{8,0},{12,4},{1,9},{5,13},{9,1},{13,5},{2,10},{6,14},... | collective-permute-start | bytes 589832 | tf_op jit(solution)/shard_map/ppermute | solution.py:107
  174.1 7.6 %collective-permute-done.25.far_ref = bf16[2,64,768]{2,1,0:T(8,128)(2,1)S(1)} collective-permute-done((bf16[2,64,768]{2,1,0:T(8,128)(2,1)S(1)}, bf16[2,64,768]{2,1,0:T(8,128)(2,1)S(1)}, u32[]{:S(2)}, u32[]{:S(2)}) %collective-permute-start.25) | collective-permute-done | bytes 196640 | tf_op jit(solution)/shard_map/ppermute | solution.py:107
  181.7 1.3 shard_map.69
  (77 shorter events, 5.3 us)
Async XLA Ops:
  0.0 5.1 %copy-start = (bf16[1,128,3072]{2,1,0:T(8,128)(2,1)S(1)}, bf16[1,128,3072]{2,1,0:T(8,128)(2,1)}, u32[]{:S(2)}) copy-start(bf16[1,128,3072]{2,1,0:T(8,128)(2,1)} %param.6) | copy-start | bytes 2359300
  0.0 4.9 %copy-start.17 = (s32[2]{0:T(128)S(1)}, s32[2]{0:T(128)}, u32[]{:S(2)}) copy-start(s32[2]{0:T(128)} %param.11) | copy-start | bytes 28
  0.0 5.0 %copy-start.18 = (s32[2]{0:T(128)S(1)}, s32[2]{0:T(128)}, u32[]{:S(2)}) copy-start(s32[2]{0:T(128)} %param.10) | copy-start | bytes 28
  0.0 5.1 %copy-start.16 = (s32[2,4]{1,0:T(2,128)S(1)}, s32[2,4]{1,0:T(2,128)}, u32[]{:S(2)}) copy-start(s32[2,4]{1,0:T(2,128)} %param.9) | copy-start | bytes 100
  2.9 18.6 %copy-start.1 = (bf16[768,768]{1,0:T(8,128)(2,1)S(1)}, bf16[768,768]{1,0:T(8,128)(2,1)}, u32[]{:S(2)}) copy-start(bf16[768,768]{1,0:T(8,128)(2,1)} %refs_4_.1) | copy-start | bytes 3538948
  2.9 50.0 %collective-permute-start.9 = (bf16[3,384,384]{2,1,0:T(8,128)(2,1)}, bf16[3,384,384]{2,1,0:T(8,128)(2,1)S(1)}, u32[]{:S(2)}, u32[]{:S(2)}) collective-permute-start(bf16[3,384,384]{2,1,0:T(8,128)(2,1)} %get-tuple-element.56), channel_id=1, source_target_pairs={{0,0},{1,8},{4,4},{5,12},{8,1},{9,9},{12,5},{13,13},{2,2},{3,10},{... | collective-permute-start | bytes 2654216 | tf_op jit(solution)/shard_map/ppermute | solution.py:351
  5.3 16.2 %collective-permute-start = (bf16[136,1536]{1,0:T(8,128)(2,1)S(1)}, bf16[136,1536]{1,0:T(8,128)(2,1)S(1)}, u32[]{:S(2)}, u32[]{:S(2)}) collective-permute-start(bf16[136,1536]{1,0:T(8,128)(2,1)S(1)} %fusion.1.refs_0_), channel_id=1, source_target_pairs={{0,4},{4,0},{8,12},{12,8},{1,5},{5,1},{9,13},{13,9},{2,6},{6,2},{1... | collective-permute-start | bytes 1253384 | tf_op jit(solution)/shard_map/ppermute | solution.py:107
  8.4 21.2 %collective-permute-start.4 = (bf16[136,1536]{1,0:T(8,128)(2,1)S(1)}, bf16[136,1536]{1,0:T(8,128)(2,1)S(1)}, u32[]{:S(2)}, u32[]{:S(2)}) collective-permute-start(bf16[136,1536]{1,0:T(8,128)(2,1)S(1)} %fusion.1.refs_0_), channel_id=1, source_target_pairs={{4,8},{8,4},{5,9},{9,5},{6,10},{10,6},{7,11},{11,7},{20,24},{24,20... | collective-permute-start | bytes 1253384 | tf_op jit(solution)/shard_map/ppermute | solution.py:360
  9.1 21.2 %collective-permute-start.1 = (bf16[128,1536]{1,0:T(8,128)(2,1)S(1)}, bf16[128,1536]{1,0:T(8,128)(2,1)S(1)}, u32[]{:S(2)}, u32[]{:S(2)}) collective-permute-start(bf16[128,1536]{1,0:T(8,128)(2,1)S(1)} %dynamic-slice_bitcast_fusion.2), channel_id=1, source_target_pairs={{0,2},{2,0},{1,3},{3,1},{4,6},{6,4},{5,7},{7,5},{8,10},{10,8},{9,1... | collective-permute-start | bytes 1179656 | tf_op jit(solution)/shard_map/ppermute | solution.py:107
  21.5 32.9 %copy-start.5 = (bf16[136,1536]{1,0:T(8,128)(2,1)}, bf16[136,1536]{1,0:T(8,128)(2,1)S(1)}, u32[]{:S(2)}) copy-start(bf16[136,1536]{1,0:T(8,128)(2,1)S(1)} %collective-permute-done.refs_1_) | copy-start | bytes 1253380
  21.5 65.8 %collective-permute-start.13 = (bf16[768,768]{1,0:T(8,128)(2,1)S(1)}, bf16[768,768]{1,0:T(8,128)(2,1)}, u32[]{:S(2)}, u32[]{:S(2)}) collective-permute-start(bf16[768,768]{1,0:T(8,128)(2,1)S(1)} %copy-done.1), channel_id=1, source_target_pairs={{0,1},{1,0},{2,3},{3,2},{4,5},{5,4},{6,7},{7,6},{8,9},{9,8},{10,11... | collective-permute-start | bytes 3538952 | tf_op jit(solution)/shard_map/ppermute | solution.py:107
  28.1 26.4 %collective-permute-start.2 = (bf16[136,1536]{1,0:T(8,128)(2,1)S(1)}, bf16[136,1536]{1,0:T(8,128)(2,1)S(1)}, u32[]{:S(2)}, u32[]{:S(2)}) collective-permute-start(bf16[136,1536]{1,0:T(8,128)(2,1)S(1)} %collective-permute-done.refs_1_), channel_id=1, source_target_pairs={{0,2},{2,0},{1,3},{3,1},{4,6},{6,4},{5,7},{7,5},{8,10},{10,8},{9,1... | collective-permute-start | bytes 1253384 | tf_op jit(solution)/shard_map/ppermute | solution.py:107
  29.6 24.9 %copy-start.2 = (bf16[136,1536]{1,0:T(8,128)(2,1)}, bf16[136,1536]{1,0:T(8,128)(2,1)S(1)}, u32[]{:S(2)}) copy-start(bf16[136,1536]{1,0:T(8,128)(2,1)S(1)} %collective-permute-done.4.refs_3_) | copy-start | bytes 1253380
  29.6 27.3 %collective-permute-start.6 = (bf16[136,1536]{1,0:T(8,128)(2,1)S(1)}, bf16[136,1536]{1,0:T(8,128)(2,1)S(1)}, u32[]{:S(2)}, u32[]{:S(2)}) collective-permute-start(bf16[136,1536]{1,0:T(8,128)(2,1)S(1)} %collective-permute-done.4.refs_3_), channel_id=1, source_target_pairs={{4,6},{6,4},{8,10},{10,8},{5,7},{7,5},{9,11},{11,9},{20,22},{22,20... | collective-permute-start | bytes 1253384 | tf_op jit(solution)/shard_map/ppermute | solution.py:340
  30.2 0.7 copy-start.14
  31.0 53.9 %collective-permute-start.11 = (bf16[3,384,384]{2,1,0:T(8,128)(2,1)}, bf16[3,384,384]{2,1,0:T(8,128)(2,1)}, u32[]{:S(2)}, u32[]{:S(2)}) collective-permute-start(bf16[3,384,384]{2,1,0:T(8,128)(2,1)} %get-tuple-element.32), channel_id=1, source_target_pairs={{0,4},{1,12},{4,0},{5,8},{8,5},{9,13},{12,1},{13,9},{2,6},{3,14},{... | collective-permute-start | bytes 2654216 | tf_op jit(solution)/shard_map/ppermute | solution.py:351
  52.9 34.5 %collective-permute-start.10 = (bf16[3,384,384]{2,1,0:T(8,128)(2,1)S(1)}, bf16[3,384,384]{2,1,0:T(8,128)(2,1)}, u32[]{:S(2)}, u32[]{:S(2)}) collective-permute-start(bf16[3,384,384]{2,1,0:T(8,128)(2,1)S(1)} %collective-permute-done.9.refs_10_), channel_id=1, source_target_pairs={{0,16},{16,0},{1,17},{17,1},{2,18},{18,2},{3,19},{19,3},{4,20},{20... | collective-permute-start | bytes 2654216 | tf_op jit(solution)/shard_map/ppermute | solution.py:107
  54.4 0.8 copy-start.8
  55.2 27.8 %collective-permute-start.3 = (bf16[136,1536]{1,0:T(8,128)(2,1)S(1)}, bf16[136,1536]{1,0:T(8,128)(2,1)}, u32[]{:S(2)}, u32[]{:S(2)}) collective-permute-start(bf16[136,1536]{1,0:T(8,128)(2,1)S(1)} %fusion.1.refs_0_), channel_id=1, source_target_pairs={{0,8},{4,12},{8,0},{12,4},{1,9},{5,13},{9,1},{13,5},{2,10},{6,14},... | collective-permute-start | bytes 1253384 | tf_op jit(solution)/shard_map/ppermute | solution.py:107
  56.8 0.8 copy-start.11
  57.6 29.8 %collective-permute-start.12 = (bf16[384,768]{1,0:T(8,128)(2,1)}, bf16[384,768]{1,0:T(8,128)(2,1)}, u32[]{:S(2)}, u32[]{:S(2)}) collective-permute-start(bf16[384,768]{1,0:T(8,128)(2,1)} %constant_dynamic-slice_fusion), channel_id=1, source_target_pairs={{0,4},{4,0},{8,12},{12,8},{1,5},{5,1},{9,13},{13,9},{2,6},{6,2},{1... | collective-permute-start | bytes 1769480 | tf_op jit(solution)/shard_map/ppermute | solution.py:107
  83.0 11.8 %collective-permute-start.5 = (bf16[136,1536]{1,0:T(8,128)(2,1)}, bf16[136,1536]{1,0:T(8,128)(2,1)}, u32[]{:S(2)}, u32[]{:S(2)}) collective-permute-start(bf16[136,1536]{1,0:T(8,128)(2,1)} %collective-permute-done.3.refs_2_), channel_id=1, source_target_pairs={{4,0},{8,12},{5,1},{9,13},{6,2},{10,14},{7,3},{11,15},{20,16},{24,... | collective-permute-start | bytes 1253384 | tf_op jit(solution)/shard_map/ppermute | solution.py:371
  84.9 20.0 %collective-permute-start.7 = (bf16[136,1536]{1,0:T(8,128)(2,1)}, bf16[136,1536]{1,0:T(8,128)(2,1)}, u32[]{:S(2)}, u32[]{:S(2)}) collective-permute-start(bf16[136,1536]{1,0:T(8,128)(2,1)} %collective-permute-done.3.refs_2_), channel_id=1, source_target_pairs={{0,2},{2,0},{1,3},{3,1},{4,6},{6,4},{5,7},{7,5},{8,10},{10,8},{9,1... | collective-permute-start | bytes 1253384 | tf_op jit(solution)/shard_map/ppermute | solution.py:107
  87.4 17.6 %collective-permute-start.14 = (bf16[3,384,384]{2,1,0:T(8,128)(2,1)}, bf16[3,384,384]{2,1,0:T(8,128)(2,1)}, u32[]{:S(2)}, u32[]{:S(2)}) collective-permute-start(bf16[3,384,384]{2,1,0:T(8,128)(2,1)} %collective-permute-done.11.refs_12_), channel_id=1, source_target_pairs={{0,16},{16,0},{1,17},{17,1},{2,18},{18,2},{3,19},{19,3},{4,20},{20... | collective-permute-start | bytes 2654216 | tf_op jit(solution)/shard_map/ppermute | solution.py:107
  95.5 10.9 %collective-permute-start.8 = (bf16[136,1536]{1,0:T(8,128)(2,1)}, bf16[136,1536]{1,0:T(8,128)(2,1)}, u32[]{:S(2)}, u32[]{:S(2)}) collective-permute-start(bf16[136,1536]{1,0:T(8,128)(2,1)} %collective-permute-done.5.refs_4_), channel_id=1, source_target_pairs={{0,2},{2,0},{12,14},{14,12},{1,3},{3,1},{13,15},{15,13},{16,18},{1... | collective-permute-start | bytes 1253384 | tf_op jit(solution)/shard_map/ppermute | solution.py:340
  106.4 1.0 copy-start.3
  107.4 1.0 copy-start.6
  108.4 1.0 copy-start.9
  109.4 1.0 copy-start.12
  110.4 1.0 copy-start.15
  111.4 5.7 %copy-start.4 = (bf16[136,1536]{1,0:T(8,128)(2,1)S(1)}, bf16[136,1536]{1,0:T(8,128)(2,1)}, u32[]{:S(2)}) copy-start(bf16[136,1536]{1,0:T(8,128)(2,1)} %copy-done.2) | copy-start | bytes 1253380
  111.4 5.7 %copy-start.7 = (bf16[136,1536]{1,0:T(8,128)(2,1)S(1)}, bf16[136,1536]{1,0:T(8,128)(2,1)}, u32[]{:S(2)}) copy-start(bf16[136,1536]{1,0:T(8,128)(2,1)} %copy-done.5) | copy-start | bytes 1253380
  111.4 5.7 %copy-start.10 = (bf16[136,1536]{1,0:T(8,128)(2,1)S(1)}, bf16[136,1536]{1,0:T(8,128)(2,1)}, u32[]{:S(2)}) copy-start(bf16[136,1536]{1,0:T(8,128)(2,1)} %copy-done.8) | copy-start | bytes 1253380
  111.4 5.7 %copy-start.13 = (bf16[136,1536]{1,0:T(8,128)(2,1)S(1)}, bf16[136,1536]{1,0:T(8,128)(2,1)}, u32[]{:S(2)}) copy-start(bf16[136,1536]{1,0:T(8,128)(2,1)} %copy-done.11) | copy-start | bytes 1253380
  117.0 6.8 %collective-permute-start.16 = (bf16[4,320,512]{2,1,0:T(8,128)(2,1)S(1)}, bf16[4,320,512]{2,1,0:T(8,128)(2,1)S(1)}, u32[]{:S(2)}, u32[]{:S(2)}) collective-permute-start(bf16[4,320,512]{2,1,0:T(8,128)(2,1)S(1)} %get-tuple-element.37), channel_id=1, source_target_pairs={{0,1},{1,0},{2,3},{3,2},{4,5},{5,4},{6,7},{7,6},{8,9},{9,8},{10,11... | collective-permute-start | bytes 3932168 | tf_op jit(solution)/shard_map/ppermute | solution.py:107
  121.8 5.8 %collective-permute-start.15 = (bf16[4,320,256]{2,1,0:T(8,128)(2,1)S(1)}, bf16[4,320,256]{2,1,0:T(8,128)(2,1)S(1)}, u32[]{:S(2)}, u32[]{:S(2)}) collective-permute-start(bf16[4,320,256]{2,1,0:T(8,128)(2,1)S(1)} %get-tuple-element.41), channel_id=1, source_target_pairs={{0,1},{1,0},{2,3},{3,2},{4,5},{5,4},{6,7},{7,6},{8,9},{9,8},{10,11... | collective-permute-start | bytes 1966088 | tf_op jit(solution)/shard_map/ppermute | solution.py:107
  122.4 15.5 %collective-permute-start.20 = (bf16[384,768]{1,0:T(8,128)(2,1)}, bf16[384,768]{1,0:T(8,128)(2,1)S(1)}, u32[]{:S(2)}, u32[]{:S(2)}) collective-permute-start(bf16[384,768]{1,0:T(8,128)(2,1)} %collective-permute-done.12.refs_6_), channel_id=1, source_target_pairs={{0,16},{16,0},{1,17},{17,1},{2,18},{18,2},{3,19},{19,3},{4,20},{20... | collective-permute-start | bytes 1769480 | tf_op jit(solution)/shard_map/ppermute | solution.py:107
  123.9 19.7 %collective-permute-start.21 = (bf16[384,768]{1,0:T(8,128)(2,1)}, bf16[384,768]{1,0:T(8,128)(2,1)S(1)}, u32[]{:S(2)}, u32[]{:S(2)}) collective-permute-start(bf16[384,768]{1,0:T(8,128)(2,1)} %collective-permute-done.12.refs_6_), channel_id=1, source_target_pairs={{0,1},{1,0},{2,3},{3,2},{4,5},{5,4},{6,7},{7,6},{8,9},{9,8},{10,11... | collective-permute-start | bytes 1769480 | tf_op jit(solution)/shard_map/ppermute | solution.py:107
  137.9 19.8 %collective-permute-start.22 = (bf16[384,768]{1,0:T(8,128)(2,1)S(1)}, bf16[384,768]{1,0:T(8,128)(2,1)S(1)}, u32[]{:S(2)}, u32[]{:S(2)}) collective-permute-start(bf16[384,768]{1,0:T(8,128)(2,1)S(1)} %collective-permute-done.20.refs_7_), channel_id=1, source_target_pairs={{0,1},{1,0},{2,3},{3,2},{4,5},{5,4},{6,7},{7,6},{8,9},{9,8},{10,11... | collective-permute-start | bytes 1769480 | tf_op jit(solution)/shard_map/ppermute | solution.py:107
  137.9 11.2 %collective-permute-start.17 = (bf16[2,128,384]{2,1,0:T(8,128)(2,1)S(1)}, bf16[2,128,384]{2,1,0:T(8,128)(2,1)S(1)}, u32[]{:S(2)}, u32[]{:S(2)}) collective-permute-start(bf16[2,128,384]{2,1,0:T(8,128)(2,1)S(1)} %get-tuple-element.47), channel_id=1, source_target_pairs={{0,4},{4,0},{8,12},{12,8},{1,5},{5,1},{9,13},{13,9},{2,6},{6,2},{1... | collective-permute-start | bytes 589832 | tf_op jit(solution)/shard_map/ppermute | solution.py:107
  138.2 19.4 %collective-permute-start.18 = (bf16[2,128,384]{2,1,0:T(8,128)(2,1)S(1)}, bf16[2,128,384]{2,1,0:T(8,128)(2,1)S(1)}, u32[]{:S(2)}, u32[]{:S(2)}) collective-permute-start(bf16[2,128,384]{2,1,0:T(8,128)(2,1)S(1)} %get-tuple-element.46.refs_0_), channel_id=1, source_target_pairs={{0,8},{4,12},{8,0},{12,4},{1,9},{5,13},{9,1},{13,5},{2,10},{6,14},... | collective-permute-start | bytes 589832 | tf_op jit(solution)/shard_map/ppermute | solution.py:107
  143.5 14.1 %collective-permute-start.19 = (bf16[2,128,384]{2,1,0:T(8,128)(2,1)S(1)}, bf16[2,128,384]{2,1,0:T(8,128)(2,1)S(1)}, u32[]{:S(2)}, u32[]{:S(2)}) collective-permute-start(bf16[2,128,384]{2,1,0:T(8,128)(2,1)S(1)} %get-tuple-element.47), channel_id=1, source_target_pairs={{0,12},{4,8},{8,4},{12,0},{1,13},{5,9},{9,5},{13,1},{2,14},{6,10},... | collective-permute-start | bytes 589832 | tf_op jit(solution)/shard_map/ppermute | solution.py:107
  161.6 6.1 %collective-permute-start.23 = (bf16[2,64,768]{2,1,0:T(8,128)(2,1)S(1)}, bf16[2,64,768]{2,1,0:T(8,128)(2,1)S(1)}, u32[]{:S(2)}, u32[]{:S(2)}) collective-permute-start(bf16[2,64,768]{2,1,0:T(8,128)(2,1)S(1)} %get-tuple-element.52), channel_id=1, source_target_pairs={{0,2},{2,0},{1,3},{3,1},{4,6},{6,4},{5,7},{7,5},{8,10},{10,8},{9,1... | collective-permute-start | bytes 589832 | tf_op jit(solution)/shard_map/ppermute | solution.py:107
  167.7 13.9 %collective-permute-start.25 = (bf16[2,64,768]{2,1,0:T(8,128)(2,1)S(1)}, bf16[2,64,768]{2,1,0:T(8,128)(2,1)S(1)}, u32[]{:S(2)}, u32[]{:S(2)}) collective-permute-start(bf16[2,64,768]{2,1,0:T(8,128)(2,1)S(1)} %add_convert_fusion), channel_id=1, source_target_pairs={{0,8},{4,12},{8,0},{12,4},{1,9},{5,13},{9,1},{13,5},{2,10},{6,14},... | collective-permute-start | bytes 589832 | tf_op jit(solution)/shard_map/ppermute | solution.py:107
  173.6 8.1 %collective-permute-start.24 = (bf16[2,64,768]{2,1,0:T(8,128)(2,1)S(1)}, bf16[2,64,768]{2,1,0:T(8,128)(2,1)S(1)}, u32[]{:S(2)}, u32[]{:S(2)}) collective-permute-start(bf16[2,64,768]{2,1,0:T(8,128)(2,1)S(1)} %get-tuple-element.53), channel_id=1, source_target_pairs={{0,2},{2,0},{1,3},{3,1},{4,6},{6,4},{5,7},{7,5},{8,10},{10,8},{9,1... | collective-permute-start | bytes 589832 | tf_op jit(solution)/shard_map/ppermute | solution.py:107

commit v19 on v17

--- a/solution.py
+++ b/solution.py
@@ -348,12 +348,13 @@
     across = swap(after(w_out, near), "heads")
     there.append(swap(here[0], "groups"))
     here.append(reshard(1, near))
-    far_2 = swap(after(joined, near, mine_x), "rows", 2)
+    far_2 = swap(after(joined, here[0], mine_x), "rows", 2)
     out_half = lax.dynamic_slice_in_dim(w_out, group * cols, cols, axis=0)
-    beside = [swap(after(out_half, here[0]), "rows")]
-    there.append(swap(after(here[1], beside[0], there[0]), "groups"))
-    far_2x = swap(after(far_2, near_x), "frames")
-    far_3 = swap(after(joined, far_2, across), "rows", 3)
+    beside = [swap(after(out_half, near), "rows")]
+    beside.append(swap(beside[0], "groups"))
+    there.append(swap(after(here[1], there[0], beside[1]), "groups"))
+    far_2x = swap(far_2, "frames")
+    far_3 = swap(after(joined, far_2, across, near_x, beside[0]), "rows", 3)
     far_3x = swap(far_3, "frames")
 
     found = jnp.stack([x[count : count + heads_n, : MAXB + 2] for x in (joined, near, far_2, far_3)])
@@ -369,12 +370,11 @@
     last = cols // (3 * HD) * HD
     first = project(place, *pieces, chunks, 0, cols - last)
     first_more = swap(first[2], "heads")
-    beside.append(swap(after(beside[0], there[1]), "groups"))
     chunks[1] = (here[1], after(there[1], first[2]))
     second = project(place, *pieces, chunks, cols - last, last)
     second_more = swap(second[2], "heads")
     attended = attend_all(place, members, counts, *first[:2], first_more)
-    beside_across = [swap(part, "heads") for part in (beside[0], after(beside[1], attended[0]))]
+    beside_across = [swap(part, "heads") for part in beside]
     same, diff = attend_all(place, members, counts, *second[:2], second_more, attended)
     attended = [same] + [swap(same if s % 2 == 0 else diff, "rows", s) for s in range(1, rows_n)]
     near_keep, near_send, far_keep, far_send = mix(place, attended, w_out, across, beside, beside_across)

time: 170 us -> 161 us (0.947)
  starting transfers between devices: 42 us -> 33 us
    ppermute x22, starting transfers between devices: 40.5 us -> 31.4 us  [swap(): return lax.ppermute(value, axis, [(i, i ^ step) for i in range(peers)])]
  transfers between devices with their start and end apart: 24 -> 24, of which waited for: 11 -> 11; matrix products, arithmetic and copies ran while one was open for 5% -> 4% of each run, Pallas kernels for 6% -> 7%
where the time goes in v19:
time: 161 us; the launch traced here: 160 us
  waiting for transfers between devices  93.4 us (58%)
  starting transfers between devices  33 us (20%)
  Pallas kernels  21.4 us (13%)
  local copies, waits for them, and re-layouts  9.51 us (6%)
  other arithmetic  2.7 us (2%)
    ppermute x22, waiting for transfers between devices, swap(): return lax.ppermute(value, axis, [(i, i ^ step) for i in range(peers)])  93.4 us
    ppermute x22, starting transfers between devices, swap(): return lax.ppermute(value, axis, [(i, i ^ step) for i in range(peers)])  31.4 us
    pallas_call x4, Pallas kernels, call(): pl.pallas_call(kernel, out_shape=out_shape, grid_spec=pltpu.PrefetchScala...  11 us
    pallas_call x2, Pallas kernels, project(): pl.pallas_call(kernel, out_shape=(jax.ShapeDtypeStruct((rows, 2 * BS, col...  10.4 us
  transfers between devices with their start and end apart: 24, of which 11 were waited for; matrix products, arithmetic and copies ran while one was open for 4% of the time, Pallas kernels for 7%

profile of v19, /device:TPU:0, one launch (start us, length us, event | category | flops | bytes accessed | tf_op | source)
XLA Modules:
  0.0 160.2 jit_solution(13345635161621881806)
XLA Ops:
  0.0 0.7 convert_bitcast_fusion
  0.8 0.7 convert_bitcast_fusion.1
  1.6 0.7 convert.13
  2.5 3.1 %collective-permute-start = (bf16[136,1536]{1,0:T(8,128)(2,1)S(1)}, bf16[136,1536]{1,0:T(8,128)(2,1)}, u32[]{:S(2)}, u32[]{:S(2)}) collective-permute-start(bf16[136,1536]{1,0:T(8,128)(2,1)S(1)} %fusion.1.refs_0_), channel_id=1, source_target_pairs={{0,4},{4,0},{8,12},{12,8},{1,5},{5,1},{9,13},{13,9},{2,6},{6,2},{1... | collective-permute-start | bytes 1253384 | tf_op jit(solution)/shard_map/ppermute | solution.py:107
  5.6 2.7 %dynamic-slice_bitcast_fusion = (bf16[3,384,384]{2,1,0:T(8,128)(2,1)}, bf16[3,384,384]{2,1,0:T(8,128)(2,1)S(1)}) fusion(bf16[768,3,768]{2,0,1:T(8,128)(2,1)} %param.7, s32[]{:T(128)S(6)} %select_n.44, s32[]{:T(128)S(6)} %select_n.51, s32[]{:T(128)S(6)} %select_n.46), kind=kLoop, calls=%fused_computation.2 | loop fusion | bytes 3538956 | tf_op jit(solution)/shard_map/dynamic_slice | solution.py:330
  8.2 1.6 collective-permute-start.1
  9.8 8.7 %collective-permute-done.refs_1_ = bf16[136,1536]{1,0:T(8,128)(2,1)} collective-permute-done((bf16[136,1536]{1,0:T(8,128)(2,1)S(1)}, bf16[136,1536]{1,0:T(8,128)(2,1)}, u32[]{:S(2)}, u32[]{:S(2)}) %collective-permute-start) | collective-permute-done | bytes 417824 | tf_op jit(solution)/shard_map/ppermute | solution.py:107
  18.5 1.7 %collective-permute-start.2 = (bf16[128,1536]{1,0:T(8,128)(2,1)S(1)}, bf16[128,1536]{1,0:T(8,128)(2,1)S(1)}, u32[]{:S(2)}, u32[]{:S(2)}) collective-permute-start(bf16[128,1536]{1,0:T(8,128)(2,1)S(1)} %copy-done.9), channel_id=1, source_target_pairs={{0,2},{2,0},{1,3},{3,1},{4,6},{6,4},{5,7},{7,5},{8,10},{10,8},{9,1... | collective-permute-start | bytes 1179656 | tf_op jit(solution)/shard_map/ppermute | solution.py:107
  20.3 0.4 collective-permute-start.5
  20.8 9.7 %collective-permute-done.2.refs_4_ = bf16[128,1536]{1,0:T(8,128)(2,1)S(1)} collective-permute-done((bf16[128,1536]{1,0:T(8,128)(2,1)S(1)}, bf16[128,1536]{1,0:T(8,128)(2,1)S(1)}, u32[]{:S(2)}, u32[]{:S(2)}) %collective-permute-start.2) | collective-permute-done | bytes 393248 | tf_op jit(solution)/shard_map/ppermute | solution.py:107
  30.5 1.7 %collective-permute-start.10 = (bf16[3,384,384]{2,1,0:T(8,128)(2,1)}, bf16[3,384,384]{2,1,0:T(8,128)(2,1)}, u32[]{:S(2)}, u32[]{:S(2)}) collective-permute-start(bf16[3,384,384]{2,1,0:T(8,128)(2,1)} %collective-permute-done.1.refs_8_), channel_id=1, source_target_pairs={{0,16},{16,0},{1,17},{17,1},{2,18},{18,2},{3,19},{19,3},{4,20},{20... | collective-permute-start | bytes 2654216 | tf_op jit(solution)/shard_map/ppermute | solution.py:107
  32.2 6.8 %collective-permute-done.5.refs_5_ = bf16[136,1536]{1,0:T(8,128)(2,1)S(1)} collective-permute-done((bf16[136,1536]{1,0:T(8,128)(2,1)}, bf16[136,1536]{1,0:T(8,128)(2,1)S(1)}, u32[]{:S(2)}, u32[]{:S(2)}) %collective-permute-start.5) | collective-permute-done | bytes 417824 | tf_op jit(solution)/shard_map/ppermute | solution.py:107
  39.0 0.8 copy-done.5
  39.7 0.7 collective-permute-start.3
  40.4 1.7 %collective-permute-done.6.refs_6_ = bf16[384,768]{1,0:T(8,128)(2,1)} collective-permute-done((bf16[384,768]{1,0:T(8,128)(2,1)S(1)}, bf16[384,768]{1,0:T(8,128)(2,1)}, u32[]{:S(2)}, u32[]{:S(2)}) %collective-permute-start.6) | collective-permute-done | bytes 589856 | tf_op jit(solution)/shard_map/ppermute | solution.py:107
  42.1 1.5 collective-permute-start.12
  43.9 26.5 %collective-permute-done.3.refs_2_ = bf16[136,1536]{1,0:T(8,128)(2,1)} collective-permute-done((bf16[136,1536]{1,0:T(8,128)(2,1)}, bf16[136,1536]{1,0:T(8,128)(2,1)}, u32[]{:S(2)}, u32[]{:S(2)}) %collective-permute-start.3) | collective-permute-done | bytes 417824 | tf_op jit(solution)/shard_map/ppermute | solution.py:107
  70.4 2.4 %collective-permute-start.7 = (bf16[136,1536]{1,0:T(8,128)(2,1)}, bf16[136,1536]{1,0:T(8,128)(2,1)}, u32[]{:S(2)}, u32[]{:S(2)}) collective-permute-start(bf16[136,1536]{1,0:T(8,128)(2,1)} %copy-done.2), channel_id=1, source_target_pairs={{0,12},{4,8},{8,4},{12,0},{1,13},{5,9},{9,5},{13,1},{2,14},{6,10},... | collective-permute-start | bytes 1253384 | tf_op jit(solution)/shard_map/ppermute | solution.py:107
  72.8 0.7 slice_bitcast_fusion.2
  73.4 1.4 collective-permute-start.8
  74.9 1.6 collective-permute-start.13
  76.4 0.7 slice_bitcast_fusion.1
  77.1 6.5 %collective-permute-done.7.refs_3_ = bf16[136,1536]{1,0:T(8,128)(2,1)} collective-permute-done((bf16[136,1536]{1,0:T(8,128)(2,1)}, bf16[136,1536]{1,0:T(8,128)(2,1)}, u32[]{:S(2)}, u32[]{:S(2)}) %collective-permute-start.7) | collective-permute-done | bytes 417824 | tf_op jit(solution)/shard_map/ppermute | solution.py:107
  83.7 1.9 %collective-permute-start.9 = (bf16[136,1536]{1,0:T(8,128)(2,1)}, bf16[136,1536]{1,0:T(8,128)(2,1)}, u32[]{:S(2)}, u32[]{:S(2)}) collective-permute-start(bf16[136,1536]{1,0:T(8,128)(2,1)} %collective-permute-done.7.refs_3_), channel_id=1, source_target_pairs={{0,2},{2,0},{1,3},{3,1},{4,6},{6,4},{5,7},{7,5},{8,10},{10,8},{9,1... | collective-permute-start | bytes 1253384 | tf_op jit(solution)/shard_map/ppermute | solution.py:107
  85.6 0.7 slice_bitcast_fusion
  86.3 0.6 gather_fusion
  87.2 0.2 fusion.3
  87.4 0.6 gather_fusion.1
  88.2 7.6 %collective-permute-done.13.refs_11_ = bf16[3,384,384]{2,1,0:T(8,128)(2,1)} collective-permute-done((bf16[3,384,384]{2,1,0:T(8,128)(2,1)}, bf16[3,384,384]{2,1,0:T(8,128)(2,1)}, u32[]{:S(2)}, u32[]{:S(2)}) %collective-permute-start.13) | collective-permute-done | bytes 884768 | tf_op jit(solution)/shard_map/ppermute | solution.py:107
  95.8 1.0 copy-done.3
  96.8 1.0 copy-done.6
  97.8 5.8 %shard_map.64 = (f32[4,128,256]{2,1,0:T(8,128)S(1)}, f32[4,256,512]{2,1,0:T(8,128)S(1)}, bf16[4,320,512]{2,1,0:T(8,128)(2,1)S(1)}) custom-call(s32[4]{0:T(128)S(1)} %pad_add_fusion.place_ref, bf16[136,1536]{1,0:T(8,128)(2,1)S(1)} %copy-done.3, bf16[136,1536]{1,0:T(8,128)(2,1)} %collective-permute-done.refs_1_, ...), custom_call_target="tpu_custom_call" | custom-call | flops 19327352832 | bytes 8053063 | tf_op jit(solution)/shard_map/pallas_call | solution.py:170
  103.7 4.6 %shard_map.65 = (f32[4,128,128]{2,1,0:T(8,128)S(1)}, f32[4,256,256]{2,1,0:T(8,128)S(1)}, bf16[4,320,256]{2,1,0:T(8,128)(2,1)S(1)}) custom-call(s32[4]{0:T(128)S(1)} %pad_add_fusion.place_ref, bf16[136,1536]{1,0:T(8,128)(2,1)S(1)} %copy-done.4, bf16[136,1536]{1,0:T(8,128)(2,1)} %collective-permute-done.refs_1_, ...), custom_call_target="tpu_custom_call" | custom-call | flops 9663676416 | bytes 4026531 | tf_op jit(solution)/shard_map/pallas_call | solution.py:170
  108.3 0.5 collective-permute-start.14
  109.0 0.4 collective-permute-start.20
  109.4 3.8 %shard_map.66 = (bf16[2,128,256]{2,1,0:T(8,128)(2,1)S(1)}, bf16[2,128,256]{2,1,0:T(8,128)(2,1)S(1)}) custom-call(s32[4]{0:T(128)S(1)} %pad_add_fusion.place_ref, s32[16]{0:T(128)S(1)} %reshape.24.members_ref, s32[4]{0:T(128)S(1)} %slice_reduce_fusion.1.counts_ref, f32[4,128,256]{2,1,0:T(8,128)S(1)} %get-tuple-element.40.q_ref, ...), custom_call_target="tpu_custom_call" | custom-call | flops 268435456 | bytes 2097152 | tf_op jit(solution)/shard_map/pallas_call | solution.py:115
  113.2 2.2 %shard_map.67 = (bf16[2,128,384]{2,1,0:T(8,128)(2,1)S(1)}, bf16[2,128,384]{2,1,0:T(8,128)(2,1)S(1)}) custom-call(s32[4]{0:T(128)S(1)} %pad_add_fusion.place_ref, s32[16]{0:T(128)S(1)} %reshape.24.members_ref, s32[4]{0:T(128)S(1)} %slice_reduce_fusion.1.counts_ref, f32[4,128,128]{2,1,0:T(8,128)S(1)} %get-tuple-element.37.q_ref, ...), custom_call_target="tpu_custom_call" | custom-call | flops 134217728 | bytes 1048576 | tf_op jit(solution)/shard_map/pallas_call | solution.py:115
  115.4 5.9 %collective-permute-start.16 = (bf16[2,128,384]{2,1,0:T(8,128)(2,1)S(1)}, bf16[2,128,384]{2,1,0:T(8,128)(2,1)S(1)}, u32[]{:S(2)}, u32[]{:S(2)}) collective-permute-start(bf16[2,128,384]{2,1,0:T(8,128)(2,1)S(1)} %get-tuple-element.45), channel_id=1, source_target_pairs={{0,4},{4,0},{8,12},{12,8},{1,5},{5,1},{9,13},{13,9},{2,6},{6,2},{1... | collective-permute-start | bytes 589832 | tf_op jit(solution)/shard_map/ppermute | solution.py:107
  121.3 2.4 %collective-permute-start.18 = (bf16[2,128,384]{2,1,0:T(8,128)(2,1)S(1)}, bf16[2,128,384]{2,1,0:T(8,128)(2,1)S(1)}, u32[]{:S(2)}, u32[]{:S(2)}) collective-permute-start(bf16[2,128,384]{2,1,0:T(8,128)(2,1)S(1)} %get-tuple-element.45), channel_id=1, source_target_pairs={{0,12},{4,8},{8,4},{12,0},{1,13},{5,9},{9,5},{13,1},{2,14},{6,10},... | collective-permute-start | bytes 589832 | tf_op jit(solution)/shard_map/ppermute | solution.py:107
  123.7 5.1 %collective-permute-done.16.refs_1_ = bf16[2,128,384]{2,1,0:T(8,128)(2,1)S(1)} collective-permute-done((bf16[2,128,384]{2,1,0:T(8,128)(2,1)S(1)}, bf16[2,128,384]{2,1,0:T(8,128)(2,1)S(1)}, u32[]{:S(2)}, u32[]{:S(2)}) %collective-permute-start.16) | collective-permute-done | bytes 196640 | tf_op jit(solution)/shard_map/ppermute | solution.py:107
  128.8 9.6 %collective-permute-done.17.refs_2_ = bf16[2,128,384]{2,1,0:T(8,128)(2,1)S(1)} collective-permute-done((bf16[2,128,384]{2,1,0:T(8,128)(2,1)S(1)}, bf16[2,128,384]{2,1,0:T(8,128)(2,1)S(1)}, u32[]{:S(2)}, u32[]{:S(2)}) %collective-permute-start.17) | collective-permute-done | bytes 196640 | tf_op jit(solution)/shard_map/ppermute | solution.py:107
  138.4 3.7 %shard_map.68 = (f32[2,64,768]{2,1,0:T(8,128)S(1)}, bf16[2,64,768]{2,1,0:T(8,128)(2,1)S(1)}, f32[2,64,768]{2,1,0:T(8,128)S(1)}, bf16[2,64,768]{2,1,0:T(8,128)(2,1)S(1)}) custom-call(s32[4]{0:T(128)S(1)} %pad_add_fusion.place_ref, bf16[2,128,384]{2,1,0:T(8,128)(2,1)S(1)} %get-tuple-element.44.refs_0_, ...), custom_call_target="tpu_custom_call" | custom-call | flops 1207959552 | bytes 4718592 | tf_op jit(solution)/shard_map/pallas_call | solution.py:115
  142.1 0.6 collective-permute-start.21
  142.7 5.1 %collective-permute-done.21 = bf16[2,64,768]{2,1,0:T(8,128)(2,1)S(1)} collective-permute-done((bf16[2,64,768]{2,1,0:T(8,128)(2,1)S(1)}, bf16[2,64,768]{2,1,0:T(8,128)(2,1)S(1)}, u32[]{:S(2)}, u32[]{:S(2)}) %collective-permute-start.21) | collective-permute-done | bytes 196640 | tf_op jit(solution)/shard_map/ppermute | solution.py:107
  147.9 3.2 %collective-permute-start.23 = (bf16[2,64,768]{2,1,0:T(8,128)(2,1)S(1)}, bf16[2,64,768]{2,1,0:T(8,128)(2,1)S(1)}, u32[]{:S(2)}, u32[]{:S(2)}) collective-permute-start(bf16[2,64,768]{2,1,0:T(8,128)(2,1)S(1)} %add_convert_fusion), channel_id=1, source_target_pairs={{0,8},{4,12},{8,0},{12,4},{1,9},{5,13},{9,1},{13,5},{2,10},{6,14},... | collective-permute-start | bytes 589832 | tf_op jit(solution)/shard_map/ppermute | solution.py:107
  151.0 1.7 %collective-permute-start.22 = (bf16[2,64,768]{2,1,0:T(8,128)(2,1)S(1)}, bf16[2,64,768]{2,1,0:T(8,128)(2,1)S(1)}, u32[]{:S(2)}, u32[]{:S(2)}) collective-permute-start(bf16[2,64,768]{2,1,0:T(8,128)(2,1)S(1)} %get-tuple-element.49), channel_id=1, source_target_pairs={{0,2},{2,0},{1,3},{3,1},{4,6},{6,4},{5,7},{7,5},{8,10},{10,8},{9,1... | collective-permute-start | bytes 589832 | tf_op jit(solution)/shard_map/ppermute | solution.py:107
  152.7 6.2 %collective-permute-done.23.far_ref = bf16[2,64,768]{2,1,0:T(8,128)(2,1)S(1)} collective-permute-done((bf16[2,64,768]{2,1,0:T(8,128)(2,1)S(1)}, bf16[2,64,768]{2,1,0:T(8,128)(2,1)S(1)}, u32[]{:S(2)}, u32[]{:S(2)}) %collective-permute-start.23) | collective-permute-done | bytes 196640 | tf_op jit(solution)/shard_map/ppermute | solution.py:107
  158.9 1.3 shard_map.69
  (53 shorter events, 1.6 us)
Async XLA Ops:
  0.0 2.3 %copy-start = (bf16[1,128,3072]{2,1,0:T(8,128)(2,1)S(1)}, bf16[1,128,3072]{2,1,0:T(8,128)(2,1)}, u32[]{:S(2)}) copy-start(bf16[1,128,3072]{2,1,0:T(8,128)(2,1)} %param.6) | copy-start | bytes 2359300
  2.3 3.2 %copy-start.8 = (bf16[128,1536]{1,0:T(8,128)(2,1)}, bf16[128,1536]{1,0:T(8,128)(2,1)S(1)}, u32[]{:S(2)}) copy-start(bf16[128,1536]{1,0:T(8,128)(2,1)S(1)} %dynamic-slice_bitcast_fusion.2) | copy-start | bytes 1179652
  2.5 5.8 %copy-start.2 = (bf16[136,1536]{1,0:T(8,128)(2,1)}, bf16[136,1536]{1,0:T(8,128)(2,1)S(1)}, u32[]{:S(2)}) copy-start(bf16[136,1536]{1,0:T(8,128)(2,1)S(1)} %fusion.1.refs_0_) | copy-start | bytes 1253380
  2.5 16.0 %collective-permute-start = (bf16[136,1536]{1,0:T(8,128)(2,1)S(1)}, bf16[136,1536]{1,0:T(8,128)(2,1)}, u32[]{:S(2)}, u32[]{:S(2)}) collective-permute-start(bf16[136,1536]{1,0:T(8,128)(2,1)S(1)} %fusion.1.refs_0_), channel_id=1, source_target_pairs={{0,4},{4,0},{8,12},{12,8},{1,5},{5,1},{9,13},{13,9},{2,6},{6,2},{1... | collective-permute-start | bytes 1253384 | tf_op jit(solution)/shard_map/ppermute | solution.py:107
  5.6 12.9 %copy-start.1 = (bf16[768,768]{1,0:T(8,128)(2,1)S(1)}, bf16[768,768]{1,0:T(8,128)(2,1)}, u32[]{:S(2)}) copy-start(bf16[768,768]{1,0:T(8,128)(2,1)} %refs_4_.1) | copy-start | bytes 3538948
  5.6 12.9 %copy-start.9 = (bf16[128,1536]{1,0:T(8,128)(2,1)S(1)}, bf16[128,1536]{1,0:T(8,128)(2,1)}, u32[]{:S(2)}) copy-start(bf16[128,1536]{1,0:T(8,128)(2,1)} %copy-done.8) | copy-start | bytes 1179652
  8.2 22.2 %collective-permute-start.1 = (bf16[3,384,384]{2,1,0:T(8,128)(2,1)S(1)}, bf16[3,384,384]{2,1,0:T(8,128)(2,1)}, u32[]{:S(2)}, u32[]{:S(2)}) collective-permute-start(bf16[3,384,384]{2,1,0:T(8,128)(2,1)S(1)} %get-tuple-element.52), channel_id=1, source_target_pairs={{0,0},{1,8},{4,4},{5,12},{8,1},{9,9},{12,5},{13,13},{2,2},{3,10},{... | collective-permute-start | bytes 2654216 | tf_op jit(solution)/shard_map/ppermute | solution.py:338
  18.5 51.9 %collective-permute-start.4 = (bf16[768,768]{1,0:T(8,128)(2,1)S(1)}, bf16[768,768]{1,0:T(8,128)(2,1)S(1)}, u32[]{:S(2)}, u32[]{:S(2)}) collective-permute-start(bf16[768,768]{1,0:T(8,128)(2,1)S(1)} %copy-done.1), channel_id=1, source_target_pairs={{0,1},{1,0},{2,3},{3,2},{4,5},{5,4},{6,7},{7,6},{8,9},{9,8},{10,11... | collective-permute-start | bytes 3538952 | tf_op jit(solution)/shard_map/ppermute | solution.py:107
  18.5 12.0 %collective-permute-start.2 = (bf16[128,1536]{1,0:T(8,128)(2,1)S(1)}, bf16[128,1536]{1,0:T(8,128)(2,1)S(1)}, u32[]{:S(2)}, u32[]{:S(2)}) collective-permute-start(bf16[128,1536]{1,0:T(8,128)(2,1)S(1)} %copy-done.9), channel_id=1, source_target_pairs={{0,2},{2,0},{1,3},{3,1},{4,6},{6,4},{5,7},{7,5},{8,10},{10,8},{9,1... | collective-permute-start | bytes 1179656 | tf_op jit(solution)/shard_map/ppermute | solution.py:107
  20.2 21.9 %collective-permute-start.6 = (bf16[384,768]{1,0:T(8,128)(2,1)S(1)}, bf16[384,768]{1,0:T(8,128)(2,1)}, u32[]{:S(2)}, u32[]{:S(2)}) collective-permute-start(bf16[384,768]{1,0:T(8,128)(2,1)S(1)} %constant_dynamic-slice_fusion), channel_id=1, source_target_pairs={{0,4},{4,0},{8,12},{12,8},{1,5},{5,1},{9,13},{13,9},{2,6},{6,2},{1... | collective-permute-start | bytes 1769480 | tf_op jit(solution)/shard_map/ppermute | solution.py:107
  20.3 18.6 %collective-permute-start.5 = (bf16[136,1536]{1,0:T(8,128)(2,1)}, bf16[136,1536]{1,0:T(8,128)(2,1)S(1)}, u32[]{:S(2)}, u32[]{:S(2)}) collective-permute-start(bf16[136,1536]{1,0:T(8,128)(2,1)} %collective-permute-done.refs_1_), channel_id=1, source_target_pairs={{0,2},{2,0},{1,3},{3,1},{4,6},{6,4},{5,7},{7,5},{8,10},{10,8},{9,1... | collective-permute-start | bytes 1253384 | tf_op jit(solution)/shard_map/ppermute | solution.py:107
  30.5 44.4 %collective-permute-start.11 = (bf16[3,384,384]{2,1,0:T(8,128)(2,1)}, bf16[3,384,384]{2,1,0:T(8,128)(2,1)}, u32[]{:S(2)}, u32[]{:S(2)}) collective-permute-start(bf16[3,384,384]{2,1,0:T(8,128)(2,1)} %get-tuple-element.32), channel_id=1, source_target_pairs={{0,4},{1,12},{4,0},{5,8},{8,5},{9,13},{12,1},{13,9},{2,6},{3,14},{... | collective-permute-start | bytes 2654216 | tf_op jit(solution)/shard_map/ppermute | solution.py:338
  30.5 44.4 %collective-permute-start.10 = (bf16[3,384,384]{2,1,0:T(8,128)(2,1)}, bf16[3,384,384]{2,1,0:T(8,128)(2,1)}, u32[]{:S(2)}, u32[]{:S(2)}) collective-permute-start(bf16[3,384,384]{2,1,0:T(8,128)(2,1)} %collective-permute-done.1.refs_8_), channel_id=1, source_target_pairs={{0,16},{16,0},{1,17},{17,1},{2,18},{18,2},{3,19},{19,3},{4,20},{20... | collective-permute-start | bytes 2654216 | tf_op jit(solution)/shard_map/ppermute | solution.py:107
  39.0 0.8 copy-start.5
  39.7 30.7 %collective-permute-start.3 = (bf16[136,1536]{1,0:T(8,128)(2,1)}, bf16[136,1536]{1,0:T(8,128)(2,1)}, u32[]{:S(2)}, u32[]{:S(2)}) collective-permute-start(bf16[136,1536]{1,0:T(8,128)(2,1)} %copy-done.2), channel_id=1, source_target_pairs={{0,8},{4,12},{8,0},{12,4},{1,9},{5,13},{9,1},{13,5},{2,10},{6,14},... | collective-permute-start | bytes 1253384 | tf_op jit(solution)/shard_map/ppermute | solution.py:107
  42.1 32.8 %collective-permute-start.12 = (bf16[384,768]{1,0:T(8,128)(2,1)}, bf16[384,768]{1,0:T(8,128)(2,1)}, u32[]{:S(2)}, u32[]{:S(2)}) collective-permute-start(bf16[384,768]{1,0:T(8,128)(2,1)} %collective-permute-done.6.refs_6_), channel_id=1, source_target_pairs={{0,16},{16,0},{1,17},{17,1},{2,18},{18,2},{3,19},{19,3},{4,20},{20... | collective-permute-start | bytes 1769480 | tf_op jit(solution)/shard_map/ppermute | solution.py:107
  70.4 13.3 %collective-permute-start.7 = (bf16[136,1536]{1,0:T(8,128)(2,1)}, bf16[136,1536]{1,0:T(8,128)(2,1)}, u32[]{:S(2)}, u32[]{:S(2)}) collective-permute-start(bf16[136,1536]{1,0:T(8,128)(2,1)} %copy-done.2), channel_id=1, source_target_pairs={{0,12},{4,8},{8,4},{12,0},{1,13},{5,9},{9,5},{13,1},{2,14},{6,10},... | collective-permute-start | bytes 1253384 | tf_op jit(solution)/shard_map/ppermute | solution.py:107
  73.4 22.3 %collective-permute-start.8 = (bf16[136,1536]{1,0:T(8,128)(2,1)}, bf16[136,1536]{1,0:T(8,128)(2,1)}, u32[]{:S(2)}, u32[]{:S(2)}) collective-permute-start(bf16[136,1536]{1,0:T(8,128)(2,1)} %collective-permute-done.3.refs_2_), channel_id=1, source_target_pairs={{0,2},{2,0},{1,3},{3,1},{4,6},{6,4},{5,7},{7,5},{8,10},{10,8},{9,1... | collective-permute-start | bytes 1253384 | tf_op jit(solution)/shard_map/ppermute | solution.py:107
  74.9 20.9 %collective-permute-start.13 = (bf16[3,384,384]{2,1,0:T(8,128)(2,1)}, bf16[3,384,384]{2,1,0:T(8,128)(2,1)}, u32[]{:S(2)}, u32[]{:S(2)}) collective-permute-start(bf16[3,384,384]{2,1,0:T(8,128)(2,1)} %collective-permute-done.11.refs_10_), channel_id=1, source_target_pairs={{0,16},{16,0},{1,17},{17,1},{2,18},{18,2},{3,19},{19,3},{4,20},{20... | collective-permute-start | bytes 2654216 | tf_op jit(solution)/shard_map/ppermute | solution.py:107
  83.7 12.1 %collective-permute-start.9 = (bf16[136,1536]{1,0:T(8,128)(2,1)}, bf16[136,1536]{1,0:T(8,128)(2,1)}, u32[]{:S(2)}, u32[]{:S(2)}) collective-permute-start(bf16[136,1536]{1,0:T(8,128)(2,1)} %collective-permute-done.7.refs_3_), channel_id=1, source_target_pairs={{0,2},{2,0},{1,3},{3,1},{4,6},{6,4},{5,7},{7,5},{8,10},{10,8},{9,1... | collective-permute-start | bytes 1253384 | tf_op jit(solution)/shard_map/ppermute | solution.py:107
  95.8 1.0 copy-start.3
  96.8 1.0 copy-start.6
  97.8 5.9 %copy-start.4 = (bf16[136,1536]{1,0:T(8,128)(2,1)S(1)}, bf16[136,1536]{1,0:T(8,128)(2,1)}, u32[]{:S(2)}) copy-start(bf16[136,1536]{1,0:T(8,128)(2,1)} %copy-done.2) | copy-start | bytes 1253380
  97.8 5.9 %copy-start.7 = (bf16[136,1536]{1,0:T(8,128)(2,1)S(1)}, bf16[136,1536]{1,0:T(8,128)(2,1)}, u32[]{:S(2)}) copy-start(bf16[136,1536]{1,0:T(8,128)(2,1)} %copy-done.5) | copy-start | bytes 1253380
  103.6 5.8 %collective-permute-start.15 = (bf16[4,320,512]{2,1,0:T(8,128)(2,1)S(1)}, bf16[4,320,512]{2,1,0:T(8,128)(2,1)S(1)}, u32[]{:S(2)}, u32[]{:S(2)}) collective-permute-start(bf16[4,320,512]{2,1,0:T(8,128)(2,1)S(1)} %get-tuple-element.35), channel_id=1, source_target_pairs={{0,1},{1,0},{2,3},{3,2},{4,5},{5,4},{6,7},{7,6},{8,9},{9,8},{10,11... | collective-permute-start | bytes 3932168 | tf_op jit(solution)/shard_map/ppermute | solution.py:107
  108.3 4.9 %collective-permute-start.14 = (bf16[4,320,256]{2,1,0:T(8,128)(2,1)S(1)}, bf16[4,320,256]{2,1,0:T(8,128)(2,1)S(1)}, u32[]{:S(2)}, u32[]{:S(2)}) collective-permute-start(bf16[4,320,256]{2,1,0:T(8,128)(2,1)S(1)} %get-tuple-element.39), channel_id=1, source_target_pairs={{0,1},{1,0},{2,3},{3,2},{4,5},{5,4},{6,7},{7,6},{8,9},{9,8},{10,11... | collective-permute-start | bytes 1966088 | tf_op jit(solution)/shard_map/ppermute | solution.py:107
  108.9 14.8 %collective-permute-start.19 = (bf16[384,768]{1,0:T(8,128)(2,1)}, bf16[384,768]{1,0:T(8,128)(2,1)S(1)}, u32[]{:S(2)}, u32[]{:S(2)}) collective-permute-start(bf16[384,768]{1,0:T(8,128)(2,1)} %collective-permute-done.6.refs_6_), channel_id=1, source_target_pairs={{0,1},{1,0},{2,3},{3,2},{4,5},{5,4},{6,7},{7,6},{8,9},{9,8},{10,11... | collective-permute-start | bytes 1769480 | tf_op jit(solution)/shard_map/ppermute | solution.py:107
  109.0 14.7 %collective-permute-start.20 = (bf16[384,768]{1,0:T(8,128)(2,1)}, bf16[384,768]{1,0:T(8,128)(2,1)S(1)}, u32[]{:S(2)}, u32[]{:S(2)}) collective-permute-start(bf16[384,768]{1,0:T(8,128)(2,1)} %collective-permute-done.12.refs_7_), channel_id=1, source_target_pairs={{0,1},{1,0},{2,3},{3,2},{4,5},{5,4},{6,7},{7,6},{8,9},{9,8},{10,11... | collective-permute-start | bytes 1769480 | tf_op jit(solution)/shard_map/ppermute | solution.py:107
  115.4 13.4 %collective-permute-start.16 = (bf16[2,128,384]{2,1,0:T(8,128)(2,1)S(1)}, bf16[2,128,384]{2,1,0:T(8,128)(2,1)S(1)}, u32[]{:S(2)}, u32[]{:S(2)}) collective-permute-start(bf16[2,128,384]{2,1,0:T(8,128)(2,1)S(1)} %get-tuple-element.45), channel_id=1, source_target_pairs={{0,4},{4,0},{8,12},{12,8},{1,5},{5,1},{9,13},{13,9},{2,6},{6,2},{1... | collective-permute-start | bytes 589832 | tf_op jit(solution)/shard_map/ppermute | solution.py:107
  121.3 17.1 %collective-permute-start.17 = (bf16[2,128,384]{2,1,0:T(8,128)(2,1)S(1)}, bf16[2,128,384]{2,1,0:T(8,128)(2,1)S(1)}, u32[]{:S(2)}, u32[]{:S(2)}) collective-permute-start(bf16[2,128,384]{2,1,0:T(8,128)(2,1)S(1)} %get-tuple-element.44.refs_0_), channel_id=1, source_target_pairs={{0,8},{4,12},{8,0},{12,4},{1,9},{5,13},{9,1},{13,5},{2,10},{6,14},... | collective-permute-start | bytes 589832 | tf_op jit(solution)/shard_map/ppermute | solution.py:107
  121.3 17.1 %collective-permute-start.18 = (bf16[2,128,384]{2,1,0:T(8,128)(2,1)S(1)}, bf16[2,128,384]{2,1,0:T(8,128)(2,1)S(1)}, u32[]{:S(2)}, u32[]{:S(2)}) collective-permute-start(bf16[2,128,384]{2,1,0:T(8,128)(2,1)S(1)} %get-tuple-element.45), channel_id=1, source_target_pairs={{0,12},{4,8},{8,4},{12,0},{1,13},{5,9},{9,5},{13,1},{2,14},{6,10},... | collective-permute-start | bytes 589832 | tf_op jit(solution)/shard_map/ppermute | solution.py:107
  142.1 5.7 %collective-permute-start.21 = (bf16[2,64,768]{2,1,0:T(8,128)(2,1)S(1)}, bf16[2,64,768]{2,1,0:T(8,128)(2,1)S(1)}, u32[]{:S(2)}, u32[]{:S(2)}) collective-permute-start(bf16[2,64,768]{2,1,0:T(8,128)(2,1)S(1)} %get-tuple-element.48), channel_id=1, source_target_pairs={{0,2},{2,0},{1,3},{3,1},{4,6},{6,4},{5,7},{7,5},{8,10},{10,8},{9,1... | collective-permute-start | bytes 589832 | tf_op jit(solution)/shard_map/ppermute | solution.py:107
  147.9 11.0 %collective-permute-start.23 = (bf16[2,64,768]{2,1,0:T(8,128)(2,1)S(1)}, bf16[2,64,768]{2,1,0:T(8,128)(2,1)S(1)}, u32[]{:S(2)}, u32[]{:S(2)}) collective-permute-start(bf16[2,64,768]{2,1,0:T(8,128)(2,1)S(1)} %add_convert_fusion), channel_id=1, source_target_pairs={{0,8},{4,12},{8,0},{12,4},{1,9},{5,13},{9,1},{13,5},{2,10},{6,14},... | collective-permute-start | bytes 589832 | tf_op jit(solution)/shard_map/ppermute | solution.py:107
  151.0 7.9 %collective-permute-start.22 = (bf16[2,64,768]{2,1,0:T(8,128)(2,1)S(1)}, bf16[2,64,768]{2,1,0:T(8,128)(2,1)S(1)}, u32[]{:S(2)}, u32[]{:S(2)}) collective-permute-start(bf16[2,64,768]{2,1,0:T(8,128)(2,1)S(1)} %get-tuple-element.49), channel_id=1, source_target_pairs={{0,2},{2,0},{1,3},{3,1},{4,6},{6,4},{5,7},{7,5},{8,10},{10,8},{9,1... | collective-permute-start | bytes 589832 | tf_op jit(solution)/shard_map/ppermute | solution.py:107

commit v20 on v19

--- a/solution.py
+++ b/solution.py
@@ -338,17 +338,17 @@
         return lax.ppermute(after(value, *others) if others else value, ("rows", "heads"), pairs)
 
     mine = lax.dynamic_slice_in_dim(latents[0], core * span * depth, span * depth, axis=1)
-    mine_x = swap(mine, "frames")
     here, there = [reshard(0)], []
     tables = jnp.concatenate([win_blocks, win_counts[:, None], block_window[:, None]], axis=1)
     tables = jnp.pad(tables, ((0, 8 - heads_n), (0, span * depth - MAXB - 2))).astype(mine.dtype)
     joined = jnp.concatenate([mine, tables], axis=0)
     near = swap(joined, "rows")
     near_x = swap(near, "frames")
+    mine_x = swap(mine, "frames")
     across = swap(after(w_out, near), "heads")
     there.append(swap(here[0], "groups"))
     here.append(reshard(1, near))
-    far_2 = swap(after(joined, here[0], mine_x), "rows", 2)
+    far_2 = swap(after(joined, here[0]), "rows", 2)
     out_half = lax.dynamic_slice_in_dim(w_out, group * cols, cols, axis=0)
     beside = [swap(after(out_half, near), "rows")]
     beside.append(swap(beside[0], "groups"))

time: 161 us -> 163 us (1.012)
  starting transfers between devices: 33 us -> 35.2 us
    ppermute x2, starting transfers between devices: 1.58 us -> 3.53 us  [reshard(): lax.ppermute(after(value, *others) if others else value, ('rows', 'heads'...]
where the time goes in v20:
time: 163 us; the launch traced here: 162 us
  waiting for transfers between devices  93.1 us (57%)
  starting transfers between devices  35.2 us (22%)
  Pallas kernels  21.5 us (13%)
  local copies, waits for them, and re-layouts  9.45 us (6%)
  other arithmetic  2.7 us (2%)
    ppermute x22, waiting for transfers between devices, swap(): return lax.ppermute(value, axis, [(i, i ^ step) for i in range(peers)])  93.1 us
    ppermute x22, starting transfers between devices, swap(): return lax.ppermute(value, axis, [(i, i ^ step) for i in range(peers)])  31.7 us
    pallas_call x4, Pallas kernels, call(): pl.pallas_call(kernel, out_shape=out_shape, grid_spec=pltpu.PrefetchScala...  11 us
    pallas_call x2, Pallas kernels, project(): pl.pallas_call(kernel, out_shape=(jax.ShapeDtypeStruct((rows, 2 * BS, col...  10.4 us
    ppermute x2, starting transfers between devices, reshard(): lax.ppermute(after(value, *others) if others else value, ('rows', 'heads'...  3.53 us
  transfers between devices with their start and end apart: 24, of which 11 were waited for; matrix products, arithmetic and copies ran while one was open for 4% of the time, Pallas kernels for 7%

profile of v20, /device:TPU:0, one launch (start us, length us, event | category | flops | bytes accessed | tf_op | source)
XLA Modules:
  0.0 162.1 jit_solution(7270624975242314675)
XLA Ops:
  0.0 0.7 convert_bitcast_fusion
  0.8 0.7 convert_bitcast_fusion.1
  1.6 0.7 convert.13
  2.5 3.1 %collective-permute-start = (bf16[136,1536]{1,0:T(8,128)(2,1)S(1)}, bf16[136,1536]{1,0:T(8,128)(2,1)}, u32[]{:S(2)}, u32[]{:S(2)}) collective-permute-start(bf16[136,1536]{1,0:T(8,128)(2,1)S(1)} %fusion.1.refs_0_), channel_id=1, source_target_pairs={{0,4},{4,0},{8,12},{12,8},{1,5},{5,1},{9,13},{13,9},{2,6},{6,2},{1... | collective-permute-start | bytes 1253384 | tf_op jit(solution)/shard_map/ppermute | solution.py:107
  5.6 2.6 %dynamic-slice_bitcast_fusion = (bf16[3,384,384]{2,1,0:T(8,128)(2,1)}, bf16[3,384,384]{2,1,0:T(8,128)(2,1)S(1)}) fusion(bf16[768,3,768]{2,0,1:T(8,128)(2,1)} %param.7, s32[]{:T(128)S(6)} %select_n.44, s32[]{:T(128)S(6)} %select_n.51, s32[]{:T(128)S(6)} %select_n.46), kind=kLoop, calls=%fused_computation.2 | loop fusion | bytes 3538956 | tf_op jit(solution)/shard_map/dynamic_slice | solution.py:330
  8.2 1.6 collective-permute-start.1
  9.8 8.7 %collective-permute-done.refs_1_ = bf16[136,1536]{1,0:T(8,128)(2,1)} collective-permute-done((bf16[136,1536]{1,0:T(8,128)(2,1)S(1)}, bf16[136,1536]{1,0:T(8,128)(2,1)}, u32[]{:S(2)}, u32[]{:S(2)}) %collective-permute-start) | collective-permute-done | bytes 417824 | tf_op jit(solution)/shard_map/ppermute | solution.py:107
  18.6 1.7 %collective-permute-start.4 = (bf16[136,1536]{1,0:T(8,128)(2,1)}, bf16[136,1536]{1,0:T(8,128)(2,1)S(1)}, u32[]{:S(2)}, u32[]{:S(2)}) collective-permute-start(bf16[136,1536]{1,0:T(8,128)(2,1)} %collective-permute-done.refs_1_), channel_id=1, source_target_pairs={{0,2},{2,0},{1,3},{3,1},{4,6},{6,4},{5,7},{7,5},{8,10},{10,8},{9,1... | collective-permute-start | bytes 1253384 | tf_op jit(solution)/shard_map/ppermute | solution.py:107
  20.4 1.9 %collective-permute-start.11 = (bf16[3,384,384]{2,1,0:T(8,128)(2,1)}, bf16[3,384,384]{2,1,0:T(8,128)(2,1)}, u32[]{:S(2)}, u32[]{:S(2)}) collective-permute-start(bf16[3,384,384]{2,1,0:T(8,128)(2,1)} %get-tuple-element.32), channel_id=1, source_target_pairs={{0,4},{1,12},{4,0},{5,8},{8,5},{9,13},{12,1},{13,9},{2,6},{3,14},{... | collective-permute-start | bytes 2654216 | tf_op jit(solution)/shard_map/ppermute | solution.py:338
  22.3 1.5 collective-permute-start.10
  23.8 7.1 %collective-permute-done.4.refs_5_ = bf16[136,1536]{1,0:T(8,128)(2,1)S(1)} collective-permute-done((bf16[136,1536]{1,0:T(8,128)(2,1)}, bf16[136,1536]{1,0:T(8,128)(2,1)S(1)}, u32[]{:S(2)}, u32[]{:S(2)}) %collective-permute-start.4) | collective-permute-done | bytes 417824 | tf_op jit(solution)/shard_map/ppermute | solution.py:107
  31.0 0.8 copy-done.5
  31.7 3.4 %collective-permute-start.2 = (bf16[136,1536]{1,0:T(8,128)(2,1)}, bf16[136,1536]{1,0:T(8,128)(2,1)}, u32[]{:S(2)}, u32[]{:S(2)}) collective-permute-start(bf16[136,1536]{1,0:T(8,128)(2,1)} %copy-done.2), channel_id=1, source_target_pairs={{0,8},{4,12},{8,0},{12,4},{1,9},{5,13},{9,1},{13,5},{2,10},{6,14},... | collective-permute-start | bytes 1253384 | tf_op jit(solution)/shard_map/ppermute | solution.py:107
  35.1 7.2 %collective-permute-done.5.refs_6_ = bf16[384,768]{1,0:T(8,128)(2,1)} collective-permute-done((bf16[384,768]{1,0:T(8,128)(2,1)S(1)}, bf16[384,768]{1,0:T(8,128)(2,1)}, u32[]{:S(2)}, u32[]{:S(2)}) %collective-permute-start.5) | collective-permute-done | bytes 589856 | tf_op jit(solution)/shard_map/ppermute | solution.py:107
  42.3 2.9 %collective-permute-start.12 = (bf16[384,768]{1,0:T(8,128)(2,1)}, bf16[384,768]{1,0:T(8,128)(2,1)}, u32[]{:S(2)}, u32[]{:S(2)}) collective-permute-start(bf16[384,768]{1,0:T(8,128)(2,1)} %collective-permute-done.5.refs_6_), channel_id=1, source_target_pairs={{0,16},{16,0},{1,17},{17,1},{2,18},{18,2},{3,19},{19,3},{4,20},{20... | collective-permute-start | bytes 1769480 | tf_op jit(solution)/shard_map/ppermute | solution.py:107
  45.5 24.8 %collective-permute-done.2.refs_2_ = bf16[136,1536]{1,0:T(8,128)(2,1)} collective-permute-done((bf16[136,1536]{1,0:T(8,128)(2,1)}, bf16[136,1536]{1,0:T(8,128)(2,1)}, u32[]{:S(2)}, u32[]{:S(2)}) %collective-permute-start.2) | collective-permute-done | bytes 417824 | tf_op jit(solution)/shard_map/ppermute | solution.py:107
  70.2 1.5 collective-permute-start.7
  71.8 0.7 slice_bitcast_fusion.2
  72.5 0.5 collective-permute-start.8
  73.0 1.5 collective-permute-start.13
  74.5 0.7 slice_bitcast_fusion.1
  75.2 8.7 %collective-permute-done.6.refs_3_ = bf16[136,1536]{1,0:T(8,128)(2,1)} collective-permute-done((bf16[136,1536]{1,0:T(8,128)(2,1)}, bf16[136,1536]{1,0:T(8,128)(2,1)}, u32[]{:S(2)}, u32[]{:S(2)}) %collective-permute-start.6) | collective-permute-done | bytes 417824 | tf_op jit(solution)/shard_map/ppermute | solution.py:107
  83.8 0.5 collective-permute-start.9
  84.4 0.7 slice_bitcast_fusion
  85.1 0.6 gather_fusion
  85.9 0.2 fusion.3
  86.1 0.6 gather_fusion.1
  87.0 8.6 %collective-permute-done.13.refs_11_ = bf16[3,384,384]{2,1,0:T(8,128)(2,1)} collective-permute-done((bf16[3,384,384]{2,1,0:T(8,128)(2,1)}, bf16[3,384,384]{2,1,0:T(8,128)(2,1)}, u32[]{:S(2)}, u32[]{:S(2)}) %collective-permute-start.13) | collective-permute-done | bytes 884768 | tf_op jit(solution)/shard_map/ppermute | solution.py:107
  95.5 0.7 collective-permute-done.9.refs_7_
  96.3 1.0 copy-done.3
  97.3 1.0 copy-done.6
  98.3 5.8 %shard_map.64 = (f32[4,128,256]{2,1,0:T(8,128)S(1)}, f32[4,256,512]{2,1,0:T(8,128)S(1)}, bf16[4,320,512]{2,1,0:T(8,128)(2,1)S(1)}) custom-call(s32[4]{0:T(128)S(1)} %pad_add_fusion.place_ref, bf16[136,1536]{1,0:T(8,128)(2,1)S(1)} %copy-done.3, bf16[136,1536]{1,0:T(8,128)(2,1)} %collective-permute-done.refs_1_, ...), custom_call_target="tpu_custom_call" | custom-call | flops 19327352832 | bytes 8053063 | tf_op jit(solution)/shard_map/pallas_call | solution.py:170
  104.2 4.6 %shard_map.65 = (f32[4,128,128]{2,1,0:T(8,128)S(1)}, f32[4,256,256]{2,1,0:T(8,128)S(1)}, bf16[4,320,256]{2,1,0:T(8,128)(2,1)S(1)}) custom-call(s32[4]{0:T(128)S(1)} %pad_add_fusion.place_ref, bf16[136,1536]{1,0:T(8,128)(2,1)S(1)} %copy-done.4, bf16[136,1536]{1,0:T(8,128)(2,1)} %collective-permute-done.refs_1_, ...), custom_call_target="tpu_custom_call" | custom-call | flops 9663676416 | bytes 4026531 | tf_op jit(solution)/shard_map/pallas_call | solution.py:170
  108.8 0.5 collective-permute-start.14
  109.4 0.4 collective-permute-start.20
  109.9 3.8 %shard_map.66 = (bf16[2,128,256]{2,1,0:T(8,128)(2,1)S(1)}, bf16[2,128,256]{2,1,0:T(8,128)(2,1)S(1)}) custom-call(s32[4]{0:T(128)S(1)} %pad_add_fusion.place_ref, s32[16]{0:T(128)S(1)} %reshape.24.members_ref, s32[4]{0:T(128)S(1)} %slice_reduce_fusion.1.counts_ref, f32[4,128,256]{2,1,0:T(8,128)S(1)} %get-tuple-element.40.q_ref, ...), custom_call_target="tpu_custom_call" | custom-call | flops 268435456 | bytes 2097152 | tf_op jit(solution)/shard_map/pallas_call | solution.py:115
  113.7 2.2 %shard_map.67 = (bf16[2,128,384]{2,1,0:T(8,128)(2,1)S(1)}, bf16[2,128,384]{2,1,0:T(8,128)(2,1)S(1)}) custom-call(s32[4]{0:T(128)S(1)} %pad_add_fusion.place_ref, s32[16]{0:T(128)S(1)} %reshape.24.members_ref, s32[4]{0:T(128)S(1)} %slice_reduce_fusion.1.counts_ref, f32[4,128,128]{2,1,0:T(8,128)S(1)} %get-tuple-element.37.q_ref, ...), custom_call_target="tpu_custom_call" | custom-call | flops 134217728 | bytes 1048576 | tf_op jit(solution)/shard_map/pallas_call | solution.py:115
  115.9 7.4 %collective-permute-start.16 = (bf16[2,128,384]{2,1,0:T(8,128)(2,1)S(1)}, bf16[2,128,384]{2,1,0:T(8,128)(2,1)S(1)}, u32[]{:S(2)}, u32[]{:S(2)}) collective-permute-start(bf16[2,128,384]{2,1,0:T(8,128)(2,1)S(1)} %get-tuple-element.45), channel_id=1, source_target_pairs={{0,4},{4,0},{8,12},{12,8},{1,5},{5,1},{9,13},{13,9},{2,6},{6,2},{1... | collective-permute-start | bytes 589832 | tf_op jit(solution)/shard_map/ppermute | solution.py:107
  123.3 2.4 %collective-permute-start.18 = (bf16[2,128,384]{2,1,0:T(8,128)(2,1)S(1)}, bf16[2,128,384]{2,1,0:T(8,128)(2,1)S(1)}, u32[]{:S(2)}, u32[]{:S(2)}) collective-permute-start(bf16[2,128,384]{2,1,0:T(8,128)(2,1)S(1)} %get-tuple-element.45), channel_id=1, source_target_pairs={{0,12},{4,8},{8,4},{12,0},{1,13},{5,9},{9,5},{13,1},{2,14},{6,10},... | collective-permute-start | bytes 589832 | tf_op jit(solution)/shard_map/ppermute | solution.py:107
  125.8 4.7 %collective-permute-done.16.refs_1_ = bf16[2,128,384]{2,1,0:T(8,128)(2,1)S(1)} collective-permute-done((bf16[2,128,384]{2,1,0:T(8,128)(2,1)S(1)}, bf16[2,128,384]{2,1,0:T(8,128)(2,1)S(1)}, u32[]{:S(2)}, u32[]{:S(2)}) %collective-permute-start.16) | collective-permute-done | bytes 196640 | tf_op jit(solution)/shard_map/ppermute | solution.py:107
  130.5 9.9 %collective-permute-done.17.refs_2_ = bf16[2,128,384]{2,1,0:T(8,128)(2,1)S(1)} collective-permute-done((bf16[2,128,384]{2,1,0:T(8,128)(2,1)S(1)}, bf16[2,128,384]{2,1,0:T(8,128)(2,1)S(1)}, u32[]{:S(2)}, u32[]{:S(2)}) %collective-permute-start.17) | collective-permute-done | bytes 196640 | tf_op jit(solution)/shard_map/ppermute | solution.py:107
  140.4 3.7 %shard_map.68 = (f32[2,64,768]{2,1,0:T(8,128)S(1)}, bf16[2,64,768]{2,1,0:T(8,128)(2,1)S(1)}, f32[2,64,768]{2,1,0:T(8,128)S(1)}, bf16[2,64,768]{2,1,0:T(8,128)(2,1)S(1)}) custom-call(s32[4]{0:T(128)S(1)} %pad_add_fusion.place_ref, bf16[2,128,384]{2,1,0:T(8,128)(2,1)S(1)} %get-tuple-element.44.refs_0_, ...), custom_call_target="tpu_custom_call" | custom-call | flops 1207959552 | bytes 4718592 | tf_op jit(solution)/shard_map/pallas_call | solution.py:115
  144.1 0.6 collective-permute-start.21
  144.7 5.1 %collective-permute-done.21 = bf16[2,64,768]{2,1,0:T(8,128)(2,1)S(1)} collective-permute-done((bf16[2,64,768]{2,1,0:T(8,128)(2,1)S(1)}, bf16[2,64,768]{2,1,0:T(8,128)(2,1)S(1)}, u32[]{:S(2)}, u32[]{:S(2)}) %collective-permute-start.21) | collective-permute-done | bytes 196640 | tf_op jit(solution)/shard_map/ppermute | solution.py:107
  149.9 2.8 %collective-permute-start.23 = (bf16[2,64,768]{2,1,0:T(8,128)(2,1)S(1)}, bf16[2,64,768]{2,1,0:T(8,128)(2,1)S(1)}, u32[]{:S(2)}, u32[]{:S(2)}) collective-permute-start(bf16[2,64,768]{2,1,0:T(8,128)(2,1)S(1)} %add_convert_fusion), channel_id=1, source_target_pairs={{0,8},{4,12},{8,0},{12,4},{1,9},{5,13},{9,1},{13,5},{2,10},{6,14},... | collective-permute-start | bytes 589832 | tf_op jit(solution)/shard_map/ppermute | solution.py:107
  152.7 0.5 collective-permute-start.22
  153.3 7.5 %collective-permute-done.23.far_ref = bf16[2,64,768]{2,1,0:T(8,128)(2,1)S(1)} collective-permute-done((bf16[2,64,768]{2,1,0:T(8,128)(2,1)S(1)}, bf16[2,64,768]{2,1,0:T(8,128)(2,1)S(1)}, u32[]{:S(2)}, u32[]{:S(2)}) %collective-permute-start.23) | collective-permute-done | bytes 196640 | tf_op jit(solution)/shard_map/ppermute | solution.py:107
  160.7 1.3 shard_map.69
  (51 shorter events, 1.6 us)
Async XLA Ops:
  0.0 2.3 %copy-start = (bf16[1,128,3072]{2,1,0:T(8,128)(2,1)S(1)}, bf16[1,128,3072]{2,1,0:T(8,128)(2,1)}, u32[]{:S(2)}) copy-start(bf16[1,128,3072]{2,1,0:T(8,128)(2,1)} %param.6) | copy-start | bytes 2359300
  2.3 3.2 %copy-start.8 = (bf16[128,1536]{1,0:T(8,128)(2,1)}, bf16[128,1536]{1,0:T(8,128)(2,1)S(1)}, u32[]{:S(2)}) copy-start(bf16[128,1536]{1,0:T(8,128)(2,1)S(1)} %dynamic-slice_bitcast_fusion.2) | copy-start | bytes 1179652
  2.5 5.7 %copy-start.2 = (bf16[136,1536]{1,0:T(8,128)(2,1)}, bf16[136,1536]{1,0:T(8,128)(2,1)S(1)}, u32[]{:S(2)}) copy-start(bf16[136,1536]{1,0:T(8,128)(2,1)S(1)} %fusion.1.refs_0_) | copy-start | bytes 1253380
  2.5 16.0 %collective-permute-start = (bf16[136,1536]{1,0:T(8,128)(2,1)S(1)}, bf16[136,1536]{1,0:T(8,128)(2,1)}, u32[]{:S(2)}, u32[]{:S(2)}) collective-permute-start(bf16[136,1536]{1,0:T(8,128)(2,1)S(1)} %fusion.1.refs_0_), channel_id=1, source_target_pairs={{0,4},{4,0},{8,12},{12,8},{1,5},{5,1},{9,13},{13,9},{2,6},{6,2},{1... | collective-permute-start | bytes 1253384 | tf_op jit(solution)/shard_map/ppermute | solution.py:107
  5.6 13.0 %copy-start.1 = (bf16[768,768]{1,0:T(8,128)(2,1)S(1)}, bf16[768,768]{1,0:T(8,128)(2,1)}, u32[]{:S(2)}) copy-start(bf16[768,768]{1,0:T(8,128)(2,1)} %refs_4_.1) | copy-start | bytes 3538948
  8.2 14.1 %collective-permute-start.1 = (bf16[3,384,384]{2,1,0:T(8,128)(2,1)S(1)}, bf16[3,384,384]{2,1,0:T(8,128)(2,1)}, u32[]{:S(2)}, u32[]{:S(2)}) collective-permute-start(bf16[3,384,384]{2,1,0:T(8,128)(2,1)S(1)} %get-tuple-element.52), channel_id=1, source_target_pairs={{0,0},{1,8},{4,4},{5,12},{8,1},{9,9},{12,5},{13,13},{2,2},{3,10},{... | collective-permute-start | bytes 2654216 | tf_op jit(solution)/shard_map/ppermute | solution.py:338
  18.5 53.2 %collective-permute-start.3 = (bf16[768,768]{1,0:T(8,128)(2,1)S(1)}, bf16[768,768]{1,0:T(8,128)(2,1)S(1)}, u32[]{:S(2)}, u32[]{:S(2)}) collective-permute-start(bf16[768,768]{1,0:T(8,128)(2,1)S(1)} %copy-done.1), channel_id=1, source_target_pairs={{0,1},{1,0},{2,3},{3,2},{4,5},{5,4},{6,7},{7,6},{8,9},{9,8},{10,11... | collective-permute-start | bytes 3538952 | tf_op jit(solution)/shard_map/ppermute | solution.py:107
  18.6 23.8 %collective-permute-start.5 = (bf16[384,768]{1,0:T(8,128)(2,1)S(1)}, bf16[384,768]{1,0:T(8,128)(2,1)}, u32[]{:S(2)}, u32[]{:S(2)}) collective-permute-start(bf16[384,768]{1,0:T(8,128)(2,1)S(1)} %constant_dynamic-slice_fusion), channel_id=1, source_target_pairs={{0,4},{4,0},{8,12},{12,8},{1,5},{5,1},{9,13},{13,9},{2,6},{6,2},{1... | collective-permute-start | bytes 1769480 | tf_op jit(solution)/shard_map/ppermute | solution.py:107
  18.6 12.3 %collective-permute-start.4 = (bf16[136,1536]{1,0:T(8,128)(2,1)}, bf16[136,1536]{1,0:T(8,128)(2,1)S(1)}, u32[]{:S(2)}, u32[]{:S(2)}) collective-permute-start(bf16[136,1536]{1,0:T(8,128)(2,1)} %collective-permute-done.refs_1_), channel_id=1, source_target_pairs={{0,2},{2,0},{1,3},{3,1},{4,6},{6,4},{5,7},{7,5},{8,10},{10,8},{9,1... | collective-permute-start | bytes 1253384 | tf_op jit(solution)/shard_map/ppermute | solution.py:107
  20.4 52.1 %collective-permute-start.11 = (bf16[3,384,384]{2,1,0:T(8,128)(2,1)}, bf16[3,384,384]{2,1,0:T(8,128)(2,1)}, u32[]{:S(2)}, u32[]{:S(2)}) collective-permute-start(bf16[3,384,384]{2,1,0:T(8,128)(2,1)} %get-tuple-element.32), channel_id=1, source_target_pairs={{0,4},{1,12},{4,0},{5,8},{8,5},{9,13},{12,1},{13,9},{2,6},{3,14},{... | collective-permute-start | bytes 2654216 | tf_op jit(solution)/shard_map/ppermute | solution.py:338
  22.3 50.7 %collective-permute-start.10 = (bf16[3,384,384]{2,1,0:T(8,128)(2,1)}, bf16[3,384,384]{2,1,0:T(8,128)(2,1)}, u32[]{:S(2)}, u32[]{:S(2)}) collective-permute-start(bf16[3,384,384]{2,1,0:T(8,128)(2,1)} %collective-permute-done.1.refs_8_), channel_id=1, source_target_pairs={{0,16},{16,0},{1,17},{17,1},{2,18},{18,2},{3,19},{19,3},{4,20},{20... | collective-permute-start | bytes 2654216 | tf_op jit(solution)/shard_map/ppermute | solution.py:107
  31.0 0.8 copy-start.5
  31.7 38.5 %collective-permute-start.2 = (bf16[136,1536]{1,0:T(8,128)(2,1)}, bf16[136,1536]{1,0:T(8,128)(2,1)}, u32[]{:S(2)}, u32[]{:S(2)}) collective-permute-start(bf16[136,1536]{1,0:T(8,128)(2,1)} %copy-done.2), channel_id=1, source_target_pairs={{0,8},{4,12},{8,0},{12,4},{1,9},{5,13},{9,1},{13,5},{2,10},{6,14},... | collective-permute-start | bytes 1253384 | tf_op jit(solution)/shard_map/ppermute | solution.py:107
  42.3 30.7 %collective-permute-start.12 = (bf16[384,768]{1,0:T(8,128)(2,1)}, bf16[384,768]{1,0:T(8,128)(2,1)}, u32[]{:S(2)}, u32[]{:S(2)}) collective-permute-start(bf16[384,768]{1,0:T(8,128)(2,1)} %collective-permute-done.5.refs_6_), channel_id=1, source_target_pairs={{0,16},{16,0},{1,17},{17,1},{2,18},{18,2},{3,19},{19,3},{4,20},{20... | collective-permute-start | bytes 1769480 | tf_op jit(solution)/shard_map/ppermute | solution.py:107
  70.2 25.3 %collective-permute-start.7 = (bf16[128,1536]{1,0:T(8,128)(2,1)}, bf16[128,1536]{1,0:T(8,128)(2,1)S(1)}, u32[]{:S(2)}, u32[]{:S(2)}) collective-permute-start(bf16[128,1536]{1,0:T(8,128)(2,1)} %copy-done.8), channel_id=1, source_target_pairs={{0,2},{2,0},{1,3},{3,1},{4,6},{6,4},{5,7},{7,5},{8,10},{10,8},{9,1... | collective-permute-start | bytes 1179656 | tf_op jit(solution)/shard_map/ppermute | solution.py:107
  71.7 12.1 %collective-permute-start.6 = (bf16[136,1536]{1,0:T(8,128)(2,1)}, bf16[136,1536]{1,0:T(8,128)(2,1)}, u32[]{:S(2)}, u32[]{:S(2)}) collective-permute-start(bf16[136,1536]{1,0:T(8,128)(2,1)} %copy-done.2), channel_id=1, source_target_pairs={{0,12},{4,8},{8,4},{12,0},{1,13},{5,9},{9,5},{13,1},{2,14},{6,10},... | collective-permute-start | bytes 1253384 | tf_op jit(solution)/shard_map/ppermute | solution.py:107
  72.5 23.1 %collective-permute-start.8 = (bf16[136,1536]{1,0:T(8,128)(2,1)}, bf16[136,1536]{1,0:T(8,128)(2,1)}, u32[]{:S(2)}, u32[]{:S(2)}) collective-permute-start(bf16[136,1536]{1,0:T(8,128)(2,1)} %collective-permute-done.2.refs_2_), channel_id=1, source_target_pairs={{0,2},{2,0},{1,3},{3,1},{4,6},{6,4},{5,7},{7,5},{8,10},{10,8},{9,1... | collective-permute-start | bytes 1253384 | tf_op jit(solution)/shard_map/ppermute | solution.py:107
  73.0 22.5 %collective-permute-start.13 = (bf16[3,384,384]{2,1,0:T(8,128)(2,1)}, bf16[3,384,384]{2,1,0:T(8,128)(2,1)}, u32[]{:S(2)}, u32[]{:S(2)}) collective-permute-start(bf16[3,384,384]{2,1,0:T(8,128)(2,1)} %collective-permute-done.11.refs_10_), channel_id=1, source_target_pairs={{0,16},{16,0},{1,17},{17,1},{2,18},{18,2},{3,19},{19,3},{4,20},{20... | collective-permute-start | bytes 2654216 | tf_op jit(solution)/shard_map/ppermute | solution.py:107
  83.8 12.4 %collective-permute-start.9 = (bf16[136,1536]{1,0:T(8,128)(2,1)}, bf16[136,1536]{1,0:T(8,128)(2,1)}, u32[]{:S(2)}, u32[]{:S(2)}) collective-permute-start(bf16[136,1536]{1,0:T(8,128)(2,1)} %collective-permute-done.6.refs_3_), channel_id=1, source_target_pairs={{0,2},{2,0},{1,3},{3,1},{4,6},{6,4},{5,7},{7,5},{8,10},{10,8},{9,1... | collective-permute-start | bytes 1253384 | tf_op jit(solution)/shard_map/ppermute | solution.py:107
  96.2 1.0 copy-start.3
  97.3 1.0 copy-start.6
  98.3 5.9 %copy-start.4 = (bf16[136,1536]{1,0:T(8,128)(2,1)S(1)}, bf16[136,1536]{1,0:T(8,128)(2,1)}, u32[]{:S(2)}) copy-start(bf16[136,1536]{1,0:T(8,128)(2,1)} %copy-done.2) | copy-start | bytes 1253380
  98.3 5.9 %copy-start.7 = (bf16[136,1536]{1,0:T(8,128)(2,1)S(1)}, bf16[136,1536]{1,0:T(8,128)(2,1)}, u32[]{:S(2)}) copy-start(bf16[136,1536]{1,0:T(8,128)(2,1)} %copy-done.5) | copy-start | bytes 1253380
  104.1 5.8 %collective-permute-start.15 = (bf16[4,320,512]{2,1,0:T(8,128)(2,1)S(1)}, bf16[4,320,512]{2,1,0:T(8,128)(2,1)S(1)}, u32[]{:S(2)}, u32[]{:S(2)}) collective-permute-start(bf16[4,320,512]{2,1,0:T(8,128)(2,1)S(1)} %get-tuple-element.35), channel_id=1, source_target_pairs={{0,1},{1,0},{2,3},{3,2},{4,5},{5,4},{6,7},{7,6},{8,9},{9,8},{10,11... | collective-permute-start | bytes 3932168 | tf_op jit(solution)/shard_map/ppermute | solution.py:107
  108.8 4.8 %collective-permute-start.14 = (bf16[4,320,256]{2,1,0:T(8,128)(2,1)S(1)}, bf16[4,320,256]{2,1,0:T(8,128)(2,1)S(1)}, u32[]{:S(2)}, u32[]{:S(2)}) collective-permute-start(bf16[4,320,256]{2,1,0:T(8,128)(2,1)S(1)} %get-tuple-element.39), channel_id=1, source_target_pairs={{0,1},{1,0},{2,3},{3,2},{4,5},{5,4},{6,7},{7,6},{8,9},{9,8},{10,11... | collective-permute-start | bytes 1966088 | tf_op jit(solution)/shard_map/ppermute | solution.py:107
  109.3 16.4 %collective-permute-start.19 = (bf16[384,768]{1,0:T(8,128)(2,1)}, bf16[384,768]{1,0:T(8,128)(2,1)S(1)}, u32[]{:S(2)}, u32[]{:S(2)}) collective-permute-start(bf16[384,768]{1,0:T(8,128)(2,1)} %collective-permute-done.5.refs_6_), channel_id=1, source_target_pairs={{0,1},{1,0},{2,3},{3,2},{4,5},{5,4},{6,7},{7,6},{8,9},{9,8},{10,11... | collective-permute-start | bytes 1769480 | tf_op jit(solution)/shard_map/ppermute | solution.py:107
  109.4 16.3 %collective-permute-start.20 = (bf16[384,768]{1,0:T(8,128)(2,1)}, bf16[384,768]{1,0:T(8,128)(2,1)S(1)}, u32[]{:S(2)}, u32[]{:S(2)}) collective-permute-start(bf16[384,768]{1,0:T(8,128)(2,1)} %collective-permute-done.12.refs_7_), channel_id=1, source_target_pairs={{0,1},{1,0},{2,3},{3,2},{4,5},{5,4},{6,7},{7,6},{8,9},{9,8},{10,11... | collective-permute-start | bytes 1769480 | tf_op jit(solution)/shard_map/ppermute | solution.py:107
  115.9 14.6 %collective-permute-start.16 = (bf16[2,128,384]{2,1,0:T(8,128)(2,1)S(1)}, bf16[2,128,384]{2,1,0:T(8,128)(2,1)S(1)}, u32[]{:S(2)}, u32[]{:S(2)}) collective-permute-start(bf16[2,128,384]{2,1,0:T(8,128)(2,1)S(1)} %get-tuple-element.45), channel_id=1, source_target_pairs={{0,4},{4,0},{8,12},{12,8},{1,5},{5,1},{9,13},{13,9},{2,6},{6,2},{1... | collective-permute-start | bytes 589832 | tf_op jit(solution)/shard_map/ppermute | solution.py:107
  123.3 17.1 %collective-permute-start.17 = (bf16[2,128,384]{2,1,0:T(8,128)(2,1)S(1)}, bf16[2,128,384]{2,1,0:T(8,128)(2,1)S(1)}, u32[]{:S(2)}, u32[]{:S(2)}) collective-permute-start(bf16[2,128,384]{2,1,0:T(8,128)(2,1)S(1)} %get-tuple-element.44.refs_0_), channel_id=1, source_target_pairs={{0,8},{4,12},{8,0},{12,4},{1,9},{5,13},{9,1},{13,5},{2,10},{6,14},... | collective-permute-start | bytes 589832 | tf_op jit(solution)/shard_map/ppermute | solution.py:107
  123.3 17.1 %collective-permute-start.18 = (bf16[2,128,384]{2,1,0:T(8,128)(2,1)S(1)}, bf16[2,128,384]{2,1,0:T(8,128)(2,1)S(1)}, u32[]{:S(2)}, u32[]{:S(2)}) collective-permute-start(bf16[2,128,384]{2,1,0:T(8,128)(2,1)S(1)} %get-tuple-element.45), channel_id=1, source_target_pairs={{0,12},{4,8},{8,4},{12,0},{1,13},{5,9},{9,5},{13,1},{2,14},{6,10},... | collective-permute-start | bytes 589832 | tf_op jit(solution)/shard_map/ppermute | solution.py:107
  144.1 5.7 %collective-permute-start.21 = (bf16[2,64,768]{2,1,0:T(8,128)(2,1)S(1)}, bf16[2,64,768]{2,1,0:T(8,128)(2,1)S(1)}, u32[]{:S(2)}, u32[]{:S(2)}) collective-permute-start(bf16[2,64,768]{2,1,0:T(8,128)(2,1)S(1)} %get-tuple-element.48), channel_id=1, source_target_pairs={{0,2},{2,0},{1,3},{3,1},{4,6},{6,4},{5,7},{7,5},{8,10},{10,8},{9,1... | collective-permute-start | bytes 589832 | tf_op jit(solution)/shard_map/ppermute | solution.py:107
  149.9 10.8 %collective-permute-start.23 = (bf16[2,64,768]{2,1,0:T(8,128)(2,1)S(1)}, bf16[2,64,768]{2,1,0:T(8,128)(2,1)S(1)}, u32[]{:S(2)}, u32[]{:S(2)}) collective-permute-start(bf16[2,64,768]{2,1,0:T(8,128)(2,1)S(1)} %add_convert_fusion), channel_id=1, source_target_pairs={{0,8},{4,12},{8,0},{12,4},{1,9},{5,13},{9,1},{13,5},{2,10},{6,14},... | collective-permute-start | bytes 589832 | tf_op jit(solution)/shard_map/ppermute | solution.py:107
  152.7 8.0 %collective-permute-start.22 = (bf16[2,64,768]{2,1,0:T(8,128)(2,1)S(1)}, bf16[2,64,768]{2,1,0:T(8,128)(2,1)S(1)}, u32[]{:S(2)}, u32[]{:S(2)}) collective-permute-start(bf16[2,64,768]{2,1,0:T(8,128)(2,1)S(1)} %get-tuple-element.49), channel_id=1, source_target_pairs={{0,2},{2,0},{1,3},{3,1},{4,6},{6,4},{5,7},{7,5},{8,10},{10,8},{9,1... | collective-permute-start | bytes 589832 | tf_op jit(solution)/shard_map/ppermute | solution.py:107

commit v21 on v20

--- a/solution.py
+++ b/solution.py
@@ -350,11 +350,11 @@
     here.append(reshard(1, near))
     far_2 = swap(after(joined, here[0]), "rows", 2)
     out_half = lax.dynamic_slice_in_dim(w_out, group * cols, cols, axis=0)
-    beside = [swap(after(out_half, near), "rows")]
+    beside = [swap(after(out_half, far_2), "rows")]
     beside.append(swap(beside[0], "groups"))
-    there.append(swap(after(here[1], there[0], beside[1]), "groups"))
+    there.append(swap(after(here[1], there[0]), "groups"))
     far_2x = swap(far_2, "frames")
-    far_3 = swap(after(joined, far_2, across, near_x, beside[0]), "rows", 3)
+    far_3 = swap(after(joined, far_2, across, near_x), "rows", 3)
     far_3x = swap(far_3, "frames")
 
     found = jnp.stack([x[count : count + heads_n, : MAXB + 2] for x in (joined, near, far_2, far_3)])
@@ -366,11 +366,11 @@
     members, counts = picked[:, :MAXB].reshape(-1), picked[:, MAXB]
 
     pieces = [joined, near, far_2, far_3], [mine_x, near_x, far_2x, far_3x]
-    chunks = [(here[0], there[0]), (here[1], after(there[1], members, counts))]
+    chunks = [(here[0], there[0]), (here[1], after(there[1], members, counts, beside[0]))]
     last = cols // (3 * HD) * HD
     first = project(place, *pieces, chunks, 0, cols - last)
     first_more = swap(first[2], "heads")
-    chunks[1] = (here[1], after(there[1], first[2]))
+    chunks[1] = (here[1], after(there[1], first[2], beside[1]))
     second = project(place, *pieces, chunks, cols - last, last)
     second_more = swap(second[2], "heads")
     attended = attend_all(place, members, counts, *first[:2], first_more)

time: 163 us -> 166 us (1.018)
  starting transfers between devices: 35.2 us -> 44.7 us
  waiting for transfers between devices: 93.1 us -> 87.4 us
    ppermute x22, starting transfers between devices: 31.7 us -> 43.2 us  [swap(): return lax.ppermute(value, axis, [(i, i ^ step) for i in range(peers)])]
    ppermute x22, waiting for transfers between devices: 93.1 us -> 87.4 us  [swap(): return lax.ppermute(value, axis, [(i, i ^ step) for i in range(peers)])]
    ppermute x2, starting transfers between devices: 3.53 us -> 1.58 us  [reshard(): lax.ppermute(after(value, *others) if others else value, ('rows', 'heads'...]
    unnamed x18 -> x12, local copies, waits for them, and re-layouts: 2.8 us -> 1.03 us
  transfers between devices with their start and end apart: 24 -> 24, of which waited for: 11 -> 9; matrix products, arithmetic and copies ran while one was open for 4% -> 5% of each run, Pallas kernels for 7% -> 10%
where the time goes in v21:
time: 166 us; the launch traced here: 165 us
  waiting for transfers between devices  87.4 us (53%)
  starting transfers between devices  44.7 us (27%)
  Pallas kernels  21.6 us (13%)
  local copies, waits for them, and re-layouts  8.49 us (5%)
  other arithmetic  2.7 us (2%)
    ppermute x22, waiting for transfers between devices, swap(): return lax.ppermute(value, axis, [(i, i ^ step) for i in range(peers)])  87.4 us
    ppermute x22, starting transfers between devices, swap(): return lax.ppermute(value, axis, [(i, i ^ step) for i in range(peers)])  43.2 us
    pallas_call x4, Pallas kernels, call(): pl.pallas_call(kernel, out_shape=out_shape, grid_spec=pltpu.PrefetchScala...  11 us
    pallas_call x2, Pallas kernels, project(): pl.pallas_call(kernel, out_shape=(jax.ShapeDtypeStruct((rows, 2 * BS, col...  10.6 us
  transfers between devices with their start and end apart: 24, of which 9 were waited for; matrix products, arithmetic and copies ran while one was open for 5% of the time, Pallas kernels for 10%

profile of v21, /device:TPU:0, one launch (start us, length us, event | category | flops | bytes accessed | tf_op | source)
XLA Modules:
  0.0 165.2 jit_solution(8129291163770780011)
XLA Ops:
  0.0 0.7 convert_bitcast_fusion
  0.8 0.7 convert_bitcast_fusion.1
  1.6 0.7 convert.13
  2.5 3.1 %collective-permute-start = (bf16[136,1536]{1,0:T(8,128)(2,1)S(1)}, bf16[136,1536]{1,0:T(8,128)(2,1)}, u32[]{:S(2)}, u32[]{:S(2)}) collective-permute-start(bf16[136,1536]{1,0:T(8,128)(2,1)S(1)} %fusion.1.refs_0_), channel_id=1, source_target_pairs={{0,4},{4,0},{8,12},{12,8},{1,5},{5,1},{9,13},{13,9},{2,6},{6,2},{1... | collective-permute-start | bytes 1253384 | tf_op jit(solution)/shard_map/ppermute | solution.py:107
  5.6 2.7 %dynamic-slice_bitcast_fusion = (bf16[3,384,384]{2,1,0:T(8,128)(2,1)}, bf16[3,384,384]{2,1,0:T(8,128)(2,1)S(1)}) fusion(bf16[768,3,768]{2,0,1:T(8,128)(2,1)} %param.7, s32[]{:T(128)S(6)} %select_n.44, s32[]{:T(128)S(6)} %select_n.51, s32[]{:T(128)S(6)} %select_n.46), kind=kLoop, calls=%fused_computation.2 | loop fusion | bytes 3538956 | tf_op jit(solution)/shard_map/dynamic_slice | solution.py:330
  8.2 1.6 collective-permute-start.1
  9.8 8.7 %collective-permute-done.refs_1_ = bf16[136,1536]{1,0:T(8,128)(2,1)} collective-permute-done((bf16[136,1536]{1,0:T(8,128)(2,1)S(1)}, bf16[136,1536]{1,0:T(8,128)(2,1)}, u32[]{:S(2)}, u32[]{:S(2)}) %collective-permute-start) | collective-permute-done | bytes 417824 | tf_op jit(solution)/shard_map/ppermute | solution.py:107
  18.5 1.8 %collective-permute-start.9 = (bf16[3,384,384]{2,1,0:T(8,128)(2,1)}, bf16[3,384,384]{2,1,0:T(8,128)(2,1)}, u32[]{:S(2)}, u32[]{:S(2)}) collective-permute-start(bf16[3,384,384]{2,1,0:T(8,128)(2,1)} %collective-permute-done.1.refs_8_), channel_id=1, source_target_pairs={{0,16},{16,0},{1,17},{17,1},{2,18},{18,2},{3,19},{19,3},{4,20},{20... | collective-permute-start | bytes 2654216 | tf_op jit(solution)/shard_map/ppermute | solution.py:107
  20.3 16.3 %collective-permute-start.2 = (bf16[136,1536]{1,0:T(8,128)(2,1)}, bf16[136,1536]{1,0:T(8,128)(2,1)}, u32[]{:S(2)}, u32[]{:S(2)}) collective-permute-start(bf16[136,1536]{1,0:T(8,128)(2,1)} %copy-done.2), channel_id=1, source_target_pairs={{0,8},{4,12},{8,0},{12,4},{1,9},{5,13},{9,1},{13,5},{2,10},{6,14},... | collective-permute-start | bytes 1253384 | tf_op jit(solution)/shard_map/ppermute | solution.py:107
  36.6 1.5 collective-permute-start.4
  38.2 0.9 constant_dynamic-slice_fusion
  39.0 31.2 %collective-permute-done.2.refs_2_ = bf16[136,1536]{1,0:T(8,128)(2,1)} collective-permute-done((bf16[136,1536]{1,0:T(8,128)(2,1)}, bf16[136,1536]{1,0:T(8,128)(2,1)}, u32[]{:S(2)}, u32[]{:S(2)}) %collective-permute-start.2) | collective-permute-done | bytes 417824 | tf_op jit(solution)/shard_map/ppermute | solution.py:107
  70.3 0.1 fusion.2
  70.5 1.6 collective-permute-start.6
  72.0 1.0 collective-permute-start.5
  73.0 0.6 slice_bitcast_fusion.2
  73.7 0.5 collective-permute-start.7
  74.2 1.5 collective-permute-start.11
  75.7 0.7 slice_bitcast_fusion.1
  76.4 7.9 %collective-permute-done.12.refs_6_ = bf16[384,768]{1,0:T(8,128)(2,1)} collective-permute-done((bf16[384,768]{1,0:T(8,128)(2,1)}, bf16[384,768]{1,0:T(8,128)(2,1)}, u32[]{:S(2)}, u32[]{:S(2)}) %collective-permute-start.12) | collective-permute-done | bytes 589856 | tf_op jit(solution)/shard_map/ppermute | solution.py:107
  84.4 1.5 collective-permute-start.13
  85.9 8.5 %collective-permute-done.5.refs_3_ = bf16[136,1536]{1,0:T(8,128)(2,1)} collective-permute-done((bf16[136,1536]{1,0:T(8,128)(2,1)}, bf16[136,1536]{1,0:T(8,128)(2,1)}, u32[]{:S(2)}, u32[]{:S(2)}) %collective-permute-start.5) | collective-permute-done | bytes 417824 | tf_op jit(solution)/shard_map/ppermute | solution.py:107
  94.4 1.5 collective-permute-start.8
  95.8 0.7 slice_bitcast_fusion
  96.6 0.6 gather_fusion
  97.1 0.2 slice_reduce_fusion
  97.4 0.2 fusion.3
  97.6 0.6 gather_fusion.1
  98.3 0.2 slice_reduce_fusion.1.counts_ref
  98.5 7.9 %collective-permute-done.8.refs_7_ = bf16[136,1536]{1,0:T(8,128)(2,1)} collective-permute-done((bf16[136,1536]{1,0:T(8,128)(2,1)}, bf16[136,1536]{1,0:T(8,128)(2,1)}, u32[]{:S(2)}, u32[]{:S(2)}) %collective-permute-start.8) | collective-permute-done | bytes 417824 | tf_op jit(solution)/shard_map/ppermute | solution.py:107
  106.4 1.0 copy-done.3
  107.4 5.9 %shard_map.64 = (f32[4,128,256]{2,1,0:T(8,128)S(1)}, f32[4,256,512]{2,1,0:T(8,128)S(1)}, bf16[4,320,512]{2,1,0:T(8,128)(2,1)S(1)}) custom-call(s32[4]{0:T(128)S(1)} %pad_add_fusion.place_ref, bf16[136,1536]{1,0:T(8,128)(2,1)S(1)} %copy-done.3, bf16[136,1536]{1,0:T(8,128)(2,1)} %collective-permute-done.refs_1_, ...), custom_call_target="tpu_custom_call" | custom-call | flops 19327352832 | bytes 8053063 | tf_op jit(solution)/shard_map/pallas_call | solution.py:170
  113.4 4.7 %shard_map.65 = (f32[4,128,128]{2,1,0:T(8,128)S(1)}, f32[4,256,256]{2,1,0:T(8,128)S(1)}, bf16[4,320,256]{2,1,0:T(8,128)(2,1)S(1)}) custom-call(s32[4]{0:T(128)S(1)} %pad_add_fusion.place_ref, bf16[136,1536]{1,0:T(8,128)(2,1)S(1)} %copy-done.4, bf16[136,1536]{1,0:T(8,128)(2,1)} %collective-permute-done.refs_1_, ...), custom_call_target="tpu_custom_call" | custom-call | flops 9663676416 | bytes 4026531 | tf_op jit(solution)/shard_map/pallas_call | solution.py:170
  118.1 0.5 collective-permute-start.14
  118.7 0.4 collective-permute-start.20
  119.2 3.8 %shard_map.66 = (bf16[2,128,256]{2,1,0:T(8,128)(2,1)S(1)}, bf16[2,128,256]{2,1,0:T(8,128)(2,1)S(1)}) custom-call(s32[4]{0:T(128)S(1)} %pad_add_fusion.place_ref, s32[16]{0:T(128)S(1)} %reshape.24.members_ref, s32[4]{0:T(128)S(1)} %slice_reduce_fusion.1.counts_ref, f32[4,128,256]{2,1,0:T(8,128)S(1)} %get-tuple-element.40.q_ref, ...), custom_call_target="tpu_custom_call" | custom-call | flops 268435456 | bytes 2097152 | tf_op jit(solution)/shard_map/pallas_call | solution.py:115
  123.0 2.2 %shard_map.67 = (bf16[2,128,384]{2,1,0:T(8,128)(2,1)S(1)}, bf16[2,128,384]{2,1,0:T(8,128)(2,1)S(1)}) custom-call(s32[4]{0:T(128)S(1)} %pad_add_fusion.place_ref, s32[16]{0:T(128)S(1)} %reshape.24.members_ref, s32[4]{0:T(128)S(1)} %slice_reduce_fusion.1.counts_ref, f32[4,128,128]{2,1,0:T(8,128)S(1)} %get-tuple-element.37.q_ref, ...), custom_call_target="tpu_custom_call" | custom-call | flops 134217728 | bytes 1048576 | tf_op jit(solution)/shard_map/pallas_call | solution.py:115
  125.2 0.9 collective-permute-start.17
  126.1 3.5 %collective-permute-start.18 = (bf16[2,128,384]{2,1,0:T(8,128)(2,1)S(1)}, bf16[2,128,384]{2,1,0:T(8,128)(2,1)S(1)}, u32[]{:S(2)}, u32[]{:S(2)}) collective-permute-start(bf16[2,128,384]{2,1,0:T(8,128)(2,1)S(1)} %get-tuple-element.45), channel_id=1, source_target_pairs={{0,12},{4,8},{8,4},{12,0},{1,13},{5,9},{9,5},{13,1},{2,14},{6,10},... | collective-permute-start | bytes 589832 | tf_op jit(solution)/shard_map/ppermute | solution.py:107
  129.6 4.4 %collective-permute-done.16.refs_1_ = bf16[2,128,384]{2,1,0:T(8,128)(2,1)S(1)} collective-permute-done((bf16[2,128,384]{2,1,0:T(8,128)(2,1)S(1)}, bf16[2,128,384]{2,1,0:T(8,128)(2,1)S(1)}, u32[]{:S(2)}, u32[]{:S(2)}) %collective-permute-start.16) | collective-permute-done | bytes 196640 | tf_op jit(solution)/shard_map/ppermute | solution.py:107
  134.0 8.4 %collective-permute-done.17.refs_2_ = bf16[2,128,384]{2,1,0:T(8,128)(2,1)S(1)} collective-permute-done((bf16[2,128,384]{2,1,0:T(8,128)(2,1)S(1)}, bf16[2,128,384]{2,1,0:T(8,128)(2,1)S(1)}, u32[]{:S(2)}, u32[]{:S(2)}) %collective-permute-start.17) | collective-permute-done | bytes 196640 | tf_op jit(solution)/shard_map/ppermute | solution.py:107
  142.4 3.7 %shard_map.68 = (f32[2,64,768]{2,1,0:T(8,128)S(1)}, bf16[2,64,768]{2,1,0:T(8,128)(2,1)S(1)}, f32[2,64,768]{2,1,0:T(8,128)S(1)}, bf16[2,64,768]{2,1,0:T(8,128)(2,1)S(1)}) custom-call(s32[4]{0:T(128)S(1)} %pad_add_fusion.place_ref, bf16[2,128,384]{2,1,0:T(8,128)(2,1)S(1)} %get-tuple-element.44.refs_0_, ...), custom_call_target="tpu_custom_call" | custom-call | flops 1207959552 | bytes 4718592 | tf_op jit(solution)/shard_map/pallas_call | solution.py:115
  146.2 1.6 collective-permute-start.21
  147.7 4.2 %collective-permute-done.21 = bf16[2,64,768]{2,1,0:T(8,128)(2,1)S(1)} collective-permute-done((bf16[2,64,768]{2,1,0:T(8,128)(2,1)S(1)}, bf16[2,64,768]{2,1,0:T(8,128)(2,1)S(1)}, u32[]{:S(2)}, u32[]{:S(2)}) %collective-permute-start.21) | collective-permute-done | bytes 196640 | tf_op jit(solution)/shard_map/ppermute | solution.py:107
  151.9 4.3 %collective-permute-start.23 = (bf16[2,64,768]{2,1,0:T(8,128)(2,1)S(1)}, bf16[2,64,768]{2,1,0:T(8,128)(2,1)S(1)}, u32[]{:S(2)}, u32[]{:S(2)}) collective-permute-start(bf16[2,64,768]{2,1,0:T(8,128)(2,1)S(1)} %add_convert_fusion), channel_id=1, source_target_pairs={{0,8},{4,12},{8,0},{12,4},{1,9},{5,13},{9,1},{13,5},{2,10},{6,14},... | collective-permute-start | bytes 589832 | tf_op jit(solution)/shard_map/ppermute | solution.py:107
  156.2 1.5 collective-permute-start.22
  157.7 6.1 %collective-permute-done.23.far_ref = bf16[2,64,768]{2,1,0:T(8,128)(2,1)S(1)} collective-permute-done((bf16[2,64,768]{2,1,0:T(8,128)(2,1)S(1)}, bf16[2,64,768]{2,1,0:T(8,128)(2,1)S(1)}, u32[]{:S(2)}, u32[]{:S(2)}) %collective-permute-start.23) | collective-permute-done | bytes 196640 | tf_op jit(solution)/shard_map/ppermute | solution.py:107
  163.8 1.3 shard_map.69
  (45 shorter events, 1.0 us)
Async XLA Ops:
  0.0 2.3 %copy-start = (bf16[1,128,3072]{2,1,0:T(8,128)(2,1)S(1)}, bf16[1,128,3072]{2,1,0:T(8,128)(2,1)}, u32[]{:S(2)}) copy-start(bf16[1,128,3072]{2,1,0:T(8,128)(2,1)} %param.6) | copy-start | bytes 2359300
  2.3 3.2 %copy-start.5 = (bf16[128,1536]{1,0:T(8,128)(2,1)}, bf16[128,1536]{1,0:T(8,128)(2,1)S(1)}, u32[]{:S(2)}) copy-start(bf16[128,1536]{1,0:T(8,128)(2,1)S(1)} %dynamic-slice_bitcast_fusion.2) | copy-start | bytes 1179652
  2.5 5.8 %copy-start.2 = (bf16[136,1536]{1,0:T(8,128)(2,1)}, bf16[136,1536]{1,0:T(8,128)(2,1)S(1)}, u32[]{:S(2)}) copy-start(bf16[136,1536]{1,0:T(8,128)(2,1)S(1)} %fusion.1.refs_0_) | copy-start | bytes 1253380
  2.5 16.0 %collective-permute-start = (bf16[136,1536]{1,0:T(8,128)(2,1)S(1)}, bf16[136,1536]{1,0:T(8,128)(2,1)}, u32[]{:S(2)}, u32[]{:S(2)}) collective-permute-start(bf16[136,1536]{1,0:T(8,128)(2,1)S(1)} %fusion.1.refs_0_), channel_id=1, source_target_pairs={{0,4},{4,0},{8,12},{12,8},{1,5},{5,1},{9,13},{13,9},{2,6},{6,2},{1... | collective-permute-start | bytes 1253384 | tf_op jit(solution)/shard_map/ppermute | solution.py:107
  5.6 12.9 %copy-start.1 = (bf16[768,768]{1,0:T(8,128)(2,1)S(1)}, bf16[768,768]{1,0:T(8,128)(2,1)}, u32[]{:S(2)}) copy-start(bf16[768,768]{1,0:T(8,128)(2,1)} %refs_4_.1) | copy-start | bytes 3538948
  8.2 10.3 %collective-permute-start.1 = (bf16[3,384,384]{2,1,0:T(8,128)(2,1)S(1)}, bf16[3,384,384]{2,1,0:T(8,128)(2,1)}, u32[]{:S(2)}, u32[]{:S(2)}) collective-permute-start(bf16[3,384,384]{2,1,0:T(8,128)(2,1)S(1)} %get-tuple-element.52), channel_id=1, source_target_pairs={{0,0},{1,8},{4,4},{5,12},{8,1},{9,9},{12,5},{13,13},{2,2},{3,10},{... | collective-permute-start | bytes 2654216 | tf_op jit(solution)/shard_map/ppermute | solution.py:338
  18.5 53.5 %collective-permute-start.3 = (bf16[768,768]{1,0:T(8,128)(2,1)S(1)}, bf16[768,768]{1,0:T(8,128)(2,1)S(1)}, u32[]{:S(2)}, u32[]{:S(2)}) collective-permute-start(bf16[768,768]{1,0:T(8,128)(2,1)S(1)} %copy-done.1), channel_id=1, source_target_pairs={{0,1},{1,0},{2,3},{3,2},{4,5},{5,4},{6,7},{7,6},{8,9},{9,8},{10,11... | collective-permute-start | bytes 3538952 | tf_op jit(solution)/shard_map/ppermute | solution.py:107
  18.5 55.2 %collective-permute-start.10 = (bf16[3,384,384]{2,1,0:T(8,128)(2,1)}, bf16[3,384,384]{2,1,0:T(8,128)(2,1)}, u32[]{:S(2)}, u32[]{:S(2)}) collective-permute-start(bf16[3,384,384]{2,1,0:T(8,128)(2,1)} %get-tuple-element.31), channel_id=1, source_target_pairs={{0,4},{1,12},{4,0},{5,8},{8,5},{9,13},{12,1},{13,9},{2,6},{3,14},{... | collective-permute-start | bytes 2654216 | tf_op jit(solution)/shard_map/ppermute | solution.py:338
  18.5 55.7 %collective-permute-start.9 = (bf16[3,384,384]{2,1,0:T(8,128)(2,1)}, bf16[3,384,384]{2,1,0:T(8,128)(2,1)}, u32[]{:S(2)}, u32[]{:S(2)}) collective-permute-start(bf16[3,384,384]{2,1,0:T(8,128)(2,1)} %collective-permute-done.1.refs_8_), channel_id=1, source_target_pairs={{0,16},{16,0},{1,17},{17,1},{2,18},{18,2},{3,19},{19,3},{4,20},{20... | collective-permute-start | bytes 2654216 | tf_op jit(solution)/shard_map/ppermute | solution.py:107
  20.3 50.0 %collective-permute-start.2 = (bf16[136,1536]{1,0:T(8,128)(2,1)}, bf16[136,1536]{1,0:T(8,128)(2,1)}, u32[]{:S(2)}, u32[]{:S(2)}) collective-permute-start(bf16[136,1536]{1,0:T(8,128)(2,1)} %copy-done.2), channel_id=1, source_target_pairs={{0,8},{4,12},{8,0},{12,4},{1,9},{5,13},{9,1},{13,5},{2,10},{6,14},... | collective-permute-start | bytes 1253384 | tf_op jit(solution)/shard_map/ppermute | solution.py:107
  36.6 33.9 %collective-permute-start.4 = (bf16[136,1536]{1,0:T(8,128)(2,1)}, bf16[136,1536]{1,0:T(8,128)(2,1)}, u32[]{:S(2)}, u32[]{:S(2)}) collective-permute-start(bf16[136,1536]{1,0:T(8,128)(2,1)} %collective-permute-done.refs_1_), channel_id=1, source_target_pairs={{0,2},{2,0},{1,3},{3,1},{4,6},{6,4},{5,7},{7,5},{8,10},{10,8},{9,1... | collective-permute-start | bytes 1253384 | tf_op jit(solution)/shard_map/ppermute | solution.py:107
  70.3 14.1 %collective-permute-start.12 = (bf16[384,768]{1,0:T(8,128)(2,1)}, bf16[384,768]{1,0:T(8,128)(2,1)}, u32[]{:S(2)}, u32[]{:S(2)}) collective-permute-start(bf16[384,768]{1,0:T(8,128)(2,1)} %constant_dynamic-slice_fusion), channel_id=1, source_target_pairs={{0,4},{4,0},{8,12},{12,8},{1,5},{5,1},{9,13},{13,9},{2,6},{6,2},{1... | collective-permute-start | bytes 1769480 | tf_op jit(solution)/shard_map/ppermute | solution.py:107
  70.5 28.0 %collective-permute-start.6 = (bf16[128,1536]{1,0:T(8,128)(2,1)}, bf16[128,1536]{1,0:T(8,128)(2,1)S(1)}, u32[]{:S(2)}, u32[]{:S(2)}) collective-permute-start(bf16[128,1536]{1,0:T(8,128)(2,1)} %copy-done.5), channel_id=1, source_target_pairs={{0,2},{2,0},{1,3},{3,1},{4,6},{6,4},{5,7},{7,5},{8,10},{10,8},{9,1... | collective-permute-start | bytes 1179656 | tf_op jit(solution)/shard_map/ppermute | solution.py:107
  72.0 22.3 %collective-permute-start.5 = (bf16[136,1536]{1,0:T(8,128)(2,1)}, bf16[136,1536]{1,0:T(8,128)(2,1)}, u32[]{:S(2)}, u32[]{:S(2)}) collective-permute-start(bf16[136,1536]{1,0:T(8,128)(2,1)} %copy-done.2), channel_id=1, source_target_pairs={{0,12},{4,8},{8,4},{12,0},{1,13},{5,9},{9,5},{13,1},{2,14},{6,10},... | collective-permute-start | bytes 1253384 | tf_op jit(solution)/shard_map/ppermute | solution.py:107
  73.7 24.8 %collective-permute-start.7 = (bf16[136,1536]{1,0:T(8,128)(2,1)}, bf16[136,1536]{1,0:T(8,128)(2,1)}, u32[]{:S(2)}, u32[]{:S(2)}) collective-permute-start(bf16[136,1536]{1,0:T(8,128)(2,1)} %collective-permute-done.2.refs_2_), channel_id=1, source_target_pairs={{0,2},{2,0},{1,3},{3,1},{4,6},{6,4},{5,7},{7,5},{8,10},{10,8},{9,1... | collective-permute-start | bytes 1253384 | tf_op jit(solution)/shard_map/ppermute | solution.py:107
  74.2 24.2 %collective-permute-start.11 = (bf16[3,384,384]{2,1,0:T(8,128)(2,1)}, bf16[3,384,384]{2,1,0:T(8,128)(2,1)}, u32[]{:S(2)}, u32[]{:S(2)}) collective-permute-start(bf16[3,384,384]{2,1,0:T(8,128)(2,1)} %collective-permute-done.10.refs_10_), channel_id=1, source_target_pairs={{0,16},{16,0},{1,17},{17,1},{2,18},{18,2},{3,19},{19,3},{4,20},{20... | collective-permute-start | bytes 2654216 | tf_op jit(solution)/shard_map/ppermute | solution.py:107
  84.4 29.0 %collective-permute-start.13 = (bf16[384,768]{1,0:T(8,128)(2,1)}, bf16[384,768]{1,0:T(8,128)(2,1)}, u32[]{:S(2)}, u32[]{:S(2)}) collective-permute-start(bf16[384,768]{1,0:T(8,128)(2,1)} %collective-permute-done.12.refs_6_), channel_id=1, source_target_pairs={{0,16},{16,0},{1,17},{17,1},{2,18},{18,2},{3,19},{19,3},{4,20},{20... | collective-permute-start | bytes 1769480 | tf_op jit(solution)/shard_map/ppermute | solution.py:107
  94.4 12.0 %collective-permute-start.8 = (bf16[136,1536]{1,0:T(8,128)(2,1)}, bf16[136,1536]{1,0:T(8,128)(2,1)}, u32[]{:S(2)}, u32[]{:S(2)}) collective-permute-start(bf16[136,1536]{1,0:T(8,128)(2,1)} %collective-permute-done.5.refs_3_), channel_id=1, source_target_pairs={{0,2},{2,0},{1,3},{3,1},{4,6},{6,4},{5,7},{7,5},{8,10},{10,8},{9,1... | collective-permute-start | bytes 1253384 | tf_op jit(solution)/shard_map/ppermute | solution.py:107
  106.4 1.0 copy-start.3
  107.4 6.0 %copy-start.4 = (bf16[136,1536]{1,0:T(8,128)(2,1)S(1)}, bf16[136,1536]{1,0:T(8,128)(2,1)}, u32[]{:S(2)}) copy-start(bf16[136,1536]{1,0:T(8,128)(2,1)} %copy-done.2) | copy-start | bytes 1253380
  113.3 5.9 %collective-permute-start.15 = (bf16[4,320,512]{2,1,0:T(8,128)(2,1)S(1)}, bf16[4,320,512]{2,1,0:T(8,128)(2,1)S(1)}, u32[]{:S(2)}, u32[]{:S(2)}) collective-permute-start(bf16[4,320,512]{2,1,0:T(8,128)(2,1)S(1)} %get-tuple-element.35), channel_id=1, source_target_pairs={{0,1},{1,0},{2,3},{3,2},{4,5},{5,4},{6,7},{7,6},{8,9},{9,8},{10,11... | collective-permute-start | bytes 3932168 | tf_op jit(solution)/shard_map/ppermute | solution.py:107
  118.1 4.9 %collective-permute-start.14 = (bf16[4,320,256]{2,1,0:T(8,128)(2,1)S(1)}, bf16[4,320,256]{2,1,0:T(8,128)(2,1)S(1)}, u32[]{:S(2)}, u32[]{:S(2)}) collective-permute-start(bf16[4,320,256]{2,1,0:T(8,128)(2,1)S(1)} %get-tuple-element.39), channel_id=1, source_target_pairs={{0,1},{1,0},{2,3},{3,2},{4,5},{5,4},{6,7},{7,6},{8,9},{9,8},{10,11... | collective-permute-start | bytes 1966088 | tf_op jit(solution)/shard_map/ppermute | solution.py:107
  118.6 11.0 %collective-permute-start.19 = (bf16[384,768]{1,0:T(8,128)(2,1)}, bf16[384,768]{1,0:T(8,128)(2,1)S(1)}, u32[]{:S(2)}, u32[]{:S(2)}) collective-permute-start(bf16[384,768]{1,0:T(8,128)(2,1)} %collective-permute-done.12.refs_6_), channel_id=1, source_target_pairs={{0,1},{1,0},{2,3},{3,2},{4,5},{5,4},{6,7},{7,6},{8,9},{9,8},{10,11... | collective-permute-start | bytes 1769480 | tf_op jit(solution)/shard_map/ppermute | solution.py:107
  118.7 10.9 %collective-permute-start.20 = (bf16[384,768]{1,0:T(8,128)(2,1)}, bf16[384,768]{1,0:T(8,128)(2,1)S(1)}, u32[]{:S(2)}, u32[]{:S(2)}) collective-permute-start(bf16[384,768]{1,0:T(8,128)(2,1)} %collective-permute-done.13.refs_7_), channel_id=1, source_target_pairs={{0,1},{1,0},{2,3},{3,2},{4,5},{5,4},{6,7},{7,6},{8,9},{9,8},{10,11... | collective-permute-start | bytes 1769480 | tf_op jit(solution)/shard_map/ppermute | solution.py:107
  125.2 8.8 %collective-permute-start.16 = (bf16[2,128,384]{2,1,0:T(8,128)(2,1)S(1)}, bf16[2,128,384]{2,1,0:T(8,128)(2,1)S(1)}, u32[]{:S(2)}, u32[]{:S(2)}) collective-permute-start(bf16[2,128,384]{2,1,0:T(8,128)(2,1)S(1)} %get-tuple-element.45), channel_id=1, source_target_pairs={{0,4},{4,0},{8,12},{12,8},{1,5},{5,1},{9,13},{13,9},{2,6},{6,2},{1... | collective-permute-start | bytes 589832 | tf_op jit(solution)/shard_map/ppermute | solution.py:107
  125.2 17.2 %collective-permute-start.17 = (bf16[2,128,384]{2,1,0:T(8,128)(2,1)S(1)}, bf16[2,128,384]{2,1,0:T(8,128)(2,1)S(1)}, u32[]{:S(2)}, u32[]{:S(2)}) collective-permute-start(bf16[2,128,384]{2,1,0:T(8,128)(2,1)S(1)} %get-tuple-element.44.refs_0_), channel_id=1, source_target_pairs={{0,8},{4,12},{8,0},{12,4},{1,9},{5,13},{9,1},{13,5},{2,10},{6,14},... | collective-permute-start | bytes 589832 | tf_op jit(solution)/shard_map/ppermute | solution.py:107
  126.1 16.3 %collective-permute-start.18 = (bf16[2,128,384]{2,1,0:T(8,128)(2,1)S(1)}, bf16[2,128,384]{2,1,0:T(8,128)(2,1)S(1)}, u32[]{:S(2)}, u32[]{:S(2)}) collective-permute-start(bf16[2,128,384]{2,1,0:T(8,128)(2,1)S(1)} %get-tuple-element.45), channel_id=1, source_target_pairs={{0,12},{4,8},{8,4},{12,0},{1,13},{5,9},{9,5},{13,1},{2,14},{6,10},... | collective-permute-start | bytes 589832 | tf_op jit(solution)/shard_map/ppermute | solution.py:107
  146.2 5.7 %collective-permute-start.21 = (bf16[2,64,768]{2,1,0:T(8,128)(2,1)S(1)}, bf16[2,64,768]{2,1,0:T(8,128)(2,1)S(1)}, u32[]{:S(2)}, u32[]{:S(2)}) collective-permute-start(bf16[2,64,768]{2,1,0:T(8,128)(2,1)S(1)} %get-tuple-element.48), channel_id=1, source_target_pairs={{0,2},{2,0},{1,3},{3,1},{4,6},{6,4},{5,7},{7,5},{8,10},{10,8},{9,1... | collective-permute-start | bytes 589832 | tf_op jit(solution)/shard_map/ppermute | solution.py:107
  151.9 11.9 %collective-permute-start.23 = (bf16[2,64,768]{2,1,0:T(8,128)(2,1)S(1)}, bf16[2,64,768]{2,1,0:T(8,128)(2,1)S(1)}, u32[]{:S(2)}, u32[]{:S(2)}) collective-permute-start(bf16[2,64,768]{2,1,0:T(8,128)(2,1)S(1)} %add_convert_fusion), channel_id=1, source_target_pairs={{0,8},{4,12},{8,0},{12,4},{1,9},{5,13},{9,1},{13,5},{2,10},{6,14},... | collective-permute-start | bytes 589832 | tf_op jit(solution)/shard_map/ppermute | solution.py:107
  156.2 7.6 %collective-permute-start.22 = (bf16[2,64,768]{2,1,0:T(8,128)(2,1)S(1)}, bf16[2,64,768]{2,1,0:T(8,128)(2,1)S(1)}, u32[]{:S(2)}, u32[]{:S(2)}) collective-permute-start(bf16[2,64,768]{2,1,0:T(8,128)(2,1)S(1)} %get-tuple-element.49), channel_id=1, source_target_pairs={{0,2},{2,0},{1,3},{3,1},{4,6},{6,4},{5,7},{7,5},{8,10},{10,8},{9,1... | collective-permute-start | bytes 589832 | tf_op jit(solution)/shard_map/ppermute | solution.py:107

commit v22 on v19

--- a/solution.py
+++ b/solution.py
@@ -146,24 +146,29 @@
                     source = w_refs[2 * k + g].at[part, :, first : first + cols]
                     into = w_all.at[pl.ds(at, half), part * cols : (part + 1) * cols]
                     copies.append(pltpu.make_async_copy(source, into, sems.at[len(copies)]))
+        fetch_x = []
         for i in range(2 * rows):
             to = x_all.at[row ^ (i % rows), (frame + i // rows) % 2]
-            copies.append(pltpu.make_async_copy(refs[i].at[pl.ds(0, count)], to, sems.at[len(copies)]))
-        for copy in copies:
+            fetch_x.append(pltpu.make_async_copy(refs[i].at[pl.ds(0, count)], to, sems.at[len(copies) + i]))
+        for copy in copies + fetch_x:
             copy.start()
         for copy in copies:
             copy.wait()
-        acc = jnp.dot(x_all[...].reshape(-1, width), w_all[...], preferred_element_type=jnp.float32)
-        kv_part = acc[:, cols:].reshape(rows, 2 * count, 2 * cols)
-        kv_keep[...] = kv_part
-        send[:, : 2 * count, :] = kv_part.astype(jnp.bfloat16)
-        total[...] = acc[:, :cols].reshape(rows, 2, count, cols)
-        own = pl.multiple_of(core * BS, BS)
-        other = pl.multiple_of((1 - core) * BS, BS)
-        q_keep[...] = total[:, :, pl.ds(own, BS), :].reshape(q_keep.shape)
-        for f in range(2):
-            at = slice(f * cols, (f + 1) * cols)
-            send[:, 2 * count :, at] = total[:, f, pl.ds(other, BS), :].astype(jnp.bfloat16)
+        for s in range(rows):
+            fetch_x[s].wait()
+            fetch_x[rows + s].wait()
+            at = row ^ s
+            acc = jnp.dot(x_all[at].reshape(-1, width), w_all[...], preferred_element_type=jnp.float32)
+            kv_part = acc[:, cols:]
+            kv_keep[at] = kv_part
+            send[at, : 2 * count, :] = kv_part.astype(jnp.bfloat16)
+            total[s] = acc[:, :cols].reshape(2, count, cols)
+            own = pl.multiple_of(core * BS, BS)
+            other = pl.multiple_of((1 - core) * BS, BS)
+            q_keep[at] = total[s, :, pl.ds(own, BS), :].reshape(2 * BS, cols)
+            for f in range(2):
+                where = slice(f * cols, (f + 1) * cols)
+                send[at, 2 * count :, where] = total[s, f, pl.ds(other, BS), :].astype(jnp.bfloat16)
 
     vmem, hbm = pl.BlockSpec(memory_space=pltpu.VMEM), pl.BlockSpec(memory_space=pltpu.HBM)
     flops = 2 * rows * 2 * count * width * 3 * cols
@@ -248,16 +253,17 @@
     )
 
 
-def mix(place, attended, w_own, w_across, beside, beside_across):
-    blocks, block_len, cols = attended[0].shape
+def mix(place, attended, w_own, w_across, beside, beside_across, far):
+    _, block_len, cols = attended[0].shape
     width = w_own.shape[1]
 
     def kernel(place_ref, *refs):
         row, group, frame, core = (place_ref[i] for i in range(4))
         w_refs = refs[4:10]
-        near_keep, near_send, far_keep, far_send, a_all, sums = refs[10:]
+        keep, send, a_all, sums = refs[10:]
+        block = 1 - row // 2 if far else row // 2
         for s in range(4):
-            a_all[s] = refs[s][...].reshape(blocks * block_len, cols)
+            a_all[s] = refs[s][block]
 
         def term(c, other):
             side = 1 - core if other else core
@@ -272,25 +278,21 @@
             return acc.astype(jnp.bfloat16).astype(jnp.float32)
 
         for c in range(2):
-            sums[...] = (term(c, 0) + term(c, 1)).reshape(blocks, 2, BS, width)
+            sums[...] = (term(c, 0) + term(c, 1)).reshape(2, BS, width)
             at = (row + c) % 2
-            near_keep[at] = sums[row // 2, frame]
-            near_send[at] = sums[row // 2, 1 - frame].astype(jnp.bfloat16)
-            far_keep[at] = sums[1 - row // 2, frame]
-            far_send[at] = sums[1 - row // 2, 1 - frame].astype(jnp.bfloat16)
-
-    kept = jax.ShapeDtypeStruct((2, BS, width), jnp.float32)
-    sent = jax.ShapeDtypeStruct((2, BS, width), jnp.bfloat16)
+            keep[at] = sums[frame]
+            send[at] = sums[1 - frame].astype(jnp.bfloat16)
+
     return call(
         kernel,
-        (kept, sent, kept, sent),
+        (
+            jax.ShapeDtypeStruct((2, BS, width), jnp.float32),
+            jax.ShapeDtypeStruct((2, BS, width), jnp.bfloat16),
+        ),
         [place],
         [*attended, w_own, w_across, *beside, *beside_across],
-        scratch=[
-            pltpu.VMEM((4, blocks * block_len, cols), jnp.bfloat16),
-            pltpu.VMEM((blocks, 2, BS, width), jnp.float32),
-        ],
-        flops=2 * blocks * block_len * 4 * cols * 2 * width,
+        scratch=[pltpu.VMEM((4, block_len, cols), jnp.bfloat16), pltpu.VMEM((2, BS, width), jnp.float32)],
+        flops=2 * block_len * 4 * cols * 2 * width,
         read=16 * cols * width,
     )
 
@@ -377,7 +379,9 @@
     beside_across = [swap(part, "heads") for part in beside]
     same, diff = attend_all(place, members, counts, *second[:2], second_more, attended)
     attended = [same] + [swap(same if s % 2 == 0 else diff, "rows", s) for s in range(1, rows_n)]
-    near_keep, near_send, far_keep, far_send = mix(place, attended, w_out, across, beside, beside_across)
+    weights = w_out, across, beside, beside_across
+    far_keep, far_send = mix(place, attended, *weights, True)
+    near_keep, near_send = mix(place, attended, *weights, False)
     far_more = swap(far_send, "frames")
     far = swap((far_keep + far_more.astype(jnp.float32)).astype(jnp.bfloat16), "rows", 2)
     near_more = swap(after(near_send, far_more), "frames")

time: 161 us -> 160 us (level)
  waiting for transfers between devices: 93.4 us -> 89.8 us
  Pallas kernels: 21.4 us -> 23.8 us
    ppermute x22, waiting for transfers between devices: 93.4 us -> 89.8 us  [swap(): return lax.ppermute(value, axis, [(i, i ^ step) for i in range(peers)])]
    pallas_call x4 -> x5, Pallas kernels: 11 us -> 13 us  [call(): pl.pallas_call(kernel, out_shape=out_shape, grid_spec=pltpu.PrefetchScala...]
  transfers between devices with their start and end apart: 24 -> 24, of which waited for: 11 -> 11; matrix products, arithmetic and copies ran while one was open for 4% -> 4% of each run, Pallas kernels for 7% -> 8%
where the time goes in v22:
time: 160 us
  waiting for transfers between devices  89.8 us (56%)
  starting transfers between devices  33.7 us (21%)
  Pallas kernels  23.8 us (15%)
  local copies, waits for them, and re-layouts  9.46 us (6%)
  other arithmetic  2.7 us (2%)
    ppermute x22, waiting for transfers between devices, swap(): return lax.ppermute(value, axis, [(i, i ^ step) for i in range(peers)])  89.8 us
    ppermute x22, starting transfers between devices, swap(): return lax.ppermute(value, axis, [(i, i ^ step) for i in range(peers)])  32.1 us
    pallas_call x5, Pallas kernels, call(): pl.pallas_call(kernel, out_shape=out_shape, grid_spec=pltpu.PrefetchScala...  13 us
    pallas_call x2, Pallas kernels, project(): pl.pallas_call(kernel, out_shape=(jax.ShapeDtypeStruct((rows, 2 * BS, col...  10.8 us
  transfers between devices with their start and end apart: 24, of which 11 were waited for; matrix products, arithmetic and copies ran while one was open for 4% of the time, Pallas kernels for 8%

profile of v22, /device:TPU:0, one launch (start us, length us, event | category | flops | bytes accessed | tf_op | source)
XLA Modules:
  0.0 159.5 jit_solution(3374674308616143054)
XLA Ops:
  0.0 0.7 convert_bitcast_fusion
  0.8 0.7 convert_bitcast_fusion.1
  1.6 0.7 convert.13
  2.5 3.1 %collective-permute-start = (bf16[136,1536]{1,0:T(8,128)(2,1)S(1)}, bf16[136,1536]{1,0:T(8,128)(2,1)}, u32[]{:S(2)}, u32[]{:S(2)}) collective-permute-start(bf16[136,1536]{1,0:T(8,128)(2,1)S(1)} %fusion.1.refs_0_), channel_id=1, source_target_pairs={{0,4},{4,0},{8,12},{12,8},{1,5},{5,1},{9,13},{13,9},{2,6},{6,2},{1... | collective-permute-start | bytes 1253384 | tf_op jit(solution)/shard_map/ppermute | solution.py:107
  5.6 2.7 %dynamic-slice_bitcast_fusion = (bf16[3,384,384]{2,1,0:T(8,128)(2,1)}, bf16[3,384,384]{2,1,0:T(8,128)(2,1)S(1)}) fusion(bf16[768,3,768]{2,0,1:T(8,128)(2,1)} %param.7, s32[]{:T(128)S(6)} %select_n.44, s32[]{:T(128)S(6)} %select_n.51, s32[]{:T(128)S(6)} %select_n.46), kind=kLoop, calls=%fused_computation.2 | loop fusion | bytes 3538956 | tf_op jit(solution)/shard_map/dynamic_slice | solution.py:332
  8.2 1.6 collective-permute-start.1
  9.8 8.7 %collective-permute-done.refs_1_ = bf16[136,1536]{1,0:T(8,128)(2,1)} collective-permute-done((bf16[136,1536]{1,0:T(8,128)(2,1)S(1)}, bf16[136,1536]{1,0:T(8,128)(2,1)}, u32[]{:S(2)}, u32[]{:S(2)}) %collective-permute-start) | collective-permute-done | bytes 417824 | tf_op jit(solution)/shard_map/ppermute | solution.py:107
  18.5 1.7 %collective-permute-start.2 = (bf16[128,1536]{1,0:T(8,128)(2,1)S(1)}, bf16[128,1536]{1,0:T(8,128)(2,1)S(1)}, u32[]{:S(2)}, u32[]{:S(2)}) collective-permute-start(bf16[128,1536]{1,0:T(8,128)(2,1)S(1)} %copy-done.9), channel_id=1, source_target_pairs={{0,2},{2,0},{1,3},{3,1},{4,6},{6,4},{5,7},{7,5},{8,10},{10,8},{9,1... | collective-permute-start | bytes 1179656 | tf_op jit(solution)/shard_map/ppermute | solution.py:107
  20.4 0.4 collective-permute-start.5
  20.8 9.7 %collective-permute-done.2.refs_4_ = bf16[128,1536]{1,0:T(8,128)(2,1)S(1)} collective-permute-done((bf16[128,1536]{1,0:T(8,128)(2,1)S(1)}, bf16[128,1536]{1,0:T(8,128)(2,1)S(1)}, u32[]{:S(2)}, u32[]{:S(2)}) %collective-permute-start.2) | collective-permute-done | bytes 393248 | tf_op jit(solution)/shard_map/ppermute | solution.py:107
  30.5 1.7 %collective-permute-start.10 = (bf16[3,384,384]{2,1,0:T(8,128)(2,1)}, bf16[3,384,384]{2,1,0:T(8,128)(2,1)}, u32[]{:S(2)}, u32[]{:S(2)}) collective-permute-start(bf16[3,384,384]{2,1,0:T(8,128)(2,1)} %collective-permute-done.1.refs_8_), channel_id=1, source_target_pairs={{0,16},{16,0},{1,17},{17,1},{2,18},{18,2},{3,19},{19,3},{4,20},{20... | collective-permute-start | bytes 2654216 | tf_op jit(solution)/shard_map/ppermute | solution.py:107
  32.2 6.8 %collective-permute-done.5.refs_5_ = bf16[136,1536]{1,0:T(8,128)(2,1)S(1)} collective-permute-done((bf16[136,1536]{1,0:T(8,128)(2,1)}, bf16[136,1536]{1,0:T(8,128)(2,1)S(1)}, u32[]{:S(2)}, u32[]{:S(2)}) %collective-permute-start.5) | collective-permute-done | bytes 417824 | tf_op jit(solution)/shard_map/ppermute | solution.py:107
  39.0 0.8 copy-done.5
  39.8 0.8 collective-permute-start.3
  40.5 1.6 collective-permute-done.6.refs_6_
  42.1 1.5 collective-permute-start.12
  43.9 26.4 %collective-permute-done.3.refs_2_ = bf16[136,1536]{1,0:T(8,128)(2,1)} collective-permute-done((bf16[136,1536]{1,0:T(8,128)(2,1)}, bf16[136,1536]{1,0:T(8,128)(2,1)}, u32[]{:S(2)}, u32[]{:S(2)}) %collective-permute-start.3) | collective-permute-done | bytes 417824 | tf_op jit(solution)/shard_map/ppermute | solution.py:107
  70.4 2.4 %collective-permute-start.7 = (bf16[136,1536]{1,0:T(8,128)(2,1)}, bf16[136,1536]{1,0:T(8,128)(2,1)}, u32[]{:S(2)}, u32[]{:S(2)}) collective-permute-start(bf16[136,1536]{1,0:T(8,128)(2,1)} %copy-done.2), channel_id=1, source_target_pairs={{0,12},{4,8},{8,4},{12,0},{1,13},{5,9},{9,5},{13,1},{2,14},{6,10},... | collective-permute-start | bytes 1253384 | tf_op jit(solution)/shard_map/ppermute | solution.py:107
  72.7 0.7 slice_bitcast_fusion.2
  73.4 1.6 collective-permute-start.8
  75.0 1.5 collective-permute-start.13
  76.5 0.7 slice_bitcast_fusion.1
  77.1 6.5 %collective-permute-done.7.refs_3_ = bf16[136,1536]{1,0:T(8,128)(2,1)} collective-permute-done((bf16[136,1536]{1,0:T(8,128)(2,1)}, bf16[136,1536]{1,0:T(8,128)(2,1)}, u32[]{:S(2)}, u32[]{:S(2)}) %collective-permute-start.7) | collective-permute-done | bytes 417824 | tf_op jit(solution)/shard_map/ppermute | solution.py:107
  83.6 2.1 %collective-permute-start.9 = (bf16[136,1536]{1,0:T(8,128)(2,1)}, bf16[136,1536]{1,0:T(8,128)(2,1)}, u32[]{:S(2)}, u32[]{:S(2)}) collective-permute-start(bf16[136,1536]{1,0:T(8,128)(2,1)} %collective-permute-done.7.refs_3_), channel_id=1, source_target_pairs={{0,2},{2,0},{1,3},{3,1},{4,6},{6,4},{5,7},{7,5},{8,10},{10,8},{9,1... | collective-permute-start | bytes 1253384 | tf_op jit(solution)/shard_map/ppermute | solution.py:107
  85.7 0.7 slice_bitcast_fusion
  86.4 0.6 gather_fusion
  87.4 0.6 gather_fusion.1
  88.3 7.6 %collective-permute-done.13.refs_11_ = bf16[3,384,384]{2,1,0:T(8,128)(2,1)} collective-permute-done((bf16[3,384,384]{2,1,0:T(8,128)(2,1)}, bf16[3,384,384]{2,1,0:T(8,128)(2,1)}, u32[]{:S(2)}, u32[]{:S(2)}) %collective-permute-start.13) | collective-permute-done | bytes 884768 | tf_op jit(solution)/shard_map/ppermute | solution.py:107
  95.9 1.0 copy-done.3
  96.9 1.0 copy-done.6
  97.9 6.4 %shard_map.64 = (f32[4,128,256]{2,1,0:T(8,128)S(1)}, f32[4,256,512]{2,1,0:T(8,128)S(1)}, bf16[4,320,512]{2,1,0:T(8,128)(2,1)S(1)}) custom-call(s32[4]{0:T(128)S(1)} %pad_add_fusion.place_ref, bf16[136,1536]{1,0:T(8,128)(2,1)S(1)} %copy-done.3, bf16[136,1536]{1,0:T(8,128)(2,1)} %collective-permute-done.refs_1_, ...), custom_call_target="tpu_custom_call" | custom-call | flops 19327352832 | bytes 8053063 | tf_op jit(solution)/shard_map/pallas_call | solution.py:175
  104.3 4.4 %shard_map.65 = (f32[4,128,128]{2,1,0:T(8,128)S(1)}, f32[4,256,256]{2,1,0:T(8,128)S(1)}, bf16[4,320,256]{2,1,0:T(8,128)(2,1)S(1)}) custom-call(s32[4]{0:T(128)S(1)} %pad_add_fusion.place_ref, bf16[136,1536]{1,0:T(8,128)(2,1)S(1)} %copy-done.4, bf16[136,1536]{1,0:T(8,128)(2,1)} %collective-permute-done.refs_1_, ...), custom_call_target="tpu_custom_call" | custom-call | flops 9663676416 | bytes 4026531 | tf_op jit(solution)/shard_map/pallas_call | solution.py:175
  108.8 0.5 collective-permute-start.14
  109.4 0.4 collective-permute-start.20
  109.8 3.8 %shard_map.66 = (bf16[2,128,256]{2,1,0:T(8,128)(2,1)S(1)}, bf16[2,128,256]{2,1,0:T(8,128)(2,1)S(1)}) custom-call(s32[4]{0:T(128)S(1)} %pad_add_fusion.place_ref, s32[16]{0:T(128)S(1)} %reshape.24.members_ref, s32[4]{0:T(128)S(1)} %slice_reduce_fusion.1.counts_ref, f32[4,128,256]{2,1,0:T(8,128)S(1)} %get-tuple-element.40.q_ref, ...), custom_call_target="tpu_custom_call" | custom-call | flops 268435456 | bytes 2097152 | tf_op jit(solution)/shard_map/pallas_call | solution.py:115
  113.6 2.2 %shard_map.67 = (bf16[2,128,384]{2,1,0:T(8,128)(2,1)S(1)}, bf16[2,128,384]{2,1,0:T(8,128)(2,1)S(1)}) custom-call(s32[4]{0:T(128)S(1)} %pad_add_fusion.place_ref, s32[16]{0:T(128)S(1)} %reshape.24.members_ref, s32[4]{0:T(128)S(1)} %slice_reduce_fusion.1.counts_ref, f32[4,128,128]{2,1,0:T(8,128)S(1)} %get-tuple-element.37.q_ref, ...), custom_call_target="tpu_custom_call" | custom-call | flops 134217728 | bytes 1048576 | tf_op jit(solution)/shard_map/pallas_call | solution.py:115
  115.8 5.5 %collective-permute-start.16 = (bf16[2,128,384]{2,1,0:T(8,128)(2,1)S(1)}, bf16[2,128,384]{2,1,0:T(8,128)(2,1)S(1)}, u32[]{:S(2)}, u32[]{:S(2)}) collective-permute-start(bf16[2,128,384]{2,1,0:T(8,128)(2,1)S(1)} %get-tuple-element.45), channel_id=1, source_target_pairs={{0,4},{4,0},{8,12},{12,8},{1,5},{5,1},{9,13},{13,9},{2,6},{6,2},{1... | collective-permute-start | bytes 589832 | tf_op jit(solution)/shard_map/ppermute | solution.py:107
  121.4 2.4 %collective-permute-start.18 = (bf16[2,128,384]{2,1,0:T(8,128)(2,1)S(1)}, bf16[2,128,384]{2,1,0:T(8,128)(2,1)S(1)}, u32[]{:S(2)}, u32[]{:S(2)}) collective-permute-start(bf16[2,128,384]{2,1,0:T(8,128)(2,1)S(1)} %get-tuple-element.45), channel_id=1, source_target_pairs={{0,12},{4,8},{8,4},{12,0},{1,13},{5,9},{9,5},{13,1},{2,14},{6,10},... | collective-permute-start | bytes 589832 | tf_op jit(solution)/shard_map/ppermute | solution.py:107
  123.8 5.5 %collective-permute-done.16.refs_1_ = bf16[2,128,384]{2,1,0:T(8,128)(2,1)S(1)} collective-permute-done((bf16[2,128,384]{2,1,0:T(8,128)(2,1)S(1)}, bf16[2,128,384]{2,1,0:T(8,128)(2,1)S(1)}, u32[]{:S(2)}, u32[]{:S(2)}) %collective-permute-start.16) | collective-permute-done | bytes 196640 | tf_op jit(solution)/shard_map/ppermute | solution.py:107
  129.3 9.2 %collective-permute-done.17.refs_2_ = bf16[2,128,384]{2,1,0:T(8,128)(2,1)S(1)} collective-permute-done((bf16[2,128,384]{2,1,0:T(8,128)(2,1)S(1)}, bf16[2,128,384]{2,1,0:T(8,128)(2,1)S(1)}, u32[]{:S(2)}, u32[]{:S(2)}) %collective-permute-start.17) | collective-permute-done | bytes 196640 | tf_op jit(solution)/shard_map/ppermute | solution.py:107
  138.5 2.8 %shard_map.69 = (f32[2,64,768]{2,1,0:T(8,128)S(1)}, bf16[2,64,768]{2,1,0:T(8,128)(2,1)S(1)}) custom-call(s32[4]{0:T(128)S(1)} %pad_add_fusion.place_ref, bf16[2,128,384]{2,1,0:T(8,128)(2,1)S(1)} %get-tuple-element.44.refs_0_, bf16[2,128,384]{2,1,0:T(8,128)(2,1)S(1)} %collective-permute-done.16.refs_1_, ...), custom_call_target="tpu_custom_call" | custom-call | flops 603979776 | bytes 4718592 | tf_op jit(solution)/shard_map/pallas_call | solution.py:115
  141.3 1.0 collective-permute-start.21
  142.3 2.8 %shard_map.68 = (f32[2,64,768]{2,1,0:T(8,128)S(1)}, bf16[2,64,768]{2,1,0:T(8,128)(2,1)S(1)}) custom-call(s32[4]{0:T(128)S(1)} %pad_add_fusion.place_ref, bf16[2,128,384]{2,1,0:T(8,128)(2,1)S(1)} %get-tuple-element.44.refs_0_, bf16[2,128,384]{2,1,0:T(8,128)(2,1)S(1)} %collective-permute-done.16.refs_1_, ...), custom_call_target="tpu_custom_call" | custom-call | flops 603979776 | bytes 4718592 | tf_op jit(solution)/shard_map/pallas_call | solution.py:115
  145.1 1.9 %collective-permute-done.21 = bf16[2,64,768]{2,1,0:T(8,128)(2,1)S(1)} collective-permute-done((bf16[2,64,768]{2,1,0:T(8,128)(2,1)S(1)}, bf16[2,64,768]{2,1,0:T(8,128)(2,1)S(1)}, u32[]{:S(2)}, u32[]{:S(2)}) %collective-permute-start.21) | collective-permute-done | bytes 196640 | tf_op jit(solution)/shard_map/ppermute | solution.py:107
  147.1 3.5 %collective-permute-start.23 = (bf16[2,64,768]{2,1,0:T(8,128)(2,1)S(1)}, bf16[2,64,768]{2,1,0:T(8,128)(2,1)S(1)}, u32[]{:S(2)}, u32[]{:S(2)}) collective-permute-start(bf16[2,64,768]{2,1,0:T(8,128)(2,1)S(1)} %add_convert_fusion), channel_id=1, source_target_pairs={{0,8},{4,12},{8,0},{12,4},{1,9},{5,13},{9,1},{13,5},{2,10},{6,14},... | collective-permute-start | bytes 589832 | tf_op jit(solution)/shard_map/ppermute | solution.py:107
  150.6 1.7 %collective-permute-start.22 = (bf16[2,64,768]{2,1,0:T(8,128)(2,1)S(1)}, bf16[2,64,768]{2,1,0:T(8,128)(2,1)S(1)}, u32[]{:S(2)}, u32[]{:S(2)}) collective-permute-start(bf16[2,64,768]{2,1,0:T(8,128)(2,1)S(1)} %get-tuple-element.49), channel_id=1, source_target_pairs={{0,2},{2,0},{1,3},{3,1},{4,6},{6,4},{5,7},{7,5},{8,10},{10,8},{9,1... | collective-permute-start | bytes 589832 | tf_op jit(solution)/shard_map/ppermute | solution.py:107
  152.3 5.9 %collective-permute-done.23.far_ref = bf16[2,64,768]{2,1,0:T(8,128)(2,1)S(1)} collective-permute-done((bf16[2,64,768]{2,1,0:T(8,128)(2,1)S(1)}, bf16[2,64,768]{2,1,0:T(8,128)(2,1)S(1)}, u32[]{:S(2)}, u32[]{:S(2)}) %collective-permute-start.23) | collective-permute-done | bytes 196640 | tf_op jit(solution)/shard_map/ppermute | solution.py:107
  158.2 1.3 shard_map.70
  (54 shorter events, 1.7 us)
Async XLA Ops:
  0.0 2.3 %copy-start = (bf16[1,128,3072]{2,1,0:T(8,128)(2,1)S(1)}, bf16[1,128,3072]{2,1,0:T(8,128)(2,1)}, u32[]{:S(2)}) copy-start(bf16[1,128,3072]{2,1,0:T(8,128)(2,1)} %param.6) | copy-start | bytes 2359300
  2.3 3.2 %copy-start.8 = (bf16[128,1536]{1,0:T(8,128)(2,1)}, bf16[128,1536]{1,0:T(8,128)(2,1)S(1)}, u32[]{:S(2)}) copy-start(bf16[128,1536]{1,0:T(8,128)(2,1)S(1)} %dynamic-slice_bitcast_fusion.2) | copy-start | bytes 1179652
  2.5 5.8 %copy-start.2 = (bf16[136,1536]{1,0:T(8,128)(2,1)}, bf16[136,1536]{1,0:T(8,128)(2,1)S(1)}, u32[]{:S(2)}) copy-start(bf16[136,1536]{1,0:T(8,128)(2,1)S(1)} %fusion.1.refs_0_) | copy-start | bytes 1253380
  2.5 16.0 %collective-permute-start = (bf16[136,1536]{1,0:T(8,128)(2,1)S(1)}, bf16[136,1536]{1,0:T(8,128)(2,1)}, u32[]{:S(2)}, u32[]{:S(2)}) collective-permute-start(bf16[136,1536]{1,0:T(8,128)(2,1)S(1)} %fusion.1.refs_0_), channel_id=1, source_target_pairs={{0,4},{4,0},{8,12},{12,8},{1,5},{5,1},{9,13},{13,9},{2,6},{6,2},{1... | collective-permute-start | bytes 1253384 | tf_op jit(solution)/shard_map/ppermute | solution.py:107
  5.6 12.9 %copy-start.1 = (bf16[768,768]{1,0:T(8,128)(2,1)S(1)}, bf16[768,768]{1,0:T(8,128)(2,1)}, u32[]{:S(2)}) copy-start(bf16[768,768]{1,0:T(8,128)(2,1)} %refs_4_.3) | copy-start | bytes 3538948
  5.6 12.9 %copy-start.9 = (bf16[128,1536]{1,0:T(8,128)(2,1)S(1)}, bf16[128,1536]{1,0:T(8,128)(2,1)}, u32[]{:S(2)}) copy-start(bf16[128,1536]{1,0:T(8,128)(2,1)} %copy-done.8) | copy-start | bytes 1179652
  8.2 22.3 %collective-permute-start.1 = (bf16[3,384,384]{2,1,0:T(8,128)(2,1)S(1)}, bf16[3,384,384]{2,1,0:T(8,128)(2,1)}, u32[]{:S(2)}, u32[]{:S(2)}) collective-permute-start(bf16[3,384,384]{2,1,0:T(8,128)(2,1)S(1)} %get-tuple-element.52), channel_id=1, source_target_pairs={{0,0},{1,8},{4,4},{5,12},{8,1},{9,9},{12,5},{13,13},{2,2},{3,10},{... | collective-permute-start | bytes 2654216 | tf_op jit(solution)/shard_map/ppermute | solution.py:340
  18.5 51.9 %collective-permute-start.4 = (bf16[768,768]{1,0:T(8,128)(2,1)S(1)}, bf16[768,768]{1,0:T(8,128)(2,1)S(1)}, u32[]{:S(2)}, u32[]{:S(2)}) collective-permute-start(bf16[768,768]{1,0:T(8,128)(2,1)S(1)} %copy-done.1), channel_id=1, source_target_pairs={{0,1},{1,0},{2,3},{3,2},{4,5},{5,4},{6,7},{7,6},{8,9},{9,8},{10,11... | collective-permute-start | bytes 3538952 | tf_op jit(solution)/shard_map/ppermute | solution.py:107
  18.5 12.0 %collective-permute-start.2 = (bf16[128,1536]{1,0:T(8,128)(2,1)S(1)}, bf16[128,1536]{1,0:T(8,128)(2,1)S(1)}, u32[]{:S(2)}, u32[]{:S(2)}) collective-permute-start(bf16[128,1536]{1,0:T(8,128)(2,1)S(1)} %copy-done.9), channel_id=1, source_target_pairs={{0,2},{2,0},{1,3},{3,1},{4,6},{6,4},{5,7},{7,5},{8,10},{10,8},{9,1... | collective-permute-start | bytes 1179656 | tf_op jit(solution)/shard_map/ppermute | solution.py:107
  20.3 21.9 %collective-permute-start.6 = (bf16[384,768]{1,0:T(8,128)(2,1)S(1)}, bf16[384,768]{1,0:T(8,128)(2,1)}, u32[]{:S(2)}, u32[]{:S(2)}) collective-permute-start(bf16[384,768]{1,0:T(8,128)(2,1)S(1)} %constant_dynamic-slice_fusion), channel_id=1, source_target_pairs={{0,4},{4,0},{8,12},{12,8},{1,5},{5,1},{9,13},{13,9},{2,6},{6,2},{1... | collective-permute-start | bytes 1769480 | tf_op jit(solution)/shard_map/ppermute | solution.py:107
  20.4 18.6 %collective-permute-start.5 = (bf16[136,1536]{1,0:T(8,128)(2,1)}, bf16[136,1536]{1,0:T(8,128)(2,1)S(1)}, u32[]{:S(2)}, u32[]{:S(2)}) collective-permute-start(bf16[136,1536]{1,0:T(8,128)(2,1)} %collective-permute-done.refs_1_), channel_id=1, source_target_pairs={{0,2},{2,0},{1,3},{3,1},{4,6},{6,4},{5,7},{7,5},{8,10},{10,8},{9,1... | collective-permute-start | bytes 1253384 | tf_op jit(solution)/shard_map/ppermute | solution.py:107
  30.5 44.5 %collective-permute-start.11 = (bf16[3,384,384]{2,1,0:T(8,128)(2,1)}, bf16[3,384,384]{2,1,0:T(8,128)(2,1)}, u32[]{:S(2)}, u32[]{:S(2)}) collective-permute-start(bf16[3,384,384]{2,1,0:T(8,128)(2,1)} %get-tuple-element.32), channel_id=1, source_target_pairs={{0,4},{1,12},{4,0},{5,8},{8,5},{9,13},{12,1},{13,9},{2,6},{3,14},{... | collective-permute-start | bytes 2654216 | tf_op jit(solution)/shard_map/ppermute | solution.py:340
  30.5 44.5 %collective-permute-start.10 = (bf16[3,384,384]{2,1,0:T(8,128)(2,1)}, bf16[3,384,384]{2,1,0:T(8,128)(2,1)}, u32[]{:S(2)}, u32[]{:S(2)}) collective-permute-start(bf16[3,384,384]{2,1,0:T(8,128)(2,1)} %collective-permute-done.1.refs_8_), channel_id=1, source_target_pairs={{0,16},{16,0},{1,17},{17,1},{2,18},{18,2},{3,19},{19,3},{4,20},{20... | collective-permute-start | bytes 2654216 | tf_op jit(solution)/shard_map/ppermute | solution.py:107
  39.0 0.8 copy-start.5
  39.8 30.6 %collective-permute-start.3 = (bf16[136,1536]{1,0:T(8,128)(2,1)}, bf16[136,1536]{1,0:T(8,128)(2,1)}, u32[]{:S(2)}, u32[]{:S(2)}) collective-permute-start(bf16[136,1536]{1,0:T(8,128)(2,1)} %copy-done.2), channel_id=1, source_target_pairs={{0,8},{4,12},{8,0},{12,4},{1,9},{5,13},{9,1},{13,5},{2,10},{6,14},... | collective-permute-start | bytes 1253384 | tf_op jit(solution)/shard_map/ppermute | solution.py:107
  42.1 32.9 %collective-permute-start.12 = (bf16[384,768]{1,0:T(8,128)(2,1)}, bf16[384,768]{1,0:T(8,128)(2,1)}, u32[]{:S(2)}, u32[]{:S(2)}) collective-permute-start(bf16[384,768]{1,0:T(8,128)(2,1)} %collective-permute-done.6.refs_6_), channel_id=1, source_target_pairs={{0,16},{16,0},{1,17},{17,1},{2,18},{18,2},{3,19},{19,3},{4,20},{20... | collective-permute-start | bytes 1769480 | tf_op jit(solution)/shard_map/ppermute | solution.py:107
  70.4 13.3 %collective-permute-start.7 = (bf16[136,1536]{1,0:T(8,128)(2,1)}, bf16[136,1536]{1,0:T(8,128)(2,1)}, u32[]{:S(2)}, u32[]{:S(2)}) collective-permute-start(bf16[136,1536]{1,0:T(8,128)(2,1)} %copy-done.2), channel_id=1, source_target_pairs={{0,12},{4,8},{8,4},{12,0},{1,13},{5,9},{9,5},{13,1},{2,14},{6,10},... | collective-permute-start | bytes 1253384 | tf_op jit(solution)/shard_map/ppermute | solution.py:107
  73.4 22.5 %collective-permute-start.8 = (bf16[136,1536]{1,0:T(8,128)(2,1)}, bf16[136,1536]{1,0:T(8,128)(2,1)}, u32[]{:S(2)}, u32[]{:S(2)}) collective-permute-start(bf16[136,1536]{1,0:T(8,128)(2,1)} %collective-permute-done.3.refs_2_), channel_id=1, source_target_pairs={{0,2},{2,0},{1,3},{3,1},{4,6},{6,4},{5,7},{7,5},{8,10},{10,8},{9,1... | collective-permute-start | bytes 1253384 | tf_op jit(solution)/shard_map/ppermute | solution.py:107
  75.0 20.9 %collective-permute-start.13 = (bf16[3,384,384]{2,1,0:T(8,128)(2,1)}, bf16[3,384,384]{2,1,0:T(8,128)(2,1)}, u32[]{:S(2)}, u32[]{:S(2)}) collective-permute-start(bf16[3,384,384]{2,1,0:T(8,128)(2,1)} %collective-permute-done.11.refs_10_), channel_id=1, source_target_pairs={{0,16},{16,0},{1,17},{17,1},{2,18},{18,2},{3,19},{19,3},{4,20},{20... | collective-permute-start | bytes 2654216 | tf_op jit(solution)/shard_map/ppermute | solution.py:107
  83.6 12.2 %collective-permute-start.9 = (bf16[136,1536]{1,0:T(8,128)(2,1)}, bf16[136,1536]{1,0:T(8,128)(2,1)}, u32[]{:S(2)}, u32[]{:S(2)}) collective-permute-start(bf16[136,1536]{1,0:T(8,128)(2,1)} %collective-permute-done.7.refs_3_), channel_id=1, source_target_pairs={{0,2},{2,0},{1,3},{3,1},{4,6},{6,4},{5,7},{7,5},{8,10},{10,8},{9,1... | collective-permute-start | bytes 1253384 | tf_op jit(solution)/shard_map/ppermute | solution.py:107
  95.9 1.0 copy-start.3
  96.9 1.0 copy-start.6
  97.9 6.4 %copy-start.4 = (bf16[136,1536]{1,0:T(8,128)(2,1)S(1)}, bf16[136,1536]{1,0:T(8,128)(2,1)}, u32[]{:S(2)}) copy-start(bf16[136,1536]{1,0:T(8,128)(2,1)} %copy-done.2) | copy-start | bytes 1253380
  97.9 6.5 %copy-start.7 = (bf16[136,1536]{1,0:T(8,128)(2,1)S(1)}, bf16[136,1536]{1,0:T(8,128)(2,1)}, u32[]{:S(2)}) copy-start(bf16[136,1536]{1,0:T(8,128)(2,1)} %copy-done.5) | copy-start | bytes 1253380
  104.2 5.6 %collective-permute-start.15 = (bf16[4,320,512]{2,1,0:T(8,128)(2,1)S(1)}, bf16[4,320,512]{2,1,0:T(8,128)(2,1)S(1)}, u32[]{:S(2)}, u32[]{:S(2)}) collective-permute-start(bf16[4,320,512]{2,1,0:T(8,128)(2,1)S(1)} %get-tuple-element.35), channel_id=1, source_target_pairs={{0,1},{1,0},{2,3},{3,2},{4,5},{5,4},{6,7},{7,6},{8,9},{9,8},{10,11... | collective-permute-start | bytes 3932168 | tf_op jit(solution)/shard_map/ppermute | solution.py:107
  108.8 4.8 %collective-permute-start.14 = (bf16[4,320,256]{2,1,0:T(8,128)(2,1)S(1)}, bf16[4,320,256]{2,1,0:T(8,128)(2,1)S(1)}, u32[]{:S(2)}, u32[]{:S(2)}) collective-permute-start(bf16[4,320,256]{2,1,0:T(8,128)(2,1)S(1)} %get-tuple-element.39), channel_id=1, source_target_pairs={{0,1},{1,0},{2,3},{3,2},{4,5},{5,4},{6,7},{7,6},{8,9},{9,8},{10,11... | collective-permute-start | bytes 1966088 | tf_op jit(solution)/shard_map/ppermute | solution.py:107
  109.3 14.5 %collective-permute-start.19 = (bf16[384,768]{1,0:T(8,128)(2,1)}, bf16[384,768]{1,0:T(8,128)(2,1)S(1)}, u32[]{:S(2)}, u32[]{:S(2)}) collective-permute-start(bf16[384,768]{1,0:T(8,128)(2,1)} %collective-permute-done.6.refs_6_), channel_id=1, source_target_pairs={{0,1},{1,0},{2,3},{3,2},{4,5},{5,4},{6,7},{7,6},{8,9},{9,8},{10,11... | collective-permute-start | bytes 1769480 | tf_op jit(solution)/shard_map/ppermute | solution.py:107
  109.4 14.4 %collective-permute-start.20 = (bf16[384,768]{1,0:T(8,128)(2,1)}, bf16[384,768]{1,0:T(8,128)(2,1)S(1)}, u32[]{:S(2)}, u32[]{:S(2)}) collective-permute-start(bf16[384,768]{1,0:T(8,128)(2,1)} %collective-permute-done.12.refs_7_), channel_id=1, source_target_pairs={{0,1},{1,0},{2,3},{3,2},{4,5},{5,4},{6,7},{7,6},{8,9},{9,8},{10,11... | collective-permute-start | bytes 1769480 | tf_op jit(solution)/shard_map/ppermute | solution.py:107
  115.8 13.4 %collective-permute-start.16 = (bf16[2,128,384]{2,1,0:T(8,128)(2,1)S(1)}, bf16[2,128,384]{2,1,0:T(8,128)(2,1)S(1)}, u32[]{:S(2)}, u32[]{:S(2)}) collective-permute-start(bf16[2,128,384]{2,1,0:T(8,128)(2,1)S(1)} %get-tuple-element.45), channel_id=1, source_target_pairs={{0,4},{4,0},{8,12},{12,8},{1,5},{5,1},{9,13},{13,9},{2,6},{6,2},{1... | collective-permute-start | bytes 589832 | tf_op jit(solution)/shard_map/ppermute | solution.py:107
  121.4 17.1 %collective-permute-start.17 = (bf16[2,128,384]{2,1,0:T(8,128)(2,1)S(1)}, bf16[2,128,384]{2,1,0:T(8,128)(2,1)S(1)}, u32[]{:S(2)}, u32[]{:S(2)}) collective-permute-start(bf16[2,128,384]{2,1,0:T(8,128)(2,1)S(1)} %get-tuple-element.44.refs_0_), channel_id=1, source_target_pairs={{0,8},{4,12},{8,0},{12,4},{1,9},{5,13},{9,1},{13,5},{2,10},{6,14},... | collective-permute-start | bytes 589832 | tf_op jit(solution)/shard_map/ppermute | solution.py:107
  121.4 17.1 %collective-permute-start.18 = (bf16[2,128,384]{2,1,0:T(8,128)(2,1)S(1)}, bf16[2,128,384]{2,1,0:T(8,128)(2,1)S(1)}, u32[]{:S(2)}, u32[]{:S(2)}) collective-permute-start(bf16[2,128,384]{2,1,0:T(8,128)(2,1)S(1)} %get-tuple-element.45), channel_id=1, source_target_pairs={{0,12},{4,8},{8,4},{12,0},{1,13},{5,9},{9,5},{13,1},{2,14},{6,10},... | collective-permute-start | bytes 589832 | tf_op jit(solution)/shard_map/ppermute | solution.py:107
  141.3 5.7 %collective-permute-start.21 = (bf16[2,64,768]{2,1,0:T(8,128)(2,1)S(1)}, bf16[2,64,768]{2,1,0:T(8,128)(2,1)S(1)}, u32[]{:S(2)}, u32[]{:S(2)}) collective-permute-start(bf16[2,64,768]{2,1,0:T(8,128)(2,1)S(1)} %get-tuple-element.48), channel_id=1, source_target_pairs={{0,2},{2,0},{1,3},{3,1},{4,6},{6,4},{5,7},{7,5},{8,10},{10,8},{9,1... | collective-permute-start | bytes 589832 | tf_op jit(solution)/shard_map/ppermute | solution.py:107
  147.1 11.1 %collective-permute-start.23 = (bf16[2,64,768]{2,1,0:T(8,128)(2,1)S(1)}, bf16[2,64,768]{2,1,0:T(8,128)(2,1)S(1)}, u32[]{:S(2)}, u32[]{:S(2)}) collective-permute-start(bf16[2,64,768]{2,1,0:T(8,128)(2,1)S(1)} %add_convert_fusion), channel_id=1, source_target_pairs={{0,8},{4,12},{8,0},{12,4},{1,9},{5,13},{9,1},{13,5},{2,10},{6,14},... | collective-permute-start | bytes 589832 | tf_op jit(solution)/shard_map/ppermute | solution.py:107
  150.6 7.6 %collective-permute-start.22 = (bf16[2,64,768]{2,1,0:T(8,128)(2,1)S(1)}, bf16[2,64,768]{2,1,0:T(8,128)(2,1)S(1)}, u32[]{:S(2)}, u32[]{:S(2)}) collective-permute-start(bf16[2,64,768]{2,1,0:T(8,128)(2,1)S(1)} %get-tuple-element.49), channel_id=1, source_target_pairs={{0,2},{2,0},{1,3},{3,1},{4,6},{6,4},{5,7},{7,5},{8,10},{10,8},{9,1... | collective-permute-start | bytes 589832 | tf_op jit(solution)/shard_map/ppermute | solution.py:107

commit v23 on v22

--- a/solution.py
+++ b/solution.py
@@ -356,7 +356,7 @@
     beside.append(swap(beside[0], "groups"))
     there.append(swap(after(here[1], there[0], beside[1]), "groups"))
     far_2x = swap(far_2, "frames")
-    far_3 = swap(after(joined, far_2, across, near_x, beside[0]), "rows", 3)
+    far_3 = swap(after(joined, here[0], across, near_x), "rows", 3)
     far_3x = swap(far_3, "frames")
 
     found = jnp.stack([x[count : count + heads_n, : MAXB + 2] for x in (joined, near, far_2, far_3)])

time: 160 us -> 163 us (1.019)
  waiting for transfers between devices: 89.8 us -> 94.4 us
  local copies, waits for them, and re-layouts: 9.46 us -> 7.71 us
    ppermute x22, waiting for transfers between devices: 89.8 us -> 94.4 us  [swap(): return lax.ppermute(value, axis, [(i, i ^ step) for i in range(peers)])]
    ppermute x2, starting transfers between devices: 1.58 us -> 3.58 us  [reshard(): lax.ppermute(after(value, *others) if others else value, ('rows', 'heads'...]
    unnamed x20 -> x14, local copies, waits for them, and re-layouts: 2.81 us -> 1.03 us
    ppermute x22, starting transfers between devices: 32.1 us -> 30.3 us  [swap(): return lax.ppermute(value, axis, [(i, i ^ step) for i in range(peers)])]
  transfers between devices with their start and end apart: 24 -> 24, of which waited for: 11 -> 9; matrix products, arithmetic and copies ran while one was open for 4% -> 4% of each run, Pallas kernels for 8% -> 8%
where the time goes in v23:
time: 163 us
  waiting for transfers between devices  94.4 us (58%)
  starting transfers between devices  33.9 us (21%)
  Pallas kernels  23.7 us (15%)
  local copies, waits for them, and re-layouts  7.71 us (5%)
  other arithmetic  2.7 us (2%)
    ppermute x22, waiting for transfers between devices, swap(): return lax.ppermute(value, axis, [(i, i ^ step) for i in range(peers)])  94.4 us
    ppermute x22, starting transfers between devices, swap(): return lax.ppermute(value, axis, [(i, i ^ step) for i in range(peers)])  30.3 us
    pallas_call x5, Pallas kernels, call(): pl.pallas_call(kernel, out_shape=out_shape, grid_spec=pltpu.PrefetchScala...  13 us
    pallas_call x2, Pallas kernels, project(): pl.pallas_call(kernel, out_shape=(jax.ShapeDtypeStruct((rows, 2 * BS, col...  10.8 us
    ppermute x2, starting transfers between devices, reshard(): lax.ppermute(after(value, *others) if others else value, ('rows', 'heads'...  3.58 us
  transfers between devices with their start and end apart: 24, of which 9 were waited for; matrix products, arithmetic and copies ran while one was open for 4% of the time, Pallas kernels for 8%

profile of v23, /device:TPU:0, one launch (start us, length us, event | category | flops | bytes accessed | tf_op | source)
XLA Modules:
  0.0 162.6 jit_solution(15091739820313043401)
XLA Ops:
  0.0 0.7 convert_bitcast_fusion
  0.8 0.7 convert_bitcast_fusion.1
  1.6 0.7 convert.13
  2.5 3.1 %collective-permute-start = (bf16[136,1536]{1,0:T(8,128)(2,1)S(1)}, bf16[136,1536]{1,0:T(8,128)(2,1)}, u32[]{:S(2)}, u32[]{:S(2)}) collective-permute-start(bf16[136,1536]{1,0:T(8,128)(2,1)S(1)} %fusion.1.refs_0_), channel_id=1, source_target_pairs={{0,4},{4,0},{8,12},{12,8},{1,5},{5,1},{9,13},{13,9},{2,6},{6,2},{1... | collective-permute-start | bytes 1253384 | tf_op jit(solution)/shard_map/ppermute | solution.py:107
  5.6 2.7 %dynamic-slice_bitcast_fusion = (bf16[3,384,384]{2,1,0:T(8,128)(2,1)}, bf16[3,384,384]{2,1,0:T(8,128)(2,1)S(1)}) fusion(bf16[768,3,768]{2,0,1:T(8,128)(2,1)} %param.7, s32[]{:T(128)S(6)} %select_n.44, s32[]{:T(128)S(6)} %select_n.51, s32[]{:T(128)S(6)} %select_n.46), kind=kLoop, calls=%fused_computation.2 | loop fusion | bytes 3538956 | tf_op jit(solution)/shard_map/dynamic_slice | solution.py:332
  8.2 1.6 collective-permute-start.1
  9.8 8.7 %collective-permute-done.refs_1_ = bf16[136,1536]{1,0:T(8,128)(2,1)} collective-permute-done((bf16[136,1536]{1,0:T(8,128)(2,1)S(1)}, bf16[136,1536]{1,0:T(8,128)(2,1)}, u32[]{:S(2)}, u32[]{:S(2)}) %collective-permute-start) | collective-permute-done | bytes 417824 | tf_op jit(solution)/shard_map/ppermute | solution.py:107
  18.5 1.7 %collective-permute-start.2 = (bf16[128,1536]{1,0:T(8,128)(2,1)S(1)}, bf16[128,1536]{1,0:T(8,128)(2,1)S(1)}, u32[]{:S(2)}, u32[]{:S(2)}) collective-permute-start(bf16[128,1536]{1,0:T(8,128)(2,1)S(1)} %copy-done.6), channel_id=1, source_target_pairs={{0,2},{2,0},{1,3},{3,1},{4,6},{6,4},{5,7},{7,5},{8,10},{10,8},{9,1... | collective-permute-start | bytes 1179656 | tf_op jit(solution)/shard_map/ppermute | solution.py:107
  20.3 2.0 %collective-permute-start.10 = (bf16[3,384,384]{2,1,0:T(8,128)(2,1)}, bf16[3,384,384]{2,1,0:T(8,128)(2,1)}, u32[]{:S(2)}, u32[]{:S(2)}) collective-permute-start(bf16[3,384,384]{2,1,0:T(8,128)(2,1)} %get-tuple-element.31), channel_id=1, source_target_pairs={{0,4},{1,12},{4,0},{5,8},{8,5},{9,13},{12,1},{13,9},{2,6},{3,14},{... | collective-permute-start | bytes 2654216 | tf_op jit(solution)/shard_map/ppermute | solution.py:340
  22.3 1.5 collective-permute-start.9
  23.9 6.1 %collective-permute-done.2.refs_4_ = bf16[128,1536]{1,0:T(8,128)(2,1)S(1)} collective-permute-done((bf16[128,1536]{1,0:T(8,128)(2,1)S(1)}, bf16[128,1536]{1,0:T(8,128)(2,1)S(1)}, u32[]{:S(2)}, u32[]{:S(2)}) %collective-permute-start.2) | collective-permute-done | bytes 393248 | tf_op jit(solution)/shard_map/ppermute | solution.py:107
  30.0 1.7 %collective-permute-start.5 = (bf16[136,1536]{1,0:T(8,128)(2,1)}, bf16[136,1536]{1,0:T(8,128)(2,1)}, u32[]{:S(2)}, u32[]{:S(2)}) collective-permute-start(bf16[136,1536]{1,0:T(8,128)(2,1)} %collective-permute-done.refs_1_), channel_id=1, source_target_pairs={{0,2},{2,0},{1,3},{3,1},{4,6},{6,4},{5,7},{7,5},{8,10},{10,8},{9,1... | collective-permute-start | bytes 1253384 | tf_op jit(solution)/shard_map/ppermute | solution.py:107
  31.7 10.4 %collective-permute-done.11.refs_6_ = bf16[384,768]{1,0:T(8,128)(2,1)} collective-permute-done((bf16[384,768]{1,0:T(8,128)(2,1)S(1)}, bf16[384,768]{1,0:T(8,128)(2,1)}, u32[]{:S(2)}, u32[]{:S(2)}) %collective-permute-start.11) | collective-permute-done | bytes 589856 | tf_op jit(solution)/shard_map/ppermute | solution.py:107
  42.1 1.5 collective-permute-start.12
  43.8 4.3 %collective-permute-start.3 = (bf16[136,1536]{1,0:T(8,128)(2,1)}, bf16[136,1536]{1,0:T(8,128)(2,1)}, u32[]{:S(2)}, u32[]{:S(2)}) collective-permute-start(bf16[136,1536]{1,0:T(8,128)(2,1)} %copy-done.2), channel_id=1, source_target_pairs={{0,8},{4,12},{8,0},{12,4},{1,9},{5,13},{9,1},{13,5},{2,10},{6,14},... | collective-permute-start | bytes 1253384 | tf_op jit(solution)/shard_map/ppermute | solution.py:107
  48.2 2.6 %collective-permute-start.6 = (bf16[136,1536]{1,0:T(8,128)(2,1)}, bf16[136,1536]{1,0:T(8,128)(2,1)}, u32[]{:S(2)}, u32[]{:S(2)}) collective-permute-start(bf16[136,1536]{1,0:T(8,128)(2,1)} %copy-done.2), channel_id=1, source_target_pairs={{0,12},{4,8},{8,4},{12,0},{1,13},{5,9},{9,5},{13,1},{2,14},{6,10},... | collective-permute-start | bytes 1253384 | tf_op jit(solution)/shard_map/ppermute | solution.py:107
  50.8 0.7 slice_bitcast_fusion.2
  51.5 31.2 %collective-permute-done.3.refs_2_ = bf16[136,1536]{1,0:T(8,128)(2,1)} collective-permute-done((bf16[136,1536]{1,0:T(8,128)(2,1)}, bf16[136,1536]{1,0:T(8,128)(2,1)}, u32[]{:S(2)}, u32[]{:S(2)}) %collective-permute-start.3) | collective-permute-done | bytes 417824 | tf_op jit(solution)/shard_map/ppermute | solution.py:107
  82.7 0.8 collective-permute-start.7
  83.5 1.0 collective-permute-start.13
  84.5 0.7 slice_bitcast_fusion.1
  85.2 1.3 collective-permute-start.8
  86.5 0.7 slice_bitcast_fusion
  87.2 0.6 gather_fusion
  87.8 0.2 slice_reduce_fusion
  88.1 0.2 fusion.3
  88.3 0.6 gather_fusion.1
  88.9 0.2 slice_reduce_fusion.1.counts_ref
  89.1 15.4 %collective-permute-done.13.refs_11_ = bf16[3,384,384]{2,1,0:T(8,128)(2,1)} collective-permute-done((bf16[3,384,384]{2,1,0:T(8,128)(2,1)}, bf16[3,384,384]{2,1,0:T(8,128)(2,1)}, u32[]{:S(2)}, u32[]{:S(2)}) %collective-permute-start.13) | collective-permute-done | bytes 884768 | tf_op jit(solution)/shard_map/ppermute | solution.py:107
  104.5 1.0 copy-done.3
  105.6 6.4 %shard_map.64 = (f32[4,128,256]{2,1,0:T(8,128)S(1)}, f32[4,256,512]{2,1,0:T(8,128)S(1)}, bf16[4,320,512]{2,1,0:T(8,128)(2,1)S(1)}) custom-call(s32[4]{0:T(128)S(1)} %pad_add_fusion.place_ref, bf16[136,1536]{1,0:T(8,128)(2,1)S(1)} %copy-done.3, bf16[136,1536]{1,0:T(8,128)(2,1)} %collective-permute-done.refs_1_, ...), custom_call_target="tpu_custom_call" | custom-call | flops 19327352832 | bytes 8053063 | tf_op jit(solution)/shard_map/pallas_call | solution.py:175
  112.0 4.4 %shard_map.65 = (f32[4,128,128]{2,1,0:T(8,128)S(1)}, f32[4,256,256]{2,1,0:T(8,128)S(1)}, bf16[4,320,256]{2,1,0:T(8,128)(2,1)S(1)}) custom-call(s32[4]{0:T(128)S(1)} %pad_add_fusion.place_ref, bf16[136,1536]{1,0:T(8,128)(2,1)S(1)} %copy-done.4, bf16[136,1536]{1,0:T(8,128)(2,1)} %collective-permute-done.refs_1_, ...), custom_call_target="tpu_custom_call" | custom-call | flops 9663676416 | bytes 4026531 | tf_op jit(solution)/shard_map/pallas_call | solution.py:175
  116.4 0.5 collective-permute-start.14
  117.1 0.4 collective-permute-start.20
  117.5 3.8 %shard_map.66 = (bf16[2,128,256]{2,1,0:T(8,128)(2,1)S(1)}, bf16[2,128,256]{2,1,0:T(8,128)(2,1)S(1)}) custom-call(s32[4]{0:T(128)S(1)} %pad_add_fusion.place_ref, s32[16]{0:T(128)S(1)} %reshape.24.members_ref, s32[4]{0:T(128)S(1)} %slice_reduce_fusion.1.counts_ref, f32[4,128,256]{2,1,0:T(8,128)S(1)} %get-tuple-element.40.q_ref, ...), custom_call_target="tpu_custom_call" | custom-call | flops 268435456 | bytes 2097152 | tf_op jit(solution)/shard_map/pallas_call | solution.py:115
  121.3 2.2 %shard_map.67 = (bf16[2,128,384]{2,1,0:T(8,128)(2,1)S(1)}, bf16[2,128,384]{2,1,0:T(8,128)(2,1)S(1)}) custom-call(s32[4]{0:T(128)S(1)} %pad_add_fusion.place_ref, s32[16]{0:T(128)S(1)} %reshape.24.members_ref, s32[4]{0:T(128)S(1)} %slice_reduce_fusion.1.counts_ref, f32[4,128,128]{2,1,0:T(8,128)S(1)} %get-tuple-element.37.q_ref, ...), custom_call_target="tpu_custom_call" | custom-call | flops 134217728 | bytes 1048576 | tf_op jit(solution)/shard_map/pallas_call | solution.py:115
  123.6 1.3 collective-permute-start.17
  124.9 3.0 %collective-permute-start.18 = (bf16[2,128,384]{2,1,0:T(8,128)(2,1)S(1)}, bf16[2,128,384]{2,1,0:T(8,128)(2,1)S(1)}, u32[]{:S(2)}, u32[]{:S(2)}) collective-permute-start(bf16[2,128,384]{2,1,0:T(8,128)(2,1)S(1)} %get-tuple-element.45), channel_id=1, source_target_pairs={{0,12},{4,8},{8,4},{12,0},{1,13},{5,9},{9,5},{13,1},{2,14},{6,10},... | collective-permute-start | bytes 589832 | tf_op jit(solution)/shard_map/ppermute | solution.py:107
  128.0 4.9 %collective-permute-done.16.refs_1_ = bf16[2,128,384]{2,1,0:T(8,128)(2,1)S(1)} collective-permute-done((bf16[2,128,384]{2,1,0:T(8,128)(2,1)S(1)}, bf16[2,128,384]{2,1,0:T(8,128)(2,1)S(1)}, u32[]{:S(2)}, u32[]{:S(2)}) %collective-permute-start.16) | collective-permute-done | bytes 196640 | tf_op jit(solution)/shard_map/ppermute | solution.py:107
  132.9 7.9 %collective-permute-done.17.refs_2_ = bf16[2,128,384]{2,1,0:T(8,128)(2,1)S(1)} collective-permute-done((bf16[2,128,384]{2,1,0:T(8,128)(2,1)S(1)}, bf16[2,128,384]{2,1,0:T(8,128)(2,1)S(1)}, u32[]{:S(2)}, u32[]{:S(2)}) %collective-permute-start.17) | collective-permute-done | bytes 196640 | tf_op jit(solution)/shard_map/ppermute | solution.py:107
  140.8 2.8 %shard_map.69 = (f32[2,64,768]{2,1,0:T(8,128)S(1)}, bf16[2,64,768]{2,1,0:T(8,128)(2,1)S(1)}) custom-call(s32[4]{0:T(128)S(1)} %pad_add_fusion.place_ref, bf16[2,128,384]{2,1,0:T(8,128)(2,1)S(1)} %get-tuple-element.44.refs_0_, bf16[2,128,384]{2,1,0:T(8,128)(2,1)S(1)} %collective-permute-done.16.refs_1_, ...), custom_call_target="tpu_custom_call" | custom-call | flops 603979776 | bytes 4718592 | tf_op jit(solution)/shard_map/pallas_call | solution.py:115
  143.6 0.3 collective-permute-start.21
  144.0 2.8 %shard_map.68 = (f32[2,64,768]{2,1,0:T(8,128)S(1)}, bf16[2,64,768]{2,1,0:T(8,128)(2,1)S(1)}) custom-call(s32[4]{0:T(128)S(1)} %pad_add_fusion.place_ref, bf16[2,128,384]{2,1,0:T(8,128)(2,1)S(1)} %get-tuple-element.44.refs_0_, bf16[2,128,384]{2,1,0:T(8,128)(2,1)S(1)} %collective-permute-done.16.refs_1_, ...), custom_call_target="tpu_custom_call" | custom-call | flops 603979776 | bytes 4718592 | tf_op jit(solution)/shard_map/pallas_call | solution.py:115
  146.8 2.6 %collective-permute-done.21 = bf16[2,64,768]{2,1,0:T(8,128)(2,1)S(1)} collective-permute-done((bf16[2,64,768]{2,1,0:T(8,128)(2,1)S(1)}, bf16[2,64,768]{2,1,0:T(8,128)(2,1)S(1)}, u32[]{:S(2)}, u32[]{:S(2)}) %collective-permute-start.21) | collective-permute-done | bytes 196640 | tf_op jit(solution)/shard_map/ppermute | solution.py:107
  149.4 4.3 %collective-permute-start.23 = (bf16[2,64,768]{2,1,0:T(8,128)(2,1)S(1)}, bf16[2,64,768]{2,1,0:T(8,128)(2,1)S(1)}, u32[]{:S(2)}, u32[]{:S(2)}) collective-permute-start(bf16[2,64,768]{2,1,0:T(8,128)(2,1)S(1)} %add_convert_fusion), channel_id=1, source_target_pairs={{0,8},{4,12},{8,0},{12,4},{1,9},{5,13},{9,1},{13,5},{2,10},{6,14},... | collective-permute-start | bytes 589832 | tf_op jit(solution)/shard_map/ppermute | solution.py:107
  153.6 0.6 collective-permute-start.22
  154.2 7.1 %collective-permute-done.23.far_ref = bf16[2,64,768]{2,1,0:T(8,128)(2,1)S(1)} collective-permute-done((bf16[2,64,768]{2,1,0:T(8,128)(2,1)S(1)}, bf16[2,64,768]{2,1,0:T(8,128)(2,1)S(1)}, u32[]{:S(2)}, u32[]{:S(2)}) %collective-permute-start.23) | collective-permute-done | bytes 196640 | tf_op jit(solution)/shard_map/ppermute | solution.py:107
  161.3 1.3 shard_map.70
  (48 shorter events, 1.3 us)
Async XLA Ops:
  0.0 2.3 %copy-start = (bf16[1,128,3072]{2,1,0:T(8,128)(2,1)S(1)}, bf16[1,128,3072]{2,1,0:T(8,128)(2,1)}, u32[]{:S(2)}) copy-start(bf16[1,128,3072]{2,1,0:T(8,128)(2,1)} %param.6) | copy-start | bytes 2359300
  2.3 3.2 %copy-start.5 = (bf16[128,1536]{1,0:T(8,128)(2,1)}, bf16[128,1536]{1,0:T(8,128)(2,1)S(1)}, u32[]{:S(2)}) copy-start(bf16[128,1536]{1,0:T(8,128)(2,1)S(1)} %dynamic-slice_bitcast_fusion.2) | copy-start | bytes 1179652
  2.5 5.8 %copy-start.2 = (bf16[136,1536]{1,0:T(8,128)(2,1)}, bf16[136,1536]{1,0:T(8,128)(2,1)S(1)}, u32[]{:S(2)}) copy-start(bf16[136,1536]{1,0:T(8,128)(2,1)S(1)} %fusion.1.refs_0_) | copy-start | bytes 1253380
  2.5 16.0 %collective-permute-start = (bf16[136,1536]{1,0:T(8,128)(2,1)S(1)}, bf16[136,1536]{1,0:T(8,128)(2,1)}, u32[]{:S(2)}, u32[]{:S(2)}) collective-permute-start(bf16[136,1536]{1,0:T(8,128)(2,1)S(1)} %fusion.1.refs_0_), channel_id=1, source_target_pairs={{0,4},{4,0},{8,12},{12,8},{1,5},{5,1},{9,13},{13,9},{2,6},{6,2},{1... | collective-permute-start | bytes 1253384 | tf_op jit(solution)/shard_map/ppermute | solution.py:107
  5.6 12.9 %copy-start.1 = (bf16[768,768]{1,0:T(8,128)(2,1)S(1)}, bf16[768,768]{1,0:T(8,128)(2,1)}, u32[]{:S(2)}) copy-start(bf16[768,768]{1,0:T(8,128)(2,1)} %refs_4_.3) | copy-start | bytes 3538948
  5.6 12.9 %copy-start.6 = (bf16[128,1536]{1,0:T(8,128)(2,1)S(1)}, bf16[128,1536]{1,0:T(8,128)(2,1)}, u32[]{:S(2)}) copy-start(bf16[128,1536]{1,0:T(8,128)(2,1)} %copy-done.5) | copy-start | bytes 1179652
  8.2 14.1 %collective-permute-start.1 = (bf16[3,384,384]{2,1,0:T(8,128)(2,1)S(1)}, bf16[3,384,384]{2,1,0:T(8,128)(2,1)}, u32[]{:S(2)}, u32[]{:S(2)}) collective-permute-start(bf16[3,384,384]{2,1,0:T(8,128)(2,1)S(1)} %get-tuple-element.52), channel_id=1, source_target_pairs={{0,0},{1,8},{4,4},{5,12},{8,1},{9,9},{12,5},{13,13},{2,2},{3,10},{... | collective-permute-start | bytes 2654216 | tf_op jit(solution)/shard_map/ppermute | solution.py:340
  18.5 29.7 %collective-permute-start.4 = (bf16[768,768]{1,0:T(8,128)(2,1)S(1)}, bf16[768,768]{1,0:T(8,128)(2,1)S(1)}, u32[]{:S(2)}, u32[]{:S(2)}) collective-permute-start(bf16[768,768]{1,0:T(8,128)(2,1)S(1)} %copy-done.1), channel_id=1, source_target_pairs={{0,1},{1,0},{2,3},{3,2},{4,5},{5,4},{6,7},{7,6},{8,9},{9,8},{10,11... | collective-permute-start | bytes 3538952 | tf_op jit(solution)/shard_map/ppermute | solution.py:107
  18.5 11.5 %collective-permute-start.2 = (bf16[128,1536]{1,0:T(8,128)(2,1)S(1)}, bf16[128,1536]{1,0:T(8,128)(2,1)S(1)}, u32[]{:S(2)}, u32[]{:S(2)}) collective-permute-start(bf16[128,1536]{1,0:T(8,128)(2,1)S(1)} %copy-done.6), channel_id=1, source_target_pairs={{0,2},{2,0},{1,3},{3,1},{4,6},{6,4},{5,7},{7,5},{8,10},{10,8},{9,1... | collective-permute-start | bytes 1179656 | tf_op jit(solution)/shard_map/ppermute | solution.py:107
  20.2 21.9 %collective-permute-start.11 = (bf16[384,768]{1,0:T(8,128)(2,1)S(1)}, bf16[384,768]{1,0:T(8,128)(2,1)}, u32[]{:S(2)}, u32[]{:S(2)}) collective-permute-start(bf16[384,768]{1,0:T(8,128)(2,1)S(1)} %constant_dynamic-slice_fusion), channel_id=1, source_target_pairs={{0,4},{4,0},{8,12},{12,8},{1,5},{5,1},{9,13},{13,9},{2,6},{6,2},{1... | collective-permute-start | bytes 1769480 | tf_op jit(solution)/shard_map/ppermute | solution.py:107
  20.3 63.2 %collective-permute-start.10 = (bf16[3,384,384]{2,1,0:T(8,128)(2,1)}, bf16[3,384,384]{2,1,0:T(8,128)(2,1)}, u32[]{:S(2)}, u32[]{:S(2)}) collective-permute-start(bf16[3,384,384]{2,1,0:T(8,128)(2,1)} %get-tuple-element.31), channel_id=1, source_target_pairs={{0,4},{1,12},{4,0},{5,8},{8,5},{9,13},{12,1},{13,9},{2,6},{3,14},{... | collective-permute-start | bytes 2654216 | tf_op jit(solution)/shard_map/ppermute | solution.py:340
  22.3 61.2 %collective-permute-start.9 = (bf16[3,384,384]{2,1,0:T(8,128)(2,1)}, bf16[3,384,384]{2,1,0:T(8,128)(2,1)}, u32[]{:S(2)}, u32[]{:S(2)}) collective-permute-start(bf16[3,384,384]{2,1,0:T(8,128)(2,1)} %collective-permute-done.1.refs_8_), channel_id=1, source_target_pairs={{0,16},{16,0},{1,17},{17,1},{2,18},{18,2},{3,19},{19,3},{4,20},{20... | collective-permute-start | bytes 2654216 | tf_op jit(solution)/shard_map/ppermute | solution.py:107
  30.0 13.8 %collective-permute-start.5 = (bf16[136,1536]{1,0:T(8,128)(2,1)}, bf16[136,1536]{1,0:T(8,128)(2,1)}, u32[]{:S(2)}, u32[]{:S(2)}) collective-permute-start(bf16[136,1536]{1,0:T(8,128)(2,1)} %collective-permute-done.refs_1_), channel_id=1, source_target_pairs={{0,2},{2,0},{1,3},{3,1},{4,6},{6,4},{5,7},{7,5},{8,10},{10,8},{9,1... | collective-permute-start | bytes 1253384 | tf_op jit(solution)/shard_map/ppermute | solution.py:107
  42.1 41.4 %collective-permute-start.12 = (bf16[384,768]{1,0:T(8,128)(2,1)}, bf16[384,768]{1,0:T(8,128)(2,1)}, u32[]{:S(2)}, u32[]{:S(2)}) collective-permute-start(bf16[384,768]{1,0:T(8,128)(2,1)} %collective-permute-done.11.refs_6_), channel_id=1, source_target_pairs={{0,16},{16,0},{1,17},{17,1},{2,18},{18,2},{3,19},{19,3},{4,20},{20... | collective-permute-start | bytes 1769480 | tf_op jit(solution)/shard_map/ppermute | solution.py:107
  43.8 38.9 %collective-permute-start.3 = (bf16[136,1536]{1,0:T(8,128)(2,1)}, bf16[136,1536]{1,0:T(8,128)(2,1)}, u32[]{:S(2)}, u32[]{:S(2)}) collective-permute-start(bf16[136,1536]{1,0:T(8,128)(2,1)} %copy-done.2), channel_id=1, source_target_pairs={{0,8},{4,12},{8,0},{12,4},{1,9},{5,13},{9,1},{13,5},{2,10},{6,14},... | collective-permute-start | bytes 1253384 | tf_op jit(solution)/shard_map/ppermute | solution.py:107
  48.2 37.0 %collective-permute-start.6 = (bf16[136,1536]{1,0:T(8,128)(2,1)}, bf16[136,1536]{1,0:T(8,128)(2,1)}, u32[]{:S(2)}, u32[]{:S(2)}) collective-permute-start(bf16[136,1536]{1,0:T(8,128)(2,1)} %copy-done.2), channel_id=1, source_target_pairs={{0,12},{4,8},{8,4},{12,0},{1,13},{5,9},{9,5},{13,1},{2,14},{6,10},... | collective-permute-start | bytes 1253384 | tf_op jit(solution)/shard_map/ppermute | solution.py:107
  82.7 21.8 %collective-permute-start.7 = (bf16[136,1536]{1,0:T(8,128)(2,1)}, bf16[136,1536]{1,0:T(8,128)(2,1)}, u32[]{:S(2)}, u32[]{:S(2)}) collective-permute-start(bf16[136,1536]{1,0:T(8,128)(2,1)} %collective-permute-done.3.refs_2_), channel_id=1, source_target_pairs={{0,2},{2,0},{1,3},{3,1},{4,6},{6,4},{5,7},{7,5},{8,10},{10,8},{9,1... | collective-permute-start | bytes 1253384 | tf_op jit(solution)/shard_map/ppermute | solution.py:107
  83.5 21.0 %collective-permute-start.13 = (bf16[3,384,384]{2,1,0:T(8,128)(2,1)}, bf16[3,384,384]{2,1,0:T(8,128)(2,1)}, u32[]{:S(2)}, u32[]{:S(2)}) collective-permute-start(bf16[3,384,384]{2,1,0:T(8,128)(2,1)} %collective-permute-done.10.refs_10_), channel_id=1, source_target_pairs={{0,16},{16,0},{1,17},{17,1},{2,18},{18,2},{3,19},{19,3},{4,20},{20... | collective-permute-start | bytes 2654216 | tf_op jit(solution)/shard_map/ppermute | solution.py:107
  85.2 19.4 %collective-permute-start.8 = (bf16[136,1536]{1,0:T(8,128)(2,1)}, bf16[136,1536]{1,0:T(8,128)(2,1)}, u32[]{:S(2)}, u32[]{:S(2)}) collective-permute-start(bf16[136,1536]{1,0:T(8,128)(2,1)} %collective-permute-done.6.refs_3_), channel_id=1, source_target_pairs={{0,2},{2,0},{1,3},{3,1},{4,6},{6,4},{5,7},{7,5},{8,10},{10,8},{9,1... | collective-permute-start | bytes 1253384 | tf_op jit(solution)/shard_map/ppermute | solution.py:107
  104.5 1.0 copy-start.3
  105.6 6.4 %copy-start.4 = (bf16[136,1536]{1,0:T(8,128)(2,1)S(1)}, bf16[136,1536]{1,0:T(8,128)(2,1)}, u32[]{:S(2)}) copy-start(bf16[136,1536]{1,0:T(8,128)(2,1)} %copy-done.2) | copy-start | bytes 1253380
  111.9 5.6 %collective-permute-start.15 = (bf16[4,320,512]{2,1,0:T(8,128)(2,1)S(1)}, bf16[4,320,512]{2,1,0:T(8,128)(2,1)S(1)}, u32[]{:S(2)}, u32[]{:S(2)}) collective-permute-start(bf16[4,320,512]{2,1,0:T(8,128)(2,1)S(1)} %get-tuple-element.35), channel_id=1, source_target_pairs={{0,1},{1,0},{2,3},{3,2},{4,5},{5,4},{6,7},{7,6},{8,9},{9,8},{10,11... | collective-permute-start | bytes 3932168 | tf_op jit(solution)/shard_map/ppermute | solution.py:107
  116.4 4.9 %collective-permute-start.14 = (bf16[4,320,256]{2,1,0:T(8,128)(2,1)S(1)}, bf16[4,320,256]{2,1,0:T(8,128)(2,1)S(1)}, u32[]{:S(2)}, u32[]{:S(2)}) collective-permute-start(bf16[4,320,256]{2,1,0:T(8,128)(2,1)S(1)} %get-tuple-element.39), channel_id=1, source_target_pairs={{0,1},{1,0},{2,3},{3,2},{4,5},{5,4},{6,7},{7,6},{8,9},{9,8},{10,11... | collective-permute-start | bytes 1966088 | tf_op jit(solution)/shard_map/ppermute | solution.py:107
  117.0 11.0 %collective-permute-start.19 = (bf16[384,768]{1,0:T(8,128)(2,1)}, bf16[384,768]{1,0:T(8,128)(2,1)S(1)}, u32[]{:S(2)}, u32[]{:S(2)}) collective-permute-start(bf16[384,768]{1,0:T(8,128)(2,1)} %collective-permute-done.11.refs_6_), channel_id=1, source_target_pairs={{0,1},{1,0},{2,3},{3,2},{4,5},{5,4},{6,7},{7,6},{8,9},{9,8},{10,11... | collective-permute-start | bytes 1769480 | tf_op jit(solution)/shard_map/ppermute | solution.py:107
  117.1 10.9 %collective-permute-start.20 = (bf16[384,768]{1,0:T(8,128)(2,1)}, bf16[384,768]{1,0:T(8,128)(2,1)S(1)}, u32[]{:S(2)}, u32[]{:S(2)}) collective-permute-start(bf16[384,768]{1,0:T(8,128)(2,1)} %collective-permute-done.12.refs_7_), channel_id=1, source_target_pairs={{0,1},{1,0},{2,3},{3,2},{4,5},{5,4},{6,7},{7,6},{8,9},{9,8},{10,11... | collective-permute-start | bytes 1769480 | tf_op jit(solution)/shard_map/ppermute | solution.py:107
  123.5 9.4 %collective-permute-start.16 = (bf16[2,128,384]{2,1,0:T(8,128)(2,1)S(1)}, bf16[2,128,384]{2,1,0:T(8,128)(2,1)S(1)}, u32[]{:S(2)}, u32[]{:S(2)}) collective-permute-start(bf16[2,128,384]{2,1,0:T(8,128)(2,1)S(1)} %get-tuple-element.45), channel_id=1, source_target_pairs={{0,4},{4,0},{8,12},{12,8},{1,5},{5,1},{9,13},{13,9},{2,6},{6,2},{1... | collective-permute-start | bytes 589832 | tf_op jit(solution)/shard_map/ppermute | solution.py:107
  123.6 17.2 %collective-permute-start.17 = (bf16[2,128,384]{2,1,0:T(8,128)(2,1)S(1)}, bf16[2,128,384]{2,1,0:T(8,128)(2,1)S(1)}, u32[]{:S(2)}, u32[]{:S(2)}) collective-permute-start(bf16[2,128,384]{2,1,0:T(8,128)(2,1)S(1)} %get-tuple-element.44.refs_0_), channel_id=1, source_target_pairs={{0,8},{4,12},{8,0},{12,4},{1,9},{5,13},{9,1},{13,5},{2,10},{6,14},... | collective-permute-start | bytes 589832 | tf_op jit(solution)/shard_map/ppermute | solution.py:107
  124.9 15.9 %collective-permute-start.18 = (bf16[2,128,384]{2,1,0:T(8,128)(2,1)S(1)}, bf16[2,128,384]{2,1,0:T(8,128)(2,1)S(1)}, u32[]{:S(2)}, u32[]{:S(2)}) collective-permute-start(bf16[2,128,384]{2,1,0:T(8,128)(2,1)S(1)} %get-tuple-element.45), channel_id=1, source_target_pairs={{0,12},{4,8},{8,4},{12,0},{1,13},{5,9},{9,5},{13,1},{2,14},{6,10},... | collective-permute-start | bytes 589832 | tf_op jit(solution)/shard_map/ppermute | solution.py:107
  143.6 5.7 %collective-permute-start.21 = (bf16[2,64,768]{2,1,0:T(8,128)(2,1)S(1)}, bf16[2,64,768]{2,1,0:T(8,128)(2,1)S(1)}, u32[]{:S(2)}, u32[]{:S(2)}) collective-permute-start(bf16[2,64,768]{2,1,0:T(8,128)(2,1)S(1)} %get-tuple-element.48), channel_id=1, source_target_pairs={{0,2},{2,0},{1,3},{3,1},{4,6},{6,4},{5,7},{7,5},{8,10},{10,8},{9,1... | collective-permute-start | bytes 589832 | tf_op jit(solution)/shard_map/ppermute | solution.py:107
  149.4 11.9 %collective-permute-start.23 = (bf16[2,64,768]{2,1,0:T(8,128)(2,1)S(1)}, bf16[2,64,768]{2,1,0:T(8,128)(2,1)S(1)}, u32[]{:S(2)}, u32[]{:S(2)}) collective-permute-start(bf16[2,64,768]{2,1,0:T(8,128)(2,1)S(1)} %add_convert_fusion), channel_id=1, source_target_pairs={{0,8},{4,12},{8,0},{12,4},{1,9},{5,13},{9,1},{13,5},{2,10},{6,14},... | collective-permute-start | bytes 589832 | tf_op jit(solution)/shard_map/ppermute | solution.py:107
  153.6 7.6 %collective-permute-start.22 = (bf16[2,64,768]{2,1,0:T(8,128)(2,1)S(1)}, bf16[2,64,768]{2,1,0:T(8,128)(2,1)S(1)}, u32[]{:S(2)}, u32[]{:S(2)}) collective-permute-start(bf16[2,64,768]{2,1,0:T(8,128)(2,1)S(1)} %get-tuple-element.49), channel_id=1, source_target_pairs={{0,2},{2,0},{1,3},{3,1},{4,6},{6,4},{5,7},{7,5},{8,10},{10,8},{9,1... | collective-permute-start | bytes 589832 | tf_op jit(solution)/shard_map/ppermute | solution.py:107

commit v24 on v22

--- a/solution.py
+++ b/solution.py
@@ -272,7 +272,7 @@
                 if c == 0:
                     weight, half = w_refs[other][i * cols : (i + 1) * cols, :], i
                 else:
-                    weight, half = w_refs[2 + 2 * other + i][...], (i + group) % 2
+                    weight, half = w_refs[2 + 2 * other + i][:cols], (i + group) % 2
                 part = jnp.dot(a_all[(2 * side + half) ^ row], weight, preferred_element_type=jnp.float32)
                 acc = part if acc is None else acc + part
             return acc.astype(jnp.bfloat16).astype(jnp.float32)
@@ -342,16 +342,18 @@
     mine = lax.dynamic_slice_in_dim(latents[0], core * span * depth, span * depth, axis=1)
     mine_x = swap(mine, "frames")
     here, there = [reshard(0)], []
-    tables = jnp.concatenate([win_blocks, win_counts[:, None], block_window[:, None]], axis=1)
-    tables = jnp.pad(tables, ((0, 8 - heads_n), (0, span * depth - MAXB - 2))).astype(mine.dtype)
-    joined = jnp.concatenate([mine, tables], axis=0)
-    near = swap(joined, "rows")
+    near = swap(mine, "rows")
     near_x = swap(near, "frames")
     across = swap(after(w_out, near), "heads")
     there.append(swap(here[0], "groups"))
     here.append(reshard(1, near))
+    tables = jnp.concatenate([win_blocks, win_counts[:, None], block_window[:, None]], axis=1)
+    tables = after(tables, near)
+    tables = jnp.pad(tables, ((0, 8 - heads_n), (0, span * depth - MAXB - 2))).astype(mine.dtype)
+    joined = jnp.concatenate([mine, tables], axis=0)
     far_2 = swap(after(joined, here[0], mine_x), "rows", 2)
     out_half = lax.dynamic_slice_in_dim(w_out, group * cols, cols, axis=0)
+    out_half = jnp.concatenate([out_half, tables[:, : out_half.shape[1]]], axis=0)
     beside = [swap(after(out_half, near), "rows")]
     beside.append(swap(beside[0], "groups"))
     there.append(swap(after(here[1], there[0], beside[1]), "groups"))
@@ -359,7 +361,8 @@
     far_3 = swap(after(joined, far_2, across, near_x, beside[0]), "rows", 3)
     far_3x = swap(far_3, "frames")
 
-    found = jnp.stack([x[count : count + heads_n, : MAXB + 2] for x in (joined, near, far_2, far_3)])
+    found = [tables, beside[0][cols:], far_2[count:], far_3[count:]]
+    found = jnp.stack([x[:heads_n, : MAXB + 2] for x in found])
     tables = found.astype(jnp.int32)[row ^ jnp.arange(rows_n)].reshape(rows_n * heads_n, MAXB + 2)
     windows = lax.dynamic_index_in_dim(
         tables[:, MAXB + 1].reshape(rows_n, heads_n), core, axis=1, keepdims=False
@@ -367,7 +370,7 @@
     picked = tables[windows]
     members, counts = picked[:, :MAXB].reshape(-1), picked[:, MAXB]
 
-    pieces = [joined, near, far_2, far_3], [mine_x, near_x, far_2x, far_3x]
+    pieces = [mine, near, far_2, far_3], [mine_x, near_x, far_2x, far_3x]
     chunks = [(here[0], there[0]), (here[1], after(there[1], members, counts))]
     last = cols // (3 * HD) * HD
     first = project(place, *pieces, chunks, 0, cols - last)

time: 160 us -> 159 us (level)
  waiting for transfers between devices: 89.8 us -> 80.7 us
  starting transfers between devices: 33.7 us -> 42.4 us
    ppermute x22, waiting for transfers between devices: 89.8 us -> 80.7 us  [swap(): return lax.ppermute(value, axis, [(i, i ^ step) for i in range(peers)])]
    ppermute x2, starting transfers between devices: 1.58 us -> 8.24 us  [reshard(): lax.ppermute(after(value, *others) if others else value, ('rows', 'heads'...]
    ppermute x22, starting transfers between devices: 32.1 us -> 34.2 us  [swap(): return lax.ppermute(value, axis, [(i, i ^ step) for i in range(peers)])]
    unnamed x20 -> x10, local copies, waits for them, and re-layouts: 2.81 us -> 1.15 us
  transfers between devices with their start and end apart: 24 -> 24, of which waited for: 11 -> 10; matrix products, arithmetic and copies ran while one was open for 4% -> 6% of each run, Pallas kernels for 8% -> 9%
where the time goes in v24:
time: 159 us; the launch traced here: 158 us
  waiting for transfers between devices  80.7 us (51%)
  starting transfers between devices  42.4 us (27%)
  Pallas kernels  24.8 us (16%)
  local copies, waits for them, and re-layouts  8.08 us (5%)
  other arithmetic  2.19 us (1%)
    ppermute x22, waiting for transfers between devices, swap(): return lax.ppermute(value, axis, [(i, i ^ step) for i in range(peers)])  80.7 us
    ppermute x22, starting transfers between devices, swap(): return lax.ppermute(value, axis, [(i, i ^ step) for i in range(peers)])  34.2 us
    pallas_call x5, Pallas kernels, call(): pl.pallas_call(kernel, out_shape=out_shape, grid_spec=pltpu.PrefetchScala...  13 us
    pallas_call x2, Pallas kernels, project(): pl.pallas_call(kernel, out_shape=(jax.ShapeDtypeStruct((rows, 2 * BS, col...  11.8 us
    ppermute x2, starting transfers between devices, reshard(): lax.ppermute(after(value, *others) if others else value, ('rows', 'heads'...  8.24 us
  transfers between devices with their start and end apart: 24, of which 10 were waited for; matrix products, arithmetic and copies ran while one was open for 6% of the time, Pallas kernels for 9%

profile of v24, /device:TPU:0, one launch (start us, length us, event | category | flops | bytes accessed | tf_op | source)
XLA Modules:
  0.0 158.3 jit_solution(116678660358105775)
XLA Ops:
  0.0 1.1 copy-done
  1.2 3.1 %collective-permute-start = (bf16[128,1536]{1,0:T(8,128)(2,1)S(1)}, bf16[128,1536]{1,0:T(8,128)(2,1)}, u32[]{:S(2)}, u32[]{:S(2)}) collective-permute-start(bf16[128,1536]{1,0:T(8,128)(2,1)S(1)} %dynamic-slice_bitcast_fusion.2.refs_0_), channel_id=1, source_target_pairs={{0,4},{4,0},{8,12},{12,8},{1,5},{5,1},{9,13},{13,9},{2,6},{6,2},{1... | collective-permute-start | bytes 1179656 | tf_op jit(solution)/shard_map/ppermute | solution.py:107
  4.3 3.0 %dynamic-slice_bitcast_fusion = (bf16[3,384,384]{2,1,0:T(8,128)(2,1)}, bf16[3,384,384]{2,1,0:T(8,128)(2,1)}) fusion(bf16[768,3,768]{2,0,1:T(8,128)(2,1)} %param.7, s32[]{:T(128)S(6)} %select_n.44, s32[]{:T(128)S(6)} %select_n.51, s32[]{:T(128)S(6)} %select_n.46), kind=kLoop, calls=%fused_computation.2 | loop fusion | bytes 3538956 | tf_op jit(solution)/shard_map/dynamic_slice | solution.py:332
  7.2 8.2 %collective-permute-start.2 = (bf16[3,384,384]{2,1,0:T(8,128)(2,1)}, bf16[3,384,384]{2,1,0:T(8,128)(2,1)}, u32[]{:S(2)}, u32[]{:S(2)}) collective-permute-start(bf16[3,384,384]{2,1,0:T(8,128)(2,1)} %get-tuple-element.54), channel_id=1, source_target_pairs={{0,0},{1,8},{4,4},{5,12},{8,1},{9,9},{12,5},{13,13},{2,2},{3,10},{... | collective-permute-start | bytes 2654216 | tf_op jit(solution)/shard_map/ppermute | solution.py:340
  15.5 1.5 collective-permute-start.3
  17.4 0.9 pad_maximum_fusion
  18.3 0.4 collective-permute-start.1
  18.9 5.9 %collective-permute-done.3.refs_4_ = bf16[128,1536]{1,0:T(8,128)(2,1)} collective-permute-done((bf16[128,1536]{1,0:T(8,128)(2,1)S(1)}, bf16[128,1536]{1,0:T(8,128)(2,1)}, u32[]{:S(2)}, u32[]{:S(2)}) %collective-permute-start.3) | collective-permute-done | bytes 393248 | tf_op jit(solution)/shard_map/ppermute | solution.py:107
  24.8 1.5 collective-permute-start.10
  26.3 0.8 pad_maximum_fusion.1
  27.1 4.7 %collective-permute-done.6.refs_5_ = bf16[128,1536]{1,0:T(8,128)(2,1)} collective-permute-done((bf16[128,1536]{1,0:T(8,128)(2,1)}, bf16[128,1536]{1,0:T(8,128)(2,1)}, u32[]{:S(2)}, u32[]{:S(2)}) %collective-permute-start.6) | collective-permute-done | bytes 393248 | tf_op jit(solution)/shard_map/ppermute | solution.py:107
  31.8 2.7 %collective-permute-start.4 = (bf16[136,1536]{1,0:T(8,128)(2,1)}, bf16[136,1536]{1,0:T(8,128)(2,1)}, u32[]{:S(2)}, u32[]{:S(2)}) collective-permute-start(bf16[136,1536]{1,0:T(8,128)(2,1)} %pad_maximum_fusion.1), channel_id=1, source_target_pairs={{0,8},{4,12},{8,0},{12,4},{1,9},{5,13},{9,1},{13,5},{2,10},{6,14},... | collective-permute-start | bytes 1253384 | tf_op jit(solution)/shard_map/ppermute | solution.py:107
  34.4 15.5 %collective-permute-done.1.refs_6_ = bf16[392,768]{1,0:T(8,128)(2,1)} collective-permute-done((bf16[392,768]{1,0:T(8,128)(2,1)}, bf16[392,768]{1,0:T(8,128)(2,1)}, u32[]{:S(2)}, u32[]{:S(2)}) %collective-permute-start.1) | collective-permute-done | bytes 602144 | tf_op jit(solution)/shard_map/ppermute | solution.py:107
  49.9 3.5 %collective-permute-start.12 = (bf16[392,768]{1,0:T(8,128)(2,1)}, bf16[392,768]{1,0:T(8,128)(2,1)}, u32[]{:S(2)}, u32[]{:S(2)}) collective-permute-start(bf16[392,768]{1,0:T(8,128)(2,1)} %collective-permute-done.1.refs_6_), channel_id=1, source_target_pairs={{0,16},{16,0},{1,17},{17,1},{2,18},{18,2},{3,19},{19,3},{4,20},{20... | collective-permute-start | bytes 1806344 | tf_op jit(solution)/shard_map/ppermute | solution.py:107
  53.7 15.9 %collective-permute-done.4.refs_2_ = bf16[136,1536]{1,0:T(8,128)(2,1)} collective-permute-done((bf16[136,1536]{1,0:T(8,128)(2,1)}, bf16[136,1536]{1,0:T(8,128)(2,1)}, u32[]{:S(2)}, u32[]{:S(2)}) %collective-permute-start.4) | collective-permute-done | bytes 417824 | tf_op jit(solution)/shard_map/ppermute | solution.py:107
  69.6 0.7 slice_bitcast_fusion.2
  70.2 1.5 collective-permute-start.8
  71.7 1.5 collective-permute-start.13
  73.2 0.7 slice_bitcast_fusion.1
  73.9 8.0 %collective-permute-done.7.refs_3_ = bf16[136,1536]{1,0:T(8,128)(2,1)} collective-permute-done((bf16[136,1536]{1,0:T(8,128)(2,1)}, bf16[136,1536]{1,0:T(8,128)(2,1)}, u32[]{:S(2)}, u32[]{:S(2)}) %collective-permute-start.7) | collective-permute-done | bytes 417824 | tf_op jit(solution)/shard_map/ppermute | solution.py:107
  81.9 1.5 collective-permute-start.9
  83.4 0.7 slice_bitcast_fusion
  84.1 0.6 gather_fusion
  84.6 0.2 slice_reduce_fusion
  84.9 0.2 fusion.1
  85.1 0.6 gather_fusion.1
  85.8 0.2 slice_reduce_fusion.1.counts_ref
  85.9 8.2 %collective-permute-done.13.refs_11_ = bf16[3,384,384]{2,1,0:T(8,128)(2,1)} collective-permute-done((bf16[3,384,384]{2,1,0:T(8,128)(2,1)}, bf16[3,384,384]{2,1,0:T(8,128)(2,1)}, u32[]{:S(2)}, u32[]{:S(2)}) %collective-permute-start.13) | collective-permute-done | bytes 884768 | tf_op jit(solution)/shard_map/ppermute | solution.py:107
  94.1 6.9 %shard_map.64 = (f32[4,128,256]{2,1,0:T(8,128)S(1)}, f32[4,256,512]{2,1,0:T(8,128)S(1)}, bf16[4,320,512]{2,1,0:T(8,128)(2,1)S(1)}) custom-call(s32[4]{0:T(128)S(1)} %pad_add_fusion.1.place_ref, bf16[128,1536]{1,0:T(8,128)(2,1)S(1)} %dynamic-slice_bitcast_fusion.2.refs_0_, bf16[128,1536]{1,0:T(8,128)(2,1)} %collective-permute-done.refs_1_, ...), custom_call_target="tpu_custom_call" | custom-call | flops 19327352832 | bytes 8053063 | tf_op jit(solution)/shard_map/pallas_call | solution.py:175
  101.0 0.4 collective-permute-start.15
  101.4 5.0 %shard_map.65 = (f32[4,128,128]{2,1,0:T(8,128)S(1)}, f32[4,256,256]{2,1,0:T(8,128)S(1)}, bf16[4,320,256]{2,1,0:T(8,128)(2,1)S(1)}) custom-call(s32[4]{0:T(128)S(1)} %pad_add_fusion.1.place_ref, bf16[128,1536]{1,0:T(8,128)(2,1)S(1)} %dynamic-slice_bitcast_fusion.2.refs_0_, bf16[128,1536]{1,0:T(8,128)(2,1)} %collective-permute-done.refs_1_, ...), custom_call_target="tpu_custom_call" | custom-call | flops 9663676416 | bytes 4026531 | tf_op jit(solution)/shard_map/pallas_call | solution.py:175
  106.4 0.2 collective-permute-start.14
  106.6 0.3 collective-permute-start.19
  106.9 0.2 collective-permute-start.20
  107.1 3.8 %shard_map.66 = (bf16[2,128,256]{2,1,0:T(8,128)(2,1)S(1)}, bf16[2,128,256]{2,1,0:T(8,128)(2,1)S(1)}) custom-call(s32[4]{0:T(128)S(1)} %pad_add_fusion.1.place_ref, s32[16]{0:T(128)S(1)} %reshape.24.members_ref, s32[4]{0:T(128)S(1)} %slice_reduce_fusion.1.counts_ref, f32[4,128,256]{2,1,0:T(8,128)S(1)} %get-tuple-element.42.q_ref, ...), custom_call_target="tpu_custom_call" | custom-call | flops 268435456 | bytes 2097152 | tf_op jit(solution)/shard_map/pallas_call | solution.py:115
  110.9 2.2 %shard_map.67 = (bf16[2,128,384]{2,1,0:T(8,128)(2,1)S(1)}, bf16[2,128,384]{2,1,0:T(8,128)(2,1)S(1)}) custom-call(s32[4]{0:T(128)S(1)} %pad_add_fusion.1.place_ref, s32[16]{0:T(128)S(1)} %reshape.24.members_ref, s32[4]{0:T(128)S(1)} %slice_reduce_fusion.1.counts_ref, f32[4,128,128]{2,1,0:T(8,128)S(1)} %get-tuple-element.39.q_ref, ...), custom_call_target="tpu_custom_call" | custom-call | flops 134217728 | bytes 1048576 | tf_op jit(solution)/shard_map/pallas_call | solution.py:115
  113.1 7.3 %collective-permute-start.16 = (bf16[2,128,384]{2,1,0:T(8,128)(2,1)S(1)}, bf16[2,128,384]{2,1,0:T(8,128)(2,1)S(1)}, u32[]{:S(2)}, u32[]{:S(2)}) collective-permute-start(bf16[2,128,384]{2,1,0:T(8,128)(2,1)S(1)} %get-tuple-element.47), channel_id=1, source_target_pairs={{0,4},{4,0},{8,12},{12,8},{1,5},{5,1},{9,13},{13,9},{2,6},{6,2},{1... | collective-permute-start | bytes 589832 | tf_op jit(solution)/shard_map/ppermute | solution.py:107
  120.4 2.4 %collective-permute-start.18 = (bf16[2,128,384]{2,1,0:T(8,128)(2,1)S(1)}, bf16[2,128,384]{2,1,0:T(8,128)(2,1)S(1)}, u32[]{:S(2)}, u32[]{:S(2)}) collective-permute-start(bf16[2,128,384]{2,1,0:T(8,128)(2,1)S(1)} %get-tuple-element.47), channel_id=1, source_target_pairs={{0,12},{4,8},{8,4},{12,0},{1,13},{5,9},{9,5},{13,1},{2,14},{6,10},... | collective-permute-start | bytes 589832 | tf_op jit(solution)/shard_map/ppermute | solution.py:107
  122.9 4.8 %collective-permute-done.16.refs_1_ = bf16[2,128,384]{2,1,0:T(8,128)(2,1)S(1)} collective-permute-done((bf16[2,128,384]{2,1,0:T(8,128)(2,1)S(1)}, bf16[2,128,384]{2,1,0:T(8,128)(2,1)S(1)}, u32[]{:S(2)}, u32[]{:S(2)}) %collective-permute-start.16) | collective-permute-done | bytes 196640 | tf_op jit(solution)/shard_map/ppermute | solution.py:107
  127.6 9.9 %collective-permute-done.17.refs_2_ = bf16[2,128,384]{2,1,0:T(8,128)(2,1)S(1)} collective-permute-done((bf16[2,128,384]{2,1,0:T(8,128)(2,1)S(1)}, bf16[2,128,384]{2,1,0:T(8,128)(2,1)S(1)}, u32[]{:S(2)}, u32[]{:S(2)}) %collective-permute-start.17) | collective-permute-done | bytes 196640 | tf_op jit(solution)/shard_map/ppermute | solution.py:107
  137.5 2.8 %shard_map.69 = (f32[2,64,768]{2,1,0:T(8,128)S(1)}, bf16[2,64,768]{2,1,0:T(8,128)(2,1)S(1)}) custom-call(s32[4]{0:T(128)S(1)} %pad_add_fusion.1.place_ref, bf16[2,128,384]{2,1,0:T(8,128)(2,1)S(1)} %get-tuple-element.46.refs_0_, bf16[2,128,384]{2,1,0:T(8,128)(2,1)S(1)} %collective-permute-done.16.refs_1_, ...), custom_call_target="tpu_custom_call" | custom-call | flops 603979776 | bytes 4718592 | tf_op jit(solution)/shard_map/pallas_call | solution.py:115
  140.4 1.5 collective-permute-start.21
  141.9 2.8 %shard_map.68 = (f32[2,64,768]{2,1,0:T(8,128)S(1)}, bf16[2,64,768]{2,1,0:T(8,128)(2,1)S(1)}) custom-call(s32[4]{0:T(128)S(1)} %pad_add_fusion.1.place_ref, bf16[2,128,384]{2,1,0:T(8,128)(2,1)S(1)} %get-tuple-element.46.refs_0_, bf16[2,128,384]{2,1,0:T(8,128)(2,1)S(1)} %collective-permute-done.16.refs_1_, ...), custom_call_target="tpu_custom_call" | custom-call | flops 603979776 | bytes 4718592 | tf_op jit(solution)/shard_map/pallas_call | solution.py:115
  144.8 1.3 collective-permute-done.21
  146.2 2.8 %collective-permute-start.23 = (bf16[2,64,768]{2,1,0:T(8,128)(2,1)S(1)}, bf16[2,64,768]{2,1,0:T(8,128)(2,1)S(1)}, u32[]{:S(2)}, u32[]{:S(2)}) collective-permute-start(bf16[2,64,768]{2,1,0:T(8,128)(2,1)S(1)} %add_convert_fusion), channel_id=1, source_target_pairs={{0,8},{4,12},{8,0},{12,4},{1,9},{5,13},{9,1},{13,5},{2,10},{6,14},... | collective-permute-start | bytes 589832 | tf_op jit(solution)/shard_map/ppermute | solution.py:107
  149.0 1.5 collective-permute-start.22
  150.5 6.5 %collective-permute-done.23.far_ref = bf16[2,64,768]{2,1,0:T(8,128)(2,1)S(1)} collective-permute-done((bf16[2,64,768]{2,1,0:T(8,128)(2,1)S(1)}, bf16[2,64,768]{2,1,0:T(8,128)(2,1)S(1)}, u32[]{:S(2)}, u32[]{:S(2)}) %collective-permute-start.23) | collective-permute-done | bytes 196640 | tf_op jit(solution)/shard_map/ppermute | solution.py:107
  157.0 1.3 shard_map.70
  (45 shorter events, 1.1 us)
Async XLA Ops:
  0.0 1.1 copy-start
  1.2 16.1 %collective-permute-start = (bf16[128,1536]{1,0:T(8,128)(2,1)S(1)}, bf16[128,1536]{1,0:T(8,128)(2,1)}, u32[]{:S(2)}, u32[]{:S(2)}) collective-permute-start(bf16[128,1536]{1,0:T(8,128)(2,1)S(1)} %dynamic-slice_bitcast_fusion.2.refs_0_), channel_id=1, source_target_pairs={{0,4},{4,0},{8,12},{12,8},{1,5},{5,1},{9,13},{13,9},{2,6},{6,2},{1... | collective-permute-start | bytes 1179656 | tf_op jit(solution)/shard_map/ppermute | solution.py:107
  4.3 12.7 %copy-start.3 = (s32[2]{0:T(128)S(1)}, s32[2]{0:T(128)}, u32[]{:S(2)}) copy-start(s32[2]{0:T(128)} %param.11) | copy-start | bytes 28
  4.3 12.8 %copy-start.4 = (s32[2]{0:T(128)S(1)}, s32[2]{0:T(128)}, u32[]{:S(2)}) copy-start(s32[2]{0:T(128)} %param.10) | copy-start | bytes 28
  4.3 12.9 %copy-start.2 = (s32[2,4]{1,0:T(2,128)S(1)}, s32[2,4]{1,0:T(2,128)}, u32[]{:S(2)}) copy-start(s32[2,4]{1,0:T(2,128)} %param.9) | copy-start | bytes 100
  4.3 13.0 %copy-start.1 = (bf16[768,768]{1,0:T(8,128)(2,1)S(1)}, bf16[768,768]{1,0:T(8,128)(2,1)}, u32[]{:S(2)}) copy-start(bf16[768,768]{1,0:T(8,128)(2,1)} %refs_4_.3) | copy-start | bytes 3538948
  7.2 17.6 %collective-permute-start.2 = (bf16[3,384,384]{2,1,0:T(8,128)(2,1)}, bf16[3,384,384]{2,1,0:T(8,128)(2,1)}, u32[]{:S(2)}, u32[]{:S(2)}) collective-permute-start(bf16[3,384,384]{2,1,0:T(8,128)(2,1)} %get-tuple-element.54), channel_id=1, source_target_pairs={{0,0},{1,8},{4,4},{5,12},{8,1},{9,9},{12,5},{13,13},{2,2},{3,10},{... | collective-permute-start | bytes 2654216 | tf_op jit(solution)/shard_map/ppermute | solution.py:340
  15.5 9.3 %collective-permute-start.3 = (bf16[128,1536]{1,0:T(8,128)(2,1)S(1)}, bf16[128,1536]{1,0:T(8,128)(2,1)}, u32[]{:S(2)}, u32[]{:S(2)}) collective-permute-start(bf16[128,1536]{1,0:T(8,128)(2,1)S(1)} %dynamic-slice_bitcast_fusion.2.refs_0_), channel_id=1, source_target_pairs={{0,2},{2,0},{1,3},{3,1},{4,6},{6,4},{5,7},{7,5},{8,10},{10,8},{9,1... | collective-permute-start | bytes 1179656 | tf_op jit(solution)/shard_map/ppermute | solution.py:107
  17.3 52.2 %collective-permute-start.5 = (bf16[768,768]{1,0:T(8,128)(2,1)S(1)}, bf16[768,768]{1,0:T(8,128)(2,1)S(1)}, u32[]{:S(2)}, u32[]{:S(2)}) collective-permute-start(bf16[768,768]{1,0:T(8,128)(2,1)S(1)} %copy-done.1), channel_id=1, source_target_pairs={{0,1},{1,0},{2,3},{3,2},{4,5},{5,4},{6,7},{7,6},{8,9},{9,8},{10,11... | collective-permute-start | bytes 3538952 | tf_op jit(solution)/shard_map/ppermute | solution.py:107
  18.3 31.6 %collective-permute-start.1 = (bf16[392,768]{1,0:T(8,128)(2,1)}, bf16[392,768]{1,0:T(8,128)(2,1)}, u32[]{:S(2)}, u32[]{:S(2)}) collective-permute-start(bf16[392,768]{1,0:T(8,128)(2,1)} %pad_maximum_fusion), channel_id=1, source_target_pairs={{0,4},{4,0},{8,12},{12,8},{1,5},{5,1},{9,13},{13,9},{2,6},{6,2},{1... | collective-permute-start | bytes 1806344 | tf_op jit(solution)/shard_map/ppermute | solution.py:107
  18.7 13.1 %collective-permute-start.6 = (bf16[128,1536]{1,0:T(8,128)(2,1)}, bf16[128,1536]{1,0:T(8,128)(2,1)}, u32[]{:S(2)}, u32[]{:S(2)}) collective-permute-start(bf16[128,1536]{1,0:T(8,128)(2,1)} %collective-permute-done.refs_1_), channel_id=1, source_target_pairs={{0,2},{2,0},{1,3},{3,1},{4,6},{6,4},{5,7},{7,5},{8,10},{10,8},{9,1... | collective-permute-start | bytes 1179656 | tf_op jit(solution)/shard_map/ppermute | solution.py:107
  24.8 46.9 %collective-permute-start.11 = (bf16[3,384,384]{2,1,0:T(8,128)(2,1)}, bf16[3,384,384]{2,1,0:T(8,128)(2,1)}, u32[]{:S(2)}, u32[]{:S(2)}) collective-permute-start(bf16[3,384,384]{2,1,0:T(8,128)(2,1)} %get-tuple-element.34), channel_id=1, source_target_pairs={{0,4},{1,12},{4,0},{5,8},{8,5},{9,13},{12,1},{13,9},{2,6},{3,14},{... | collective-permute-start | bytes 2654216 | tf_op jit(solution)/shard_map/ppermute | solution.py:340
  24.8 46.9 %collective-permute-start.10 = (bf16[3,384,384]{2,1,0:T(8,128)(2,1)}, bf16[3,384,384]{2,1,0:T(8,128)(2,1)}, u32[]{:S(2)}, u32[]{:S(2)}) collective-permute-start(bf16[3,384,384]{2,1,0:T(8,128)(2,1)} %collective-permute-done.2.refs_8_), channel_id=1, source_target_pairs={{0,16},{16,0},{1,17},{17,1},{2,18},{18,2},{3,19},{19,3},{4,20},{20... | collective-permute-start | bytes 2654216 | tf_op jit(solution)/shard_map/ppermute | solution.py:107
  31.8 37.8 %collective-permute-start.4 = (bf16[136,1536]{1,0:T(8,128)(2,1)}, bf16[136,1536]{1,0:T(8,128)(2,1)}, u32[]{:S(2)}, u32[]{:S(2)}) collective-permute-start(bf16[136,1536]{1,0:T(8,128)(2,1)} %pad_maximum_fusion.1), channel_id=1, source_target_pairs={{0,8},{4,12},{8,0},{12,4},{1,9},{5,13},{9,1},{13,5},{2,10},{6,14},... | collective-permute-start | bytes 1253384 | tf_op jit(solution)/shard_map/ppermute | solution.py:107
  49.9 21.8 %collective-permute-start.12 = (bf16[392,768]{1,0:T(8,128)(2,1)}, bf16[392,768]{1,0:T(8,128)(2,1)}, u32[]{:S(2)}, u32[]{:S(2)}) collective-permute-start(bf16[392,768]{1,0:T(8,128)(2,1)} %collective-permute-done.1.refs_6_), channel_id=1, source_target_pairs={{0,16},{16,0},{1,17},{17,1},{2,18},{18,2},{3,19},{19,3},{4,20},{20... | collective-permute-start | bytes 1806344 | tf_op jit(solution)/shard_map/ppermute | solution.py:107
  69.5 12.3 %collective-permute-start.7 = (bf16[136,1536]{1,0:T(8,128)(2,1)}, bf16[136,1536]{1,0:T(8,128)(2,1)}, u32[]{:S(2)}, u32[]{:S(2)}) collective-permute-start(bf16[136,1536]{1,0:T(8,128)(2,1)} %pad_maximum_fusion.1), channel_id=1, source_target_pairs={{0,12},{4,8},{8,4},{12,0},{1,13},{5,9},{9,5},{13,1},{2,14},{6,10},... | collective-permute-start | bytes 1253384 | tf_op jit(solution)/shard_map/ppermute | solution.py:107
  70.2 23.9 %collective-permute-start.8 = (bf16[136,1536]{1,0:T(8,128)(2,1)}, bf16[136,1536]{1,0:T(8,128)(2,1)}, u32[]{:S(2)}, u32[]{:S(2)}) collective-permute-start(bf16[136,1536]{1,0:T(8,128)(2,1)} %collective-permute-done.4.refs_2_), channel_id=1, source_target_pairs={{0,2},{2,0},{1,3},{3,1},{4,6},{6,4},{5,7},{7,5},{8,10},{10,8},{9,1... | collective-permute-start | bytes 1253384 | tf_op jit(solution)/shard_map/ppermute | solution.py:107
  71.7 22.4 %collective-permute-start.13 = (bf16[3,384,384]{2,1,0:T(8,128)(2,1)}, bf16[3,384,384]{2,1,0:T(8,128)(2,1)}, u32[]{:S(2)}, u32[]{:S(2)}) collective-permute-start(bf16[3,384,384]{2,1,0:T(8,128)(2,1)} %collective-permute-done.11.refs_10_), channel_id=1, source_target_pairs={{0,16},{16,0},{1,17},{17,1},{2,18},{18,2},{3,19},{19,3},{4,20},{20... | collective-permute-start | bytes 2654216 | tf_op jit(solution)/shard_map/ppermute | solution.py:107
  81.9 12.2 %collective-permute-start.9 = (bf16[136,1536]{1,0:T(8,128)(2,1)}, bf16[136,1536]{1,0:T(8,128)(2,1)}, u32[]{:S(2)}, u32[]{:S(2)}) collective-permute-start(bf16[136,1536]{1,0:T(8,128)(2,1)} %collective-permute-done.7.refs_3_), channel_id=1, source_target_pairs={{0,2},{2,0},{1,3},{3,1},{4,6},{6,4},{5,7},{7,5},{8,10},{10,8},{9,1... | collective-permute-start | bytes 1253384 | tf_op jit(solution)/shard_map/ppermute | solution.py:107
  101.0 6.1 %collective-permute-start.15 = (bf16[4,320,512]{2,1,0:T(8,128)(2,1)S(1)}, bf16[4,320,512]{2,1,0:T(8,128)(2,1)S(1)}, u32[]{:S(2)}, u32[]{:S(2)}) collective-permute-start(bf16[4,320,512]{2,1,0:T(8,128)(2,1)S(1)} %get-tuple-element.37), channel_id=1, source_target_pairs={{0,1},{1,0},{2,3},{3,2},{4,5},{5,4},{6,7},{7,6},{8,9},{9,8},{10,11... | collective-permute-start | bytes 3932168 | tf_op jit(solution)/shard_map/ppermute | solution.py:107
  106.4 4.6 %collective-permute-start.14 = (bf16[4,320,256]{2,1,0:T(8,128)(2,1)S(1)}, bf16[4,320,256]{2,1,0:T(8,128)(2,1)S(1)}, u32[]{:S(2)}, u32[]{:S(2)}) collective-permute-start(bf16[4,320,256]{2,1,0:T(8,128)(2,1)S(1)} %get-tuple-element.41), channel_id=1, source_target_pairs={{0,1},{1,0},{2,3},{3,2},{4,5},{5,4},{6,7},{7,6},{8,9},{9,8},{10,11... | collective-permute-start | bytes 1966088 | tf_op jit(solution)/shard_map/ppermute | solution.py:107
  106.6 16.2 %collective-permute-start.19 = (bf16[392,768]{1,0:T(8,128)(2,1)}, bf16[392,768]{1,0:T(8,128)(2,1)S(1)}, u32[]{:S(2)}, u32[]{:S(2)}) collective-permute-start(bf16[392,768]{1,0:T(8,128)(2,1)} %collective-permute-done.1.refs_6_), channel_id=1, source_target_pairs={{0,1},{1,0},{2,3},{3,2},{4,5},{5,4},{6,7},{7,6},{8,9},{9,8},{10,11... | collective-permute-start | bytes 1806344 | tf_op jit(solution)/shard_map/ppermute | solution.py:107
  106.9 15.9 %collective-permute-start.20 = (bf16[392,768]{1,0:T(8,128)(2,1)}, bf16[392,768]{1,0:T(8,128)(2,1)S(1)}, u32[]{:S(2)}, u32[]{:S(2)}) collective-permute-start(bf16[392,768]{1,0:T(8,128)(2,1)} %collective-permute-done.12.refs_7_), channel_id=1, source_target_pairs={{0,1},{1,0},{2,3},{3,2},{4,5},{5,4},{6,7},{7,6},{8,9},{9,8},{10,11... | collective-permute-start | bytes 1806344 | tf_op jit(solution)/shard_map/ppermute | solution.py:107
  113.1 14.5 %collective-permute-start.16 = (bf16[2,128,384]{2,1,0:T(8,128)(2,1)S(1)}, bf16[2,128,384]{2,1,0:T(8,128)(2,1)S(1)}, u32[]{:S(2)}, u32[]{:S(2)}) collective-permute-start(bf16[2,128,384]{2,1,0:T(8,128)(2,1)S(1)} %get-tuple-element.47), channel_id=1, source_target_pairs={{0,4},{4,0},{8,12},{12,8},{1,5},{5,1},{9,13},{13,9},{2,6},{6,2},{1... | collective-permute-start | bytes 589832 | tf_op jit(solution)/shard_map/ppermute | solution.py:107
  120.4 17.1 %collective-permute-start.17 = (bf16[2,128,384]{2,1,0:T(8,128)(2,1)S(1)}, bf16[2,128,384]{2,1,0:T(8,128)(2,1)S(1)}, u32[]{:S(2)}, u32[]{:S(2)}) collective-permute-start(bf16[2,128,384]{2,1,0:T(8,128)(2,1)S(1)} %get-tuple-element.46.refs_0_), channel_id=1, source_target_pairs={{0,8},{4,12},{8,0},{12,4},{1,9},{5,13},{9,1},{13,5},{2,10},{6,14},... | collective-permute-start | bytes 589832 | tf_op jit(solution)/shard_map/ppermute | solution.py:107
  120.4 17.1 %collective-permute-start.18 = (bf16[2,128,384]{2,1,0:T(8,128)(2,1)S(1)}, bf16[2,128,384]{2,1,0:T(8,128)(2,1)S(1)}, u32[]{:S(2)}, u32[]{:S(2)}) collective-permute-start(bf16[2,128,384]{2,1,0:T(8,128)(2,1)S(1)} %get-tuple-element.47), channel_id=1, source_target_pairs={{0,12},{4,8},{8,4},{12,0},{1,13},{5,9},{9,5},{13,1},{2,14},{6,10},... | collective-permute-start | bytes 589832 | tf_op jit(solution)/shard_map/ppermute | solution.py:107
  140.4 5.7 %collective-permute-start.21 = (bf16[2,64,768]{2,1,0:T(8,128)(2,1)S(1)}, bf16[2,64,768]{2,1,0:T(8,128)(2,1)S(1)}, u32[]{:S(2)}, u32[]{:S(2)}) collective-permute-start(bf16[2,64,768]{2,1,0:T(8,128)(2,1)S(1)} %get-tuple-element.50), channel_id=1, source_target_pairs={{0,2},{2,0},{1,3},{3,1},{4,6},{6,4},{5,7},{7,5},{8,10},{10,8},{9,1... | collective-permute-start | bytes 589832 | tf_op jit(solution)/shard_map/ppermute | solution.py:107
  146.2 10.8 %collective-permute-start.23 = (bf16[2,64,768]{2,1,0:T(8,128)(2,1)S(1)}, bf16[2,64,768]{2,1,0:T(8,128)(2,1)S(1)}, u32[]{:S(2)}, u32[]{:S(2)}) collective-permute-start(bf16[2,64,768]{2,1,0:T(8,128)(2,1)S(1)} %add_convert_fusion), channel_id=1, source_target_pairs={{0,8},{4,12},{8,0},{12,4},{1,9},{5,13},{9,1},{13,5},{2,10},{6,14},... | collective-permute-start | bytes 589832 | tf_op jit(solution)/shard_map/ppermute | solution.py:107
  149.0 8.0 %collective-permute-start.22 = (bf16[2,64,768]{2,1,0:T(8,128)(2,1)S(1)}, bf16[2,64,768]{2,1,0:T(8,128)(2,1)S(1)}, u32[]{:S(2)}, u32[]{:S(2)}) collective-permute-start(bf16[2,64,768]{2,1,0:T(8,128)(2,1)S(1)} %get-tuple-element.51), channel_id=1, source_target_pairs={{0,2},{2,0},{1,3},{3,1},{4,6},{6,4},{5,7},{7,5},{8,10},{10,8},{9,1... | collective-permute-start | bytes 589832 | tf_op jit(solution)/shard_map/ppermute | solution.py:107

commit v25 on v23

--- a/solution.py
+++ b/solution.py
@@ -351,13 +351,13 @@
     there.append(swap(here[0], "groups"))
     here.append(reshard(1, near))
     far_2 = swap(after(joined, here[0], mine_x), "rows", 2)
+    there.append(swap(after(here[1], there[0]), "groups"))
+    far_2x = swap(far_2, "frames")
+    far_3 = swap(after(joined, far_2, across, near_x), "rows", 3)
+    far_3x = swap(far_3, "frames")
     out_half = lax.dynamic_slice_in_dim(w_out, group * cols, cols, axis=0)
-    beside = [swap(after(out_half, near), "rows")]
+    beside = [swap(after(out_half, far_3), "rows")]
     beside.append(swap(beside[0], "groups"))
-    there.append(swap(after(here[1], there[0], beside[1]), "groups"))
-    far_2x = swap(far_2, "frames")
-    far_3 = swap(after(joined, here[0], across, near_x), "rows", 3)
-    far_3x = swap(far_3, "frames")
 
     found = jnp.stack([x[count : count + heads_n, : MAXB + 2] for x in (joined, near, far_2, far_3)])
     tables = found.astype(jnp.int32)[row ^ jnp.arange(rows_n)].reshape(rows_n * heads_n, MAXB + 2)

time: 163 us -> 167 us (1.025)
  starting transfers between devices: 33.9 us -> 41.5 us
  waiting for transfers between devices: 94.4 us -> 87.2 us
  local copies, waits for them, and re-layouts: 7.71 us -> 11 us
    ppermute x22, starting transfers between devices: 30.3 us -> 39.9 us  [swap(): return lax.ppermute(value, axis, [(i, i ^ step) for i in range(peers)])]
    ppermute x22, waiting for transfers between devices: 94.4 us -> 87.2 us  [swap(): return lax.ppermute(value, axis, [(i, i ^ step) for i in range(peers)])]
    ppermute x2, starting transfers between devices: 3.58 us -> 1.59 us  [reshard(): lax.ppermute(after(value, *others) if others else value, ('rows', 'heads'...]
    unnamed x14 -> x16, local copies, waits for them, and re-layouts: 1.03 us -> 2.77 us
  transfers between devices with their start and end apart: 24 -> 24, of which waited for: 9 -> 10; matrix products, arithmetic and copies ran while one was open for 4% -> 5% of each run, Pallas kernels for 8% -> 12%
where the time goes in v25:
time: 167 us
  waiting for transfers between devices  87.2 us (52%)
  starting transfers between devices  41.5 us (25%)
  Pallas kernels  23.4 us (14%)
  local copies, waits for them, and re-layouts  11 us (7%)
  other arithmetic  3.69 us (2%)
    ppermute x22, waiting for transfers between devices, swap(): return lax.ppermute(value, axis, [(i, i ^ step) for i in range(peers)])  87.2 us
    ppermute x22, starting transfers between devices, swap(): return lax.ppermute(value, axis, [(i, i ^ step) for i in range(peers)])  39.9 us
    pallas_call x5, Pallas kernels, call(): pl.pallas_call(kernel, out_shape=out_shape, grid_spec=pltpu.PrefetchScala...  12.6 us
    pallas_call x2, Pallas kernels, project(): pl.pallas_call(kernel, out_shape=(jax.ShapeDtypeStruct((rows, 2 * BS, col...  10.8 us
  transfers between devices with their start and end apart: 24, of which 10 were waited for; matrix products, arithmetic and copies ran while one was open for 5% of the time, Pallas kernels for 12%

profile of v25, /device:TPU:0, one launch (start us, length us, event | category | flops | bytes accessed | tf_op | source)
XLA Modules:
  0.0 166.9 jit_solution(5876136232894674077)
XLA Ops:
  0.0 0.7 convert_bitcast_fusion
  0.8 0.7 convert_bitcast_fusion.1
  1.6 0.7 convert.13
  2.3 0.8 dynamic-slice_bitcast_fusion.2
  3.1 1.0 fusion.1.refs_0_
  4.2 3.1 %collective-permute-start = (bf16[136,1536]{1,0:T(8,128)(2,1)S(1)}, bf16[136,1536]{1,0:T(8,128)(2,1)}, u32[]{:S(2)}, u32[]{:S(2)}) collective-permute-start(bf16[136,1536]{1,0:T(8,128)(2,1)S(1)} %fusion.1.refs_0_), channel_id=1, source_target_pairs={{0,4},{4,0},{8,12},{12,8},{1,5},{5,1},{9,13},{13,9},{2,6},{6,2},{1... | collective-permute-start | bytes 1253384 | tf_op jit(solution)/shard_map/ppermute | solution.py:107
  7.3 2.6 %dynamic-slice_bitcast_fusion = (bf16[3,384,384]{2,1,0:T(8,128)(2,1)}, bf16[3,384,384]{2,1,0:T(8,128)(2,1)S(1)}) fusion(bf16[768,3,768]{2,0,1:T(8,128)(2,1)} %param.7, s32[]{:T(128)S(6)} %select_n.44, s32[]{:T(128)S(6)} %select_n.51, s32[]{:T(128)S(6)} %select_n.46), kind=kLoop, calls=%fused_computation.2 | loop fusion | bytes 3538956 | tf_op jit(solution)/shard_map/dynamic_slice | solution.py:332
  9.9 1.6 collective-permute-start.1
  11.5 8.7 %collective-permute-done.refs_1_ = bf16[136,1536]{1,0:T(8,128)(2,1)} collective-permute-done((bf16[136,1536]{1,0:T(8,128)(2,1)S(1)}, bf16[136,1536]{1,0:T(8,128)(2,1)}, u32[]{:S(2)}, u32[]{:S(2)}) %collective-permute-start) | collective-permute-done | bytes 417824 | tf_op jit(solution)/shard_map/ppermute | solution.py:107
  20.2 1.7 collective-permute-start.2
  21.9 1.5 collective-permute-start.9
  23.5 0.6 collective-permute-start.5
  24.1 7.8 %collective-permute-done.2.refs_4_ = bf16[128,1536]{1,0:T(8,128)(2,1)S(1)} collective-permute-done((bf16[128,1536]{1,0:T(8,128)(2,1)}, bf16[128,1536]{1,0:T(8,128)(2,1)S(1)}, u32[]{:S(2)}, u32[]{:S(2)}) %collective-permute-start.2) | collective-permute-done | bytes 393248 | tf_op jit(solution)/shard_map/ppermute | solution.py:107
  32.0 8.4 %collective-permute-start.3 = (bf16[136,1536]{1,0:T(8,128)(2,1)}, bf16[136,1536]{1,0:T(8,128)(2,1)}, u32[]{:S(2)}, u32[]{:S(2)}) collective-permute-start(bf16[136,1536]{1,0:T(8,128)(2,1)} %copy-done.2), channel_id=1, source_target_pairs={{0,8},{4,12},{8,0},{12,4},{1,9},{5,13},{9,1},{13,5},{2,10},{6,14},... | collective-permute-start | bytes 1253384 | tf_op jit(solution)/shard_map/ppermute | solution.py:107
  40.5 0.9 constant_dynamic-slice_fusion
  41.4 0.7 copy-done.5
  42.1 29.8 %collective-permute-done.3.refs_2_ = bf16[136,1536]{1,0:T(8,128)(2,1)} collective-permute-done((bf16[136,1536]{1,0:T(8,128)(2,1)}, bf16[136,1536]{1,0:T(8,128)(2,1)}, u32[]{:S(2)}, u32[]{:S(2)}) %collective-permute-start.3) | collective-permute-done | bytes 417824 | tf_op jit(solution)/shard_map/ppermute | solution.py:107
  72.0 0.7 slice_bitcast_fusion.2
  72.6 1.5 collective-permute-start.7
  74.1 1.5 collective-permute-start.11
  75.7 0.7 slice_bitcast_fusion.1
  76.3 7.9 %collective-permute-done.6.refs_3_ = bf16[136,1536]{1,0:T(8,128)(2,1)} collective-permute-done((bf16[136,1536]{1,0:T(8,128)(2,1)}, bf16[136,1536]{1,0:T(8,128)(2,1)}, u32[]{:S(2)}, u32[]{:S(2)}) %collective-permute-start.6) | collective-permute-done | bytes 417824 | tf_op jit(solution)/shard_map/ppermute | solution.py:107
  84.2 7.2 %collective-permute-start.17 = (bf16[384,768]{1,0:T(8,128)(2,1)}, bf16[384,768]{1,0:T(8,128)(2,1)}, u32[]{:S(2)}, u32[]{:S(2)}) collective-permute-start(bf16[384,768]{1,0:T(8,128)(2,1)} %constant_dynamic-slice_fusion), channel_id=1, source_target_pairs={{0,4},{4,0},{8,12},{12,8},{1,5},{5,1},{9,13},{13,9},{2,6},{6,2},{1... | collective-permute-start | bytes 1769480 | tf_op jit(solution)/shard_map/ppermute | solution.py:107
  91.4 1.5 collective-permute-start.8
  93.0 0.7 slice_bitcast_fusion
  93.7 0.6 gather_fusion
  94.7 0.6 gather_fusion.1
  95.5 10.2 %collective-permute-done.17.refs_6_ = bf16[384,768]{1,0:T(8,128)(2,1)} collective-permute-done((bf16[384,768]{1,0:T(8,128)(2,1)}, bf16[384,768]{1,0:T(8,128)(2,1)}, u32[]{:S(2)}, u32[]{:S(2)}) %collective-permute-start.17) | collective-permute-done | bytes 589856 | tf_op jit(solution)/shard_map/ppermute | solution.py:107
  105.8 1.5 collective-permute-start.18
  107.3 1.0 copy-done.3
  108.3 1.0 copy-done.6
  109.3 6.4 %shard_map.64 = (f32[4,128,256]{2,1,0:T(8,128)S(1)}, f32[4,256,512]{2,1,0:T(8,128)S(1)}, bf16[4,320,512]{2,1,0:T(8,128)(2,1)S(1)}) custom-call(s32[4]{0:T(128)S(1)} %pad_add_fusion.place_ref, bf16[136,1536]{1,0:T(8,128)(2,1)S(1)} %copy-done.3, bf16[136,1536]{1,0:T(8,128)(2,1)} %collective-permute-done.refs_1_, ...), custom_call_target="tpu_custom_call" | custom-call | flops 19327352832 | bytes 8053063 | tf_op jit(solution)/shard_map/pallas_call | solution.py:175
  115.8 4.4 %shard_map.65 = (f32[4,128,128]{2,1,0:T(8,128)S(1)}, f32[4,256,256]{2,1,0:T(8,128)S(1)}, bf16[4,320,256]{2,1,0:T(8,128)(2,1)S(1)}) custom-call(s32[4]{0:T(128)S(1)} %pad_add_fusion.place_ref, bf16[136,1536]{1,0:T(8,128)(2,1)S(1)} %copy-done.4, bf16[136,1536]{1,0:T(8,128)(2,1)} %collective-permute-done.refs_1_, ...), custom_call_target="tpu_custom_call" | custom-call | flops 9663676416 | bytes 4026531 | tf_op jit(solution)/shard_map/pallas_call | solution.py:175
  120.2 0.5 collective-permute-start.12
  121.3 3.8 %shard_map.66 = (bf16[2,128,256]{2,1,0:T(8,128)(2,1)S(1)}, bf16[2,128,256]{2,1,0:T(8,128)(2,1)S(1)}) custom-call(s32[4]{0:T(128)S(1)} %pad_add_fusion.place_ref, s32[16]{0:T(128)S(1)} %reshape.24.members_ref, s32[4]{0:T(128)S(1)} %slice_reduce_fusion.1.counts_ref, f32[4,128,256]{2,1,0:T(8,128)S(1)} %get-tuple-element.39.q_ref, ...), custom_call_target="tpu_custom_call" | custom-call | flops 268435456 | bytes 2097152 | tf_op jit(solution)/shard_map/pallas_call | solution.py:115
  125.1 2.2 %shard_map.67 = (bf16[2,128,384]{2,1,0:T(8,128)(2,1)S(1)}, bf16[2,128,384]{2,1,0:T(8,128)(2,1)S(1)}) custom-call(s32[4]{0:T(128)S(1)} %pad_add_fusion.place_ref, s32[16]{0:T(128)S(1)} %reshape.24.members_ref, s32[4]{0:T(128)S(1)} %slice_reduce_fusion.1.counts_ref, f32[4,128,128]{2,1,0:T(8,128)S(1)} %get-tuple-element.36.q_ref, ...), custom_call_target="tpu_custom_call" | custom-call | flops 134217728 | bytes 1048576 | tf_op jit(solution)/shard_map/pallas_call | solution.py:115
  127.3 1.8 %collective-permute-start.14 = (bf16[2,128,384]{2,1,0:T(8,128)(2,1)S(1)}, bf16[2,128,384]{2,1,0:T(8,128)(2,1)S(1)}, u32[]{:S(2)}, u32[]{:S(2)}) collective-permute-start(bf16[2,128,384]{2,1,0:T(8,128)(2,1)S(1)} %get-tuple-element.44), channel_id=1, source_target_pairs={{0,4},{4,0},{8,12},{12,8},{1,5},{5,1},{9,13},{13,9},{2,6},{6,2},{1... | collective-permute-start | bytes 589832 | tf_op jit(solution)/shard_map/ppermute | solution.py:107
  129.1 2.7 %collective-permute-start.16 = (bf16[2,128,384]{2,1,0:T(8,128)(2,1)S(1)}, bf16[2,128,384]{2,1,0:T(8,128)(2,1)S(1)}, u32[]{:S(2)}, u32[]{:S(2)}) collective-permute-start(bf16[2,128,384]{2,1,0:T(8,128)(2,1)S(1)} %get-tuple-element.44), channel_id=1, source_target_pairs={{0,12},{4,8},{8,4},{12,0},{1,13},{5,9},{9,5},{13,1},{2,14},{6,10},... | collective-permute-start | bytes 589832 | tf_op jit(solution)/shard_map/ppermute | solution.py:107
  131.8 4.7 %collective-permute-done.14.refs_1_ = bf16[2,128,384]{2,1,0:T(8,128)(2,1)S(1)} collective-permute-done((bf16[2,128,384]{2,1,0:T(8,128)(2,1)S(1)}, bf16[2,128,384]{2,1,0:T(8,128)(2,1)S(1)}, u32[]{:S(2)}, u32[]{:S(2)}) %collective-permute-start.14) | collective-permute-done | bytes 196640 | tf_op jit(solution)/shard_map/ppermute | solution.py:107
  136.5 9.7 %collective-permute-done.15.refs_2_ = bf16[2,128,384]{2,1,0:T(8,128)(2,1)S(1)} collective-permute-done((bf16[2,128,384]{2,1,0:T(8,128)(2,1)S(1)}, bf16[2,128,384]{2,1,0:T(8,128)(2,1)S(1)}, u32[]{:S(2)}, u32[]{:S(2)}) %collective-permute-start.15) | collective-permute-done | bytes 196640 | tf_op jit(solution)/shard_map/ppermute | solution.py:107
  146.2 2.6 %shard_map.69 = (f32[2,64,768]{2,1,0:T(8,128)S(1)}, bf16[2,64,768]{2,1,0:T(8,128)(2,1)S(1)}) custom-call(s32[4]{0:T(128)S(1)} %pad_add_fusion.place_ref, bf16[2,128,384]{2,1,0:T(8,128)(2,1)S(1)} %get-tuple-element.43.refs_0_, bf16[2,128,384]{2,1,0:T(8,128)(2,1)S(1)} %collective-permute-done.14.refs_1_, ...), custom_call_target="tpu_custom_call" | custom-call | flops 603979776 | bytes 4718592 | tf_op jit(solution)/shard_map/pallas_call | solution.py:115
  148.8 1.6 collective-permute-start.21
  150.4 2.6 %shard_map.68 = (f32[2,64,768]{2,1,0:T(8,128)S(1)}, bf16[2,64,768]{2,1,0:T(8,128)(2,1)S(1)}) custom-call(s32[4]{0:T(128)S(1)} %pad_add_fusion.place_ref, bf16[2,128,384]{2,1,0:T(8,128)(2,1)S(1)} %get-tuple-element.43.refs_0_, bf16[2,128,384]{2,1,0:T(8,128)(2,1)S(1)} %collective-permute-done.14.refs_1_, ...), custom_call_target="tpu_custom_call" | custom-call | flops 603979776 | bytes 4718592 | tf_op jit(solution)/shard_map/pallas_call | solution.py:115
  153.0 1.5 collective-permute-done.21
  154.6 3.1 %collective-permute-start.23 = (bf16[2,64,768]{2,1,0:T(8,128)(2,1)S(1)}, bf16[2,64,768]{2,1,0:T(8,128)(2,1)S(1)}, u32[]{:S(2)}, u32[]{:S(2)}) collective-permute-start(bf16[2,64,768]{2,1,0:T(8,128)(2,1)S(1)} %add_convert_fusion), channel_id=1, source_target_pairs={{0,8},{4,12},{8,0},{12,4},{1,9},{5,13},{9,1},{13,5},{2,10},{6,14},... | collective-permute-start | bytes 589832 | tf_op jit(solution)/shard_map/ppermute | solution.py:107
  157.7 1.5 collective-permute-start.22
  159.1 6.4 %collective-permute-done.23.far_ref = bf16[2,64,768]{2,1,0:T(8,128)(2,1)S(1)} collective-permute-done((bf16[2,64,768]{2,1,0:T(8,128)(2,1)S(1)}, bf16[2,64,768]{2,1,0:T(8,128)(2,1)S(1)}, u32[]{:S(2)}, u32[]{:S(2)}) %collective-permute-start.23) | collective-permute-done | bytes 196640 | tf_op jit(solution)/shard_map/ppermute | solution.py:107
  165.5 1.3 shard_map.70
  (50 shorter events, 2.0 us)
Async XLA Ops:
  0.0 2.3 %copy-start = (bf16[1,128,3072]{2,1,0:T(8,128)(2,1)S(1)}, bf16[1,128,3072]{2,1,0:T(8,128)(2,1)}, u32[]{:S(2)}) copy-start(bf16[1,128,3072]{2,1,0:T(8,128)(2,1)} %param.6) | copy-start | bytes 2359300
  4.2 5.7 %copy-start.2 = (bf16[136,1536]{1,0:T(8,128)(2,1)}, bf16[136,1536]{1,0:T(8,128)(2,1)S(1)}, u32[]{:S(2)}) copy-start(bf16[136,1536]{1,0:T(8,128)(2,1)S(1)} %fusion.1.refs_0_) | copy-start | bytes 1253380
  4.2 16.1 %collective-permute-start = (bf16[136,1536]{1,0:T(8,128)(2,1)S(1)}, bf16[136,1536]{1,0:T(8,128)(2,1)}, u32[]{:S(2)}, u32[]{:S(2)}) collective-permute-start(bf16[136,1536]{1,0:T(8,128)(2,1)S(1)} %fusion.1.refs_0_), channel_id=1, source_target_pairs={{0,4},{4,0},{8,12},{12,8},{1,5},{5,1},{9,13},{13,9},{2,6},{6,2},{1... | collective-permute-start | bytes 1253384 | tf_op jit(solution)/shard_map/ppermute | solution.py:107
  7.3 13.0 %copy-start.1 = (bf16[768,768]{1,0:T(8,128)(2,1)S(1)}, bf16[768,768]{1,0:T(8,128)(2,1)}, u32[]{:S(2)}) copy-start(bf16[768,768]{1,0:T(8,128)(2,1)} %refs_4_.3) | copy-start | bytes 3538948
  9.9 12.0 %collective-permute-start.1 = (bf16[3,384,384]{2,1,0:T(8,128)(2,1)S(1)}, bf16[3,384,384]{2,1,0:T(8,128)(2,1)}, u32[]{:S(2)}, u32[]{:S(2)}) collective-permute-start(bf16[3,384,384]{2,1,0:T(8,128)(2,1)S(1)} %get-tuple-element.52), channel_id=1, source_target_pairs={{0,0},{1,8},{4,4},{5,12},{8,1},{9,9},{12,5},{13,13},{2,2},{3,10},{... | collective-permute-start | bytes 2654216 | tf_op jit(solution)/shard_map/ppermute | solution.py:340
  20.2 51.7 %collective-permute-start.4 = (bf16[768,768]{1,0:T(8,128)(2,1)S(1)}, bf16[768,768]{1,0:T(8,128)(2,1)S(1)}, u32[]{:S(2)}, u32[]{:S(2)}) collective-permute-start(bf16[768,768]{1,0:T(8,128)(2,1)S(1)} %copy-done.1), channel_id=1, source_target_pairs={{0,1},{1,0},{2,3},{3,2},{4,5},{5,4},{6,7},{7,6},{8,9},{9,8},{10,11... | collective-permute-start | bytes 3538952 | tf_op jit(solution)/shard_map/ppermute | solution.py:107
  20.2 11.7 %collective-permute-start.2 = (bf16[128,1536]{1,0:T(8,128)(2,1)}, bf16[128,1536]{1,0:T(8,128)(2,1)S(1)}, u32[]{:S(2)}, u32[]{:S(2)}) collective-permute-start(bf16[128,1536]{1,0:T(8,128)(2,1)} %dynamic-slice_bitcast_fusion.2), channel_id=1, source_target_pairs={{0,2},{2,0},{1,3},{3,1},{4,6},{6,4},{5,7},{7,5},{8,10},{10,8},{9,1... | collective-permute-start | bytes 1179656 | tf_op jit(solution)/shard_map/ppermute | solution.py:107
  21.9 52.2 %collective-permute-start.10 = (bf16[3,384,384]{2,1,0:T(8,128)(2,1)}, bf16[3,384,384]{2,1,0:T(8,128)(2,1)}, u32[]{:S(2)}, u32[]{:S(2)}) collective-permute-start(bf16[3,384,384]{2,1,0:T(8,128)(2,1)} %get-tuple-element.31), channel_id=1, source_target_pairs={{0,4},{1,12},{4,0},{5,8},{8,5},{9,13},{12,1},{13,9},{2,6},{3,14},{... | collective-permute-start | bytes 2654216 | tf_op jit(solution)/shard_map/ppermute | solution.py:340
  21.9 52.2 %collective-permute-start.9 = (bf16[3,384,384]{2,1,0:T(8,128)(2,1)}, bf16[3,384,384]{2,1,0:T(8,128)(2,1)}, u32[]{:S(2)}, u32[]{:S(2)}) collective-permute-start(bf16[3,384,384]{2,1,0:T(8,128)(2,1)} %collective-permute-done.1.refs_8_), channel_id=1, source_target_pairs={{0,16},{16,0},{1,17},{17,1},{2,18},{18,2},{3,19},{19,3},{4,20},{20... | collective-permute-start | bytes 2654216 | tf_op jit(solution)/shard_map/ppermute | solution.py:107
  23.5 17.8 %collective-permute-start.5 = (bf16[136,1536]{1,0:T(8,128)(2,1)}, bf16[136,1536]{1,0:T(8,128)(2,1)S(1)}, u32[]{:S(2)}, u32[]{:S(2)}) collective-permute-start(bf16[136,1536]{1,0:T(8,128)(2,1)} %collective-permute-done.refs_1_), channel_id=1, source_target_pairs={{0,2},{2,0},{1,3},{3,1},{4,6},{6,4},{5,7},{7,5},{8,10},{10,8},{9,1... | collective-permute-start | bytes 1253384 | tf_op jit(solution)/shard_map/ppermute | solution.py:107
  32.0 40.0 %collective-permute-start.3 = (bf16[136,1536]{1,0:T(8,128)(2,1)}, bf16[136,1536]{1,0:T(8,128)(2,1)}, u32[]{:S(2)}, u32[]{:S(2)}) collective-permute-start(bf16[136,1536]{1,0:T(8,128)(2,1)} %copy-done.2), channel_id=1, source_target_pairs={{0,8},{4,12},{8,0},{12,4},{1,9},{5,13},{9,1},{13,5},{2,10},{6,14},... | collective-permute-start | bytes 1253384 | tf_op jit(solution)/shard_map/ppermute | solution.py:107
  41.4 0.7 copy-start.5
  72.0 12.3 %collective-permute-start.6 = (bf16[136,1536]{1,0:T(8,128)(2,1)}, bf16[136,1536]{1,0:T(8,128)(2,1)}, u32[]{:S(2)}, u32[]{:S(2)}) collective-permute-start(bf16[136,1536]{1,0:T(8,128)(2,1)} %copy-done.2), channel_id=1, source_target_pairs={{0,12},{4,8},{8,4},{12,0},{1,13},{5,9},{9,5},{13,1},{2,14},{6,10},... | collective-permute-start | bytes 1253384 | tf_op jit(solution)/shard_map/ppermute | solution.py:107
  72.6 34.6 %collective-permute-start.7 = (bf16[136,1536]{1,0:T(8,128)(2,1)}, bf16[136,1536]{1,0:T(8,128)(2,1)}, u32[]{:S(2)}, u32[]{:S(2)}) collective-permute-start(bf16[136,1536]{1,0:T(8,128)(2,1)} %collective-permute-done.3.refs_2_), channel_id=1, source_target_pairs={{0,2},{2,0},{1,3},{3,1},{4,6},{6,4},{5,7},{7,5},{8,10},{10,8},{9,1... | collective-permute-start | bytes 1253384 | tf_op jit(solution)/shard_map/ppermute | solution.py:107
  74.1 33.1 %collective-permute-start.11 = (bf16[3,384,384]{2,1,0:T(8,128)(2,1)}, bf16[3,384,384]{2,1,0:T(8,128)(2,1)}, u32[]{:S(2)}, u32[]{:S(2)}) collective-permute-start(bf16[3,384,384]{2,1,0:T(8,128)(2,1)} %collective-permute-done.10.refs_10_), channel_id=1, source_target_pairs={{0,16},{16,0},{1,17},{17,1},{2,18},{18,2},{3,19},{19,3},{4,20},{20... | collective-permute-start | bytes 2654216 | tf_op jit(solution)/shard_map/ppermute | solution.py:107
  84.2 21.5 %collective-permute-start.17 = (bf16[384,768]{1,0:T(8,128)(2,1)}, bf16[384,768]{1,0:T(8,128)(2,1)}, u32[]{:S(2)}, u32[]{:S(2)}) collective-permute-start(bf16[384,768]{1,0:T(8,128)(2,1)} %constant_dynamic-slice_fusion), channel_id=1, source_target_pairs={{0,4},{4,0},{8,12},{12,8},{1,5},{5,1},{9,13},{13,9},{2,6},{6,2},{1... | collective-permute-start | bytes 1769480 | tf_op jit(solution)/shard_map/ppermute | solution.py:107
  91.4 15.9 %collective-permute-start.8 = (bf16[136,1536]{1,0:T(8,128)(2,1)}, bf16[136,1536]{1,0:T(8,128)(2,1)}, u32[]{:S(2)}, u32[]{:S(2)}) collective-permute-start(bf16[136,1536]{1,0:T(8,128)(2,1)} %collective-permute-done.6.refs_3_), channel_id=1, source_target_pairs={{0,2},{2,0},{1,3},{3,1},{4,6},{6,4},{5,7},{7,5},{8,10},{10,8},{9,1... | collective-permute-start | bytes 1253384 | tf_op jit(solution)/shard_map/ppermute | solution.py:107
  105.8 15.4 %collective-permute-start.18 = (bf16[384,768]{1,0:T(8,128)(2,1)}, bf16[384,768]{1,0:T(8,128)(2,1)S(1)}, u32[]{:S(2)}, u32[]{:S(2)}) collective-permute-start(bf16[384,768]{1,0:T(8,128)(2,1)} %collective-permute-done.17.refs_6_), channel_id=1, source_target_pairs={{0,16},{16,0},{1,17},{17,1},{2,18},{18,2},{3,19},{19,3},{4,20},{20... | collective-permute-start | bytes 1769480 | tf_op jit(solution)/shard_map/ppermute | solution.py:107
  107.3 1.0 copy-start.3
  108.3 1.0 copy-start.6
  109.3 6.4 %copy-start.4 = (bf16[136,1536]{1,0:T(8,128)(2,1)S(1)}, bf16[136,1536]{1,0:T(8,128)(2,1)}, u32[]{:S(2)}) copy-start(bf16[136,1536]{1,0:T(8,128)(2,1)} %copy-done.2) | copy-start | bytes 1253380
  109.3 6.5 %copy-start.7 = (bf16[136,1536]{1,0:T(8,128)(2,1)S(1)}, bf16[136,1536]{1,0:T(8,128)(2,1)}, u32[]{:S(2)}) copy-start(bf16[136,1536]{1,0:T(8,128)(2,1)} %copy-done.5) | copy-start | bytes 1253380
  115.7 5.6 %collective-permute-start.13 = (bf16[4,320,512]{2,1,0:T(8,128)(2,1)S(1)}, bf16[4,320,512]{2,1,0:T(8,128)(2,1)S(1)}, u32[]{:S(2)}, u32[]{:S(2)}) collective-permute-start(bf16[4,320,512]{2,1,0:T(8,128)(2,1)S(1)} %get-tuple-element.34), channel_id=1, source_target_pairs={{0,1},{1,0},{2,3},{3,2},{4,5},{5,4},{6,7},{7,6},{8,9},{9,8},{10,11... | collective-permute-start | bytes 3932168 | tf_op jit(solution)/shard_map/ppermute | solution.py:107
  120.2 4.8 %collective-permute-start.12 = (bf16[4,320,256]{2,1,0:T(8,128)(2,1)S(1)}, bf16[4,320,256]{2,1,0:T(8,128)(2,1)S(1)}, u32[]{:S(2)}, u32[]{:S(2)}) collective-permute-start(bf16[4,320,256]{2,1,0:T(8,128)(2,1)S(1)} %get-tuple-element.38), channel_id=1, source_target_pairs={{0,1},{1,0},{2,3},{3,2},{4,5},{5,4},{6,7},{7,6},{8,9},{9,8},{10,11... | collective-permute-start | bytes 1966088 | tf_op jit(solution)/shard_map/ppermute | solution.py:107
  120.7 11.0 %collective-permute-start.19 = (bf16[384,768]{1,0:T(8,128)(2,1)}, bf16[384,768]{1,0:T(8,128)(2,1)S(1)}, u32[]{:S(2)}, u32[]{:S(2)}) collective-permute-start(bf16[384,768]{1,0:T(8,128)(2,1)} %collective-permute-done.17.refs_6_), channel_id=1, source_target_pairs={{0,1},{1,0},{2,3},{3,2},{4,5},{5,4},{6,7},{7,6},{8,9},{9,8},{10,11... | collective-permute-start | bytes 1769480 | tf_op jit(solution)/shard_map/ppermute | solution.py:107
  121.1 10.6 %collective-permute-start.20 = (bf16[384,768]{1,0:T(8,128)(2,1)S(1)}, bf16[384,768]{1,0:T(8,128)(2,1)S(1)}, u32[]{:S(2)}, u32[]{:S(2)}) collective-permute-start(bf16[384,768]{1,0:T(8,128)(2,1)S(1)} %collective-permute-done.18.refs_7_), channel_id=1, source_target_pairs={{0,1},{1,0},{2,3},{3,2},{4,5},{5,4},{6,7},{7,6},{8,9},{9,8},{10,11... | collective-permute-start | bytes 1769480 | tf_op jit(solution)/shard_map/ppermute | solution.py:107
  127.3 9.2 %collective-permute-start.14 = (bf16[2,128,384]{2,1,0:T(8,128)(2,1)S(1)}, bf16[2,128,384]{2,1,0:T(8,128)(2,1)S(1)}, u32[]{:S(2)}, u32[]{:S(2)}) collective-permute-start(bf16[2,128,384]{2,1,0:T(8,128)(2,1)S(1)} %get-tuple-element.44), channel_id=1, source_target_pairs={{0,4},{4,0},{8,12},{12,8},{1,5},{5,1},{9,13},{13,9},{2,6},{6,2},{1... | collective-permute-start | bytes 589832 | tf_op jit(solution)/shard_map/ppermute | solution.py:107
  129.1 17.1 %collective-permute-start.15 = (bf16[2,128,384]{2,1,0:T(8,128)(2,1)S(1)}, bf16[2,128,384]{2,1,0:T(8,128)(2,1)S(1)}, u32[]{:S(2)}, u32[]{:S(2)}) collective-permute-start(bf16[2,128,384]{2,1,0:T(8,128)(2,1)S(1)} %get-tuple-element.43.refs_0_), channel_id=1, source_target_pairs={{0,8},{4,12},{8,0},{12,4},{1,9},{5,13},{9,1},{13,5},{2,10},{6,14},... | collective-permute-start | bytes 589832 | tf_op jit(solution)/shard_map/ppermute | solution.py:107
  129.1 17.1 %collective-permute-start.16 = (bf16[2,128,384]{2,1,0:T(8,128)(2,1)S(1)}, bf16[2,128,384]{2,1,0:T(8,128)(2,1)S(1)}, u32[]{:S(2)}, u32[]{:S(2)}) collective-permute-start(bf16[2,128,384]{2,1,0:T(8,128)(2,1)S(1)} %get-tuple-element.44), channel_id=1, source_target_pairs={{0,12},{4,8},{8,4},{12,0},{1,13},{5,9},{9,5},{13,1},{2,14},{6,10},... | collective-permute-start | bytes 589832 | tf_op jit(solution)/shard_map/ppermute | solution.py:107
  148.8 5.7 %collective-permute-start.21 = (bf16[2,64,768]{2,1,0:T(8,128)(2,1)S(1)}, bf16[2,64,768]{2,1,0:T(8,128)(2,1)S(1)}, u32[]{:S(2)}, u32[]{:S(2)}) collective-permute-start(bf16[2,64,768]{2,1,0:T(8,128)(2,1)S(1)} %get-tuple-element.48), channel_id=1, source_target_pairs={{0,2},{2,0},{1,3},{3,1},{4,6},{6,4},{5,7},{7,5},{8,10},{10,8},{9,1... | collective-permute-start | bytes 589832 | tf_op jit(solution)/shard_map/ppermute | solution.py:107
  154.6 10.9 %collective-permute-start.23 = (bf16[2,64,768]{2,1,0:T(8,128)(2,1)S(1)}, bf16[2,64,768]{2,1,0:T(8,128)(2,1)S(1)}, u32[]{:S(2)}, u32[]{:S(2)}) collective-permute-start(bf16[2,64,768]{2,1,0:T(8,128)(2,1)S(1)} %add_convert_fusion), channel_id=1, source_target_pairs={{0,8},{4,12},{8,0},{12,4},{1,9},{5,13},{9,1},{13,5},{2,10},{6,14},... | collective-permute-start | bytes 589832 | tf_op jit(solution)/shard_map/ppermute | solution.py:107
  157.7 7.9 %collective-permute-start.22 = (bf16[2,64,768]{2,1,0:T(8,128)(2,1)S(1)}, bf16[2,64,768]{2,1,0:T(8,128)(2,1)S(1)}, u32[]{:S(2)}, u32[]{:S(2)}) collective-permute-start(bf16[2,64,768]{2,1,0:T(8,128)(2,1)S(1)} %get-tuple-element.49), channel_id=1, source_target_pairs={{0,2},{2,0},{1,3},{3,1},{4,6},{6,4},{5,7},{7,5},{8,10},{10,8},{9,1... | collective-permute-start | bytes 589832 | tf_op jit(solution)/shard_map/ppermute | solution.py:107

commit v26 on v24

--- a/solution.py
+++ b/solution.py
@@ -128,15 +128,15 @@
 
 
 def project(place, mine, theirs, chunks, first, cols):
-    rows, (count, width) = len(mine), theirs[0].shape
+    rows, (count, width) = len(mine) - 1, theirs[0].shape
     half = chunks[0][0].shape[1]
     slices = len(chunks)
     flat = [w for of_round in chunks for w in of_round]
-    fetched = 2 * rows + len(flat)
+    fetched = 2 * len(mine) + len(flat)
 
     def kernel(place_ref, *refs):
         row, group, frame, core = (place_ref[i] for i in range(4))
-        w_refs = refs[2 * rows : fetched]
+        w_refs = refs[2 * len(mine) : fetched]
         q_keep, kv_keep, send, x_all, w_all, total, sems = refs[fetched:]
         copies = []
         for k in range(slices):
@@ -146,12 +146,21 @@
                     source = w_refs[2 * k + g].at[part, :, first : first + cols]
                     into = w_all.at[pl.ds(at, half), part * cols : (part + 1) * cols]
                     copies.append(pltpu.make_async_copy(source, into, sems.at[len(copies)]))
+        for copy in copies:
+            copy.start()
+        middle = (row == 1) | (row == 2)
         fetch_x = []
         for i in range(2 * rows):
-            to = x_all.at[row ^ (i % rows), (frame + i // rows) % 2]
-            fetch_x.append(pltpu.make_async_copy(refs[i].at[pl.ds(0, count)], to, sems.at[len(copies) + i]))
-        for copy in copies + fetch_x:
-            copy.start()
+            f, s = divmod(i, rows)
+            to, sem = x_all.at[row ^ s, (frame + f) % 2], sems.at[len(copies) + i]
+            x_refs = refs[f * len(mine) : (f + 1) * len(mine)]
+            fetch_x.append(pltpu.make_async_copy(x_refs[s].at[pl.ds(0, count)], to, sem))
+            if s < rows - 1:
+                fetch_x[-1].start()
+            else:
+                other = pltpu.make_async_copy(x_refs[rows].at[pl.ds(0, count)], to, sem)
+                pl.when(middle)(fetch_x[-1].start)
+                pl.when(jnp.logical_not(middle))(other.start)
         for copy in copies:
             copy.wait()
         for s in range(rows):
@@ -328,6 +337,10 @@
     half = depth // 2
     place = jnp.stack([row, group, frame, core]).astype(jnp.int32)
 
+    def over_frames(value, rows):
+        pairs = [(2 * r + f, 2 * r + 1 - f) for r in rows for f in range(2)]
+        return lax.ppermute(value, ("rows", "frames"), pairs)
+
     def reshard(k, *others):
         value = lax.dynamic_slice(
             w_qkv.transpose(1, 0, 2), (0, group * half, (k + row) % span * cols), (3, half, cols)
@@ -351,17 +364,21 @@
     tables = after(tables, near)
     tables = jnp.pad(tables, ((0, 8 - heads_n), (0, span * depth - MAXB - 2))).astype(mine.dtype)
     joined = jnp.concatenate([mine, tables], axis=0)
-    far_2 = swap(after(joined, here[0], mine_x), "rows", 2)
+    in_3 = lax.ppermute(joined, "rows", [(1, 2), (2, 1)])
+    far_2 = swap(after(joined, here[0], mine_x, in_3), "rows", 2)
     out_half = lax.dynamic_slice_in_dim(w_out, group * cols, cols, axis=0)
     out_half = jnp.concatenate([out_half, tables[:, : out_half.shape[1]]], axis=0)
     beside = [swap(after(out_half, near), "rows")]
     beside.append(swap(beside[0], "groups"))
     there.append(swap(after(here[1], there[0], beside[1]), "groups"))
     far_2x = swap(far_2, "frames")
-    far_3 = swap(after(joined, far_2, across, near_x, beside[0]), "rows", 3)
-    far_3x = swap(far_3, "frames")
-
-    found = [tables, beside[0][cols:], far_2[count:], far_3[count:]]
+    in_3x = over_frames(in_3, (1, 2))
+    out_3 = after(far_2, across, near_x, beside[0], in_3x)
+    out_3 = lax.ppermute(out_3, "rows", [(1, 0), (2, 3)])
+    out_3x = over_frames(out_3, (0, 3))
+
+    extra = jnp.where((row == 1) | (row == 2), in_3[count:], out_3[count:])
+    found = [tables, beside[0][cols:], far_2[count:], extra]
     found = jnp.stack([x[:heads_n, : MAXB + 2] for x in found])
     tables = found.astype(jnp.int32)[row ^ jnp.arange(rows_n)].reshape(rows_n * heads_n, MAXB + 2)
     windows = lax.dynamic_index_in_dim(
@@ -370,7 +387,7 @@
     picked = tables[windows]
     members, counts = picked[:, :MAXB].reshape(-1), picked[:, MAXB]
 
-    pieces = [mine, near, far_2, far_3], [mine_x, near_x, far_2x, far_3x]
+    pieces = [mine, near, far_2, in_3, out_3], [mine_x, near_x, far_2x, in_3x, out_3x]
     chunks = [(here[0], there[0]), (here[1], after(there[1], members, counts))]
     last = cols // (3 * HD) * HD
     first = project(place, *pieces, chunks, 0, cols - last)

time: 159 us -> 174 us (1.094)
  starting transfers between devices: 42.4 us -> 71 us
  waiting for transfers between devices: 80.7 us -> 63 us
  local copies, waits for them, and re-layouts: 8.08 us -> 12.3 us
    ppermute x22 -> x20, waiting for transfers between devices: 80.7 us -> 54.1 us  [swap(): return lax.ppermute(value, axis, [(i, i ^ step) for i in range(peers)])]
    ppermute x2, starting transfers between devices: 8.24 us -> 32.5 us  [reshard(): lax.ppermute(after(value, *others) if others else value, ('rows', 'heads'...]
    ppermute x0 -> x4, waiting for transfers between devices: none -> 8.91 us  [the longest x1 4.55 us: by_heads(): out_3 = lax.ppermute(out_3, 'rows', [(1, 0), (2, 3)])]
    ppermute x0 -> x4, starting transfers between devices: none -> 7.48 us  [the longest x2 4.78 us: over_frames(): return lax.ppermute(value, ('rows', 'frames'), pairs)]
    unnamed x10 -> x24, local copies, waits for them, and re-layouts: 1.15 us -> 4.64 us
    ppermute x22 -> x20, starting transfers between devices: 34.2 us -> 31 us  [swap(): return lax.ppermute(value, axis, [(i, i ^ step) for i in range(peers)])]
  transfers between devices with their start and end apart: 24 -> 26, of which waited for: 10 -> 9; matrix products, arithmetic and copies ran while one was open for 6% -> 5% of each run, Pallas kernels for 9% -> 8%
where the time goes in v26:
time: 174 us; the launch traced here: 173 us
  starting transfers between devices  71 us (41%)
  waiting for transfers between devices  63 us (36%)
  Pallas kernels  24.7 us (14%)
  local copies, waits for them, and re-layouts  12.3 us (7%)
    ppermute x20, waiting for transfers between devices, swap(): return lax.ppermute(value, axis, [(i, i ^ step) for i in range(peers)])  54.1 us
    ppermute x2, starting transfers between devices, reshard(): lax.ppermute(after(value, *others) if others else value, ('rows', 'heads'...  32.5 us
    ppermute x20, starting transfers between devices, swap(): return lax.ppermute(value, axis, [(i, i ^ step) for i in range(peers)])  31 us
    pallas_call x5, Pallas kernels, call(): pl.pallas_call(kernel, out_shape=out_shape, grid_spec=pltpu.PrefetchScala...  13 us
    pallas_call x2, Pallas kernels, project(): pl.pallas_call(kernel, out_shape=(jax.ShapeDtypeStruct((rows, 2 * BS, col...  11.7 us
    ppermute x2, starting transfers between devices, over_frames(): return lax.ppermute(value, ('rows', 'frames'), pairs)  4.78 us
    unnamed x24, local copies, waits for them, and re-layouts  4.64 us
    ppermute x1, waiting for transfers between devices, by_heads(): out_3 = lax.ppermute(out_3, 'rows', [(1, 0), (2, 3)])  4.55 us
  transfers between devices with their start and end apart: 26, of which 9 were waited for; matrix products, arithmetic and copies ran while one was open for 5% of the time, Pallas kernels for 8%

profile of v26, /device:TPU:0, one launch (start us, length us, event | category | flops | bytes accessed | tf_op | source)
XLA Modules:
  0.0 172.7 jit_solution(2813330588595805777)
XLA Ops:
  0.0 1.1 copy-done
  1.2 3.1 %collective-permute-start = (bf16[128,1536]{1,0:T(8,128)(2,1)S(1)}, bf16[128,1536]{1,0:T(8,128)(2,1)S(1)}, u32[]{:S(2)}, u32[]{:S(2)}) collective-permute-start(bf16[128,1536]{1,0:T(8,128)(2,1)S(1)} %dynamic-slice_bitcast_fusion.2.refs_0_), channel_id=1, source_target_pairs={{0,4},{4,0},{8,12},{12,8},{1,5},{5,1},{9,13},{13,9},{2,6},{6,2},{1... | collective-permute-start | bytes 1179656 | tf_op jit(solution)/shard_map/ppermute | solution.py:107
  4.3 1.5 collective-permute-start.3
  5.8 2.9 %dynamic-slice_bitcast_fusion = (bf16[3,384,384]{2,1,0:T(8,128)(2,1)}, bf16[3,384,384]{2,1,0:T(8,128)(2,1)}) fusion(bf16[768,3,768]{2,0,1:T(8,128)(2,1)} %param.7, s32[]{:T(128)S(6)} %select_n.52, s32[]{:T(128)S(6)} %select_n.61, s32[]{:T(128)S(6)} %select_n.54), kind=kLoop, calls=%fused_computation.2 | loop fusion | bytes 3538956 | tf_op jit(solution)/shard_map/dynamic_slice | solution.py:345
  8.7 8.2 %collective-permute-start.2 = (bf16[3,384,384]{2,1,0:T(8,128)(2,1)}, bf16[3,384,384]{2,1,0:T(8,128)(2,1)}, u32[]{:S(2)}, u32[]{:S(2)}) collective-permute-start(bf16[3,384,384]{2,1,0:T(8,128)(2,1)} %get-tuple-element.54), channel_id=1, source_target_pairs={{0,0},{1,8},{4,4},{5,12},{8,1},{9,9},{12,5},{13,13},{2,2},{3,10},{... | collective-permute-start | bytes 2654216 | tf_op jit(solution)/shard_map/ppermute | solution.py:353
  17.3 0.7 copy-done.2
  18.0 1.4 collective-permute-start.4
  19.4 0.6 collective-permute-start.7
  20.0 0.9 pad_maximum_fusion
  20.9 2.6 %collective-permute-start.1 = (bf16[392,768]{1,0:T(8,128)(2,1)}, bf16[392,768]{1,0:T(8,128)(2,1)}, u32[]{:S(2)}, u32[]{:S(2)}) collective-permute-start(bf16[392,768]{1,0:T(8,128)(2,1)} %pad_maximum_fusion), channel_id=1, source_target_pairs={{0,4},{4,0},{8,12},{12,8},{1,5},{5,1},{9,13},{13,9},{2,6},{6,2},{1... | collective-permute-start | bytes 1806344 | tf_op jit(solution)/shard_map/ppermute | solution.py:107
  23.5 1.4 collective-permute-start.8
  24.9 6.2 %collective-permute-done.7.refs_6_ = bf16[128,1536]{1,0:T(8,128)(2,1)S(1)} collective-permute-done((bf16[128,1536]{1,0:T(8,128)(2,1)}, bf16[128,1536]{1,0:T(8,128)(2,1)S(1)}, u32[]{:S(2)}, u32[]{:S(2)}) %collective-permute-start.7) | collective-permute-done | bytes 393248 | tf_op jit(solution)/shard_map/ppermute | solution.py:107
  31.2 0.8 copy-done.5
  32.0 24.3 %collective-permute-start.13 = (bf16[3,384,384]{2,1,0:T(8,128)(2,1)}, bf16[3,384,384]{2,1,0:T(8,128)(2,1)}, u32[]{:S(2)}, u32[]{:S(2)}) collective-permute-start(bf16[3,384,384]{2,1,0:T(8,128)(2,1)} %get-tuple-element.34), channel_id=1, source_target_pairs={{0,4},{1,12},{4,0},{5,8},{8,5},{9,13},{12,1},{13,9},{2,6},{3,14},{... | collective-permute-start | bytes 2654216 | tf_op jit(solution)/shard_map/ppermute | solution.py:353
  56.3 1.5 collective-permute-start.12
  57.8 0.6 collective-permute-start.14
  58.6 0.7 slice.50
  59.3 25.9 %collective-permute-done.5.refs_2_ = bf16[136,1536]{1,0:T(8,128)(2,1)} collective-permute-done((bf16[136,1536]{1,0:T(8,128)(2,1)}, bf16[136,1536]{1,0:T(8,128)(2,1)}, u32[]{:S(2)}, u32[]{:S(2)}) %collective-permute-start.5) | collective-permute-done | bytes 417824 | tf_op jit(solution)/shard_map/ppermute | solution.py:107
  85.2 1.3 collective-permute-start.9
  86.5 0.7 slice_bitcast_fusion.1
  87.2 1.4 collective-permute-start.10
  88.6 1.6 collective-permute-start.15
  90.2 0.7 slice_bitcast_fusion
  90.9 4.5 %collective-permute-done.9.refs_4_ = bf16[136,1536]{1,0:T(8,128)(2,1)} collective-permute-done((bf16[136,1536]{1,0:T(8,128)(2,1)}, bf16[136,1536]{1,0:T(8,128)(2,1)}, u32[]{:S(2)}, u32[]{:S(2)}) %collective-permute-start.9) | collective-permute-done | bytes 417824 | tf_op jit(solution)/shard_map/ppermute | solution.py:377
  95.4 0.7 slice.51
  96.2 3.4 %collective-permute-start.11 = (bf16[136,1536]{1,0:T(8,128)(2,1)}, bf16[136,1536]{1,0:T(8,128)(2,1)}, u32[]{:S(2)}, u32[]{:S(2)}) collective-permute-start(bf16[136,1536]{1,0:T(8,128)(2,1)} %collective-permute-done.9.refs_4_), channel_id=1, source_target_pairs={{0,2},{2,0},{12,14},{14,12},{1,3},{3,1},{13,15},{15,13},{16,18},{1... | collective-permute-start | bytes 1253384 | tf_op jit(solution)/shard_map/ppermute | solution.py:342
  99.6 0.6 gather_fusion
  101.5 0.6 collective-permute-done.15.refs_13_
  102.0 4.4 %collective-permute-done.11.refs_9_ = bf16[136,1536]{1,0:T(8,128)(2,1)} collective-permute-done((bf16[136,1536]{1,0:T(8,128)(2,1)}, bf16[136,1536]{1,0:T(8,128)(2,1)}, u32[]{:S(2)}, u32[]{:S(2)}) %collective-permute-start.11) | collective-permute-done | bytes 417824 | tf_op jit(solution)/shard_map/ppermute | solution.py:342
  106.4 1.0 copy-done.3
  107.4 1.0 copy-done.6
  108.4 6.8 %shard_map.64 = (f32[4,128,256]{2,1,0:T(8,128)S(1)}, f32[4,256,512]{2,1,0:T(8,128)S(1)}, bf16[4,320,512]{2,1,0:T(8,128)(2,1)S(1)}) custom-call(s32[4]{0:T(128)S(1)} %pad_add_fusion.1.place_ref, bf16[128,1536]{1,0:T(8,128)(2,1)S(1)} %dynamic-slice_bitcast_fusion.2.refs_0_, bf16[128,1536]{1,0:T(8,128)(2,1)S(1)} %copy-done.3, ...), custom_call_target="tpu_custom_call" | custom-call | flops 19327352832 | bytes 8053063 | tf_op jit(solution)/shard_map/pallas_call | solution.py:184
  115.3 4.9 %shard_map.65 = (f32[4,128,128]{2,1,0:T(8,128)S(1)}, f32[4,256,256]{2,1,0:T(8,128)S(1)}, bf16[4,320,256]{2,1,0:T(8,128)(2,1)S(1)}) custom-call(s32[4]{0:T(128)S(1)} %pad_add_fusion.1.place_ref, bf16[128,1536]{1,0:T(8,128)(2,1)S(1)} %dynamic-slice_bitcast_fusion.2.refs_0_, bf16[128,1536]{1,0:T(8,128)(2,1)S(1)} %copy-done.4, ...), custom_call_target="tpu_custom_call" | custom-call | flops 9663676416 | bytes 4026531 | tf_op jit(solution)/shard_map/pallas_call | solution.py:184
  121.3 3.8 %shard_map.66 = (bf16[2,128,256]{2,1,0:T(8,128)(2,1)S(1)}, bf16[2,128,256]{2,1,0:T(8,128)(2,1)S(1)}) custom-call(s32[4]{0:T(128)S(1)} %pad_add_fusion.1.place_ref, s32[16]{0:T(128)S(1)} %reshape.24.members_ref, s32[4]{0:T(128)S(1)} %slice_reduce_fusion.1.counts_ref, f32[4,128,256]{2,1,0:T(8,128)S(1)} %get-tuple-element.42.q_ref, ...), custom_call_target="tpu_custom_call" | custom-call | flops 268435456 | bytes 2097152 | tf_op jit(solution)/shard_map/pallas_call | solution.py:115
  125.1 2.2 %shard_map.67 = (bf16[2,128,384]{2,1,0:T(8,128)(2,1)S(1)}, bf16[2,128,384]{2,1,0:T(8,128)(2,1)S(1)}) custom-call(s32[4]{0:T(128)S(1)} %pad_add_fusion.1.place_ref, s32[16]{0:T(128)S(1)} %reshape.24.members_ref, s32[4]{0:T(128)S(1)} %slice_reduce_fusion.1.counts_ref, f32[4,128,128]{2,1,0:T(8,128)S(1)} %get-tuple-element.39.q_ref, ...), custom_call_target="tpu_custom_call" | custom-call | flops 134217728 | bytes 1048576 | tf_op jit(solution)/shard_map/pallas_call | solution.py:115
  127.3 4.8 %collective-permute-start.18 = (bf16[2,128,384]{2,1,0:T(8,128)(2,1)S(1)}, bf16[2,128,384]{2,1,0:T(8,128)(2,1)S(1)}, u32[]{:S(2)}, u32[]{:S(2)}) collective-permute-start(bf16[2,128,384]{2,1,0:T(8,128)(2,1)S(1)} %get-tuple-element.47), channel_id=1, source_target_pairs={{0,4},{4,0},{8,12},{12,8},{1,5},{5,1},{9,13},{13,9},{2,6},{6,2},{1... | collective-permute-start | bytes 589832 | tf_op jit(solution)/shard_map/ppermute | solution.py:107
  132.0 2.3 %collective-permute-start.19 = (bf16[2,128,384]{2,1,0:T(8,128)(2,1)S(1)}, bf16[2,128,384]{2,1,0:T(8,128)(2,1)S(1)}, u32[]{:S(2)}, u32[]{:S(2)}) collective-permute-start(bf16[2,128,384]{2,1,0:T(8,128)(2,1)S(1)} %get-tuple-element.46.refs_0_), channel_id=1, source_target_pairs={{0,8},{4,12},{8,0},{12,4},{1,9},{5,13},{9,1},{13,5},{2,10},{6,14},... | collective-permute-start | bytes 589832 | tf_op jit(solution)/shard_map/ppermute | solution.py:107
  134.4 1.4 collective-permute-start.20
  135.8 5.5 %collective-permute-done.18.refs_1_ = bf16[2,128,384]{2,1,0:T(8,128)(2,1)S(1)} collective-permute-done((bf16[2,128,384]{2,1,0:T(8,128)(2,1)S(1)}, bf16[2,128,384]{2,1,0:T(8,128)(2,1)S(1)}, u32[]{:S(2)}, u32[]{:S(2)}) %collective-permute-start.18) | collective-permute-done | bytes 196640 | tf_op jit(solution)/shard_map/ppermute | solution.py:107
  141.3 7.9 %collective-permute-done.19.refs_2_ = bf16[2,128,384]{2,1,0:T(8,128)(2,1)S(1)} collective-permute-done((bf16[2,128,384]{2,1,0:T(8,128)(2,1)S(1)}, bf16[2,128,384]{2,1,0:T(8,128)(2,1)S(1)}, u32[]{:S(2)}, u32[]{:S(2)}) %collective-permute-start.19) | collective-permute-done | bytes 196640 | tf_op jit(solution)/shard_map/ppermute | solution.py:107
  149.2 2.8 %shard_map.69 = (f32[2,64,768]{2,1,0:T(8,128)S(1)}, bf16[2,64,768]{2,1,0:T(8,128)(2,1)S(1)}) custom-call(s32[4]{0:T(128)S(1)} %pad_add_fusion.1.place_ref, bf16[2,128,384]{2,1,0:T(8,128)(2,1)S(1)} %get-tuple-element.46.refs_0_, bf16[2,128,384]{2,1,0:T(8,128)(2,1)S(1)} %collective-permute-done.18.refs_1_, ...), custom_call_target="tpu_custom_call" | custom-call | flops 603979776 | bytes 4718592 | tf_op jit(solution)/shard_map/pallas_call | solution.py:115
  152.0 1.6 collective-permute-start.23
  153.6 2.8 %shard_map.68 = (f32[2,64,768]{2,1,0:T(8,128)S(1)}, bf16[2,64,768]{2,1,0:T(8,128)(2,1)S(1)}) custom-call(s32[4]{0:T(128)S(1)} %pad_add_fusion.1.place_ref, bf16[2,128,384]{2,1,0:T(8,128)(2,1)S(1)} %get-tuple-element.46.refs_0_, bf16[2,128,384]{2,1,0:T(8,128)(2,1)S(1)} %collective-permute-done.18.refs_1_, ...), custom_call_target="tpu_custom_call" | custom-call | flops 603979776 | bytes 4718592 | tf_op jit(solution)/shard_map/pallas_call | solution.py:115
  156.4 1.6 collective-permute-done.23
  158.1 5.8 %collective-permute-start.25 = (bf16[2,64,768]{2,1,0:T(8,128)(2,1)S(1)}, bf16[2,64,768]{2,1,0:T(8,128)(2,1)S(1)}, u32[]{:S(2)}, u32[]{:S(2)}) collective-permute-start(bf16[2,64,768]{2,1,0:T(8,128)(2,1)S(1)} %add_convert_fusion), channel_id=1, source_target_pairs={{0,8},{4,12},{8,0},{12,4},{1,9},{5,13},{9,1},{13,5},{2,10},{6,14},... | collective-permute-start | bytes 589832 | tf_op jit(solution)/shard_map/ppermute | solution.py:107
  163.9 1.1 collective-permute-start.24
  165.0 6.4 %collective-permute-done.25.far_ref = bf16[2,64,768]{2,1,0:T(8,128)(2,1)S(1)} collective-permute-done((bf16[2,64,768]{2,1,0:T(8,128)(2,1)S(1)}, bf16[2,64,768]{2,1,0:T(8,128)(2,1)S(1)}, u32[]{:S(2)}, u32[]{:S(2)}) %collective-permute-start.25) | collective-permute-done | bytes 196640 | tf_op jit(solution)/shard_map/ppermute | solution.py:107
  171.4 1.3 shard_map.70
  (65 shorter events, 3.1 us)
Async XLA Ops:
  0.0 1.1 copy-start
  1.2 16.1 %collective-permute-start = (bf16[128,1536]{1,0:T(8,128)(2,1)S(1)}, bf16[128,1536]{1,0:T(8,128)(2,1)S(1)}, u32[]{:S(2)}, u32[]{:S(2)}) collective-permute-start(bf16[128,1536]{1,0:T(8,128)(2,1)S(1)} %dynamic-slice_bitcast_fusion.2.refs_0_), channel_id=1, source_target_pairs={{0,4},{4,0},{8,12},{12,8},{1,5},{5,1},{9,13},{13,9},{2,6},{6,2},{1... | collective-permute-start | bytes 1179656 | tf_op jit(solution)/shard_map/ppermute | solution.py:107
  4.3 16.6 %collective-permute-start.3 = (bf16[128,1536]{1,0:T(8,128)(2,1)S(1)}, bf16[128,1536]{1,0:T(8,128)(2,1)}, u32[]{:S(2)}, u32[]{:S(2)}) collective-permute-start(bf16[128,1536]{1,0:T(8,128)(2,1)S(1)} %dynamic-slice_bitcast_fusion.2.refs_0_), channel_id=1, source_target_pairs={{0,2},{2,0},{1,3},{3,1},{4,6},{6,4},{5,7},{7,5},{8,10},{10,8},{9,1... | collective-permute-start | bytes 1179656 | tf_op jit(solution)/shard_map/ppermute | solution.py:107
  5.7 11.2 %copy-start.10 = (s32[2]{0:T(128)S(1)}, s32[2]{0:T(128)}, u32[]{:S(2)}) copy-start(s32[2]{0:T(128)} %param.11) | copy-start | bytes 28
  5.7 11.3 %copy-start.11 = (s32[2]{0:T(128)S(1)}, s32[2]{0:T(128)}, u32[]{:S(2)}) copy-start(s32[2]{0:T(128)} %param.10) | copy-start | bytes 28
  5.7 11.3 %copy-start.1 = (bf16[768,768]{1,0:T(8,128)(2,1)S(1)}, bf16[768,768]{1,0:T(8,128)(2,1)}, u32[]{:S(2)}) copy-start(bf16[768,768]{1,0:T(8,128)(2,1)} %refs_4_.3) | copy-start | bytes 3538948
  5.8 11.4 %copy-start.9 = (s32[2,4]{1,0:T(2,128)S(1)}, s32[2,4]{1,0:T(2,128)}, u32[]{:S(2)}) copy-start(s32[2,4]{1,0:T(2,128)} %param.9) | copy-start | bytes 100
  8.7 47.6 %collective-permute-start.2 = (bf16[3,384,384]{2,1,0:T(8,128)(2,1)}, bf16[3,384,384]{2,1,0:T(8,128)(2,1)}, u32[]{:S(2)}, u32[]{:S(2)}) collective-permute-start(bf16[3,384,384]{2,1,0:T(8,128)(2,1)} %get-tuple-element.54), channel_id=1, source_target_pairs={{0,0},{1,8},{4,4},{5,12},{8,1},{9,9},{12,5},{13,13},{2,2},{3,10},{... | collective-permute-start | bytes 2654216 | tf_op jit(solution)/shard_map/ppermute | solution.py:353
  17.2 0.7 copy-start.2
  18.0 13.2 %copy-start.8 = (bf16[136,1536]{1,0:T(8,128)(2,1)}, bf16[136,1536]{1,0:T(8,128)(2,1)S(1)}, u32[]{:S(2)}) copy-start(bf16[136,1536]{1,0:T(8,128)(2,1)S(1)} %pad_maximum_fusion.1) | copy-start | bytes 1253380
  18.0 5.5 %collective-permute-start.4 = (bf16[136,1536]{1,0:T(8,128)(2,1)S(1)}, bf16[136,1536]{1,0:T(8,128)(2,1)}, u32[]{:S(2)}, u32[]{:S(2)}) collective-permute-start(bf16[136,1536]{1,0:T(8,128)(2,1)S(1)} %pad_maximum_fusion.1), channel_id=1, source_target_pairs={{4,8},{8,4},{5,9},{9,5},{6,10},{10,6},{7,11},{11,7},{20,24},{24,20... | collective-permute-start | bytes 1253384 | tf_op jit(solution)/shard_map/ppermute | solution.py:367
  19.4 65.8 %collective-permute-start.6 = (bf16[768,768]{1,0:T(8,128)(2,1)S(1)}, bf16[768,768]{1,0:T(8,128)(2,1)S(1)}, u32[]{:S(2)}, u32[]{:S(2)}) collective-permute-start(bf16[768,768]{1,0:T(8,128)(2,1)S(1)} %copy-done.1), channel_id=1, source_target_pairs={{0,1},{1,0},{2,3},{3,2},{4,5},{5,4},{6,7},{7,6},{8,9},{9,8},{10,11... | collective-permute-start | bytes 3538952 | tf_op jit(solution)/shard_map/ppermute | solution.py:107
  19.4 11.7 %collective-permute-start.7 = (bf16[128,1536]{1,0:T(8,128)(2,1)}, bf16[128,1536]{1,0:T(8,128)(2,1)S(1)}, u32[]{:S(2)}, u32[]{:S(2)}) collective-permute-start(bf16[128,1536]{1,0:T(8,128)(2,1)} %copy-done.2), channel_id=1, source_target_pairs={{0,2},{2,0},{1,3},{3,1},{4,6},{6,4},{5,7},{7,5},{8,10},{10,8},{9,1... | collective-permute-start | bytes 1179656 | tf_op jit(solution)/shard_map/ppermute | solution.py:107
  20.9 36.9 %collective-permute-start.1 = (bf16[392,768]{1,0:T(8,128)(2,1)}, bf16[392,768]{1,0:T(8,128)(2,1)}, u32[]{:S(2)}, u32[]{:S(2)}) collective-permute-start(bf16[392,768]{1,0:T(8,128)(2,1)} %pad_maximum_fusion), channel_id=1, source_target_pairs={{0,4},{4,0},{8,12},{12,8},{1,5},{5,1},{9,13},{13,9},{2,6},{6,2},{1... | collective-permute-start | bytes 1806344 | tf_op jit(solution)/shard_map/ppermute | solution.py:107
  23.5 34.2 %collective-permute-start.8 = (bf16[136,1536]{1,0:T(8,128)(2,1)}, bf16[136,1536]{1,0:T(8,128)(2,1)}, u32[]{:S(2)}, u32[]{:S(2)}) collective-permute-start(bf16[136,1536]{1,0:T(8,128)(2,1)} %collective-permute-done.4.refs_3_), channel_id=1, source_target_pairs={{4,6},{6,4},{8,10},{10,8},{5,7},{7,5},{9,11},{11,9},{20,22},{22,20... | collective-permute-start | bytes 1253384 | tf_op jit(solution)/shard_map/ppermute | solution.py:342
  31.2 0.8 copy-start.5
  32.0 56.6 %collective-permute-start.13 = (bf16[3,384,384]{2,1,0:T(8,128)(2,1)}, bf16[3,384,384]{2,1,0:T(8,128)(2,1)}, u32[]{:S(2)}, u32[]{:S(2)}) collective-permute-start(bf16[3,384,384]{2,1,0:T(8,128)(2,1)} %get-tuple-element.34), channel_id=1, source_target_pairs={{0,4},{1,12},{4,0},{5,8},{8,5},{9,13},{12,1},{13,9},{2,6},{3,14},{... | collective-permute-start | bytes 2654216 | tf_op jit(solution)/shard_map/ppermute | solution.py:353
  56.3 32.4 %collective-permute-start.12 = (bf16[3,384,384]{2,1,0:T(8,128)(2,1)}, bf16[3,384,384]{2,1,0:T(8,128)(2,1)}, u32[]{:S(2)}, u32[]{:S(2)}) collective-permute-start(bf16[3,384,384]{2,1,0:T(8,128)(2,1)} %collective-permute-done.2.refs_10_), channel_id=1, source_target_pairs={{0,16},{16,0},{1,17},{17,1},{2,18},{18,2},{3,19},{19,3},{4,20},{20... | collective-permute-start | bytes 2654216 | tf_op jit(solution)/shard_map/ppermute | solution.py:107
  57.8 27.4 %collective-permute-start.5 = (bf16[136,1536]{1,0:T(8,128)(2,1)}, bf16[136,1536]{1,0:T(8,128)(2,1)}, u32[]{:S(2)}, u32[]{:S(2)}) collective-permute-start(bf16[136,1536]{1,0:T(8,128)(2,1)} %copy-done.8), channel_id=1, source_target_pairs={{0,8},{4,12},{8,0},{12,4},{1,9},{5,13},{9,1},{13,5},{2,10},{6,14},... | collective-permute-start | bytes 1253384 | tf_op jit(solution)/shard_map/ppermute | solution.py:107
  57.8 30.8 %collective-permute-start.14 = (bf16[392,768]{1,0:T(8,128)(2,1)}, bf16[392,768]{1,0:T(8,128)(2,1)}, u32[]{:S(2)}, u32[]{:S(2)}) collective-permute-start(bf16[392,768]{1,0:T(8,128)(2,1)} %collective-permute-done.1.refs_6_), channel_id=1, source_target_pairs={{0,16},{16,0},{1,17},{17,1},{2,18},{18,2},{3,19},{19,3},{4,20},{20... | collective-permute-start | bytes 1806344 | tf_op jit(solution)/shard_map/ppermute | solution.py:107
  85.2 10.2 %collective-permute-start.9 = (bf16[136,1536]{1,0:T(8,128)(2,1)}, bf16[136,1536]{1,0:T(8,128)(2,1)}, u32[]{:S(2)}, u32[]{:S(2)}) collective-permute-start(bf16[136,1536]{1,0:T(8,128)(2,1)} %collective-permute-done.5.refs_2_), channel_id=1, source_target_pairs={{4,0},{8,12},{5,1},{9,13},{6,2},{10,14},{7,3},{11,15},{20,16},{24,... | collective-permute-start | bytes 1253384 | tf_op jit(solution)/shard_map/ppermute | solution.py:377
  87.2 14.9 %collective-permute-start.10 = (bf16[136,1536]{1,0:T(8,128)(2,1)}, bf16[136,1536]{1,0:T(8,128)(2,1)}, u32[]{:S(2)}, u32[]{:S(2)}) collective-permute-start(bf16[136,1536]{1,0:T(8,128)(2,1)} %collective-permute-done.5.refs_2_), channel_id=1, source_target_pairs={{0,2},{2,0},{1,3},{3,1},{4,6},{6,4},{5,7},{7,5},{8,10},{10,8},{9,1... | collective-permute-start | bytes 1253384 | tf_op jit(solution)/shard_map/ppermute | solution.py:107
  88.6 13.4 %collective-permute-start.15 = (bf16[3,384,384]{2,1,0:T(8,128)(2,1)}, bf16[3,384,384]{2,1,0:T(8,128)(2,1)}, u32[]{:S(2)}, u32[]{:S(2)}) collective-permute-start(bf16[3,384,384]{2,1,0:T(8,128)(2,1)} %collective-permute-done.13.refs_12_), channel_id=1, source_target_pairs={{0,16},{16,0},{1,17},{17,1},{2,18},{18,2},{3,19},{19,3},{4,20},{20... | collective-permute-start | bytes 2654216 | tf_op jit(solution)/shard_map/ppermute | solution.py:107
  96.2 10.2 %collective-permute-start.11 = (bf16[136,1536]{1,0:T(8,128)(2,1)}, bf16[136,1536]{1,0:T(8,128)(2,1)}, u32[]{:S(2)}, u32[]{:S(2)}) collective-permute-start(bf16[136,1536]{1,0:T(8,128)(2,1)} %collective-permute-done.9.refs_4_), channel_id=1, source_target_pairs={{0,2},{2,0},{12,14},{14,12},{1,3},{3,1},{13,15},{15,13},{16,18},{1... | collective-permute-start | bytes 1253384 | tf_op jit(solution)/shard_map/ppermute | solution.py:342
  106.4 1.0 copy-start.3
  107.4 1.0 copy-start.6
  108.4 6.9 %copy-start.4 = (bf16[128,1536]{1,0:T(8,128)(2,1)S(1)}, bf16[128,1536]{1,0:T(8,128)(2,1)}, u32[]{:S(2)}) copy-start(bf16[128,1536]{1,0:T(8,128)(2,1)} %copy-done.2) | copy-start | bytes 1179652
  108.4 6.9 %copy-start.7 = (bf16[128,1536]{1,0:T(8,128)(2,1)S(1)}, bf16[128,1536]{1,0:T(8,128)(2,1)}, u32[]{:S(2)}) copy-start(bf16[128,1536]{1,0:T(8,128)(2,1)} %copy-done.5) | copy-start | bytes 1179652
  115.2 6.1 %collective-permute-start.17 = (bf16[4,320,512]{2,1,0:T(8,128)(2,1)S(1)}, bf16[4,320,512]{2,1,0:T(8,128)(2,1)S(1)}, u32[]{:S(2)}, u32[]{:S(2)}) collective-permute-start(bf16[4,320,512]{2,1,0:T(8,128)(2,1)S(1)} %get-tuple-element.37), channel_id=1, source_target_pairs={{0,1},{1,0},{2,3},{3,2},{4,5},{5,4},{6,7},{7,6},{8,9},{9,8},{10,11... | collective-permute-start | bytes 3932168 | tf_op jit(solution)/shard_map/ppermute | solution.py:107
  120.2 4.8 %collective-permute-start.16 = (bf16[4,320,256]{2,1,0:T(8,128)(2,1)S(1)}, bf16[4,320,256]{2,1,0:T(8,128)(2,1)S(1)}, u32[]{:S(2)}, u32[]{:S(2)}) collective-permute-start(bf16[4,320,256]{2,1,0:T(8,128)(2,1)S(1)} %get-tuple-element.41), channel_id=1, source_target_pairs={{0,1},{1,0},{2,3},{3,2},{4,5},{5,4},{6,7},{7,6},{8,9},{9,8},{10,11... | collective-permute-start | bytes 1966088 | tf_op jit(solution)/shard_map/ppermute | solution.py:107
  120.7 15.0 %collective-permute-start.21 = (bf16[392,768]{1,0:T(8,128)(2,1)}, bf16[392,768]{1,0:T(8,128)(2,1)S(1)}, u32[]{:S(2)}, u32[]{:S(2)}) collective-permute-start(bf16[392,768]{1,0:T(8,128)(2,1)} %collective-permute-done.1.refs_6_), channel_id=1, source_target_pairs={{0,1},{1,0},{2,3},{3,2},{4,5},{5,4},{6,7},{7,6},{8,9},{9,8},{10,11... | collective-permute-start | bytes 1806344 | tf_op jit(solution)/shard_map/ppermute | solution.py:107
  120.8 14.9 %collective-permute-start.22 = (bf16[392,768]{1,0:T(8,128)(2,1)}, bf16[392,768]{1,0:T(8,128)(2,1)S(1)}, u32[]{:S(2)}, u32[]{:S(2)}) collective-permute-start(bf16[392,768]{1,0:T(8,128)(2,1)} %collective-permute-done.14.refs_7_), channel_id=1, source_target_pairs={{0,1},{1,0},{2,3},{3,2},{4,5},{5,4},{6,7},{7,6},{8,9},{9,8},{10,11... | collective-permute-start | bytes 1806344 | tf_op jit(solution)/shard_map/ppermute | solution.py:107
  127.3 14.0 %collective-permute-start.18 = (bf16[2,128,384]{2,1,0:T(8,128)(2,1)S(1)}, bf16[2,128,384]{2,1,0:T(8,128)(2,1)S(1)}, u32[]{:S(2)}, u32[]{:S(2)}) collective-permute-start(bf16[2,128,384]{2,1,0:T(8,128)(2,1)S(1)} %get-tuple-element.47), channel_id=1, source_target_pairs={{0,4},{4,0},{8,12},{12,8},{1,5},{5,1},{9,13},{13,9},{2,6},{6,2},{1... | collective-permute-start | bytes 589832 | tf_op jit(solution)/shard_map/ppermute | solution.py:107
  132.0 17.1 %collective-permute-start.19 = (bf16[2,128,384]{2,1,0:T(8,128)(2,1)S(1)}, bf16[2,128,384]{2,1,0:T(8,128)(2,1)S(1)}, u32[]{:S(2)}, u32[]{:S(2)}) collective-permute-start(bf16[2,128,384]{2,1,0:T(8,128)(2,1)S(1)} %get-tuple-element.46.refs_0_), channel_id=1, source_target_pairs={{0,8},{4,12},{8,0},{12,4},{1,9},{5,13},{9,1},{13,5},{2,10},{6,14},... | collective-permute-start | bytes 589832 | tf_op jit(solution)/shard_map/ppermute | solution.py:107
  134.4 14.8 %collective-permute-start.20 = (bf16[2,128,384]{2,1,0:T(8,128)(2,1)S(1)}, bf16[2,128,384]{2,1,0:T(8,128)(2,1)S(1)}, u32[]{:S(2)}, u32[]{:S(2)}) collective-permute-start(bf16[2,128,384]{2,1,0:T(8,128)(2,1)S(1)} %get-tuple-element.47), channel_id=1, source_target_pairs={{0,12},{4,8},{8,4},{12,0},{1,13},{5,9},{9,5},{13,1},{2,14},{6,10},... | collective-permute-start | bytes 589832 | tf_op jit(solution)/shard_map/ppermute | solution.py:107
  152.0 6.0 %collective-permute-start.23 = (bf16[2,64,768]{2,1,0:T(8,128)(2,1)S(1)}, bf16[2,64,768]{2,1,0:T(8,128)(2,1)S(1)}, u32[]{:S(2)}, u32[]{:S(2)}) collective-permute-start(bf16[2,64,768]{2,1,0:T(8,128)(2,1)S(1)} %get-tuple-element.50), channel_id=1, source_target_pairs={{0,2},{2,0},{1,3},{3,1},{4,6},{6,4},{5,7},{7,5},{8,10},{10,8},{9,1... | collective-permute-start | bytes 589832 | tf_op jit(solution)/shard_map/ppermute | solution.py:107
  158.1 13.3 %collective-permute-start.25 = (bf16[2,64,768]{2,1,0:T(8,128)(2,1)S(1)}, bf16[2,64,768]{2,1,0:T(8,128)(2,1)S(1)}, u32[]{:S(2)}, u32[]{:S(2)}) collective-permute-start(bf16[2,64,768]{2,1,0:T(8,128)(2,1)S(1)} %add_convert_fusion), channel_id=1, source_target_pairs={{0,8},{4,12},{8,0},{12,4},{1,9},{5,13},{9,1},{13,5},{2,10},{6,14},... | collective-permute-start | bytes 589832 | tf_op jit(solution)/shard_map/ppermute | solution.py:107
  163.9 7.5 %collective-permute-start.24 = (bf16[2,64,768]{2,1,0:T(8,128)(2,1)S(1)}, bf16[2,64,768]{2,1,0:T(8,128)(2,1)S(1)}, u32[]{:S(2)}, u32[]{:S(2)}) collective-permute-start(bf16[2,64,768]{2,1,0:T(8,128)(2,1)S(1)} %get-tuple-element.51), channel_id=1, source_target_pairs={{0,2},{2,0},{1,3},{3,1},{4,6},{6,4},{5,7},{7,5},{8,10},{10,8},{9,1... | collective-permute-start | bytes 589832 | tf_op jit(solution)/shard_map/ppermute | solution.py:107

commit v27 on v24

--- a/solution.py
+++ b/solution.py
@@ -127,7 +127,7 @@
     )(*prefetch, *operands)
 
 
-def project(place, mine, theirs, chunks, first, cols):
+def project(place, mine, theirs, chunks, firsts, cols):
     rows, (count, width) = len(mine), theirs[0].shape
     half = chunks[0][0].shape[1]
     slices = len(chunks)
@@ -143,7 +143,7 @@
             for g in range(2):
                 at = pl.multiple_of((row + slices - k) % slices * (2 * half) + (group + g) % 2 * half, half)
                 for part in range(3):
-                    source = w_refs[2 * k + g].at[part, :, first : first + cols]
+                    source = w_refs[2 * k + g].at[part, :, firsts[k] : firsts[k] + cols]
                     into = w_all.at[pl.ds(at, half), part * cols : (part + 1) * cols]
                     copies.append(pltpu.make_async_copy(source, into, sems.at[len(copies)]))
         fetch_x = []
@@ -328,10 +328,11 @@
     half = depth // 2
     place = jnp.stack([row, group, frame, core]).astype(jnp.int32)
 
-    def reshard(k, *others):
-        value = lax.dynamic_slice(
-            w_qkv.transpose(1, 0, 2), (0, group * half, (k + row) % span * cols), (3, half, cols)
-        )
+    last = cols // (3 * HD) * HD
+
+    def reshard(k, at, wide, *others):
+        start = (0, group * half, (k + row) % span * cols + at)
+        value = lax.dynamic_slice(w_qkv.transpose(1, 0, 2), start, (3, half, wide))
         pairs = [
             (r * heads_n + h, (h * span + (k + r) % span) * heads_n + r // span)
             for r in range(rows_n)
@@ -341,12 +342,12 @@
 
     mine = lax.dynamic_slice_in_dim(latents[0], core * span * depth, span * depth, axis=1)
     mine_x = swap(mine, "frames")
-    here, there = [reshard(0)], []
+    here, there = [reshard(0, 0, cols)], []
     near = swap(mine, "rows")
     near_x = swap(near, "frames")
     across = swap(after(w_out, near), "heads")
     there.append(swap(here[0], "groups"))
-    here.append(reshard(1, near))
+    here.append(reshard(1, 0, cols - last, near))
     tables = jnp.concatenate([win_blocks, win_counts[:, None], block_window[:, None]], axis=1)
     tables = after(tables, near)
     tables = jnp.pad(tables, ((0, 8 - heads_n), (0, span * depth - MAXB - 2))).astype(mine.dtype)
@@ -360,6 +361,8 @@
     far_2x = swap(far_2, "frames")
     far_3 = swap(after(joined, far_2, across, near_x, beside[0]), "rows", 3)
     far_3x = swap(far_3, "frames")
+    here.append(reshard(1, cols - last, last, far_3))
+    there.append(swap(here[2], "groups"))
 
     found = [tables, beside[0][cols:], far_2[count:], far_3[count:]]
     found = jnp.stack([x[:heads_n, : MAXB + 2] for x in found])
@@ -372,11 +375,10 @@
 
     pieces = [mine, near, far_2, far_3], [mine_x, near_x, far_2x, far_3x]
     chunks = [(here[0], there[0]), (here[1], after(there[1], members, counts))]
-    last = cols // (3 * HD) * HD
-    first = project(place, *pieces, chunks, 0, cols - last)
+    first = project(place, *pieces, chunks, (0, 0), cols - last)
     first_more = swap(first[2], "heads")
-    chunks[1] = (here[1], after(there[1], first[2]))
-    second = project(place, *pieces, chunks, cols - last, last)
+    chunks[1] = (here[2], after(there[2], first[2]))
+    second = project(place, *pieces, chunks, (cols - last, 0), last)
     second_more = swap(second[2], "heads")
     attended = attend_all(place, members, counts, *first[:2], first_more)
     beside_across = [swap(part, "heads") for part in beside]

time: 159 us -> 159 us (level)
  waiting for transfers between devices: 80.7 us -> 39.5 us
  starting transfers between devices: 42.4 us -> 76.5 us
  local copies, waits for them, and re-layouts: 8.08 us -> 13.1 us
    ppermute x22 -> x23, waiting for transfers between devices: 80.7 us -> 37.7 us  [swap(): return lax.ppermute(value, axis, [(i, i ^ step) for i in range(peers)])]
    ppermute x22 -> x23, starting transfers between devices: 34.2 us -> 52.9 us  [swap(): return lax.ppermute(value, axis, [(i, i ^ step) for i in range(peers)])]
    ppermute x2 -> x3, starting transfers between devices: 8.24 us -> 23.6 us  [reshard(): lax.ppermute(after(value, *others) if others else value, ('rows', 'heads'...]
    unnamed x10 -> x22, local copies, waits for them, and re-layouts: 1.15 us -> 3.88 us
    dynamic_slice x1, local copies, waits for them, and re-layouts: 0.03 us -> 1.92 us  [by_heads(): lax.dynamic_slice_in_dim(latents[0], core * span * depth, span * depth, a...]
    ppermute x2 -> x3, waiting for transfers between devices: 0.01 us -> 1.89 us  [reshard(): lax.ppermute(after(value, *others) if others else value, ('rows', 'heads'...]
  transfers between devices with their start and end apart: 24 -> 26, of which waited for: 10 -> 8; matrix products, arithmetic and copies ran while one was open for 6% -> 7% of each run, Pallas kernels for 9% -> 13%
where the time goes in v27:
time: 159 us; the launch traced here: 158 us
  starting transfers between devices  76.5 us (48%)
  waiting for transfers between devices  39.5 us (25%)
  Pallas kernels  25.4 us (16%)
  local copies, waits for them, and re-layouts  13.1 us (8%)
  other arithmetic  3.46 us (2%)
    ppermute x23, starting transfers between devices, swap(): return lax.ppermute(value, axis, [(i, i ^ step) for i in range(peers)])  52.9 us
    ppermute x23, waiting for transfers between devices, swap(): return lax.ppermute(value, axis, [(i, i ^ step) for i in range(peers)])  37.7 us
    ppermute x3, starting transfers between devices, reshard(): lax.ppermute(after(value, *others) if others else value, ('rows', 'heads'...  23.6 us
    pallas_call x5, Pallas kernels, call(): pl.pallas_call(kernel, out_shape=out_shape, grid_spec=pltpu.PrefetchScala...  13.7 us
    pallas_call x2, Pallas kernels, project(): pl.pallas_call(kernel, out_shape=(jax.ShapeDtypeStruct((rows, 2 * BS, col...  11.7 us
    unnamed x22, local copies, waits for them, and re-layouts  3.88 us
  transfers between devices with their start and end apart: 26, of which 8 were waited for; matrix products, arithmetic and copies ran while one was open for 7% of the time, Pallas kernels for 13%

profile of v27, /device:TPU:0, one launch (start us, length us, event | category | flops | bytes accessed | tf_op | source)
XLA Modules:
  0.0 158.2 jit_solution(11574366522693097747)
XLA Ops:
  0.0 1.9 %dynamic-slice_bitcast_fusion.2.refs_0_ = bf16[128,1536]{1,0:T(8,128)(2,1)} fusion(bf16[1,128,3072]{2,1,0:T(8,128)(2,1)} %param.6, s32[]{:T(128)S(6)} %select_n.49), kind=kLoop, calls=%fused_computation.7 | loop fusion | bytes 786436 | tf_op jit(solution)/shard_map/dynamic_slice | solution.py:343
  1.9 3.0 %collective-permute-start = (bf16[128,1536]{1,0:T(8,128)(2,1)}, bf16[128,1536]{1,0:T(8,128)(2,1)}, u32[]{:S(2)}, u32[]{:S(2)}) collective-permute-start(bf16[128,1536]{1,0:T(8,128)(2,1)} %dynamic-slice_bitcast_fusion.2.refs_0_), channel_id=1, source_target_pairs={{0,4},{4,0},{8,12},{12,8},{1,5},{5,1},{9,13},{13,9},{2,6},{6,2},{1... | collective-permute-start | bytes 1179656 | tf_op jit(solution)/shard_map/ppermute | solution.py:107
  4.9 1.5 collective-permute-start.3
  6.4 1.0 dynamic-slice_bitcast_fusion
  7.5 8.2 %collective-permute-start.2 = (bf16[3,384,384]{2,1,0:T(8,128)(2,1)}, bf16[3,384,384]{2,1,0:T(8,128)(2,1)}, u32[]{:S(2)}, u32[]{:S(2)}) collective-permute-start(bf16[3,384,384]{2,1,0:T(8,128)(2,1)} %dynamic-slice_bitcast_fusion), channel_id=1, source_target_pairs={{0,0},{1,8},{4,4},{5,12},{8,1},{9,9},{12,5},{13,13},{2,2},{3,10},{... | collective-permute-start | bytes 2654216 | tf_op jit(solution)/shard_map/ppermute | solution.py:341
  15.7 0.9 constant_dynamic-slice_fusion
  16.6 0.7 copy.9
  17.6 1.9 %pad_maximum_fusion = bf16[392,768]{1,0:T(8,128)(2,1)} fusion(bf16[8,768]{1,0:T(8,128)(2,1)S(1)} %pad_slice_fusion, bf16[384,768]{1,0:T(8,128)(2,1)} %constant_dynamic-slice_fusion), kind=kLoop, calls=%fused_computation.3 | loop fusion | flops 1204224 | bytes 1204224 | tf_op jit(solution)/shard_map/concatenate | solution.py:357
  19.9 0.8 dynamic-slice_bitcast_fusion.3
  20.7 2.0 %collective-permute-start.6 = (bf16[128,1536]{1,0:T(8,128)(2,1)}, bf16[128,1536]{1,0:T(8,128)(2,1)S(1)}, u32[]{:S(2)}, u32[]{:S(2)}) collective-permute-start(bf16[128,1536]{1,0:T(8,128)(2,1)} %collective-permute-done.refs_1_), channel_id=1, source_target_pairs={{0,2},{2,0},{1,3},{3,1},{4,6},{6,4},{5,7},{7,5},{8,10},{10,8},{9,1... | collective-permute-start | bytes 1179656 | tf_op jit(solution)/shard_map/ppermute | solution.py:107
  22.8 1.0 pad_maximum_fusion.1
  23.8 8.6 %collective-permute-start.4 = (bf16[136,1536]{1,0:T(8,128)(2,1)S(1)}, bf16[136,1536]{1,0:T(8,128)(2,1)}, u32[]{:S(2)}, u32[]{:S(2)}) collective-permute-start(bf16[136,1536]{1,0:T(8,128)(2,1)S(1)} %pad_maximum_fusion.1), channel_id=1, source_target_pairs={{0,8},{4,12},{8,0},{12,4},{1,9},{5,13},{9,1},{13,5},{2,10},{6,14},... | collective-permute-start | bytes 1253384 | tf_op jit(solution)/shard_map/ppermute | solution.py:107
  32.4 1.5 collective-permute-start.10
  34.1 0.8 copy-done.6
  34.8 3.3 %collective-permute-start.13 = (bf16[3,384,256]{2,1,0:T(8,128)(2,1)S(1)}, bf16[3,384,256]{2,1,0:T(8,128)(2,1)}, u32[]{:S(2)}, u32[]{:S(2)}) collective-permute-start(bf16[3,384,256]{2,1,0:T(8,128)(2,1)S(1)} %dynamic-slice_bitcast_fusion.1), channel_id=1, source_target_pairs={{0,4},{1,12},{4,0},{5,8},{8,5},{9,13},{12,1},{13,9},{2,6},{3,14},{... | collective-permute-start | bytes 1769480 | tf_op jit(solution)/shard_map/ppermute | solution.py:341
  38.1 10.8 %collective-permute-done.1.refs_6_ = bf16[392,768]{1,0:T(8,128)(2,1)} collective-permute-done((bf16[392,768]{1,0:T(8,128)(2,1)}, bf16[392,768]{1,0:T(8,128)(2,1)}, u32[]{:S(2)}, u32[]{:S(2)}) %collective-permute-start.1) | collective-permute-done | bytes 602144 | tf_op jit(solution)/shard_map/ppermute | solution.py:107
  49.0 1.5 collective-permute-start.14
  50.5 17.4 %collective-permute-start.7 = (bf16[136,1536]{1,0:T(8,128)(2,1)S(1)}, bf16[136,1536]{1,0:T(8,128)(2,1)}, u32[]{:S(2)}, u32[]{:S(2)}) collective-permute-start(bf16[136,1536]{1,0:T(8,128)(2,1)S(1)} %pad_maximum_fusion.1), channel_id=1, source_target_pairs={{0,12},{4,8},{8,4},{12,0},{1,13},{5,9},{9,5},{13,1},{2,14},{6,10},... | collective-permute-start | bytes 1253384 | tf_op jit(solution)/shard_map/ppermute | solution.py:107
  67.9 0.7 slice_bitcast_fusion.2
  68.6 0.8 collective-permute-start.8
  69.4 0.7 slice_bitcast_fusion.1
  70.1 0.9 copy-done.3
  71.1 1.5 collective-permute-start.15
  72.6 1.6 collective-permute-done.7.refs_3_
  74.1 12.1 %collective-permute-start.11 = (bf16[3,384,128]{2,1,0:T(8,128)(2,1)}, bf16[3,384,128]{2,1,0:T(8,128)(2,1)}, u32[]{:S(2)}, u32[]{:S(2)}) collective-permute-start(bf16[3,384,128]{2,1,0:T(8,128)(2,1)} %dynamic-slice_bitcast_fusion.3), channel_id=1, source_target_pairs={{0,4},{1,12},{4,0},{5,8},{8,5},{9,13},{12,1},{13,9},{2,6},{3,14},{... | collective-permute-start | bytes 884744 | tf_op jit(solution)/shard_map/ppermute | solution.py:341
  86.8 0.7 slice_bitcast_fusion
  87.5 0.6 gather_fusion
  89.4 1.9 %collective-permute-done.11.refs_10_ = bf16[3,384,128]{2,1,0:T(8,128)(2,1)} collective-permute-done((bf16[3,384,128]{2,1,0:T(8,128)(2,1)}, bf16[3,384,128]{2,1,0:T(8,128)(2,1)}, u32[]{:S(2)}, u32[]{:S(2)}) %collective-permute-start.11) | collective-permute-done | bytes 294944 | tf_op jit(solution)/shard_map/ppermute | solution.py:341
  91.3 1.5 collective-permute-start.12
  92.8 1.8 %collective-permute-done.9.refs_7_ = bf16[136,1536]{1,0:T(8,128)(2,1)} collective-permute-done((bf16[136,1536]{1,0:T(8,128)(2,1)}, bf16[136,1536]{1,0:T(8,128)(2,1)}, u32[]{:S(2)}, u32[]{:S(2)}) %collective-permute-start.9) | collective-permute-done | bytes 417824 | tf_op jit(solution)/shard_map/ppermute | solution.py:107
  94.6 1.2 copy-done.4
  95.8 1.0 copy-done.7
  96.8 6.8 %shard_map.64 = (f32[4,128,256]{2,1,0:T(8,128)S(1)}, f32[4,256,512]{2,1,0:T(8,128)S(1)}, bf16[4,320,512]{2,1,0:T(8,128)(2,1)S(1)}) custom-call(s32[4]{0:T(128)S(1)} %pad_add_fusion.1.place_ref, bf16[128,1536]{1,0:T(8,128)(2,1)} %dynamic-slice_bitcast_fusion.2.refs_0_, bf16[128,1536]{1,0:T(8,128)(2,1)} %collective-permute-done.refs_1_, ...), custom_call_target="tpu_custom_call" | custom-call | flops 19327352832 | bytes 8053063 | tf_op jit(solution)/shard_map/pallas_call | solution.py:175
  103.7 4.9 %shard_map.65 = (f32[4,128,128]{2,1,0:T(8,128)S(1)}, f32[4,256,256]{2,1,0:T(8,128)S(1)}, bf16[4,320,256]{2,1,0:T(8,128)(2,1)S(1)}) custom-call(s32[4]{0:T(128)S(1)} %pad_add_fusion.1.place_ref, bf16[128,1536]{1,0:T(8,128)(2,1)} %dynamic-slice_bitcast_fusion.2.refs_0_, bf16[128,1536]{1,0:T(8,128)(2,1)} %collective-permute-done.refs_1_, ...), custom_call_target="tpu_custom_call" | custom-call | flops 9663676416 | bytes 4026531 | tf_op jit(solution)/shard_map/pallas_call | solution.py:175
  109.7 3.8 %shard_map.66 = (bf16[2,128,256]{2,1,0:T(8,128)(2,1)S(1)}, bf16[2,128,256]{2,1,0:T(8,128)(2,1)S(1)}) custom-call(s32[4]{0:T(128)S(1)} %pad_add_fusion.1.place_ref, s32[16]{0:T(128)S(1)} %reshape.24.members_ref, s32[4]{0:T(128)S(1)} %slice_reduce_fusion.1.counts_ref, f32[4,128,256]{2,1,0:T(8,128)S(1)} %get-tuple-element.44.q_ref, ...), custom_call_target="tpu_custom_call" | custom-call | flops 268435456 | bytes 2097152 | tf_op jit(solution)/shard_map/pallas_call | solution.py:115
  113.5 2.2 %shard_map.67 = (bf16[2,128,384]{2,1,0:T(8,128)(2,1)S(1)}, bf16[2,128,384]{2,1,0:T(8,128)(2,1)S(1)}) custom-call(s32[4]{0:T(128)S(1)} %pad_add_fusion.1.place_ref, s32[16]{0:T(128)S(1)} %reshape.24.members_ref, s32[4]{0:T(128)S(1)} %slice_reduce_fusion.1.counts_ref, f32[4,128,128]{2,1,0:T(8,128)S(1)} %get-tuple-element.41.q_ref, ...), custom_call_target="tpu_custom_call" | custom-call | flops 134217728 | bytes 1048576 | tf_op jit(solution)/shard_map/pallas_call | solution.py:115
  115.7 3.1 %collective-permute-start.18 = (bf16[2,128,384]{2,1,0:T(8,128)(2,1)S(1)}, bf16[2,128,384]{2,1,0:T(8,128)(2,1)S(1)}, u32[]{:S(2)}, u32[]{:S(2)}) collective-permute-start(bf16[2,128,384]{2,1,0:T(8,128)(2,1)S(1)} %get-tuple-element.49), channel_id=1, source_target_pairs={{0,4},{4,0},{8,12},{12,8},{1,5},{5,1},{9,13},{13,9},{2,6},{6,2},{1... | collective-permute-start | bytes 589832 | tf_op jit(solution)/shard_map/ppermute | solution.py:107
  118.8 0.8 collective-permute-start.19
  119.6 1.6 %collective-permute-start.20 = (bf16[2,128,384]{2,1,0:T(8,128)(2,1)S(1)}, bf16[2,128,384]{2,1,0:T(8,128)(2,1)S(1)}, u32[]{:S(2)}, u32[]{:S(2)}) collective-permute-start(bf16[2,128,384]{2,1,0:T(8,128)(2,1)S(1)} %get-tuple-element.49), channel_id=1, source_target_pairs={{0,12},{4,8},{8,4},{12,0},{1,13},{5,9},{9,5},{13,1},{2,14},{6,10},... | collective-permute-start | bytes 589832 | tf_op jit(solution)/shard_map/ppermute | solution.py:107
  121.2 6.2 %collective-permute-done.18.refs_1_ = bf16[2,128,384]{2,1,0:T(8,128)(2,1)S(1)} collective-permute-done((bf16[2,128,384]{2,1,0:T(8,128)(2,1)S(1)}, bf16[2,128,384]{2,1,0:T(8,128)(2,1)S(1)}, u32[]{:S(2)}, u32[]{:S(2)}) %collective-permute-start.18) | collective-permute-done | bytes 196640 | tf_op jit(solution)/shard_map/ppermute | solution.py:107
  127.4 8.5 %collective-permute-done.19.refs_2_ = bf16[2,128,384]{2,1,0:T(8,128)(2,1)S(1)} collective-permute-done((bf16[2,128,384]{2,1,0:T(8,128)(2,1)S(1)}, bf16[2,128,384]{2,1,0:T(8,128)(2,1)S(1)}, u32[]{:S(2)}, u32[]{:S(2)}) %collective-permute-start.19) | collective-permute-done | bytes 196640 | tf_op jit(solution)/shard_map/ppermute | solution.py:107
  135.9 3.2 %shard_map.69 = (f32[2,64,768]{2,1,0:T(8,128)S(1)}, bf16[2,64,768]{2,1,0:T(8,128)(2,1)S(1)}) custom-call(s32[4]{0:T(128)S(1)} %pad_add_fusion.1.place_ref, bf16[2,128,384]{2,1,0:T(8,128)(2,1)S(1)} %get-tuple-element.48.refs_0_, bf16[2,128,384]{2,1,0:T(8,128)(2,1)S(1)} %collective-permute-done.18.refs_1_, ...), custom_call_target="tpu_custom_call" | custom-call | flops 603979776 | bytes 4718592 | tf_op jit(solution)/shard_map/pallas_call | solution.py:115
  139.1 0.6 collective-permute-start.23
  139.7 3.2 %shard_map.68 = (f32[2,64,768]{2,1,0:T(8,128)S(1)}, bf16[2,64,768]{2,1,0:T(8,128)(2,1)S(1)}) custom-call(s32[4]{0:T(128)S(1)} %pad_add_fusion.1.place_ref, bf16[2,128,384]{2,1,0:T(8,128)(2,1)S(1)} %get-tuple-element.48.refs_0_, bf16[2,128,384]{2,1,0:T(8,128)(2,1)S(1)} %collective-permute-done.18.refs_1_, ...), custom_call_target="tpu_custom_call" | custom-call | flops 603979776 | bytes 4718592 | tf_op jit(solution)/shard_map/pallas_call | solution.py:115
  143.0 1.9 %collective-permute-done.23 = bf16[2,64,768]{2,1,0:T(8,128)(2,1)S(1)} collective-permute-done((bf16[2,64,768]{2,1,0:T(8,128)(2,1)S(1)}, bf16[2,64,768]{2,1,0:T(8,128)(2,1)S(1)}, u32[]{:S(2)}, u32[]{:S(2)}) %collective-permute-start.23) | collective-permute-done | bytes 196640 | tf_op jit(solution)/shard_map/ppermute | solution.py:107
  144.9 4.6 %collective-permute-start.25 = (bf16[2,64,768]{2,1,0:T(8,128)(2,1)S(1)}, bf16[2,64,768]{2,1,0:T(8,128)(2,1)S(1)}, u32[]{:S(2)}, u32[]{:S(2)}) collective-permute-start(bf16[2,64,768]{2,1,0:T(8,128)(2,1)S(1)} %add_convert_fusion), channel_id=1, source_target_pairs={{0,8},{4,12},{8,0},{12,4},{1,9},{5,13},{9,1},{13,5},{2,10},{6,14},... | collective-permute-start | bytes 589832 | tf_op jit(solution)/shard_map/ppermute | solution.py:107
  150.0 6.8 %collective-permute-done.25.far_ref = bf16[2,64,768]{2,1,0:T(8,128)(2,1)S(1)} collective-permute-done((bf16[2,64,768]{2,1,0:T(8,128)(2,1)S(1)}, bf16[2,64,768]{2,1,0:T(8,128)(2,1)S(1)}, u32[]{:S(2)}, u32[]{:S(2)}) %collective-permute-start.25) | collective-permute-done | bytes 196640 | tf_op jit(solution)/shard_map/ppermute | solution.py:107
  156.9 1.3 shard_map.70
  (63 shorter events, 4.5 us)
Async XLA Ops:
  0.0 6.4 %copy-start = (bf16[768,3,768]{2,0,1:T(8,128)(2,1)S(1)}, bf16[768,3,768]{2,0,1:T(8,128)(2,1)}, u32[]{:S(2)}) copy-start(bf16[768,3,768]{2,0,1:T(8,128)(2,1)} %param.7) | copy-start | bytes 10616836
  1.9 15.4 %collective-permute-start = (bf16[128,1536]{1,0:T(8,128)(2,1)}, bf16[128,1536]{1,0:T(8,128)(2,1)}, u32[]{:S(2)}, u32[]{:S(2)}) collective-permute-start(bf16[128,1536]{1,0:T(8,128)(2,1)} %dynamic-slice_bitcast_fusion.2.refs_0_), channel_id=1, source_target_pairs={{0,4},{4,0},{8,12},{12,8},{1,5},{5,1},{9,13},{13,9},{2,6},{6,2},{1... | collective-permute-start | bytes 1179656 | tf_op jit(solution)/shard_map/ppermute | solution.py:107
  4.9 18.8 %collective-permute-start.3 = (bf16[128,1536]{1,0:T(8,128)(2,1)}, bf16[128,1536]{1,0:T(8,128)(2,1)}, u32[]{:S(2)}, u32[]{:S(2)}) collective-permute-start(bf16[128,1536]{1,0:T(8,128)(2,1)} %dynamic-slice_bitcast_fusion.2.refs_0_), channel_id=1, source_target_pairs={{0,2},{2,0},{1,3},{3,1},{4,6},{6,4},{5,7},{7,5},{8,10},{10,8},{9,1... | collective-permute-start | bytes 1179656 | tf_op jit(solution)/shard_map/ppermute | solution.py:107
  6.4 9.2 %copy-start.1 = (bf16[768,768]{1,0:T(8,128)(2,1)S(1)}, bf16[768,768]{1,0:T(8,128)(2,1)}, u32[]{:S(2)}) copy-start(bf16[768,768]{1,0:T(8,128)(2,1)} %refs_4_.3) | copy-start | bytes 3538948
  6.4 10.1 %copy-start.10 = (s32[2]{0:T(128)S(1)}, s32[2]{0:T(128)}, u32[]{:S(2)}) copy-start(s32[2]{0:T(128)} %param.11) | copy-start | bytes 28
  6.4 10.9 %copy-start.9 = (s32[2,4]{1,0:T(2,128)S(1)}, s32[2,4]{1,0:T(2,128)}, u32[]{:S(2)}) copy-start(s32[2,4]{1,0:T(2,128)} %param.9) | copy-start | bytes 100
  7.5 16.3 %collective-permute-start.2 = (bf16[3,384,384]{2,1,0:T(8,128)(2,1)}, bf16[3,384,384]{2,1,0:T(8,128)(2,1)}, u32[]{:S(2)}, u32[]{:S(2)}) collective-permute-start(bf16[3,384,384]{2,1,0:T(8,128)(2,1)} %dynamic-slice_bitcast_fusion), channel_id=1, source_target_pairs={{0,0},{1,8},{4,4},{5,12},{8,1},{9,9},{12,5},{13,13},{2,2},{3,10},{... | collective-permute-start | bytes 2654216 | tf_op jit(solution)/shard_map/ppermute | solution.py:341
  17.4 33.2 %collective-permute-start.5 = (bf16[768,768]{1,0:T(8,128)(2,1)}, bf16[768,768]{1,0:T(8,128)(2,1)}, u32[]{:S(2)}, u32[]{:S(2)}) collective-permute-start(bf16[768,768]{1,0:T(8,128)(2,1)} %refs_4_.3), channel_id=1, source_target_pairs={{0,1},{1,0},{2,3},{3,2},{4,5},{5,4},{6,7},{7,6},{8,9},{9,8},{10,11... | collective-permute-start | bytes 3538952 | tf_op jit(solution)/shard_map/ppermute | solution.py:107
  19.5 29.5 %collective-permute-start.1 = (bf16[392,768]{1,0:T(8,128)(2,1)}, bf16[392,768]{1,0:T(8,128)(2,1)}, u32[]{:S(2)}, u32[]{:S(2)}) collective-permute-start(bf16[392,768]{1,0:T(8,128)(2,1)} %pad_maximum_fusion), channel_id=1, source_target_pairs={{0,4},{4,0},{8,12},{12,8},{1,5},{5,1},{9,13},{13,9},{2,6},{6,2},{1... | collective-permute-start | bytes 1806344 | tf_op jit(solution)/shard_map/ppermute | solution.py:107
  20.7 13.3 %collective-permute-start.6 = (bf16[128,1536]{1,0:T(8,128)(2,1)}, bf16[128,1536]{1,0:T(8,128)(2,1)S(1)}, u32[]{:S(2)}, u32[]{:S(2)}) collective-permute-start(bf16[128,1536]{1,0:T(8,128)(2,1)} %collective-permute-done.refs_1_), channel_id=1, source_target_pairs={{0,2},{2,0},{1,3},{3,1},{4,6},{6,4},{5,7},{7,5},{8,10},{10,8},{9,1... | collective-permute-start | bytes 1179656 | tf_op jit(solution)/shard_map/ppermute | solution.py:107
  23.8 26.7 %collective-permute-start.4 = (bf16[136,1536]{1,0:T(8,128)(2,1)S(1)}, bf16[136,1536]{1,0:T(8,128)(2,1)}, u32[]{:S(2)}, u32[]{:S(2)}) collective-permute-start(bf16[136,1536]{1,0:T(8,128)(2,1)S(1)} %pad_maximum_fusion.1), channel_id=1, source_target_pairs={{0,8},{4,12},{8,0},{12,4},{1,9},{5,13},{9,1},{13,5},{2,10},{6,14},... | collective-permute-start | bytes 1253384 | tf_op jit(solution)/shard_map/ppermute | solution.py:107
  32.4 37.7 %collective-permute-start.10 = (bf16[3,384,384]{2,1,0:T(8,128)(2,1)}, bf16[3,384,384]{2,1,0:T(8,128)(2,1)S(1)}, u32[]{:S(2)}, u32[]{:S(2)}) collective-permute-start(bf16[3,384,384]{2,1,0:T(8,128)(2,1)} %collective-permute-done.2.refs_8_), channel_id=1, source_target_pairs={{0,16},{16,0},{1,17},{17,1},{2,18},{18,2},{3,19},{19,3},{4,20},{20... | collective-permute-start | bytes 2654216 | tf_op jit(solution)/shard_map/ppermute | solution.py:107
  34.1 0.8 copy-start.6
  34.8 35.3 %collective-permute-start.13 = (bf16[3,384,256]{2,1,0:T(8,128)(2,1)S(1)}, bf16[3,384,256]{2,1,0:T(8,128)(2,1)}, u32[]{:S(2)}, u32[]{:S(2)}) collective-permute-start(bf16[3,384,256]{2,1,0:T(8,128)(2,1)S(1)} %dynamic-slice_bitcast_fusion.1), channel_id=1, source_target_pairs={{0,4},{1,12},{4,0},{5,8},{8,5},{9,13},{12,1},{13,9},{2,6},{3,14},{... | collective-permute-start | bytes 1769480 | tf_op jit(solution)/shard_map/ppermute | solution.py:341
  49.0 21.2 %collective-permute-start.14 = (bf16[392,768]{1,0:T(8,128)(2,1)}, bf16[392,768]{1,0:T(8,128)(2,1)}, u32[]{:S(2)}, u32[]{:S(2)}) collective-permute-start(bf16[392,768]{1,0:T(8,128)(2,1)} %collective-permute-done.1.refs_6_), channel_id=1, source_target_pairs={{0,16},{16,0},{1,17},{17,1},{2,18},{18,2},{3,19},{19,3},{4,20},{20... | collective-permute-start | bytes 1806344 | tf_op jit(solution)/shard_map/ppermute | solution.py:107
  50.5 23.6 %collective-permute-start.7 = (bf16[136,1536]{1,0:T(8,128)(2,1)S(1)}, bf16[136,1536]{1,0:T(8,128)(2,1)}, u32[]{:S(2)}, u32[]{:S(2)}) collective-permute-start(bf16[136,1536]{1,0:T(8,128)(2,1)S(1)} %pad_maximum_fusion.1), channel_id=1, source_target_pairs={{0,12},{4,8},{8,4},{12,0},{1,13},{5,9},{9,5},{13,1},{2,14},{6,10},... | collective-permute-start | bytes 1253384 | tf_op jit(solution)/shard_map/ppermute | solution.py:107
  68.6 24.2 %collective-permute-start.8 = (bf16[136,1536]{1,0:T(8,128)(2,1)}, bf16[136,1536]{1,0:T(8,128)(2,1)}, u32[]{:S(2)}, u32[]{:S(2)}) collective-permute-start(bf16[136,1536]{1,0:T(8,128)(2,1)} %collective-permute-done.4.refs_2_), channel_id=1, source_target_pairs={{0,2},{2,0},{1,3},{3,1},{4,6},{6,4},{5,7},{7,5},{8,10},{10,8},{9,1... | collective-permute-start | bytes 1253384 | tf_op jit(solution)/shard_map/ppermute | solution.py:107
  70.1 0.9 copy-start.3
  71.1 21.7 %collective-permute-start.15 = (bf16[3,384,256]{2,1,0:T(8,128)(2,1)}, bf16[3,384,256]{2,1,0:T(8,128)(2,1)}, u32[]{:S(2)}, u32[]{:S(2)}) collective-permute-start(bf16[3,384,256]{2,1,0:T(8,128)(2,1)} %collective-permute-done.13.refs_10_), channel_id=1, source_target_pairs={{0,16},{16,0},{1,17},{17,1},{2,18},{18,2},{3,19},{19,3},{4,20},{20... | collective-permute-start | bytes 1769480 | tf_op jit(solution)/shard_map/ppermute | solution.py:107
  74.1 17.1 %collective-permute-start.11 = (bf16[3,384,128]{2,1,0:T(8,128)(2,1)}, bf16[3,384,128]{2,1,0:T(8,128)(2,1)}, u32[]{:S(2)}, u32[]{:S(2)}) collective-permute-start(bf16[3,384,128]{2,1,0:T(8,128)(2,1)} %dynamic-slice_bitcast_fusion.3), channel_id=1, source_target_pairs={{0,4},{1,12},{4,0},{5,8},{8,5},{9,13},{12,1},{13,9},{2,6},{3,14},{... | collective-permute-start | bytes 884744 | tf_op jit(solution)/shard_map/ppermute | solution.py:341
  86.3 8.4 %collective-permute-start.9 = (bf16[136,1536]{1,0:T(8,128)(2,1)}, bf16[136,1536]{1,0:T(8,128)(2,1)}, u32[]{:S(2)}, u32[]{:S(2)}) collective-permute-start(bf16[136,1536]{1,0:T(8,128)(2,1)} %collective-permute-done.7.refs_3_), channel_id=1, source_target_pairs={{0,2},{2,0},{1,3},{3,1},{4,6},{6,4},{5,7},{7,5},{8,10},{10,8},{9,1... | collective-permute-start | bytes 1253384 | tf_op jit(solution)/shard_map/ppermute | solution.py:107
  91.3 12.4 %collective-permute-start.12 = (bf16[3,384,128]{2,1,0:T(8,128)(2,1)}, bf16[3,384,128]{2,1,0:T(8,128)(2,1)S(1)}, u32[]{:S(2)}, u32[]{:S(2)}) collective-permute-start(bf16[3,384,128]{2,1,0:T(8,128)(2,1)} %collective-permute-done.11.refs_10_), channel_id=1, source_target_pairs={{0,16},{16,0},{1,17},{17,1},{2,18},{18,2},{3,19},{19,3},{4,20},{20... | collective-permute-start | bytes 884744 | tf_op jit(solution)/shard_map/ppermute | solution.py:107
  94.6 1.2 copy-start.4
  95.8 1.0 copy-start.7
  96.8 6.9 %copy-start.5 = (bf16[3,384,384]{2,1,0:T(8,128)(2,1)S(1)}, bf16[3,384,384]{2,1,0:T(8,128)(2,1)}, u32[]{:S(2)}) copy-start(bf16[3,384,384]{2,1,0:T(8,128)(2,1)} %copy-done.3) | copy-start | bytes 2654212
  96.8 6.9 %copy-start.8 = (bf16[128,1536]{1,0:T(8,128)(2,1)S(1)}, bf16[128,1536]{1,0:T(8,128)(2,1)}, u32[]{:S(2)}) copy-start(bf16[128,1536]{1,0:T(8,128)(2,1)} %copy-done.6) | copy-start | bytes 1179652
  103.6 6.1 %collective-permute-start.17 = (bf16[4,320,512]{2,1,0:T(8,128)(2,1)S(1)}, bf16[4,320,512]{2,1,0:T(8,128)(2,1)S(1)}, u32[]{:S(2)}, u32[]{:S(2)}) collective-permute-start(bf16[4,320,512]{2,1,0:T(8,128)(2,1)S(1)} %get-tuple-element.39), channel_id=1, source_target_pairs={{0,1},{1,0},{2,3},{3,2},{4,5},{5,4},{6,7},{7,6},{8,9},{9,8},{10,11... | collective-permute-start | bytes 3932168 | tf_op jit(solution)/shard_map/ppermute | solution.py:107
  108.6 4.9 %collective-permute-start.16 = (bf16[4,320,256]{2,1,0:T(8,128)(2,1)S(1)}, bf16[4,320,256]{2,1,0:T(8,128)(2,1)S(1)}, u32[]{:S(2)}, u32[]{:S(2)}) collective-permute-start(bf16[4,320,256]{2,1,0:T(8,128)(2,1)S(1)} %get-tuple-element.43), channel_id=1, source_target_pairs={{0,1},{1,0},{2,3},{3,2},{4,5},{5,4},{6,7},{7,6},{8,9},{9,8},{10,11... | collective-permute-start | bytes 1966088 | tf_op jit(solution)/shard_map/ppermute | solution.py:107
  109.1 12.1 %collective-permute-start.21 = (bf16[392,768]{1,0:T(8,128)(2,1)}, bf16[392,768]{1,0:T(8,128)(2,1)S(1)}, u32[]{:S(2)}, u32[]{:S(2)}) collective-permute-start(bf16[392,768]{1,0:T(8,128)(2,1)} %collective-permute-done.1.refs_6_), channel_id=1, source_target_pairs={{0,1},{1,0},{2,3},{3,2},{4,5},{5,4},{6,7},{7,6},{8,9},{9,8},{10,11... | collective-permute-start | bytes 1806344 | tf_op jit(solution)/shard_map/ppermute | solution.py:107
  109.2 12.0 %collective-permute-start.22 = (bf16[392,768]{1,0:T(8,128)(2,1)}, bf16[392,768]{1,0:T(8,128)(2,1)S(1)}, u32[]{:S(2)}, u32[]{:S(2)}) collective-permute-start(bf16[392,768]{1,0:T(8,128)(2,1)} %collective-permute-done.14.refs_7_), channel_id=1, source_target_pairs={{0,1},{1,0},{2,3},{3,2},{4,5},{5,4},{6,7},{7,6},{8,9},{9,8},{10,11... | collective-permute-start | bytes 1806344 | tf_op jit(solution)/shard_map/ppermute | solution.py:107
  113.4 22.5 %copy-start.2 = (bf16[768,768]{1,0:T(8,128)(2,1)S(1)}, bf16[768,768]{1,0:T(8,128)(2,1)}, u32[]{:S(2)}) copy-start(bf16[768,768]{1,0:T(8,128)(2,1)} %refs_4_.3) | copy-start | bytes 3538948
  115.7 11.7 %collective-permute-start.18 = (bf16[2,128,384]{2,1,0:T(8,128)(2,1)S(1)}, bf16[2,128,384]{2,1,0:T(8,128)(2,1)S(1)}, u32[]{:S(2)}, u32[]{:S(2)}) collective-permute-start(bf16[2,128,384]{2,1,0:T(8,128)(2,1)S(1)} %get-tuple-element.49), channel_id=1, source_target_pairs={{0,4},{4,0},{8,12},{12,8},{1,5},{5,1},{9,13},{13,9},{2,6},{6,2},{1... | collective-permute-start | bytes 589832 | tf_op jit(solution)/shard_map/ppermute | solution.py:107
  118.8 17.1 %collective-permute-start.19 = (bf16[2,128,384]{2,1,0:T(8,128)(2,1)S(1)}, bf16[2,128,384]{2,1,0:T(8,128)(2,1)S(1)}, u32[]{:S(2)}, u32[]{:S(2)}) collective-permute-start(bf16[2,128,384]{2,1,0:T(8,128)(2,1)S(1)} %get-tuple-element.48.refs_0_), channel_id=1, source_target_pairs={{0,8},{4,12},{8,0},{12,4},{1,9},{5,13},{9,1},{13,5},{2,10},{6,14},... | collective-permute-start | bytes 589832 | tf_op jit(solution)/shard_map/ppermute | solution.py:107
  119.6 16.3 %collective-permute-start.20 = (bf16[2,128,384]{2,1,0:T(8,128)(2,1)S(1)}, bf16[2,128,384]{2,1,0:T(8,128)(2,1)S(1)}, u32[]{:S(2)}, u32[]{:S(2)}) collective-permute-start(bf16[2,128,384]{2,1,0:T(8,128)(2,1)S(1)} %get-tuple-element.49), channel_id=1, source_target_pairs={{0,12},{4,8},{8,4},{12,0},{1,13},{5,9},{9,5},{13,1},{2,14},{6,10},... | collective-permute-start | bytes 589832 | tf_op jit(solution)/shard_map/ppermute | solution.py:107
  139.1 5.7 %collective-permute-start.23 = (bf16[2,64,768]{2,1,0:T(8,128)(2,1)S(1)}, bf16[2,64,768]{2,1,0:T(8,128)(2,1)S(1)}, u32[]{:S(2)}, u32[]{:S(2)}) collective-permute-start(bf16[2,64,768]{2,1,0:T(8,128)(2,1)S(1)} %get-tuple-element.52), channel_id=1, source_target_pairs={{0,2},{2,0},{1,3},{3,1},{4,6},{6,4},{5,7},{7,5},{8,10},{10,8},{9,1... | collective-permute-start | bytes 589832 | tf_op jit(solution)/shard_map/ppermute | solution.py:107
  144.9 11.9 %collective-permute-start.25 = (bf16[2,64,768]{2,1,0:T(8,128)(2,1)S(1)}, bf16[2,64,768]{2,1,0:T(8,128)(2,1)S(1)}, u32[]{:S(2)}, u32[]{:S(2)}) collective-permute-start(bf16[2,64,768]{2,1,0:T(8,128)(2,1)S(1)} %add_convert_fusion), channel_id=1, source_target_pairs={{0,8},{4,12},{8,0},{12,4},{1,9},{5,13},{9,1},{13,5},{2,10},{6,14},... | collective-permute-start | bytes 589832 | tf_op jit(solution)/shard_map/ppermute | solution.py:107
  149.5 7.4 %collective-permute-start.24 = (bf16[2,64,768]{2,1,0:T(8,128)(2,1)S(1)}, bf16[2,64,768]{2,1,0:T(8,128)(2,1)S(1)}, u32[]{:S(2)}, u32[]{:S(2)}) collective-permute-start(bf16[2,64,768]{2,1,0:T(8,128)(2,1)S(1)} %get-tuple-element.53), channel_id=1, source_target_pairs={{0,2},{2,0},{1,3},{3,1},{4,6},{6,4},{5,7},{7,5},{8,10},{10,8},{9,1... | collective-permute-start | bytes 589832 | tf_op jit(solution)/shard_map/ppermute | solution.py:107

commit v28 on v27

--- a/solution.py
+++ b/solution.py
@@ -361,7 +361,7 @@
     far_2x = swap(far_2, "frames")
     far_3 = swap(after(joined, far_2, across, near_x, beside[0]), "rows", 3)
     far_3x = swap(far_3, "frames")
-    here.append(reshard(1, cols - last, last, far_3))
+    here.append(reshard(1, cols - last, last, far_3, there[1]))
     there.append(swap(here[2], "groups"))
 
     found = [tables, beside[0][cols:], far_2[count:], far_3[count:]]

time: 159 us -> 157 us (0.987)
  waiting for transfers between devices: 39.5 us -> 68.2 us
  starting transfers between devices: 76.5 us -> 50.1 us
  local copies, waits for them, and re-layouts: 13.1 us -> 8.78 us
    ppermute x23, waiting for transfers between devices: 37.7 us -> 64.5 us  [swap(): return lax.ppermute(value, axis, [(i, i ^ step) for i in range(peers)])]
    ppermute x23, starting transfers between devices: 52.9 us -> 34.7 us  [swap(): return lax.ppermute(value, axis, [(i, i ^ step) for i in range(peers)])]
    ppermute x3, starting transfers between devices: 23.6 us -> 15.4 us  [reshard(): lax.ppermute(after(value, *others) if others else value, ('rows', 'heads'...]
    unnamed x22 -> x8, local copies, waits for them, and re-layouts: 3.88 us -> 0.02 us
    ppermute x3, waiting for transfers between devices: 1.89 us -> 3.73 us  [reshard(): lax.ppermute(after(value, *others) if others else value, ('rows', 'heads'...]
  transfers between devices with their start and end apart: 26 -> 26, of which waited for: 8 -> 11; matrix products, arithmetic and copies ran while one was open for 7% -> 6% of each run, Pallas kernels for 13% -> 14%
where the time goes in v28:
time: 157 us; the launch traced here: 156 us
  waiting for transfers between devices  68.2 us (43%)
  starting transfers between devices  50.1 us (32%)
  Pallas kernels  26.3 us (17%)
  local copies, waits for them, and re-layouts  8.78 us (6%)
  other arithmetic  2.41 us (2%)
    ppermute x23, waiting for transfers between devices, swap(): return lax.ppermute(value, axis, [(i, i ^ step) for i in range(peers)])  64.5 us
    ppermute x23, starting transfers between devices, swap(): return lax.ppermute(value, axis, [(i, i ^ step) for i in range(peers)])  34.7 us
    ppermute x3, starting transfers between devices, reshard(): lax.ppermute(after(value, *others) if others else value, ('rows', 'heads'...  15.4 us
    pallas_call x5, Pallas kernels, call(): pl.pallas_call(kernel, out_shape=out_shape, grid_spec=pltpu.PrefetchScala...  14.4 us
    pallas_call x2, Pallas kernels, project(): pl.pallas_call(kernel, out_shape=(jax.ShapeDtypeStruct((rows, 2 * BS, col...  11.9 us
    ppermute x3, waiting for transfers between devices, reshard(): lax.ppermute(after(value, *others) if others else value, ('rows', 'heads'...  3.73 us
  transfers between devices with their start and end apart: 26, of which 11 were waited for; matrix products, arithmetic and copies ran while one was open for 6% of the time, Pallas kernels for 14%

profile of v28, /device:TPU:0, one launch (start us, length us, event | category | flops | bytes accessed | tf_op | source)
XLA Modules:
  0.0 156.0 jit_solution(6158119287684719875)
XLA Ops:
  0.0 1.9 %dynamic-slice_bitcast_fusion.2.refs_0_ = bf16[128,1536]{1,0:T(8,128)(2,1)} fusion(bf16[1,128,3072]{2,1,0:T(8,128)(2,1)} %param.6, s32[]{:T(128)S(6)} %select_n.49), kind=kLoop, calls=%fused_computation.7 | loop fusion | bytes 786436 | tf_op jit(solution)/shard_map/dynamic_slice | solution.py:343
  1.9 3.0 %collective-permute-start = (bf16[128,1536]{1,0:T(8,128)(2,1)}, bf16[128,1536]{1,0:T(8,128)(2,1)}, u32[]{:S(2)}, u32[]{:S(2)}) collective-permute-start(bf16[128,1536]{1,0:T(8,128)(2,1)} %dynamic-slice_bitcast_fusion.2.refs_0_), channel_id=1, source_target_pairs={{0,4},{4,0},{8,12},{12,8},{1,5},{5,1},{9,13},{13,9},{2,6},{6,2},{1... | collective-permute-start | bytes 1179656 | tf_op jit(solution)/shard_map/ppermute | solution.py:107
  5.0 1.0 dynamic-slice_bitcast_fusion
  6.0 8.2 %collective-permute-start.2 = (bf16[3,384,384]{2,1,0:T(8,128)(2,1)}, bf16[3,384,384]{2,1,0:T(8,128)(2,1)}, u32[]{:S(2)}, u32[]{:S(2)}) collective-permute-start(bf16[3,384,384]{2,1,0:T(8,128)(2,1)} %dynamic-slice_bitcast_fusion), channel_id=1, source_target_pairs={{0,0},{1,8},{4,4},{5,12},{8,1},{9,9},{12,5},{13,13},{2,2},{3,10},{... | collective-permute-start | bytes 2654216 | tf_op jit(solution)/shard_map/ppermute | solution.py:341
  14.5 1.1 constant_dynamic-slice_fusion
  15.6 3.1 %collective-permute-done.refs_1_ = bf16[128,1536]{1,0:T(8,128)(2,1)} collective-permute-done((bf16[128,1536]{1,0:T(8,128)(2,1)}, bf16[128,1536]{1,0:T(8,128)(2,1)}, u32[]{:S(2)}, u32[]{:S(2)}) %collective-permute-start) | collective-permute-done | bytes 393248 | tf_op jit(solution)/shard_map/ppermute | solution.py:107
  18.7 0.9 pad_maximum_fusion
  19.6 1.7 %collective-permute-start.3 = (bf16[128,1536]{1,0:T(8,128)(2,1)}, bf16[128,1536]{1,0:T(8,128)(2,1)}, u32[]{:S(2)}, u32[]{:S(2)}) collective-permute-start(bf16[128,1536]{1,0:T(8,128)(2,1)} %dynamic-slice_bitcast_fusion.2.refs_0_), channel_id=1, source_target_pairs={{0,2},{2,0},{1,3},{3,1},{4,6},{6,4},{5,7},{7,5},{8,10},{10,8},{9,1... | collective-permute-start | bytes 1179656 | tf_op jit(solution)/shard_map/ppermute | solution.py:107
  21.8 1.7 %collective-permute-start.10 = (bf16[3,384,384]{2,1,0:T(8,128)(2,1)}, bf16[3,384,384]{2,1,0:T(8,128)(2,1)}, u32[]{:S(2)}, u32[]{:S(2)}) collective-permute-start(bf16[3,384,384]{2,1,0:T(8,128)(2,1)} %collective-permute-done.2.refs_8_), channel_id=1, source_target_pairs={{0,16},{16,0},{1,17},{17,1},{2,18},{18,2},{3,19},{19,3},{4,20},{20... | collective-permute-start | bytes 2654216 | tf_op jit(solution)/shard_map/ppermute | solution.py:107
  23.6 8.3 %collective-permute-done.3.refs_4_ = bf16[128,1536]{1,0:T(8,128)(2,1)} collective-permute-done((bf16[128,1536]{1,0:T(8,128)(2,1)}, bf16[128,1536]{1,0:T(8,128)(2,1)}, u32[]{:S(2)}, u32[]{:S(2)}) %collective-permute-start.3) | collective-permute-done | bytes 393248 | tf_op jit(solution)/shard_map/ppermute | solution.py:107
  31.8 2.0 %collective-permute-start.11 = (bf16[3,384,256]{2,1,0:T(8,128)(2,1)S(1)}, bf16[3,384,256]{2,1,0:T(8,128)(2,1)}, u32[]{:S(2)}, u32[]{:S(2)}) collective-permute-start(bf16[3,384,256]{2,1,0:T(8,128)(2,1)S(1)} %dynamic-slice_bitcast_fusion.1), channel_id=1, source_target_pairs={{0,4},{1,12},{4,0},{5,8},{8,5},{9,13},{12,1},{13,9},{2,6},{3,14},{... | collective-permute-start | bytes 1769480 | tf_op jit(solution)/shard_map/ppermute | solution.py:341
  33.9 6.0 %collective-permute-done.1.refs_6_ = bf16[392,768]{1,0:T(8,128)(2,1)} collective-permute-done((bf16[392,768]{1,0:T(8,128)(2,1)}, bf16[392,768]{1,0:T(8,128)(2,1)}, u32[]{:S(2)}, u32[]{:S(2)}) %collective-permute-start.1) | collective-permute-done | bytes 602144 | tf_op jit(solution)/shard_map/ppermute | solution.py:107
  39.8 1.4 collective-permute-start.12
  41.2 1.0 pad_maximum_fusion.1
  42.2 6.8 %collective-permute-start.4 = (bf16[136,1536]{1,0:T(8,128)(2,1)S(1)}, bf16[136,1536]{1,0:T(8,128)(2,1)}, u32[]{:S(2)}, u32[]{:S(2)}) collective-permute-start(bf16[136,1536]{1,0:T(8,128)(2,1)S(1)} %pad_maximum_fusion.1), channel_id=1, source_target_pairs={{0,8},{4,12},{8,0},{12,4},{1,9},{5,13},{9,1},{13,5},{2,10},{6,14},... | collective-permute-start | bytes 1253384 | tf_op jit(solution)/shard_map/ppermute | solution.py:107
  49.1 0.8 dynamic-slice_bitcast_fusion.3
  49.9 17.6 %collective-permute-done.4.refs_2_ = bf16[136,1536]{1,0:T(8,128)(2,1)} collective-permute-done((bf16[136,1536]{1,0:T(8,128)(2,1)S(1)}, bf16[136,1536]{1,0:T(8,128)(2,1)}, u32[]{:S(2)}, u32[]{:S(2)}) %collective-permute-start.4) | collective-permute-done | bytes 417824 | tf_op jit(solution)/shard_map/ppermute | solution.py:107
  67.5 2.9 %collective-permute-start.7 = (bf16[136,1536]{1,0:T(8,128)(2,1)S(1)}, bf16[136,1536]{1,0:T(8,128)(2,1)}, u32[]{:S(2)}, u32[]{:S(2)}) collective-permute-start(bf16[136,1536]{1,0:T(8,128)(2,1)S(1)} %pad_maximum_fusion.1), channel_id=1, source_target_pairs={{0,12},{4,8},{8,4},{12,0},{1,13},{5,9},{9,5},{13,1},{2,14},{6,10},... | collective-permute-start | bytes 1253384 | tf_op jit(solution)/shard_map/ppermute | solution.py:107
  70.4 1.6 %collective-permute-start.13 = (bf16[3,384,256]{2,1,0:T(8,128)(2,1)}, bf16[3,384,256]{2,1,0:T(8,128)(2,1)}, u32[]{:S(2)}, u32[]{:S(2)}) collective-permute-start(bf16[3,384,256]{2,1,0:T(8,128)(2,1)} %collective-permute-done.11.refs_10_), channel_id=1, source_target_pairs={{0,16},{16,0},{1,17},{17,1},{2,18},{18,2},{3,19},{19,3},{4,20},{20... | collective-permute-start | bytes 1769480 | tf_op jit(solution)/shard_map/ppermute | solution.py:107
  72.0 0.6 slice_bitcast_fusion.2
  72.6 1.5 collective-permute-start.8
  74.1 0.7 slice_bitcast_fusion.1
  74.8 4.1 %collective-permute-done.7.refs_3_ = bf16[136,1536]{1,0:T(8,128)(2,1)} collective-permute-done((bf16[136,1536]{1,0:T(8,128)(2,1)S(1)}, bf16[136,1536]{1,0:T(8,128)(2,1)}, u32[]{:S(2)}, u32[]{:S(2)}) %collective-permute-start.7) | collective-permute-done | bytes 417824 | tf_op jit(solution)/shard_map/ppermute | solution.py:107
  78.9 1.5 collective-permute-start.9
  80.4 0.7 slice_bitcast_fusion
  81.1 0.6 gather_fusion
  81.7 2.5 %collective-permute-done.13.refs_11_ = bf16[3,384,256]{2,1,0:T(8,128)(2,1)} collective-permute-done((bf16[3,384,256]{2,1,0:T(8,128)(2,1)}, bf16[3,384,256]{2,1,0:T(8,128)(2,1)}, u32[]{:S(2)}, u32[]{:S(2)}) %collective-permute-start.13) | collective-permute-done | bytes 589856 | tf_op jit(solution)/shard_map/ppermute | solution.py:107
  84.2 5.2 %collective-permute-start.14 = (bf16[3,384,128]{2,1,0:T(8,128)(2,1)}, bf16[3,384,128]{2,1,0:T(8,128)(2,1)}, u32[]{:S(2)}, u32[]{:S(2)}) collective-permute-start(bf16[3,384,128]{2,1,0:T(8,128)(2,1)} %dynamic-slice_bitcast_fusion.3), channel_id=1, source_target_pairs={{0,4},{1,12},{4,0},{5,8},{8,5},{9,13},{12,1},{13,9},{2,6},{3,14},{... | collective-permute-start | bytes 884744 | tf_op jit(solution)/shard_map/ppermute | solution.py:341
  89.9 0.6 gather_fusion.1
  90.7 3.7 %collective-permute-done.14.refs_10_ = bf16[3,384,128]{2,1,0:T(8,128)(2,1)} collective-permute-done((bf16[3,384,128]{2,1,0:T(8,128)(2,1)}, bf16[3,384,128]{2,1,0:T(8,128)(2,1)}, u32[]{:S(2)}, u32[]{:S(2)}) %collective-permute-start.14) | collective-permute-done | bytes 294944 | tf_op jit(solution)/shard_map/ppermute | solution.py:341
  94.4 1.5 collective-permute-start.15
  96.0 6.9 %shard_map.64 = (f32[4,128,256]{2,1,0:T(8,128)S(1)}, f32[4,256,512]{2,1,0:T(8,128)S(1)}, bf16[4,320,512]{2,1,0:T(8,128)(2,1)S(1)}) custom-call(s32[4]{0:T(128)S(1)} %pad_add_fusion.1.place_ref, bf16[128,1536]{1,0:T(8,128)(2,1)} %dynamic-slice_bitcast_fusion.2.refs_0_, bf16[128,1536]{1,0:T(8,128)(2,1)} %collective-permute-done.refs_1_, ...), custom_call_target="tpu_custom_call" | custom-call | flops 19327352832 | bytes 8053063 | tf_op jit(solution)/shard_map/pallas_call | solution.py:175
  103.0 5.0 %shard_map.65 = (f32[4,128,128]{2,1,0:T(8,128)S(1)}, f32[4,256,256]{2,1,0:T(8,128)S(1)}, bf16[4,320,256]{2,1,0:T(8,128)(2,1)S(1)}) custom-call(s32[4]{0:T(128)S(1)} %pad_add_fusion.1.place_ref, bf16[128,1536]{1,0:T(8,128)(2,1)} %dynamic-slice_bitcast_fusion.2.refs_0_, bf16[128,1536]{1,0:T(8,128)(2,1)} %collective-permute-done.refs_1_, ...), custom_call_target="tpu_custom_call" | custom-call | flops 9663676416 | bytes 4026531 | tf_op jit(solution)/shard_map/pallas_call | solution.py:175
  108.0 0.6 collective-permute-start.16
  109.0 3.8 %shard_map.66 = (bf16[2,128,256]{2,1,0:T(8,128)(2,1)S(1)}, bf16[2,128,256]{2,1,0:T(8,128)(2,1)S(1)}) custom-call(s32[4]{0:T(128)S(1)} %pad_add_fusion.1.place_ref, s32[16]{0:T(128)S(1)} %reshape.24.members_ref, s32[4]{0:T(128)S(1)} %slice_reduce_fusion.1.counts_ref, f32[4,128,256]{2,1,0:T(8,128)S(1)} %get-tuple-element.44.q_ref, ...), custom_call_target="tpu_custom_call" | custom-call | flops 268435456 | bytes 2097152 | tf_op jit(solution)/shard_map/pallas_call | solution.py:115
  112.8 2.2 %shard_map.67 = (bf16[2,128,384]{2,1,0:T(8,128)(2,1)S(1)}, bf16[2,128,384]{2,1,0:T(8,128)(2,1)S(1)}) custom-call(s32[4]{0:T(128)S(1)} %pad_add_fusion.1.place_ref, s32[16]{0:T(128)S(1)} %reshape.24.members_ref, s32[4]{0:T(128)S(1)} %slice_reduce_fusion.1.counts_ref, f32[4,128,128]{2,1,0:T(8,128)S(1)} %get-tuple-element.41.q_ref, ...), custom_call_target="tpu_custom_call" | custom-call | flops 134217728 | bytes 1048576 | tf_op jit(solution)/shard_map/pallas_call | solution.py:115
  115.0 2.1 %collective-permute-start.18 = (bf16[2,128,384]{2,1,0:T(8,128)(2,1)S(1)}, bf16[2,128,384]{2,1,0:T(8,128)(2,1)S(1)}, u32[]{:S(2)}, u32[]{:S(2)}) collective-permute-start(bf16[2,128,384]{2,1,0:T(8,128)(2,1)S(1)} %get-tuple-element.49), channel_id=1, source_target_pairs={{0,4},{4,0},{8,12},{12,8},{1,5},{5,1},{9,13},{13,9},{2,6},{6,2},{1... | collective-permute-start | bytes 589832 | tf_op jit(solution)/shard_map/ppermute | solution.py:107
  117.1 2.4 %collective-permute-start.20 = (bf16[2,128,384]{2,1,0:T(8,128)(2,1)S(1)}, bf16[2,128,384]{2,1,0:T(8,128)(2,1)S(1)}, u32[]{:S(2)}, u32[]{:S(2)}) collective-permute-start(bf16[2,128,384]{2,1,0:T(8,128)(2,1)S(1)} %get-tuple-element.49), channel_id=1, source_target_pairs={{0,12},{4,8},{8,4},{12,0},{1,13},{5,9},{9,5},{13,1},{2,14},{6,10},... | collective-permute-start | bytes 589832 | tf_op jit(solution)/shard_map/ppermute | solution.py:107
  119.6 5.5 %collective-permute-done.18.refs_1_ = bf16[2,128,384]{2,1,0:T(8,128)(2,1)S(1)} collective-permute-done((bf16[2,128,384]{2,1,0:T(8,128)(2,1)S(1)}, bf16[2,128,384]{2,1,0:T(8,128)(2,1)S(1)}, u32[]{:S(2)}, u32[]{:S(2)}) %collective-permute-start.18) | collective-permute-done | bytes 196640 | tf_op jit(solution)/shard_map/ppermute | solution.py:107
  125.1 9.2 %collective-permute-done.19.refs_2_ = bf16[2,128,384]{2,1,0:T(8,128)(2,1)S(1)} collective-permute-done((bf16[2,128,384]{2,1,0:T(8,128)(2,1)S(1)}, bf16[2,128,384]{2,1,0:T(8,128)(2,1)S(1)}, u32[]{:S(2)}, u32[]{:S(2)}) %collective-permute-start.19) | collective-permute-done | bytes 196640 | tf_op jit(solution)/shard_map/ppermute | solution.py:107
  134.2 3.5 %shard_map.69 = (f32[2,64,768]{2,1,0:T(8,128)S(1)}, bf16[2,64,768]{2,1,0:T(8,128)(2,1)S(1)}) custom-call(s32[4]{0:T(128)S(1)} %pad_add_fusion.1.place_ref, bf16[2,128,384]{2,1,0:T(8,128)(2,1)S(1)} %get-tuple-element.48.refs_0_, bf16[2,128,384]{2,1,0:T(8,128)(2,1)S(1)} %collective-permute-done.18.refs_1_, ...), custom_call_target="tpu_custom_call" | custom-call | flops 603979776 | bytes 4718592 | tf_op jit(solution)/shard_map/pallas_call | solution.py:115
  137.8 0.6 collective-permute-start.23
  138.4 3.5 %shard_map.68 = (f32[2,64,768]{2,1,0:T(8,128)S(1)}, bf16[2,64,768]{2,1,0:T(8,128)(2,1)S(1)}) custom-call(s32[4]{0:T(128)S(1)} %pad_add_fusion.1.place_ref, bf16[2,128,384]{2,1,0:T(8,128)(2,1)S(1)} %get-tuple-element.48.refs_0_, bf16[2,128,384]{2,1,0:T(8,128)(2,1)S(1)} %collective-permute-done.18.refs_1_, ...), custom_call_target="tpu_custom_call" | custom-call | flops 603979776 | bytes 4718592 | tf_op jit(solution)/shard_map/pallas_call | solution.py:115
  142.0 1.6 %collective-permute-done.23 = bf16[2,64,768]{2,1,0:T(8,128)(2,1)S(1)} collective-permute-done((bf16[2,64,768]{2,1,0:T(8,128)(2,1)S(1)}, bf16[2,64,768]{2,1,0:T(8,128)(2,1)S(1)}, u32[]{:S(2)}, u32[]{:S(2)}) %collective-permute-start.23) | collective-permute-done | bytes 196640 | tf_op jit(solution)/shard_map/ppermute | solution.py:107
  143.6 3.5 %collective-permute-start.25 = (bf16[2,64,768]{2,1,0:T(8,128)(2,1)S(1)}, bf16[2,64,768]{2,1,0:T(8,128)(2,1)S(1)}, u32[]{:S(2)}, u32[]{:S(2)}) collective-permute-start(bf16[2,64,768]{2,1,0:T(8,128)(2,1)S(1)} %add_convert_fusion), channel_id=1, source_target_pairs={{0,8},{4,12},{8,0},{12,4},{1,9},{5,13},{9,1},{13,5},{2,10},{6,14},... | collective-permute-start | bytes 589832 | tf_op jit(solution)/shard_map/ppermute | solution.py:107
  147.1 0.9 collective-permute-start.24
  148.1 6.6 %collective-permute-done.25.far_ref = bf16[2,64,768]{2,1,0:T(8,128)(2,1)S(1)} collective-permute-done((bf16[2,64,768]{2,1,0:T(8,128)(2,1)S(1)}, bf16[2,64,768]{2,1,0:T(8,128)(2,1)S(1)}, u32[]{:S(2)}, u32[]{:S(2)}) %collective-permute-start.25) | collective-permute-done | bytes 196640 | tf_op jit(solution)/shard_map/ppermute | solution.py:107
  154.7 1.3 shard_map.70
  (49 shorter events, 2.4 us)
Async XLA Ops:
  0.0 5.0 %copy-start = (bf16[768,3,768]{2,0,1:T(8,128)(2,1)S(1)}, bf16[768,3,768]{2,0,1:T(8,128)(2,1)}, u32[]{:S(2)}) copy-start(bf16[768,3,768]{2,0,1:T(8,128)(2,1)} %param.7) | copy-start | bytes 10616836
  0.0 14.2 %copy-start.2 = (s32[2]{0:T(128)S(1)}, s32[2]{0:T(128)}, u32[]{:S(2)}) copy-start(s32[2]{0:T(128)} %param.11) | copy-start | bytes 28
  0.0 14.3 %copy-start.3 = (s32[2]{0:T(128)S(1)}, s32[2]{0:T(128)}, u32[]{:S(2)}) copy-start(s32[2]{0:T(128)} %param.10) | copy-start | bytes 28
  0.0 14.4 %copy-start.1 = (s32[2,4]{1,0:T(2,128)S(1)}, s32[2,4]{1,0:T(2,128)}, u32[]{:S(2)}) copy-start(s32[2,4]{1,0:T(2,128)} %param.9) | copy-start | bytes 100
  1.9 16.8 %collective-permute-start = (bf16[128,1536]{1,0:T(8,128)(2,1)}, bf16[128,1536]{1,0:T(8,128)(2,1)}, u32[]{:S(2)}, u32[]{:S(2)}) collective-permute-start(bf16[128,1536]{1,0:T(8,128)(2,1)} %dynamic-slice_bitcast_fusion.2.refs_0_), channel_id=1, source_target_pairs={{0,4},{4,0},{8,12},{12,8},{1,5},{5,1},{9,13},{13,9},{2,6},{6,2},{1... | collective-permute-start | bytes 1179656 | tf_op jit(solution)/shard_map/ppermute | solution.py:107
  6.0 15.8 %collective-permute-start.2 = (bf16[3,384,384]{2,1,0:T(8,128)(2,1)}, bf16[3,384,384]{2,1,0:T(8,128)(2,1)}, u32[]{:S(2)}, u32[]{:S(2)}) collective-permute-start(bf16[3,384,384]{2,1,0:T(8,128)(2,1)} %dynamic-slice_bitcast_fusion), channel_id=1, source_target_pairs={{0,0},{1,8},{4,4},{5,12},{8,1},{9,9},{12,5},{13,13},{2,2},{3,10},{... | collective-permute-start | bytes 2654216 | tf_op jit(solution)/shard_map/ppermute | solution.py:341
  19.6 20.3 %collective-permute-start.1 = (bf16[392,768]{1,0:T(8,128)(2,1)}, bf16[392,768]{1,0:T(8,128)(2,1)}, u32[]{:S(2)}, u32[]{:S(2)}) collective-permute-start(bf16[392,768]{1,0:T(8,128)(2,1)} %pad_maximum_fusion), channel_id=1, source_target_pairs={{0,4},{4,0},{8,12},{12,8},{1,5},{5,1},{9,13},{13,9},{2,6},{6,2},{1... | collective-permute-start | bytes 1806344 | tf_op jit(solution)/shard_map/ppermute | solution.py:107
  19.6 47.9 %collective-permute-start.5 = (bf16[768,768]{1,0:T(8,128)(2,1)}, bf16[768,768]{1,0:T(8,128)(2,1)}, u32[]{:S(2)}, u32[]{:S(2)}) collective-permute-start(bf16[768,768]{1,0:T(8,128)(2,1)} %refs_4_.3), channel_id=1, source_target_pairs={{0,1},{1,0},{2,3},{3,2},{4,5},{5,4},{6,7},{7,6},{8,9},{9,8},{10,11... | collective-permute-start | bytes 3538952 | tf_op jit(solution)/shard_map/ppermute | solution.py:107
  19.6 12.2 %collective-permute-start.3 = (bf16[128,1536]{1,0:T(8,128)(2,1)}, bf16[128,1536]{1,0:T(8,128)(2,1)}, u32[]{:S(2)}, u32[]{:S(2)}) collective-permute-start(bf16[128,1536]{1,0:T(8,128)(2,1)} %dynamic-slice_bitcast_fusion.2.refs_0_), channel_id=1, source_target_pairs={{0,2},{2,0},{1,3},{3,1},{4,6},{6,4},{5,7},{7,5},{8,10},{10,8},{9,1... | collective-permute-start | bytes 1179656 | tf_op jit(solution)/shard_map/ppermute | solution.py:107
  21.4 20.9 %collective-permute-start.6 = (bf16[128,1536]{1,0:T(8,128)(2,1)}, bf16[128,1536]{1,0:T(8,128)(2,1)}, u32[]{:S(2)}, u32[]{:S(2)}) collective-permute-start(bf16[128,1536]{1,0:T(8,128)(2,1)} %collective-permute-done.refs_1_), channel_id=1, source_target_pairs={{0,2},{2,0},{1,3},{3,1},{4,6},{6,4},{5,7},{7,5},{8,10},{10,8},{9,1... | collective-permute-start | bytes 1179656 | tf_op jit(solution)/shard_map/ppermute | solution.py:107
  21.8 48.6 %collective-permute-start.10 = (bf16[3,384,384]{2,1,0:T(8,128)(2,1)}, bf16[3,384,384]{2,1,0:T(8,128)(2,1)}, u32[]{:S(2)}, u32[]{:S(2)}) collective-permute-start(bf16[3,384,384]{2,1,0:T(8,128)(2,1)} %collective-permute-done.2.refs_8_), channel_id=1, source_target_pairs={{0,16},{16,0},{1,17},{17,1},{2,18},{18,2},{3,19},{19,3},{4,20},{20... | collective-permute-start | bytes 2654216 | tf_op jit(solution)/shard_map/ppermute | solution.py:107
  31.8 38.6 %collective-permute-start.11 = (bf16[3,384,256]{2,1,0:T(8,128)(2,1)S(1)}, bf16[3,384,256]{2,1,0:T(8,128)(2,1)}, u32[]{:S(2)}, u32[]{:S(2)}) collective-permute-start(bf16[3,384,256]{2,1,0:T(8,128)(2,1)S(1)} %dynamic-slice_bitcast_fusion.1), channel_id=1, source_target_pairs={{0,4},{1,12},{4,0},{5,8},{8,5},{9,13},{12,1},{13,9},{2,6},{3,14},{... | collective-permute-start | bytes 1769480 | tf_op jit(solution)/shard_map/ppermute | solution.py:341
  39.8 30.6 %collective-permute-start.12 = (bf16[392,768]{1,0:T(8,128)(2,1)}, bf16[392,768]{1,0:T(8,128)(2,1)}, u32[]{:S(2)}, u32[]{:S(2)}) collective-permute-start(bf16[392,768]{1,0:T(8,128)(2,1)} %collective-permute-done.1.refs_6_), channel_id=1, source_target_pairs={{0,16},{16,0},{1,17},{17,1},{2,18},{18,2},{3,19},{19,3},{4,20},{20... | collective-permute-start | bytes 1806344 | tf_op jit(solution)/shard_map/ppermute | solution.py:107
  42.2 25.2 %collective-permute-start.4 = (bf16[136,1536]{1,0:T(8,128)(2,1)S(1)}, bf16[136,1536]{1,0:T(8,128)(2,1)}, u32[]{:S(2)}, u32[]{:S(2)}) collective-permute-start(bf16[136,1536]{1,0:T(8,128)(2,1)S(1)} %pad_maximum_fusion.1), channel_id=1, source_target_pairs={{0,8},{4,12},{8,0},{12,4},{1,9},{5,13},{9,1},{13,5},{2,10},{6,14},... | collective-permute-start | bytes 1253384 | tf_op jit(solution)/shard_map/ppermute | solution.py:107
  67.5 11.4 %collective-permute-start.7 = (bf16[136,1536]{1,0:T(8,128)(2,1)S(1)}, bf16[136,1536]{1,0:T(8,128)(2,1)}, u32[]{:S(2)}, u32[]{:S(2)}) collective-permute-start(bf16[136,1536]{1,0:T(8,128)(2,1)S(1)} %pad_maximum_fusion.1), channel_id=1, source_target_pairs={{0,12},{4,8},{8,4},{12,0},{1,13},{5,9},{9,5},{13,1},{2,14},{6,10},... | collective-permute-start | bytes 1253384 | tf_op jit(solution)/shard_map/ppermute | solution.py:107
  70.4 13.8 %collective-permute-start.13 = (bf16[3,384,256]{2,1,0:T(8,128)(2,1)}, bf16[3,384,256]{2,1,0:T(8,128)(2,1)}, u32[]{:S(2)}, u32[]{:S(2)}) collective-permute-start(bf16[3,384,256]{2,1,0:T(8,128)(2,1)} %collective-permute-done.11.refs_10_), channel_id=1, source_target_pairs={{0,16},{16,0},{1,17},{17,1},{2,18},{18,2},{3,19},{19,3},{4,20},{20... | collective-permute-start | bytes 1769480 | tf_op jit(solution)/shard_map/ppermute | solution.py:107
  72.6 23.3 %collective-permute-start.8 = (bf16[136,1536]{1,0:T(8,128)(2,1)}, bf16[136,1536]{1,0:T(8,128)(2,1)}, u32[]{:S(2)}, u32[]{:S(2)}) collective-permute-start(bf16[136,1536]{1,0:T(8,128)(2,1)} %collective-permute-done.4.refs_2_), channel_id=1, source_target_pairs={{0,2},{2,0},{1,3},{3,1},{4,6},{6,4},{5,7},{7,5},{8,10},{10,8},{9,1... | collective-permute-start | bytes 1253384 | tf_op jit(solution)/shard_map/ppermute | solution.py:107
  78.9 17.0 %collective-permute-start.9 = (bf16[136,1536]{1,0:T(8,128)(2,1)}, bf16[136,1536]{1,0:T(8,128)(2,1)}, u32[]{:S(2)}, u32[]{:S(2)}) collective-permute-start(bf16[136,1536]{1,0:T(8,128)(2,1)} %collective-permute-done.7.refs_3_), channel_id=1, source_target_pairs={{0,2},{2,0},{1,3},{3,1},{4,6},{6,4},{5,7},{7,5},{8,10},{10,8},{9,1... | collective-permute-start | bytes 1253384 | tf_op jit(solution)/shard_map/ppermute | solution.py:107
  84.2 10.2 %collective-permute-start.14 = (bf16[3,384,128]{2,1,0:T(8,128)(2,1)}, bf16[3,384,128]{2,1,0:T(8,128)(2,1)}, u32[]{:S(2)}, u32[]{:S(2)}) collective-permute-start(bf16[3,384,128]{2,1,0:T(8,128)(2,1)} %dynamic-slice_bitcast_fusion.3), channel_id=1, source_target_pairs={{0,4},{1,12},{4,0},{5,8},{8,5},{9,13},{12,1},{13,9},{2,6},{3,14},{... | collective-permute-start | bytes 884744 | tf_op jit(solution)/shard_map/ppermute | solution.py:341
  94.4 8.6 %collective-permute-start.15 = (bf16[3,384,128]{2,1,0:T(8,128)(2,1)}, bf16[3,384,128]{2,1,0:T(8,128)(2,1)S(1)}, u32[]{:S(2)}, u32[]{:S(2)}) collective-permute-start(bf16[3,384,128]{2,1,0:T(8,128)(2,1)} %collective-permute-done.14.refs_10_), channel_id=1, source_target_pairs={{0,16},{16,0},{1,17},{17,1},{2,18},{18,2},{3,19},{19,3},{4,20},{20... | collective-permute-start | bytes 884744 | tf_op jit(solution)/shard_map/ppermute | solution.py:107
  102.9 6.1 %collective-permute-start.17 = (bf16[4,320,512]{2,1,0:T(8,128)(2,1)S(1)}, bf16[4,320,512]{2,1,0:T(8,128)(2,1)S(1)}, u32[]{:S(2)}, u32[]{:S(2)}) collective-permute-start(bf16[4,320,512]{2,1,0:T(8,128)(2,1)S(1)} %get-tuple-element.39), channel_id=1, source_target_pairs={{0,1},{1,0},{2,3},{3,2},{4,5},{5,4},{6,7},{7,6},{8,9},{9,8},{10,11... | collective-permute-start | bytes 3932168 | tf_op jit(solution)/shard_map/ppermute | solution.py:107
  108.0 4.9 %collective-permute-start.16 = (bf16[4,320,256]{2,1,0:T(8,128)(2,1)S(1)}, bf16[4,320,256]{2,1,0:T(8,128)(2,1)S(1)}, u32[]{:S(2)}, u32[]{:S(2)}) collective-permute-start(bf16[4,320,256]{2,1,0:T(8,128)(2,1)S(1)} %get-tuple-element.43), channel_id=1, source_target_pairs={{0,1},{1,0},{2,3},{3,2},{4,5},{5,4},{6,7},{7,6},{8,9},{9,8},{10,11... | collective-permute-start | bytes 1966088 | tf_op jit(solution)/shard_map/ppermute | solution.py:107
  108.5 11.0 %collective-permute-start.21 = (bf16[392,768]{1,0:T(8,128)(2,1)}, bf16[392,768]{1,0:T(8,128)(2,1)S(1)}, u32[]{:S(2)}, u32[]{:S(2)}) collective-permute-start(bf16[392,768]{1,0:T(8,128)(2,1)} %collective-permute-done.1.refs_6_), channel_id=1, source_target_pairs={{0,1},{1,0},{2,3},{3,2},{4,5},{5,4},{6,7},{7,6},{8,9},{9,8},{10,11... | collective-permute-start | bytes 1806344 | tf_op jit(solution)/shard_map/ppermute | solution.py:107
  108.6 11.0 %collective-permute-start.22 = (bf16[392,768]{1,0:T(8,128)(2,1)}, bf16[392,768]{1,0:T(8,128)(2,1)S(1)}, u32[]{:S(2)}, u32[]{:S(2)}) collective-permute-start(bf16[392,768]{1,0:T(8,128)(2,1)} %collective-permute-done.12.refs_7_), channel_id=1, source_target_pairs={{0,1},{1,0},{2,3},{3,2},{4,5},{5,4},{6,7},{7,6},{8,9},{9,8},{10,11... | collective-permute-start | bytes 1806344 | tf_op jit(solution)/shard_map/ppermute | solution.py:107
  115.0 10.1 %collective-permute-start.18 = (bf16[2,128,384]{2,1,0:T(8,128)(2,1)S(1)}, bf16[2,128,384]{2,1,0:T(8,128)(2,1)S(1)}, u32[]{:S(2)}, u32[]{:S(2)}) collective-permute-start(bf16[2,128,384]{2,1,0:T(8,128)(2,1)S(1)} %get-tuple-element.49), channel_id=1, source_target_pairs={{0,4},{4,0},{8,12},{12,8},{1,5},{5,1},{9,13},{13,9},{2,6},{6,2},{1... | collective-permute-start | bytes 589832 | tf_op jit(solution)/shard_map/ppermute | solution.py:107
  117.1 17.1 %collective-permute-start.19 = (bf16[2,128,384]{2,1,0:T(8,128)(2,1)S(1)}, bf16[2,128,384]{2,1,0:T(8,128)(2,1)S(1)}, u32[]{:S(2)}, u32[]{:S(2)}) collective-permute-start(bf16[2,128,384]{2,1,0:T(8,128)(2,1)S(1)} %get-tuple-element.48.refs_0_), channel_id=1, source_target_pairs={{0,8},{4,12},{8,0},{12,4},{1,9},{5,13},{9,1},{13,5},{2,10},{6,14},... | collective-permute-start | bytes 589832 | tf_op jit(solution)/shard_map/ppermute | solution.py:107
  117.1 17.1 %collective-permute-start.20 = (bf16[2,128,384]{2,1,0:T(8,128)(2,1)S(1)}, bf16[2,128,384]{2,1,0:T(8,128)(2,1)S(1)}, u32[]{:S(2)}, u32[]{:S(2)}) collective-permute-start(bf16[2,128,384]{2,1,0:T(8,128)(2,1)S(1)} %get-tuple-element.49), channel_id=1, source_target_pairs={{0,12},{4,8},{8,4},{12,0},{1,13},{5,9},{9,5},{13,1},{2,14},{6,10},... | collective-permute-start | bytes 589832 | tf_op jit(solution)/shard_map/ppermute | solution.py:107
  137.8 5.7 %collective-permute-start.23 = (bf16[2,64,768]{2,1,0:T(8,128)(2,1)S(1)}, bf16[2,64,768]{2,1,0:T(8,128)(2,1)S(1)}, u32[]{:S(2)}, u32[]{:S(2)}) collective-permute-start(bf16[2,64,768]{2,1,0:T(8,128)(2,1)S(1)} %get-tuple-element.52), channel_id=1, source_target_pairs={{0,2},{2,0},{1,3},{3,1},{4,6},{6,4},{5,7},{7,5},{8,10},{10,8},{9,1... | collective-permute-start | bytes 589832 | tf_op jit(solution)/shard_map/ppermute | solution.py:107
  143.6 11.1 %collective-permute-start.25 = (bf16[2,64,768]{2,1,0:T(8,128)(2,1)S(1)}, bf16[2,64,768]{2,1,0:T(8,128)(2,1)S(1)}, u32[]{:S(2)}, u32[]{:S(2)}) collective-permute-start(bf16[2,64,768]{2,1,0:T(8,128)(2,1)S(1)} %add_convert_fusion), channel_id=1, source_target_pairs={{0,8},{4,12},{8,0},{12,4},{1,9},{5,13},{9,1},{13,5},{2,10},{6,14},... | collective-permute-start | bytes 589832 | tf_op jit(solution)/shard_map/ppermute | solution.py:107
  147.1 7.6 %collective-permute-start.24 = (bf16[2,64,768]{2,1,0:T(8,128)(2,1)S(1)}, bf16[2,64,768]{2,1,0:T(8,128)(2,1)S(1)}, u32[]{:S(2)}, u32[]{:S(2)}) collective-permute-start(bf16[2,64,768]{2,1,0:T(8,128)(2,1)S(1)} %get-tuple-element.53), channel_id=1, source_target_pairs={{0,2},{2,0},{1,3},{3,1},{4,6},{6,4},{5,7},{7,5},{8,10},{10,8},{9,1... | collective-permute-start | bytes 589832 | tf_op jit(solution)/shard_map/ppermute | solution.py:107

commit v29 on v28

--- a/solution.py
+++ b/solution.py
@@ -127,17 +127,21 @@
     )(*prefetch, *operands)
 
 
-def project(place, mine, theirs, chunks, firsts, cols):
+def project(place, mine, theirs, chunks, firsts, cols, tokens=None):
     rows, (count, width) = len(mine), theirs[0].shape
+    pieces = [] if tokens is not None else [*mine, *theirs]
     half = chunks[0][0].shape[1]
     slices = len(chunks)
     flat = [w for of_round in chunks for w in of_round]
-    fetched = 2 * rows + len(flat)
+    fetched = len(pieces) + len(flat)
 
     def kernel(place_ref, *refs):
         row, group, frame, core = (place_ref[i] for i in range(4))
-        w_refs = refs[2 * rows : fetched]
-        q_keep, kv_keep, send, x_all, w_all, total, sems = refs[fetched:]
+        w_refs = refs[len(pieces) : fetched]
+        if pieces:
+            q_keep, kv_keep, send, x_all, w_all, total, sems = refs[fetched:]
+        else:
+            x_all, q_keep, kv_keep, send, w_all, total, sems = refs[fetched:]
         copies = []
         for k in range(slices):
             for g in range(2):
@@ -147,7 +151,7 @@
                     into = w_all.at[pl.ds(at, half), part * cols : (part + 1) * cols]
                     copies.append(pltpu.make_async_copy(source, into, sems.at[len(copies)]))
         fetch_x = []
-        for i in range(2 * rows):
+        for i in range(len(pieces)):
             to = x_all.at[row ^ (i % rows), (frame + i // rows) % 2]
             fetch_x.append(pltpu.make_async_copy(refs[i].at[pl.ds(0, count)], to, sems.at[len(copies) + i]))
         for copy in copies + fetch_x:
@@ -155,8 +159,9 @@
         for copy in copies:
             copy.wait()
         for s in range(rows):
-            fetch_x[s].wait()
-            fetch_x[rows + s].wait()
+            if pieces:
+                fetch_x[s].wait()
+                fetch_x[rows + s].wait()
             at = row ^ s
             acc = jnp.dot(x_all[at].reshape(-1, width), w_all[...], preferred_element_type=jnp.float32)
             kv_part = acc[:, cols:]
@@ -178,14 +183,14 @@
             jax.ShapeDtypeStruct((rows, 2 * BS, cols), jnp.float32),
             jax.ShapeDtypeStruct((rows, 2 * count, 2 * cols), jnp.float32),
             jax.ShapeDtypeStruct((rows, 2 * count + BS, 2 * cols), jnp.bfloat16),
-        ),
+        )
+        + ((jax.ShapeDtypeStruct((rows, 2, count, width), jnp.bfloat16),) if pieces else ()),
         grid_spec=pltpu.PrefetchScalarGridSpec(
             num_scalar_prefetch=1,
             grid=(),
-            in_specs=[hbm] * fetched,
-            out_specs=(vmem, vmem, vmem),
+            in_specs=[hbm] * fetched + [vmem] * (not pieces),
+            out_specs=(vmem,) * (4 if pieces else 3),
             scratch_shapes=[
-                pltpu.VMEM((rows, 2, count, width), jnp.bfloat16),
                 pltpu.VMEM((width, 3 * cols), jnp.bfloat16),
                 pltpu.VMEM((rows, 2, count, cols), jnp.float32),
                 pltpu.SemaphoreType.DMA((2 * rows + 3 * len(flat),)),
@@ -193,7 +198,7 @@
         ),
         compiler_params=pltpu.CompilerParams(vmem_limit_bytes=VMEM_BYTES),
         cost_estimate=pl.CostEstimate(flops=8 * flops, bytes_accessed=flops // 300, transcendentals=0),
-    )(place, *mine, *theirs, *flat)
+    )(place, *pieces, *flat, *([] if pieces else [tokens]))
 
 
 def attend_all(place, members, counts, queries, keyvals, more, earlier=()):
@@ -267,12 +272,13 @@
 
         def term(c, other):
             side = 1 - core if other else core
+            if c == 0:
+                both = jnp.concatenate([a_all[(2 * side) ^ row], a_all[(2 * side + 1) ^ row]], axis=1)
+                acc = jnp.dot(both, w_refs[other][...], preferred_element_type=jnp.float32)
+                return acc.astype(jnp.bfloat16).astype(jnp.float32)
             acc = None
             for i in range(2):
-                if c == 0:
-                    weight, half = w_refs[other][i * cols : (i + 1) * cols, :], i
-                else:
-                    weight, half = w_refs[2 + 2 * other + i][:cols], (i + group) % 2
+                weight, half = w_refs[2 + 2 * other + i][:cols], (i + group) % 2
                 part = jnp.dot(a_all[(2 * side + half) ^ row], weight, preferred_element_type=jnp.float32)
                 acc = part if acc is None else acc + part
             return acc.astype(jnp.bfloat16).astype(jnp.float32)
@@ -375,10 +381,10 @@
 
     pieces = [mine, near, far_2, far_3], [mine_x, near_x, far_2x, far_3x]
     chunks = [(here[0], there[0]), (here[1], after(there[1], members, counts))]
-    first = project(place, *pieces, chunks, (0, 0), cols - last)
+    *first, tokens = project(place, *pieces, chunks, (0, 0), cols - last)
     first_more = swap(first[2], "heads")
     chunks[1] = (here[2], after(there[2], first[2]))
-    second = project(place, *pieces, chunks, (cols - last, 0), last)
+    second = project(place, *pieces, chunks, (cols - last, 0), last, tokens)
     second_more = swap(second[2], "heads")
     attended = attend_all(place, members, counts, *first[:2], first_more)
     beside_across = [swap(part, "heads") for part in beside]

time: 157 us -> 156 us (level)
  transfers between devices with their start and end apart: 26 -> 26, of which waited for: 11 -> 11; matrix products, arithmetic and copies ran while one was open for 6% -> 6% of each run, Pallas kernels for 14% -> 13%
where the time goes in v29:
time: 156 us; the launch traced here: 155 us
  waiting for transfers between devices  68.4 us (44%)
  starting transfers between devices  50.1 us (32%)
  Pallas kernels  25 us (16%)
  local copies, waits for them, and re-layouts  8.78 us (6%)
  other arithmetic  2.41 us (2%)
    ppermute x23, waiting for transfers between devices, swap(): return lax.ppermute(value, axis, [(i, i ^ step) for i in range(peers)])  64.6 us
    ppermute x23, starting transfers between devices, swap(): return lax.ppermute(value, axis, [(i, i ^ step) for i in range(peers)])  34.7 us
    ppermute x3, starting transfers between devices, reshard(): lax.ppermute(after(value, *others) if others else value, ('rows', 'heads'...  15.4 us
    pallas_call x5, Pallas kernels, call(): pl.pallas_call(kernel, out_shape=out_shape, grid_spec=pltpu.PrefetchScala...  14.2 us
    pallas_call x2, Pallas kernels, project(): pl.pallas_call(kernel, out_shape=(jax.ShapeDtypeStruct((rows, 2 * BS, col...  10.8 us
    ppermute x3, waiting for transfers between devices, reshard(): lax.ppermute(after(value, *others) if others else value, ('rows', 'heads'...  3.73 us
  transfers between devices with their start and end apart: 26, of which 11 were waited for; matrix products, arithmetic and copies ran while one was open for 6% of the time, Pallas kernels for 13%

profile of v29, /device:TPU:0, one launch (start us, length us, event | category | flops | bytes accessed | tf_op | source)
XLA Modules:
  0.0 154.8 jit_solution(14188774775039236177)
XLA Ops:
  0.0 1.9 %dynamic-slice_bitcast_fusion.2.refs_0_ = bf16[128,1536]{1,0:T(8,128)(2,1)} fusion(bf16[1,128,3072]{2,1,0:T(8,128)(2,1)} %param.6, s32[]{:T(128)S(6)} %select_n.49), kind=kLoop, calls=%fused_computation.7 | loop fusion | bytes 786436 | tf_op jit(solution)/shard_map/dynamic_slice | solution.py:349
  1.9 3.0 %collective-permute-start = (bf16[128,1536]{1,0:T(8,128)(2,1)}, bf16[128,1536]{1,0:T(8,128)(2,1)}, u32[]{:S(2)}, u32[]{:S(2)}) collective-permute-start(bf16[128,1536]{1,0:T(8,128)(2,1)} %dynamic-slice_bitcast_fusion.2.refs_0_), channel_id=1, source_target_pairs={{0,4},{4,0},{8,12},{12,8},{1,5},{5,1},{9,13},{13,9},{2,6},{6,2},{1... | collective-permute-start | bytes 1179656 | tf_op jit(solution)/shard_map/ppermute | solution.py:107
  5.0 1.0 dynamic-slice_bitcast_fusion
  6.0 8.2 %collective-permute-start.2 = (bf16[3,384,384]{2,1,0:T(8,128)(2,1)}, bf16[3,384,384]{2,1,0:T(8,128)(2,1)}, u32[]{:S(2)}, u32[]{:S(2)}) collective-permute-start(bf16[3,384,384]{2,1,0:T(8,128)(2,1)} %dynamic-slice_bitcast_fusion), channel_id=1, source_target_pairs={{0,0},{1,8},{4,4},{5,12},{8,1},{9,9},{12,5},{13,13},{2,2},{3,10},{... | collective-permute-start | bytes 2654216 | tf_op jit(solution)/shard_map/ppermute | solution.py:347
  14.5 1.1 constant_dynamic-slice_fusion
  15.6 3.1 %collective-permute-done.refs_1_ = bf16[128,1536]{1,0:T(8,128)(2,1)} collective-permute-done((bf16[128,1536]{1,0:T(8,128)(2,1)}, bf16[128,1536]{1,0:T(8,128)(2,1)}, u32[]{:S(2)}, u32[]{:S(2)}) %collective-permute-start) | collective-permute-done | bytes 393248 | tf_op jit(solution)/shard_map/ppermute | solution.py:107
  18.7 0.9 pad_maximum_fusion
  19.6 1.7 %collective-permute-start.3 = (bf16[128,1536]{1,0:T(8,128)(2,1)}, bf16[128,1536]{1,0:T(8,128)(2,1)}, u32[]{:S(2)}, u32[]{:S(2)}) collective-permute-start(bf16[128,1536]{1,0:T(8,128)(2,1)} %dynamic-slice_bitcast_fusion.2.refs_0_), channel_id=1, source_target_pairs={{0,2},{2,0},{1,3},{3,1},{4,6},{6,4},{5,7},{7,5},{8,10},{10,8},{9,1... | collective-permute-start | bytes 1179656 | tf_op jit(solution)/shard_map/ppermute | solution.py:107
  21.8 1.7 %collective-permute-start.8 = (bf16[3,384,384]{2,1,0:T(8,128)(2,1)}, bf16[3,384,384]{2,1,0:T(8,128)(2,1)}, u32[]{:S(2)}, u32[]{:S(2)}) collective-permute-start(bf16[3,384,384]{2,1,0:T(8,128)(2,1)} %collective-permute-done.2.refs_8_.refs_0_), channel_id=1, source_target_pairs={{0,16},{16,0},{1,17},{17,1},{2,18},{18,2},{3,19},{19,3},{4,20},{20... | collective-permute-start | bytes 2654216 | tf_op jit(solution)/shard_map/ppermute | solution.py:107
  23.6 8.3 %collective-permute-done.3.refs_4_ = bf16[128,1536]{1,0:T(8,128)(2,1)} collective-permute-done((bf16[128,1536]{1,0:T(8,128)(2,1)}, bf16[128,1536]{1,0:T(8,128)(2,1)}, u32[]{:S(2)}, u32[]{:S(2)}) %collective-permute-start.3) | collective-permute-done | bytes 393248 | tf_op jit(solution)/shard_map/ppermute | solution.py:107
  31.8 2.0 %collective-permute-start.9 = (bf16[3,384,256]{2,1,0:T(8,128)(2,1)S(1)}, bf16[3,384,256]{2,1,0:T(8,128)(2,1)}, u32[]{:S(2)}, u32[]{:S(2)}) collective-permute-start(bf16[3,384,256]{2,1,0:T(8,128)(2,1)S(1)} %dynamic-slice_bitcast_fusion.1), channel_id=1, source_target_pairs={{0,4},{1,12},{4,0},{5,8},{8,5},{9,13},{12,1},{13,9},{2,6},{3,14},{... | collective-permute-start | bytes 1769480 | tf_op jit(solution)/shard_map/ppermute | solution.py:347
  33.9 6.0 %collective-permute-done.1.refs_6_ = bf16[392,768]{1,0:T(8,128)(2,1)} collective-permute-done((bf16[392,768]{1,0:T(8,128)(2,1)}, bf16[392,768]{1,0:T(8,128)(2,1)}, u32[]{:S(2)}, u32[]{:S(2)}) %collective-permute-start.1) | collective-permute-done | bytes 602144 | tf_op jit(solution)/shard_map/ppermute | solution.py:107
  39.8 1.4 collective-permute-start.10
  41.2 1.0 pad_maximum_fusion.1
  42.2 6.8 %collective-permute-start.4 = (bf16[136,1536]{1,0:T(8,128)(2,1)S(1)}, bf16[136,1536]{1,0:T(8,128)(2,1)}, u32[]{:S(2)}, u32[]{:S(2)}) collective-permute-start(bf16[136,1536]{1,0:T(8,128)(2,1)S(1)} %pad_maximum_fusion.1), channel_id=1, source_target_pairs={{0,8},{4,12},{8,0},{12,4},{1,9},{5,13},{9,1},{13,5},{2,10},{6,14},... | collective-permute-start | bytes 1253384 | tf_op jit(solution)/shard_map/ppermute | solution.py:107
  49.1 0.8 dynamic-slice_bitcast_fusion.3
  49.9 17.6 %collective-permute-done.4.refs_2_ = bf16[136,1536]{1,0:T(8,128)(2,1)} collective-permute-done((bf16[136,1536]{1,0:T(8,128)(2,1)S(1)}, bf16[136,1536]{1,0:T(8,128)(2,1)}, u32[]{:S(2)}, u32[]{:S(2)}) %collective-permute-start.4) | collective-permute-done | bytes 417824 | tf_op jit(solution)/shard_map/ppermute | solution.py:107
  67.5 2.9 %collective-permute-start.7 = (bf16[136,1536]{1,0:T(8,128)(2,1)S(1)}, bf16[136,1536]{1,0:T(8,128)(2,1)}, u32[]{:S(2)}, u32[]{:S(2)}) collective-permute-start(bf16[136,1536]{1,0:T(8,128)(2,1)S(1)} %pad_maximum_fusion.1), channel_id=1, source_target_pairs={{0,12},{4,8},{8,4},{12,0},{1,13},{5,9},{9,5},{13,1},{2,14},{6,10},... | collective-permute-start | bytes 1253384 | tf_op jit(solution)/shard_map/ppermute | solution.py:107
  70.4 1.6 %collective-permute-start.11 = (bf16[3,384,256]{2,1,0:T(8,128)(2,1)}, bf16[3,384,256]{2,1,0:T(8,128)(2,1)}, u32[]{:S(2)}, u32[]{:S(2)}) collective-permute-start(bf16[3,384,256]{2,1,0:T(8,128)(2,1)} %collective-permute-done.9.refs_10_), channel_id=1, source_target_pairs={{0,16},{16,0},{1,17},{17,1},{2,18},{18,2},{3,19},{19,3},{4,20},{20... | collective-permute-start | bytes 1769480 | tf_op jit(solution)/shard_map/ppermute | solution.py:107
  72.0 0.6 slice_bitcast_fusion.2
  72.6 1.5 collective-permute-start.14
  74.1 0.7 slice_bitcast_fusion.1
  74.8 4.1 %collective-permute-done.7.refs_3_ = bf16[136,1536]{1,0:T(8,128)(2,1)} collective-permute-done((bf16[136,1536]{1,0:T(8,128)(2,1)S(1)}, bf16[136,1536]{1,0:T(8,128)(2,1)}, u32[]{:S(2)}, u32[]{:S(2)}) %collective-permute-start.7) | collective-permute-done | bytes 417824 | tf_op jit(solution)/shard_map/ppermute | solution.py:107
  78.9 1.5 collective-permute-start.15
  80.4 0.7 slice_bitcast_fusion
  81.1 0.6 gather_fusion
  81.7 2.5 %collective-permute-done.11.refs_11_ = bf16[3,384,256]{2,1,0:T(8,128)(2,1)} collective-permute-done((bf16[3,384,256]{2,1,0:T(8,128)(2,1)}, bf16[3,384,256]{2,1,0:T(8,128)(2,1)}, u32[]{:S(2)}, u32[]{:S(2)}) %collective-permute-start.11) | collective-permute-done | bytes 589856 | tf_op jit(solution)/shard_map/ppermute | solution.py:107
  84.2 5.2 %collective-permute-start.12 = (bf16[3,384,128]{2,1,0:T(8,128)(2,1)}, bf16[3,384,128]{2,1,0:T(8,128)(2,1)}, u32[]{:S(2)}, u32[]{:S(2)}) collective-permute-start(bf16[3,384,128]{2,1,0:T(8,128)(2,1)} %dynamic-slice_bitcast_fusion.3), channel_id=1, source_target_pairs={{0,4},{1,12},{4,0},{5,8},{8,5},{9,13},{12,1},{13,9},{2,6},{3,14},{... | collective-permute-start | bytes 884744 | tf_op jit(solution)/shard_map/ppermute | solution.py:347
  89.9 0.6 gather_fusion.1
  90.7 3.7 %collective-permute-done.12.refs_2_ = bf16[3,384,128]{2,1,0:T(8,128)(2,1)} collective-permute-done((bf16[3,384,128]{2,1,0:T(8,128)(2,1)}, bf16[3,384,128]{2,1,0:T(8,128)(2,1)}, u32[]{:S(2)}, u32[]{:S(2)}) %collective-permute-start.12) | collective-permute-done | bytes 294944 | tf_op jit(solution)/shard_map/ppermute | solution.py:347
  94.4 1.5 collective-permute-start.13
  96.0 7.0 %shard_map.64 = (f32[4,128,256]{2,1,0:T(8,128)S(1)}, f32[4,256,512]{2,1,0:T(8,128)S(1)}, bf16[4,320,512]{2,1,0:T(8,128)(2,1)S(1)}, bf16[4,2,128,1536]{3,2,1,0:T(8,128)(2,1)S(1)}) custom-call(s32[4]{0:T(128)S(1)} %pad_add_fusion.1.place_ref, bf16[128,1536]{1,0:T(8,128)(2,1)} %dynamic-slice_bitcast_fusion.2.refs_0_, ...), custom_call_target="tpu_custom_call" | custom-call | flops 19327352832 | bytes 8053063 | tf_op jit(solution)/shard_map/pallas_call | solution.py:180
  103.0 3.8 %shard_map.65 = (f32[4,128,128]{2,1,0:T(8,128)S(1)}, f32[4,256,256]{2,1,0:T(8,128)S(1)}, bf16[4,320,256]{2,1,0:T(8,128)(2,1)S(1)}) custom-call(s32[4]{0:T(128)S(1)} %pad_add_fusion.1.place_ref, bf16[3,384,384]{2,1,0:T(8,128)(2,1)} %collective-permute-done.2.refs_8_.refs_0_, bf16[3,384,384]{2,1,0:T(8,128)(2,1)} %collective-permute-done.8.refs_9_.refs_1_, ...), custom_call_target="tpu_custom_call" | custom-call | flops 9663676416 | bytes 4026531 | tf_op jit(solution)/shard_map/pallas_call | solution.py:180
  106.8 0.6 collective-permute-start.16
  107.9 3.8 %shard_map.66 = (bf16[2,128,256]{2,1,0:T(8,128)(2,1)S(1)}, bf16[2,128,256]{2,1,0:T(8,128)(2,1)S(1)}) custom-call(s32[4]{0:T(128)S(1)} %pad_add_fusion.1.place_ref, s32[16]{0:T(128)S(1)} %reshape.24.members_ref, s32[4]{0:T(128)S(1)} %slice_reduce_fusion.1.counts_ref, f32[4,128,256]{2,1,0:T(8,128)S(1)} %get-tuple-element.46.q_ref, ...), custom_call_target="tpu_custom_call" | custom-call | flops 268435456 | bytes 2097152 | tf_op jit(solution)/shard_map/pallas_call | solution.py:115
  111.7 2.2 %shard_map.67 = (bf16[2,128,384]{2,1,0:T(8,128)(2,1)S(1)}, bf16[2,128,384]{2,1,0:T(8,128)(2,1)S(1)}) custom-call(s32[4]{0:T(128)S(1)} %pad_add_fusion.1.place_ref, s32[16]{0:T(128)S(1)} %reshape.24.members_ref, s32[4]{0:T(128)S(1)} %slice_reduce_fusion.1.counts_ref, f32[4,128,128]{2,1,0:T(8,128)S(1)} %get-tuple-element.43.q_ref, ...), custom_call_target="tpu_custom_call" | custom-call | flops 134217728 | bytes 1048576 | tf_op jit(solution)/shard_map/pallas_call | solution.py:115
  113.9 2.1 %collective-permute-start.18 = (bf16[2,128,384]{2,1,0:T(8,128)(2,1)S(1)}, bf16[2,128,384]{2,1,0:T(8,128)(2,1)S(1)}, u32[]{:S(2)}, u32[]{:S(2)}) collective-permute-start(bf16[2,128,384]{2,1,0:T(8,128)(2,1)S(1)} %get-tuple-element.51), channel_id=1, source_target_pairs={{0,4},{4,0},{8,12},{12,8},{1,5},{5,1},{9,13},{13,9},{2,6},{6,2},{1... | collective-permute-start | bytes 589832 | tf_op jit(solution)/shard_map/ppermute | solution.py:107
  116.0 2.4 %collective-permute-start.20 = (bf16[2,128,384]{2,1,0:T(8,128)(2,1)S(1)}, bf16[2,128,384]{2,1,0:T(8,128)(2,1)S(1)}, u32[]{:S(2)}, u32[]{:S(2)}) collective-permute-start(bf16[2,128,384]{2,1,0:T(8,128)(2,1)S(1)} %get-tuple-element.51), channel_id=1, source_target_pairs={{0,12},{4,8},{8,4},{12,0},{1,13},{5,9},{9,5},{13,1},{2,14},{6,10},... | collective-permute-start | bytes 589832 | tf_op jit(solution)/shard_map/ppermute | solution.py:107
  118.4 5.5 %collective-permute-done.18.refs_1_ = bf16[2,128,384]{2,1,0:T(8,128)(2,1)S(1)} collective-permute-done((bf16[2,128,384]{2,1,0:T(8,128)(2,1)S(1)}, bf16[2,128,384]{2,1,0:T(8,128)(2,1)S(1)}, u32[]{:S(2)}, u32[]{:S(2)}) %collective-permute-start.18) | collective-permute-done | bytes 196640 | tf_op jit(solution)/shard_map/ppermute | solution.py:107
  124.0 9.2 %collective-permute-done.19.refs_2_ = bf16[2,128,384]{2,1,0:T(8,128)(2,1)S(1)} collective-permute-done((bf16[2,128,384]{2,1,0:T(8,128)(2,1)S(1)}, bf16[2,128,384]{2,1,0:T(8,128)(2,1)S(1)}, u32[]{:S(2)}, u32[]{:S(2)}) %collective-permute-start.19) | collective-permute-done | bytes 196640 | tf_op jit(solution)/shard_map/ppermute | solution.py:107
  133.1 3.5 %shard_map.69 = (f32[2,64,768]{2,1,0:T(8,128)S(1)}, bf16[2,64,768]{2,1,0:T(8,128)(2,1)S(1)}) custom-call(s32[4]{0:T(128)S(1)} %pad_add_fusion.1.place_ref, bf16[2,128,384]{2,1,0:T(8,128)(2,1)S(1)} %get-tuple-element.50.refs_0_, bf16[2,128,384]{2,1,0:T(8,128)(2,1)S(1)} %collective-permute-done.18.refs_1_, ...), custom_call_target="tpu_custom_call" | custom-call | flops 603979776 | bytes 4718592 | tf_op jit(solution)/shard_map/pallas_call | solution.py:115
  136.6 0.6 collective-permute-start.23
  137.2 3.5 %shard_map.68 = (f32[2,64,768]{2,1,0:T(8,128)S(1)}, bf16[2,64,768]{2,1,0:T(8,128)(2,1)S(1)}) custom-call(s32[4]{0:T(128)S(1)} %pad_add_fusion.1.place_ref, bf16[2,128,384]{2,1,0:T(8,128)(2,1)S(1)} %get-tuple-element.50.refs_0_, bf16[2,128,384]{2,1,0:T(8,128)(2,1)S(1)} %collective-permute-done.18.refs_1_, ...), custom_call_target="tpu_custom_call" | custom-call | flops 603979776 | bytes 4718592 | tf_op jit(solution)/shard_map/pallas_call | solution.py:115
  140.6 1.7 %collective-permute-done.23 = bf16[2,64,768]{2,1,0:T(8,128)(2,1)S(1)} collective-permute-done((bf16[2,64,768]{2,1,0:T(8,128)(2,1)S(1)}, bf16[2,64,768]{2,1,0:T(8,128)(2,1)S(1)}, u32[]{:S(2)}, u32[]{:S(2)}) %collective-permute-start.23) | collective-permute-done | bytes 196640 | tf_op jit(solution)/shard_map/ppermute | solution.py:107
  142.4 3.5 %collective-permute-start.25 = (bf16[2,64,768]{2,1,0:T(8,128)(2,1)S(1)}, bf16[2,64,768]{2,1,0:T(8,128)(2,1)S(1)}, u32[]{:S(2)}, u32[]{:S(2)}) collective-permute-start(bf16[2,64,768]{2,1,0:T(8,128)(2,1)S(1)} %add_convert_fusion), channel_id=1, source_target_pairs={{0,8},{4,12},{8,0},{12,4},{1,9},{5,13},{9,1},{13,5},{2,10},{6,14},... | collective-permute-start | bytes 589832 | tf_op jit(solution)/shard_map/ppermute | solution.py:107
  145.9 0.9 collective-permute-start.24
  146.8 6.7 %collective-permute-done.25.far_ref = bf16[2,64,768]{2,1,0:T(8,128)(2,1)S(1)} collective-permute-done((bf16[2,64,768]{2,1,0:T(8,128)(2,1)S(1)}, bf16[2,64,768]{2,1,0:T(8,128)(2,1)S(1)}, u32[]{:S(2)}, u32[]{:S(2)}) %collective-permute-start.25) | collective-permute-done | bytes 196640 | tf_op jit(solution)/shard_map/ppermute | solution.py:107
  153.5 1.3 shard_map.70
  (49 shorter events, 2.4 us)
Async XLA Ops:
  0.0 5.0 %copy-start = (bf16[768,3,768]{2,0,1:T(8,128)(2,1)S(1)}, bf16[768,3,768]{2,0,1:T(8,128)(2,1)}, u32[]{:S(2)}) copy-start(bf16[768,3,768]{2,0,1:T(8,128)(2,1)} %param.7) | copy-start | bytes 10616836
  0.0 14.2 %copy-start.2 = (s32[2]{0:T(128)S(1)}, s32[2]{0:T(128)}, u32[]{:S(2)}) copy-start(s32[2]{0:T(128)} %param.11) | copy-start | bytes 28
  0.0 14.3 %copy-start.3 = (s32[2]{0:T(128)S(1)}, s32[2]{0:T(128)}, u32[]{:S(2)}) copy-start(s32[2]{0:T(128)} %param.10) | copy-start | bytes 28
  0.0 14.4 %copy-start.1 = (s32[2,4]{1,0:T(2,128)S(1)}, s32[2,4]{1,0:T(2,128)}, u32[]{:S(2)}) copy-start(s32[2,4]{1,0:T(2,128)} %param.9) | copy-start | bytes 100
  1.9 16.8 %collective-permute-start = (bf16[128,1536]{1,0:T(8,128)(2,1)}, bf16[128,1536]{1,0:T(8,128)(2,1)}, u32[]{:S(2)}, u32[]{:S(2)}) collective-permute-start(bf16[128,1536]{1,0:T(8,128)(2,1)} %dynamic-slice_bitcast_fusion.2.refs_0_), channel_id=1, source_target_pairs={{0,4},{4,0},{8,12},{12,8},{1,5},{5,1},{9,13},{13,9},{2,6},{6,2},{1... | collective-permute-start | bytes 1179656 | tf_op jit(solution)/shard_map/ppermute | solution.py:107
  6.0 15.8 %collective-permute-start.2 = (bf16[3,384,384]{2,1,0:T(8,128)(2,1)}, bf16[3,384,384]{2,1,0:T(8,128)(2,1)}, u32[]{:S(2)}, u32[]{:S(2)}) collective-permute-start(bf16[3,384,384]{2,1,0:T(8,128)(2,1)} %dynamic-slice_bitcast_fusion), channel_id=1, source_target_pairs={{0,0},{1,8},{4,4},{5,12},{8,1},{9,9},{12,5},{13,13},{2,2},{3,10},{... | collective-permute-start | bytes 2654216 | tf_op jit(solution)/shard_map/ppermute | solution.py:347
  19.6 20.3 %collective-permute-start.1 = (bf16[392,768]{1,0:T(8,128)(2,1)}, bf16[392,768]{1,0:T(8,128)(2,1)}, u32[]{:S(2)}, u32[]{:S(2)}) collective-permute-start(bf16[392,768]{1,0:T(8,128)(2,1)} %pad_maximum_fusion), channel_id=1, source_target_pairs={{0,4},{4,0},{8,12},{12,8},{1,5},{5,1},{9,13},{13,9},{2,6},{6,2},{1... | collective-permute-start | bytes 1806344 | tf_op jit(solution)/shard_map/ppermute | solution.py:107
  19.6 47.9 %collective-permute-start.5 = (bf16[768,768]{1,0:T(8,128)(2,1)}, bf16[768,768]{1,0:T(8,128)(2,1)}, u32[]{:S(2)}, u32[]{:S(2)}) collective-permute-start(bf16[768,768]{1,0:T(8,128)(2,1)} %refs_4_.3), channel_id=1, source_target_pairs={{0,1},{1,0},{2,3},{3,2},{4,5},{5,4},{6,7},{7,6},{8,9},{9,8},{10,11... | collective-permute-start | bytes 3538952 | tf_op jit(solution)/shard_map/ppermute | solution.py:107
  19.6 12.2 %collective-permute-start.3 = (bf16[128,1536]{1,0:T(8,128)(2,1)}, bf16[128,1536]{1,0:T(8,128)(2,1)}, u32[]{:S(2)}, u32[]{:S(2)}) collective-permute-start(bf16[128,1536]{1,0:T(8,128)(2,1)} %dynamic-slice_bitcast_fusion.2.refs_0_), channel_id=1, source_target_pairs={{0,2},{2,0},{1,3},{3,1},{4,6},{6,4},{5,7},{7,5},{8,10},{10,8},{9,1... | collective-permute-start | bytes 1179656 | tf_op jit(solution)/shard_map/ppermute | solution.py:107
  21.4 20.9 %collective-permute-start.6 = (bf16[128,1536]{1,0:T(8,128)(2,1)}, bf16[128,1536]{1,0:T(8,128)(2,1)}, u32[]{:S(2)}, u32[]{:S(2)}) collective-permute-start(bf16[128,1536]{1,0:T(8,128)(2,1)} %collective-permute-done.refs_1_), channel_id=1, source_target_pairs={{0,2},{2,0},{1,3},{3,1},{4,6},{6,4},{5,7},{7,5},{8,10},{10,8},{9,1... | collective-permute-start | bytes 1179656 | tf_op jit(solution)/shard_map/ppermute | solution.py:107
  21.8 48.6 %collective-permute-start.8 = (bf16[3,384,384]{2,1,0:T(8,128)(2,1)}, bf16[3,384,384]{2,1,0:T(8,128)(2,1)}, u32[]{:S(2)}, u32[]{:S(2)}) collective-permute-start(bf16[3,384,384]{2,1,0:T(8,128)(2,1)} %collective-permute-done.2.refs_8_.refs_0_), channel_id=1, source_target_pairs={{0,16},{16,0},{1,17},{17,1},{2,18},{18,2},{3,19},{19,3},{4,20},{20... | collective-permute-start | bytes 2654216 | tf_op jit(solution)/shard_map/ppermute | solution.py:107
  31.8 38.6 %collective-permute-start.9 = (bf16[3,384,256]{2,1,0:T(8,128)(2,1)S(1)}, bf16[3,384,256]{2,1,0:T(8,128)(2,1)}, u32[]{:S(2)}, u32[]{:S(2)}) collective-permute-start(bf16[3,384,256]{2,1,0:T(8,128)(2,1)S(1)} %dynamic-slice_bitcast_fusion.1), channel_id=1, source_target_pairs={{0,4},{1,12},{4,0},{5,8},{8,5},{9,13},{12,1},{13,9},{2,6},{3,14},{... | collective-permute-start | bytes 1769480 | tf_op jit(solution)/shard_map/ppermute | solution.py:347
  39.8 30.6 %collective-permute-start.10 = (bf16[392,768]{1,0:T(8,128)(2,1)}, bf16[392,768]{1,0:T(8,128)(2,1)}, u32[]{:S(2)}, u32[]{:S(2)}) collective-permute-start(bf16[392,768]{1,0:T(8,128)(2,1)} %collective-permute-done.1.refs_6_), channel_id=1, source_target_pairs={{0,16},{16,0},{1,17},{17,1},{2,18},{18,2},{3,19},{19,3},{4,20},{20... | collective-permute-start | bytes 1806344 | tf_op jit(solution)/shard_map/ppermute | solution.py:107
  42.2 25.2 %collective-permute-start.4 = (bf16[136,1536]{1,0:T(8,128)(2,1)S(1)}, bf16[136,1536]{1,0:T(8,128)(2,1)}, u32[]{:S(2)}, u32[]{:S(2)}) collective-permute-start(bf16[136,1536]{1,0:T(8,128)(2,1)S(1)} %pad_maximum_fusion.1), channel_id=1, source_target_pairs={{0,8},{4,12},{8,0},{12,4},{1,9},{5,13},{9,1},{13,5},{2,10},{6,14},... | collective-permute-start | bytes 1253384 | tf_op jit(solution)/shard_map/ppermute | solution.py:107
  67.5 11.4 %collective-permute-start.7 = (bf16[136,1536]{1,0:T(8,128)(2,1)S(1)}, bf16[136,1536]{1,0:T(8,128)(2,1)}, u32[]{:S(2)}, u32[]{:S(2)}) collective-permute-start(bf16[136,1536]{1,0:T(8,128)(2,1)S(1)} %pad_maximum_fusion.1), channel_id=1, source_target_pairs={{0,12},{4,8},{8,4},{12,0},{1,13},{5,9},{9,5},{13,1},{2,14},{6,10},... | collective-permute-start | bytes 1253384 | tf_op jit(solution)/shard_map/ppermute | solution.py:107
  70.4 13.8 %collective-permute-start.11 = (bf16[3,384,256]{2,1,0:T(8,128)(2,1)}, bf16[3,384,256]{2,1,0:T(8,128)(2,1)}, u32[]{:S(2)}, u32[]{:S(2)}) collective-permute-start(bf16[3,384,256]{2,1,0:T(8,128)(2,1)} %collective-permute-done.9.refs_10_), channel_id=1, source_target_pairs={{0,16},{16,0},{1,17},{17,1},{2,18},{18,2},{3,19},{19,3},{4,20},{20... | collective-permute-start | bytes 1769480 | tf_op jit(solution)/shard_map/ppermute | solution.py:107
  72.6 23.3 %collective-permute-start.14 = (bf16[136,1536]{1,0:T(8,128)(2,1)}, bf16[136,1536]{1,0:T(8,128)(2,1)}, u32[]{:S(2)}, u32[]{:S(2)}) collective-permute-start(bf16[136,1536]{1,0:T(8,128)(2,1)} %collective-permute-done.4.refs_2_), channel_id=1, source_target_pairs={{0,2},{2,0},{1,3},{3,1},{4,6},{6,4},{5,7},{7,5},{8,10},{10,8},{9,1... | collective-permute-start | bytes 1253384 | tf_op jit(solution)/shard_map/ppermute | solution.py:107
  78.9 17.0 %collective-permute-start.15 = (bf16[136,1536]{1,0:T(8,128)(2,1)}, bf16[136,1536]{1,0:T(8,128)(2,1)}, u32[]{:S(2)}, u32[]{:S(2)}) collective-permute-start(bf16[136,1536]{1,0:T(8,128)(2,1)} %collective-permute-done.7.refs_3_), channel_id=1, source_target_pairs={{0,2},{2,0},{1,3},{3,1},{4,6},{6,4},{5,7},{7,5},{8,10},{10,8},{9,1... | collective-permute-start | bytes 1253384 | tf_op jit(solution)/shard_map/ppermute | solution.py:107
  84.2 10.2 %collective-permute-start.12 = (bf16[3,384,128]{2,1,0:T(8,128)(2,1)}, bf16[3,384,128]{2,1,0:T(8,128)(2,1)}, u32[]{:S(2)}, u32[]{:S(2)}) collective-permute-start(bf16[3,384,128]{2,1,0:T(8,128)(2,1)} %dynamic-slice_bitcast_fusion.3), channel_id=1, source_target_pairs={{0,4},{1,12},{4,0},{5,8},{8,5},{9,13},{12,1},{13,9},{2,6},{3,14},{... | collective-permute-start | bytes 884744 | tf_op jit(solution)/shard_map/ppermute | solution.py:347
  94.4 8.6 %collective-permute-start.13 = (bf16[3,384,128]{2,1,0:T(8,128)(2,1)}, bf16[3,384,128]{2,1,0:T(8,128)(2,1)S(1)}, u32[]{:S(2)}, u32[]{:S(2)}) collective-permute-start(bf16[3,384,128]{2,1,0:T(8,128)(2,1)} %collective-permute-done.12.refs_2_), channel_id=1, source_target_pairs={{0,16},{16,0},{1,17},{17,1},{2,18},{18,2},{3,19},{19,3},{4,20},{20... | collective-permute-start | bytes 884744 | tf_op jit(solution)/shard_map/ppermute | solution.py:107
  102.9 5.0 %collective-permute-start.17 = (bf16[4,320,512]{2,1,0:T(8,128)(2,1)S(1)}, bf16[4,320,512]{2,1,0:T(8,128)(2,1)S(1)}, u32[]{:S(2)}, u32[]{:S(2)}) collective-permute-start(bf16[4,320,512]{2,1,0:T(8,128)(2,1)S(1)} %get-tuple-element.40), channel_id=1, source_target_pairs={{0,1},{1,0},{2,3},{3,2},{4,5},{5,4},{6,7},{7,6},{8,9},{9,8},{10,11... | collective-permute-start | bytes 3932168 | tf_op jit(solution)/shard_map/ppermute | solution.py:107
  106.8 4.9 %collective-permute-start.16 = (bf16[4,320,256]{2,1,0:T(8,128)(2,1)S(1)}, bf16[4,320,256]{2,1,0:T(8,128)(2,1)S(1)}, u32[]{:S(2)}, u32[]{:S(2)}) collective-permute-start(bf16[4,320,256]{2,1,0:T(8,128)(2,1)S(1)} %get-tuple-element.45), channel_id=1, source_target_pairs={{0,1},{1,0},{2,3},{3,2},{4,5},{5,4},{6,7},{7,6},{8,9},{9,8},{10,11... | collective-permute-start | bytes 1966088 | tf_op jit(solution)/shard_map/ppermute | solution.py:107
  107.4 11.1 %collective-permute-start.21 = (bf16[392,768]{1,0:T(8,128)(2,1)}, bf16[392,768]{1,0:T(8,128)(2,1)S(1)}, u32[]{:S(2)}, u32[]{:S(2)}) collective-permute-start(bf16[392,768]{1,0:T(8,128)(2,1)} %collective-permute-done.1.refs_6_), channel_id=1, source_target_pairs={{0,1},{1,0},{2,3},{3,2},{4,5},{5,4},{6,7},{7,6},{8,9},{9,8},{10,11... | collective-permute-start | bytes 1806344 | tf_op jit(solution)/shard_map/ppermute | solution.py:107
  107.5 11.0 %collective-permute-start.22 = (bf16[392,768]{1,0:T(8,128)(2,1)}, bf16[392,768]{1,0:T(8,128)(2,1)S(1)}, u32[]{:S(2)}, u32[]{:S(2)}) collective-permute-start(bf16[392,768]{1,0:T(8,128)(2,1)} %collective-permute-done.10.refs_7_), channel_id=1, source_target_pairs={{0,1},{1,0},{2,3},{3,2},{4,5},{5,4},{6,7},{7,6},{8,9},{9,8},{10,11... | collective-permute-start | bytes 1806344 | tf_op jit(solution)/shard_map/ppermute | solution.py:107
  113.9 10.1 %collective-permute-start.18 = (bf16[2,128,384]{2,1,0:T(8,128)(2,1)S(1)}, bf16[2,128,384]{2,1,0:T(8,128)(2,1)S(1)}, u32[]{:S(2)}, u32[]{:S(2)}) collective-permute-start(bf16[2,128,384]{2,1,0:T(8,128)(2,1)S(1)} %get-tuple-element.51), channel_id=1, source_target_pairs={{0,4},{4,0},{8,12},{12,8},{1,5},{5,1},{9,13},{13,9},{2,6},{6,2},{1... | collective-permute-start | bytes 589832 | tf_op jit(solution)/shard_map/ppermute | solution.py:107
  116.0 17.1 %collective-permute-start.19 = (bf16[2,128,384]{2,1,0:T(8,128)(2,1)S(1)}, bf16[2,128,384]{2,1,0:T(8,128)(2,1)S(1)}, u32[]{:S(2)}, u32[]{:S(2)}) collective-permute-start(bf16[2,128,384]{2,1,0:T(8,128)(2,1)S(1)} %get-tuple-element.50.refs_0_), channel_id=1, source_target_pairs={{0,8},{4,12},{8,0},{12,4},{1,9},{5,13},{9,1},{13,5},{2,10},{6,14},... | collective-permute-start | bytes 589832 | tf_op jit(solution)/shard_map/ppermute | solution.py:107
  116.0 17.1 %collective-permute-start.20 = (bf16[2,128,384]{2,1,0:T(8,128)(2,1)S(1)}, bf16[2,128,384]{2,1,0:T(8,128)(2,1)S(1)}, u32[]{:S(2)}, u32[]{:S(2)}) collective-permute-start(bf16[2,128,384]{2,1,0:T(8,128)(2,1)S(1)} %get-tuple-element.51), channel_id=1, source_target_pairs={{0,12},{4,8},{8,4},{12,0},{1,13},{5,9},{9,5},{13,1},{2,14},{6,10},... | collective-permute-start | bytes 589832 | tf_op jit(solution)/shard_map/ppermute | solution.py:107
  136.6 5.7 %collective-permute-start.23 = (bf16[2,64,768]{2,1,0:T(8,128)(2,1)S(1)}, bf16[2,64,768]{2,1,0:T(8,128)(2,1)S(1)}, u32[]{:S(2)}, u32[]{:S(2)}) collective-permute-start(bf16[2,64,768]{2,1,0:T(8,128)(2,1)S(1)} %get-tuple-element.54), channel_id=1, source_target_pairs={{0,2},{2,0},{1,3},{3,1},{4,6},{6,4},{5,7},{7,5},{8,10},{10,8},{9,1... | collective-permute-start | bytes 589832 | tf_op jit(solution)/shard_map/ppermute | solution.py:107
  142.4 11.1 %collective-permute-start.25 = (bf16[2,64,768]{2,1,0:T(8,128)(2,1)S(1)}, bf16[2,64,768]{2,1,0:T(8,128)(2,1)S(1)}, u32[]{:S(2)}, u32[]{:S(2)}) collective-permute-start(bf16[2,64,768]{2,1,0:T(8,128)(2,1)S(1)} %add_convert_fusion), channel_id=1, source_target_pairs={{0,8},{4,12},{8,0},{12,4},{1,9},{5,13},{9,1},{13,5},{2,10},{6,14},... | collective-permute-start | bytes 589832 | tf_op jit(solution)/shard_map/ppermute | solution.py:107
  145.9 7.6 %collective-permute-start.24 = (bf16[2,64,768]{2,1,0:T(8,128)(2,1)S(1)}, bf16[2,64,768]{2,1,0:T(8,128)(2,1)S(1)}, u32[]{:S(2)}, u32[]{:S(2)}) collective-permute-start(bf16[2,64,768]{2,1,0:T(8,128)(2,1)S(1)} %get-tuple-element.55), channel_id=1, source_target_pairs={{0,2},{2,0},{1,3},{3,1},{4,6},{6,4},{5,7},{7,5},{8,10},{10,8},{9,1... | collective-permute-start | bytes 589832 | tf_op jit(solution)/shard_map/ppermute | solution.py:107
